TPU v7x, 32 devices: a whole 2x2x4 slice. The times are simulated.
32 devices in a mesh: seq: 8 (over y, x, core), vocab: 4 (over z).
Axes of the slice: x: 2, y: 2, z: 4, core: 2. Of those that a mesh axis runs over, the one named last changes fastest.
Arguments:
- hidden: bfloat16 [1024, 8192], P('seq'), may hold values from -120 to 120
- head: bfloat16 [8192, 8192], P(None, ('seq', 'vocab')), may hold values from -0.5 to 0.5
- mask: int32 [1024], P('seq'), may hold values from 0 to 1, as said below
Outputs:
- positionwise_uncertainty: float32 [1024], P('seq')
- average_uncertainty_reward: float32 [], replicated
- derivative_wrt_latent_vectors: bfloat16 [1024, 8192], P('seq', 'vocab')
Inputs may be any that keep to these rules, and one draw needn't show every extreme that they name: Among the 128 tokens of one index of seq at least half of 16 and at most 16 have mask 1, and the last index of seq has exactly 16; later indices have no fewer than earlier ones.
All inputs are finite; a program needn't handle non-finite values.
Results may differ from a plain program's by a relative error of at most 0.019.
Values may be sent and summed in bfloat16 or wider, within the bound.
No kernel may reach another device: no remote copies, remote signals or barrier semaphores. Data moves between devices by JAX's collectives and lax.ppermute only.
A program may use at most 64 MiB of HBM per device.

v0:
```python
import jax
import jax.numpy as jnp
from jax import lax
from jax.sharding import PartitionSpec as P

ACT_DEV = 16


def body(hidden, head, mask):
    inclusion_indicator = mask.astype(jnp.float32)
    slots = jnp.cumsum(mask) - 1
    picker = (slots[None, :] == jnp.arange(ACT_DEV, dtype=jnp.int32)[:, None]) & (
        mask[None, :] == 1
    )
    picker = picker.astype(jnp.bfloat16)
    source = jnp.dot(picker, hidden, preferred_element_type=jnp.float32).astype(jnp.bfloat16)
    rows_here = source.shape[0]
    logits = jnp.dot(
        lax.all_gather(source, "seq", axis=0, tiled=True), head, preferred_element_type=jnp.float32
    )
    local_top = jnp.max(logits, axis=1)
    top = lax.pmax(local_top, ("seq", "vocab"))
    ex = jnp.exp(logits - top[:, None])
    total, weighted = lax.psum(
        (jnp.sum(ex, axis=1), jnp.sum(ex * logits, axis=1)), ("seq", "vocab")
    )
    mean_logit = weighted / total
    distribution_uncertainty = top + jnp.log(total) - mean_logit
    prob = ex / total[:, None]
    score_grad = (-(prob * (logits - mean_logit[:, None]))).astype(jnp.bfloat16)
    partial_grad = lax.psum_scatter(
        lax.dot_general(
            score_grad, head, (((1,), (1,)), ((), ())), preferred_element_type=jnp.float32
        ).astype(jnp.bfloat16),
        "seq",
        scatter_dimension=0,
        tiled=True,
    )
    column_grad = lax.psum_scatter(partial_grad, "vocab", scatter_dimension=1, tiled=True).astype(
        jnp.float32
    )
    position = lax.axis_index("seq") * rows_here
    mine = lax.dynamic_slice_in_dim(distribution_uncertainty, position, rows_here, 0)
    spread = picker.astype(jnp.float32)
    mine = lax.dot_general(
        spread, mine[:, None], (((0,), (0,)), ((), ())), precision=lax.Precision.HIGHEST
    )[:, 0]
    column_grad = lax.dot_general(
        spread, column_grad, (((0,), (0,)), ((), ())), precision=lax.Precision.HIGHEST
    )
    positionwise_uncertainty = inclusion_indicator * mine
    aggregate_uncertainty, response_length_total = lax.psum(
        (jnp.sum(positionwise_uncertainty), jnp.sum(inclusion_indicator)), "seq"
    )
    average_uncertainty_reward = aggregate_uncertainty / response_length_total
    derivative_wrt_latent_vectors = (inclusion_indicator[:, None] * column_grad).astype(
        jnp.bfloat16
    )
    return (positionwise_uncertainty, average_uncertainty_reward, derivative_wrt_latent_vectors)


def solution(mesh):
    return jax.shard_map(
        body,
        mesh=mesh,
        in_specs=(P("seq", None), P(None, ("seq", "vocab")), P("seq")),
        out_specs=(P("seq"), P(), P("seq", "vocab")),
        check_vma=False,
    )
```

profile of v0, /device:TPU:0, one launch (start us, length us, event | category | flops | bytes accessed | tf_op | source)
XLA Modules:
  0.0 203.2 jit_solution(17039689155941618077)
XLA Ops:
  7.2 0.0 copy-start
  7.2 0.0 all-gather.2.cloned.1.call-start
  7.2 0.8 broadcast_compare_fusion
  8.0 0.8 copy.7
  8.8 0.2 reduce-window.8
  9.0 0.1 add_reduce_fusion
  9.1 0.0 copy-done
  9.1 1.1 convolution_convert_fusion.1
  10.2 0.0 all-gather.2.cloned.1.call-update
  10.2 0.0 reduce-scatter.3.cloned.1.call-start
  10.2 30.9 %all-gather.2.cloned.1.call-done = bf16[128,8192]{1,0:T(8,128)(2,1)} async-done(((bf16[16,8192]{1,0:T(8,128)(2,1)}), bf16[128,8192]{1,0:T(8,128)(2,1)}) %all-gather.2.cloned.1.call-update) | async-done | bytes 2097168 | tf_op jit(solution)/shard_map/all_gather | solution.py:19
  41.1 3.6 %fusion.16 = (f32[128]{0:T(128)S(1)}, f32[128,256]{1,0:T(8,128)S(1)}) fusion(bf16[128,8192]{1,0:T(8,128)(2,1)} %all-gather.2.cloned.1.call-done, bf16[8192,256]{1,0:T(8,128)(2,1)} %param.4), kind=kOutput, calls=%fused_computation.26 | convolution fusion | flops 536903552 | bytes 6423040 | tf_op jit(solution)/shard_map/dot_general | solution.py:18
  44.7 39.4 %pmax.7 = f32[128]{0:T(128)S(1)} all-reduce(f32[128]{0:T(128)S(1)} %get-tuple-element.11), channel_id=1, replica_groups=mesh['seq'=8,'vocab'=4] {'seq','vocab'}, use_global_device_ids=true, to_apply=%region_2.3 | all-reduce | flops 128 | bytes 1024 | tf_op jit(solution)/shard_map/pmax | solution.py:22
  84.1 0.2 fusion.2
  84.3 41.0 %all-reduce = (f32[128]{0:T(128)S(1)}, f32[128]{0:T(128)S(1)}) all-reduce(f32[128]{0:T(128)S(1)} %get-tuple-element.4, f32[128]{0:T(128)S(1)} %get-tuple-element.3), channel_id=1, replica_groups=mesh['seq'=8,'vocab'=4] {'seq','vocab'}, use_global_device_ids=true, to_apply=%region_6.7 | all-reduce | flops 256 | bytes 2048 | tf_op jit(solution)/shard_map/psum | solution.py:24
  125.3 5.0 %convolution_convert_fusion = bf16[128,8192]{1,0:T(8,128)(2,1)} fusion(bf16[8192,256]{1,0:T(8,128)(2,1)} %param.4, f32[128,256]{1,0:T(8,128)S(1)} %get-tuple-element.12, f32[128]{0:T(128)S(1)} %get-tuple-element.10, f32[128]{0:T(128)S(1)} %get-tuple-element.6, f32[128]{0:T(128)S(1)} %pmax.7), kind=kOutput, calls=%fused_computation | convolution fusion | flops 538116096 | bytes 6424064 | tf_op jit(solution)/shard_map/dot_general | solution.py:32
  130.3 0.0 copy-start.1
  130.3 0.0 reduce-scatter.3.cloned.1.call-update
  130.3 0.0 reduce-scatter.5.cloned.1.call-start
  130.4 41.1 %reduce-scatter.3.cloned.1.call-done = bf16[16,8192]{1,0:T(8,128)(2,1)} async-done(((bf16[128,8192]{1,0:T(8,128)(2,1)}), bf16[16,8192]{1,0:T(8,128)(2,1)}) %reduce-scatter.3.cloned.1.call-update) | async-done | bytes 262160 | tf_op jit(solution)/shard_map/reduce_scatter | solution.py:31
  171.5 0.0 reduce-scatter.5.cloned.1.call-update
  171.5 0.0 copy-done.1
  171.6 0.6 convert_reduce_fusion
  172.2 1.3 fusion.17
  173.5 13.3 %all-reduce.1 = (f32[]{:T(128)}, f32[]{:T(128)}) all-reduce(f32[]{:T(128)} %get-tuple-element.13, f32[]{:T(128)} %convert_reduce_fusion), channel_id=1, replica_groups=mesh['seq'=8,'vocab'=4] {'seq'}, use_global_device_ids=true, to_apply=%region_8.9 | all-reduce | flops 2 | bytes 16 | tf_op jit(solution)/shard_map/psum | solution.py:52
  188.1 5.4 %reduce-scatter.5.cloned.1.call-done = bf16[16,2048]{1,0:T(8,128)(2,1)} async-done(((bf16[16,8192]{1,0:T(8,128)(2,1)}), bf16[16,2048]{1,0:T(8,128)(2,1)}) %reduce-scatter.5.cloned.1.call-update) | async-done | bytes 65552 | tf_op jit(solution)/shard_map/reduce_scatter | solution.py:39
  193.6 2.0 fusion
  (2 shorter events, 0.0 us)
Async XLA Ops:
  7.2 1.9 copy-start
  7.2 33.9 %all-gather.2.cloned.1.call-start = ((), (), s32[]{:S(2)}) async-start(), calls=%async_computation.2 | async-start | bytes 2359296 | tf_op jit(solution)/shard_map/all_gather | solution.py:19
  10.2 161.3 %reduce-scatter.3.cloned.1.call-start = ((), (), s32[]{:S(2)}) async-start(), calls=%async_computation.3 | async-start | bytes 2359296 | tf_op jit(solution)/shard_map/reduce_scatter | solution.py:31
  130.3 41.2 %copy-start.1 = (s32[128]{0:T(128)S(1)}, s32[128]{0:T(128)}, u32[]{:S(2)}) copy-start(s32[128]{0:T(128)} %param.5) | copy-start | bytes 1540
  130.3 63.2 %reduce-scatter.5.cloned.1.call-start = ((), (), s32[]{:S(2)}) async-start(), calls=%async_computation.4 | async-start | bytes 327680 | tf_op jit(solution)/shard_map/reduce_scatter | solution.py:39
Sparse Core Ops, SparseCore 0:
  10.5 30.5 all-gather.1
  130.5 40.9 reduce-scatter.2
  173.9 19.6 reduce-scatter.4
where the time goes:
time: 204 us; the launch traced here: 203 us
  blocking collectives  93.7 us (46%)
  waiting for transfers between devices  77.5 us (38%)
  between operations  16.3 us (8%)
  matrix products  13 us (6%)
    reduce_scatter x1, waiting for transfers between devices, body(): lax.psum_scatter(lax.dot_general(score_grad, head, (((1,), (1,)), ((), ()...  41.1 us
    psum x1, blocking collectives, body(): lax.psum((jnp.sum(ex, axis=1), jnp.sum(ex * logits, axis=1)), ('seq', 'vo...  41 us
    pmax x1, blocking collectives, body(): top = lax.pmax(local_top, ('seq', 'vocab'))  39.4 us
    all_gather x1, waiting for transfers between devices, body(): lax.all_gather(source, 'seq', axis=0, tiled=True)  30.9 us
    psum x1, blocking collectives, body(): lax.psum((jnp.sum(positionwise_uncertainty), jnp.sum(inclusion_indicator)...  13.3 us
    reduce_scatter x1, waiting for transfers between devices, body(): lax.psum_scatter(partial_grad, 'vocab', scatter_dimension=1, tiled=True)  5.45 us
    dot_general x1, matrix products, body(): lax.dot_general(score_grad, head, (((1,), (1,)), ((), ())), preferred_ele...  5.04 us
  transfers between devices with their start and end apart: 3, of which 3 were waited for; matrix products, arithmetic and copies ran while one was open for 1% of the time, Pallas kernels for 0%

commit v1 on v0

v1 whole, which is shorter than its diff:
```python
import jax
import jax.numpy as jnp
from jax import lax
from jax.sharding import PartitionSpec as P

ACT_DEV = 16


def swap(value, axis, size, mask):
    return lax.ppermute(value, axis, [(i, i ^ mask) for i in range(size)])


def body(n_seq, n_vocab, hidden, head, mask):
    f32, bf16 = jnp.float32, jnp.bfloat16
    n_chip = n_seq // 2
    width = hidden.shape[1]
    me = lax.axis_index("seq")
    column = lax.axis_index("vocab")

    slots = jnp.cumsum(mask) - 1
    picker = (slots[None, :] == jnp.arange(ACT_DEV, dtype=jnp.int32)[:, None]) & (
        mask[None, :] == 1
    )
    count = jnp.sum(mask).astype(f32)
    own = jnp.dot(picker.astype(bf16), hidden, preferred_element_type=f32).astype(bf16)

    near = [own] + [swap(own, "seq", n_seq, g << 1) for g in range(1, n_chip)]
    near = jnp.concatenate(near, axis=0)
    far = swap(near, "seq", n_seq, 1)
    rows = jnp.concatenate([near, far], axis=0)

    logits = jnp.dot(rows, head, preferred_element_type=f32)
    local_top = jnp.max(logits, axis=1)
    local_ex = jnp.exp(logits - local_top[:, None])
    local_total = jnp.sum(local_ex, axis=1)
    local_weighted = jnp.sum(local_ex * (logits - local_top[:, None]), axis=1)

    place = jnp.arange(n_seq, dtype=jnp.int32)
    relative = (place % n_chip) * 2 + place // n_chip
    order = (relative ^ me)[:, None] == place[None, :]

    def to_device_order(value):
        value = value.reshape(n_seq, ACT_DEV)
        return jnp.sum(jnp.where(order[:, :, None], value[:, None, :], 0.0), axis=0).reshape(-1)

    def to_relative_order(value):
        value = value.reshape(n_seq, ACT_DEV)
        return jnp.sum(jnp.where(order[:, :, None], value[None, :, :], 0.0), axis=1).reshape(-1)

    stats = jnp.stack(
        [
            to_device_order(local_top),
            to_device_order(local_total),
            to_device_order(local_weighted),
            jnp.full_like(local_top, count),
        ]
    )
    n_all = n_seq * n_vocab
    stats = jnp.broadcast_to(stats[None], (n_all,) + stats.shape)
    stats = lax.all_to_all(stats, ("seq", "vocab"), 0, 0, tiled=True)
    tops, totals, weights = stats[:, 0], stats[:, 1], stats[:, 2]
    top = jnp.max(tops, axis=0)
    offset = tops - top[None]
    scale = jnp.exp(offset)
    total = jnp.sum(scale * totals, axis=0)
    centred = jnp.sum(scale * (weights + offset * totals), axis=0) / total
    entropy = jnp.log(total) - centred
    counts = stats.reshape(n_seq, n_vocab, 4, -1)[:, 0, 3, :ACT_DEV]
    valid = jnp.arange(ACT_DEV, dtype=jnp.int32).astype(f32)[None, :] < counts
    entropy = entropy.reshape(n_seq, ACT_DEV)
    average = jnp.sum(jnp.where(valid, entropy, 0.0)) / jnp.sum(counts[:, 0])
    mine = jnp.sum(jnp.where((place == me)[:, None], entropy, 0.0), axis=0)
    positionwise = jnp.sum(jnp.where(picker, mine[:, None], 0.0), axis=0)

    row_top = to_relative_order(top)[:, None]
    row_total = to_relative_order(total)[:, None]
    row_mean = row_top + to_relative_order(centred)[:, None]
    prob = jnp.exp(logits - row_top) / row_total
    score = (-(prob * (logits - row_mean))).astype(bf16)

    half = n_chip * ACT_DEV

    def gradient(part):
        return lax.dot_general(part, head, (((1,), (1,)), ((), ())), preferred_element_type=f32)

    away = swap(gradient(score[half:]).astype(bf16), "seq", n_seq, 1)
    here = gradient(score[:half]) + away.astype(f32)
    sums = here[:ACT_DEV]
    for g in range(1, n_chip):
        block = here[g * ACT_DEV : (g + 1) * ACT_DEV].astype(bf16)
        sums = sums + swap(block, "seq", n_seq, g << 1).astype(f32)

    wide = width // n_vocab

    def columns(k):
        return lax.dynamic_slice_in_dim(sums, (column ^ k) * wide, wide, 1)

    result = columns(0)
    for k in range(1, n_vocab):
        result = result + swap(columns(k).astype(bf16), "vocab", n_vocab, k).astype(f32)
    spread = picker.astype(bf16)
    derivative = lax.dot_general(
        spread, result.astype(bf16), (((0,), (0,)), ((), ())), preferred_element_type=f32
    ).astype(bf16)
    return positionwise, average, derivative


def solution(mesh):
    n_seq, n_vocab = mesh.shape["seq"], mesh.shape["vocab"]

    def run(hidden, head, mask):
        return body(n_seq, n_vocab, hidden, head, mask)

    return jax.shard_map(
        run,
        mesh=mesh,
        in_specs=(P("seq", None), P(None, ("seq", "vocab")), P("seq")),
        out_specs=(P("seq"), P(), P("seq", "vocab")),
        check_vma=False,
    )
```

time: 204 us -> 78 us (0.38)
  blocking collectives: 93.7 us -> 0 us
  waiting for transfers between devices: 77.5 us -> 33.2 us
  starting transfers between devices: 0.12 us -> 17.5 us
  between operations: 16.3 us -> 3.91 us
  local copies, waits for them, and re-layouts: 0.77 us -> 6.54 us
  other arithmetic: 1.87 us -> 5.48 us
    psum x2 -> x0, blocking collectives: 54.3 us -> none  [the longest x1 41 us: body(): lax.psum((jnp.sum(ex, axis=1), jnp.sum(ex * logits, axis=1)), ('seq', 'vo...]
    reduce_scatter x2 -> x0, waiting for transfers between devices: 46.6 us -> none  [the longest x1 41.1 us: body(): lax.psum_scatter(lax.dot_general(score_grad, head, (((1,), (1,)), ((), ()...]
    pmax x1 -> x0, blocking collectives: 39.4 us -> none  [body(): top = lax.pmax(local_top, ('seq', 'vocab'))]
    all_gather x1 -> x0, waiting for transfers between devices: 30.9 us -> none  [body(): lax.all_gather(source, 'seq', axis=0, tiled=True)]
    ppermute x0 -> x11, waiting for transfers between devices: none -> 25.7 us  [swap(): return lax.ppermute(value, axis, [(i, i ^ mask) for i in range(size)])]
    ppermute x0 -> x11, starting transfers between devices: none -> 12.5 us  [swap(): return lax.ppermute(value, axis, [(i, i ^ mask) for i in range(size)])]
    all_to_all x0 -> x1, waiting for transfers between devices: none -> 7.47 us  [body(): stats = lax.all_to_all(stats, ('seq', 'vocab'), 0, 0, tiled=True)]
    all_to_all x0 -> x1, starting transfers between devices: none -> 4.92 us  [body(): stats = lax.all_to_all(stats, ('seq', 'vocab'), 0, 0, tiled=True)]
  transfers between devices with their start and end apart: 3 -> 12, of which waited for: 3 -> 9; matrix products, arithmetic and copies ran while one was open for 1% -> 5% of each run, Pallas kernels for 0% -> 0%
where the time goes in v1:
time: 78 us; the launch traced here: 77.7 us
  waiting for transfers between devices  33.2 us (43%)
  starting transfers between devices  17.5 us (22%)
  matrix products  11.1 us (14%)
  local copies, waits for them, and re-layouts  6.54 us (8%)
  other arithmetic  5.48 us (7%)
  between operations  3.91 us (5%)
    ppermute x11, waiting for transfers between devices, swap(): return lax.ppermute(value, axis, [(i, i ^ mask) for i in range(size)])  25.7 us
    ppermute x11, starting transfers between devices, swap(): return lax.ppermute(value, axis, [(i, i ^ mask) for i in range(size)])  12.5 us
    all_to_all x1, waiting for transfers between devices, body(): stats = lax.all_to_all(stats, ('seq', 'vocab'), 0, 0, tiled=True)  7.47 us
    dot_general x2, matrix products, gradient(): lax.dot_general(part, head, (((1,), (1,)), ((), ())), preferred_element_t...  6.44 us
    all_to_all x1, starting transfers between devices, body(): stats = lax.all_to_all(stats, ('seq', 'vocab'), 0, 0, tiled=True)  4.92 us
    dot_general x1, matrix products, body(): logits = jnp.dot(rows, head, preferred_element_type=f32)  2.42 us
    unnamed x11, local copies, waits for them, and re-layouts  2.19 us
  transfers between devices with their start and end apart: 12, of which 9 were waited for; matrix products, arithmetic and copies ran while one was open for 5% of the time, Pallas kernels for 0%

profile of v1, /device:TPU:0, one launch (start us, length us, event | category | flops | bytes accessed | tf_op | source)
XLA Modules:
  0.0 77.7 jit_solution(1790961563639874386)
XLA Ops:
  0.7 0.8 %broadcast_compare_fusion = pred[128]{0:T(512)(128)(4,1)S(1)} fusion(s32[128]{0:T(128)} %param.5), kind=kLoop, calls=%fused_computation.61 | loop fusion | flops 128 | bytes 640 | tf_op jit(solution)/shard_map/eq | solution.py:22
  1.5 0.8 copy.14
  2.2 0.2 reduce-window.8
  2.4 0.1 add_reduce_fusion
  2.5 1.1 %constant_dynamic-update-slice_fusion.4 = (bf16[128,8192]{1,0:T(8,128)(2,1)}, bf16[16,8192]{1,0:T(8,128)(2,1)S(1)}) fusion(bf16[128,8192]{1,0:T(8,128)(2,1)S(1)} %copy-done, s32[128]{0:T(128)S(1)} %add_reduce_fusion, pred[128]{0:T(512)(128)(4,1)S(1)} %broadcast_compare_fusion), kind=kOutput, calls=%fused_computation.36 | convolution fusion | flops 33689600 | bytes 2622080 | tf_op jit(solution)/shard_map/dot_general | solution.py:25
  3.6 2.9 %collective-permute-start = (bf16[16,8192]{1,0:T(8,128)(2,1)S(1)}, bf16[16,8192]{1,0:T(8,128)(2,1)S(1)}, u32[]{:S(2)}, u32[]{:S(2)}) collective-permute-start(bf16[16,8192]{1,0:T(8,128)(2,1)S(1)} %get-tuple-element.23), channel_id=1, source_target_pairs={{0,8},{4,12},{8,0},{12,4},{16,24},{20,28},{24,16},{28,20},{1,9},{5... | collective-permute-start | bytes 786440 | tf_op jit(solution)/shard_map/ppermute | solution.py:10
  6.5 1.5 %collective-permute-start.1 = (bf16[16,8192]{1,0:T(8,128)(2,1)S(1)}, bf16[16,8192]{1,0:T(8,128)(2,1)S(1)}, u32[]{:S(2)}, u32[]{:S(2)}) collective-permute-start(bf16[16,8192]{1,0:T(8,128)(2,1)S(1)} %get-tuple-element.23), channel_id=1, source_target_pairs={{0,16},{4,20},{8,24},{12,28},{16,0},{20,4},{24,8},{28,12},{1,17},{... | collective-permute-start | bytes 786440 | tf_op jit(solution)/shard_map/ppermute | solution.py:10
  8.1 0.6 reduce_sum.144
  9.5 4.2 %collective-permute-done = bf16[16,8192]{1,0:T(8,128)(2,1)S(1)} collective-permute-done((bf16[16,8192]{1,0:T(8,128)(2,1)S(1)}, bf16[16,8192]{1,0:T(8,128)(2,1)S(1)}, u32[]{:S(2)}, u32[]{:S(2)}) %collective-permute-start) | collective-permute-done | bytes 262176 | tf_op jit(solution)/shard_map/ppermute | solution.py:10
  13.7 6.3 %collective-permute-done.1 = bf16[16,8192]{1,0:T(8,128)(2,1)S(1)} collective-permute-done((bf16[16,8192]{1,0:T(8,128)(2,1)S(1)}, bf16[16,8192]{1,0:T(8,128)(2,1)S(1)}, u32[]{:S(2)}, u32[]{:S(2)}) %collective-permute-start.1) | collective-permute-done | bytes 262176 | tf_op jit(solution)/shard_map/ppermute | solution.py:10
  20.1 0.7 constant_dynamic-update-slice_fusion.3
  20.8 0.7 constant_dynamic-update-slice_fusion.2
  21.5 0.7 constant_dynamic-update-slice_fusion.1
  22.2 0.5 collective-permute-done.3
  22.7 1.1 %constant_dynamic-update-slice_fusion = bf16[128,8192]{1,0:T(8,128)(2,1)} fusion(bf16[128,8192]{1,0:T(8,128)(2,1)} %constant_dynamic-update-slice_fusion.1, bf16[64,8192]{1,0:T(8,128)(2,1)S(1)} %collective-permute-done.3), kind=kLoop, calls=%fused_computation.32 | loop fusion | bytes 2097152 | tf_op jit(solution)/shard_map/concatenate | solution.py:30
  23.8 2.4 %fusion.21 = (f32[128]{0:T(128)S(1)}, f32[128,256]{1,0:T(8,128)S(1)}) fusion(bf16[128,8192]{1,0:T(8,128)(2,1)} %constant_dynamic-update-slice_fusion, bf16[8192,256]{1,0:T(8,128)(2,1)S(1)} %copy-done.1), kind=kOutput, calls=%fused_computation.63 | convolution fusion | flops 536903552 | bytes 6423040 | tf_op jit(solution)/shard_map/dot_general | solution.py:32
  26.3 0.1 broadcast_in_dim.131
  26.3 0.2 exponential_reduce_fusion
  26.7 0.1 select_reduce_fusion.5
  26.8 0.1 stack_reshape.11
  26.9 0.1 stack_reshape.10
  27.0 0.1 stack_reshape.9
  27.1 0.7 broadcast_in_dim.138
  27.8 4.9 %all-to-all-start = ((f32[32,4,128]{2,1,0:T(4,128)}), f32[32,4,128]{2,1,0:T(4,128)S(1)}, u32[]{:S(2)}, u32[]{:S(2)}) async-start(f32[32,4,128]{2,1,0:T(4,128)} %broadcast_in_dim.138), calls=%async_computation | async-start | bytes 131072 | tf_op jit(solution)/shard_map/all_to_all | solution.py:60
  32.7 7.5 %all-to-all-done = f32[32,4,128]{2,1,0:T(4,128)S(1)} async-done(((f32[32,4,128]{2,1,0:T(4,128)}), f32[32,4,128]{2,1,0:T(4,128)S(1)}, u32[]{:S(2)}, u32[]{:S(2)}) %all-to-all-start) | async-done | bytes 65568 | tf_op jit(solution)/shard_map/all_to_all | solution.py:60
  40.4 0.1 reduce_sum.146
  40.5 0.6 select_reduce_fusion.7
  41.1 0.1 select_reduce_fusion.1
  41.2 0.1 sub.60
  41.5 0.1 negate_convert_fusion
  41.6 3.7 %convolution_convert_fusion = bf16[64,8192]{1,0:T(8,128)(2,1)S(1)} fusion(bf16[8192,256]{1,0:T(8,128)(2,1)} %param.4, bf16[128,256]{1,0:T(8,128)(2,1)S(1)} %negate_convert_fusion), kind=kOutput, calls=%fused_computation | convolution fusion | flops 268959744 | bytes 5275648 | tf_op jit(solution)/shard_map/dot_general | solution.py:84
  45.4 2.6 %collective-permute-done.4 = bf16[64,8192]{1,0:T(8,128)(2,1)S(1)} collective-permute-done((bf16[64,8192]{1,0:T(8,128)(2,1)S(1)}, bf16[64,8192]{1,0:T(8,128)(2,1)S(1)}, u32[]{:S(2)}, u32[]{:S(2)}) %collective-permute-start.4) | collective-permute-done | bytes 1048608 | tf_op jit(solution)/shard_map/ppermute | solution.py:10
  48.1 2.7 %fusion.22 = (bf16[64,8192]{1,0:T(8,128)(2,1)S(1)}, f32[64,8192]{1,0:T(8,128)}) fusion(bf16[64,8192]{1,0:T(8,128)(2,1)S(1)} %collective-permute-done.4, bf16[8192,256]{1,0:T(8,128)(2,1)S(1)} %copy-done.2, bf16[128,256]{1,0:T(8,128)(2,1)S(1)} %negate_convert_fusion), kind=kOutput, calls=%fused_computation.64 | convolution fusion | flops 270008320 | bytes 8421376 | tf_op jit(solution)/shard_map/dot_general | solution.py:84
  50.8 0.8 fusion.20
  51.6 0.6 collective-permute-start.7
  52.2 1.5 %collective-permute-start.6 = (bf16[16,8192]{1,0:T(8,128)(2,1)S(1)}, bf16[16,8192]{1,0:T(8,128)(2,1)S(1)}, u32[]{:S(2)}, u32[]{:S(2)}) collective-permute-start(bf16[16,8192]{1,0:T(8,128)(2,1)S(1)} %get-tuple-element.18), channel_id=1, source_target_pairs={{0,16},{4,20},{8,24},{12,28},{16,0},{20,4},{24,8},{28,12},{1,17},{... | collective-permute-start | bytes 786440 | tf_op jit(solution)/shard_map/ppermute | solution.py:10
  53.7 1.4 %collective-permute-start.5 = (bf16[16,8192]{1,0:T(8,128)(2,1)S(1)}, bf16[16,8192]{1,0:T(8,128)(2,1)S(1)}, u32[]{:S(2)}, u32[]{:S(2)}) collective-permute-start(bf16[16,8192]{1,0:T(8,128)(2,1)S(1)} %get-tuple-element.16), channel_id=1, source_target_pairs={{0,8},{4,12},{8,0},{12,4},{16,24},{20,28},{24,16},{28,20},{1,9},{5... | collective-permute-start | bytes 786440 | tf_op jit(solution)/shard_map/ppermute | solution.py:10
  55.1 0.6 slice_reduce_fusion.1
  57.0 4.9 %collective-permute-done.7 = bf16[16,8192]{1,0:T(8,128)(2,1)S(1)} collective-permute-done((bf16[16,8192]{1,0:T(8,128)(2,1)}, bf16[16,8192]{1,0:T(8,128)(2,1)S(1)}, u32[]{:S(2)}, u32[]{:S(2)}) %collective-permute-start.7) | collective-permute-done | bytes 262176 | tf_op jit(solution)/shard_map/ppermute | solution.py:10
  61.9 4.0 %collective-permute-done.6 = bf16[16,8192]{1,0:T(8,128)(2,1)S(1)} collective-permute-done((bf16[16,8192]{1,0:T(8,128)(2,1)S(1)}, bf16[16,8192]{1,0:T(8,128)(2,1)S(1)}, u32[]{:S(2)}, u32[]{:S(2)}) %collective-permute-start.6) | collective-permute-done | bytes 262176 | tf_op jit(solution)/shard_map/ppermute | solution.py:10
  65.9 1.1 %fusion.1 = f32[16,8192]{1,0:T(8,128)S(1)} fusion(f32[64,8192]{1,0:T(8,128)} %get-tuple-element.27, bf16[16,8192]{1,0:T(8,128)(2,1)S(1)} %collective-permute-done.7, bf16[16,8192]{1,0:T(8,128)(2,1)S(1)} %collective-permute-done.6, bf16[16,8192]{1,0:T(8,128)(2,1)S(1)} %collective-permute-done.5), kind=kLoop, calls=%fused_computation.7 | loop fusion | flops 786432 | bytes 1835008 | tf_op jit(solution)/shard_map/add | solution.py:91
  67.1 0.9 %collective-permute-start.10 = (bf16[16,2048]{1,0:T(8,128)(2,1)S(1)}, bf16[16,2048]{1,0:T(8,128)(2,1)S(1)}, u32[]{:S(2)}, u32[]{:S(2)}) collective-permute-start(bf16[16,2048]{1,0:T(8,128)(2,1)S(1)} %get-tuple-element.20), channel_id=1, source_target_pairs={{0,3},{1,2},{2,1},{3,0},{4,7},{5,6},{6,5},{7,4},{8,11},{9,10},{10,... | collective-permute-start | bytes 196616 | tf_op jit(solution)/shard_map/ppermute | solution.py:10
  68.0 1.0 %collective-permute-start.9 = (bf16[16,2048]{1,0:T(8,128)(2,1)S(1)}, bf16[16,2048]{1,0:T(8,128)(2,1)S(1)}, u32[]{:S(2)}, u32[]{:S(2)}) collective-permute-start(bf16[16,2048]{1,0:T(8,128)(2,1)S(1)} %get-tuple-element.21), channel_id=1, source_target_pairs={{0,2},{1,3},{2,0},{3,1},{4,6},{5,7},{6,4},{7,5},{8,10},{9,11},{10,... | collective-permute-start | bytes 196616 | tf_op jit(solution)/shard_map/ppermute | solution.py:10
  68.9 2.6 %collective-permute-start.8 = (bf16[16,2048]{1,0:T(8,128)(2,1)S(1)}, bf16[16,2048]{1,0:T(8,128)(2,1)S(1)}, u32[]{:S(2)}, u32[]{:S(2)}) collective-permute-start(bf16[16,2048]{1,0:T(8,128)(2,1)S(1)} %get-tuple-element.19), channel_id=1, source_target_pairs={{0,1},{1,0},{2,3},{3,2},{4,5},{5,4},{6,7},{7,6},{8,9},{9,8},{10,11... | collective-permute-start | bytes 196616 | tf_op jit(solution)/shard_map/ppermute | solution.py:10
  71.5 0.6 select_reduce_fusion.6
  72.1 1.6 %collective-permute-done.10 = bf16[16,2048]{1,0:T(8,128)(2,1)S(1)} collective-permute-done((bf16[16,2048]{1,0:T(8,128)(2,1)S(1)}, bf16[16,2048]{1,0:T(8,128)(2,1)S(1)}, u32[]{:S(2)}, u32[]{:S(2)}) %collective-permute-start.10) | collective-permute-done | bytes 65568 | tf_op jit(solution)/shard_map/ppermute | solution.py:10
  73.8 1.6 %collective-permute-done.9 = bf16[16,2048]{1,0:T(8,128)(2,1)S(1)} collective-permute-done((bf16[16,2048]{1,0:T(8,128)(2,1)S(1)}, bf16[16,2048]{1,0:T(8,128)(2,1)S(1)}, u32[]{:S(2)}, u32[]{:S(2)}) %collective-permute-start.9) | collective-permute-done | bytes 65568 | tf_op jit(solution)/shard_map/ppermute | solution.py:10
  75.4 1.1 %convolution_convert_fusion.2 = bf16[128,2048]{1,0:T(8,128)(2,1)} fusion(bf16[16,2048]{1,0:T(8,128)(2,1)S(1)} %collective-permute-done.10, bf16[16,2048]{1,0:T(8,128)(2,1)S(1)} %collective-permute-done.9, bf16[16,2048]{1,0:T(8,128)(2,1)S(1)} %collective-permute-done.8, f32[16,8192]{1,0:T(8,128)S(1)} %fusion.1, s32[]{:T(128)S(6)} %select_n.75, ...), kind=kOutput, calls=%fused_computation.2 | convolution fusion | flops 8884224 | bytes 852996 | tf_op jit(solution)/shard_map/dot_general | solution.py:102
  (34 shorter events, 1.1 us)
Async XLA Ops:
  0.6 1.9 %copy-start = (bf16[128,8192]{1,0:T(8,128)(2,1)S(1)}, bf16[128,8192]{1,0:T(8,128)(2,1)}, u32[]{:S(2)}) copy-start(bf16[128,8192]{1,0:T(8,128)(2,1)} %param.3) | copy-start | bytes 6291460
  0.6 7.4 %copy-start.3 = (s32[128]{0:T(128)S(1)}, s32[128]{0:T(128)}, u32[]{:S(2)}) copy-start(s32[128]{0:T(128)} %param.5) | copy-start | bytes 1540
  3.6 10.1 %collective-permute-start = (bf16[16,8192]{1,0:T(8,128)(2,1)S(1)}, bf16[16,8192]{1,0:T(8,128)(2,1)S(1)}, u32[]{:S(2)}, u32[]{:S(2)}) collective-permute-start(bf16[16,8192]{1,0:T(8,128)(2,1)S(1)} %get-tuple-element.23), channel_id=1, source_target_pairs={{0,8},{4,12},{8,0},{12,4},{16,24},{20,28},{24,16},{28,20},{1,9},{5... | collective-permute-start | bytes 786440 | tf_op jit(solution)/shard_map/ppermute | solution.py:10
  6.5 13.4 %collective-permute-start.1 = (bf16[16,8192]{1,0:T(8,128)(2,1)S(1)}, bf16[16,8192]{1,0:T(8,128)(2,1)S(1)}, u32[]{:S(2)}, u32[]{:S(2)}) collective-permute-start(bf16[16,8192]{1,0:T(8,128)(2,1)S(1)} %get-tuple-element.23), channel_id=1, source_target_pairs={{0,16},{4,20},{8,24},{12,28},{16,0},{20,4},{24,8},{28,12},{1,17},{... | collective-permute-start | bytes 786440 | tf_op jit(solution)/shard_map/ppermute | solution.py:10
  8.1 11.9 %collective-permute-start.2 = (bf16[16,8192]{1,0:T(8,128)(2,1)S(1)}, bf16[16,8192]{1,0:T(8,128)(2,1)S(1)}, u32[]{:S(2)}, u32[]{:S(2)}) collective-permute-start(bf16[16,8192]{1,0:T(8,128)(2,1)S(1)} %get-tuple-element.23), channel_id=1, source_target_pairs={{0,24},{4,28},{8,16},{12,20},{16,8},{20,12},{24,0},{28,4},{1,25},{... | collective-permute-start | bytes 786440 | tf_op jit(solution)/shard_map/ppermute | solution.py:10
  19.9 3.9 %copy-start.1 = (bf16[8192,256]{1,0:T(8,128)(2,1)S(1)}, bf16[8192,256]{1,0:T(8,128)(2,1)}, u32[]{:S(2)}) copy-start(bf16[8192,256]{1,0:T(8,128)(2,1)} %param.4) | copy-start | bytes 12582916
  20.0 2.7 %collective-permute-start.3 = (bf16[64,8192]{1,0:T(8,128)(2,1)S(1)}, bf16[64,8192]{1,0:T(8,128)(2,1)S(1)}, u32[]{:S(2)}, u32[]{:S(2)}) collective-permute-start(bf16[64,8192]{1,0:T(8,128)(2,1)S(1)} %pad_maximum_fusion), channel_id=1, source_target_pairs={{0,4},{4,0},{8,12},{12,8},{16,20},{20,16},{24,28},{28,24},{1,5},{5... | collective-permute-start | bytes 3145736 | tf_op jit(solution)/shard_map/ppermute | solution.py:10
  27.8 12.4 %all-to-all-start = ((f32[32,4,128]{2,1,0:T(4,128)}), f32[32,4,128]{2,1,0:T(4,128)S(1)}, u32[]{:S(2)}, u32[]{:S(2)}) async-start(f32[32,4,128]{2,1,0:T(4,128)} %broadcast_in_dim.138), calls=%async_computation | async-start | bytes 131072 | tf_op jit(solution)/shard_map/all_to_all | solution.py:60
  41.6 6.5 %copy-start.2 = (bf16[8192,256]{1,0:T(8,128)(2,1)S(1)}, bf16[8192,256]{1,0:T(8,128)(2,1)}, u32[]{:S(2)}) copy-start(bf16[8192,256]{1,0:T(8,128)(2,1)} %param.4) | copy-start | bytes 12582916
  45.4 2.7 %collective-permute-start.4 = (bf16[64,8192]{1,0:T(8,128)(2,1)S(1)}, bf16[64,8192]{1,0:T(8,128)(2,1)S(1)}, u32[]{:S(2)}, u32[]{:S(2)}) collective-permute-start(bf16[64,8192]{1,0:T(8,128)(2,1)S(1)} %convolution_convert_fusion), channel_id=1, source_target_pairs={{0,4},{4,0},{8,12},{12,8},{16,20},{20,16},{24,28},{28,24},{1,5},{5... | collective-permute-start | bytes 3145736 | tf_op jit(solution)/shard_map/ppermute | solution.py:10
  51.6 10.3 %collective-permute-start.7 = (bf16[16,8192]{1,0:T(8,128)(2,1)}, bf16[16,8192]{1,0:T(8,128)(2,1)S(1)}, u32[]{:S(2)}, u32[]{:S(2)}) collective-permute-start(bf16[16,8192]{1,0:T(8,128)(2,1)} %get-tuple-element.17), channel_id=1, source_target_pairs={{0,24},{4,28},{8,16},{12,20},{16,8},{20,12},{24,0},{28,4},{1,25},{... | collective-permute-start | bytes 786440 | tf_op jit(solution)/shard_map/ppermute | solution.py:10
  52.2 13.7 %collective-permute-start.6 = (bf16[16,8192]{1,0:T(8,128)(2,1)S(1)}, bf16[16,8192]{1,0:T(8,128)(2,1)S(1)}, u32[]{:S(2)}, u32[]{:S(2)}) collective-permute-start(bf16[16,8192]{1,0:T(8,128)(2,1)S(1)} %get-tuple-element.18), channel_id=1, source_target_pairs={{0,16},{4,20},{8,24},{12,28},{16,0},{20,4},{24,8},{28,12},{1,17},{... | collective-permute-start | bytes 786440 | tf_op jit(solution)/shard_map/ppermute | solution.py:10
  53.7 12.2 %collective-permute-start.5 = (bf16[16,8192]{1,0:T(8,128)(2,1)S(1)}, bf16[16,8192]{1,0:T(8,128)(2,1)S(1)}, u32[]{:S(2)}, u32[]{:S(2)}) collective-permute-start(bf16[16,8192]{1,0:T(8,128)(2,1)S(1)} %get-tuple-element.16), channel_id=1, source_target_pairs={{0,8},{4,12},{8,0},{12,4},{16,24},{20,28},{24,16},{28,20},{1,9},{5... | collective-permute-start | bytes 786440 | tf_op jit(solution)/shard_map/ppermute | solution.py:10
  67.1 6.7 %collective-permute-start.10 = (bf16[16,2048]{1,0:T(8,128)(2,1)S(1)}, bf16[16,2048]{1,0:T(8,128)(2,1)S(1)}, u32[]{:S(2)}, u32[]{:S(2)}) collective-permute-start(bf16[16,2048]{1,0:T(8,128)(2,1)S(1)} %get-tuple-element.20), channel_id=1, source_target_pairs={{0,3},{1,2},{2,1},{3,0},{4,7},{5,6},{6,5},{7,4},{8,11},{9,10},{10,... | collective-permute-start | bytes 196616 | tf_op jit(solution)/shard_map/ppermute | solution.py:10
  68.0 7.4 %collective-permute-start.9 = (bf16[16,2048]{1,0:T(8,128)(2,1)S(1)}, bf16[16,2048]{1,0:T(8,128)(2,1)S(1)}, u32[]{:S(2)}, u32[]{:S(2)}) collective-permute-start(bf16[16,2048]{1,0:T(8,128)(2,1)S(1)} %get-tuple-element.21), channel_id=1, source_target_pairs={{0,2},{1,3},{2,0},{3,1},{4,6},{5,7},{6,4},{7,5},{8,10},{9,11},{10,... | collective-permute-start | bytes 196616 | tf_op jit(solution)/shard_map/ppermute | solution.py:10
  68.9 6.4 %collective-permute-start.8 = (bf16[16,2048]{1,0:T(8,128)(2,1)S(1)}, bf16[16,2048]{1,0:T(8,128)(2,1)S(1)}, u32[]{:S(2)}, u32[]{:S(2)}) collective-permute-start(bf16[16,2048]{1,0:T(8,128)(2,1)S(1)} %get-tuple-element.19), channel_id=1, source_target_pairs={{0,1},{1,0},{2,3},{3,2},{4,5},{5,4},{6,7},{7,6},{8,9},{9,8},{10,11... | collective-permute-start | bytes 196616 | tf_op jit(solution)/shard_map/ppermute | solution.py:10

commit v2 on v0

v2 whole, which is shorter than its diff:
```python
import functools

import jax
import jax.numpy as jnp
from jax import lax
from jax.experimental import pallas as pl
from jax.experimental.pallas import tpu as pltpu
from jax.sharding import PartitionSpec as P

ACT_DEV = 16
VMEM_BYTES = 16 * 2**20
F32, BF16 = jnp.float32, jnp.bfloat16


def params():
    return pltpu.CompilerParams(vmem_limit_bytes=VMEM_BYTES)


def iota(shape, axis):
    return lax.broadcasted_iota(jnp.int32, shape, axis)


def turn(bits, index):
    return sum(((index >> b) & 1) << (bits - 1 - b) for b in range(bits))


def owner_of(n_seq, core, chip):
    me = lax.axis_index("seq")
    bits = (n_seq // 2).bit_length() - 1
    odd = (me & 1) ^ core
    return me ^ (jnp.where(odd == 1, turn(bits, chip), chip) * 2 + core)


def select_kernel(mask_ref, hidden_ref, own_ref, picker_ref):
    tokens = mask_ref.shape[1]
    mask = mask_ref[...]
    upper = (iota((tokens, tokens), 0) <= iota((tokens, tokens), 1)).astype(BF16)
    ones = jnp.broadcast_to(mask.astype(F32).astype(BF16), (ACT_DEV, tokens))
    slots = jnp.dot(ones, upper, preferred_element_type=F32).astype(jnp.int32) - 1
    picker = (slots == iota((ACT_DEV, tokens), 0)) & (mask == 1)
    picker = picker.astype(F32).astype(BF16)
    picker_ref[...] = picker
    own_ref[...] = jnp.dot(picker, hidden_ref[...], preferred_element_type=F32).astype(BF16)


def select(mask, hidden):
    tokens, width = hidden.shape
    step = width // 4
    return pl.pallas_call(
        select_kernel,
        grid=(width // step,),
        in_specs=[
            pl.BlockSpec((1, tokens), lambda i: (0, 0)),
            pl.BlockSpec((tokens, step), lambda i: (0, i)),
        ],
        out_specs=[
            pl.BlockSpec((ACT_DEV, step), lambda i: (0, i)),
            pl.BlockSpec((ACT_DEV, tokens), lambda i: (0, 0)),
        ],
        out_shape=[
            jax.ShapeDtypeStruct((ACT_DEV, width), BF16),
            jax.ShapeDtypeStruct((ACT_DEV, tokens), BF16),
        ],
        compiler_params=params(),
        name="select_rows",
    )(mask.reshape(1, tokens), hidden)


def logits_kernel(
    n_seq, near_ref, far_ref, head_ref, picker_ref, logits_ref, stats_ref, total, packed
):
    step = pl.program_id(0)
    rows = jnp.concatenate([near_ref[...], far_ref[...]], axis=0)
    part = jnp.dot(rows, head_ref[...], preferred_element_type=F32)

    @pl.when(step == 0)
    def _():
        total[...] = part

    @pl.when(step > 0)
    def _():
        total[...] += part

    @pl.when(step == pl.num_programs(0) - 1)
    def _():
        logits = total[...]
        logits_ref[...] = logits
        top = jnp.max(logits, axis=1, keepdims=True)
        away = logits - top
        ex = jnp.exp(away)
        sums = jnp.sum(ex, axis=1, keepdims=True)
        weighted = jnp.sum(ex * away, axis=1, keepdims=True)
        count = jnp.sum(picker_ref[...].astype(F32))
        lane = iota((logits.shape[0], 128), 1)
        pack = jnp.where(lane == 0, top, jnp.where(lane == 1, sums, weighted))
        pack = jnp.where(lane == 3, count, pack)
        n_chip = n_seq // 2
        for q in range(n_seq):
            place = pl.multiple_of(owner_of(n_seq, q // n_chip, q % n_chip) * ACT_DEV, ACT_DEV)
            packed[pl.ds(place, ACT_DEV), :] = pack[q * ACT_DEV : (q + 1) * ACT_DEV]
        rows8 = packed[...].T[:8]
        stats_ref[...] = jnp.broadcast_to(rows8[None], stats_ref.shape)


def local_logits(n_seq, n_vocab, near, far, head, picker):
    half, width = near.shape
    shard = head.shape[1]
    step = width // 8
    rows = 2 * half
    return pl.pallas_call(
        functools.partial(logits_kernel, n_seq),
        grid=(width // step,),
        in_specs=[
            pl.BlockSpec((half, step), lambda i: (0, i)),
            pl.BlockSpec((half, step), lambda i: (0, i)),
            pl.BlockSpec((step, shard), lambda i: (i, 0)),
            pl.BlockSpec(picker.shape, lambda i: (0, 0)),
        ],
        out_specs=[
            pl.BlockSpec((rows, shard), lambda i: (0, 0)),
            pl.BlockSpec((n_vocab, 8, rows), lambda i: (0, 0, 0)),
        ],
        out_shape=[
            jax.ShapeDtypeStruct((rows, shard), F32),
            jax.ShapeDtypeStruct((n_vocab, 8, rows), F32),
        ],
        scratch_shapes=[pltpu.VMEM((rows, shard), F32), pltpu.VMEM((rows, 128), F32)],
        compiler_params=params(),
        name="local_logits",
    )(near, far, head, picker)


def merged(stats):
    tops, sums, weights = stats[:, 0], stats[:, 1], stats[:, 2]
    top = jnp.max(tops, axis=0, keepdims=True)
    offset = tops - top
    scale = jnp.exp(offset)
    total = jnp.sum(scale * sums, axis=0, keepdims=True)
    weighted = jnp.sum(scale * (weights + offset * sums), axis=0, keepdims=True)
    return top, total, weighted


def stack_rows(top, total, weighted, other):
    row = iota((8, top.shape[1]), 0)
    low = jnp.where(row == 0, top, total)
    high = jnp.where(row == 2, weighted, other)
    return jnp.where(row < 2, low, high)


def merge_kernel(stats_ref, out_ref):
    stats = stats_ref[...]
    top, total, weighted = merged(stats)
    out_ref[...] = jnp.broadcast_to(
        stack_rows(top, total, weighted, stats[0, 3:4])[None], out_ref.shape
    )


def merge(stats, copies):
    return pl.pallas_call(
        merge_kernel,
        out_shape=jax.ShapeDtypeStruct((copies,) + stats.shape[1:], F32),
        compiler_params=params(),
        name="merge_stats",
    )(stats)


def entropy_kernel(stats_ref, picker_ref, each_ref, average_ref, column):
    stats = stats_ref[...]
    n_seq, _, rows = stats.shape
    top, total, weighted = merged(stats)
    entropy = jnp.log(total) - weighted / total
    block = iota((n_seq, rows), 1) // ACT_DEV
    counts = jnp.where(block == iota((n_seq, rows), 0), stats[:, 3], 0.0)
    counts = jnp.sum(counts, axis=0, keepdims=True)
    valid = (iota((1, rows), 1) % ACT_DEV).astype(F32) < counts
    sums = jnp.sum(jnp.where(valid, entropy, 0.0), axis=1, keepdims=True)
    average_ref[...] = sums / jnp.sum(valid.astype(F32), axis=1, keepdims=True)
    column[...] = jnp.broadcast_to(entropy, (128, rows)).T
    place = pl.multiple_of(lax.axis_index("seq") * ACT_DEV, ACT_DEV)
    mine = column[pl.ds(place, ACT_DEV), :][:, :1]
    each_ref[...] = jnp.sum(
        jnp.where(picker_ref[...].astype(F32) > 0.5, mine, 0.0), axis=0, keepdims=True
    )


def entropies(stats, picker):
    tokens = picker.shape[1]
    return pl.pallas_call(
        entropy_kernel,
        out_shape=[
            jax.ShapeDtypeStruct((1, tokens), F32),
            jax.ShapeDtypeStruct((1, 1), F32),
        ],
        scratch_shapes=[pltpu.VMEM((stats.shape[2], 128), F32)],
        compiler_params=params(),
        name="entropies",
    )(stats, picker)


def gradient_kernel(n_seq, stats_ref, logits_ref, head_ref, near_ref, far_ref, columns, ordered, score):
    n_chip = n_seq // 2

    @pl.when(pl.program_id(0) == 0)
    def _():
        top, total, weighted = merged(stats_ref[...])
        rows = top.shape[1]
        mean = top + weighted / total
        lines = stack_rows(top, 1.0 / total, mean, mean)
        columns[...] = jnp.concatenate([lines] * 16, axis=0).T
        for q in range(n_seq):
            place = pl.multiple_of(owner_of(n_seq, q // n_chip, q % n_chip) * ACT_DEV, ACT_DEV)
            ordered[q * ACT_DEV : (q + 1) * ACT_DEV] = columns[pl.ds(place, ACT_DEV), :]
        logits = logits_ref[...]
        prob = jnp.exp(logits - ordered[:, 0:1]) * ordered[:, 1:2]
        score[...] = (prob * (ordered[:, 2:3] - logits)).astype(BF16)

    part = lax.dot_general(
        score[...], head_ref[...], (((1,), (1,)), ((), ())), preferred_element_type=F32
    ).astype(BF16)
    shape = near_ref.shape
    half = n_chip * ACT_DEV
    near_ref[...] = part[:half].reshape(shape)
    far_ref[...] = part[half:].reshape(shape)


def gradients(n_seq, n_vocab, stats, logits, head):
    rows, shard = logits.shape
    width = head.shape[0]
    wide = width // n_vocab
    n_chip = n_seq // 2
    out = jax.ShapeDtypeStruct((n_chip, n_vocab, ACT_DEV, wide), BF16)
    out_spec = pl.BlockSpec((n_chip, 1, ACT_DEV, wide), lambda i: (0, i, 0, 0))
    return pl.pallas_call(
        functools.partial(gradient_kernel, n_seq),
        grid=(n_vocab,),
        in_specs=[
            pl.BlockSpec(stats.shape, lambda i: (0, 0, 0)),
            pl.BlockSpec(logits.shape, lambda i: (0, 0)),
            pl.BlockSpec((wide, shard), lambda i: (i, 0)),
        ],
        out_specs=[out_spec, out_spec],
        out_shape=[out, out],
        scratch_shapes=[
            pltpu.VMEM((rows, 128), F32),
            pltpu.VMEM((rows, 128), F32),
            pltpu.VMEM((rows, shard), BF16),
        ],
        compiler_params=params(),
        name="gradients",
    )(stats, logits, head)


def body(n_seq, n_vocab, hidden, head, mask):
    n_chip = n_seq // 2
    bits = n_chip.bit_length() - 1

    def swap_core(value):
        return lax.ppermute(value, "seq", [(i, i ^ 1) for i in range(n_seq)])

    def swap_chip(value, step):
        flips = (2 << step, 2 << (bits - 1 - step))
        return lax.ppermute(value, "seq", [(i, i ^ flips[i & 1]) for i in range(n_seq)])

    own, picker = select(mask, hidden)

    blocks = [own]
    for a in range(1, n_chip):
        step = a.bit_length() - 1
        blocks.append(swap_chip(blocks[a ^ (1 << step)], step))
    near = jnp.concatenate(blocks, axis=0)
    far = swap_core(near)

    logits, stats = local_logits(n_seq, n_vocab, near, far, head, picker)
    stats = lax.all_to_all(stats, "vocab", 0, 0, tiled=True)
    stats = merge(stats, n_seq)
    stats = lax.all_to_all(stats, "seq", 0, 0, tiled=True)

    near, far = gradients(n_seq, n_vocab, stats, logits, head)
    each, average = entropies(stats, picker)

    here = near.astype(F32) + swap_core(far).astype(F32)
    sums = [here[a] for a in range(n_chip)]
    for a in range(n_chip - 1, 0, -1):
        step = a.bit_length() - 1
        moved = swap_chip(sums[a].astype(BF16), step)
        sums[a ^ (1 << step)] += moved.astype(F32)
    parts = lax.all_to_all(sums[0].astype(BF16), "vocab", 0, 0, tiled=True)
    result = jnp.sum(parts.astype(F32), axis=0).astype(BF16)
    derivative = lax.dot_general(
        picker, result, (((0,), (0,)), ((), ())), preferred_element_type=F32
    ).astype(BF16)
    return each.reshape(-1), average.reshape(()), derivative


def solution(mesh):
    n_seq, n_vocab = mesh.shape["seq"], mesh.shape["vocab"]

    def run(hidden, head, mask):
        return body(n_seq, n_vocab, hidden, head, mask)

    return jax.shard_map(
        run,
        mesh=mesh,
        in_specs=(P("seq", None), P(None, ("seq", "vocab")), P("seq")),
        out_specs=(P("seq"), P(), P("seq", "vocab")),
        check_vma=False,
    )
```

time: 204 us -> 76.8 us (0.38)
  blocking collectives: 93.7 us -> 18.8 us
  waiting for transfers between devices: 77.5 us -> 32.7 us
  between operations: 16.3 us -> 0.74 us
  starting transfers between devices: 0.12 us -> 12.5 us
  matrix products: 13 us -> 1.12 us
  Pallas kernels: 0 us -> 6.98 us
    psum x2 -> x0, blocking collectives: 54.3 us -> none  [the longest x1 41 us: body(): lax.psum((jnp.sum(ex, axis=1), jnp.sum(ex * logits, axis=1)), ('seq', 'vo...]
    reduce_scatter x2 -> x0, waiting for transfers between devices: 46.6 us -> none  [the longest x1 41.1 us: body(): lax.psum_scatter(lax.dot_general(score_grad, head, (((1,), (1,)), ((), ()...]
    pmax x1 -> x0, blocking collectives: 39.4 us -> none  [body(): top = lax.pmax(local_top, ('seq', 'vocab'))]
    all_gather x1 -> x0, waiting for transfers between devices: 30.9 us -> none  [body(): lax.all_gather(source, 'seq', axis=0, tiled=True)]
    ppermute x0 -> x8, waiting for transfers between devices: none -> 25 us  [the longest x6 19.7 us: swap_chip(): lax.ppermute(value, 'seq', [(i, i ^ flips[i & 1]) for i in range(n_seq)])]
    all_to_all x0 -> x2, blocking collectives: none -> 18.8 us  [the longest x1 10.5 us: body(): stats = lax.all_to_all(stats, 'vocab', 0, 0, tiled=True)]
    dot_general x5 -> x1, matrix products: 13 us -> 1.12 us  [body(): lax.dot_general(picker, result, (((0,), (0,)), ((), ())), preferred_eleme...]
    ppermute x0 -> x8, starting transfers between devices: none -> 9.05 us  [the longest x6 8.91 us: swap_chip(): lax.ppermute(value, 'seq', [(i, i ^ flips[i & 1]) for i in range(n_seq)])]
  transfers between devices with their start and end apart: 3 -> 9, of which waited for: 3 -> 8; matrix products, arithmetic and copies ran while one was open for 1% -> 0% of each run, Pallas kernels for 0% -> 1%
where the time goes in v2:
time: 76.8 us; the launch traced here: 76.5 us
  waiting for transfers between devices  32.7 us (43%)
  blocking collectives  18.8 us (24%)
  starting transfers between devices  12.5 us (16%)
  Pallas kernels  6.98 us (9%)
  local copies, waits for them, and re-layouts  2.35 us (3%)
  other arithmetic  1.34 us (2%)
  matrix products  1.12 us (1%)
    ppermute x6, waiting for transfers between devices, swap_chip(): lax.ppermute(value, 'seq', [(i, i ^ flips[i & 1]) for i in range(n_seq)])  19.7 us
    all_to_all x1, blocking collectives, body(): stats = lax.all_to_all(stats, 'vocab', 0, 0, tiled=True)  10.5 us
    ppermute x6, starting transfers between devices, swap_chip(): lax.ppermute(value, 'seq', [(i, i ^ flips[i & 1]) for i in range(n_seq)])  8.91 us
    all_to_all x1, blocking collectives, body(): stats = lax.all_to_all(stats, 'seq', 0, 0, tiled=True)  8.36 us
    all_to_all x1, waiting for transfers between devices, body(): parts = lax.all_to_all(sums[0].astype(BF16), 'vocab', 0, 0, tiled=True)  7.76 us
    ppermute x2, waiting for transfers between devices, swap_core(): return lax.ppermute(value, 'seq', [(i, i ^ 1) for i in range(n_seq)])  5.29 us
    all_to_all x1, starting transfers between devices, body(): parts = lax.all_to_all(sums[0].astype(BF16), 'vocab', 0, 0, tiled=True)  3.41 us
    pallas_call x1, Pallas kernels, local_logits(): pl.pallas_call(functools.partial(logits_kernel, n_seq), grid=(width // st...  2.5 us
  transfers between devices with their start and end apart: 9, of which 8 were waited for; matrix products, arithmetic and copies ran while one was open for 0% of the time, Pallas kernels for 1%

profile of v2, /device:TPU:0, one launch (start us, length us, event | category | flops | bytes accessed | tf_op | source)
XLA Modules:
  0.0 76.5 jit_solution(15119288685810246665)
XLA Ops:
  0.6 0.0 copy-start.1
  0.6 1.6 %copy-done.1 = bf16[128,8192]{1,0:T(8,128)(2,1)S(1)} copy-done((bf16[128,8192]{1,0:T(8,128)(2,1)S(1)}, bf16[128,8192]{1,0:T(8,128)(2,1)}, u32[]{:S(2)}) %copy-start.1) | copy-done | bytes 2097176
  2.2 0.0 copy-start.2
  2.2 0.7 copy-done.2
  2.9 0.0 copy-start
  2.9 1.4 %select_rows.1 = (bf16[16,8192]{1,0:T(8,128)(2,1)S(1)}, bf16[16,128]{1,0:T(8,128)(2,1)S(1)}) custom-call(s32[1,128]{1,0:T(1,128)S(1)} %bitcast.23, bf16[128,8192]{1,0:T(8,128)(2,1)S(1)} %copy-done.1), custom_call_target="tpu_custom_call" | custom-call | tf_op jit(solution)/shard_map/select_rows/pallas_call | solution.py:49
  4.3 3.0 %collective-permute-start.1 = (bf16[16,8192]{1,0:T(8,128)(2,1)S(1)}, bf16[16,8192]{1,0:T(8,128)(2,1)S(1)}, u32[]{:S(2)}, u32[]{:S(2)}) collective-permute-start(bf16[16,8192]{1,0:T(8,128)(2,1)S(1)} %get-tuple-element.11), channel_id=1, source_target_pairs={{0,16},{4,12},{8,24},{12,4},{16,0},{20,28},{24,8},{28,20},{1,17},{... | collective-permute-start | bytes 786440 | tf_op jit(solution)/shard_map/ppermute | solution.py:262
  7.3 1.5 %collective-permute-start = (bf16[16,8192]{1,0:T(8,128)(2,1)S(1)}, bf16[16,8192]{1,0:T(8,128)(2,1)S(1)}, u32[]{:S(2)}, u32[]{:S(2)}) collective-permute-start(bf16[16,8192]{1,0:T(8,128)(2,1)S(1)} %get-tuple-element.11), channel_id=1, source_target_pairs={{0,8},{4,20},{8,0},{12,28},{16,24},{20,4},{24,16},{28,12},{1,9},{5... | collective-permute-start | bytes 786440 | tf_op jit(solution)/shard_map/ppermute | solution.py:262
  8.8 4.9 %collective-permute-done = bf16[16,8192]{1,0:T(8,128)(2,1)S(1)} collective-permute-done((bf16[16,8192]{1,0:T(8,128)(2,1)S(1)}, bf16[16,8192]{1,0:T(8,128)(2,1)S(1)}, u32[]{:S(2)}, u32[]{:S(2)}) %collective-permute-start) | collective-permute-done | bytes 262176 | tf_op jit(solution)/shard_map/ppermute | solution.py:262
  13.7 1.7 %collective-permute-start.2 = (bf16[16,8192]{1,0:T(8,128)(2,1)S(1)}, bf16[16,8192]{1,0:T(8,128)(2,1)S(1)}, u32[]{:S(2)}, u32[]{:S(2)}) collective-permute-start(bf16[16,8192]{1,0:T(8,128)(2,1)S(1)} %collective-permute-done), channel_id=1, source_target_pairs={{0,16},{4,12},{8,24},{12,4},{16,0},{20,28},{24,8},{28,20},{1,17},{... | collective-permute-start | bytes 786440 | tf_op jit(solution)/shard_map/ppermute | solution.py:262
  15.4 0.0 collective-permute-done.1
  15.4 4.6 %collective-permute-done.2 = bf16[16,8192]{1,0:T(8,128)(2,1)S(1)} collective-permute-done((bf16[16,8192]{1,0:T(8,128)(2,1)S(1)}, bf16[16,8192]{1,0:T(8,128)(2,1)S(1)}, u32[]{:S(2)}, u32[]{:S(2)}) %collective-permute-start.2) | collective-permute-done | bytes 262176 | tf_op jit(solution)/shard_map/ppermute | solution.py:262
  20.1 0.1 collective-permute-start.3
  20.2 2.6 %collective-permute-done.3.far_ref = bf16[64,8192]{1,0:T(8,128)(2,1)S(1)} collective-permute-done((bf16[64,8192]{1,0:T(8,128)(2,1)S(1)}, bf16[64,8192]{1,0:T(8,128)(2,1)S(1)}, u32[]{:S(2)}, u32[]{:S(2)}) %collective-permute-start.3) | collective-permute-done | bytes 1048608 | tf_op jit(solution)/shard_map/ppermute | solution.py:258
  22.8 0.0 copy-done
  22.8 2.5 %local_logits.1 = (f32[128,256]{1,0:T(8,128)S(1)}, f32[4,8,128]{2,1,0:T(8,128)S(1)}) custom-call(bf16[64,8192]{1,0:T(8,128)(2,1)S(1)} %constant_dynamic-update-slice_fusion.near_ref, bf16[64,8192]{1,0:T(8,128)(2,1)S(1)} %collective-permute-done.3.far_ref, bf16[8192,256]{1,0:T(8,128)(2,1)S(1)} %copy-done, bf16[16,128]{1,0:T(8,128)(2,1)S(1)} %get-tuple-element.12.picker_ref), custom_call_target="tpu_custom_call" | custom-call | tf_op jit(solution)/shard_map/local_logits/pallas_call | solution.py:110
  25.3 10.5 %all_to_all.15.stats_ref = f32[4,8,128]{2,1,0:T(8,128)S(1)} all-to-all(f32[4,8,128]{2,1,0:T(8,128)S(1)} %get-tuple-element.13), channel_id=1, replica_groups=mesh['seq'=8,'vocab'=4] {'vocab'}, dimensions={0} | all-to-all | bytes 32768 | tf_op jit(solution)/shard_map/all_to_all | solution.py:274
  35.8 8.4 %all_to_all.16.stats_ref = f32[8,8,128]{2,1,0:T(8,128)S(1)} all-to-all(f32[8,8,128]{2,1,0:T(8,128)S(1)} %merge_stats.1), channel_id=1, replica_groups=mesh['seq'=8,'vocab'=4] {'seq'}, dimensions={0} | all-to-all | bytes 65536 | tf_op jit(solution)/shard_map/all_to_all | solution.py:276
  44.2 2.3 %gradients.1 = (bf16[4,4,16,2048]{3,2,1,0:T(8,128)(2,1)S(1)}, bf16[4,4,16,2048]{3,2,1,0:T(8,128)(2,1)S(1)}) custom-call(f32[8,8,128]{2,1,0:T(8,128)S(1)} %all_to_all.16.stats_ref, f32[128,256]{1,0:T(8,128)S(1)} %get-tuple-element.16.logits_ref, bf16[8192,256]{1,0:T(8,128)(2,1)S(1)} %copy-done), custom_call_target="tpu_custom_call" | custom-call | tf_op jit(solution)/shard_map/gradients/pallas_call | solution.py:233
  46.5 0.1 collective-permute-start.4
  46.6 2.6 %collective-permute-done.4 = bf16[4,4,16,2048]{3,2,1,0:T(8,128)(2,1)S(1)} collective-permute-done((bf16[4,4,16,2048]{3,2,1,0:T(8,128)(2,1)S(1)}, bf16[4,4,16,2048]{3,2,1,0:T(8,128)(2,1)S(1)}, u32[]{:S(2)}, u32[]{:S(2)}) %collective-permute-start.4) | collective-permute-done | bytes 1048608 | tf_op jit(solution)/shard_map/ppermute | solution.py:258
  49.2 0.4 fusion.5
  49.7 0.6 collective-permute-start.6
  50.3 1.5 %collective-permute-start.5 = (bf16[4,16,2048]{2,1,0:T(8,128)(2,1)S(1)}, bf16[4,16,2048]{2,1,0:T(8,128)(2,1)S(1)}, u32[]{:S(2)}, u32[]{:S(2)}) collective-permute-start(bf16[4,16,2048]{2,1,0:T(8,128)(2,1)S(1)} %get-tuple-element.21), channel_id=1, source_target_pairs={{0,16},{4,12},{8,24},{12,4},{16,0},{20,28},{24,8},{28,20},{1,17},{... | collective-permute-start | bytes 786440 | tf_op jit(solution)/shard_map/ppermute | solution.py:262
  51.8 4.3 %collective-permute-done.6 = bf16[4,16,2048]{2,1,0:T(8,128)(2,1)S(1)} collective-permute-done((bf16[4,16,2048]{2,1,0:T(8,128)(2,1)S(1)}, bf16[4,16,2048]{2,1,0:T(8,128)(2,1)S(1)}, u32[]{:S(2)}, u32[]{:S(2)}) %collective-permute-start.6) | collective-permute-done | bytes 262176 | tf_op jit(solution)/shard_map/ppermute | solution.py:262
  56.1 0.1 fusion.1
  56.2 0.6 collective-permute-start.7
  56.8 2.9 %collective-permute-done.5 = bf16[4,16,2048]{2,1,0:T(8,128)(2,1)S(1)} collective-permute-done((bf16[4,16,2048]{2,1,0:T(8,128)(2,1)S(1)}, bf16[4,16,2048]{2,1,0:T(8,128)(2,1)S(1)}, u32[]{:S(2)}, u32[]{:S(2)}) %collective-permute-start.5) | collective-permute-done | bytes 262176 | tf_op jit(solution)/shard_map/ppermute | solution.py:262
  59.7 3.0 %collective-permute-done.7 = bf16[4,16,2048]{2,1,0:T(8,128)(2,1)S(1)} collective-permute-done((bf16[4,16,2048]{2,1,0:T(8,128)(2,1)S(1)}, bf16[4,16,2048]{2,1,0:T(8,128)(2,1)S(1)}, u32[]{:S(2)}, u32[]{:S(2)}) %collective-permute-start.7) | collective-permute-done | bytes 262176 | tf_op jit(solution)/shard_map/ppermute | solution.py:262
  62.6 0.8 %fusion.4 = bf16[4,16,2048]{2,1,0:T(8,128)(2,1)} fusion(f32[4,4,16,2048]{3,2,1,0:T(8,128)S(1)} %get-tuple-element.20, bf16[4,16,2048]{2,1,0:T(8,128)(2,1)S(1)} %collective-permute-done.7, bf16[4,16,2048]{2,1,0:T(8,128)(2,1)S(1)} %collective-permute-done.5), kind=kLoop, calls=%fused_computation.8 | loop fusion | flops 655360 | bytes 1310720 | tf_op jit(solution)/shard_map/convert_element_type | solution.py:287
  63.4 3.4 %all-to-all-start.2 = ((bf16[4,16,2048]{2,1,0:T(8,128)(2,1)}), bf16[4,16,2048]{2,1,0:T(8,128)(2,1)S(1)}, u32[]{:S(2)}, u32[]{:S(2)}) async-start(bf16[4,16,2048]{2,1,0:T(8,128)(2,1)} %fusion.4), calls=%async_computation.2 | async-start | bytes 524288 | tf_op jit(solution)/shard_map/all_to_all | solution.py:287
  66.8 0.8 entropies.1
  67.6 7.8 %all-to-all-done.2 = bf16[4,16,2048]{2,1,0:T(8,128)(2,1)S(1)} async-done(((bf16[4,16,2048]{2,1,0:T(8,128)(2,1)}), bf16[4,16,2048]{2,1,0:T(8,128)(2,1)S(1)}, u32[]{:S(2)}, u32[]{:S(2)}) %all-to-all-start.2) | async-done | bytes 262176 | tf_op jit(solution)/shard_map/all_to_all | solution.py:287
  75.4 1.1 %convolution_convert_fusion = bf16[128,2048]{1,0:T(8,128)(2,1)} fusion(bf16[16,128]{1,0:T(8,128)(2,1)S(1)} %get-tuple-element.12.picker_ref, bf16[16,2048]{1,0:T(8,128)(2,1)S(1)} %reduce_sum.12), kind=kOutput, calls=%fused_computation | convolution fusion | flops 8650752 | bytes 593920 | tf_op jit(solution)/shard_map/dot_general | solution.py:289
  (7 shorter events, 0.2 us)
Async XLA Ops:
  0.6 1.6 %copy-start.1 = (bf16[128,8192]{1,0:T(8,128)(2,1)S(1)}, bf16[128,8192]{1,0:T(8,128)(2,1)}, u32[]{:S(2)}) copy-start(bf16[128,8192]{1,0:T(8,128)(2,1)} %hidden_ref.1) | copy-start | bytes 6291460
  2.2 0.7 copy-start.2
  2.9 19.9 %copy-start = (bf16[8192,256]{1,0:T(8,128)(2,1)S(1)}, bf16[8192,256]{1,0:T(8,128)(2,1)}, u32[]{:S(2)}) copy-start(bf16[8192,256]{1,0:T(8,128)(2,1)} %head_ref.3) | copy-start | bytes 12582916
  4.3 11.1 %collective-permute-start.1 = (bf16[16,8192]{1,0:T(8,128)(2,1)S(1)}, bf16[16,8192]{1,0:T(8,128)(2,1)S(1)}, u32[]{:S(2)}, u32[]{:S(2)}) collective-permute-start(bf16[16,8192]{1,0:T(8,128)(2,1)S(1)} %get-tuple-element.11), channel_id=1, source_target_pairs={{0,16},{4,12},{8,24},{12,4},{16,0},{20,28},{24,8},{28,20},{1,17},{... | collective-permute-start | bytes 786440 | tf_op jit(solution)/shard_map/ppermute | solution.py:262
  7.3 6.4 %collective-permute-start = (bf16[16,8192]{1,0:T(8,128)(2,1)S(1)}, bf16[16,8192]{1,0:T(8,128)(2,1)S(1)}, u32[]{:S(2)}, u32[]{:S(2)}) collective-permute-start(bf16[16,8192]{1,0:T(8,128)(2,1)S(1)} %get-tuple-element.11), channel_id=1, source_target_pairs={{0,8},{4,20},{8,0},{12,28},{16,24},{20,4},{24,16},{28,12},{1,9},{5... | collective-permute-start | bytes 786440 | tf_op jit(solution)/shard_map/ppermute | solution.py:262
  13.7 6.4 %collective-permute-start.2 = (bf16[16,8192]{1,0:T(8,128)(2,1)S(1)}, bf16[16,8192]{1,0:T(8,128)(2,1)S(1)}, u32[]{:S(2)}, u32[]{:S(2)}) collective-permute-start(bf16[16,8192]{1,0:T(8,128)(2,1)S(1)} %collective-permute-done), channel_id=1, source_target_pairs={{0,16},{4,12},{8,24},{12,4},{16,0},{20,28},{24,8},{28,20},{1,17},{... | collective-permute-start | bytes 786440 | tf_op jit(solution)/shard_map/ppermute | solution.py:262
  20.1 2.7 %collective-permute-start.3 = (bf16[64,8192]{1,0:T(8,128)(2,1)S(1)}, bf16[64,8192]{1,0:T(8,128)(2,1)S(1)}, u32[]{:S(2)}, u32[]{:S(2)}) collective-permute-start(bf16[64,8192]{1,0:T(8,128)(2,1)S(1)} %constant_dynamic-update-slice_fusion.near_ref), channel_id=1, source_target_pairs={{0,4},{4,0},{8,12},{12,8},{16,20},{20,16},{24,28},{28,24},{1,5},{5... | collective-permute-start | bytes 3145736 | tf_op jit(solution)/shard_map/ppermute | solution.py:258
  46.5 2.7 %collective-permute-start.4 = (bf16[4,4,16,2048]{3,2,1,0:T(8,128)(2,1)S(1)}, bf16[4,4,16,2048]{3,2,1,0:T(8,128)(2,1)S(1)}, u32[]{:S(2)}, u32[]{:S(2)}) collective-permute-start(bf16[4,4,16,2048]{3,2,1,0:T(8,128)(2,1)S(1)} %get-tuple-element.18), channel_id=1, source_target_pairs={{0,4},{4,0},{8,12},{12,8},{16,20},{20,16},{24,28},{28,24},{1,5},{5... | collective-permute-start | bytes 3145736 | tf_op jit(solution)/shard_map/ppermute | solution.py:258
  49.7 6.4 %collective-permute-start.6 = (bf16[4,16,2048]{2,1,0:T(8,128)(2,1)S(1)}, bf16[4,16,2048]{2,1,0:T(8,128)(2,1)S(1)}, u32[]{:S(2)}, u32[]{:S(2)}) collective-permute-start(bf16[4,16,2048]{2,1,0:T(8,128)(2,1)S(1)} %get-tuple-element.22), channel_id=1, source_target_pairs={{0,16},{4,12},{8,24},{12,4},{16,0},{20,28},{24,8},{28,20},{1,17},{... | collective-permute-start | bytes 786440 | tf_op jit(solution)/shard_map/ppermute | solution.py:262
  50.3 9.4 %collective-permute-start.5 = (bf16[4,16,2048]{2,1,0:T(8,128)(2,1)S(1)}, bf16[4,16,2048]{2,1,0:T(8,128)(2,1)S(1)}, u32[]{:S(2)}, u32[]{:S(2)}) collective-permute-start(bf16[4,16,2048]{2,1,0:T(8,128)(2,1)S(1)} %get-tuple-element.21), channel_id=1, source_target_pairs={{0,16},{4,12},{8,24},{12,4},{16,0},{20,28},{24,8},{28,20},{1,17},{... | collective-permute-start | bytes 786440 | tf_op jit(solution)/shard_map/ppermute | solution.py:262
  56.2 6.4 %collective-permute-start.7 = (bf16[4,16,2048]{2,1,0:T(8,128)(2,1)S(1)}, bf16[4,16,2048]{2,1,0:T(8,128)(2,1)S(1)}, u32[]{:S(2)}, u32[]{:S(2)}) collective-permute-start(bf16[4,16,2048]{2,1,0:T(8,128)(2,1)S(1)} %fusion.1), channel_id=1, source_target_pairs={{0,8},{4,20},{8,0},{12,28},{16,24},{20,4},{24,16},{28,12},{1,9},{5... | collective-permute-start | bytes 786440 | tf_op jit(solution)/shard_map/ppermute | solution.py:262
  63.4 11.9 %all-to-all-start.2 = ((bf16[4,16,2048]{2,1,0:T(8,128)(2,1)}), bf16[4,16,2048]{2,1,0:T(8,128)(2,1)S(1)}, u32[]{:S(2)}, u32[]{:S(2)}) async-start(bf16[4,16,2048]{2,1,0:T(8,128)(2,1)} %fusion.4), calls=%async_computation.2 | async-start | bytes 524288 | tf_op jit(solution)/shard_map/all_to_all | solution.py:287

commit v3 on v0

v3 whole, which is shorter than its diff:
```python
import functools

import jax
import jax.numpy as jnp
from jax import lax
from jax.experimental import pallas as pl
from jax.experimental.pallas import tpu as pltpu
from jax.sharding import PartitionSpec as P

ACT_DEV = 16
VMEM_BYTES = 16 * 2**20
F32, BF16 = jnp.float32, jnp.bfloat16


def params():
    return pltpu.CompilerParams(vmem_limit_bytes=VMEM_BYTES)


def iota(shape, axis):
    return lax.broadcasted_iota(jnp.int32, shape, axis)


def turn(bits, index):
    return sum(((index >> b) & 1) << (bits - 1 - b) for b in range(bits))


def owner_of(n_seq, core, chip):
    me = lax.axis_index("seq")
    bits = (n_seq // 2).bit_length() - 1
    odd = (me & 1) ^ core
    return me ^ (jnp.where(odd == 1, turn(bits, chip), chip) * 2 + core)


def select_kernel(mask_ref, hidden_ref, own_ref, picker_ref, mask_here, hidden_here, mask_sem, sems):
    parts, tokens, step = hidden_here.shape
    copies = [
        pltpu.make_async_copy(
            hidden_ref.at[:, pl.ds(i * step, step)], hidden_here.at[i], sems.at[i]
        )
        for i in range(parts)
    ]
    mask_copy = pltpu.make_async_copy(mask_ref, mask_here, mask_sem)
    mask_copy.start()
    for copy in copies:
        copy.start()
    mask_copy.wait()
    mask = mask_here[...]
    upper = (iota((tokens, tokens), 0) <= iota((tokens, tokens), 1)).astype(BF16)
    ones = jnp.broadcast_to(mask.astype(F32).astype(BF16), (ACT_DEV, tokens))
    slots = jnp.dot(ones, upper, preferred_element_type=F32).astype(jnp.int32) - 1
    picker = (slots == iota((ACT_DEV, tokens), 0)) & (mask == 1)
    picker = picker.astype(F32).astype(BF16)
    picker_ref[...] = picker
    for i in range(parts):
        copies[i].wait()
        own = jnp.dot(picker, hidden_here[i], preferred_element_type=F32)
        own_ref[:, i * step : (i + 1) * step] = own.astype(BF16)


def select(mask, hidden):
    tokens, width = hidden.shape
    parts = 4
    return pl.pallas_call(
        select_kernel,
        in_specs=[pl.BlockSpec(memory_space=pltpu.HBM)] * 2,
        out_shape=[
            jax.ShapeDtypeStruct((ACT_DEV, width), BF16),
            jax.ShapeDtypeStruct((ACT_DEV, tokens), BF16),
        ],
        scratch_shapes=[
            pltpu.VMEM((1, tokens), jnp.int32),
            pltpu.VMEM((parts, tokens, width // parts), BF16),
            pltpu.SemaphoreType.DMA,
            pltpu.SemaphoreType.DMA((parts,)),
        ],
        compiler_params=params(),
        name="select_rows",
    )(mask.reshape(1, tokens), hidden)


def row_order(n_seq):
    last = n_seq // 2 - 1
    early = [(core, chip) for core in (0, 1) for chip in range(last)]
    return early + [(0, last), (1, last)]


def product(block_refs, head_ref):
    width = head_ref.shape[0]
    step = width // 8
    total = None
    for i in range(8):
        rows = jnp.concatenate([ref[:, i * step : (i + 1) * step] for ref in block_refs], axis=0)
        part = jnp.dot(rows, head_ref[i * step : (i + 1) * step, :], preferred_element_type=F32)
        total = part if total is None else total + part
    return total


def early_kernel(*refs):
    *blocks, head_ref, out_ref = refs
    out_ref[...] = product(blocks, head_ref)


def early_logits(blocks, head):
    rows = sum(block.shape[0] for block in blocks)
    return pl.pallas_call(
        early_kernel,
        out_shape=jax.ShapeDtypeStruct((rows, head.shape[1]), F32),
        compiler_params=params(),
        name="early_logits",
    )(*blocks, head)


def late_kernel(n_seq, early_ref, near_ref, far_ref, head_ref, picker_ref, logits_ref, stats_ref, packed):
    late = product([near_ref, far_ref], head_ref)
    logits = jnp.concatenate([early_ref[...], late], axis=0)
    logits_ref[...] = logits
    top = jnp.max(logits, axis=1, keepdims=True)
    away = logits - top
    ex = jnp.exp(away)
    sums = jnp.sum(ex, axis=1, keepdims=True)
    weighted = jnp.sum(ex * away, axis=1, keepdims=True)
    lane = iota((logits.shape[0], 128), 1)
    pack = jnp.where(lane == 0, top, jnp.where(lane == 1, sums, weighted))
    for q, (core, chip) in enumerate(row_order(n_seq)):
        place = pl.multiple_of(owner_of(n_seq, core, chip) * ACT_DEV, ACT_DEV)
        packed[pl.ds(place, ACT_DEV), :] = pack[q * ACT_DEV : (q + 1) * ACT_DEV]
    lines = packed[...].T[:8]
    count = jnp.sum(picker_ref[...].astype(F32))
    mine = iota(lines.shape, 1) // ACT_DEV == lax.axis_index("seq")
    counts = jnp.where(mine, count, 0.0)
    stats_ref[...] = jnp.where(iota(lines.shape, 0) == 3, counts, lines)


def late_logits(n_seq, early, near, far, head, picker):
    shard = head.shape[1]
    rows = n_seq * ACT_DEV
    return pl.pallas_call(
        functools.partial(late_kernel, n_seq),
        out_shape=[
            jax.ShapeDtypeStruct((rows, shard), F32),
            jax.ShapeDtypeStruct((8, rows), F32),
        ],
        scratch_shapes=[pltpu.VMEM((rows, 128), F32)],
        compiler_params=params(),
        name="late_logits",
    )(early, near, far, head, picker)


def merged(refs, index):
    stats = [ref[...] for ref in refs]
    for b in range(len(refs).bit_length() - 1):
        here = ((index >> b) & 1) == 1
        stats = [jnp.where(here, stats[k ^ (1 << b)], stats[k]) for k in range(len(refs))]
    top = functools.reduce(jnp.maximum, [s[0:1] for s in stats])
    total = jnp.zeros_like(top)
    weighted = jnp.zeros_like(top)
    counts = jnp.zeros_like(top)
    for s in stats:
        offset = s[0:1] - top
        scale = jnp.exp(offset)
        total += scale * s[1:2]
        weighted += scale * (s[2:3] + offset * s[1:2])
        counts += s[3:4]
    return top, total, weighted, counts


def stack_rows(first, second, third, fourth):
    row = iota((8, first.shape[1]), 0)
    low = jnp.where(row == 0, first, second)
    high = jnp.where(row == 2, third, fourth)
    return jnp.where(row < 2, low, high)


def merge_kernel(position, *refs):
    *stats, out_ref = refs
    out_ref[...] = stack_rows(*merged(stats, position()))


def merge(stats, position):
    return pl.pallas_call(
        functools.partial(merge_kernel, position),
        out_shape=jax.ShapeDtypeStruct(stats[0].shape, F32),
        compiler_params=params(),
        name="merge_stats",
    )(*stats)


def entropy_kernel(*refs):
    *stats, picker_ref, each_ref, average_ref, column = refs
    top, total, weighted, counts = merged(stats, lax.axis_index("vocab"))
    counts = counts * (1.0 / len(stats))
    rows = top.shape[1]
    entropy = jnp.log(total) - weighted / total
    valid = (iota((1, rows), 1) % ACT_DEV).astype(F32) + 0.5 < counts
    sums = jnp.sum(jnp.where(valid, entropy, 0.0), axis=1, keepdims=True)
    average_ref[...] = sums / jnp.sum(valid.astype(F32), axis=1, keepdims=True)
    column[...] = jnp.broadcast_to(entropy, (128, rows)).T
    place = pl.multiple_of(lax.axis_index("seq") * ACT_DEV, ACT_DEV)
    mine = column[pl.ds(place, ACT_DEV), :][:, :1]
    each_ref[...] = jnp.sum(
        jnp.where(picker_ref[...].astype(F32) > 0.5, mine, 0.0), axis=0, keepdims=True
    )


def entropies(stats, picker):
    tokens = picker.shape[1]
    return pl.pallas_call(
        entropy_kernel,
        out_shape=[
            jax.ShapeDtypeStruct((1, tokens), F32),
            jax.ShapeDtypeStruct((1, 1), F32),
        ],
        scratch_shapes=[pltpu.VMEM((stats[0].shape[1], 128), F32)],
        compiler_params=params(),
        name="entropies",
    )(*stats, picker)


def gradient_kernel(n_seq, *refs):
    *stats, logits_ref, head_ref, near_ref, far_ref, last_ref, columns, ordered = refs
    top, total, weighted, _ = merged(stats, lax.axis_index("vocab"))
    mean = top + weighted / total
    lines = stack_rows(top, 1.0 / total, mean, mean)
    columns[...] = jnp.concatenate([lines] * 16, axis=0).T
    for q, (core, chip) in enumerate(row_order(n_seq)):
        place = pl.multiple_of(owner_of(n_seq, core, chip) * ACT_DEV, ACT_DEV)
        ordered[q * ACT_DEV : (q + 1) * ACT_DEV] = columns[pl.ds(place, ACT_DEV), :]
    logits = logits_ref[...]
    prob = jnp.exp(logits - ordered[:, 0:1]) * ordered[:, 1:2]
    score = (prob * (ordered[:, 2:3] - logits)).astype(BF16)
    n_chip, n_vocab, _, wide = near_ref.shape
    most = (n_chip - 1) * ACT_DEV
    for v in range(n_vocab):
        part = lax.dot_general(
            score,
            head_ref[v * wide : (v + 1) * wide, :],
            (((1,), (1,)), ((), ())),
            preferred_element_type=F32,
        ).astype(BF16)
        blocks = part.reshape(2 * n_chip, ACT_DEV, wide)
        near_ref[: n_chip - 1, v] = blocks[: n_chip - 1]
        near_ref[n_chip - 1, v] = blocks[2 * n_chip - 2]
        far_ref[:, v] = blocks[n_chip - 1 : 2 * n_chip - 2]
        last_ref[v] = blocks[2 * n_chip - 1]


def gradients(n_seq, n_vocab, stats, logits, head):
    rows, shard = logits.shape
    n_chip = n_seq // 2
    block = (n_vocab, ACT_DEV, head.shape[0] // n_vocab)
    return pl.pallas_call(
        functools.partial(gradient_kernel, n_seq),
        out_shape=[
            jax.ShapeDtypeStruct((n_chip,) + block, BF16),
            jax.ShapeDtypeStruct((n_chip - 1,) + block, BF16),
            jax.ShapeDtypeStruct(block, BF16),
        ],
        scratch_shapes=[pltpu.VMEM((rows, 128), F32), pltpu.VMEM((rows, 128), F32)],
        compiler_params=params(),
        name="gradients",
    )(*stats, logits, head)


def body(n_seq, n_vocab, hidden, head, mask):
    n_chip = n_seq // 2
    last = n_chip - 1
    bits = n_chip.bit_length() - 1

    def swap_core(value):
        return lax.ppermute(value, "seq", [(i, i ^ 1) for i in range(n_seq)])

    def swap_chip(value, step):
        flips = (2 << step, 2 << (bits - 1 - step))
        return lax.ppermute(value, "seq", [(i, i ^ flips[i & 1]) for i in range(n_seq)])

    def send_chip(value, chip):
        return lax.ppermute(value, "seq", [(i, i ^ (2 * chip)) for i in range(n_seq)])

    def send_vocab(value, k):
        return lax.ppermute(value, "vocab", [(i, i ^ k) for i in range(n_vocab)])

    own, picker = select(mask, hidden)

    near, far = [own], []
    for a in range(1, n_chip):
        step = a.bit_length() - 1
        source = near[a ^ (1 << step)]
        if a == 2:
            source, far[0] = lax.optimization_barrier((source, far[0]))
        near.append(swap_chip(source, step))
        if a == 1:
            far.append(swap_core(own))
        else:
            far.append(swap_core(near[a - 1]))
    far.append(swap_core(near[last]))

    early = early_logits(near[:last] + far[:last], head)
    logits, stats = late_logits(n_seq, early, near[last], far[last], head, picker)

    stats = merge([stats, swap_core(stats)], lambda: lax.axis_index("seq") & 1)
    stats = merge(
        [stats] + [send_chip(stats, g) for g in range(1, n_chip)], lambda: lax.axis_index("seq") >> 1
    )
    stats = [stats] + [send_vocab(stats, k) for k in range(1, n_vocab)]

    near, far, far_last = gradients(n_seq, n_vocab, stats, logits, head)
    each, average = entropies(stats, picker)

    moved = swap_core(far_last)
    far, moved = lax.optimization_barrier((far, moved))
    far = swap_core(far)
    sums = [near[a].astype(F32) + far[a].astype(F32) for a in range(last)]
    sums.append(near[last].astype(F32) + moved.astype(F32))
    for a in range(last, 0, -1):
        step = a.bit_length() - 1
        sums[a ^ (1 << step)] += swap_chip(sums[a].astype(BF16), step).astype(F32)

    column = lax.axis_index("vocab")

    def piece(k):
        return lax.dynamic_index_in_dim(sums[0], column ^ k, 0, keepdims=False)

    result = piece(0)
    for k in range(n_vocab - 1, 0, -1):
        result = result + send_vocab(piece(k).astype(BF16), k).astype(F32)
    derivative = lax.dot_general(
        picker, result.astype(BF16), (((0,), (0,)), ((), ())), preferred_element_type=F32
    ).astype(BF16)
    return each.reshape(-1), average.reshape(()), derivative


def solution(mesh):
    n_seq, n_vocab = mesh.shape["seq"], mesh.shape["vocab"]

    def run(hidden, head, mask):
        return body(n_seq, n_vocab, hidden, head, mask)

    return jax.shard_map(
        run,
        mesh=mesh,
        in_specs=(P("seq", None), P(None, ("seq", "vocab")), P("seq")),
        out_specs=(P("seq"), P(), P("seq", "vocab")),
        check_vma=False,
    )
```

time: 204 us -> 71.7 us (0.35)
  blocking collectives: 93.7 us -> 0 us
  waiting for transfers between devices: 77.5 us -> 35.6 us
  starting transfers between devices: 0.12 us -> 22.5 us
  between operations: 16.3 us -> 0.74 us
  matrix products: 13 us -> 1.11 us
  Pallas kernels: 0 us -> 5.35 us
  local copies, waits for them, and re-layouts: 0.77 us -> 5.83 us
    psum x2 -> x0, blocking collectives: 54.3 us -> none  [the longest x1 41 us: body(): lax.psum((jnp.sum(ex, axis=1), jnp.sum(ex * logits, axis=1)), ('seq', 'vo...]
    reduce_scatter x2 -> x0, waiting for transfers between devices: 46.6 us -> none  [the longest x1 41.1 us: body(): lax.psum_scatter(lax.dot_general(score_grad, head, (((1,), (1,)), ((), ()...]
    pmax x1 -> x0, blocking collectives: 39.4 us -> none  [body(): top = lax.pmax(local_top, ('seq', 'vocab'))]
    ppermute x0 -> x22, waiting for transfers between devices: none -> 35.6 us  [the longest x6 21.2 us: swap_chip(): lax.ppermute(value, 'seq', [(i, i ^ flips[i & 1]) for i in range(n_seq)])]
    all_gather x1 -> x0, waiting for transfers between devices: 30.9 us -> none  [body(): lax.all_gather(source, 'seq', axis=0, tiled=True)]
    ppermute x0 -> x22, starting transfers between devices: none -> 22.5 us  [the longest x6 8.9 us: send_vocab(): return lax.ppermute(value, 'vocab', [(i, i ^ k) for i in range(n_vocab)])]
    dot_general x5 -> x1, matrix products: 13 us -> 1.11 us  [body(): lax.dot_general(picker, result.astype(BF16), (((0,), (0,)), ((), ())), pr...]
    unnamed x4 -> x8, local copies, waits for them, and re-layouts: 0.01 us -> 5.8 us
  transfers between devices with their start and end apart: 3 -> 22, of which waited for: 3 -> 13; matrix products, arithmetic and copies ran while one was open for 1% -> 0% of each run, Pallas kernels for 0% -> 2%
where the time goes in v3:
time: 71.7 us; the launch traced here: 71.5 us
  waiting for transfers between devices  35.6 us (50%)
  starting transfers between devices  22.5 us (31%)
  local copies, waits for them, and re-layouts  5.83 us (8%)
  Pallas kernels  5.35 us (7%)
  matrix products  1.11 us (2%)
  between operations  0.74 us (1%)
    ppermute x6, waiting for transfers between devices, swap_chip(): lax.ppermute(value, 'seq', [(i, i ^ flips[i & 1]) for i in range(n_seq)])  21.2 us
    ppermute x6, starting transfers between devices, send_vocab(): return lax.ppermute(value, 'vocab', [(i, i ^ k) for i in range(n_vocab)])  8.9 us
    ppermute x6, starting transfers between devices, swap_chip(): lax.ppermute(value, 'seq', [(i, i ^ flips[i & 1]) for i in range(n_seq)])  8.24 us
    ppermute x6, waiting for transfers between devices, send_vocab(): return lax.ppermute(value, 'vocab', [(i, i ^ k) for i in range(n_vocab)])  7.47 us
    unnamed x8, local copies, waits for them, and re-layouts  5.8 us
    ppermute x3, waiting for transfers between devices, send_chip(): return lax.ppermute(value, 'seq', [(i, i ^ 2 * chip) for i in range(n_seq)])  4.5 us
    ppermute x3, starting transfers between devices, send_chip(): return lax.ppermute(value, 'seq', [(i, i ^ 2 * chip) for i in range(n_seq)])  3.58 us
    ppermute x7, waiting for transfers between devices, swap_core(): return lax.ppermute(value, 'seq', [(i, i ^ 1) for i in range(n_seq)])  2.36 us
  transfers between devices with their start and end apart: 22, of which 13 were waited for; matrix products, arithmetic and copies ran while one was open for 0% of the time, Pallas kernels for 2%

profile of v3, /device:TPU:0, one launch (start us, length us, event | category | flops | bytes accessed | tf_op | source)
XLA Modules:
  0.0 71.5 jit_solution(8061952504662114040)
XLA Ops:
  0.6 1.6 %copy-done.2 = bf16[128,8192]{1,0:T(8,128)(2,1)S(1)} copy-done((bf16[128,8192]{1,0:T(8,128)(2,1)S(1)}, bf16[128,8192]{1,0:T(8,128)(2,1)}, u32[]{:S(2)}) %copy-start.2) | copy-done | bytes 2097176
  2.2 0.7 copy-done.3
  2.9 1.1 %select_rows.1 = (bf16[16,8192]{1,0:T(8,128)(2,1)S(1)}, bf16[16,128]{1,0:T(8,128)(2,1)S(1)}) custom-call(s32[1,128]{1,0:T(1,128)S(1)} %bitcast.32, bf16[128,8192]{1,0:T(8,128)(2,1)S(1)} %copy-done.2), custom_call_target="tpu_custom_call" | custom-call | tf_op jit(solution)/shard_map/select_rows/pallas_call | solution.py:63
  4.0 0.5 collective-permute-start.1
  4.5 2.6 %collective-permute-start = (bf16[16,8192]{1,0:T(8,128)(2,1)S(1)}, bf16[16,8192]{1,0:T(8,128)(2,1)S(1)}, u32[]{:S(2)}, u32[]{:S(2)}) collective-permute-start(bf16[16,8192]{1,0:T(8,128)(2,1)S(1)} %get-tuple-element.17.refs_0_), channel_id=1, source_target_pairs={{0,8},{4,20},{8,0},{12,28},{16,24},{20,4},{24,16},{28,12},{1,9},{5... | collective-permute-start | bytes 786440 | tf_op jit(solution)/shard_map/ppermute | solution.py:274
  7.0 0.0 collective-permute-done.1.refs_3_
  7.0 1.5 %collective-permute-start.2 = (bf16[16,8192]{1,0:T(8,128)(2,1)S(1)}, bf16[16,8192]{1,0:T(8,128)(2,1)S(1)}, u32[]{:S(2)}, u32[]{:S(2)}) collective-permute-start(bf16[16,8192]{1,0:T(8,128)(2,1)S(1)} %get-tuple-element.17.refs_0_), channel_id=1, source_target_pairs={{0,16},{4,12},{8,24},{12,4},{16,0},{20,28},{24,8},{28,20},{1,17},{... | collective-permute-start | bytes 786440 | tf_op jit(solution)/shard_map/ppermute | solution.py:274
  8.6 4.5 %collective-permute-done.refs_1_ = bf16[16,8192]{1,0:T(8,128)(2,1)S(1)} collective-permute-done((bf16[16,8192]{1,0:T(8,128)(2,1)S(1)}, bf16[16,8192]{1,0:T(8,128)(2,1)S(1)}, u32[]{:S(2)}, u32[]{:S(2)}) %collective-permute-start) | collective-permute-done | bytes 262176 | tf_op jit(solution)/shard_map/ppermute | solution.py:274
  13.1 2.6 %collective-permute-start.5 = (bf16[16,8192]{1,0:T(8,128)(2,1)S(1)}, bf16[16,8192]{1,0:T(8,128)(2,1)S(1)}, u32[]{:S(2)}, u32[]{:S(2)}) collective-permute-start(bf16[16,8192]{1,0:T(8,128)(2,1)S(1)} %collective-permute-done.refs_1_), channel_id=1, source_target_pairs={{0,16},{4,12},{8,24},{12,4},{16,0},{20,28},{24,8},{28,20},{1,17},{... | collective-permute-start | bytes 786440 | tf_op jit(solution)/shard_map/ppermute | solution.py:274
  15.7 0.5 collective-permute-start.4
  16.2 3.8 %collective-permute-done.5.near_ref = bf16[16,8192]{1,0:T(8,128)(2,1)S(1)} collective-permute-done((bf16[16,8192]{1,0:T(8,128)(2,1)S(1)}, bf16[16,8192]{1,0:T(8,128)(2,1)S(1)}, u32[]{:S(2)}, u32[]{:S(2)}) %collective-permute-start.5) | collective-permute-done | bytes 262176 | tf_op jit(solution)/shard_map/ppermute | solution.py:274
  20.0 0.0 copy-start
  20.1 2.2 %copy-done = bf16[8192,256]{1,0:T(8,128)(2,1)S(1)} copy-done((bf16[8192,256]{1,0:T(8,128)(2,1)S(1)}, bf16[8192,256]{1,0:T(8,128)(2,1)}, u32[]{:S(2)}) %copy-start) | copy-done | bytes 4194328
  22.2 0.8 %early_logits.1.early_ref = f32[96,256]{1,0:T(8,128)S(1)} custom-call(bf16[16,8192]{1,0:T(8,128)(2,1)S(1)} %get-tuple-element.17.refs_0_, bf16[16,8192]{1,0:T(8,128)(2,1)S(1)} %collective-permute-done.refs_1_, bf16[16,8192]{1,0:T(8,128)(2,1)S(1)} %collective-permute-done.2.refs_2_, bf16[16,8192]{1,0:T(8,128)(2,1)S(1)} %collective-permute-done.1.refs_3_, ...), custom_call_target="tpu_custom_call" | custom-call | tf_op jit(solution)/shard_map/early_logits/pallas_call | solution.py:105
  23.0 1.4 %copy-done.1 = bf16[8192,256]{1,0:T(8,128)(2,1)S(1)} copy-done((bf16[8192,256]{1,0:T(8,128)(2,1)S(1)}, bf16[8192,256]{1,0:T(8,128)(2,1)}, u32[]{:S(2)}) %copy-start.1) | copy-done | bytes 4194328
  24.4 1.1 %late_logits.1 = (f32[128,256]{1,0:T(8,128)S(1)}, f32[8,128]{1,0:T(8,128)S(1)}) custom-call(f32[96,256]{1,0:T(8,128)S(1)} %early_logits.1.early_ref, bf16[16,8192]{1,0:T(8,128)(2,1)S(1)} %collective-permute-done.5.near_ref, bf16[16,8192]{1,0:T(8,128)(2,1)S(1)} %collective-permute-done.6.far_ref, bf16[8192,256]{1,0:T(8,128)(2,1)S(1)} %copy-done.1, ...), custom_call_target="tpu_custom_call" | custom-call | tf_op jit(solution)/shard_map/late_logits/pallas_call | solution.py:137
  25.5 0.5 collective-permute-start.7
  26.0 0.8 %collective-permute-done.7.refs_1_ = f32[8,128]{1,0:T(8,128)S(1)} collective-permute-done((f32[8,128]{1,0:T(8,128)S(1)}, f32[8,128]{1,0:T(8,128)S(1)}, u32[]{:S(2)}, u32[]{:S(2)}) %collective-permute-start.7) | collective-permute-done | bytes 4128 | tf_op jit(solution)/shard_map/ppermute | solution.py:270
  26.9 2.0 %collective-permute-start.8 = (f32[8,128]{1,0:T(8,128)S(1)}, f32[8,128]{1,0:T(8,128)S(1)}, u32[]{:S(2)}, u32[]{:S(2)}) collective-permute-start(f32[8,128]{1,0:T(8,128)S(1)} %merge_stats.2.refs_0_), channel_id=1, source_target_pairs={{0,8},{4,12},{8,0},{12,4},{16,24},{20,28},{24,16},{28,20},{1,9},{5... | collective-permute-start | bytes 12296 | tf_op jit(solution)/shard_map/ppermute | solution.py:277
  28.8 1.6 %collective-permute-start.9 = (f32[8,128]{1,0:T(8,128)S(1)}, f32[8,128]{1,0:T(8,128)S(1)}, u32[]{:S(2)}, u32[]{:S(2)}) collective-permute-start(f32[8,128]{1,0:T(8,128)S(1)} %merge_stats.2.refs_0_), channel_id=1, source_target_pairs={{0,16},{4,20},{8,24},{12,28},{16,0},{20,4},{24,8},{28,12},{1,17},{... | collective-permute-start | bytes 12296 | tf_op jit(solution)/shard_map/ppermute | solution.py:277
  30.5 0.1 collective-permute-done.8.refs_1_
  30.5 1.9 %collective-permute-done.9.refs_2_ = f32[8,128]{1,0:T(8,128)S(1)} collective-permute-done((f32[8,128]{1,0:T(8,128)S(1)}, f32[8,128]{1,0:T(8,128)S(1)}, u32[]{:S(2)}, u32[]{:S(2)}) %collective-permute-start.9) | collective-permute-done | bytes 4128 | tf_op jit(solution)/shard_map/ppermute | solution.py:277
  32.5 2.5 %collective-permute-done.10.refs_3_ = f32[8,128]{1,0:T(8,128)S(1)} collective-permute-done((f32[8,128]{1,0:T(8,128)S(1)}, f32[8,128]{1,0:T(8,128)S(1)}, u32[]{:S(2)}, u32[]{:S(2)}) %collective-permute-start.10) | collective-permute-done | bytes 4128 | tf_op jit(solution)/shard_map/ppermute | solution.py:277
  35.0 1.6 %collective-permute-start.11 = (f32[8,128]{1,0:T(8,128)S(1)}, f32[8,128]{1,0:T(8,128)S(1)}, u32[]{:S(2)}, u32[]{:S(2)}) collective-permute-start(f32[8,128]{1,0:T(8,128)S(1)} %merge_stats.3.refs_0_), channel_id=1, source_target_pairs={{0,1},{1,0},{2,3},{3,2},{4,5},{5,4},{6,7},{7,6},{8,9},{9,8},{10,11... | collective-permute-start | bytes 12296 | tf_op jit(solution)/shard_map/ppermute | solution.py:280
  36.6 2.6 %collective-permute-start.12 = (f32[8,128]{1,0:T(8,128)S(1)}, f32[8,128]{1,0:T(8,128)S(1)}, u32[]{:S(2)}, u32[]{:S(2)}) collective-permute-start(f32[8,128]{1,0:T(8,128)S(1)} %merge_stats.3.refs_0_), channel_id=1, source_target_pairs={{0,2},{1,3},{2,0},{3,1},{4,6},{5,7},{6,4},{7,5},{8,10},{9,11},{10,... | collective-permute-start | bytes 12296 | tf_op jit(solution)/shard_map/ppermute | solution.py:280
  39.2 0.2 collective-permute-start.13
  39.4 1.7 %collective-permute-done.12.refs_2_ = f32[8,128]{1,0:T(8,128)S(1)} collective-permute-done((f32[8,128]{1,0:T(8,128)S(1)}, f32[8,128]{1,0:T(8,128)S(1)}, u32[]{:S(2)}, u32[]{:S(2)}) %collective-permute-start.12) | collective-permute-done | bytes 4128 | tf_op jit(solution)/shard_map/ppermute | solution.py:280
  41.1 3.5 %collective-permute-done.13.refs_3_ = f32[8,128]{1,0:T(8,128)S(1)} collective-permute-done((f32[8,128]{1,0:T(8,128)S(1)}, f32[8,128]{1,0:T(8,128)S(1)}, u32[]{:S(2)}, u32[]{:S(2)}) %collective-permute-start.13) | collective-permute-done | bytes 4128 | tf_op jit(solution)/shard_map/ppermute | solution.py:280
  44.6 1.6 %gradients.1 = (bf16[4,4,16,2048]{3,2,1,0:T(8,128)(2,1)S(1)}, bf16[3,4,16,2048]{3,2,1,0:T(8,128)(2,1)S(1)}, bf16[4,16,2048]{2,1,0:T(8,128)(2,1)S(1)}) custom-call(f32[8,128]{1,0:T(8,128)S(1)} %merge_stats.3.refs_0_, f32[8,128]{1,0:T(8,128)S(1)} %collective-permute-done.11.refs_1_, f32[8,128]{1,0:T(8,128)S(1)} %collective-permute-done.12.refs_2_, ...), custom_call_target="tpu_custom_call" | custom-call | tf_op jit(solution)/shard_map/gradients/pallas_call | solution.py:251
  46.3 0.1 collective-permute-start.14
  46.3 1.5 %collective-permute-done.14 = bf16[4,16,2048]{2,1,0:T(8,128)(2,1)S(1)} collective-permute-done((bf16[4,16,2048]{2,1,0:T(8,128)(2,1)S(1)}, bf16[4,16,2048]{2,1,0:T(8,128)(2,1)S(1)}, u32[]{:S(2)}, u32[]{:S(2)}) %collective-permute-start.14) | collective-permute-done | bytes 262176 | tf_op jit(solution)/shard_map/ppermute | solution.py:270
  47.9 0.1 collective-permute-start.15
  48.0 0.1 fusion
  48.1 0.5 collective-permute-start.17
  48.5 6.0 %collective-permute-done.17 = bf16[4,16,2048]{2,1,0:T(8,128)(2,1)S(1)} collective-permute-done((bf16[4,16,2048]{2,1,0:T(8,128)(2,1)S(1)}, bf16[4,16,2048]{2,1,0:T(8,128)(2,1)S(1)}, u32[]{:S(2)}, u32[]{:S(2)}) %collective-permute-start.17) | collective-permute-done | bytes 262176 | tf_op jit(solution)/shard_map/ppermute | solution.py:274
  54.5 0.1 fusion.1
  54.6 0.6 collective-permute-start.18
  55.2 0.1 fusion.3
  55.3 0.5 collective-permute-start.16
  55.8 6.9 %collective-permute-done.18 = bf16[4,16,2048]{2,1,0:T(8,128)(2,1)S(1)} collective-permute-done((bf16[4,16,2048]{2,1,0:T(8,128)(2,1)S(1)}, bf16[4,16,2048]{2,1,0:T(8,128)(2,1)S(1)}, u32[]{:S(2)}, u32[]{:S(2)}) %collective-permute-start.18) | collective-permute-done | bytes 262176 | tf_op jit(solution)/shard_map/ppermute | solution.py:274
  62.7 0.1 fusion.2
  62.9 0.1 collective-permute-start.21
  62.9 0.8 %collective-permute-start.20 = (bf16[16,2048]{1,0:T(8,128)(2,1)S(1)}, bf16[16,2048]{1,0:T(8,128)(2,1)S(1)}, u32[]{:S(2)}, u32[]{:S(2)}) collective-permute-start(bf16[16,2048]{1,0:T(8,128)(2,1)S(1)} %get-tuple-element.31), channel_id=1, source_target_pairs={{0,2},{1,3},{2,0},{3,1},{4,6},{5,7},{6,4},{7,5},{8,10},{9,11},{10,... | collective-permute-start | bytes 196616 | tf_op jit(solution)/shard_map/ppermute | solution.py:280
  63.7 3.6 %collective-permute-start.19 = (bf16[16,2048]{1,0:T(8,128)(2,1)S(1)}, bf16[16,2048]{1,0:T(8,128)(2,1)S(1)}, u32[]{:S(2)}, u32[]{:S(2)}) collective-permute-start(bf16[16,2048]{1,0:T(8,128)(2,1)S(1)} %get-tuple-element.29), channel_id=1, source_target_pairs={{0,3},{1,2},{2,1},{3,0},{4,7},{5,6},{6,5},{7,4},{8,11},{9,10},{10,... | collective-permute-start | bytes 196616 | tf_op jit(solution)/shard_map/ppermute | solution.py:280
  67.3 0.8 %entropies.1 = (f32[1,128]{1,0:T(1,128)}, f32[1,1]{1,0:T(1,128)}) custom-call(f32[8,128]{1,0:T(8,128)S(1)} %merge_stats.3.refs_0_, f32[8,128]{1,0:T(8,128)S(1)} %collective-permute-done.11.refs_1_, f32[8,128]{1,0:T(8,128)S(1)} %collective-permute-done.12.refs_2_, f32[8,128]{1,0:T(8,128)S(1)} %collective-permute-done.13.refs_3_, ...), custom_call_target="tpu_custom_call" | custom-call | tf_op jit(solution)/shard_map/entropies/pallas_call | solution.py:207
  68.1 0.9 %collective-permute-done.20 = bf16[16,2048]{1,0:T(8,128)(2,1)S(1)} collective-permute-done((bf16[16,2048]{1,0:T(8,128)(2,1)S(1)}, bf16[16,2048]{1,0:T(8,128)(2,1)S(1)}, u32[]{:S(2)}, u32[]{:S(2)}) %collective-permute-start.20) | collective-permute-done | bytes 65568 | tf_op jit(solution)/shard_map/ppermute | solution.py:280
  68.9 1.4 %collective-permute-done.19 = bf16[16,2048]{1,0:T(8,128)(2,1)S(1)} collective-permute-done((bf16[16,2048]{1,0:T(8,128)(2,1)S(1)}, bf16[16,2048]{1,0:T(8,128)(2,1)S(1)}, u32[]{:S(2)}, u32[]{:S(2)}) %collective-permute-start.19) | collective-permute-done | bytes 65568 | tf_op jit(solution)/shard_map/ppermute | solution.py:280
  70.4 1.1 %convolution_convert_fusion = bf16[128,2048]{1,0:T(8,128)(2,1)} fusion(bf16[16,128]{1,0:T(8,128)(2,1)S(1)} %get-tuple-element.19.picker_ref.refs_4_, bf16[16,2048]{1,0:T(8,128)(2,1)S(1)} %collective-permute-done.21, bf16[16,2048]{1,0:T(8,128)(2,1)S(1)} %collective-permute-done.20, bf16[16,2048]{1,0:T(8,128)(2,1)S(1)} %collective-permute-done.19, ...), kind=kOutput, calls=%fused_computation | convolution fusion | flops 8880128 | bytes 856068 | tf_op jit(solution)/shard_map/dot_general | solution.py:326
  (17 shorter events, 0.1 us)
Async XLA Ops:
  0.6 1.6 %copy-start.2 = (bf16[128,8192]{1,0:T(8,128)(2,1)S(1)}, bf16[128,8192]{1,0:T(8,128)(2,1)}, u32[]{:S(2)}) copy-start(bf16[128,8192]{1,0:T(8,128)(2,1)} %hidden_ref.1) | copy-start | bytes 6291460
  2.2 0.7 copy-start.3
  4.0 3.1 %collective-permute-start.1 = (bf16[16,8192]{1,0:T(8,128)(2,1)S(1)}, bf16[16,8192]{1,0:T(8,128)(2,1)S(1)}, u32[]{:S(2)}, u32[]{:S(2)}) collective-permute-start(bf16[16,8192]{1,0:T(8,128)(2,1)S(1)} %get-tuple-element.17.refs_0_), channel_id=1, source_target_pairs={{0,4},{4,0},{8,12},{12,8},{16,20},{20,16},{24,28},{28,24},{1,5},{5... | collective-permute-start | bytes 786440 | tf_op jit(solution)/shard_map/ppermute | solution.py:270
  4.5 8.6 %collective-permute-start = (bf16[16,8192]{1,0:T(8,128)(2,1)S(1)}, bf16[16,8192]{1,0:T(8,128)(2,1)S(1)}, u32[]{:S(2)}, u32[]{:S(2)}) collective-permute-start(bf16[16,8192]{1,0:T(8,128)(2,1)S(1)} %get-tuple-element.17.refs_0_), channel_id=1, source_target_pairs={{0,8},{4,20},{8,0},{12,28},{16,24},{20,4},{24,16},{28,12},{1,9},{5... | collective-permute-start | bytes 786440 | tf_op jit(solution)/shard_map/ppermute | solution.py:274
  7.0 8.6 %collective-permute-start.2 = (bf16[16,8192]{1,0:T(8,128)(2,1)S(1)}, bf16[16,8192]{1,0:T(8,128)(2,1)S(1)}, u32[]{:S(2)}, u32[]{:S(2)}) collective-permute-start(bf16[16,8192]{1,0:T(8,128)(2,1)S(1)} %get-tuple-element.17.refs_0_), channel_id=1, source_target_pairs={{0,16},{4,12},{8,24},{12,4},{16,0},{20,28},{24,8},{28,20},{1,17},{... | collective-permute-start | bytes 786440 | tf_op jit(solution)/shard_map/ppermute | solution.py:274
  13.1 7.0 %collective-permute-start.5 = (bf16[16,8192]{1,0:T(8,128)(2,1)S(1)}, bf16[16,8192]{1,0:T(8,128)(2,1)S(1)}, u32[]{:S(2)}, u32[]{:S(2)}) collective-permute-start(bf16[16,8192]{1,0:T(8,128)(2,1)S(1)} %collective-permute-done.refs_1_), channel_id=1, source_target_pairs={{0,16},{4,12},{8,24},{12,4},{16,0},{20,28},{24,8},{28,20},{1,17},{... | collective-permute-start | bytes 786440 | tf_op jit(solution)/shard_map/ppermute | solution.py:274
  15.7 4.4 %collective-permute-start.3 = (bf16[16,8192]{1,0:T(8,128)(2,1)S(1)}, bf16[16,8192]{1,0:T(8,128)(2,1)S(1)}, u32[]{:S(2)}, u32[]{:S(2)}) collective-permute-start(bf16[16,8192]{1,0:T(8,128)(2,1)S(1)} %collective-permute-done.refs_1_), channel_id=1, source_target_pairs={{0,4},{4,0},{8,12},{12,8},{16,20},{20,16},{24,28},{28,24},{1,5},{5... | collective-permute-start | bytes 786440 | tf_op jit(solution)/shard_map/ppermute | solution.py:270
  15.7 4.4 %collective-permute-start.4 = (bf16[16,8192]{1,0:T(8,128)(2,1)S(1)}, bf16[16,8192]{1,0:T(8,128)(2,1)S(1)}, u32[]{:S(2)}, u32[]{:S(2)}) collective-permute-start(bf16[16,8192]{1,0:T(8,128)(2,1)S(1)} %collective-permute-done.2.refs_2_), channel_id=1, source_target_pairs={{0,4},{4,0},{8,12},{12,8},{16,20},{20,16},{24,28},{28,24},{1,5},{5... | collective-permute-start | bytes 786440 | tf_op jit(solution)/shard_map/ppermute | solution.py:270
  20.0 3.0 %collective-permute-start.6 = (bf16[16,8192]{1,0:T(8,128)(2,1)S(1)}, bf16[16,8192]{1,0:T(8,128)(2,1)S(1)}, u32[]{:S(2)}, u32[]{:S(2)}) collective-permute-start(bf16[16,8192]{1,0:T(8,128)(2,1)S(1)} %collective-permute-done.5.near_ref), channel_id=1, source_target_pairs={{0,4},{4,0},{8,12},{12,8},{16,20},{20,16},{24,28},{28,24},{1,5},{5... | collective-permute-start | bytes 786440 | tf_op jit(solution)/shard_map/ppermute | solution.py:270
  20.0 2.2 %copy-start = (bf16[8192,256]{1,0:T(8,128)(2,1)S(1)}, bf16[8192,256]{1,0:T(8,128)(2,1)}, u32[]{:S(2)}) copy-start(bf16[8192,256]{1,0:T(8,128)(2,1)} %refs_5_.1) | copy-start | bytes 12582916
  22.2 2.2 %copy-start.1 = (bf16[8192,256]{1,0:T(8,128)(2,1)S(1)}, bf16[8192,256]{1,0:T(8,128)(2,1)}, u32[]{:S(2)}) copy-start(bf16[8192,256]{1,0:T(8,128)(2,1)} %refs_5_.1) | copy-start | bytes 12582916
  25.5 1.4 %collective-permute-start.7 = (f32[8,128]{1,0:T(8,128)S(1)}, f32[8,128]{1,0:T(8,128)S(1)}, u32[]{:S(2)}, u32[]{:S(2)}) collective-permute-start(f32[8,128]{1,0:T(8,128)S(1)} %get-tuple-element.20.refs_0_), channel_id=1, source_target_pairs={{0,4},{4,0},{8,12},{12,8},{16,20},{20,16},{24,28},{28,24},{1,5},{5... | collective-permute-start | bytes 12296 | tf_op jit(solution)/shard_map/ppermute | solution.py:270
  26.9 3.7 %collective-permute-start.8 = (f32[8,128]{1,0:T(8,128)S(1)}, f32[8,128]{1,0:T(8,128)S(1)}, u32[]{:S(2)}, u32[]{:S(2)}) collective-permute-start(f32[8,128]{1,0:T(8,128)S(1)} %merge_stats.2.refs_0_), channel_id=1, source_target_pairs={{0,8},{4,12},{8,0},{12,4},{16,24},{20,28},{24,16},{28,20},{1,9},{5... | collective-permute-start | bytes 12296 | tf_op jit(solution)/shard_map/ppermute | solution.py:277
  28.8 3.6 %collective-permute-start.9 = (f32[8,128]{1,0:T(8,128)S(1)}, f32[8,128]{1,0:T(8,128)S(1)}, u32[]{:S(2)}, u32[]{:S(2)}) collective-permute-start(f32[8,128]{1,0:T(8,128)S(1)} %merge_stats.2.refs_0_), channel_id=1, source_target_pairs={{0,16},{4,20},{8,24},{12,28},{16,0},{20,4},{24,8},{28,12},{1,17},{... | collective-permute-start | bytes 12296 | tf_op jit(solution)/shard_map/ppermute | solution.py:277
  30.5 4.5 %collective-permute-start.10 = (f32[8,128]{1,0:T(8,128)S(1)}, f32[8,128]{1,0:T(8,128)S(1)}, u32[]{:S(2)}, u32[]{:S(2)}) collective-permute-start(f32[8,128]{1,0:T(8,128)S(1)} %merge_stats.2.refs_0_), channel_id=1, source_target_pairs={{0,24},{4,28},{8,16},{12,20},{16,8},{20,12},{24,0},{28,4},{1,25},{... | collective-permute-start | bytes 12296 | tf_op jit(solution)/shard_map/ppermute | solution.py:277
  35.0 4.5 %collective-permute-start.11 = (f32[8,128]{1,0:T(8,128)S(1)}, f32[8,128]{1,0:T(8,128)S(1)}, u32[]{:S(2)}, u32[]{:S(2)}) collective-permute-start(f32[8,128]{1,0:T(8,128)S(1)} %merge_stats.3.refs_0_), channel_id=1, source_target_pairs={{0,1},{1,0},{2,3},{3,2},{4,5},{5,4},{6,7},{7,6},{8,9},{9,8},{10,11... | collective-permute-start | bytes 12296 | tf_op jit(solution)/shard_map/ppermute | solution.py:280
  36.6 4.5 %collective-permute-start.12 = (f32[8,128]{1,0:T(8,128)S(1)}, f32[8,128]{1,0:T(8,128)S(1)}, u32[]{:S(2)}, u32[]{:S(2)}) collective-permute-start(f32[8,128]{1,0:T(8,128)S(1)} %merge_stats.3.refs_0_), channel_id=1, source_target_pairs={{0,2},{1,3},{2,0},{3,1},{4,6},{5,7},{6,4},{7,5},{8,10},{9,11},{10,... | collective-permute-start | bytes 12296 | tf_op jit(solution)/shard_map/ppermute | solution.py:280
  39.2 5.4 %collective-permute-start.13 = (f32[8,128]{1,0:T(8,128)S(1)}, f32[8,128]{1,0:T(8,128)S(1)}, u32[]{:S(2)}, u32[]{:S(2)}) collective-permute-start(f32[8,128]{1,0:T(8,128)S(1)} %merge_stats.3.refs_0_), channel_id=1, source_target_pairs={{0,3},{1,2},{2,1},{3,0},{4,7},{5,6},{6,5},{7,4},{8,11},{9,10},{10,... | collective-permute-start | bytes 12296 | tf_op jit(solution)/shard_map/ppermute | solution.py:280
  46.3 1.6 %collective-permute-start.14 = (bf16[4,16,2048]{2,1,0:T(8,128)(2,1)S(1)}, bf16[4,16,2048]{2,1,0:T(8,128)(2,1)S(1)}, u32[]{:S(2)}, u32[]{:S(2)}) collective-permute-start(bf16[4,16,2048]{2,1,0:T(8,128)(2,1)S(1)} %get-tuple-element.26), channel_id=1, source_target_pairs={{0,4},{4,0},{8,12},{12,8},{16,20},{20,16},{24,28},{28,24},{1,5},{5... | collective-permute-start | bytes 786440 | tf_op jit(solution)/shard_map/ppermute | solution.py:270
  47.9 6.7 %collective-permute-start.15 = (bf16[3,4,16,2048]{3,2,1,0:T(8,128)(2,1)S(1)}, bf16[3,4,16,2048]{3,2,1,0:T(8,128)(2,1)S(1)}, u32[]{:S(2)}, u32[]{:S(2)}) collective-permute-start(bf16[3,4,16,2048]{3,2,1,0:T(8,128)(2,1)S(1)} %get-tuple-element.27), channel_id=1, source_target_pairs={{0,4},{4,0},{8,12},{12,8},{16,20},{20,16},{24,28},{28,24},{1,5},{5... | collective-permute-start | bytes 2359304 | tf_op jit(solution)/shard_map/ppermute | solution.py:270
  48.1 6.4 %collective-permute-start.17 = (bf16[4,16,2048]{2,1,0:T(8,128)(2,1)S(1)}, bf16[4,16,2048]{2,1,0:T(8,128)(2,1)S(1)}, u32[]{:S(2)}, u32[]{:S(2)}) collective-permute-start(bf16[4,16,2048]{2,1,0:T(8,128)(2,1)S(1)} %fusion), channel_id=1, source_target_pairs={{0,16},{4,12},{8,24},{12,4},{16,0},{20,28},{24,8},{28,20},{1,17},{... | collective-permute-start | bytes 786440 | tf_op jit(solution)/shard_map/ppermute | solution.py:274
  54.6 8.1 %collective-permute-start.18 = (bf16[4,16,2048]{2,1,0:T(8,128)(2,1)S(1)}, bf16[4,16,2048]{2,1,0:T(8,128)(2,1)S(1)}, u32[]{:S(2)}, u32[]{:S(2)}) collective-permute-start(bf16[4,16,2048]{2,1,0:T(8,128)(2,1)S(1)} %fusion.1), channel_id=1, source_target_pairs={{0,8},{4,20},{8,0},{12,28},{16,24},{20,4},{24,16},{28,12},{1,9},{5... | collective-permute-start | bytes 786440 | tf_op jit(solution)/shard_map/ppermute | solution.py:274
  55.3 7.4 %collective-permute-start.16 = (bf16[4,16,2048]{2,1,0:T(8,128)(2,1)S(1)}, bf16[4,16,2048]{2,1,0:T(8,128)(2,1)S(1)}, u32[]{:S(2)}, u32[]{:S(2)}) collective-permute-start(bf16[4,16,2048]{2,1,0:T(8,128)(2,1)S(1)} %fusion.3), channel_id=1, source_target_pairs={{0,16},{4,12},{8,24},{12,4},{16,0},{20,28},{24,8},{28,20},{1,17},{... | collective-permute-start | bytes 786440 | tf_op jit(solution)/shard_map/ppermute | solution.py:274
  62.9 5.2 %collective-permute-start.21 = (bf16[16,2048]{1,0:T(8,128)(2,1)S(1)}, bf16[16,2048]{1,0:T(8,128)(2,1)S(1)}, u32[]{:S(2)}, u32[]{:S(2)}) collective-permute-start(bf16[16,2048]{1,0:T(8,128)(2,1)S(1)} %get-tuple-element.30), channel_id=1, source_target_pairs={{0,1},{1,0},{2,3},{3,2},{4,5},{5,4},{6,7},{7,6},{8,9},{9,8},{10,11... | collective-permute-start | bytes 196616 | tf_op jit(solution)/shard_map/ppermute | solution.py:280
  62.9 6.0 %collective-permute-start.20 = (bf16[16,2048]{1,0:T(8,128)(2,1)S(1)}, bf16[16,2048]{1,0:T(8,128)(2,1)S(1)}, u32[]{:S(2)}, u32[]{:S(2)}) collective-permute-start(bf16[16,2048]{1,0:T(8,128)(2,1)S(1)} %get-tuple-element.31), channel_id=1, source_target_pairs={{0,2},{1,3},{2,0},{3,1},{4,6},{5,7},{6,4},{7,5},{8,10},{9,11},{10,... | collective-permute-start | bytes 196616 | tf_op jit(solution)/shard_map/ppermute | solution.py:280
  63.7 6.7 %collective-permute-start.19 = (bf16[16,2048]{1,0:T(8,128)(2,1)S(1)}, bf16[16,2048]{1,0:T(8,128)(2,1)S(1)}, u32[]{:S(2)}, u32[]{:S(2)}) collective-permute-start(bf16[16,2048]{1,0:T(8,128)(2,1)S(1)} %get-tuple-element.29), channel_id=1, source_target_pairs={{0,3},{1,2},{2,1},{3,0},{4,7},{5,6},{6,5},{7,4},{8,11},{9,10},{10,... | collective-permute-start | bytes 196616 | tf_op jit(solution)/shard_map/ppermute | solution.py:280

commit v4 on v0

v4 whole, which is shorter than its diff:
```python
import functools

import jax
import jax.numpy as jnp
from jax import lax
from jax.experimental import pallas as pl
from jax.experimental.pallas import tpu as pltpu
from jax.sharding import PartitionSpec as P

ACT_DEV = 16
HALVES = 2
ROWS = ACT_DEV // HALVES
LANES = 128
VMEM_BYTES = 16 * 2**20
F32, BF16 = jnp.float32, jnp.bfloat16


def params():
    return pltpu.CompilerParams(vmem_limit_bytes=VMEM_BYTES)


def cost(flops, size):
    return pl.CostEstimate(flops=flops, bytes_accessed=size, transcendentals=0)


def iota(shape, axis):
    return lax.broadcasted_iota(jnp.int32, shape, axis)


def owner_of(q, n_seq):
    n_chip = n_seq // 2
    return lax.axis_index("seq") ^ ((q % n_chip) * 2 + q // n_chip)


def lanes_of(n_seq):
    return -(-n_seq * ROWS // LANES) * LANES


def select_kernel(mask_ref, hidden_ref, *refs):
    *own_refs, picker_ref, mask_here, hidden_here, mask_sem, sems = refs
    parts, tokens, step = hidden_here.shape
    copies = [
        pltpu.make_async_copy(
            hidden_ref.at[:, pl.ds(i * step, step)], hidden_here.at[i], sems.at[i]
        )
        for i in range(parts)
    ]
    mask_copy = pltpu.make_async_copy(mask_ref, mask_here, mask_sem)
    mask_copy.start()
    for copy in copies:
        copy.start()
    mask_copy.wait()
    mask = mask_here[...]
    upper = (iota((tokens, tokens), 0) <= iota((tokens, tokens), 1)).astype(BF16)
    ones = jnp.broadcast_to(mask.astype(F32).astype(BF16), (ACT_DEV, tokens))
    slots = jnp.dot(ones, upper, preferred_element_type=F32).astype(jnp.int32) - 1
    picker = (slots == iota((ACT_DEV, tokens), 0)) & (mask == 1)
    picker = picker.astype(F32).astype(BF16)
    picker_ref[...] = picker
    for i in range(parts):
        copies[i].wait()
        own = jnp.dot(picker, hidden_here[i], preferred_element_type=F32)
        for h, own_ref in enumerate(own_refs):
            own_ref[:, i * step : (i + 1) * step] = own[h * ROWS : (h + 1) * ROWS].astype(BF16)


def select(mask, hidden):
    tokens, width = hidden.shape
    parts = 4
    hbm = functools.partial(pltpu.with_memory_space_constraint, memory_space=pltpu.HBM)
    own = jax.ShapeDtypeStruct((ROWS, width), BF16)
    *own, picker = pl.pallas_call(
        select_kernel,
        in_specs=[pl.BlockSpec(memory_space=pltpu.HBM)] * 2,
        out_shape=[own] * HALVES + [jax.ShapeDtypeStruct((ACT_DEV, tokens), BF16)],
        scratch_shapes=[
            pltpu.VMEM((1, tokens), jnp.int32),
            pltpu.VMEM((parts, tokens, width // parts), BF16),
            pltpu.SemaphoreType.DMA,
            pltpu.SemaphoreType.DMA((parts,)),
        ],
        compiler_params=params(),
        name="select_rows",
    )(hbm(mask.reshape(1, tokens)), hbm(hidden))
    return own, picker


def stage_kernel(head_ref, token_ref, out_ref, sem):
    copy = pltpu.make_async_copy(head_ref, out_ref, sem)
    copy.start()
    copy.wait()


def stage(head, token):
    return pl.pallas_call(
        stage_kernel,
        in_specs=[pl.BlockSpec(memory_space=pltpu.HBM), pl.BlockSpec(memory_space=pl.ANY)],
        out_shape=jax.ShapeDtypeStruct(head.shape, head.dtype),
        scratch_shapes=[pltpu.SemaphoreType.DMA],
        cost_estimate=cost(0, 2 * head.size * 2),
        compiler_params=params(),
        name="stage_head",
    )(pltpu.with_memory_space_constraint(head, pltpu.HBM), token)


def logits_kernel(n_seq, near_ref, far_ref, head_ref, picker_ref, logits_ref, stats_ref, packed):
    width = head_ref.shape[0]
    step = width // 8
    logits = None
    for i in range(8):
        cut = slice(i * step, (i + 1) * step)
        rows = jnp.concatenate([near_ref[:, cut], far_ref[:, cut]], axis=0)
        part = jnp.dot(rows, head_ref[cut, :], preferred_element_type=F32)
        logits = part if logits is None else logits + part
    logits_ref[...] = logits
    top = jnp.max(logits, axis=1, keepdims=True)
    away = logits - top
    ex = jnp.exp(away)
    sums = jnp.sum(ex, axis=1, keepdims=True)
    weighted = jnp.sum(ex * away, axis=1, keepdims=True)
    lane = iota((logits.shape[0], LANES), 1)
    pack = jnp.where(lane == 0, top, jnp.where(lane == 1, sums, weighted))
    packed[...] = jnp.ones(packed.shape, F32)
    for q in range(n_seq):
        place = pl.multiple_of(owner_of(q, n_seq) * ROWS, ROWS)
        packed[pl.ds(place, ROWS), :] = pack[q * ROWS : (q + 1) * ROWS]
    lines = packed[...].T[:8]
    count = jnp.sum(picker_ref[...].astype(F32))
    mine = iota(lines.shape, 1) // ROWS == lax.axis_index("seq")
    lines = jnp.where(iota(lines.shape, 0) == 3, jnp.where(mine, count, 0.0), lines)
    stats_ref[...] = jnp.broadcast_to(lines[None], stats_ref.shape)


def local_logits(n_seq, n_vocab, near, far, head, picker):
    width, shard = head.shape
    rows, lanes = n_seq * ROWS, lanes_of(n_seq)
    return pl.pallas_call(
        functools.partial(logits_kernel, n_seq),
        out_shape=[
            jax.ShapeDtypeStruct((rows, shard), F32),
            jax.ShapeDtypeStruct((n_seq * n_vocab, 8, lanes), F32),
        ],
        scratch_shapes=[pltpu.VMEM((lanes, LANES), F32)],
        cost_estimate=cost(2 * rows * width * shard, 2 * width * (shard + rows)),
        compiler_params=params(),
        name="local_logits",
    )(near, far, head, picker)


def merged(stats):
    tops, sums, weights = stats[:, 0], stats[:, 1], stats[:, 2]
    top = jnp.max(tops, axis=0, keepdims=True)
    offset = tops - top
    scale = jnp.exp(offset)
    total = jnp.sum(scale * sums, axis=0, keepdims=True)
    weighted = jnp.sum(scale * (weights + offset * sums), axis=0, keepdims=True)
    return top, total, weighted / total


def entropy_kernel(n_vocab, *refs):
    *stats_refs, picker_ref, each_ref, average_ref, column = refs
    each, sums, number = 0.0, 0.0, 0.0
    for h, stats_ref in enumerate(stats_refs):
        stats = stats_ref[...]
        _, total, centred = merged(stats)
        entropy = jnp.log(total) - centred
        counts = jnp.sum(stats[:, 3], axis=0, keepdims=True) / n_vocab
        slot = iota(entropy.shape, 1) % ROWS + h * ROWS
        valid = slot.astype(F32) + 0.5 < counts
        sums += jnp.sum(jnp.where(valid, entropy, 0.0), axis=1, keepdims=True)
        number += jnp.sum(valid.astype(F32), axis=1, keepdims=True)
        column[...] = jnp.broadcast_to(entropy, (LANES, entropy.shape[1])).T
        place = pl.multiple_of(lax.axis_index("seq") * ROWS, ROWS)
        mine = column[pl.ds(place, ROWS), :][:, :1]
        picked = picker_ref[...].astype(F32)[h * ROWS : (h + 1) * ROWS] > 0.5
        each += jnp.sum(jnp.where(picked, mine, 0.0), axis=0, keepdims=True)
    each_ref[...] = each
    average_ref[...] = sums / number


def entropies(n_vocab, stats, picker):
    tokens = picker.shape[1]
    return pl.pallas_call(
        functools.partial(entropy_kernel, n_vocab),
        out_shape=[
            jax.ShapeDtypeStruct((1, tokens), F32),
            jax.ShapeDtypeStruct((1, 1), F32),
        ],
        scratch_shapes=[pltpu.VMEM((stats[0].shape[2], LANES), F32)],
        cost_estimate=cost(0, 2**20),
        compiler_params=params(),
        name="entropies",
    )(*stats, picker)


def gradient_kernel(n_seq, stats_ref, logits_ref, head_ref, near_ref, far_ref, columns, ordered):
    top, total, centred = merged(stats_ref[...])
    row = iota((8, top.shape[1]), 0)
    lines = jnp.where(row == 0, top, jnp.where(row == 1, 1.0 / total, top + centred))
    columns[...] = jnp.concatenate([lines] * (LANES // 8), axis=0).T
    for q in range(n_seq):
        place = pl.multiple_of(owner_of(q, n_seq) * ROWS, ROWS)
        ordered[q * ROWS : (q + 1) * ROWS] = columns[pl.ds(place, ROWS), :]
    logits = logits_ref[...]
    prob = jnp.exp(logits - ordered[:, 0:1]) * ordered[:, 1:2]
    score = (prob * (ordered[:, 2:3] - logits)).astype(BF16)
    n_chip, n_vocab, _, wide = near_ref.shape
    for v in range(n_vocab):
        part = lax.dot_general(
            score,
            head_ref[v * wide : (v + 1) * wide, :],
            (((1,), (1,)), ((), ())),
            preferred_element_type=F32,
        )
        for q in range(n_seq):
            out = near_ref if q < n_chip else far_ref
            out[q % n_chip, v] = part[q * ROWS : (q + 1) * ROWS].astype(BF16)


def gradients(n_seq, n_vocab, stats, logits, head):
    rows, shard = logits.shape
    width = head.shape[0]
    out = jax.ShapeDtypeStruct((n_seq // 2, n_vocab, ROWS, width // n_vocab), BF16)
    return pl.pallas_call(
        functools.partial(gradient_kernel, n_seq),
        out_shape=[out, out],
        scratch_shapes=[
            pltpu.VMEM((stats.shape[2], LANES), F32),
            pltpu.VMEM((rows, LANES), F32),
        ],
        cost_estimate=cost(2 * rows * width * shard, 2 * width * (shard + rows)),
        compiler_params=params(),
        name="gradients",
    )(stats, logits, head)


def body(n_seq, n_vocab, hidden, head, mask):
    n_chip = n_seq // 2
    column = lax.axis_index("vocab")

    def swap_core(value):
        return lax.ppermute(value, "seq", [(i, i ^ 1) for i in range(n_seq)])

    def send_chip(value, chip):
        return lax.ppermute(value, "seq", [(i, i ^ (2 * chip)) for i in range(n_seq)])

    def send_vocab(value, k):
        return lax.ppermute(value, "vocab", [(i, i ^ k) for i in range(n_vocab)])

    own, picker = select(mask, hidden)
    head = stage(head, own[0])

    logits, stats = [], []
    for h in range(HALVES):
        near = [own[h]] + [send_chip(own[h], g) for g in range(1, n_chip)]
        near, _ = lax.optimization_barrier((near, logits[-1:]))
        near = jnp.concatenate(near, axis=0)
        part, sent = local_logits(n_seq, n_vocab, near, swap_core(near), head, picker)
        logits.append(part)
        stats.append(lax.all_to_all(sent, ("seq", "vocab"), 0, 0, tiled=True))

    each, average = entropies(n_vocab, stats, picker)

    results = []
    for h in range(HALVES):
        near, far = gradients(n_seq, n_vocab, stats[h], logits[h], head)
        here = near.astype(F32) + swap_core(far).astype(F32)
        sums = here[0]
        for g in range(1, n_chip):
            sums = sums + send_chip(here[g].astype(BF16), g).astype(F32)

        def piece(k):
            return lax.dynamic_index_in_dim(sums, column ^ k, 0, keepdims=False)

        result = piece(0)
        for k in range(1, n_vocab):
            result = result + send_vocab(piece(k).astype(BF16), k).astype(F32)
        results.append(result)
    result = jnp.concatenate(results, axis=0).astype(BF16)
    derivative = lax.dot_general(
        picker, result, (((0,), (0,)), ((), ())), preferred_element_type=F32
    ).astype(BF16)
    return each.reshape(-1), average.reshape(()), derivative


def solution(mesh):
    n_seq, n_vocab = mesh.shape["seq"], mesh.shape["vocab"]

    def run(hidden, head, mask):
        return body(n_seq, n_vocab, hidden, head, mask)

    return jax.shard_map(
        run,
        mesh=mesh,
        in_specs=(P("seq", None), P(None, ("seq", "vocab")), P("seq")),
        out_specs=(P("seq"), P(), P("seq", "vocab")),
        check_vma=False,
    )
```

time: 204 us -> 78.5 us (0.38)
  blocking collectives: 93.7 us -> 0 us
  waiting for transfers between devices: 77.5 us -> 24.2 us
  starting transfers between devices: 0.12 us -> 31 us
  between operations: 16.3 us -> 0.89 us
  matrix products: 13 us -> 1.12 us
  Pallas kernels: 0 us -> 11.8 us
  local copies, waits for them, and re-layouts: 0.77 us -> 7.8 us
    psum x2 -> x0, blocking collectives: 54.3 us -> none  [the longest x1 41 us: body(): lax.psum((jnp.sum(ex, axis=1), jnp.sum(ex * logits, axis=1)), ('seq', 'vo...]
    reduce_scatter x2 -> x0, waiting for transfers between devices: 46.6 us -> none  [the longest x1 41.1 us: body(): lax.psum_scatter(lax.dot_general(score_grad, head, (((1,), (1,)), ((), ()...]
    pmax x1 -> x0, blocking collectives: 39.4 us -> none  [body(): top = lax.pmax(local_top, ('seq', 'vocab'))]
    all_gather x1 -> x0, waiting for transfers between devices: 30.9 us -> none  [body(): lax.all_gather(source, 'seq', axis=0, tiled=True)]
    ppermute x0 -> x22, starting transfers between devices: none -> 23.3 us  [the longest x12 15.2 us: send_chip(): return lax.ppermute(value, 'seq', [(i, i ^ 2 * chip) for i in range(n_seq)])]
    ppermute x0 -> x22, waiting for transfers between devices: none -> 12.2 us  [the longest x12 8.83 us: send_chip(): return lax.ppermute(value, 'seq', [(i, i ^ 2 * chip) for i in range(n_seq)])]
    all_to_all x0 -> x2, waiting for transfers between devices: none -> 12 us  [body(): stats.append(lax.all_to_all(sent, ('seq', 'vocab'), 0, 0, tiled=True))]
    dot_general x5 -> x1, matrix products: 13 us -> 1.12 us  [body(): lax.dot_general(picker, result, (((0,), (0,)), ((), ())), preferred_eleme...]
  transfers between devices with their start and end apart: 3 -> 24, of which waited for: 3 -> 12; matrix products, arithmetic and copies ran while one was open for 1% -> 3% of each run, Pallas kernels for 0% -> 12%
where the time goes in v4:
time: 78.5 us; the launch traced here: 78.1 us
  starting transfers between devices  31 us (39%)
  waiting for transfers between devices  24.2 us (31%)
  Pallas kernels  11.8 us (15%)
  local copies, waits for them, and re-layouts  7.8 us (10%)
  other arithmetic  1.37 us (2%)
  matrix products  1.12 us (1%)
  between operations  0.89 us (1%)
    ppermute x12, starting transfers between devices, send_chip(): return lax.ppermute(value, 'seq', [(i, i ^ 2 * chip) for i in range(n_seq)])  15.2 us
    all_to_all x2, waiting for transfers between devices, body(): stats.append(lax.all_to_all(sent, ('seq', 'vocab'), 0, 0, tiled=True))  12 us
    ppermute x12, waiting for transfers between devices, send_chip(): return lax.ppermute(value, 'seq', [(i, i ^ 2 * chip) for i in range(n_seq)])  8.83 us
    all_to_all x2, starting transfers between devices, body(): stats.append(lax.all_to_all(sent, ('seq', 'vocab'), 0, 0, tiled=True))  7.63 us
    ppermute x6, starting transfers between devices, send_vocab(): return lax.ppermute(value, 'vocab', [(i, i ^ k) for i in range(n_vocab)])  7.6 us
    unnamed x14, local copies, waits for them, and re-layouts  6.95 us
    pallas_call x2, Pallas kernels, local_logits(): pl.pallas_call(functools.partial(logits_kernel, n_seq), out_shape=[jax.Sh...  3.54 us
    ppermute x6, waiting for transfers between devices, send_vocab(): return lax.ppermute(value, 'vocab', [(i, i ^ k) for i in range(n_vocab)])  3.31 us
  transfers between devices with their start and end apart: 24, of which 12 were waited for; matrix products, arithmetic and copies ran while one was open for 3% of the time, Pallas kernels for 12%

profile of v4, /device:TPU:0, one launch (start us, length us, event | category | flops | bytes accessed | tf_op | source)
XLA Modules:
  0.0 78.1 jit_solution(5431327444843290576)
XLA Ops:
  0.6 2.1 %select_rows.1 = (bf16[8,8192]{1,0:T(8,128)(2,1)S(1)}, bf16[8,8192]{1,0:T(8,128)(2,1)S(1)}, bf16[16,128]{1,0:T(8,128)(2,1)S(1)}) custom-call(s32[1,128]{1,0:T(1,128)} %bitcast.60, bf16[128,8192]{1,0:T(8,128)(2,1)} %hidden_ref.1), custom_call_target="tpu_custom_call" | custom-call | tf_op jit(solution)/shard_map/select_rows/pallas_call | solution.py:72
  2.7 4.0 %collective-permute-start.2 = (bf16[8,8192]{1,0:T(8,128)(2,1)S(1)}, bf16[8,8192]{1,0:T(8,128)(2,1)S(1)}, u32[]{:S(2)}, u32[]{:S(2)}) collective-permute-start(bf16[8,8192]{1,0:T(8,128)(2,1)S(1)} %get-tuple-element.25.token_ref), channel_id=1, source_target_pairs={{0,24},{4,28},{8,16},{12,20},{16,8},{20,12},{24,0},{28,4},{1,25},{... | collective-permute-start | bytes 393224 | tf_op jit(solution)/shard_map/ppermute | solution.py:245
  6.7 0.5 collective-permute-start.1
  7.2 0.1 collective-permute-start
  7.3 3.3 %collective-permute-done.2 = bf16[8,8192]{1,0:T(8,128)(2,1)S(1)} collective-permute-done((bf16[8,8192]{1,0:T(8,128)(2,1)S(1)}, bf16[8,8192]{1,0:T(8,128)(2,1)S(1)}, u32[]{:S(2)}, u32[]{:S(2)}) %collective-permute-start.2) | collective-permute-done | bytes 131104 | tf_op jit(solution)/shard_map/ppermute | solution.py:245
  10.6 2.4 %collective-permute-done.1 = bf16[8,8192]{1,0:T(8,128)(2,1)S(1)} collective-permute-done((bf16[8,8192]{1,0:T(8,128)(2,1)S(1)}, bf16[8,8192]{1,0:T(8,128)(2,1)S(1)}, u32[]{:S(2)}, u32[]{:S(2)}) %collective-permute-start.1) | collective-permute-done | bytes 131104 | tf_op jit(solution)/shard_map/ppermute | solution.py:245
  13.0 0.2 collective-permute-done
  13.4 1.6 %collective-permute-start.6 = (bf16[8,8192]{1,0:T(8,128)(2,1)S(1)}, bf16[8,8192]{1,0:T(8,128)(2,1)S(1)}, u32[]{:S(2)}, u32[]{:S(2)}) collective-permute-start(bf16[8,8192]{1,0:T(8,128)(2,1)S(1)} %get-tuple-element.33), channel_id=1, source_target_pairs={{0,24},{4,28},{8,16},{12,20},{16,8},{20,12},{24,0},{28,4},{1,25},{... | collective-permute-start | bytes 393224 | tf_op jit(solution)/shard_map/ppermute | solution.py:245
  15.0 1.4 %collective-permute-start.5 = (bf16[8,8192]{1,0:T(8,128)(2,1)S(1)}, bf16[8,8192]{1,0:T(8,128)(2,1)S(1)}, u32[]{:S(2)}, u32[]{:S(2)}) collective-permute-start(bf16[8,8192]{1,0:T(8,128)(2,1)S(1)} %get-tuple-element.33), channel_id=1, source_target_pairs={{0,16},{4,20},{8,24},{12,28},{16,0},{20,4},{24,8},{28,12},{1,17},{... | collective-permute-start | bytes 393224 | tf_op jit(solution)/shard_map/ppermute | solution.py:245
  16.5 0.5 collective-permute-start.4
  17.0 2.2 %stage_head.1.head_ref = bf16[8192,256]{1,0:T(8,128)(2,1)S(1)} custom-call(bf16[8192,256]{1,0:T(8,128)(2,1)} %head_ref.1, bf16[8,8192]{1,0:T(8,128)(2,1)S(1)} %get-tuple-element.25.token_ref), custom_call_target="tpu_custom_call" | custom-call | bytes 8388608 | tf_op jit(solution)/shard_map/stage_head/pallas_call | solution.py:95
  19.2 1.8 %local_logits.2 = (f32[64,256]{1,0:T(8,128)S(1)}, f32[32,8,128]{2,1,0:T(8,128)}) custom-call(bf16[32,8192]{1,0:T(8,128)(2,1)S(1)} %constant_dynamic-update-slice_fusion.near_ref, bf16[32,8192]{1,0:T(8,128)(2,1)S(1)} %collective-permute-done.3.far_ref, bf16[8192,256]{1,0:T(8,128)(2,1)S(1)} %stage_head.1.head_ref, ...), custom_call_target="tpu_custom_call" | custom-call | flops 268435456 | bytes 5242880 | tf_op jit(solution)/shard_map/local_logits/pallas_call | solution.py:137
  20.9 2.0 %copy-done = bf16[8192,256]{1,0:T(8,128)(2,1)} copy-done((bf16[8192,256]{1,0:T(8,128)(2,1)}, bf16[8192,256]{1,0:T(8,128)(2,1)S(1)}, u32[]{:S(2)}) %copy-start) | copy-done | bytes 4194328
  22.9 0.1 collective-permute-done.5
  23.1 5.1 %all-to-all-start = ((f32[32,8,128]{2,1,0:T(8,128)}), f32[32,8,128]{2,1,0:T(8,128)S(1)}, u32[]{:S(2)}, u32[]{:S(2)}) async-start(f32[32,8,128]{2,1,0:T(8,128)} %get-tuple-element.30), calls=%async_computation | async-start | bytes 262144 | tf_op jit(solution)/shard_map/all_to_all | solution.py:260
  28.2 0.3 collective-permute-start.7
  28.5 8.0 %all-to-all-done.refs_0_.stats_ref = f32[32,8,128]{2,1,0:T(8,128)S(1)} async-done(((f32[32,8,128]{2,1,0:T(8,128)}), f32[32,8,128]{2,1,0:T(8,128)S(1)}, u32[]{:S(2)}, u32[]{:S(2)}) %all-to-all-start) | async-done | bytes 131104 | tf_op jit(solution)/shard_map/all_to_all | solution.py:260
  36.5 2.2 %copy-done.1 = bf16[8192,256]{1,0:T(8,128)(2,1)S(1)} copy-done((bf16[8192,256]{1,0:T(8,128)(2,1)S(1)}, bf16[8192,256]{1,0:T(8,128)(2,1)}, u32[]{:S(2)}) %copy-start.1) | copy-done | bytes 4194328
  38.7 1.6 %gradients.2 = (bf16[4,4,8,2048]{3,2,1,0:T(8,128)(2,1)S(1)}, bf16[4,4,8,2048]{3,2,1,0:T(8,128)(2,1)S(1)}) custom-call(f32[32,8,128]{2,1,0:T(8,128)S(1)} %all-to-all-done.refs_0_.stats_ref, f32[64,256]{1,0:T(8,128)S(1)} %get-tuple-element.32.logits_ref, bf16[8192,256]{1,0:T(8,128)(2,1)S(1)} %copy-done.1), custom_call_target="tpu_custom_call" | custom-call | flops 268435456 | bytes 5242880 | tf_op jit(solution)/shard_map/gradients/pallas_call | solution.py:224
  40.4 0.5 copy-done.2
  40.9 1.8 %local_logits.3 = (f32[64,256]{1,0:T(8,128)S(1)}, f32[32,8,128]{2,1,0:T(8,128)}) custom-call(bf16[32,8192]{1,0:T(8,128)(2,1)S(1)} %constant_dynamic-update-slice_fusion.4.near_ref, bf16[32,8192]{1,0:T(8,128)(2,1)S(1)} %collective-permute-done.7.far_ref, bf16[8192,256]{1,0:T(8,128)(2,1)S(1)} %copy-done.2, bf16[16,128]{1,0:T(8,128)(2,1)S(1)} %get-tuple-element.29.picker_ref.refs_2_), custom_call_target="tpu_custom_call" | custom-call | flops 268435456 | bytes 5242880 | tf_op jit(solution)/shard_map/local_logits/pallas_call | solution.py:137
  42.7 2.6 %all-to-all-start.1 = ((f32[32,8,128]{2,1,0:T(8,128)}), f32[32,8,128]{2,1,0:T(8,128)S(1)}, u32[]{:S(2)}, u32[]{:S(2)}) async-start(f32[32,8,128]{2,1,0:T(8,128)} %get-tuple-element.37), calls=%async_computation.1 | async-start | bytes 262144 | tf_op jit(solution)/shard_map/all_to_all | solution.py:260
  45.3 0.1 fusion.22
  45.4 0.8 slice_bitcast_fusion.7
  46.2 1.6 %collective-permute-start.9 = (bf16[4,8,2048]{2,1,0:T(8,128)(2,1)}, bf16[4,8,2048]{2,1,0:T(8,128)(2,1)S(1)}, u32[]{:S(2)}, u32[]{:S(2)}) collective-permute-start(bf16[4,8,2048]{2,1,0:T(8,128)(2,1)} %get-tuple-element.49), channel_id=1, source_target_pairs={{0,8},{4,12},{8,0},{12,4},{16,24},{20,28},{24,16},{28,20},{1,9},{5... | collective-permute-start | bytes 393224 | tf_op jit(solution)/shard_map/ppermute | solution.py:245
  47.8 1.5 %collective-permute-start.11 = (bf16[4,8,2048]{2,1,0:T(8,128)(2,1)}, bf16[4,8,2048]{2,1,0:T(8,128)(2,1)S(1)}, u32[]{:S(2)}, u32[]{:S(2)}) collective-permute-start(bf16[4,8,2048]{2,1,0:T(8,128)(2,1)} %get-tuple-element.50), channel_id=1, source_target_pairs={{0,24},{4,28},{8,16},{12,20},{16,8},{20,12},{24,0},{28,4},{1,25},{... | collective-permute-start | bytes 393224 | tf_op jit(solution)/shard_map/ppermute | solution.py:245
  49.3 0.4 collective-permute-start.10
  49.7 4.0 %all-to-all-done.1.refs_1_.stats_ref = f32[32,8,128]{2,1,0:T(8,128)S(1)} async-done(((f32[32,8,128]{2,1,0:T(8,128)}), f32[32,8,128]{2,1,0:T(8,128)S(1)}, u32[]{:S(2)}, u32[]{:S(2)}) %all-to-all-start.1) | async-done | bytes 131104 | tf_op jit(solution)/shard_map/all_to_all | solution.py:260
  53.7 2.2 %copy-done.3 = bf16[8192,256]{1,0:T(8,128)(2,1)S(1)} copy-done((bf16[8192,256]{1,0:T(8,128)(2,1)S(1)}, bf16[8192,256]{1,0:T(8,128)(2,1)}, u32[]{:S(2)}) %copy-start.3) | copy-done | bytes 4194328
  55.9 1.6 %gradients.3 = (bf16[4,4,8,2048]{3,2,1,0:T(8,128)(2,1)S(1)}, bf16[4,4,8,2048]{3,2,1,0:T(8,128)(2,1)S(1)}) custom-call(f32[32,8,128]{2,1,0:T(8,128)S(1)} %all-to-all-done.1.refs_1_.stats_ref, f32[64,256]{1,0:T(8,128)S(1)} %get-tuple-element.42.logits_ref, bf16[8192,256]{1,0:T(8,128)(2,1)S(1)} %copy-done.3), custom_call_target="tpu_custom_call" | custom-call | flops 268435456 | bytes 5242880 | tf_op jit(solution)/shard_map/gradients/pallas_call | solution.py:224
  57.5 0.8 %entropies.1 = (f32[1,128]{1,0:T(1,128)}, f32[1,1]{1,0:T(1,128)}) custom-call(f32[32,8,128]{2,1,0:T(8,128)S(1)} %all-to-all-done.refs_0_.stats_ref, f32[32,8,128]{2,1,0:T(8,128)S(1)} %all-to-all-done.1.refs_1_.stats_ref, bf16[16,128]{1,0:T(8,128)(2,1)S(1)} %get-tuple-element.29.picker_ref.refs_2_), custom_call_target="tpu_custom_call" | custom-call | bytes 1048576 | tf_op jit(solution)/shard_map/entropies/pallas_call | solution.py:183
  58.4 1.0 %fusion.5 = f32[4,8,2048]{2,1,0:T(8,128)S(1)} fusion(f32[4,4,8,2048]{3,2,1,0:T(8,128)S(1)} %get-tuple-element.46, bf16[4,8,2048]{2,1,0:T(8,128)(2,1)S(1)} %collective-permute-done.11, bf16[4,8,2048]{2,1,0:T(8,128)(2,1)} %collective-permute-done.10, bf16[4,8,2048]{2,1,0:T(8,128)(2,1)S(1)} %collective-permute-done.9), kind=kLoop, calls=%fused_computation.10 | loop fusion | flops 393216 | bytes 917504 | tf_op jit(solution)/shard_map/add | solution.py:270
  59.3 0.1 collective-permute-done.15
  59.4 0.1 fusion.23
  59.6 0.9 %collective-permute-start.16 = (bf16[4,8,2048]{2,1,0:T(8,128)(2,1)S(1)}, bf16[4,8,2048]{2,1,0:T(8,128)(2,1)S(1)}, u32[]{:S(2)}, u32[]{:S(2)}) collective-permute-start(bf16[4,8,2048]{2,1,0:T(8,128)(2,1)S(1)} %get-tuple-element.52), channel_id=1, source_target_pairs={{0,8},{4,12},{8,0},{12,4},{16,24},{20,28},{24,16},{28,20},{1,9},{5... | collective-permute-start | bytes 393224 | tf_op jit(solution)/shard_map/ppermute | solution.py:245
  60.5 1.4 %collective-permute-start.18 = (bf16[4,8,2048]{2,1,0:T(8,128)(2,1)S(1)}, bf16[4,8,2048]{2,1,0:T(8,128)(2,1)S(1)}, u32[]{:S(2)}, u32[]{:S(2)}) collective-permute-start(bf16[4,8,2048]{2,1,0:T(8,128)(2,1)S(1)} %get-tuple-element.53), channel_id=1, source_target_pairs={{0,24},{4,28},{8,16},{12,20},{16,8},{20,12},{24,0},{28,4},{1,25},{... | collective-permute-start | bytes 393224 | tf_op jit(solution)/shard_map/ppermute | solution.py:245
  61.9 1.2 %collective-permute-start.17 = (bf16[4,8,2048]{2,1,0:T(8,128)(2,1)S(1)}, bf16[4,8,2048]{2,1,0:T(8,128)(2,1)S(1)}, u32[]{:S(2)}, u32[]{:S(2)}) collective-permute-start(bf16[4,8,2048]{2,1,0:T(8,128)(2,1)S(1)} %get-tuple-element.54), channel_id=1, source_target_pairs={{0,16},{4,20},{8,24},{12,28},{16,0},{20,4},{24,8},{28,12},{1,17},{... | collective-permute-start | bytes 393224 | tf_op jit(solution)/shard_map/ppermute | solution.py:245
  63.2 0.7 collective-permute-start.12
  63.9 2.3 %collective-permute-start.14 = (bf16[8,2048]{1,0:T(8,128)(2,1)S(1)}, bf16[8,2048]{1,0:T(8,128)(2,1)S(1)}, u32[]{:S(2)}, u32[]{:S(2)}) collective-permute-start(bf16[8,2048]{1,0:T(8,128)(2,1)S(1)} %get-tuple-element.56), channel_id=1, source_target_pairs={{0,3},{1,2},{2,1},{3,0},{4,7},{5,6},{6,5},{7,4},{8,11},{9,10},{10,... | collective-permute-start | bytes 98312 | tf_op jit(solution)/shard_map/ppermute | solution.py:248
  66.2 1.0 %collective-permute-start.13 = (bf16[8,2048]{1,0:T(8,128)(2,1)S(1)}, bf16[8,2048]{1,0:T(8,128)(2,1)S(1)}, u32[]{:S(2)}, u32[]{:S(2)}) collective-permute-start(bf16[8,2048]{1,0:T(8,128)(2,1)S(1)} %get-tuple-element.57), channel_id=1, source_target_pairs={{0,2},{1,3},{2,0},{3,1},{4,6},{5,7},{6,4},{7,5},{8,10},{9,11},{10,... | collective-permute-start | bytes 98312 | tf_op jit(solution)/shard_map/ppermute | solution.py:248
  67.2 1.4 %collective-permute-done.18 = bf16[4,8,2048]{2,1,0:T(8,128)(2,1)S(1)} collective-permute-done((bf16[4,8,2048]{2,1,0:T(8,128)(2,1)S(1)}, bf16[4,8,2048]{2,1,0:T(8,128)(2,1)S(1)}, u32[]{:S(2)}, u32[]{:S(2)}) %collective-permute-start.18) | collective-permute-done | bytes 131104 | tf_op jit(solution)/shard_map/ppermute | solution.py:245
  68.6 1.4 %collective-permute-done.17 = bf16[4,8,2048]{2,1,0:T(8,128)(2,1)S(1)} collective-permute-done((bf16[4,8,2048]{2,1,0:T(8,128)(2,1)S(1)}, bf16[4,8,2048]{2,1,0:T(8,128)(2,1)S(1)}, u32[]{:S(2)}, u32[]{:S(2)}) %collective-permute-start.17) | collective-permute-done | bytes 131104 | tf_op jit(solution)/shard_map/ppermute | solution.py:245
  70.2 1.7 %collective-permute-start.21 = (bf16[8,2048]{1,0:T(8,128)(2,1)S(1)}, bf16[8,2048]{1,0:T(8,128)(2,1)S(1)}, u32[]{:S(2)}, u32[]{:S(2)}) collective-permute-start(bf16[8,2048]{1,0:T(8,128)(2,1)S(1)} %get-tuple-element.59), channel_id=1, source_target_pairs={{0,3},{1,2},{2,1},{3,0},{4,7},{5,6},{6,5},{7,4},{8,11},{9,10},{10,... | collective-permute-start | bytes 98312 | tf_op jit(solution)/shard_map/ppermute | solution.py:248
  71.8 1.8 %collective-permute-start.20 = (bf16[8,2048]{1,0:T(8,128)(2,1)S(1)}, bf16[8,2048]{1,0:T(8,128)(2,1)S(1)}, u32[]{:S(2)}, u32[]{:S(2)}) collective-permute-start(bf16[8,2048]{1,0:T(8,128)(2,1)S(1)} %get-tuple-element.60), channel_id=1, source_target_pairs={{0,2},{1,3},{2,0},{3,1},{4,6},{5,7},{6,4},{7,5},{8,10},{9,11},{10,... | collective-permute-start | bytes 98312 | tf_op jit(solution)/shard_map/ppermute | solution.py:248
  73.7 0.8 %collective-permute-done.19 = bf16[8,2048]{1,0:T(8,128)(2,1)S(1)} collective-permute-done((bf16[8,2048]{1,0:T(8,128)(2,1)S(1)}, bf16[8,2048]{1,0:T(8,128)(2,1)S(1)}, u32[]{:S(2)}, u32[]{:S(2)}) %collective-permute-start.19) | collective-permute-done | bytes 32800 | tf_op jit(solution)/shard_map/ppermute | solution.py:248
  74.5 1.5 %collective-permute-done.21 = bf16[8,2048]{1,0:T(8,128)(2,1)S(1)} collective-permute-done((bf16[8,2048]{1,0:T(8,128)(2,1)S(1)}, bf16[8,2048]{1,0:T(8,128)(2,1)S(1)}, u32[]{:S(2)}, u32[]{:S(2)}) %collective-permute-start.21) | collective-permute-done | bytes 32800 | tf_op jit(solution)/shard_map/ppermute | solution.py:248
  75.9 1.0 %collective-permute-done.20 = bf16[8,2048]{1,0:T(8,128)(2,1)S(1)} collective-permute-done((bf16[8,2048]{1,0:T(8,128)(2,1)S(1)}, bf16[8,2048]{1,0:T(8,128)(2,1)S(1)}, u32[]{:S(2)}, u32[]{:S(2)}) %collective-permute-start.20) | collective-permute-done | bytes 32800 | tf_op jit(solution)/shard_map/ppermute | solution.py:248
  77.0 1.1 %convolution_convert_fusion = bf16[128,2048]{1,0:T(8,128)(2,1)} fusion(bf16[16,128]{1,0:T(8,128)(2,1)S(1)} %get-tuple-element.29.picker_ref.refs_2_, bf16[8,2048]{1,0:T(8,128)(2,1)S(1)} %fusion.11, bf16[8,2048]{1,0:T(8,128)(2,1)S(1)} %fusion.14), kind=kOutput, calls=%fused_computation | convolution fusion | flops 8781824 | bytes 593920 | tf_op jit(solution)/shard_map/dot_general | solution.py:280
  (34 shorter events, 0.6 us)
Async XLA Ops:
  2.7 7.9 %collective-permute-start.2 = (bf16[8,8192]{1,0:T(8,128)(2,1)S(1)}, bf16[8,8192]{1,0:T(8,128)(2,1)S(1)}, u32[]{:S(2)}, u32[]{:S(2)}) collective-permute-start(bf16[8,8192]{1,0:T(8,128)(2,1)S(1)} %get-tuple-element.25.token_ref), channel_id=1, source_target_pairs={{0,24},{4,28},{8,16},{12,20},{16,8},{20,12},{24,0},{28,4},{1,25},{... | collective-permute-start | bytes 393224 | tf_op jit(solution)/shard_map/ppermute | solution.py:245
  6.7 6.3 %collective-permute-start.1 = (bf16[8,8192]{1,0:T(8,128)(2,1)S(1)}, bf16[8,8192]{1,0:T(8,128)(2,1)S(1)}, u32[]{:S(2)}, u32[]{:S(2)}) collective-permute-start(bf16[8,8192]{1,0:T(8,128)(2,1)S(1)} %get-tuple-element.25.token_ref), channel_id=1, source_target_pairs={{0,16},{4,20},{8,24},{12,28},{16,0},{20,4},{24,8},{28,12},{1,17},{... | collective-permute-start | bytes 393224 | tf_op jit(solution)/shard_map/ppermute | solution.py:245
  7.2 6.0 %collective-permute-start = (bf16[8,8192]{1,0:T(8,128)(2,1)S(1)}, bf16[8,8192]{1,0:T(8,128)(2,1)S(1)}, u32[]{:S(2)}, u32[]{:S(2)}) collective-permute-start(bf16[8,8192]{1,0:T(8,128)(2,1)S(1)} %get-tuple-element.25.token_ref), channel_id=1, source_target_pairs={{0,8},{4,12},{8,0},{12,4},{16,24},{20,28},{24,16},{28,20},{1,9},{5... | collective-permute-start | bytes 393224 | tf_op jit(solution)/shard_map/ppermute | solution.py:245
  13.3 5.8 %collective-permute-start.3 = (bf16[32,8192]{1,0:T(8,128)(2,1)S(1)}, bf16[32,8192]{1,0:T(8,128)(2,1)S(1)}, u32[]{:S(2)}, u32[]{:S(2)}) collective-permute-start(bf16[32,8192]{1,0:T(8,128)(2,1)S(1)} %constant_dynamic-update-slice_fusion.near_ref), channel_id=1, source_target_pairs={{0,4},{4,0},{8,12},{12,8},{16,20},{20,16},{24,28},{28,24},{1,5},{5... | collective-permute-start | bytes 1572872 | tf_op jit(solution)/shard_map/ppermute | solution.py:242
  13.4 9.5 %collective-permute-start.6 = (bf16[8,8192]{1,0:T(8,128)(2,1)S(1)}, bf16[8,8192]{1,0:T(8,128)(2,1)S(1)}, u32[]{:S(2)}, u32[]{:S(2)}) collective-permute-start(bf16[8,8192]{1,0:T(8,128)(2,1)S(1)} %get-tuple-element.33), channel_id=1, source_target_pairs={{0,24},{4,28},{8,16},{12,20},{16,8},{20,12},{24,0},{28,4},{1,25},{... | collective-permute-start | bytes 393224 | tf_op jit(solution)/shard_map/ppermute | solution.py:245
  15.0 8.0 %collective-permute-start.5 = (bf16[8,8192]{1,0:T(8,128)(2,1)S(1)}, bf16[8,8192]{1,0:T(8,128)(2,1)S(1)}, u32[]{:S(2)}, u32[]{:S(2)}) collective-permute-start(bf16[8,8192]{1,0:T(8,128)(2,1)S(1)} %get-tuple-element.33), channel_id=1, source_target_pairs={{0,16},{4,20},{8,24},{12,28},{16,0},{20,4},{24,8},{28,12},{1,17},{... | collective-permute-start | bytes 393224 | tf_op jit(solution)/shard_map/ppermute | solution.py:245
  16.5 6.6 %collective-permute-start.4 = (bf16[8,8192]{1,0:T(8,128)(2,1)S(1)}, bf16[8,8192]{1,0:T(8,128)(2,1)S(1)}, u32[]{:S(2)}, u32[]{:S(2)}) collective-permute-start(bf16[8,8192]{1,0:T(8,128)(2,1)S(1)} %get-tuple-element.33), channel_id=1, source_target_pairs={{0,8},{4,12},{8,0},{12,4},{16,24},{20,28},{24,16},{28,20},{1,9},{5... | collective-permute-start | bytes 393224 | tf_op jit(solution)/shard_map/ppermute | solution.py:245
  20.9 2.0 %copy-start = (bf16[8192,256]{1,0:T(8,128)(2,1)}, bf16[8192,256]{1,0:T(8,128)(2,1)S(1)}, u32[]{:S(2)}) copy-start(bf16[8192,256]{1,0:T(8,128)(2,1)S(1)} %stage_head.1.head_ref) | copy-start | bytes 12582916
  23.1 13.5 %all-to-all-start = ((f32[32,8,128]{2,1,0:T(8,128)}), f32[32,8,128]{2,1,0:T(8,128)S(1)}, u32[]{:S(2)}, u32[]{:S(2)}) async-start(f32[32,8,128]{2,1,0:T(8,128)} %get-tuple-element.30), calls=%async_computation | async-start | bytes 262144 | tf_op jit(solution)/shard_map/all_to_all | solution.py:260
  28.2 12.2 %collective-permute-start.7 = (bf16[32,8192]{1,0:T(8,128)(2,1)S(1)}, bf16[32,8192]{1,0:T(8,128)(2,1)S(1)}, u32[]{:S(2)}, u32[]{:S(2)}) collective-permute-start(bf16[32,8192]{1,0:T(8,128)(2,1)S(1)} %constant_dynamic-update-slice_fusion.4.near_ref), channel_id=1, source_target_pairs={{0,4},{4,0},{8,12},{12,8},{16,20},{20,16},{24,28},{28,24},{1,5},{5... | collective-permute-start | bytes 1572872 | tf_op jit(solution)/shard_map/ppermute | solution.py:242
  36.5 2.2 %copy-start.1 = (bf16[8192,256]{1,0:T(8,128)(2,1)S(1)}, bf16[8192,256]{1,0:T(8,128)(2,1)}, u32[]{:S(2)}) copy-start(bf16[8192,256]{1,0:T(8,128)(2,1)} %copy-done) | copy-start | bytes 12582916
  38.7 2.2 %copy-start.2 = (bf16[8192,256]{1,0:T(8,128)(2,1)S(1)}, bf16[8192,256]{1,0:T(8,128)(2,1)}, u32[]{:S(2)}) copy-start(bf16[8192,256]{1,0:T(8,128)(2,1)} %copy-done) | copy-start | bytes 12582916
  40.3 5.0 %collective-permute-start.8 = (bf16[4,4,8,2048]{3,2,1,0:T(8,128)(2,1)S(1)}, bf16[4,4,8,2048]{3,2,1,0:T(8,128)(2,1)S(1)}, u32[]{:S(2)}, u32[]{:S(2)}) collective-permute-start(bf16[4,4,8,2048]{3,2,1,0:T(8,128)(2,1)S(1)} %get-tuple-element.41), channel_id=1, source_target_pairs={{0,4},{4,0},{8,12},{12,8},{16,20},{20,16},{24,28},{28,24},{1,5},{5... | collective-permute-start | bytes 1572872 | tf_op jit(solution)/shard_map/ppermute | solution.py:242
  42.7 11.0 %all-to-all-start.1 = ((f32[32,8,128]{2,1,0:T(8,128)}), f32[32,8,128]{2,1,0:T(8,128)S(1)}, u32[]{:S(2)}, u32[]{:S(2)}) async-start(f32[32,8,128]{2,1,0:T(8,128)} %get-tuple-element.37), calls=%async_computation.1 | async-start | bytes 262144 | tf_op jit(solution)/shard_map/all_to_all | solution.py:260
  46.2 12.1 %collective-permute-start.9 = (bf16[4,8,2048]{2,1,0:T(8,128)(2,1)}, bf16[4,8,2048]{2,1,0:T(8,128)(2,1)S(1)}, u32[]{:S(2)}, u32[]{:S(2)}) collective-permute-start(bf16[4,8,2048]{2,1,0:T(8,128)(2,1)} %get-tuple-element.49), channel_id=1, source_target_pairs={{0,8},{4,12},{8,0},{12,4},{16,24},{20,28},{24,16},{28,20},{1,9},{5... | collective-permute-start | bytes 393224 | tf_op jit(solution)/shard_map/ppermute | solution.py:245
  47.8 10.5 %collective-permute-start.11 = (bf16[4,8,2048]{2,1,0:T(8,128)(2,1)}, bf16[4,8,2048]{2,1,0:T(8,128)(2,1)S(1)}, u32[]{:S(2)}, u32[]{:S(2)}) collective-permute-start(bf16[4,8,2048]{2,1,0:T(8,128)(2,1)} %get-tuple-element.50), channel_id=1, source_target_pairs={{0,24},{4,28},{8,16},{12,20},{16,8},{20,12},{24,0},{28,4},{1,25},{... | collective-permute-start | bytes 393224 | tf_op jit(solution)/shard_map/ppermute | solution.py:245
  49.3 9.0 %collective-permute-start.10 = (bf16[4,8,2048]{2,1,0:T(8,128)(2,1)}, bf16[4,8,2048]{2,1,0:T(8,128)(2,1)}, u32[]{:S(2)}, u32[]{:S(2)}) collective-permute-start(bf16[4,8,2048]{2,1,0:T(8,128)(2,1)} %get-tuple-element.51), channel_id=1, source_target_pairs={{0,16},{4,20},{8,24},{12,28},{16,0},{20,4},{24,8},{28,12},{1,17},{... | collective-permute-start | bytes 393224 | tf_op jit(solution)/shard_map/ppermute | solution.py:245
  53.7 2.2 %copy-start.3 = (bf16[8192,256]{1,0:T(8,128)(2,1)S(1)}, bf16[8192,256]{1,0:T(8,128)(2,1)}, u32[]{:S(2)}) copy-start(bf16[8192,256]{1,0:T(8,128)(2,1)} %copy-done) | copy-start | bytes 12582916
  57.4 2.0 %collective-permute-start.15 = (bf16[4,4,8,2048]{3,2,1,0:T(8,128)(2,1)S(1)}, bf16[4,4,8,2048]{3,2,1,0:T(8,128)(2,1)S(1)}, u32[]{:S(2)}, u32[]{:S(2)}) collective-permute-start(bf16[4,4,8,2048]{3,2,1,0:T(8,128)(2,1)S(1)} %get-tuple-element.44), channel_id=1, source_target_pairs={{0,4},{4,0},{8,12},{12,8},{16,20},{20,16},{24,28},{28,24},{1,5},{5... | collective-permute-start | bytes 1572872 | tf_op jit(solution)/shard_map/ppermute | solution.py:242
  59.6 6.6 %collective-permute-start.16 = (bf16[4,8,2048]{2,1,0:T(8,128)(2,1)S(1)}, bf16[4,8,2048]{2,1,0:T(8,128)(2,1)S(1)}, u32[]{:S(2)}, u32[]{:S(2)}) collective-permute-start(bf16[4,8,2048]{2,1,0:T(8,128)(2,1)S(1)} %get-tuple-element.52), channel_id=1, source_target_pairs={{0,8},{4,12},{8,0},{12,4},{16,24},{20,28},{24,16},{28,20},{1,9},{5... | collective-permute-start | bytes 393224 | tf_op jit(solution)/shard_map/ppermute | solution.py:245
  60.5 8.1 %collective-permute-start.18 = (bf16[4,8,2048]{2,1,0:T(8,128)(2,1)S(1)}, bf16[4,8,2048]{2,1,0:T(8,128)(2,1)S(1)}, u32[]{:S(2)}, u32[]{:S(2)}) collective-permute-start(bf16[4,8,2048]{2,1,0:T(8,128)(2,1)S(1)} %get-tuple-element.53), channel_id=1, source_target_pairs={{0,24},{4,28},{8,16},{12,20},{16,8},{20,12},{24,0},{28,4},{1,25},{... | collective-permute-start | bytes 393224 | tf_op jit(solution)/shard_map/ppermute | solution.py:245
  61.9 8.1 %collective-permute-start.17 = (bf16[4,8,2048]{2,1,0:T(8,128)(2,1)S(1)}, bf16[4,8,2048]{2,1,0:T(8,128)(2,1)S(1)}, u32[]{:S(2)}, u32[]{:S(2)}) collective-permute-start(bf16[4,8,2048]{2,1,0:T(8,128)(2,1)S(1)} %get-tuple-element.54), channel_id=1, source_target_pairs={{0,16},{4,20},{8,24},{12,28},{16,0},{20,4},{24,8},{28,12},{1,17},{... | collective-permute-start | bytes 393224 | tf_op jit(solution)/shard_map/ppermute | solution.py:245
  63.2 8.7 %collective-permute-start.12 = (bf16[8,2048]{1,0:T(8,128)(2,1)S(1)}, bf16[8,2048]{1,0:T(8,128)(2,1)S(1)}, u32[]{:S(2)}, u32[]{:S(2)}) collective-permute-start(bf16[8,2048]{1,0:T(8,128)(2,1)S(1)} %get-tuple-element.55), channel_id=1, source_target_pairs={{0,1},{1,0},{2,3},{3,2},{4,5},{5,4},{6,7},{7,6},{8,9},{9,8},{10,11... | collective-permute-start | bytes 98312 | tf_op jit(solution)/shard_map/ppermute | solution.py:248
  63.9 9.8 %collective-permute-start.14 = (bf16[8,2048]{1,0:T(8,128)(2,1)S(1)}, bf16[8,2048]{1,0:T(8,128)(2,1)S(1)}, u32[]{:S(2)}, u32[]{:S(2)}) collective-permute-start(bf16[8,2048]{1,0:T(8,128)(2,1)S(1)} %get-tuple-element.56), channel_id=1, source_target_pairs={{0,3},{1,2},{2,1},{3,0},{4,7},{5,6},{6,5},{7,4},{8,11},{9,10},{10,... | collective-permute-start | bytes 98312 | tf_op jit(solution)/shard_map/ppermute | solution.py:248
  66.2 7.4 %collective-permute-start.13 = (bf16[8,2048]{1,0:T(8,128)(2,1)S(1)}, bf16[8,2048]{1,0:T(8,128)(2,1)S(1)}, u32[]{:S(2)}, u32[]{:S(2)}) collective-permute-start(bf16[8,2048]{1,0:T(8,128)(2,1)S(1)} %get-tuple-element.57), channel_id=1, source_target_pairs={{0,2},{1,3},{2,0},{3,1},{4,6},{5,7},{6,4},{7,5},{8,10},{9,11},{10,... | collective-permute-start | bytes 98312 | tf_op jit(solution)/shard_map/ppermute | solution.py:248
  70.1 4.4 %collective-permute-start.19 = (bf16[8,2048]{1,0:T(8,128)(2,1)S(1)}, bf16[8,2048]{1,0:T(8,128)(2,1)S(1)}, u32[]{:S(2)}, u32[]{:S(2)}) collective-permute-start(bf16[8,2048]{1,0:T(8,128)(2,1)S(1)} %get-tuple-element.58), channel_id=1, source_target_pairs={{0,1},{1,0},{2,3},{3,2},{4,5},{5,4},{6,7},{7,6},{8,9},{9,8},{10,11... | collective-permute-start | bytes 98312 | tf_op jit(solution)/shard_map/ppermute | solution.py:248
  70.2 5.8 %collective-permute-start.21 = (bf16[8,2048]{1,0:T(8,128)(2,1)S(1)}, bf16[8,2048]{1,0:T(8,128)(2,1)S(1)}, u32[]{:S(2)}, u32[]{:S(2)}) collective-permute-start(bf16[8,2048]{1,0:T(8,128)(2,1)S(1)} %get-tuple-element.59), channel_id=1, source_target_pairs={{0,3},{1,2},{2,1},{3,0},{4,7},{5,6},{6,5},{7,4},{8,11},{9,10},{10,... | collective-permute-start | bytes 98312 | tf_op jit(solution)/shard_map/ppermute | solution.py:248
  71.8 5.1 %collective-permute-start.20 = (bf16[8,2048]{1,0:T(8,128)(2,1)S(1)}, bf16[8,2048]{1,0:T(8,128)(2,1)S(1)}, u32[]{:S(2)}, u32[]{:S(2)}) collective-permute-start(bf16[8,2048]{1,0:T(8,128)(2,1)S(1)} %get-tuple-element.60), channel_id=1, source_target_pairs={{0,2},{1,3},{2,0},{3,1},{4,6},{5,7},{6,4},{7,5},{8,10},{9,11},{10,... | collective-permute-start | bytes 98312 | tf_op jit(solution)/shard_map/ppermute | solution.py:248

commit v5 on v4

--- a/solution.py
+++ b/solution.py
@@ -85,6 +85,10 @@
     return own, picker
 
 
+def in_vmem(value):
+    return pltpu.with_memory_space_constraint(value, pltpu.VMEM)
+
+
 def stage_kernel(head_ref, token_ref, out_ref, sem):
     copy = pltpu.make_async_copy(head_ref, out_ref, sem)
     copy.start()
@@ -95,7 +99,7 @@
     return pl.pallas_call(
         stage_kernel,
         in_specs=[pl.BlockSpec(memory_space=pltpu.HBM), pl.BlockSpec(memory_space=pl.ANY)],
-        out_shape=jax.ShapeDtypeStruct(head.shape, head.dtype),
+        out_shape=pltpu.VMEM(head.shape, head.dtype),
         scratch_shapes=[pltpu.SemaphoreType.DMA],
         cost_estimate=cost(0, 2 * head.size * 2),
         compiler_params=params(),
@@ -144,7 +148,7 @@
         cost_estimate=cost(2 * rows * width * shard, 2 * width * (shard + rows)),
         compiler_params=params(),
         name="local_logits",
-    )(near, far, head, picker)
+    )(near, far, in_vmem(head), picker)
 
 
 def merged(stats):
@@ -231,12 +235,76 @@
         cost_estimate=cost(2 * rows * width * shard, 2 * width * (shard + rows)),
         compiler_params=params(),
         name="gradients",
-    )(stats, logits, head)
+    )(stats, logits, in_vmem(head))
+
+
+def split_kernel(near_ref, moved_ref, mine_ref, *block_refs):
+    mine_ref[...] = near_ref[0].astype(F32) + moved_ref[0].astype(F32)
+    for g, block_ref in enumerate(block_refs, 1):
+        total = near_ref[g].astype(F32) + moved_ref[g].astype(F32)
+        block_ref[...] = total.astype(BF16)
+
+
+def split(near, moved):
+    block = near.shape[1:]
+    return pl.pallas_call(
+        split_kernel,
+        out_shape=[jax.ShapeDtypeStruct(block, F32)]
+        + [jax.ShapeDtypeStruct(block, BF16)] * (near.shape[0] - 1),
+        cost_estimate=cost(0, 6 * near.size),
+        compiler_params=params(),
+        name="add_cores",
+    )(near, moved)
+
+
+def plane_kernel(mine_ref, *refs):
+    n_vocab = mine_ref.shape[0]
+    column = lax.axis_index("vocab")
+    moved_refs, out_refs = refs[:-n_vocab], refs[-n_vocab:]
+    for k, out_ref in enumerate(out_refs):
+        total = mine_ref[column ^ k]
+        for moved_ref in moved_refs:
+            total = total + moved_ref[column ^ k].astype(F32)
+        out_ref[...] = total.astype(out_ref.dtype)
+
+
+def plane_sum(mine, moved):
+    n_vocab, rows, wide = mine.shape
+    return pl.pallas_call(
+        plane_kernel,
+        out_shape=[jax.ShapeDtypeStruct((rows, wide), F32)]
+        + [jax.ShapeDtypeStruct((rows, wide), BF16)] * (n_vocab - 1),
+        cost_estimate=cost(0, 10 * mine.size),
+        compiler_params=params(),
+        name="add_chips",
+    )(mine, *moved)
+
+
+def place_kernel(n_vocab, picker_ref, *refs):
+    *parts, out_ref = refs
+    rows = []
+    for h in range(HALVES):
+        total = parts[h * n_vocab][...]
+        for part in parts[h * n_vocab + 1 : (h + 1) * n_vocab]:
+            total = total + part[...].astype(F32)
+        rows.append(total)
+    result = jnp.concatenate(rows, axis=0).astype(BF16)
+    out_ref[...] = lax.dot_general(
+        picker_ref[...], result, (((0,), (0,)), ((), ())), preferred_element_type=F32
+    ).astype(BF16)
+
+
+def place(n_vocab, picker, parts):
+    return pl.pallas_call(
+        functools.partial(place_kernel, n_vocab),
+        out_shape=jax.ShapeDtypeStruct((picker.shape[1], parts[0].shape[1]), BF16),
+        compiler_params=params(),
+        name="place_rows",
+    )(picker, *parts)
 
 
 def body(n_seq, n_vocab, hidden, head, mask):
     n_chip = n_seq // 2
-    column = lax.axis_index("vocab")
 
     def swap_core(value):
         return lax.ppermute(value, "seq", [(i, i ^ 1) for i in range(n_seq)])
@@ -250,36 +318,29 @@
     own, picker = select(mask, hidden)
     head = stage(head, own[0])
 
-    logits, stats = [], []
+    logits, sent, stats = [], [], []
     for h in range(HALVES):
-        near = [own[h]] + [send_chip(own[h], g) for g in range(1, n_chip)]
+        source = [own[h]] * n_chip
+        if h == 0:
+            source[-1], head = lax.optimization_barrier((source[-1], head))
+        near = [own[h]] + [send_chip(source[g], g) for g in range(1, n_chip)]
         near, _ = lax.optimization_barrier((near, logits[-1:]))
         near = jnp.concatenate(near, axis=0)
-        part, sent = local_logits(n_seq, n_vocab, near, swap_core(near), head, picker)
+        part, lines = local_logits(n_seq, n_vocab, near, swap_core(near), head, picker)
         logits.append(part)
-        stats.append(lax.all_to_all(sent, ("seq", "vocab"), 0, 0, tiled=True))
-
+        sent.append(lines)
+        stats.append(lax.all_to_all(lines, ("seq", "vocab"), 0, 0, tiled=True))
+
+    parts = []
+    for h in range(HALVES):
+        lines, _ = lax.optimization_barrier((stats[h], logits))
+        near, far = gradients(n_seq, n_vocab, lines, logits[h], head)
+        mine, *blocks = split(near, swap_core(far))
+        moved = [send_chip(block, g) for g, block in enumerate(blocks, 1)]
+        mine, *pieces = plane_sum(mine, moved)
+        parts += [mine] + [send_vocab(piece, k) for k, piece in enumerate(pieces, 1)]
+    derivative = place(n_vocab, picker, parts)
     each, average = entropies(n_vocab, stats, picker)
-
-    results = []
-    for h in range(HALVES):
-        near, far = gradients(n_seq, n_vocab, stats[h], logits[h], head)
-        here = near.astype(F32) + swap_core(far).astype(F32)
-        sums = here[0]
-        for g in range(1, n_chip):
-            sums = sums + send_chip(here[g].astype(BF16), g).astype(F32)
-
-        def piece(k):
-            return lax.dynamic_index_in_dim(sums, column ^ k, 0, keepdims=False)
-
-        result = piece(0)
-        for k in range(1, n_vocab):
-            result = result + send_vocab(piece(k).astype(BF16), k).astype(F32)
-        results.append(result)
-    result = jnp.concatenate(results, axis=0).astype(BF16)
-    derivative = lax.dot_general(
-        picker, result, (((0,), (0,)), ((), ())), preferred_element_type=F32
-    ).astype(BF16)
     return each.reshape(-1), average.reshape(()), derivative
 
 

time: 78.5 us -> 76.9 us (0.980)
  Pallas kernels: 11.8 us -> 13.2 us
  other arithmetic: 1.37 us -> 0 us
  matrix products: 1.12 us -> 0 us
  starting transfers between devices: 31 us -> 30.1 us
  local copies, waits for them, and re-layouts: 7.8 us -> 8.62 us
    ppermute x12, waiting for transfers between devices: 8.83 us -> 12.7 us  [send_chip(): return lax.ppermute(value, 'seq', [(i, i ^ 2 * chip) for i in range(n_seq)])]
    all_to_all x2, waiting for transfers between devices: 12 us -> 8.9 us  [body(): stats.append(lax.all_to_all(lines, ('seq', 'vocab'), 0, 0, tiled=True))]
    unnamed x14, local copies, waits for them, and re-layouts: 6.95 us -> 8.6 us
    pallas_call x0 -> x5, Pallas kernels: none -> 1.46 us  [the longest x1 1.11 us: place(): pl.pallas_call(functools.partial(place_kernel, n_vocab), out_shape=jax.Sh...]
    ppermute x12, starting transfers between devices: 15.2 us -> 14 us  [send_chip(): return lax.ppermute(value, 'seq', [(i, i ^ 2 * chip) for i in range(n_seq)])]
    ppermute x6, waiting for transfers between devices: 3.31 us -> 2.19 us  [send_vocab(): return lax.ppermute(value, 'vocab', [(i, i ^ k) for i in range(n_vocab)])]
    dot_general x1 -> x0, matrix products: 1.12 us -> none  [body(): lax.dot_general(picker, result, (((0,), (0,)), ((), ())), preferred_eleme...]
    add x2 -> x0, other arithmetic: 1.04 us -> none  [body(): sums = sums + send_chip(here[g].astype(BF16), g).astype(F32)]
  transfers between devices with their start and end apart: 24 -> 24, of which waited for: 12 -> 10; matrix products, arithmetic and copies ran while one was open for 3% -> 0% of each run, Pallas kernels for 12% -> 13%
where the time goes in v5:
time: 76.9 us; the launch traced here: 76.5 us
  starting transfers between devices  30.1 us (39%)
  waiting for transfers between devices  23.8 us (31%)
  Pallas kernels  13.2 us (17%)
  local copies, waits for them, and re-layouts  8.62 us (11%)
  between operations  0.85 us (1%)
    ppermute x12, starting transfers between devices, send_chip(): return lax.ppermute(value, 'seq', [(i, i ^ 2 * chip) for i in range(n_seq)])  14 us
    ppermute x12, waiting for transfers between devices, send_chip(): return lax.ppermute(value, 'seq', [(i, i ^ 2 * chip) for i in range(n_seq)])  12.7 us
    all_to_all x2, waiting for transfers between devices, body(): stats.append(lax.all_to_all(lines, ('seq', 'vocab'), 0, 0, tiled=True))  8.9 us
    unnamed x14, local copies, waits for them, and re-layouts  8.6 us
    ppermute x6, starting transfers between devices, send_vocab(): return lax.ppermute(value, 'vocab', [(i, i ^ k) for i in range(n_vocab)])  8.19 us
    all_to_all x2, starting transfers between devices, body(): stats.append(lax.all_to_all(lines, ('seq', 'vocab'), 0, 0, tiled=True))  7.57 us
    pallas_call x2, Pallas kernels, local_logits(): pl.pallas_call(functools.partial(logits_kernel, n_seq), out_shape=[jax.Sh...  3.51 us
    pallas_call x2, Pallas kernels, gradients(): pl.pallas_call(functools.partial(gradient_kernel, n_seq), out_shape=[out,...  3.12 us
  transfers between devices with their start and end apart: 24, of which 10 were waited for; matrix products, arithmetic and copies ran while one was open for 0% of the time, Pallas kernels for 13%

profile of v5, /device:TPU:0, one launch (start us, length us, event | category | flops | bytes accessed | tf_op | source)
XLA Modules:
  0.0 76.5 jit_solution(12940032686700819111)
XLA Ops:
  0.6 2.1 %select_rows.1 = (bf16[8,8192]{1,0:T(8,128)(2,1)S(1)}, bf16[8,8192]{1,0:T(8,128)(2,1)S(1)}, bf16[16,128]{1,0:T(8,128)(2,1)S(1)}) custom-call(s32[1,128]{1,0:T(1,128)} %bitcast.3, bf16[128,8192]{1,0:T(8,128)(2,1)} %hidden_ref.1), custom_call_target="tpu_custom_call" | custom-call | tf_op jit(solution)/shard_map/select_rows/pallas_call | solution.py:72
  2.7 3.0 %collective-permute-start = (bf16[8,8192]{1,0:T(8,128)(2,1)S(1)}, bf16[8,8192]{1,0:T(8,128)(2,1)S(1)}, u32[]{:S(2)}, u32[]{:S(2)}) collective-permute-start(bf16[8,8192]{1,0:T(8,128)(2,1)S(1)} %get-tuple-element.46.token_ref), channel_id=1, source_target_pairs={{0,8},{4,12},{8,0},{12,4},{16,24},{20,28},{24,16},{28,20},{1,9},{5... | collective-permute-start | bytes 393224 | tf_op jit(solution)/shard_map/ppermute | solution.py:313
  5.7 1.5 %collective-permute-start.1 = (bf16[8,8192]{1,0:T(8,128)(2,1)S(1)}, bf16[8,8192]{1,0:T(8,128)(2,1)S(1)}, u32[]{:S(2)}, u32[]{:S(2)}) collective-permute-start(bf16[8,8192]{1,0:T(8,128)(2,1)S(1)} %get-tuple-element.46.token_ref), channel_id=1, source_target_pairs={{0,16},{4,20},{8,24},{12,28},{16,0},{20,4},{24,8},{28,12},{1,17},{... | collective-permute-start | bytes 393224 | tf_op jit(solution)/shard_map/ppermute | solution.py:313
  7.3 2.2 %stage_head.1.head_ref = bf16[8192,256]{1,0:T(8,128)(2,1)S(1)} custom-call(bf16[8192,256]{1,0:T(8,128)(2,1)} %head_ref.1, bf16[8,8192]{1,0:T(8,128)(2,1)S(1)} %get-tuple-element.46.token_ref), custom_call_target="tpu_custom_call" | custom-call | bytes 8388608 | tf_op jit(solution)/shard_map/stage_head/pallas_call | solution.py:99
  9.5 0.1 collective-permute-start.2
  9.6 1.2 %collective-permute-done.1 = bf16[8,8192]{1,0:T(8,128)(2,1)S(1)} collective-permute-done((bf16[8,8192]{1,0:T(8,128)(2,1)S(1)}, bf16[8,8192]{1,0:T(8,128)(2,1)S(1)}, u32[]{:S(2)}, u32[]{:S(2)}) %collective-permute-start.1) | collective-permute-done | bytes 131104 | tf_op jit(solution)/shard_map/ppermute | solution.py:313
  10.7 4.7 %collective-permute-done.2 = bf16[8,8192]{1,0:T(8,128)(2,1)S(1)} collective-permute-done((bf16[8,8192]{1,0:T(8,128)(2,1)S(1)}, bf16[8,8192]{1,0:T(8,128)(2,1)S(1)}, u32[]{:S(2)}, u32[]{:S(2)}) %collective-permute-start.2) | collective-permute-done | bytes 131104 | tf_op jit(solution)/shard_map/ppermute | solution.py:313
  15.5 0.1 collective-permute-start.3
  15.5 0.6 collective-permute-start.4
  16.2 2.9 %collective-permute-start.6 = (bf16[8,8192]{1,0:T(8,128)(2,1)S(1)}, bf16[8,8192]{1,0:T(8,128)(2,1)S(1)}, u32[]{:S(2)}, u32[]{:S(2)}) collective-permute-start(bf16[8,8192]{1,0:T(8,128)(2,1)S(1)} %get-tuple-element.55), channel_id=1, source_target_pairs={{0,24},{4,28},{8,16},{12,20},{16,8},{20,12},{24,0},{28,4},{1,25},{... | collective-permute-start | bytes 393224 | tf_op jit(solution)/shard_map/ppermute | solution.py:313
  19.1 1.7 %local_logits.2 = (f32[64,256]{1,0:T(8,128)S(1)}, f32[32,8,128]{2,1,0:T(8,128)}) custom-call(bf16[32,8192]{1,0:T(8,128)(2,1)S(1)} %constant_dynamic-update-slice_fusion.near_ref, bf16[32,8192]{1,0:T(8,128)(2,1)S(1)} %collective-permute-done.3.far_ref, bf16[8192,256]{1,0:T(8,128)(2,1)S(1)} %stage_head.1.head_ref, ...), custom_call_target="tpu_custom_call" | custom-call | flops 268435456 | bytes 5242880 | tf_op jit(solution)/shard_map/local_logits/pallas_call | solution.py:141
  20.9 2.0 %copy-done = bf16[8192,256]{1,0:T(8,128)(2,1)} copy-done((bf16[8192,256]{1,0:T(8,128)(2,1)}, bf16[8192,256]{1,0:T(8,128)(2,1)S(1)}, u32[]{:S(2)}) %copy-start) | copy-done | bytes 4194328
  22.8 1.7 %collective-permute-done.5 = bf16[8,8192]{1,0:T(8,128)(2,1)S(1)} collective-permute-done((bf16[8,8192]{1,0:T(8,128)(2,1)S(1)}, bf16[8,8192]{1,0:T(8,128)(2,1)S(1)}, u32[]{:S(2)}, u32[]{:S(2)}) %collective-permute-start.5) | collective-permute-done | bytes 131104 | tf_op jit(solution)/shard_map/ppermute | solution.py:313
  24.6 0.1 collective-permute-start.7
  24.7 5.0 %all-to-all-start = ((f32[32,8,128]{2,1,0:T(8,128)}), f32[32,8,128]{2,1,0:T(8,128)S(1)}, u32[]{:S(2)}, u32[]{:S(2)}) async-start(f32[32,8,128]{2,1,0:T(8,128)} %get-tuple-element.52), calls=%async_computation | async-start | bytes 262144 | tf_op jit(solution)/shard_map/all_to_all | solution.py:332
  29.7 2.2 %copy-done.1 = bf16[8192,256]{1,0:T(8,128)(2,1)S(1)} copy-done((bf16[8192,256]{1,0:T(8,128)(2,1)S(1)}, bf16[8192,256]{1,0:T(8,128)(2,1)}, u32[]{:S(2)}) %copy-start.1) | copy-done | bytes 4194328
  31.9 1.8 %local_logits.3 = (f32[64,256]{1,0:T(8,128)S(1)}, f32[32,8,128]{2,1,0:T(8,128)}) custom-call(bf16[32,8192]{1,0:T(8,128)(2,1)S(1)} %constant_dynamic-update-slice_fusion.4.near_ref, bf16[32,8192]{1,0:T(8,128)(2,1)S(1)} %collective-permute-done.7.far_ref, bf16[8192,256]{1,0:T(8,128)(2,1)S(1)} %copy-done.1, bf16[16,128]{1,0:T(8,128)(2,1)S(1)} %get-tuple-element.51.picker_ref.refs_2_), custom_call_target="tpu_custom_call" | custom-call | flops 268435456 | bytes 5242880 | tf_op jit(solution)/shard_map/local_logits/pallas_call | solution.py:141
  33.6 4.4 %all-to-all-done.refs_0_.stats_ref = f32[32,8,128]{2,1,0:T(8,128)S(1)} async-done(((f32[32,8,128]{2,1,0:T(8,128)}), f32[32,8,128]{2,1,0:T(8,128)S(1)}, u32[]{:S(2)}, u32[]{:S(2)}) %all-to-all-start) | async-done | bytes 131104 | tf_op jit(solution)/shard_map/all_to_all | solution.py:332
  38.1 2.6 %all-to-all-start.1 = ((f32[32,8,128]{2,1,0:T(8,128)}), f32[32,8,128]{2,1,0:T(8,128)S(1)}, u32[]{:S(2)}, u32[]{:S(2)}) async-start(f32[32,8,128]{2,1,0:T(8,128)} %get-tuple-element.59), calls=%async_computation.1 | async-start | bytes 262144 | tf_op jit(solution)/shard_map/all_to_all | solution.py:332
  40.7 2.2 %copy-done.2 = bf16[8192,256]{1,0:T(8,128)(2,1)S(1)} copy-done((bf16[8192,256]{1,0:T(8,128)(2,1)S(1)}, bf16[8192,256]{1,0:T(8,128)(2,1)}, u32[]{:S(2)}) %copy-start.2) | copy-done | bytes 4194328
  42.9 1.6 %gradients.2 = (bf16[4,4,8,2048]{3,2,1,0:T(8,128)(2,1)S(1)}, bf16[4,4,8,2048]{3,2,1,0:T(8,128)(2,1)S(1)}) custom-call(f32[32,8,128]{2,1,0:T(8,128)S(1)} %all-to-all-done.refs_0_.stats_ref, f32[64,256]{1,0:T(8,128)S(1)} %get-tuple-element.54.logits_ref, bf16[8192,256]{1,0:T(8,128)(2,1)S(1)} %copy-done.2), custom_call_target="tpu_custom_call" | custom-call | flops 268435456 | bytes 5242880 | tf_op jit(solution)/shard_map/gradients/pallas_call | solution.py:228
  44.4 0.2 collective-permute-start.8
  44.6 4.5 %all-to-all-done.1.refs_1_.stats_ref = f32[32,8,128]{2,1,0:T(8,128)S(1)} async-done(((f32[32,8,128]{2,1,0:T(8,128)}), f32[32,8,128]{2,1,0:T(8,128)S(1)}, u32[]{:S(2)}, u32[]{:S(2)}) %all-to-all-start.1) | async-done | bytes 131104 | tf_op jit(solution)/shard_map/all_to_all | solution.py:332
  49.1 2.2 %copy-done.3 = bf16[8192,256]{1,0:T(8,128)(2,1)S(1)} copy-done((bf16[8192,256]{1,0:T(8,128)(2,1)S(1)}, bf16[8192,256]{1,0:T(8,128)(2,1)}, u32[]{:S(2)}) %copy-start.3) | copy-done | bytes 4194328
  51.3 1.6 %gradients.3 = (bf16[4,4,8,2048]{3,2,1,0:T(8,128)(2,1)S(1)}, bf16[4,4,8,2048]{3,2,1,0:T(8,128)(2,1)S(1)}) custom-call(f32[32,8,128]{2,1,0:T(8,128)S(1)} %all-to-all-done.1.refs_1_.stats_ref, f32[64,256]{1,0:T(8,128)S(1)} %get-tuple-element.62.logits_ref, bf16[8192,256]{1,0:T(8,128)(2,1)S(1)} %copy-done.3), custom_call_target="tpu_custom_call" | custom-call | flops 268435456 | bytes 5242880 | tf_op jit(solution)/shard_map/gradients/pallas_call | solution.py:228
  52.8 0.1 collective-permute-start.15
  52.9 0.1 add_cores.2
  53.0 0.8 %collective-permute-start.9 = (bf16[4,8,2048]{2,1,0:T(8,128)(2,1)S(1)}, bf16[4,8,2048]{2,1,0:T(8,128)(2,1)S(1)}, u32[]{:S(2)}, u32[]{:S(2)}) collective-permute-start(bf16[4,8,2048]{2,1,0:T(8,128)(2,1)S(1)} %get-tuple-element.67), channel_id=1, source_target_pairs={{0,8},{4,12},{8,0},{12,4},{16,24},{20,28},{24,16},{28,20},{1,9},{5... | collective-permute-start | bytes 393224 | tf_op jit(solution)/shard_map/ppermute | solution.py:313
  53.9 0.5 collective-permute-start.10
  54.4 2.2 %collective-permute-start.11 = (bf16[4,8,2048]{2,1,0:T(8,128)(2,1)S(1)}, bf16[4,8,2048]{2,1,0:T(8,128)(2,1)S(1)}, u32[]{:S(2)}, u32[]{:S(2)}) collective-permute-start(bf16[4,8,2048]{2,1,0:T(8,128)(2,1)S(1)} %get-tuple-element.69), channel_id=1, source_target_pairs={{0,24},{4,28},{8,16},{12,20},{16,8},{20,12},{24,0},{28,4},{1,25},{... | collective-permute-start | bytes 393224 | tf_op jit(solution)/shard_map/ppermute | solution.py:313
  56.6 0.1 add_cores.3
  56.7 0.8 %collective-permute-start.16 = (bf16[4,8,2048]{2,1,0:T(8,128)(2,1)S(1)}, bf16[4,8,2048]{2,1,0:T(8,128)(2,1)S(1)}, u32[]{:S(2)}, u32[]{:S(2)}) collective-permute-start(bf16[4,8,2048]{2,1,0:T(8,128)(2,1)S(1)} %get-tuple-element.78), channel_id=1, source_target_pairs={{0,8},{4,12},{8,0},{12,4},{16,24},{20,28},{24,16},{28,20},{1,9},{5... | collective-permute-start | bytes 393224 | tf_op jit(solution)/shard_map/ppermute | solution.py:313
  57.5 0.5 collective-permute-start.17
  58.1 1.3 %collective-permute-done.9.refs_0_ = bf16[4,8,2048]{2,1,0:T(8,128)(2,1)S(1)} collective-permute-done((bf16[4,8,2048]{2,1,0:T(8,128)(2,1)S(1)}, bf16[4,8,2048]{2,1,0:T(8,128)(2,1)S(1)}, u32[]{:S(2)}, u32[]{:S(2)}) %collective-permute-start.9) | collective-permute-done | bytes 131104 | tf_op jit(solution)/shard_map/ppermute | solution.py:313
  59.4 0.9 %collective-permute-start.18 = (bf16[4,8,2048]{2,1,0:T(8,128)(2,1)S(1)}, bf16[4,8,2048]{2,1,0:T(8,128)(2,1)S(1)}, u32[]{:S(2)}, u32[]{:S(2)}) collective-permute-start(bf16[4,8,2048]{2,1,0:T(8,128)(2,1)S(1)} %get-tuple-element.80), channel_id=1, source_target_pairs={{0,24},{4,28},{8,16},{12,20},{16,8},{20,12},{24,0},{28,4},{1,25},{... | collective-permute-start | bytes 393224 | tf_op jit(solution)/shard_map/ppermute | solution.py:313
  60.3 2.2 %collective-permute-done.10.refs_1_ = bf16[4,8,2048]{2,1,0:T(8,128)(2,1)S(1)} collective-permute-done((bf16[4,8,2048]{2,1,0:T(8,128)(2,1)S(1)}, bf16[4,8,2048]{2,1,0:T(8,128)(2,1)S(1)}, u32[]{:S(2)}, u32[]{:S(2)}) %collective-permute-start.10) | collective-permute-done | bytes 131104 | tf_op jit(solution)/shard_map/ppermute | solution.py:313
  62.5 0.1 add_chips.2
  62.6 0.4 collective-permute-start.12
  62.9 1.4 %collective-permute-start.13 = (bf16[8,2048]{1,0:T(8,128)(2,1)S(1)}, bf16[8,2048]{1,0:T(8,128)(2,1)S(1)}, u32[]{:S(2)}, u32[]{:S(2)}) collective-permute-start(bf16[8,2048]{1,0:T(8,128)(2,1)S(1)} %get-tuple-element.72), channel_id=1, source_target_pairs={{0,2},{1,3},{2,0},{3,1},{4,6},{5,7},{6,4},{7,5},{8,10},{9,11},{10,... | collective-permute-start | bytes 98312 | tf_op jit(solution)/shard_map/ppermute | solution.py:316
  64.3 0.7 collective-permute-done.16.refs_0_
  65.1 2.0 %collective-permute-start.14 = (bf16[8,2048]{1,0:T(8,128)(2,1)S(1)}, bf16[8,2048]{1,0:T(8,128)(2,1)S(1)}, u32[]{:S(2)}, u32[]{:S(2)}) collective-permute-start(bf16[8,2048]{1,0:T(8,128)(2,1)S(1)} %get-tuple-element.73), channel_id=1, source_target_pairs={{0,3},{1,2},{2,1},{3,0},{4,7},{5,6},{6,5},{7,4},{8,11},{9,10},{10,... | collective-permute-start | bytes 98312 | tf_op jit(solution)/shard_map/ppermute | solution.py:316
  67.0 0.8 %collective-permute-done.17.refs_1_ = bf16[4,8,2048]{2,1,0:T(8,128)(2,1)S(1)} collective-permute-done((bf16[4,8,2048]{2,1,0:T(8,128)(2,1)S(1)}, bf16[4,8,2048]{2,1,0:T(8,128)(2,1)S(1)}, u32[]{:S(2)}, u32[]{:S(2)}) %collective-permute-start.17) | collective-permute-done | bytes 131104 | tf_op jit(solution)/shard_map/ppermute | solution.py:313
  68.0 0.1 collective-permute-start.19
  68.0 1.7 %collective-permute-start.20 = (bf16[8,2048]{1,0:T(8,128)(2,1)S(1)}, bf16[8,2048]{1,0:T(8,128)(2,1)S(1)}, u32[]{:S(2)}, u32[]{:S(2)}) collective-permute-start(bf16[8,2048]{1,0:T(8,128)(2,1)S(1)} %get-tuple-element.83), channel_id=1, source_target_pairs={{0,2},{1,3},{2,0},{3,1},{4,6},{5,7},{6,4},{7,5},{8,10},{9,11},{10,... | collective-permute-start | bytes 98312 | tf_op jit(solution)/shard_map/ppermute | solution.py:316
  69.7 2.7 %collective-permute-start.21 = (bf16[8,2048]{1,0:T(8,128)(2,1)S(1)}, bf16[8,2048]{1,0:T(8,128)(2,1)S(1)}, u32[]{:S(2)}, u32[]{:S(2)}) collective-permute-start(bf16[8,2048]{1,0:T(8,128)(2,1)S(1)} %get-tuple-element.84), channel_id=1, source_target_pairs={{0,3},{1,2},{2,1},{3,0},{4,7},{5,6},{6,5},{7,4},{8,11},{9,10},{10,... | collective-permute-start | bytes 98312 | tf_op jit(solution)/shard_map/ppermute | solution.py:316
  72.4 0.8 %entropies.1 = (f32[1,128]{1,0:T(1,128)}, f32[1,1]{1,0:T(1,128)}) custom-call(f32[32,8,128]{2,1,0:T(8,128)S(1)} %all-to-all-done.refs_0_.stats_ref, f32[32,8,128]{2,1,0:T(8,128)S(1)} %all-to-all-done.1.refs_1_.stats_ref, bf16[16,128]{1,0:T(8,128)(2,1)S(1)} %get-tuple-element.51.picker_ref.refs_2_), custom_call_target="tpu_custom_call" | custom-call | bytes 1048576 | tf_op jit(solution)/shard_map/entropies/pallas_call | solution.py:187
  73.2 2.2 %collective-permute-done.21.refs_7_ = bf16[8,2048]{1,0:T(8,128)(2,1)S(1)} collective-permute-done((bf16[8,2048]{1,0:T(8,128)(2,1)S(1)}, bf16[8,2048]{1,0:T(8,128)(2,1)S(1)}, u32[]{:S(2)}, u32[]{:S(2)}) %collective-permute-start.21) | collective-permute-done | bytes 32800 | tf_op jit(solution)/shard_map/ppermute | solution.py:316
  75.4 1.1 %place_rows.1 = bf16[128,2048]{1,0:T(8,128)(2,1)} custom-call(bf16[16,128]{1,0:T(8,128)(2,1)S(1)} %get-tuple-element.51.picker_ref.refs_2_, f32[8,2048]{1,0:T(8,128)S(1)} %get-tuple-element.70.refs_0_, bf16[8,2048]{1,0:T(8,128)(2,1)S(1)} %collective-permute-done.12.refs_1_, bf16[8,2048]{1,0:T(8,128)(2,1)S(1)} %collective-permute-done.13.refs_2_, ...), custom_call_target="tpu_custom_call" | custom-call | tf_op jit(solution)/shard_map/place_rows/pallas_call | solution.py:298
  (28 shorter events, 0.2 us)
Async XLA Ops:
  2.7 6.8 %collective-permute-start = (bf16[8,8192]{1,0:T(8,128)(2,1)S(1)}, bf16[8,8192]{1,0:T(8,128)(2,1)S(1)}, u32[]{:S(2)}, u32[]{:S(2)}) collective-permute-start(bf16[8,8192]{1,0:T(8,128)(2,1)S(1)} %get-tuple-element.46.token_ref), channel_id=1, source_target_pairs={{0,8},{4,12},{8,0},{12,4},{16,24},{20,28},{24,16},{28,20},{1,9},{5... | collective-permute-start | bytes 393224 | tf_op jit(solution)/shard_map/ppermute | solution.py:313
  5.7 5.0 %collective-permute-start.1 = (bf16[8,8192]{1,0:T(8,128)(2,1)S(1)}, bf16[8,8192]{1,0:T(8,128)(2,1)S(1)}, u32[]{:S(2)}, u32[]{:S(2)}) collective-permute-start(bf16[8,8192]{1,0:T(8,128)(2,1)S(1)} %get-tuple-element.46.token_ref), channel_id=1, source_target_pairs={{0,16},{4,20},{8,24},{12,28},{16,0},{20,4},{24,8},{28,12},{1,17},{... | collective-permute-start | bytes 393224 | tf_op jit(solution)/shard_map/ppermute | solution.py:313
  9.5 5.9 %collective-permute-start.2 = (bf16[8,8192]{1,0:T(8,128)(2,1)S(1)}, bf16[8,8192]{1,0:T(8,128)(2,1)S(1)}, u32[]{:S(2)}, u32[]{:S(2)}) collective-permute-start(bf16[8,8192]{1,0:T(8,128)(2,1)S(1)} %get-tuple-element.46.token_ref), channel_id=1, source_target_pairs={{0,24},{4,28},{8,16},{12,20},{16,8},{20,12},{24,0},{28,4},{1,25},{... | collective-permute-start | bytes 393224 | tf_op jit(solution)/shard_map/ppermute | solution.py:313
  15.5 3.6 %collective-permute-start.3 = (bf16[32,8192]{1,0:T(8,128)(2,1)S(1)}, bf16[32,8192]{1,0:T(8,128)(2,1)S(1)}, u32[]{:S(2)}, u32[]{:S(2)}) collective-permute-start(bf16[32,8192]{1,0:T(8,128)(2,1)S(1)} %constant_dynamic-update-slice_fusion.near_ref), channel_id=1, source_target_pairs={{0,4},{4,0},{8,12},{12,8},{16,20},{20,16},{24,28},{28,24},{1,5},{5... | collective-permute-start | bytes 1572872 | tf_op jit(solution)/shard_map/ppermute | solution.py:310
  15.5 7.3 %collective-permute-start.4 = (bf16[8,8192]{1,0:T(8,128)(2,1)S(1)}, bf16[8,8192]{1,0:T(8,128)(2,1)S(1)}, u32[]{:S(2)}, u32[]{:S(2)}) collective-permute-start(bf16[8,8192]{1,0:T(8,128)(2,1)S(1)} %get-tuple-element.55), channel_id=1, source_target_pairs={{0,8},{4,12},{8,0},{12,4},{16,24},{20,28},{24,16},{28,20},{1,9},{5... | collective-permute-start | bytes 393224 | tf_op jit(solution)/shard_map/ppermute | solution.py:313
  16.1 8.4 %collective-permute-start.5 = (bf16[8,8192]{1,0:T(8,128)(2,1)S(1)}, bf16[8,8192]{1,0:T(8,128)(2,1)S(1)}, u32[]{:S(2)}, u32[]{:S(2)}) collective-permute-start(bf16[8,8192]{1,0:T(8,128)(2,1)S(1)} %get-tuple-element.55), channel_id=1, source_target_pairs={{0,16},{4,20},{8,24},{12,28},{16,0},{20,4},{24,8},{28,12},{1,17},{... | collective-permute-start | bytes 393224 | tf_op jit(solution)/shard_map/ppermute | solution.py:313
  16.2 8.3 %collective-permute-start.6 = (bf16[8,8192]{1,0:T(8,128)(2,1)S(1)}, bf16[8,8192]{1,0:T(8,128)(2,1)S(1)}, u32[]{:S(2)}, u32[]{:S(2)}) collective-permute-start(bf16[8,8192]{1,0:T(8,128)(2,1)S(1)} %get-tuple-element.55), channel_id=1, source_target_pairs={{0,24},{4,28},{8,16},{12,20},{16,8},{20,12},{24,0},{28,4},{1,25},{... | collective-permute-start | bytes 393224 | tf_op jit(solution)/shard_map/ppermute | solution.py:313
  20.9 2.0 %copy-start = (bf16[8192,256]{1,0:T(8,128)(2,1)}, bf16[8192,256]{1,0:T(8,128)(2,1)S(1)}, u32[]{:S(2)}) copy-start(bf16[8192,256]{1,0:T(8,128)(2,1)S(1)} %stage_head.1.head_ref) | copy-start | bytes 12582916
  24.6 5.1 %collective-permute-start.7 = (bf16[32,8192]{1,0:T(8,128)(2,1)S(1)}, bf16[32,8192]{1,0:T(8,128)(2,1)S(1)}, u32[]{:S(2)}, u32[]{:S(2)}) collective-permute-start(bf16[32,8192]{1,0:T(8,128)(2,1)S(1)} %constant_dynamic-update-slice_fusion.4.near_ref), channel_id=1, source_target_pairs={{0,4},{4,0},{8,12},{12,8},{16,20},{20,16},{24,28},{28,24},{1,5},{5... | collective-permute-start | bytes 1572872 | tf_op jit(solution)/shard_map/ppermute | solution.py:310
  24.7 13.4 %all-to-all-start = ((f32[32,8,128]{2,1,0:T(8,128)}), f32[32,8,128]{2,1,0:T(8,128)S(1)}, u32[]{:S(2)}, u32[]{:S(2)}) async-start(f32[32,8,128]{2,1,0:T(8,128)} %get-tuple-element.52), calls=%async_computation | async-start | bytes 262144 | tf_op jit(solution)/shard_map/all_to_all | solution.py:332
  29.7 2.2 %copy-start.1 = (bf16[8192,256]{1,0:T(8,128)(2,1)S(1)}, bf16[8192,256]{1,0:T(8,128)(2,1)}, u32[]{:S(2)}) copy-start(bf16[8192,256]{1,0:T(8,128)(2,1)} %copy-done) | copy-start | bytes 12582916
  38.1 11.0 %all-to-all-start.1 = ((f32[32,8,128]{2,1,0:T(8,128)}), f32[32,8,128]{2,1,0:T(8,128)S(1)}, u32[]{:S(2)}, u32[]{:S(2)}) async-start(f32[32,8,128]{2,1,0:T(8,128)} %get-tuple-element.59), calls=%async_computation.1 | async-start | bytes 262144 | tf_op jit(solution)/shard_map/all_to_all | solution.py:332
  40.7 2.2 %copy-start.2 = (bf16[8192,256]{1,0:T(8,128)(2,1)S(1)}, bf16[8192,256]{1,0:T(8,128)(2,1)}, u32[]{:S(2)}) copy-start(bf16[8192,256]{1,0:T(8,128)(2,1)} %copy-done) | copy-start | bytes 12582916
  44.4 8.5 %collective-permute-start.8 = (bf16[4,4,8,2048]{3,2,1,0:T(8,128)(2,1)S(1)}, bf16[4,4,8,2048]{3,2,1,0:T(8,128)(2,1)S(1)}, u32[]{:S(2)}, u32[]{:S(2)}) collective-permute-start(bf16[4,4,8,2048]{3,2,1,0:T(8,128)(2,1)S(1)} %get-tuple-element.65), channel_id=1, source_target_pairs={{0,4},{4,0},{8,12},{12,8},{16,20},{20,16},{24,28},{28,24},{1,5},{5... | collective-permute-start | bytes 1572872 | tf_op jit(solution)/shard_map/ppermute | solution.py:310
  49.1 2.2 %copy-start.3 = (bf16[8192,256]{1,0:T(8,128)(2,1)S(1)}, bf16[8192,256]{1,0:T(8,128)(2,1)}, u32[]{:S(2)}) copy-start(bf16[8192,256]{1,0:T(8,128)(2,1)} %copy-done) | copy-start | bytes 12582916
  52.8 3.8 %collective-permute-start.15 = (bf16[4,4,8,2048]{3,2,1,0:T(8,128)(2,1)S(1)}, bf16[4,4,8,2048]{3,2,1,0:T(8,128)(2,1)S(1)}, u32[]{:S(2)}, u32[]{:S(2)}) collective-permute-start(bf16[4,4,8,2048]{3,2,1,0:T(8,128)(2,1)S(1)} %get-tuple-element.76), channel_id=1, source_target_pairs={{0,4},{4,0},{8,12},{12,8},{16,20},{20,16},{24,28},{28,24},{1,5},{5... | collective-permute-start | bytes 1572872 | tf_op jit(solution)/shard_map/ppermute | solution.py:310
  53.0 6.4 %collective-permute-start.9 = (bf16[4,8,2048]{2,1,0:T(8,128)(2,1)S(1)}, bf16[4,8,2048]{2,1,0:T(8,128)(2,1)S(1)}, u32[]{:S(2)}, u32[]{:S(2)}) collective-permute-start(bf16[4,8,2048]{2,1,0:T(8,128)(2,1)S(1)} %get-tuple-element.67), channel_id=1, source_target_pairs={{0,8},{4,12},{8,0},{12,4},{16,24},{20,28},{24,16},{28,20},{1,9},{5... | collective-permute-start | bytes 393224 | tf_op jit(solution)/shard_map/ppermute | solution.py:313
  53.9 8.7 %collective-permute-start.10 = (bf16[4,8,2048]{2,1,0:T(8,128)(2,1)S(1)}, bf16[4,8,2048]{2,1,0:T(8,128)(2,1)S(1)}, u32[]{:S(2)}, u32[]{:S(2)}) collective-permute-start(bf16[4,8,2048]{2,1,0:T(8,128)(2,1)S(1)} %get-tuple-element.68), channel_id=1, source_target_pairs={{0,16},{4,20},{8,24},{12,28},{16,0},{20,4},{24,8},{28,12},{1,17},{... | collective-permute-start | bytes 393224 | tf_op jit(solution)/shard_map/ppermute | solution.py:313
  54.4 8.1 %collective-permute-start.11 = (bf16[4,8,2048]{2,1,0:T(8,128)(2,1)S(1)}, bf16[4,8,2048]{2,1,0:T(8,128)(2,1)S(1)}, u32[]{:S(2)}, u32[]{:S(2)}) collective-permute-start(bf16[4,8,2048]{2,1,0:T(8,128)(2,1)S(1)} %get-tuple-element.69), channel_id=1, source_target_pairs={{0,24},{4,28},{8,16},{12,20},{16,8},{20,12},{24,0},{28,4},{1,25},{... | collective-permute-start | bytes 393224 | tf_op jit(solution)/shard_map/ppermute | solution.py:313
  56.7 8.3 %collective-permute-start.16 = (bf16[4,8,2048]{2,1,0:T(8,128)(2,1)S(1)}, bf16[4,8,2048]{2,1,0:T(8,128)(2,1)S(1)}, u32[]{:S(2)}, u32[]{:S(2)}) collective-permute-start(bf16[4,8,2048]{2,1,0:T(8,128)(2,1)S(1)} %get-tuple-element.78), channel_id=1, source_target_pairs={{0,8},{4,12},{8,0},{12,4},{16,24},{20,28},{24,16},{28,20},{1,9},{5... | collective-permute-start | bytes 393224 | tf_op jit(solution)/shard_map/ppermute | solution.py:313
  57.5 10.4 %collective-permute-start.17 = (bf16[4,8,2048]{2,1,0:T(8,128)(2,1)S(1)}, bf16[4,8,2048]{2,1,0:T(8,128)(2,1)S(1)}, u32[]{:S(2)}, u32[]{:S(2)}) collective-permute-start(bf16[4,8,2048]{2,1,0:T(8,128)(2,1)S(1)} %get-tuple-element.79), channel_id=1, source_target_pairs={{0,16},{4,20},{8,24},{12,28},{16,0},{20,4},{24,8},{28,12},{1,17},{... | collective-permute-start | bytes 393224 | tf_op jit(solution)/shard_map/ppermute | solution.py:313
  59.4 8.5 %collective-permute-start.18 = (bf16[4,8,2048]{2,1,0:T(8,128)(2,1)S(1)}, bf16[4,8,2048]{2,1,0:T(8,128)(2,1)S(1)}, u32[]{:S(2)}, u32[]{:S(2)}) collective-permute-start(bf16[4,8,2048]{2,1,0:T(8,128)(2,1)S(1)} %get-tuple-element.80), channel_id=1, source_target_pairs={{0,24},{4,28},{8,16},{12,20},{16,8},{20,12},{24,0},{28,4},{1,25},{... | collective-permute-start | bytes 393224 | tf_op jit(solution)/shard_map/ppermute | solution.py:313
  62.6 7.1 %collective-permute-start.12 = (bf16[8,2048]{1,0:T(8,128)(2,1)S(1)}, bf16[8,2048]{1,0:T(8,128)(2,1)S(1)}, u32[]{:S(2)}, u32[]{:S(2)}) collective-permute-start(bf16[8,2048]{1,0:T(8,128)(2,1)S(1)} %get-tuple-element.71), channel_id=1, source_target_pairs={{0,1},{1,0},{2,3},{3,2},{4,5},{5,4},{6,7},{7,6},{8,9},{9,8},{10,11... | collective-permute-start | bytes 98312 | tf_op jit(solution)/shard_map/ppermute | solution.py:316
  62.9 10.3 %collective-permute-start.13 = (bf16[8,2048]{1,0:T(8,128)(2,1)S(1)}, bf16[8,2048]{1,0:T(8,128)(2,1)S(1)}, u32[]{:S(2)}, u32[]{:S(2)}) collective-permute-start(bf16[8,2048]{1,0:T(8,128)(2,1)S(1)} %get-tuple-element.72), channel_id=1, source_target_pairs={{0,2},{1,3},{2,0},{3,1},{4,6},{5,7},{6,4},{7,5},{8,10},{9,11},{10,... | collective-permute-start | bytes 98312 | tf_op jit(solution)/shard_map/ppermute | solution.py:316
  65.1 8.2 %collective-permute-start.14 = (bf16[8,2048]{1,0:T(8,128)(2,1)S(1)}, bf16[8,2048]{1,0:T(8,128)(2,1)S(1)}, u32[]{:S(2)}, u32[]{:S(2)}) collective-permute-start(bf16[8,2048]{1,0:T(8,128)(2,1)S(1)} %get-tuple-element.73), channel_id=1, source_target_pairs={{0,3},{1,2},{2,1},{3,0},{4,7},{5,6},{6,5},{7,4},{8,11},{9,10},{10,... | collective-permute-start | bytes 98312 | tf_op jit(solution)/shard_map/ppermute | solution.py:316
  68.0 5.3 %collective-permute-start.19 = (bf16[8,2048]{1,0:T(8,128)(2,1)S(1)}, bf16[8,2048]{1,0:T(8,128)(2,1)S(1)}, u32[]{:S(2)}, u32[]{:S(2)}) collective-permute-start(bf16[8,2048]{1,0:T(8,128)(2,1)S(1)} %get-tuple-element.82), channel_id=1, source_target_pairs={{0,1},{1,0},{2,3},{3,2},{4,5},{5,4},{6,7},{7,6},{8,9},{9,8},{10,11... | collective-permute-start | bytes 98312 | tf_op jit(solution)/shard_map/ppermute | solution.py:316
  68.0 5.2 %collective-permute-start.20 = (bf16[8,2048]{1,0:T(8,128)(2,1)S(1)}, bf16[8,2048]{1,0:T(8,128)(2,1)S(1)}, u32[]{:S(2)}, u32[]{:S(2)}) collective-permute-start(bf16[8,2048]{1,0:T(8,128)(2,1)S(1)} %get-tuple-element.83), channel_id=1, source_target_pairs={{0,2},{1,3},{2,0},{3,1},{4,6},{5,7},{6,4},{7,5},{8,10},{9,11},{10,... | collective-permute-start | bytes 98312 | tf_op jit(solution)/shard_map/ppermute | solution.py:316
  69.7 5.7 %collective-permute-start.21 = (bf16[8,2048]{1,0:T(8,128)(2,1)S(1)}, bf16[8,2048]{1,0:T(8,128)(2,1)S(1)}, u32[]{:S(2)}, u32[]{:S(2)}) collective-permute-start(bf16[8,2048]{1,0:T(8,128)(2,1)S(1)} %get-tuple-element.84), channel_id=1, source_target_pairs={{0,3},{1,2},{2,1},{3,0},{4,7},{5,6},{6,5},{7,4},{8,11},{9,10},{10,... | collective-permute-start | bytes 98312 | tf_op jit(solution)/shard_map/ppermute | solution.py:316

commit v6 on v4

v6 whole, which is shorter than its diff:
```python
import functools

import jax
import jax.numpy as jnp
from jax import lax
from jax.experimental import pallas as pl
from jax.experimental.pallas import tpu as pltpu
from jax.sharding import PartitionSpec as P

ACT_DEV = 16
PARTS = 2
LANES = 128
CHUNKS = 8
VMEM_BYTES = 24 * 2**20
F32, BF16 = jnp.float32, jnp.bfloat16


def params():
    return pltpu.CompilerParams(vmem_limit_bytes=VMEM_BYTES)


def in_hbm(value):
    return pltpu.with_memory_space_constraint(value, pltpu.HBM)


def iota(shape, axis):
    return lax.broadcasted_iota(jnp.int32, shape, axis)


def turn(bits, index):
    return sum(((index >> b) & 1) << (bits - 1 - b) for b in range(bits))


def row_order(n_seq):
    last = n_seq // 2 - 1
    early = [(core, chip) for core in (0, 1) for chip in range(last)]
    return early + [(0, last), (1, last)]


def owner_of(n_seq, core, chip):
    me = lax.axis_index("seq")
    bits = (n_seq // 2).bit_length() - 1
    odd = (me & 1) ^ core
    return me ^ (jnp.where(odd == 1, turn(bits, chip), chip) * 2 + core)


def lanes_of(n_seq):
    return -(-n_seq * ACT_DEV // LANES) * LANES


def select_kernel(mask_ref, hidden_ref, *refs):
    *own_refs, picker_ref, mask_here, hidden_here, mask_sem, sems = refs
    chunks, tokens, step = hidden_here.shape
    copies = [
        pltpu.make_async_copy(
            hidden_ref.at[:, pl.ds(i * step, step)], hidden_here.at[i], sems.at[i]
        )
        for i in range(chunks)
    ]
    mask_copy = pltpu.make_async_copy(mask_ref, mask_here, mask_sem)
    mask_copy.start()
    for copy in copies:
        copy.start()
    mask_copy.wait()
    mask = mask_here[...]
    upper = (iota((tokens, tokens), 0) <= iota((tokens, tokens), 1)).astype(BF16)
    ones = jnp.broadcast_to(mask.astype(F32).astype(BF16), (ACT_DEV, tokens))
    slots = jnp.dot(ones, upper, preferred_element_type=F32).astype(jnp.int32) - 1
    picker = (slots == iota((ACT_DEV, tokens), 0)) & (mask == 1)
    picker = picker.astype(F32).astype(BF16)
    picker_ref[...] = picker
    each = chunks // len(own_refs)
    for i in range(chunks):
        copies[i].wait()
        own = jnp.dot(picker, hidden_here[i], preferred_element_type=F32)
        at = (i % each) * step
        own_refs[i // each][:, at : at + step] = own.astype(BF16)


def select(mask, hidden):
    tokens, width = hidden.shape
    chunks = 4
    own = jax.ShapeDtypeStruct((ACT_DEV, width // PARTS), BF16)
    *own, picker = pl.pallas_call(
        select_kernel,
        in_specs=[pl.BlockSpec(memory_space=pltpu.HBM)] * 2,
        out_shape=[own] * PARTS + [jax.ShapeDtypeStruct((ACT_DEV, tokens), BF16)],
        scratch_shapes=[
            pltpu.VMEM((1, tokens), jnp.int32),
            pltpu.VMEM((chunks, tokens, width // chunks), BF16),
            pltpu.SemaphoreType.DMA,
            pltpu.SemaphoreType.DMA((chunks,)),
        ],
        compiler_params=params(),
        name="select_rows",
    )(in_hbm(mask.reshape(1, tokens)), in_hbm(hidden))
    return own, picker


def head_copies(head_ref, head_here, sems):
    chunks, step, _ = head_here.shape
    copies = [
        pltpu.make_async_copy(head_ref.at[pl.ds(i * step, step), :], head_here.at[i], sems.at[i])
        for i in range(chunks)
    ]
    for copy in copies:
        copy.start()
    return copies


def head_scratch(head):
    width, shard = head.shape
    return [
        pltpu.VMEM((CHUNKS, width // CHUNKS, shard), BF16),
        pltpu.SemaphoreType.DMA((CHUNKS,)),
    ]


def logits_kernel(n_seq, *refs):
    block_refs, head_ref, picker_ref, logits_ref, stats_ref, packed, head_here, sems = (
        refs[:4],
        *refs[4:],
    )
    copies = head_copies(head_ref, head_here, sems)
    step = head_here.shape[1]
    each = CHUNKS // PARTS
    logits = None
    for i in range(CHUNKS):
        at = (i % each) * step
        rows = []
        for ref in block_refs:
            size = ref.shape[0] // PARTS
            start = (i // each) * size
            rows.append(ref[start : start + size, at : at + step])
        rows = jnp.concatenate(rows, axis=0)
        copies[i].wait()
        part = jnp.dot(rows, head_here[i], preferred_element_type=F32)
        logits = part if logits is None else logits + part
    logits_ref[...] = logits
    top = jnp.max(logits, axis=1, keepdims=True)
    away = logits - top
    ex = jnp.exp(away)
    sums = jnp.sum(ex, axis=1, keepdims=True)
    weighted = jnp.sum(ex * away, axis=1, keepdims=True)
    lane = iota((logits.shape[0], LANES), 1)
    pack = jnp.where(lane == 0, top, jnp.where(lane == 1, sums, weighted))
    if packed.shape[0] > n_seq * ACT_DEV:
        packed[...] = jnp.ones(packed.shape, F32)
    for q, (core, chip) in enumerate(row_order(n_seq)):
        place = pl.multiple_of(owner_of(n_seq, core, chip) * ACT_DEV, ACT_DEV)
        packed[pl.ds(place, ACT_DEV), :] = pack[q * ACT_DEV : (q + 1) * ACT_DEV]
    lines = packed[...].T[:8]
    count = jnp.sum(picker_ref[...].astype(F32))
    mine = iota(lines.shape, 1) // ACT_DEV == lax.axis_index("seq")
    lines = jnp.where(iota(lines.shape, 0) == 3, jnp.where(mine, count, 0.0), lines)
    stats_ref[...] = jnp.broadcast_to(lines[None], stats_ref.shape)


def local_logits(n_seq, n_vocab, blocks, head, picker):
    shard = head.shape[1]
    rows, lanes = n_seq * ACT_DEV, lanes_of(n_seq)
    vmem = pl.BlockSpec(memory_space=pltpu.VMEM)
    return pl.pallas_call(
        functools.partial(logits_kernel, n_seq),
        in_specs=[vmem] * 4 + [pl.BlockSpec(memory_space=pltpu.HBM), vmem],
        out_shape=[
            jax.ShapeDtypeStruct((rows, shard), F32),
            jax.ShapeDtypeStruct((n_seq * n_vocab, 8, lanes), F32),
        ],
        scratch_shapes=[pltpu.VMEM((lanes, LANES), F32)] + head_scratch(head),
        compiler_params=params(),
        name="local_logits",
    )(*blocks, in_hbm(head), picker)


def merged(stats):
    tops, sums, weights = stats[:, 0], stats[:, 1], stats[:, 2]
    top = jnp.max(tops, axis=0, keepdims=True)
    offset = tops - top
    scale = jnp.exp(offset)
    total = jnp.sum(scale * sums, axis=0, keepdims=True)
    weighted = jnp.sum(scale * (weights + offset * sums), axis=0, keepdims=True)
    return top, total, weighted / total


def entropy_kernel(n_vocab, stats_ref, picker_ref, each_ref, average_ref, column):
    stats = stats_ref[...]
    _, total, centred = merged(stats)
    entropy = jnp.log(total) - centred
    counts = jnp.sum(stats[:, 3], axis=0, keepdims=True) / n_vocab
    valid = (iota(entropy.shape, 1) % ACT_DEV).astype(F32) + 0.5 < counts
    sums = jnp.sum(jnp.where(valid, entropy, 0.0), axis=1, keepdims=True)
    average_ref[...] = sums / jnp.sum(valid.astype(F32), axis=1, keepdims=True)
    column[...] = jnp.broadcast_to(entropy, (LANES, entropy.shape[1])).T
    place = pl.multiple_of(lax.axis_index("seq") * ACT_DEV, ACT_DEV)
    mine = column[pl.ds(place, ACT_DEV), :][:, :1]
    picked = picker_ref[...].astype(F32) > 0.5
    each_ref[...] = jnp.sum(jnp.where(picked, mine, 0.0), axis=0, keepdims=True)


def entropies(n_vocab, stats, picker):
    tokens = picker.shape[1]
    return pl.pallas_call(
        functools.partial(entropy_kernel, n_vocab),
        out_shape=[
            jax.ShapeDtypeStruct((1, tokens), F32),
            jax.ShapeDtypeStruct((1, 1), F32),
        ],
        scratch_shapes=[pltpu.VMEM((stats.shape[2], LANES), F32)],
        compiler_params=params(),
        name="entropies",
    )(stats, picker)


def gradient_kernel(n_seq, n_vocab, stats_ref, logits_ref, head_ref, *refs):
    *out_refs, last_ref, columns, ordered, head_here, sems = refs
    near_refs, far_refs = out_refs[:PARTS], out_refs[PARTS:]
    copies = head_copies(head_ref, head_here, sems)
    top, total, centred = merged(stats_ref[...])
    row = iota((8, top.shape[1]), 0)
    lines = jnp.where(row == 0, top, jnp.where(row == 1, 1.0 / total, top + centred))
    columns[...] = jnp.concatenate([lines] * (LANES // 8), axis=0).T
    for q, (core, chip) in enumerate(row_order(n_seq)):
        place = pl.multiple_of(owner_of(n_seq, core, chip) * ACT_DEV, ACT_DEV)
        ordered[q * ACT_DEV : (q + 1) * ACT_DEV] = columns[pl.ds(place, ACT_DEV), :]
    logits = logits_ref[...]
    prob = jnp.exp(logits - ordered[:, 0:1]) * ordered[:, 1:2]
    score = (prob * (ordered[:, 2:3] - logits)).astype(BF16)
    n_chip = n_seq // 2
    last = n_chip - 1
    step = head_here.shape[1]
    span = step * CHUNKS // (n_vocab * PARTS)
    size = min(step, span)
    for i in range(CHUNKS):
        copies[i].wait()
        for j in range(step // size):
            start = i * step + j * size
            v, c, at = start // (span * PARTS), start // span % PARTS, start % span
            part = lax.dot_general(
                score,
                head_here[i, j * size : (j + 1) * size, :],
                (((1,), (1,)), ((), ())),
                preferred_element_type=F32,
            ).astype(BF16)
            blocks = part.reshape(n_seq, ACT_DEV, size)
            cut = slice(at, at + size)
            near_refs[c][:last, v, :, cut] = blocks[:last]
            far_refs[c][:, v, :, cut] = blocks[last : 2 * last]
            near_refs[c][last, v, :, cut] = blocks[2 * last]
            last_ref[c, v, :, cut] = blocks[2 * last + 1]


def gradients(n_seq, n_vocab, stats, logits, head):
    rows = logits.shape[0]
    n_chip = n_seq // 2
    block = (n_vocab, ACT_DEV, head.shape[0] // (n_vocab * PARTS))
    vmem = pl.BlockSpec(memory_space=pltpu.VMEM)
    outs = [jax.ShapeDtypeStruct((n_chip,) + block, BF16)] * PARTS
    outs += [jax.ShapeDtypeStruct((n_chip - 1,) + block, BF16)] * PARTS
    outs += [jax.ShapeDtypeStruct((PARTS,) + block, BF16)]
    *outs, far_last = pl.pallas_call(
        functools.partial(gradient_kernel, n_seq, n_vocab),
        in_specs=[vmem, vmem, pl.BlockSpec(memory_space=pltpu.HBM)],
        out_shape=outs,
        scratch_shapes=[
            pltpu.VMEM((stats.shape[2], LANES), F32),
            pltpu.VMEM((rows, LANES), F32),
        ]
        + head_scratch(head),
        compiler_params=params(),
        name="gradients",
    )(stats, logits, in_hbm(head))
    return outs[:PARTS], outs[PARTS:], far_last


def body(n_seq, n_vocab, hidden, head, mask):
    n_chip = n_seq // 2
    last = n_chip - 1
    bits = n_chip.bit_length() - 1

    def swap_core(value):
        return lax.ppermute(value, "seq", [(i, i ^ 1) for i in range(n_seq)])

    def swap_chip(value, step):
        flips = (2 << step, 2 << (bits - 1 - step))
        return lax.ppermute(value, "seq", [(i, i ^ flips[i & 1]) for i in range(n_seq)])

    def send_vocab(value, k):
        return lax.ppermute(value, "vocab", [(i, i ^ k) for i in range(n_vocab)])

    own, picker = select(mask, hidden)

    near = [own]
    for a in range(1, n_chip):
        step = a.bit_length() - 1
        near.append([swap_chip(part, step) for part in near[a ^ (1 << step)]])
    early = jnp.concatenate([near[a][c] for c in range(PARTS) for a in range(last)], axis=0)
    late = jnp.concatenate(near[last], axis=0)
    blocks = [early, swap_core(early), late, swap_core(late)]

    logits, stats = local_logits(n_seq, n_vocab, blocks, head, picker)
    stats = lax.all_to_all(stats, ("seq", "vocab"), 0, 0, tiled=True)
    near, far, far_last = gradients(n_seq, n_vocab, stats, logits, head)
    each, average = entropies(n_vocab, stats, picker)

    moved = swap_core(far_last)
    far, moved = lax.optimization_barrier((far, moved))
    far = [swap_core(part) for part in far]
    sums = [[near[c][a].astype(F32) + far[c][a].astype(F32) for c in range(PARTS)] for a in range(last)]
    sums.append([near[c][last].astype(F32) + moved[c].astype(F32) for c in range(PARTS)])
    for a in range(last, 0, -1):
        step = a.bit_length() - 1
        for c in range(PARTS):
            sums[a ^ (1 << step)][c] += swap_chip(sums[a][c].astype(BF16), step).astype(F32)

    column = lax.axis_index("vocab")

    def piece(k):
        parts = [lax.dynamic_index_in_dim(part, column ^ k, 0, keepdims=False) for part in sums[0]]
        return jnp.concatenate(parts, axis=1)

    result = piece(0)
    for k in range(n_vocab - 1, 0, -1):
        result = result + send_vocab(piece(k).astype(BF16), k).astype(F32)
    derivative = lax.dot_general(
        picker, result.astype(BF16), (((0,), (0,)), ((), ())), preferred_element_type=F32
    ).astype(BF16)
    return each.reshape(-1), average.reshape(()), derivative


def solution(mesh):
    n_seq, n_vocab = mesh.shape["seq"], mesh.shape["vocab"]

    def run(hidden, head, mask):
        return body(n_seq, n_vocab, hidden, head, mask)

    return jax.shard_map(
        run,
        mesh=mesh,
        in_specs=(P("seq", None), P(None, ("seq", "vocab")), P("seq")),
        out_specs=(P("seq"), P(), P("seq", "vocab")),
        check_vma=False,
    )
```

time: 78.5 us -> 67.6 us (0.86)
  blocking collectives: 0 us -> 14.2 us
  starting transfers between devices: 31 us -> 17.6 us
  local copies, waits for them, and re-layouts: 7.8 us -> 0.14 us
  Pallas kernels: 11.8 us -> 9.8 us
  other arithmetic: 1.37 us -> 0.4 us
  waiting for transfers between devices: 24.2 us -> 23.4 us
    all_to_all x0 -> x1, blocking collectives: none -> 14.2 us  [body(): stats = lax.all_to_all(stats, ('seq', 'vocab'), 0, 0, tiled=True)]
    all_to_all x2 -> x0, waiting for transfers between devices: 12 us -> none  [body(): stats.append(lax.all_to_all(sent, ('seq', 'vocab'), 0, 0, tiled=True))]
    ppermute x12, waiting for transfers between devices: 8.83 us -> 16.5 us  [swap_chip(): lax.ppermute(value, 'seq', [(i, i ^ flips[i & 1]) for i in range(n_seq)])]
    all_to_all x2 -> x0, starting transfers between devices: 7.63 us -> none  [body(): stats.append(lax.all_to_all(sent, ('seq', 'vocab'), 0, 0, tiled=True))]
    unnamed x14 -> x6, local copies, waits for them, and re-layouts: 6.95 us -> 0.06 us
    ppermute x4 -> x5, waiting for transfers between devices: 0.09 us -> 3.5 us  [swap_core(): return lax.ppermute(value, 'seq', [(i, i ^ 1) for i in range(n_seq)])]
    ppermute x6 -> x3, starting transfers between devices: 7.6 us -> 4.44 us  [send_vocab(): return lax.ppermute(value, 'vocab', [(i, i ^ k) for i in range(n_vocab)])]
    ppermute x12, starting transfers between devices: 15.2 us -> 12.4 us  [swap_chip(): lax.ppermute(value, 'seq', [(i, i ^ flips[i & 1]) for i in range(n_seq)])]
  transfers between devices with their start and end apart: 24 -> 20, of which waited for: 12 -> 17; matrix products, arithmetic and copies ran while one was open for 3% -> 1% of each run, Pallas kernels for 12% -> 1%
where the time goes in v6:
time: 67.6 us; the launch traced here: 67.4 us
  waiting for transfers between devices  23.4 us (35%)
  starting transfers between devices  17.6 us (26%)
  blocking collectives  14.2 us (21%)
  Pallas kernels  9.8 us (14%)
  matrix products  1.11 us (2%)
  between operations  0.8 us (1%)
    ppermute x12, waiting for transfers between devices, swap_chip(): lax.ppermute(value, 'seq', [(i, i ^ flips[i & 1]) for i in range(n_seq)])  16.5 us
    all_to_all x1, blocking collectives, body(): stats = lax.all_to_all(stats, ('seq', 'vocab'), 0, 0, tiled=True)  14.2 us
    ppermute x12, starting transfers between devices, swap_chip(): lax.ppermute(value, 'seq', [(i, i ^ flips[i & 1]) for i in range(n_seq)])  12.4 us
    ppermute x3, starting transfers between devices, send_vocab(): return lax.ppermute(value, 'vocab', [(i, i ^ k) for i in range(n_vocab)])  4.44 us
    pallas_call x1, Pallas kernels, gradients(): pl.pallas_call(functools.partial(gradient_kernel, n_seq, n_vocab), in_spe...  3.76 us
    ppermute x5, waiting for transfers between devices, swap_core(): return lax.ppermute(value, 'seq', [(i, i ^ 1) for i in range(n_seq)])  3.5 us
    ppermute x3, waiting for transfers between devices, send_vocab(): return lax.ppermute(value, 'vocab', [(i, i ^ k) for i in range(n_vocab)])  3.44 us
    pallas_call x1, Pallas kernels, local_logits(): pl.pallas_call(functools.partial(logits_kernel, n_seq), in_specs=[vmem] *...  3.16 us
  transfers between devices with their start and end apart: 20, of which 17 were waited for; matrix products, arithmetic and copies ran while one was open for 1% of the time, Pallas kernels for 1%

profile of v6, /device:TPU:0, one launch (start us, length us, event | category | flops | bytes accessed | tf_op | source)
XLA Modules:
  0.0 67.4 jit_solution(3695004953654479009)
XLA Ops:
  0.6 2.1 %select_rows.1 = (bf16[16,4096]{1,0:T(8,128)(2,1)S(1)}, bf16[16,4096]{1,0:T(8,128)(2,1)S(1)}, bf16[16,128]{1,0:T(8,128)(2,1)S(1)}) custom-call(s32[1,128]{1,0:T(1,128)} %bitcast.44, bf16[128,8192]{1,0:T(8,128)(2,1)} %hidden_ref.1), custom_call_target="tpu_custom_call" | custom-call | tf_op jit(solution)/shard_map/select_rows/pallas_call | solution.py:84
  2.8 3.0 %collective-permute-start = (bf16[16,4096]{1,0:T(8,128)(2,1)S(1)}, bf16[16,4096]{1,0:T(8,128)(2,1)S(1)}, u32[]{:S(2)}, u32[]{:S(2)}) collective-permute-start(bf16[16,4096]{1,0:T(8,128)(2,1)S(1)} %get-tuple-element.18), channel_id=1, source_target_pairs={{0,8},{4,20},{8,0},{12,28},{16,24},{20,4},{24,16},{28,12},{1,9},{5... | collective-permute-start | bytes 393224 | tf_op jit(solution)/shard_map/ppermute | solution.py:286
  5.8 1.5 %collective-permute-start.1 = (bf16[16,4096]{1,0:T(8,128)(2,1)S(1)}, bf16[16,4096]{1,0:T(8,128)(2,1)S(1)}, u32[]{:S(2)}, u32[]{:S(2)}) collective-permute-start(bf16[16,4096]{1,0:T(8,128)(2,1)S(1)} %get-tuple-element.18), channel_id=1, source_target_pairs={{0,16},{4,12},{8,24},{12,4},{16,0},{20,28},{24,8},{28,20},{1,17},{... | collective-permute-start | bytes 393224 | tf_op jit(solution)/shard_map/ppermute | solution.py:286
  7.3 0.5 collective-permute-start.2
  7.9 1.7 %collective-permute-done = bf16[16,4096]{1,0:T(8,128)(2,1)S(1)} collective-permute-done((bf16[16,4096]{1,0:T(8,128)(2,1)S(1)}, bf16[16,4096]{1,0:T(8,128)(2,1)S(1)}, u32[]{:S(2)}, u32[]{:S(2)}) %collective-permute-start) | collective-permute-done | bytes 131104 | tf_op jit(solution)/shard_map/ppermute | solution.py:286
  9.6 2.4 %collective-permute-done.1 = bf16[16,4096]{1,0:T(8,128)(2,1)S(1)} collective-permute-done((bf16[16,4096]{1,0:T(8,128)(2,1)S(1)}, bf16[16,4096]{1,0:T(8,128)(2,1)S(1)}, u32[]{:S(2)}, u32[]{:S(2)}) %collective-permute-start.1) | collective-permute-done | bytes 131104 | tf_op jit(solution)/shard_map/ppermute | solution.py:286
  12.0 0.6 collective-permute-start.5
  12.6 0.4 collective-permute-done.2
  12.9 0.4 collective-permute-done.3
  13.4 0.1 collective-permute-start.4
  13.5 0.9 %collective-permute-start.6 = (bf16[16,4096]{1,0:T(8,128)(2,1)S(1)}, bf16[16,4096]{1,0:T(8,128)(2,1)S(1)}, u32[]{:S(2)}, u32[]{:S(2)}) collective-permute-start(bf16[16,4096]{1,0:T(8,128)(2,1)S(1)} %collective-permute-done.2), channel_id=1, source_target_pairs={{0,16},{4,12},{8,24},{12,4},{16,0},{20,28},{24,8},{28,20},{1,17},{... | collective-permute-start | bytes 393224 | tf_op jit(solution)/shard_map/ppermute | solution.py:286
  14.3 2.7 %collective-permute-done.5 = bf16[16,4096]{1,0:T(8,128)(2,1)S(1)} collective-permute-done((bf16[16,4096]{1,0:T(8,128)(2,1)S(1)}, bf16[16,4096]{1,0:T(8,128)(2,1)S(1)}, u32[]{:S(2)}, u32[]{:S(2)}) %collective-permute-start.5) | collective-permute-done | bytes 131104 | tf_op jit(solution)/shard_map/ppermute | solution.py:286
  17.0 1.5 %collective-permute-done.6 = bf16[16,4096]{1,0:T(8,128)(2,1)S(1)} collective-permute-done((bf16[16,4096]{1,0:T(8,128)(2,1)S(1)}, bf16[16,4096]{1,0:T(8,128)(2,1)S(1)}, u32[]{:S(2)}, u32[]{:S(2)}) %collective-permute-start.6) | collective-permute-done | bytes 131104 | tf_op jit(solution)/shard_map/ppermute | solution.py:286
  18.5 0.1 collective-permute-start.7
  18.6 1.5 %collective-permute-done.7.refs_3_ = bf16[32,4096]{1,0:T(8,128)(2,1)S(1)} collective-permute-done((bf16[32,4096]{1,0:T(8,128)(2,1)S(1)}, bf16[32,4096]{1,0:T(8,128)(2,1)S(1)}, u32[]{:S(2)}, u32[]{:S(2)}) %collective-permute-start.7) | collective-permute-done | bytes 262176 | tf_op jit(solution)/shard_map/ppermute | solution.py:282
  20.1 3.2 %local_logits.1 = (f32[128,256]{1,0:T(8,128)S(1)}, f32[32,8,128]{2,1,0:T(8,128)S(1)}) custom-call(bf16[96,4096]{1,0:T(8,128)(2,1)S(1)} %constant_dynamic-update-slice_fusion.refs_0_, bf16[96,4096]{1,0:T(8,128)(2,1)S(1)} %collective-permute-done.4.refs_1_, bf16[32,4096]{1,0:T(8,128)(2,1)S(1)} %constant_dynamic-update-slice_fusion.6.refs_2_, ...), custom_call_target="tpu_custom_call" | custom-call | tf_op jit(solution)/shard_map/local_logits/pallas_call | solution.py:163
  23.3 14.2 %all_to_all.5.stats_ref = f32[32,8,128]{2,1,0:T(8,128)S(1)} all-to-all(f32[32,8,128]{2,1,0:T(8,128)S(1)} %get-tuple-element.21), channel_id=1, replica_groups=mesh['seq'=8,'vocab'=4] {'seq','vocab'}, dimensions={0} | all-to-all | bytes 262144 | tf_op jit(solution)/shard_map/all_to_all | solution.py:302
  37.4 3.8 %gradients.1 = (bf16[4,4,16,1024]{3,2,1,0:T(8,128)(2,1)S(1)}, bf16[4,4,16,1024]{3,2,1,0:T(8,128)(2,1)S(1)}, bf16[3,4,16,1024]{3,2,1,0:T(8,128)(2,1)S(1)}, bf16[3...) custom-call(f32[32,8,128]{2,1,0:T(8,128)S(1)} %all_to_all.5.stats_ref, ...), custom_call_target="tpu_custom_call" | custom-call | tf_op jit(solution)/shard_map/gradients/pallas_call | solution.py:261
  41.2 0.1 collective-permute-start.8
  41.3 1.5 %collective-permute-done.8 = bf16[2,4,16,1024]{3,2,1,0:T(8,128)(2,1)S(1)} collective-permute-done((bf16[2,4,16,1024]{3,2,1,0:T(8,128)(2,1)S(1)}, bf16[2,4,16,1024]{3,2,1,0:T(8,128)(2,1)S(1)}, u32[]{:S(2)}, u32[]{:S(2)}) %collective-permute-start.8) | collective-permute-done | bytes 262176 | tf_op jit(solution)/shard_map/ppermute | solution.py:282
  42.8 0.1 collective-permute-start.13
  42.9 0.4 collective-permute-start.9
  43.3 0.8 %entropies.1 = (f32[1,128]{1,0:T(1,128)}, f32[1,1]{1,0:T(1,128)}) custom-call(f32[32,8,128]{2,1,0:T(8,128)S(1)} %all_to_all.5.stats_ref, bf16[16,128]{1,0:T(8,128)(2,1)S(1)} %get-tuple-element.20.refs_5_.picker_ref), custom_call_target="tpu_custom_call" | custom-call | tf_op jit(solution)/shard_map/entropies/pallas_call | solution.py:203
  44.1 0.4 collective-permute-done.13
  44.5 0.1 fusion.6
  44.6 0.8 %collective-permute-start.15 = (bf16[4,16,1024]{2,1,0:T(8,128)(2,1)S(1)}, bf16[4,16,1024]{2,1,0:T(8,128)(2,1)S(1)}, u32[]{:S(2)}, u32[]{:S(2)}) collective-permute-start(bf16[4,16,1024]{2,1,0:T(8,128)(2,1)S(1)} %get-tuple-element.36), channel_id=1, source_target_pairs={{0,16},{4,12},{8,24},{12,4},{16,0},{20,28},{24,8},{28,20},{1,17},{... | collective-permute-start | bytes 393224 | tf_op jit(solution)/shard_map/ppermute | solution.py:286
  45.4 1.2 %collective-permute-start.14 = (bf16[4,16,1024]{2,1,0:T(8,128)(2,1)S(1)}, bf16[4,16,1024]{2,1,0:T(8,128)(2,1)S(1)}, u32[]{:S(2)}, u32[]{:S(2)}) collective-permute-start(bf16[4,16,1024]{2,1,0:T(8,128)(2,1)S(1)} %get-tuple-element.35), channel_id=1, source_target_pairs={{0,16},{4,12},{8,24},{12,4},{16,0},{20,28},{24,8},{28,20},{1,17},{... | collective-permute-start | bytes 393224 | tf_op jit(solution)/shard_map/ppermute | solution.py:286
  46.7 0.1 fusion.4
  46.8 0.8 %collective-permute-start.11 = (bf16[4,16,1024]{2,1,0:T(8,128)(2,1)S(1)}, bf16[4,16,1024]{2,1,0:T(8,128)(2,1)S(1)}, u32[]{:S(2)}, u32[]{:S(2)}) collective-permute-start(bf16[4,16,1024]{2,1,0:T(8,128)(2,1)S(1)} %get-tuple-element.34), channel_id=1, source_target_pairs={{0,16},{4,12},{8,24},{12,4},{16,0},{20,28},{24,8},{28,20},{1,17},{... | collective-permute-start | bytes 393224 | tf_op jit(solution)/shard_map/ppermute | solution.py:286
  47.6 1.2 %collective-permute-start.10 = (bf16[4,16,1024]{2,1,0:T(8,128)(2,1)S(1)}, bf16[4,16,1024]{2,1,0:T(8,128)(2,1)S(1)}, u32[]{:S(2)}, u32[]{:S(2)}) collective-permute-start(bf16[4,16,1024]{2,1,0:T(8,128)(2,1)S(1)} %get-tuple-element.33), channel_id=1, source_target_pairs={{0,16},{4,12},{8,24},{12,4},{16,0},{20,28},{24,8},{28,20},{1,17},{... | collective-permute-start | bytes 393224 | tf_op jit(solution)/shard_map/ppermute | solution.py:286
  48.9 0.8 %collective-permute-done.15 = bf16[4,16,1024]{2,1,0:T(8,128)(2,1)S(1)} collective-permute-done((bf16[4,16,1024]{2,1,0:T(8,128)(2,1)S(1)}, bf16[4,16,1024]{2,1,0:T(8,128)(2,1)S(1)}, u32[]{:S(2)}, u32[]{:S(2)}) %collective-permute-start.15) | collective-permute-done | bytes 131104 | tf_op jit(solution)/shard_map/ppermute | solution.py:286
  49.6 0.1 fusion
  49.7 0.8 %collective-permute-start.16 = (bf16[4,16,1024]{2,1,0:T(8,128)(2,1)S(1)}, bf16[4,16,1024]{2,1,0:T(8,128)(2,1)S(1)}, u32[]{:S(2)}, u32[]{:S(2)}) collective-permute-start(bf16[4,16,1024]{2,1,0:T(8,128)(2,1)S(1)} %fusion), channel_id=1, source_target_pairs={{0,8},{4,20},{8,0},{12,28},{16,24},{20,4},{24,16},{28,12},{1,9},{5... | collective-permute-start | bytes 393224 | tf_op jit(solution)/shard_map/ppermute | solution.py:286
  50.5 2.7 %collective-permute-done.11 = bf16[4,16,1024]{2,1,0:T(8,128)(2,1)S(1)} collective-permute-done((bf16[4,16,1024]{2,1,0:T(8,128)(2,1)S(1)}, bf16[4,16,1024]{2,1,0:T(8,128)(2,1)S(1)}, u32[]{:S(2)}, u32[]{:S(2)}) %collective-permute-start.11) | collective-permute-done | bytes 131104 | tf_op jit(solution)/shard_map/ppermute | solution.py:286
  53.2 0.1 fusion.2
  53.2 0.8 %collective-permute-start.12 = (bf16[4,16,1024]{2,1,0:T(8,128)(2,1)S(1)}, bf16[4,16,1024]{2,1,0:T(8,128)(2,1)S(1)}, u32[]{:S(2)}, u32[]{:S(2)}) collective-permute-start(bf16[4,16,1024]{2,1,0:T(8,128)(2,1)S(1)} %fusion.2), channel_id=1, source_target_pairs={{0,8},{4,20},{8,0},{12,28},{16,24},{20,4},{24,16},{28,12},{1,9},{5... | collective-permute-start | bytes 393224 | tf_op jit(solution)/shard_map/ppermute | solution.py:286
  54.1 0.7 collective-permute-done.16
  54.7 0.1 fusion.1
  54.8 1.1 %collective-permute-done.10 = bf16[4,16,1024]{2,1,0:T(8,128)(2,1)S(1)} collective-permute-done((bf16[4,16,1024]{2,1,0:T(8,128)(2,1)S(1)}, bf16[4,16,1024]{2,1,0:T(8,128)(2,1)S(1)}, u32[]{:S(2)}, u32[]{:S(2)}) %collective-permute-start.10) | collective-permute-done | bytes 131104 | tf_op jit(solution)/shard_map/ppermute | solution.py:286
  56.0 2.3 %collective-permute-done.12 = bf16[4,16,1024]{2,1,0:T(8,128)(2,1)S(1)} collective-permute-done((bf16[4,16,1024]{2,1,0:T(8,128)(2,1)S(1)}, bf16[4,16,1024]{2,1,0:T(8,128)(2,1)S(1)}, u32[]{:S(2)}, u32[]{:S(2)}) %collective-permute-start.12) | collective-permute-done | bytes 131104 | tf_op jit(solution)/shard_map/ppermute | solution.py:286
  58.3 0.1 fusion.3
  58.4 0.1 collective-permute-start.19
  58.5 1.7 %collective-permute-start.18 = (bf16[16,2048]{1,0:T(8,128)(2,1)S(1)}, bf16[16,2048]{1,0:T(8,128)(2,1)S(1)}, u32[]{:S(2)}, u32[]{:S(2)}) collective-permute-start(bf16[16,2048]{1,0:T(8,128)(2,1)S(1)} %pad_maximum_fusion.1), channel_id=1, source_target_pairs={{0,2},{1,3},{2,0},{3,1},{4,6},{5,7},{6,4},{7,5},{8,10},{9,11},{10,... | collective-permute-start | bytes 196616 | tf_op jit(solution)/shard_map/ppermute | solution.py:289
  60.2 2.6 %collective-permute-start.17 = (bf16[16,2048]{1,0:T(8,128)(2,1)S(1)}, bf16[16,2048]{1,0:T(8,128)(2,1)S(1)}, u32[]{:S(2)}, u32[]{:S(2)}) collective-permute-start(bf16[16,2048]{1,0:T(8,128)(2,1)S(1)} %pad_maximum_fusion), channel_id=1, source_target_pairs={{0,3},{1,2},{2,1},{3,0},{4,7},{5,6},{6,5},{7,4},{8,11},{9,10},{10,... | collective-permute-start | bytes 196616 | tf_op jit(solution)/shard_map/ppermute | solution.py:289
  62.9 0.2 collective-permute-done.19
  63.1 1.1 %collective-permute-done.18 = bf16[16,2048]{1,0:T(8,128)(2,1)S(1)} collective-permute-done((bf16[16,2048]{1,0:T(8,128)(2,1)S(1)}, bf16[16,2048]{1,0:T(8,128)(2,1)S(1)}, u32[]{:S(2)}, u32[]{:S(2)}) %collective-permute-start.18) | collective-permute-done | bytes 65568 | tf_op jit(solution)/shard_map/ppermute | solution.py:289
  64.1 2.2 %collective-permute-done.17 = bf16[16,2048]{1,0:T(8,128)(2,1)S(1)} collective-permute-done((bf16[16,2048]{1,0:T(8,128)(2,1)S(1)}, bf16[16,2048]{1,0:T(8,128)(2,1)S(1)}, u32[]{:S(2)}, u32[]{:S(2)}) %collective-permute-start.17) | collective-permute-done | bytes 65568 | tf_op jit(solution)/shard_map/ppermute | solution.py:289
  66.3 1.1 %convolution_convert_fusion = bf16[128,2048]{1,0:T(8,128)(2,1)} fusion(bf16[16,128]{1,0:T(8,128)(2,1)S(1)} %get-tuple-element.20.refs_5_.picker_ref, f32[16,1024]{1,0:T(8,128)S(1)} %dynamic-slice_bitcast_fusion, f32[16,1024]{1,0:T(8,128)S(1)} %dynamic-slice_bitcast_fusion.1, bf16[16,2048]{1,0:T(8,128)(2,1)S(1)} %collective-permute-done.19, ...), kind=kOutput, calls=%fused_computation | convolution fusion | flops 8912896 | bytes 856064 | tf_op jit(solution)/shard_map/dot_general | solution.py:325
  (19 shorter events, 0.2 us)
Async XLA Ops:
  2.8 6.8 %collective-permute-start = (bf16[16,4096]{1,0:T(8,128)(2,1)S(1)}, bf16[16,4096]{1,0:T(8,128)(2,1)S(1)}, u32[]{:S(2)}, u32[]{:S(2)}) collective-permute-start(bf16[16,4096]{1,0:T(8,128)(2,1)S(1)} %get-tuple-element.18), channel_id=1, source_target_pairs={{0,8},{4,20},{8,0},{12,28},{16,24},{20,4},{24,16},{28,12},{1,9},{5... | collective-permute-start | bytes 393224 | tf_op jit(solution)/shard_map/ppermute | solution.py:286
  5.8 6.2 %collective-permute-start.1 = (bf16[16,4096]{1,0:T(8,128)(2,1)S(1)}, bf16[16,4096]{1,0:T(8,128)(2,1)S(1)}, u32[]{:S(2)}, u32[]{:S(2)}) collective-permute-start(bf16[16,4096]{1,0:T(8,128)(2,1)S(1)} %get-tuple-element.18), channel_id=1, source_target_pairs={{0,16},{4,12},{8,24},{12,4},{16,0},{20,28},{24,8},{28,20},{1,17},{... | collective-permute-start | bytes 393224 | tf_op jit(solution)/shard_map/ppermute | solution.py:286
  7.3 5.6 %collective-permute-start.2 = (bf16[16,4096]{1,0:T(8,128)(2,1)S(1)}, bf16[16,4096]{1,0:T(8,128)(2,1)S(1)}, u32[]{:S(2)}, u32[]{:S(2)}) collective-permute-start(bf16[16,4096]{1,0:T(8,128)(2,1)S(1)} %get-tuple-element.19), channel_id=1, source_target_pairs={{0,8},{4,20},{8,0},{12,28},{16,24},{20,4},{24,16},{28,12},{1,9},{5... | collective-permute-start | bytes 393224 | tf_op jit(solution)/shard_map/ppermute | solution.py:286
  7.8 5.5 %collective-permute-start.3 = (bf16[16,4096]{1,0:T(8,128)(2,1)S(1)}, bf16[16,4096]{1,0:T(8,128)(2,1)S(1)}, u32[]{:S(2)}, u32[]{:S(2)}) collective-permute-start(bf16[16,4096]{1,0:T(8,128)(2,1)S(1)} %get-tuple-element.19), channel_id=1, source_target_pairs={{0,16},{4,12},{8,24},{12,4},{16,0},{20,28},{24,8},{28,20},{1,17},{... | collective-permute-start | bytes 393224 | tf_op jit(solution)/shard_map/ppermute | solution.py:286
  12.0 5.0 %collective-permute-start.5 = (bf16[16,4096]{1,0:T(8,128)(2,1)S(1)}, bf16[16,4096]{1,0:T(8,128)(2,1)S(1)}, u32[]{:S(2)}, u32[]{:S(2)}) collective-permute-start(bf16[16,4096]{1,0:T(8,128)(2,1)S(1)} %collective-permute-done), channel_id=1, source_target_pairs={{0,16},{4,12},{8,24},{12,4},{16,0},{20,28},{24,8},{28,20},{1,17},{... | collective-permute-start | bytes 393224 | tf_op jit(solution)/shard_map/ppermute | solution.py:286
  13.4 6.7 %collective-permute-start.4 = (bf16[96,4096]{1,0:T(8,128)(2,1)S(1)}, bf16[96,4096]{1,0:T(8,128)(2,1)S(1)}, u32[]{:S(2)}, u32[]{:S(2)}) collective-permute-start(bf16[96,4096]{1,0:T(8,128)(2,1)S(1)} %constant_dynamic-update-slice_fusion.refs_0_), channel_id=1, source_target_pairs={{0,4},{4,0},{8,12},{12,8},{16,20},{20,16},{24,28},{28,24},{1,5},{5... | collective-permute-start | bytes 2359304 | tf_op jit(solution)/shard_map/ppermute | solution.py:282
  13.5 5.0 %collective-permute-start.6 = (bf16[16,4096]{1,0:T(8,128)(2,1)S(1)}, bf16[16,4096]{1,0:T(8,128)(2,1)S(1)}, u32[]{:S(2)}, u32[]{:S(2)}) collective-permute-start(bf16[16,4096]{1,0:T(8,128)(2,1)S(1)} %collective-permute-done.2), channel_id=1, source_target_pairs={{0,16},{4,12},{8,24},{12,4},{16,0},{20,28},{24,8},{28,20},{1,17},{... | collective-permute-start | bytes 393224 | tf_op jit(solution)/shard_map/ppermute | solution.py:286
  18.5 1.6 %collective-permute-start.7 = (bf16[32,4096]{1,0:T(8,128)(2,1)S(1)}, bf16[32,4096]{1,0:T(8,128)(2,1)S(1)}, u32[]{:S(2)}, u32[]{:S(2)}) collective-permute-start(bf16[32,4096]{1,0:T(8,128)(2,1)S(1)} %constant_dynamic-update-slice_fusion.6.refs_2_), channel_id=1, source_target_pairs={{0,4},{4,0},{8,12},{12,8},{16,20},{20,16},{24,28},{28,24},{1,5},{5... | collective-permute-start | bytes 786440 | tf_op jit(solution)/shard_map/ppermute | solution.py:282
  41.2 1.6 %collective-permute-start.8 = (bf16[2,4,16,1024]{3,2,1,0:T(8,128)(2,1)S(1)}, bf16[2,4,16,1024]{3,2,1,0:T(8,128)(2,1)S(1)}, u32[]{:S(2)}, u32[]{:S(2)}) collective-permute-start(bf16[2,4,16,1024]{3,2,1,0:T(8,128)(2,1)S(1)} %get-tuple-element.28), channel_id=1, source_target_pairs={{0,4},{4,0},{8,12},{12,8},{16,20},{20,16},{24,28},{28,24},{1,5},{5... | collective-permute-start | bytes 786440 | tf_op jit(solution)/shard_map/ppermute | solution.py:282
  42.8 1.7 %collective-permute-start.13 = (bf16[3,4,16,1024]{3,2,1,0:T(8,128)(2,1)S(1)}, bf16[3,4,16,1024]{3,2,1,0:T(8,128)(2,1)S(1)}, u32[]{:S(2)}, u32[]{:S(2)}) collective-permute-start(bf16[3,4,16,1024]{3,2,1,0:T(8,128)(2,1)S(1)} %get-tuple-element.32), channel_id=1, source_target_pairs={{0,4},{4,0},{8,12},{12,8},{16,20},{20,16},{24,28},{28,24},{1,5},{5... | collective-permute-start | bytes 1179656 | tf_op jit(solution)/shard_map/ppermute | solution.py:282
  42.9 3.8 %collective-permute-start.9 = (bf16[3,4,16,1024]{3,2,1,0:T(8,128)(2,1)S(1)}, bf16[3,4,16,1024]{3,2,1,0:T(8,128)(2,1)S(1)}, u32[]{:S(2)}, u32[]{:S(2)}) collective-permute-start(bf16[3,4,16,1024]{3,2,1,0:T(8,128)(2,1)S(1)} %get-tuple-element.29), channel_id=1, source_target_pairs={{0,4},{4,0},{8,12},{12,8},{16,20},{20,16},{24,28},{28,24},{1,5},{5... | collective-permute-start | bytes 1179656 | tf_op jit(solution)/shard_map/ppermute | solution.py:282
  44.6 5.0 %collective-permute-start.15 = (bf16[4,16,1024]{2,1,0:T(8,128)(2,1)S(1)}, bf16[4,16,1024]{2,1,0:T(8,128)(2,1)S(1)}, u32[]{:S(2)}, u32[]{:S(2)}) collective-permute-start(bf16[4,16,1024]{2,1,0:T(8,128)(2,1)S(1)} %get-tuple-element.36), channel_id=1, source_target_pairs={{0,16},{4,12},{8,24},{12,4},{16,0},{20,28},{24,8},{28,20},{1,17},{... | collective-permute-start | bytes 393224 | tf_op jit(solution)/shard_map/ppermute | solution.py:286
  45.4 8.6 %collective-permute-start.14 = (bf16[4,16,1024]{2,1,0:T(8,128)(2,1)S(1)}, bf16[4,16,1024]{2,1,0:T(8,128)(2,1)S(1)}, u32[]{:S(2)}, u32[]{:S(2)}) collective-permute-start(bf16[4,16,1024]{2,1,0:T(8,128)(2,1)S(1)} %get-tuple-element.35), channel_id=1, source_target_pairs={{0,16},{4,12},{8,24},{12,4},{16,0},{20,28},{24,8},{28,20},{1,17},{... | collective-permute-start | bytes 393224 | tf_op jit(solution)/shard_map/ppermute | solution.py:286
  46.8 6.4 %collective-permute-start.11 = (bf16[4,16,1024]{2,1,0:T(8,128)(2,1)S(1)}, bf16[4,16,1024]{2,1,0:T(8,128)(2,1)S(1)}, u32[]{:S(2)}, u32[]{:S(2)}) collective-permute-start(bf16[4,16,1024]{2,1,0:T(8,128)(2,1)S(1)} %get-tuple-element.34), channel_id=1, source_target_pairs={{0,16},{4,12},{8,24},{12,4},{16,0},{20,28},{24,8},{28,20},{1,17},{... | collective-permute-start | bytes 393224 | tf_op jit(solution)/shard_map/ppermute | solution.py:286
  47.6 8.4 %collective-permute-start.10 = (bf16[4,16,1024]{2,1,0:T(8,128)(2,1)S(1)}, bf16[4,16,1024]{2,1,0:T(8,128)(2,1)S(1)}, u32[]{:S(2)}, u32[]{:S(2)}) collective-permute-start(bf16[4,16,1024]{2,1,0:T(8,128)(2,1)S(1)} %get-tuple-element.33), channel_id=1, source_target_pairs={{0,16},{4,12},{8,24},{12,4},{16,0},{20,28},{24,8},{28,20},{1,17},{... | collective-permute-start | bytes 393224 | tf_op jit(solution)/shard_map/ppermute | solution.py:286
  49.7 5.0 %collective-permute-start.16 = (bf16[4,16,1024]{2,1,0:T(8,128)(2,1)S(1)}, bf16[4,16,1024]{2,1,0:T(8,128)(2,1)S(1)}, u32[]{:S(2)}, u32[]{:S(2)}) collective-permute-start(bf16[4,16,1024]{2,1,0:T(8,128)(2,1)S(1)} %fusion), channel_id=1, source_target_pairs={{0,8},{4,20},{8,0},{12,28},{16,24},{20,4},{24,16},{28,12},{1,9},{5... | collective-permute-start | bytes 393224 | tf_op jit(solution)/shard_map/ppermute | solution.py:286
  53.2 5.0 %collective-permute-start.12 = (bf16[4,16,1024]{2,1,0:T(8,128)(2,1)S(1)}, bf16[4,16,1024]{2,1,0:T(8,128)(2,1)S(1)}, u32[]{:S(2)}, u32[]{:S(2)}) collective-permute-start(bf16[4,16,1024]{2,1,0:T(8,128)(2,1)S(1)} %fusion.2), channel_id=1, source_target_pairs={{0,8},{4,20},{8,0},{12,28},{16,24},{20,4},{24,16},{28,12},{1,9},{5... | collective-permute-start | bytes 393224 | tf_op jit(solution)/shard_map/ppermute | solution.py:286
  58.4 4.7 %collective-permute-start.19 = (bf16[16,2048]{1,0:T(8,128)(2,1)S(1)}, bf16[16,2048]{1,0:T(8,128)(2,1)S(1)}, u32[]{:S(2)}, u32[]{:S(2)}) collective-permute-start(bf16[16,2048]{1,0:T(8,128)(2,1)S(1)} %pad_maximum_fusion.2), channel_id=1, source_target_pairs={{0,1},{1,0},{2,3},{3,2},{4,5},{5,4},{6,7},{7,6},{8,9},{9,8},{10,11... | collective-permute-start | bytes 196616 | tf_op jit(solution)/shard_map/ppermute | solution.py:289
  58.5 5.6 %collective-permute-start.18 = (bf16[16,2048]{1,0:T(8,128)(2,1)S(1)}, bf16[16,2048]{1,0:T(8,128)(2,1)S(1)}, u32[]{:S(2)}, u32[]{:S(2)}) collective-permute-start(bf16[16,2048]{1,0:T(8,128)(2,1)S(1)} %pad_maximum_fusion.1), channel_id=1, source_target_pairs={{0,2},{1,3},{2,0},{3,1},{4,6},{5,7},{6,4},{7,5},{8,10},{9,11},{10,... | collective-permute-start | bytes 196616 | tf_op jit(solution)/shard_map/ppermute | solution.py:289
  60.2 6.1 %collective-permute-start.17 = (bf16[16,2048]{1,0:T(8,128)(2,1)S(1)}, bf16[16,2048]{1,0:T(8,128)(2,1)S(1)}, u32[]{:S(2)}, u32[]{:S(2)}) collective-permute-start(bf16[16,2048]{1,0:T(8,128)(2,1)S(1)} %pad_maximum_fusion), channel_id=1, source_target_pairs={{0,3},{1,2},{2,1},{3,0},{4,7},{5,6},{6,5},{7,4},{8,11},{9,10},{10,... | collective-permute-start | bytes 196616 | tf_op jit(solution)/shard_map/ppermute | solution.py:289

commit v7 on v6

--- a/solution.py
+++ b/solution.py
@@ -11,6 +11,7 @@
 PARTS = 2
 LANES = 128
 CHUNKS = 8
+FLIGHT = 3
 VMEM_BYTES = 24 * 2**20
 F32, BF16 = jnp.float32, jnp.bfloat16
 
@@ -59,7 +60,7 @@
     ]
     mask_copy = pltpu.make_async_copy(mask_ref, mask_here, mask_sem)
     mask_copy.start()
-    for copy in copies:
+    for copy in copies[:FLIGHT]:
         copy.start()
     mask_copy.wait()
     mask = mask_here[...]
@@ -71,7 +72,7 @@
     picker_ref[...] = picker
     each = chunks // len(own_refs)
     for i in range(chunks):
-        copies[i].wait()
+        arrive(copies, i)
         own = jnp.dot(picker, hidden_here[i], preferred_element_type=F32)
         at = (i % each) * step
         own_refs[i // each][:, at : at + step] = own.astype(BF16)
@@ -103,9 +104,15 @@
         pltpu.make_async_copy(head_ref.at[pl.ds(i * step, step), :], head_here.at[i], sems.at[i])
         for i in range(chunks)
     ]
-    for copy in copies:
+    for copy in copies[:FLIGHT]:
         copy.start()
     return copies
+
+
+def arrive(copies, i):
+    copies[i].wait()
+    if i + FLIGHT < len(copies):
+        copies[i + FLIGHT].start()
 
 
 def head_scratch(head):
@@ -133,7 +140,7 @@
             start = (i // each) * size
             rows.append(ref[start : start + size, at : at + step])
         rows = jnp.concatenate(rows, axis=0)
-        copies[i].wait()
+        arrive(copies, i)
         part = jnp.dot(rows, head_here[i], preferred_element_type=F32)
         logits = part if logits is None else logits + part
     logits_ref[...] = logits
@@ -149,7 +156,7 @@
     for q, (core, chip) in enumerate(row_order(n_seq)):
         place = pl.multiple_of(owner_of(n_seq, core, chip) * ACT_DEV, ACT_DEV)
         packed[pl.ds(place, ACT_DEV), :] = pack[q * ACT_DEV : (q + 1) * ACT_DEV]
-    lines = packed[...].T[:8]
+    lines = packed[...].T[:4]
     count = jnp.sum(picker_ref[...].astype(F32))
     mine = iota(lines.shape, 1) // ACT_DEV == lax.axis_index("seq")
     lines = jnp.where(iota(lines.shape, 0) == 3, jnp.where(mine, count, 0.0), lines)
@@ -162,15 +169,15 @@
     vmem = pl.BlockSpec(memory_space=pltpu.VMEM)
     return pl.pallas_call(
         functools.partial(logits_kernel, n_seq),
-        in_specs=[vmem] * 4 + [pl.BlockSpec(memory_space=pltpu.HBM), vmem],
+        in_specs=[vmem] * 4 + [pl.BlockSpec(memory_space=pl.ANY), vmem],
         out_shape=[
             jax.ShapeDtypeStruct((rows, shard), F32),
-            jax.ShapeDtypeStruct((n_seq * n_vocab, 8, lanes), F32),
+            jax.ShapeDtypeStruct((n_seq * n_vocab, 4, lanes), F32),
         ],
         scratch_shapes=[pltpu.VMEM((lanes, LANES), F32)] + head_scratch(head),
         compiler_params=params(),
         name="local_logits",
-    )(*blocks, in_hbm(head), picker)
+    )(*blocks, head, picker)
 
 
 def merged(stats):
@@ -232,7 +239,7 @@
     span = step * CHUNKS // (n_vocab * PARTS)
     size = min(step, span)
     for i in range(CHUNKS):
-        copies[i].wait()
+        arrive(copies, i)
         for j in range(step // size):
             start = i * step + j * size
             v, c, at = start // (span * PARTS), start // span % PARTS, start % span
@@ -260,7 +267,7 @@
     outs += [jax.ShapeDtypeStruct((PARTS,) + block, BF16)]
     *outs, far_last = pl.pallas_call(
         functools.partial(gradient_kernel, n_seq, n_vocab),
-        in_specs=[vmem, vmem, pl.BlockSpec(memory_space=pltpu.HBM)],
+        in_specs=[vmem, vmem, pl.BlockSpec(memory_space=pl.ANY)],
         out_shape=outs,
         scratch_shapes=[
             pltpu.VMEM((stats.shape[2], LANES), F32),
@@ -269,7 +276,7 @@
         + head_scratch(head),
         compiler_params=params(),
         name="gradients",
-    )(stats, logits, in_hbm(head))
+    )(stats, logits, head)
     return outs[:PARTS], outs[PARTS:], far_last
 
 
@@ -295,6 +302,7 @@
         step = a.bit_length() - 1
         near.append([swap_chip(part, step) for part in near[a ^ (1 << step)]])
     early = jnp.concatenate([near[a][c] for c in range(PARTS) for a in range(last)], axis=0)
+    early, near[last][0] = lax.optimization_barrier((early, near[last][0]))
     late = jnp.concatenate(near[last], axis=0)
     blocks = [early, swap_core(early), late, swap_core(late)]
 
@@ -304,10 +312,11 @@
     each, average = entropies(n_vocab, stats, picker)
 
     moved = swap_core(far_last)
-    far, moved = lax.optimization_barrier((far, moved))
+    first = [(near[c][last].astype(F32) + moved[c].astype(F32)).astype(BF16) for c in range(PARTS)]
+    far, first = lax.optimization_barrier((far, first))
     far = [swap_core(part) for part in far]
     sums = [[near[c][a].astype(F32) + far[c][a].astype(F32) for c in range(PARTS)] for a in range(last)]
-    sums.append([near[c][last].astype(F32) + moved[c].astype(F32) for c in range(PARTS)])
+    sums.append(first)
     for a in range(last, 0, -1):
         step = a.bit_length() - 1
         for c in range(PARTS):

time: 67.6 us -> 63.6 us (0.941)
  waiting for transfers between devices: 23.4 us -> 20.9 us
  blocking collectives: 14.2 us -> 13.1 us
  Pallas kernels: 9.8 us -> 8.92 us
    ppermute x12, waiting for transfers between devices: 16.5 us -> 14.5 us  [swap_chip(): lax.ppermute(value, 'seq', [(i, i ^ flips[i & 1]) for i in range(n_seq)])]
    all_to_all x1, blocking collectives: 14.2 us -> 13.1 us  [body(): stats = lax.all_to_all(stats, ('seq', 'vocab'), 0, 0, tiled=True)]
    pallas_call x1, Pallas kernels: 3.16 us -> 2.26 us  [local_logits(): pl.pallas_call(functools.partial(logits_kernel, n_seq), in_specs=[vmem] *...]
    ppermute x12, starting transfers between devices: 12.4 us -> 13.2 us  [swap_chip(): lax.ppermute(value, 'seq', [(i, i ^ flips[i & 1]) for i in range(n_seq)])]
  transfers between devices with their start and end apart: 20 -> 20, of which waited for: 17 -> 11; matrix products, arithmetic and copies ran while one was open for 1% -> 1% of each run, Pallas kernels for 1% -> 1%
where the time goes in v7:
time: 63.6 us; the launch traced here: 63.4 us
  waiting for transfers between devices  20.9 us (33%)
  starting transfers between devices  18 us (28%)
  blocking collectives  13.1 us (21%)
  Pallas kernels  8.92 us (14%)
  matrix products  1.11 us (2%)
  between operations  0.81 us (1%)
    ppermute x12, waiting for transfers between devices, swap_chip(): lax.ppermute(value, 'seq', [(i, i ^ flips[i & 1]) for i in range(n_seq)])  14.5 us
    ppermute x12, starting transfers between devices, swap_chip(): lax.ppermute(value, 'seq', [(i, i ^ flips[i & 1]) for i in range(n_seq)])  13.2 us
    all_to_all x1, blocking collectives, body(): stats = lax.all_to_all(stats, ('seq', 'vocab'), 0, 0, tiled=True)  13.1 us
    ppermute x3, starting transfers between devices, send_vocab(): return lax.ppermute(value, 'vocab', [(i, i ^ k) for i in range(n_vocab)])  4.45 us
    ppermute x3, waiting for transfers between devices, send_vocab(): return lax.ppermute(value, 'vocab', [(i, i ^ k) for i in range(n_vocab)])  3.27 us
    pallas_call x1, Pallas kernels, gradients(): pl.pallas_call(functools.partial(gradient_kernel, n_seq, n_vocab), in_spe...  3.14 us
    ppermute x5, waiting for transfers between devices, swap_core(): return lax.ppermute(value, 'seq', [(i, i ^ 1) for i in range(n_seq)])  3.05 us
    pallas_call x1, Pallas kernels, select(): pl.pallas_call(select_kernel, in_specs=[pl.BlockSpec(memory_space=pltpu.H...  2.75 us
  transfers between devices with their start and end apart: 20, of which 11 were waited for; matrix products, arithmetic and copies ran while one was open for 1% of the time, Pallas kernels for 1%

profile of v7, /device:TPU:0, one launch (start us, length us, event | category | flops | bytes accessed | tf_op | source)
XLA Modules:
  0.0 63.4 jit_solution(1793365053497030850)
XLA Ops:
  0.6 2.8 %select_rows.1 = (bf16[16,4096]{1,0:T(8,128)(2,1)S(1)}, bf16[16,4096]{1,0:T(8,128)(2,1)S(1)}, bf16[16,128]{1,0:T(8,128)(2,1)S(1)}) custom-call(s32[1,128]{1,0:T(1,128)} %bitcast.44, bf16[128,8192]{1,0:T(8,128)(2,1)} %hidden_ref.1), custom_call_target="tpu_custom_call" | custom-call | tf_op jit(solution)/shard_map/select_rows/pallas_call | solution.py:85
  3.4 3.0 %collective-permute-start = (bf16[16,4096]{1,0:T(8,128)(2,1)S(1)}, bf16[16,4096]{1,0:T(8,128)(2,1)S(1)}, u32[]{:S(2)}, u32[]{:S(2)}) collective-permute-start(bf16[16,4096]{1,0:T(8,128)(2,1)S(1)} %get-tuple-element.21), channel_id=1, source_target_pairs={{0,8},{4,20},{8,0},{12,28},{16,24},{20,4},{24,16},{28,12},{1,9},{5... | collective-permute-start | bytes 393224 | tf_op jit(solution)/shard_map/ppermute | solution.py:293
  6.4 1.5 %collective-permute-start.1 = (bf16[16,4096]{1,0:T(8,128)(2,1)S(1)}, bf16[16,4096]{1,0:T(8,128)(2,1)S(1)}, u32[]{:S(2)}, u32[]{:S(2)}) collective-permute-start(bf16[16,4096]{1,0:T(8,128)(2,1)S(1)} %get-tuple-element.21), channel_id=1, source_target_pairs={{0,16},{4,12},{8,24},{12,4},{16,0},{20,28},{24,8},{28,20},{1,17},{... | collective-permute-start | bytes 393224 | tf_op jit(solution)/shard_map/ppermute | solution.py:293
  7.9 0.5 collective-permute-start.2
  8.5 0.1 collective-permute-start.3
  8.5 1.7 %collective-permute-done = bf16[16,4096]{1,0:T(8,128)(2,1)S(1)} collective-permute-done((bf16[16,4096]{1,0:T(8,128)(2,1)S(1)}, bf16[16,4096]{1,0:T(8,128)(2,1)S(1)}, u32[]{:S(2)}, u32[]{:S(2)}) %collective-permute-start) | collective-permute-done | bytes 131104 | tf_op jit(solution)/shard_map/ppermute | solution.py:293
  10.2 2.4 %collective-permute-done.1 = bf16[16,4096]{1,0:T(8,128)(2,1)S(1)} collective-permute-done((bf16[16,4096]{1,0:T(8,128)(2,1)S(1)}, bf16[16,4096]{1,0:T(8,128)(2,1)S(1)}, u32[]{:S(2)}, u32[]{:S(2)}) %collective-permute-start.1) | collective-permute-done | bytes 131104 | tf_op jit(solution)/shard_map/ppermute | solution.py:293
  12.6 0.6 collective-permute-start.4
  13.2 0.4 collective-permute-done.2
  13.6 1.2 %collective-permute-start.6 = (bf16[16,4096]{1,0:T(8,128)(2,1)S(1)}, bf16[16,4096]{1,0:T(8,128)(2,1)S(1)}, u32[]{:S(2)}, u32[]{:S(2)}) collective-permute-start(bf16[16,4096]{1,0:T(8,128)(2,1)S(1)} %collective-permute-done.2), channel_id=1, source_target_pairs={{0,16},{4,12},{8,24},{12,4},{16,0},{20,28},{24,8},{28,20},{1,17},{... | collective-permute-start | bytes 393224 | tf_op jit(solution)/shard_map/ppermute | solution.py:293
  14.8 0.0 collective-permute-done.3
  14.8 2.8 %collective-permute-done.4 = bf16[16,4096]{1,0:T(8,128)(2,1)S(1)} collective-permute-done((bf16[16,4096]{1,0:T(8,128)(2,1)S(1)}, bf16[16,4096]{1,0:T(8,128)(2,1)S(1)}, u32[]{:S(2)}, u32[]{:S(2)}) %collective-permute-start.4) | collective-permute-done | bytes 131104 | tf_op jit(solution)/shard_map/ppermute | solution.py:293
  17.7 0.0 collective-permute-start.5
  17.7 1.4 %collective-permute-done.6 = bf16[16,4096]{1,0:T(8,128)(2,1)S(1)} collective-permute-done((bf16[16,4096]{1,0:T(8,128)(2,1)S(1)}, bf16[16,4096]{1,0:T(8,128)(2,1)S(1)}, u32[]{:S(2)}, u32[]{:S(2)}) %collective-permute-start.6) | collective-permute-done | bytes 131104 | tf_op jit(solution)/shard_map/ppermute | solution.py:293
  19.1 0.1 collective-permute-start.7
  19.2 1.5 %collective-permute-done.7.refs_3_ = bf16[32,4096]{1,0:T(8,128)(2,1)S(1)} collective-permute-done((bf16[32,4096]{1,0:T(8,128)(2,1)S(1)}, bf16[32,4096]{1,0:T(8,128)(2,1)S(1)}, u32[]{:S(2)}, u32[]{:S(2)}) %collective-permute-start.7) | collective-permute-done | bytes 262176 | tf_op jit(solution)/shard_map/ppermute | solution.py:289
  20.7 0.0 collective-permute-done.5.refs_1_
  20.7 2.3 %local_logits.1 = (f32[128,256]{1,0:T(8,128)S(1)}, f32[32,4,128]{2,1,0:T(4,128)S(1)}) custom-call(bf16[96,4096]{1,0:T(8,128)(2,1)S(1)} %constant_dynamic-update-slice_fusion.refs_0_, bf16[96,4096]{1,0:T(8,128)(2,1)S(1)} %collective-permute-done.5.refs_1_, bf16[32,4096]{1,0:T(8,128)(2,1)S(1)} %constant_dynamic-update-slice_fusion.6.refs_2_, ...), custom_call_target="tpu_custom_call" | custom-call | tf_op jit(solution)/shard_map/local_logits/pallas_call | solution.py:170
  23.0 13.1 %all_to_all.5.stats_ref = f32[32,4,128]{2,1,0:T(4,128)S(1)} all-to-all(f32[32,4,128]{2,1,0:T(4,128)S(1)} %get-tuple-element.26), channel_id=1, replica_groups=mesh['seq'=8,'vocab'=4] {'seq','vocab'}, dimensions={0} | all-to-all | bytes 131072 | tf_op jit(solution)/shard_map/all_to_all | solution.py:310
  36.1 3.1 %gradients.1 = (bf16[4,4,16,1024]{3,2,1,0:T(8,128)(2,1)S(1)}, bf16[4,4,16,1024]{3,2,1,0:T(8,128)(2,1)S(1)}, bf16[3,4,16,1024]{3,2,1,0:T(8,128)(2,1)S(1)}, bf16[3...) custom-call(f32[32,4,128]{2,1,0:T(4,128)S(1)} %all_to_all.5.stats_ref, ...), custom_call_target="tpu_custom_call" | custom-call | tf_op jit(solution)/shard_map/gradients/pallas_call | solution.py:268
  39.2 0.1 collective-permute-start.8
  39.3 1.5 %collective-permute-done.8 = bf16[2,4,16,1024]{3,2,1,0:T(8,128)(2,1)S(1)} collective-permute-done((bf16[2,4,16,1024]{3,2,1,0:T(8,128)(2,1)S(1)}, bf16[2,4,16,1024]{3,2,1,0:T(8,128)(2,1)S(1)}, u32[]{:S(2)}, u32[]{:S(2)}) %collective-permute-start.8) | collective-permute-done | bytes 262176 | tf_op jit(solution)/shard_map/ppermute | solution.py:289
  40.8 0.1 fusion.5
  40.9 0.2 collective-permute-start.13
  41.1 0.7 %collective-permute-start.15 = (bf16[4,16,1024]{2,1,0:T(8,128)(2,1)S(1)}, bf16[4,16,1024]{2,1,0:T(8,128)(2,1)S(1)}, u32[]{:S(2)}, u32[]{:S(2)}) collective-permute-start(bf16[4,16,1024]{2,1,0:T(8,128)(2,1)S(1)} %get-tuple-element.38), channel_id=1, source_target_pairs={{0,16},{4,12},{8,24},{12,4},{16,0},{20,28},{24,8},{28,20},{1,17},{... | collective-permute-start | bytes 393224 | tf_op jit(solution)/shard_map/ppermute | solution.py:293
  41.8 0.8 %entropies.1 = (f32[1,128]{1,0:T(1,128)}, f32[1,1]{1,0:T(1,128)}) custom-call(f32[32,4,128]{2,1,0:T(4,128)S(1)} %all_to_all.5.stats_ref, bf16[16,128]{1,0:T(8,128)(2,1)S(1)} %get-tuple-element.25.refs_5_.picker_ref), custom_call_target="tpu_custom_call" | custom-call | tf_op jit(solution)/shard_map/entropies/pallas_call | solution.py:210
  42.6 1.3 %collective-permute-start.11 = (bf16[4,16,1024]{2,1,0:T(8,128)(2,1)S(1)}, bf16[4,16,1024]{2,1,0:T(8,128)(2,1)S(1)}, u32[]{:S(2)}, u32[]{:S(2)}) collective-permute-start(bf16[4,16,1024]{2,1,0:T(8,128)(2,1)S(1)} %get-tuple-element.36), channel_id=1, source_target_pairs={{0,16},{4,12},{8,24},{12,4},{16,0},{20,28},{24,8},{28,20},{1,17},{... | collective-permute-start | bytes 393224 | tf_op jit(solution)/shard_map/ppermute | solution.py:293
  43.9 0.0 collective-permute-start.9
  43.9 2.2 %collective-permute-done.15 = bf16[4,16,1024]{2,1,0:T(8,128)(2,1)S(1)} collective-permute-done((bf16[4,16,1024]{2,1,0:T(8,128)(2,1)S(1)}, bf16[4,16,1024]{2,1,0:T(8,128)(2,1)S(1)}, u32[]{:S(2)}, u32[]{:S(2)}) %collective-permute-start.15) | collective-permute-done | bytes 131104 | tf_op jit(solution)/shard_map/ppermute | solution.py:293
  46.1 0.0 collective-permute-done.13
  46.1 0.1 fusion
  46.1 0.7 %collective-permute-start.16 = (bf16[4,16,1024]{2,1,0:T(8,128)(2,1)S(1)}, bf16[4,16,1024]{2,1,0:T(8,128)(2,1)S(1)}, u32[]{:S(2)}, u32[]{:S(2)}) collective-permute-start(bf16[4,16,1024]{2,1,0:T(8,128)(2,1)S(1)} %fusion), channel_id=1, source_target_pairs={{0,8},{4,20},{8,0},{12,28},{16,24},{20,4},{24,16},{28,12},{1,9},{5... | collective-permute-start | bytes 393224 | tf_op jit(solution)/shard_map/ppermute | solution.py:293
  46.9 0.6 collective-permute-start.14
  47.5 0.0 collective-permute-done.11
  47.5 0.1 fusion.2
  47.6 1.6 %collective-permute-start.12 = (bf16[4,16,1024]{2,1,0:T(8,128)(2,1)S(1)}, bf16[4,16,1024]{2,1,0:T(8,128)(2,1)S(1)}, u32[]{:S(2)}, u32[]{:S(2)}) collective-permute-start(bf16[4,16,1024]{2,1,0:T(8,128)(2,1)S(1)} %fusion.2), channel_id=1, source_target_pairs={{0,8},{4,20},{8,0},{12,28},{16,24},{20,4},{24,16},{28,12},{1,9},{5... | collective-permute-start | bytes 393224 | tf_op jit(solution)/shard_map/ppermute | solution.py:293
  49.2 1.4 %collective-permute-start.10 = (bf16[4,16,1024]{2,1,0:T(8,128)(2,1)S(1)}, bf16[4,16,1024]{2,1,0:T(8,128)(2,1)S(1)}, u32[]{:S(2)}, u32[]{:S(2)}) collective-permute-start(bf16[4,16,1024]{2,1,0:T(8,128)(2,1)S(1)} %fusion.6), channel_id=1, source_target_pairs={{0,16},{4,12},{8,24},{12,4},{16,0},{20,28},{24,8},{28,20},{1,17},{... | collective-permute-start | bytes 393224 | tf_op jit(solution)/shard_map/ppermute | solution.py:293
  50.6 2.0 %collective-permute-done.16 = bf16[4,16,1024]{2,1,0:T(8,128)(2,1)S(1)} collective-permute-done((bf16[4,16,1024]{2,1,0:T(8,128)(2,1)S(1)}, bf16[4,16,1024]{2,1,0:T(8,128)(2,1)S(1)}, u32[]{:S(2)}, u32[]{:S(2)}) %collective-permute-start.16) | collective-permute-done | bytes 131104 | tf_op jit(solution)/shard_map/ppermute | solution.py:293
  52.6 0.1 fusion.1
  52.7 1.7 %collective-permute-done.12 = bf16[4,16,1024]{2,1,0:T(8,128)(2,1)S(1)} collective-permute-done((bf16[4,16,1024]{2,1,0:T(8,128)(2,1)S(1)}, bf16[4,16,1024]{2,1,0:T(8,128)(2,1)S(1)}, u32[]{:S(2)}, u32[]{:S(2)}) %collective-permute-start.12) | collective-permute-done | bytes 131104 | tf_op jit(solution)/shard_map/ppermute | solution.py:293
  54.4 0.0 collective-permute-done.10
  54.4 0.1 fusion.3
  54.6 0.3 collective-permute-start.19
  54.9 1.1 %collective-permute-start.18 = (bf16[16,2048]{1,0:T(8,128)(2,1)S(1)}, bf16[16,2048]{1,0:T(8,128)(2,1)S(1)}, u32[]{:S(2)}, u32[]{:S(2)}) collective-permute-start(bf16[16,2048]{1,0:T(8,128)(2,1)S(1)} %pad_maximum_fusion.1), channel_id=1, source_target_pairs={{0,2},{1,3},{2,0},{3,1},{4,6},{5,7},{6,4},{7,5},{8,10},{9,11},{10,... | collective-permute-start | bytes 196616 | tf_op jit(solution)/shard_map/ppermute | solution.py:296
  56.0 3.0 %collective-permute-start.17 = (bf16[16,2048]{1,0:T(8,128)(2,1)S(1)}, bf16[16,2048]{1,0:T(8,128)(2,1)S(1)}, u32[]{:S(2)}, u32[]{:S(2)}) collective-permute-start(bf16[16,2048]{1,0:T(8,128)(2,1)S(1)} %pad_maximum_fusion), channel_id=1, source_target_pairs={{0,3},{1,2},{2,1},{3,0},{4,7},{5,6},{6,5},{7,4},{8,11},{9,10},{10,... | collective-permute-start | bytes 196616 | tf_op jit(solution)/shard_map/ppermute | solution.py:296
  59.0 0.0 collective-permute-done.19
  59.0 3.3 %collective-permute-done.18 = bf16[16,2048]{1,0:T(8,128)(2,1)S(1)} collective-permute-done((bf16[16,2048]{1,0:T(8,128)(2,1)S(1)}, bf16[16,2048]{1,0:T(8,128)(2,1)S(1)}, u32[]{:S(2)}, u32[]{:S(2)}) %collective-permute-start.18) | collective-permute-done | bytes 65568 | tf_op jit(solution)/shard_map/ppermute | solution.py:296
  62.3 1.1 %convolution_convert_fusion = bf16[128,2048]{1,0:T(8,128)(2,1)} fusion(bf16[16,128]{1,0:T(8,128)(2,1)S(1)} %get-tuple-element.25.refs_5_.picker_ref, f32[16,1024]{1,0:T(8,128)S(1)} %dynamic-slice_bitcast_fusion, f32[16,1024]{1,0:T(8,128)S(1)} %dynamic-slice_bitcast_fusion.1, bf16[16,2048]{1,0:T(8,128)(2,1)S(1)} %collective-permute-done.19, ...), kind=kOutput, calls=%fused_computation | convolution fusion | flops 8912896 | bytes 856064 | tf_op jit(solution)/shard_map/dot_general | solution.py:334
  (22 shorter events, 0.2 us)
Async XLA Ops:
  0.6 20.1 %copy-start = (bf16[8192,256]{1,0:T(8,128)(2,1)S(1)}, bf16[8192,256]{1,0:T(8,128)(2,1)}, u32[]{:S(2)}) copy-start(bf16[8192,256]{1,0:T(8,128)(2,1)} %head_ref.1) | copy-start | bytes 12582916
  3.4 6.8 %collective-permute-start = (bf16[16,4096]{1,0:T(8,128)(2,1)S(1)}, bf16[16,4096]{1,0:T(8,128)(2,1)S(1)}, u32[]{:S(2)}, u32[]{:S(2)}) collective-permute-start(bf16[16,4096]{1,0:T(8,128)(2,1)S(1)} %get-tuple-element.21), channel_id=1, source_target_pairs={{0,8},{4,20},{8,0},{12,28},{16,24},{20,4},{24,16},{28,12},{1,9},{5... | collective-permute-start | bytes 393224 | tf_op jit(solution)/shard_map/ppermute | solution.py:293
  6.4 6.2 %collective-permute-start.1 = (bf16[16,4096]{1,0:T(8,128)(2,1)S(1)}, bf16[16,4096]{1,0:T(8,128)(2,1)S(1)}, u32[]{:S(2)}, u32[]{:S(2)}) collective-permute-start(bf16[16,4096]{1,0:T(8,128)(2,1)S(1)} %get-tuple-element.21), channel_id=1, source_target_pairs={{0,16},{4,12},{8,24},{12,4},{16,0},{20,28},{24,8},{28,20},{1,17},{... | collective-permute-start | bytes 393224 | tf_op jit(solution)/shard_map/ppermute | solution.py:293
  7.9 5.6 %collective-permute-start.2 = (bf16[16,4096]{1,0:T(8,128)(2,1)S(1)}, bf16[16,4096]{1,0:T(8,128)(2,1)S(1)}, u32[]{:S(2)}, u32[]{:S(2)}) collective-permute-start(bf16[16,4096]{1,0:T(8,128)(2,1)S(1)} %get-tuple-element.22), channel_id=1, source_target_pairs={{0,8},{4,20},{8,0},{12,28},{16,24},{20,4},{24,16},{28,12},{1,9},{5... | collective-permute-start | bytes 393224 | tf_op jit(solution)/shard_map/ppermute | solution.py:293
  8.5 6.4 %collective-permute-start.3 = (bf16[16,4096]{1,0:T(8,128)(2,1)S(1)}, bf16[16,4096]{1,0:T(8,128)(2,1)S(1)}, u32[]{:S(2)}, u32[]{:S(2)}) collective-permute-start(bf16[16,4096]{1,0:T(8,128)(2,1)S(1)} %get-tuple-element.22), channel_id=1, source_target_pairs={{0,16},{4,12},{8,24},{12,4},{16,0},{20,28},{24,8},{28,20},{1,17},{... | collective-permute-start | bytes 393224 | tf_op jit(solution)/shard_map/ppermute | solution.py:293
  12.6 5.0 %collective-permute-start.4 = (bf16[16,4096]{1,0:T(8,128)(2,1)S(1)}, bf16[16,4096]{1,0:T(8,128)(2,1)S(1)}, u32[]{:S(2)}, u32[]{:S(2)}) collective-permute-start(bf16[16,4096]{1,0:T(8,128)(2,1)S(1)} %collective-permute-done), channel_id=1, source_target_pairs={{0,16},{4,12},{8,24},{12,4},{16,0},{20,28},{24,8},{28,20},{1,17},{... | collective-permute-start | bytes 393224 | tf_op jit(solution)/shard_map/ppermute | solution.py:293
  13.6 5.5 %collective-permute-start.6 = (bf16[16,4096]{1,0:T(8,128)(2,1)S(1)}, bf16[16,4096]{1,0:T(8,128)(2,1)S(1)}, u32[]{:S(2)}, u32[]{:S(2)}) collective-permute-start(bf16[16,4096]{1,0:T(8,128)(2,1)S(1)} %collective-permute-done.2), channel_id=1, source_target_pairs={{0,16},{4,12},{8,24},{12,4},{16,0},{20,28},{24,8},{28,20},{1,17},{... | collective-permute-start | bytes 393224 | tf_op jit(solution)/shard_map/ppermute | solution.py:293
  17.7 3.0 %collective-permute-start.5 = (bf16[96,4096]{1,0:T(8,128)(2,1)S(1)}, bf16[96,4096]{1,0:T(8,128)(2,1)S(1)}, u32[]{:S(2)}, u32[]{:S(2)}) collective-permute-start(bf16[96,4096]{1,0:T(8,128)(2,1)S(1)} %constant_dynamic-update-slice_fusion.refs_0_), channel_id=1, source_target_pairs={{0,4},{4,0},{8,12},{12,8},{16,20},{20,16},{24,28},{28,24},{1,5},{5... | collective-permute-start | bytes 2359304 | tf_op jit(solution)/shard_map/ppermute | solution.py:289
  19.1 1.6 %collective-permute-start.7 = (bf16[32,4096]{1,0:T(8,128)(2,1)S(1)}, bf16[32,4096]{1,0:T(8,128)(2,1)S(1)}, u32[]{:S(2)}, u32[]{:S(2)}) collective-permute-start(bf16[32,4096]{1,0:T(8,128)(2,1)S(1)} %constant_dynamic-update-slice_fusion.6.refs_2_), channel_id=1, source_target_pairs={{0,4},{4,0},{8,12},{12,8},{16,20},{20,16},{24,28},{28,24},{1,5},{5... | collective-permute-start | bytes 786440 | tf_op jit(solution)/shard_map/ppermute | solution.py:289
  39.2 1.6 %collective-permute-start.8 = (bf16[2,4,16,1024]{3,2,1,0:T(8,128)(2,1)S(1)}, bf16[2,4,16,1024]{3,2,1,0:T(8,128)(2,1)S(1)}, u32[]{:S(2)}, u32[]{:S(2)}) collective-permute-start(bf16[2,4,16,1024]{3,2,1,0:T(8,128)(2,1)S(1)} %get-tuple-element.33), channel_id=1, source_target_pairs={{0,4},{4,0},{8,12},{12,8},{16,20},{20,16},{24,28},{28,24},{1,5},{5... | collective-permute-start | bytes 786440 | tf_op jit(solution)/shard_map/ppermute | solution.py:289
  40.9 5.2 %collective-permute-start.13 = (bf16[3,4,16,1024]{3,2,1,0:T(8,128)(2,1)S(1)}, bf16[3,4,16,1024]{3,2,1,0:T(8,128)(2,1)S(1)}, u32[]{:S(2)}, u32[]{:S(2)}) collective-permute-start(bf16[3,4,16,1024]{3,2,1,0:T(8,128)(2,1)S(1)} %get-tuple-element.37), channel_id=1, source_target_pairs={{0,4},{4,0},{8,12},{12,8},{16,20},{20,16},{24,28},{28,24},{1,5},{5... | collective-permute-start | bytes 1179656 | tf_op jit(solution)/shard_map/ppermute | solution.py:289
  41.1 5.0 %collective-permute-start.15 = (bf16[4,16,1024]{2,1,0:T(8,128)(2,1)S(1)}, bf16[4,16,1024]{2,1,0:T(8,128)(2,1)S(1)}, u32[]{:S(2)}, u32[]{:S(2)}) collective-permute-start(bf16[4,16,1024]{2,1,0:T(8,128)(2,1)S(1)} %get-tuple-element.38), channel_id=1, source_target_pairs={{0,16},{4,12},{8,24},{12,4},{16,0},{20,28},{24,8},{28,20},{1,17},{... | collective-permute-start | bytes 393224 | tf_op jit(solution)/shard_map/ppermute | solution.py:293
  42.6 5.0 %collective-permute-start.11 = (bf16[4,16,1024]{2,1,0:T(8,128)(2,1)S(1)}, bf16[4,16,1024]{2,1,0:T(8,128)(2,1)S(1)}, u32[]{:S(2)}, u32[]{:S(2)}) collective-permute-start(bf16[4,16,1024]{2,1,0:T(8,128)(2,1)S(1)} %get-tuple-element.36), channel_id=1, source_target_pairs={{0,16},{4,12},{8,24},{12,4},{16,0},{20,28},{24,8},{28,20},{1,17},{... | collective-permute-start | bytes 393224 | tf_op jit(solution)/shard_map/ppermute | solution.py:293
  43.9 3.6 %collective-permute-start.9 = (bf16[3,4,16,1024]{3,2,1,0:T(8,128)(2,1)S(1)}, bf16[3,4,16,1024]{3,2,1,0:T(8,128)(2,1)S(1)}, u32[]{:S(2)}, u32[]{:S(2)}) collective-permute-start(bf16[3,4,16,1024]{3,2,1,0:T(8,128)(2,1)S(1)} %get-tuple-element.35), channel_id=1, source_target_pairs={{0,4},{4,0},{8,12},{12,8},{16,20},{20,16},{24,28},{28,24},{1,5},{5... | collective-permute-start | bytes 1179656 | tf_op jit(solution)/shard_map/ppermute | solution.py:289
  46.1 6.4 %collective-permute-start.16 = (bf16[4,16,1024]{2,1,0:T(8,128)(2,1)S(1)}, bf16[4,16,1024]{2,1,0:T(8,128)(2,1)S(1)}, u32[]{:S(2)}, u32[]{:S(2)}) collective-permute-start(bf16[4,16,1024]{2,1,0:T(8,128)(2,1)S(1)} %fusion), channel_id=1, source_target_pairs={{0,8},{4,20},{8,0},{12,28},{16,24},{20,4},{24,16},{28,12},{1,9},{5... | collective-permute-start | bytes 393224 | tf_op jit(solution)/shard_map/ppermute | solution.py:293
  46.9 5.7 %collective-permute-start.14 = (bf16[4,16,1024]{2,1,0:T(8,128)(2,1)S(1)}, bf16[4,16,1024]{2,1,0:T(8,128)(2,1)S(1)}, u32[]{:S(2)}, u32[]{:S(2)}) collective-permute-start(bf16[4,16,1024]{2,1,0:T(8,128)(2,1)S(1)} %fusion.7), channel_id=1, source_target_pairs={{0,16},{4,12},{8,24},{12,4},{16,0},{20,28},{24,8},{28,20},{1,17},{... | collective-permute-start | bytes 393224 | tf_op jit(solution)/shard_map/ppermute | solution.py:293
  47.6 6.9 %collective-permute-start.12 = (bf16[4,16,1024]{2,1,0:T(8,128)(2,1)S(1)}, bf16[4,16,1024]{2,1,0:T(8,128)(2,1)S(1)}, u32[]{:S(2)}, u32[]{:S(2)}) collective-permute-start(bf16[4,16,1024]{2,1,0:T(8,128)(2,1)S(1)} %fusion.2), channel_id=1, source_target_pairs={{0,8},{4,20},{8,0},{12,28},{16,24},{20,4},{24,16},{28,12},{1,9},{5... | collective-permute-start | bytes 393224 | tf_op jit(solution)/shard_map/ppermute | solution.py:293
  49.2 5.3 %collective-permute-start.10 = (bf16[4,16,1024]{2,1,0:T(8,128)(2,1)S(1)}, bf16[4,16,1024]{2,1,0:T(8,128)(2,1)S(1)}, u32[]{:S(2)}, u32[]{:S(2)}) collective-permute-start(bf16[4,16,1024]{2,1,0:T(8,128)(2,1)S(1)} %fusion.6), channel_id=1, source_target_pairs={{0,16},{4,12},{8,24},{12,4},{16,0},{20,28},{24,8},{28,20},{1,17},{... | collective-permute-start | bytes 393224 | tf_op jit(solution)/shard_map/ppermute | solution.py:293
  54.6 4.5 %collective-permute-start.19 = (bf16[16,2048]{1,0:T(8,128)(2,1)S(1)}, bf16[16,2048]{1,0:T(8,128)(2,1)S(1)}, u32[]{:S(2)}, u32[]{:S(2)}) collective-permute-start(bf16[16,2048]{1,0:T(8,128)(2,1)S(1)} %pad_maximum_fusion.2), channel_id=1, source_target_pairs={{0,1},{1,0},{2,3},{3,2},{4,5},{5,4},{6,7},{7,6},{8,9},{9,8},{10,11... | collective-permute-start | bytes 196616 | tf_op jit(solution)/shard_map/ppermute | solution.py:296
  54.9 7.4 %collective-permute-start.18 = (bf16[16,2048]{1,0:T(8,128)(2,1)S(1)}, bf16[16,2048]{1,0:T(8,128)(2,1)S(1)}, u32[]{:S(2)}, u32[]{:S(2)}) collective-permute-start(bf16[16,2048]{1,0:T(8,128)(2,1)S(1)} %pad_maximum_fusion.1), channel_id=1, source_target_pairs={{0,2},{1,3},{2,0},{3,1},{4,6},{5,7},{6,4},{7,5},{8,10},{9,11},{10,... | collective-permute-start | bytes 196616 | tf_op jit(solution)/shard_map/ppermute | solution.py:296
  56.0 6.3 %collective-permute-start.17 = (bf16[16,2048]{1,0:T(8,128)(2,1)S(1)}, bf16[16,2048]{1,0:T(8,128)(2,1)S(1)}, u32[]{:S(2)}, u32[]{:S(2)}) collective-permute-start(bf16[16,2048]{1,0:T(8,128)(2,1)S(1)} %pad_maximum_fusion), channel_id=1, source_target_pairs={{0,3},{1,2},{2,1},{3,0},{4,7},{5,6},{6,5},{7,4},{8,11},{9,10},{10,... | collective-permute-start | bytes 196616 | tf_op jit(solution)/shard_map/ppermute | solution.py:296

commit v8 on v7

--- a/solution.py
+++ b/solution.py
@@ -47,6 +47,12 @@
 
 def lanes_of(n_seq):
     return -(-n_seq * ACT_DEV // LANES) * LANES
+
+
+def arrive(copies, i):
+    copies[i].wait()
+    if i + FLIGHT < len(copies):
+        copies[i + FLIGHT].start()
 
 
 def select_kernel(mask_ref, hidden_ref, *refs):
@@ -98,38 +104,9 @@
     return own, picker
 
 
-def head_copies(head_ref, head_here, sems):
-    chunks, step, _ = head_here.shape
-    copies = [
-        pltpu.make_async_copy(head_ref.at[pl.ds(i * step, step), :], head_here.at[i], sems.at[i])
-        for i in range(chunks)
-    ]
-    for copy in copies[:FLIGHT]:
-        copy.start()
-    return copies
-
-
-def arrive(copies, i):
-    copies[i].wait()
-    if i + FLIGHT < len(copies):
-        copies[i + FLIGHT].start()
-
-
-def head_scratch(head):
-    width, shard = head.shape
-    return [
-        pltpu.VMEM((CHUNKS, width // CHUNKS, shard), BF16),
-        pltpu.SemaphoreType.DMA((CHUNKS,)),
-    ]
-
-
 def logits_kernel(n_seq, *refs):
-    block_refs, head_ref, picker_ref, logits_ref, stats_ref, packed, head_here, sems = (
-        refs[:4],
-        *refs[4:],
-    )
-    copies = head_copies(head_ref, head_here, sems)
-    step = head_here.shape[1]
+    *block_refs, head_ref, picker_ref, logits_ref, stats_ref, packed = refs
+    step = head_ref.shape[0] // CHUNKS
     each = CHUNKS // PARTS
     logits = None
     for i in range(CHUNKS):
@@ -140,8 +117,8 @@
             start = (i // each) * size
             rows.append(ref[start : start + size, at : at + step])
         rows = jnp.concatenate(rows, axis=0)
-        arrive(copies, i)
-        part = jnp.dot(rows, head_here[i], preferred_element_type=F32)
+        head = head_ref[i * step : (i + 1) * step, :]
+        part = jnp.dot(rows, head, preferred_element_type=F32)
         logits = part if logits is None else logits + part
     logits_ref[...] = logits
     top = jnp.max(logits, axis=1, keepdims=True)
@@ -166,15 +143,14 @@
 def local_logits(n_seq, n_vocab, blocks, head, picker):
     shard = head.shape[1]
     rows, lanes = n_seq * ACT_DEV, lanes_of(n_seq)
-    vmem = pl.BlockSpec(memory_space=pltpu.VMEM)
     return pl.pallas_call(
         functools.partial(logits_kernel, n_seq),
-        in_specs=[vmem] * 4 + [pl.BlockSpec(memory_space=pl.ANY), vmem],
+        in_specs=[pl.BlockSpec(memory_space=pltpu.VMEM)] * 6,
         out_shape=[
             jax.ShapeDtypeStruct((rows, shard), F32),
             jax.ShapeDtypeStruct((n_seq * n_vocab, 4, lanes), F32),
         ],
-        scratch_shapes=[pltpu.VMEM((lanes, LANES), F32)] + head_scratch(head),
+        scratch_shapes=[pltpu.VMEM((lanes, LANES), F32)],
         compiler_params=params(),
         name="local_logits",
     )(*blocks, head, picker)
@@ -220,9 +196,8 @@
 
 
 def gradient_kernel(n_seq, n_vocab, stats_ref, logits_ref, head_ref, *refs):
-    *out_refs, last_ref, columns, ordered, head_here, sems = refs
+    *out_refs, last_ref, columns, ordered = refs
     near_refs, far_refs = out_refs[:PARTS], out_refs[PARTS:]
-    copies = head_copies(head_ref, head_here, sems)
     top, total, centred = merged(stats_ref[...])
     row = iota((8, top.shape[1]), 0)
     lines = jnp.where(row == 0, top, jnp.where(row == 1, 1.0 / total, top + centred))
@@ -235,45 +210,38 @@
     score = (prob * (ordered[:, 2:3] - logits)).astype(BF16)
     n_chip = n_seq // 2
     last = n_chip - 1
-    step = head_here.shape[1]
-    span = step * CHUNKS // (n_vocab * PARTS)
-    size = min(step, span)
-    for i in range(CHUNKS):
-        arrive(copies, i)
-        for j in range(step // size):
-            start = i * step + j * size
-            v, c, at = start // (span * PARTS), start // span % PARTS, start % span
+    size = near_refs[0].shape[3]
+    for v in range(n_vocab):
+        for c in range(PARTS):
+            start = (v * PARTS + c) * size
             part = lax.dot_general(
                 score,
-                head_here[i, j * size : (j + 1) * size, :],
+                head_ref[start : start + size, :],
                 (((1,), (1,)), ((), ())),
                 preferred_element_type=F32,
             ).astype(BF16)
             blocks = part.reshape(n_seq, ACT_DEV, size)
-            cut = slice(at, at + size)
-            near_refs[c][:last, v, :, cut] = blocks[:last]
-            far_refs[c][:, v, :, cut] = blocks[last : 2 * last]
-            near_refs[c][last, v, :, cut] = blocks[2 * last]
-            last_ref[c, v, :, cut] = blocks[2 * last + 1]
+            near_refs[c][:last, v] = blocks[:last]
+            far_refs[c][:, v] = blocks[last : 2 * last]
+            near_refs[c][last, v] = blocks[2 * last]
+            last_ref[c, v] = blocks[2 * last + 1]
 
 
 def gradients(n_seq, n_vocab, stats, logits, head):
     rows = logits.shape[0]
     n_chip = n_seq // 2
     block = (n_vocab, ACT_DEV, head.shape[0] // (n_vocab * PARTS))
-    vmem = pl.BlockSpec(memory_space=pltpu.VMEM)
     outs = [jax.ShapeDtypeStruct((n_chip,) + block, BF16)] * PARTS
     outs += [jax.ShapeDtypeStruct((n_chip - 1,) + block, BF16)] * PARTS
     outs += [jax.ShapeDtypeStruct((PARTS,) + block, BF16)]
     *outs, far_last = pl.pallas_call(
         functools.partial(gradient_kernel, n_seq, n_vocab),
-        in_specs=[vmem, vmem, pl.BlockSpec(memory_space=pl.ANY)],
+        in_specs=[pl.BlockSpec(memory_space=pltpu.VMEM)] * 3,
         out_shape=outs,
         scratch_shapes=[
             pltpu.VMEM((stats.shape[2], LANES), F32),
             pltpu.VMEM((rows, LANES), F32),
-        ]
-        + head_scratch(head),
+        ],
         compiler_params=params(),
         name="gradients",
     )(stats, logits, head)
@@ -300,7 +268,12 @@
     near = [own]
     for a in range(1, n_chip):
         step = a.bit_length() - 1
-        near.append([swap_chip(part, step) for part in near[a ^ (1 << step)]])
+        source = near[a ^ (1 << step)]
+        if a > 1 and a == 1 << step:
+            moved = swap_chip(jnp.concatenate(source, axis=1), step)
+            near.append(jnp.split(moved, PARTS, axis=1))
+        else:
+            near.append([swap_chip(part, step) for part in source])
     early = jnp.concatenate([near[a][c] for c in range(PARTS) for a in range(last)], axis=0)
     early, near[last][0] = lax.optimization_barrier((early, near[last][0]))
     late = jnp.concatenate(near[last], axis=0)
@@ -309,8 +282,6 @@
     logits, stats = local_logits(n_seq, n_vocab, blocks, head, picker)
     stats = lax.all_to_all(stats, ("seq", "vocab"), 0, 0, tiled=True)
     near, far, far_last = gradients(n_seq, n_vocab, stats, logits, head)
-    each, average = entropies(n_vocab, stats, picker)
-
     moved = swap_core(far_last)
     first = [(near[c][last].astype(F32) + moved[c].astype(F32)).astype(BF16) for c in range(PARTS)]
     far, first = lax.optimization_barrier((far, first))
@@ -319,9 +290,17 @@
     sums.append(first)
     for a in range(last, 0, -1):
         step = a.bit_length() - 1
+        parts = [part.astype(BF16) for part in sums[a]]
+        if a > 1 and a == 1 << step:
+            moved = jnp.split(swap_chip(jnp.concatenate(parts, axis=2), step), PARTS, axis=2)
+        else:
+            moved = [swap_chip(part, step) for part in parts]
+        target = sums[a ^ (1 << step)]
         for c in range(PARTS):
-            sums[a ^ (1 << step)][c] += swap_chip(sums[a][c].astype(BF16), step).astype(F32)
-
+            target[c] += moved[c].astype(F32)
+
+    stats, _ = lax.optimization_barrier((stats, sums[0]))
+    each, average = entropies(n_vocab, stats, picker)
     column = lax.axis_index("vocab")
 
     def piece(k):

time: 63.6 us -> 61.1 us (0.961)
  Pallas kernels: 8.92 us -> 6.13 us
  waiting for transfers between devices: 20.9 us -> 18.8 us
  starting transfers between devices: 18 us -> 19.8 us
    ppermute x12 -> x10, waiting for transfers between devices: 14.5 us -> 12.8 us  [swap_chip(): lax.ppermute(value, 'seq', [(i, i ^ flips[i & 1]) for i in range(n_seq)])]
    ppermute x12 -> x10, starting transfers between devices: 13.2 us -> 14.9 us  [swap_chip(): lax.ppermute(value, 'seq', [(i, i ^ flips[i & 1]) for i in range(n_seq)])]
    pallas_call x1, Pallas kernels: 3.14 us -> 1.64 us  [gradients(): pl.pallas_call(functools.partial(gradient_kernel, n_seq, n_vocab), in_spe...]
    pallas_call x1, Pallas kernels: 2.26 us -> 0.97 us  [local_logits(): pl.pallas_call(functools.partial(logits_kernel, n_seq), in_specs=[pl.Bloc...]
  transfers between devices with their start and end apart: 20 -> 18, of which waited for: 11 -> 10; matrix products, arithmetic and copies ran while one was open for 1% -> 1% of each run, Pallas kernels for 1% -> 1%
where the time goes in v8:
time: 61.1 us; the launch traced here: 61 us
  starting transfers between devices  19.8 us (32%)
  waiting for transfers between devices  18.8 us (31%)
  blocking collectives  13.7 us (22%)
  Pallas kernels  6.13 us (10%)
  matrix products  1.11 us (2%)
  between operations  0.82 us (1%)
    ppermute x10, starting transfers between devices, swap_chip(): lax.ppermute(value, 'seq', [(i, i ^ flips[i & 1]) for i in range(n_seq)])  14.9 us
    all_to_all x1, blocking collectives, body(): stats = lax.all_to_all(stats, ('seq', 'vocab'), 0, 0, tiled=True)  13.7 us
    ppermute x10, waiting for transfers between devices, swap_chip(): lax.ppermute(value, 'seq', [(i, i ^ flips[i & 1]) for i in range(n_seq)])  12.8 us
    ppermute x3, starting transfers between devices, send_vocab(): return lax.ppermute(value, 'vocab', [(i, i ^ k) for i in range(n_vocab)])  4.45 us
    ppermute x5, waiting for transfers between devices, swap_core(): return lax.ppermute(value, 'seq', [(i, i ^ 1) for i in range(n_seq)])  3.05 us
    ppermute x3, waiting for transfers between devices, send_vocab(): return lax.ppermute(value, 'vocab', [(i, i ^ k) for i in range(n_vocab)])  2.98 us
    pallas_call x1, Pallas kernels, select(): pl.pallas_call(select_kernel, in_specs=[pl.BlockSpec(memory_space=pltpu.H...  2.75 us
    pallas_call x1, Pallas kernels, gradients(): pl.pallas_call(functools.partial(gradient_kernel, n_seq, n_vocab), in_spe...  1.64 us
  transfers between devices with their start and end apart: 18, of which 10 were waited for; matrix products, arithmetic and copies ran while one was open for 1% of the time, Pallas kernels for 1%

profile of v8, /device:TPU:0, one launch (start us, length us, event | category | flops | bytes accessed | tf_op | source)
XLA Modules:
  0.0 61.0 jit_solution(13053948202864452286)
XLA Ops:
  0.6 0.0 copy-start
  0.6 2.8 %select_rows.1 = (bf16[16,4096]{1,0:T(8,128)(2,1)S(1)}, bf16[16,4096]{1,0:T(8,128)(2,1)S(1)}, bf16[16,128]{1,0:T(8,128)(2,1)S(1)}) custom-call(s32[1,128]{1,0:T(1,128)} %bitcast.44, bf16[128,8192]{1,0:T(8,128)(2,1)} %hidden_ref.1), custom_call_target="tpu_custom_call" | custom-call | tf_op jit(solution)/shard_map/select_rows/pallas_call | solution.py:91
  3.4 3.0 %collective-permute-start = (bf16[16,4096]{1,0:T(8,128)(2,1)S(1)}, bf16[16,4096]{1,0:T(8,128)(2,1)S(1)}, u32[]{:S(2)}, u32[]{:S(2)}) collective-permute-start(bf16[16,4096]{1,0:T(8,128)(2,1)S(1)} %get-tuple-element.22), channel_id=1, source_target_pairs={{0,8},{4,20},{8,0},{12,28},{16,24},{20,4},{24,16},{28,12},{1,9},{5... | collective-permute-start | bytes 393224 | tf_op jit(solution)/shard_map/ppermute | solution.py:261
  6.4 0.1 collective-permute-start.2
  6.5 2.0 %collective-permute-start.1 = (bf16[16,8192]{1,0:T(8,128)(2,1)S(1)}, bf16[16,8192]{1,0:T(8,128)(2,1)S(1)}, u32[]{:S(2)}, u32[]{:S(2)}) collective-permute-start(bf16[16,8192]{1,0:T(8,128)(2,1)S(1)} %pad_maximum_fusion), channel_id=1, source_target_pairs={{0,16},{4,12},{8,24},{12,4},{16,0},{20,28},{24,8},{28,20},{1,17},{... | collective-permute-start | bytes 786440 | tf_op jit(solution)/shard_map/ppermute | solution.py:261
  8.6 1.4 %collective-permute-done = bf16[16,4096]{1,0:T(8,128)(2,1)S(1)} collective-permute-done((bf16[16,4096]{1,0:T(8,128)(2,1)S(1)}, bf16[16,4096]{1,0:T(8,128)(2,1)S(1)}, u32[]{:S(2)}, u32[]{:S(2)}) %collective-permute-start) | collective-permute-done | bytes 131104 | tf_op jit(solution)/shard_map/ppermute | solution.py:261
  10.0 2.5 %collective-permute-start.3 = (bf16[16,4096]{1,0:T(8,128)(2,1)S(1)}, bf16[16,4096]{1,0:T(8,128)(2,1)S(1)}, u32[]{:S(2)}, u32[]{:S(2)}) collective-permute-start(bf16[16,4096]{1,0:T(8,128)(2,1)S(1)} %collective-permute-done), channel_id=1, source_target_pairs={{0,16},{4,12},{8,24},{12,4},{16,0},{20,28},{24,8},{28,20},{1,17},{... | collective-permute-start | bytes 393224 | tf_op jit(solution)/shard_map/ppermute | solution.py:261
  12.5 0.3 collective-permute-done.2
  12.8 2.5 %collective-permute-start.5 = (bf16[16,4096]{1,0:T(8,128)(2,1)S(1)}, bf16[16,4096]{1,0:T(8,128)(2,1)S(1)}, u32[]{:S(2)}, u32[]{:S(2)}) collective-permute-start(bf16[16,4096]{1,0:T(8,128)(2,1)S(1)} %collective-permute-done.2), channel_id=1, source_target_pairs={{0,16},{4,12},{8,24},{12,4},{16,0},{20,28},{24,8},{28,20},{1,17},{... | collective-permute-start | bytes 393224 | tf_op jit(solution)/shard_map/ppermute | solution.py:261
  15.3 0.0 collective-permute-done.1
  15.4 0.0 collective-permute-done.3
  15.4 0.0 collective-permute-start.4
  15.5 2.7 %collective-permute-done.5 = bf16[16,4096]{1,0:T(8,128)(2,1)S(1)} collective-permute-done((bf16[16,4096]{1,0:T(8,128)(2,1)S(1)}, bf16[16,4096]{1,0:T(8,128)(2,1)S(1)}, u32[]{:S(2)}, u32[]{:S(2)}) %collective-permute-start.5) | collective-permute-done | bytes 131104 | tf_op jit(solution)/shard_map/ppermute | solution.py:261
  18.2 0.1 collective-permute-start.6
  18.3 1.5 %collective-permute-done.6.refs_3_ = bf16[32,4096]{1,0:T(8,128)(2,1)S(1)} collective-permute-done((bf16[32,4096]{1,0:T(8,128)(2,1)S(1)}, bf16[32,4096]{1,0:T(8,128)(2,1)S(1)}, u32[]{:S(2)}, u32[]{:S(2)}) %collective-permute-start.6) | collective-permute-done | bytes 262176 | tf_op jit(solution)/shard_map/ppermute | solution.py:257
  19.8 0.0 collective-permute-done.4.refs_1_
  19.8 0.0 copy-done
  19.8 1.0 %local_logits.1 = (f32[128,256]{1,0:T(8,128)S(1)}, f32[32,4,128]{2,1,0:T(4,128)S(1)}) custom-call(bf16[96,4096]{1,0:T(8,128)(2,1)S(1)} %slice_dynamic-update-slice_fusion.refs_0_, bf16[96,4096]{1,0:T(8,128)(2,1)S(1)} %collective-permute-done.4.refs_1_, bf16[32,4096]{1,0:T(8,128)(2,1)S(1)} %constant_dynamic-update-slice_fusion.4.refs_2_, ...), custom_call_target="tpu_custom_call" | custom-call | tf_op jit(solution)/shard_map/local_logits/pallas_call | solution.py:146
  20.8 13.7 %all_to_all.5.stats_ref = f32[32,4,128]{2,1,0:T(4,128)S(1)} all-to-all(f32[32,4,128]{2,1,0:T(4,128)S(1)} %get-tuple-element.27), channel_id=1, replica_groups=mesh['seq'=8,'vocab'=4] {'seq','vocab'}, dimensions={0} | all-to-all | bytes 131072 | tf_op jit(solution)/shard_map/all_to_all | solution.py:283
  34.5 1.6 %gradients.1 = (bf16[4,4,16,1024]{3,2,1,0:T(8,128)(2,1)S(1)}, bf16[4,4,16,1024]{3,2,1,0:T(8,128)(2,1)S(1)}, bf16[3,4,16,1024]{3,2,1,0:T(8,128)(2,1)S(1)}, bf16[3...) custom-call(f32[32,4,128]{2,1,0:T(4,128)S(1)} %all_to_all.5.stats_ref, ...), custom_call_target="tpu_custom_call" | custom-call | tf_op jit(solution)/shard_map/gradients/pallas_call | solution.py:237
  36.1 0.1 collective-permute-start.7
  36.2 1.5 %collective-permute-done.7 = bf16[2,4,16,1024]{3,2,1,0:T(8,128)(2,1)S(1)} collective-permute-done((bf16[2,4,16,1024]{3,2,1,0:T(8,128)(2,1)S(1)}, bf16[2,4,16,1024]{3,2,1,0:T(8,128)(2,1)S(1)}, u32[]{:S(2)}, u32[]{:S(2)}) %collective-permute-start.7) | collective-permute-done | bytes 262176 | tf_op jit(solution)/shard_map/ppermute | solution.py:257
  37.7 0.1 fusion.5
  37.8 0.2 collective-permute-start.8
  38.0 0.7 %collective-permute-start.11 = (bf16[4,16,1024]{2,1,0:T(8,128)(2,1)S(1)}, bf16[4,16,1024]{2,1,0:T(8,128)(2,1)S(1)}, u32[]{:S(2)}, u32[]{:S(2)}) collective-permute-start(bf16[4,16,1024]{2,1,0:T(8,128)(2,1)S(1)} %get-tuple-element.36), channel_id=1, source_target_pairs={{0,16},{4,12},{8,24},{12,4},{16,0},{20,28},{24,8},{28,20},{1,17},{... | collective-permute-start | bytes 393224 | tf_op jit(solution)/shard_map/ppermute | solution.py:261
  38.7 0.1 collective-permute-start.9
  38.7 1.3 %collective-permute-start.13 = (bf16[4,16,1024]{2,1,0:T(8,128)(2,1)S(1)}, bf16[4,16,1024]{2,1,0:T(8,128)(2,1)S(1)}, u32[]{:S(2)}, u32[]{:S(2)}) collective-permute-start(bf16[4,16,1024]{2,1,0:T(8,128)(2,1)S(1)} %get-tuple-element.37), channel_id=1, source_target_pairs={{0,16},{4,12},{8,24},{12,4},{16,0},{20,28},{24,8},{28,20},{1,17},{... | collective-permute-start | bytes 393224 | tf_op jit(solution)/shard_map/ppermute | solution.py:261
  40.0 2.9 %collective-permute-done.11 = bf16[4,16,1024]{2,1,0:T(8,128)(2,1)S(1)} collective-permute-done((bf16[4,16,1024]{2,1,0:T(8,128)(2,1)S(1)}, bf16[4,16,1024]{2,1,0:T(8,128)(2,1)S(1)}, u32[]{:S(2)}, u32[]{:S(2)}) %collective-permute-start.11) | collective-permute-done | bytes 131104 | tf_op jit(solution)/shard_map/ppermute | solution.py:261
  43.0 0.0 collective-permute-done.8
  43.0 0.1 fusion.2
  43.0 0.7 %collective-permute-start.12 = (bf16[4,16,1024]{2,1,0:T(8,128)(2,1)S(1)}, bf16[4,16,1024]{2,1,0:T(8,128)(2,1)S(1)}, u32[]{:S(2)}, u32[]{:S(2)}) collective-permute-start(bf16[4,16,1024]{2,1,0:T(8,128)(2,1)S(1)} %fusion.2), channel_id=1, source_target_pairs={{0,8},{4,20},{8,0},{12,28},{16,24},{20,4},{24,16},{28,12},{1,9},{5... | collective-permute-start | bytes 393224 | tf_op jit(solution)/shard_map/ppermute | solution.py:261
  43.8 0.0 collective-permute-done.9
  43.9 0.6 collective-permute-start.10
  44.5 0.0 collective-permute-done.13
  44.5 0.1 fusion
  44.5 1.6 %collective-permute-start.14 = (bf16[4,16,1024]{2,1,0:T(8,128)(2,1)S(1)}, bf16[4,16,1024]{2,1,0:T(8,128)(2,1)S(1)}, u32[]{:S(2)}, u32[]{:S(2)}) collective-permute-start(bf16[4,16,1024]{2,1,0:T(8,128)(2,1)S(1)} %fusion), channel_id=1, source_target_pairs={{0,8},{4,20},{8,0},{12,28},{16,24},{20,4},{24,16},{28,12},{1,9},{5... | collective-permute-start | bytes 393224 | tf_op jit(solution)/shard_map/ppermute | solution.py:261
  46.1 3.3 %collective-permute-done.12 = bf16[4,16,1024]{2,1,0:T(8,128)(2,1)S(1)} collective-permute-done((bf16[4,16,1024]{2,1,0:T(8,128)(2,1)S(1)}, bf16[4,16,1024]{2,1,0:T(8,128)(2,1)S(1)}, u32[]{:S(2)}, u32[]{:S(2)}) %collective-permute-start.12) | collective-permute-done | bytes 131104 | tf_op jit(solution)/shard_map/ppermute | solution.py:261
  49.4 2.0 %collective-permute-done.14 = bf16[4,16,1024]{2,1,0:T(8,128)(2,1)S(1)} collective-permute-done((bf16[4,16,1024]{2,1,0:T(8,128)(2,1)S(1)}, bf16[4,16,1024]{2,1,0:T(8,128)(2,1)S(1)}, u32[]{:S(2)}, u32[]{:S(2)}) %collective-permute-start.14) | collective-permute-done | bytes 131104 | tf_op jit(solution)/shard_map/ppermute | solution.py:261
  51.4 0.0 collective-permute-done.10
  51.4 0.2 fusion.1
  51.6 0.9 %collective-permute-start.15 = (bf16[16,2048]{1,0:T(8,128)(2,1)S(1)}, bf16[16,2048]{1,0:T(8,128)(2,1)S(1)}, u32[]{:S(2)}, u32[]{:S(2)}) collective-permute-start(bf16[16,2048]{1,0:T(8,128)(2,1)S(1)} %pad_maximum_fusion.2), channel_id=1, source_target_pairs={{0,3},{1,2},{2,1},{3,0},{4,7},{5,6},{6,5},{7,4},{8,11},{9,10},{10,... | collective-permute-start | bytes 196616 | tf_op jit(solution)/shard_map/ppermute | solution.py:264
  52.5 0.9 %collective-permute-start.16 = (bf16[16,2048]{1,0:T(8,128)(2,1)S(1)}, bf16[16,2048]{1,0:T(8,128)(2,1)S(1)}, u32[]{:S(2)}, u32[]{:S(2)}) collective-permute-start(bf16[16,2048]{1,0:T(8,128)(2,1)S(1)} %pad_maximum_fusion.3), channel_id=1, source_target_pairs={{0,2},{1,3},{2,0},{3,1},{4,6},{5,7},{6,4},{7,5},{8,10},{9,11},{10,... | collective-permute-start | bytes 196616 | tf_op jit(solution)/shard_map/ppermute | solution.py:264
  53.4 2.7 %collective-permute-start.17 = (bf16[16,2048]{1,0:T(8,128)(2,1)S(1)}, bf16[16,2048]{1,0:T(8,128)(2,1)S(1)}, u32[]{:S(2)}, u32[]{:S(2)}) collective-permute-start(bf16[16,2048]{1,0:T(8,128)(2,1)S(1)} %pad_maximum_fusion.4), channel_id=1, source_target_pairs={{0,1},{1,0},{2,3},{3,2},{4,5},{5,4},{6,7},{7,6},{8,9},{9,8},{10,11... | collective-permute-start | bytes 196616 | tf_op jit(solution)/shard_map/ppermute | solution.py:264
  56.1 0.8 %entropies.1 = (f32[1,128]{1,0:T(1,128)}, f32[1,1]{1,0:T(1,128)}) custom-call(f32[32,4,128]{2,1,0:T(4,128)S(1)} %all_to_all.5.stats_ref, bf16[16,128]{1,0:T(8,128)(2,1)S(1)} %get-tuple-element.26.refs_5_.picker_ref), custom_call_target="tpu_custom_call" | custom-call | tf_op jit(solution)/shard_map/entropies/pallas_call | solution.py:186
  56.9 1.4 %collective-permute-done.15 = bf16[16,2048]{1,0:T(8,128)(2,1)S(1)} collective-permute-done((bf16[16,2048]{1,0:T(8,128)(2,1)S(1)}, bf16[16,2048]{1,0:T(8,128)(2,1)S(1)}, u32[]{:S(2)}, u32[]{:S(2)}) %collective-permute-start.15) | collective-permute-done | bytes 65568 | tf_op jit(solution)/shard_map/ppermute | solution.py:264
  58.2 1.6 %collective-permute-done.16 = bf16[16,2048]{1,0:T(8,128)(2,1)S(1)} collective-permute-done((bf16[16,2048]{1,0:T(8,128)(2,1)S(1)}, bf16[16,2048]{1,0:T(8,128)(2,1)S(1)}, u32[]{:S(2)}, u32[]{:S(2)}) %collective-permute-start.16) | collective-permute-done | bytes 65568 | tf_op jit(solution)/shard_map/ppermute | solution.py:264
  59.8 0.0 collective-permute-done.17
  59.8 1.1 %convolution_convert_fusion = bf16[128,2048]{1,0:T(8,128)(2,1)} fusion(bf16[16,128]{1,0:T(8,128)(2,1)S(1)} %get-tuple-element.26.refs_5_.picker_ref, f32[16,1024]{1,0:T(8,128)S(1)} %get-tuple-element.51, f32[16,1024]{1,0:T(8,128)S(1)} %get-tuple-element.52, bf16[16,2048]{1,0:T(8,128)(2,1)S(1)} %collective-permute-done.17, ...), kind=kOutput, calls=%fused_computation | convolution fusion | flops 8912896 | bytes 856064 | tf_op jit(solution)/shard_map/dot_general | solution.py:313
  (17 shorter events, 0.3 us)
Async XLA Ops:
  0.6 19.2 %copy-start = (bf16[8192,256]{1,0:T(8,128)(2,1)S(1)}, bf16[8192,256]{1,0:T(8,128)(2,1)}, u32[]{:S(2)}) copy-start(bf16[8192,256]{1,0:T(8,128)(2,1)} %head_ref.1) | copy-start | bytes 12582916
  3.4 6.6 %collective-permute-start = (bf16[16,4096]{1,0:T(8,128)(2,1)S(1)}, bf16[16,4096]{1,0:T(8,128)(2,1)S(1)}, u32[]{:S(2)}, u32[]{:S(2)}) collective-permute-start(bf16[16,4096]{1,0:T(8,128)(2,1)S(1)} %get-tuple-element.22), channel_id=1, source_target_pairs={{0,8},{4,20},{8,0},{12,28},{16,24},{20,4},{24,16},{28,12},{1,9},{5... | collective-permute-start | bytes 393224 | tf_op jit(solution)/shard_map/ppermute | solution.py:261
  6.4 6.4 %collective-permute-start.2 = (bf16[16,4096]{1,0:T(8,128)(2,1)S(1)}, bf16[16,4096]{1,0:T(8,128)(2,1)S(1)}, u32[]{:S(2)}, u32[]{:S(2)}) collective-permute-start(bf16[16,4096]{1,0:T(8,128)(2,1)S(1)} %get-tuple-element.23), channel_id=1, source_target_pairs={{0,8},{4,20},{8,0},{12,28},{16,24},{20,4},{24,16},{28,12},{1,9},{5... | collective-permute-start | bytes 393224 | tf_op jit(solution)/shard_map/ppermute | solution.py:261
  6.5 8.8 %collective-permute-start.1 = (bf16[16,8192]{1,0:T(8,128)(2,1)S(1)}, bf16[16,8192]{1,0:T(8,128)(2,1)S(1)}, u32[]{:S(2)}, u32[]{:S(2)}) collective-permute-start(bf16[16,8192]{1,0:T(8,128)(2,1)S(1)} %pad_maximum_fusion), channel_id=1, source_target_pairs={{0,16},{4,12},{8,24},{12,4},{16,0},{20,28},{24,8},{28,20},{1,17},{... | collective-permute-start | bytes 786440 | tf_op jit(solution)/shard_map/ppermute | solution.py:261
  10.0 5.4 %collective-permute-start.3 = (bf16[16,4096]{1,0:T(8,128)(2,1)S(1)}, bf16[16,4096]{1,0:T(8,128)(2,1)S(1)}, u32[]{:S(2)}, u32[]{:S(2)}) collective-permute-start(bf16[16,4096]{1,0:T(8,128)(2,1)S(1)} %collective-permute-done), channel_id=1, source_target_pairs={{0,16},{4,12},{8,24},{12,4},{16,0},{20,28},{24,8},{28,20},{1,17},{... | collective-permute-start | bytes 393224 | tf_op jit(solution)/shard_map/ppermute | solution.py:261
  12.8 5.4 %collective-permute-start.5 = (bf16[16,4096]{1,0:T(8,128)(2,1)S(1)}, bf16[16,4096]{1,0:T(8,128)(2,1)S(1)}, u32[]{:S(2)}, u32[]{:S(2)}) collective-permute-start(bf16[16,4096]{1,0:T(8,128)(2,1)S(1)} %collective-permute-done.2), channel_id=1, source_target_pairs={{0,16},{4,12},{8,24},{12,4},{16,0},{20,28},{24,8},{28,20},{1,17},{... | collective-permute-start | bytes 393224 | tf_op jit(solution)/shard_map/ppermute | solution.py:261
  15.4 4.4 %collective-permute-start.4 = (bf16[96,4096]{1,0:T(8,128)(2,1)S(1)}, bf16[96,4096]{1,0:T(8,128)(2,1)S(1)}, u32[]{:S(2)}, u32[]{:S(2)}) collective-permute-start(bf16[96,4096]{1,0:T(8,128)(2,1)S(1)} %slice_dynamic-update-slice_fusion.refs_0_), channel_id=1, source_target_pairs={{0,4},{4,0},{8,12},{12,8},{16,20},{20,16},{24,28},{28,24},{1,5},{5... | collective-permute-start | bytes 2359304 | tf_op jit(solution)/shard_map/ppermute | solution.py:257
  18.2 1.6 %collective-permute-start.6 = (bf16[32,4096]{1,0:T(8,128)(2,1)S(1)}, bf16[32,4096]{1,0:T(8,128)(2,1)S(1)}, u32[]{:S(2)}, u32[]{:S(2)}) collective-permute-start(bf16[32,4096]{1,0:T(8,128)(2,1)S(1)} %constant_dynamic-update-slice_fusion.4.refs_2_), channel_id=1, source_target_pairs={{0,4},{4,0},{8,12},{12,8},{16,20},{20,16},{24,28},{28,24},{1,5},{5... | collective-permute-start | bytes 786440 | tf_op jit(solution)/shard_map/ppermute | solution.py:257
  36.1 1.6 %collective-permute-start.7 = (bf16[2,4,16,1024]{3,2,1,0:T(8,128)(2,1)S(1)}, bf16[2,4,16,1024]{3,2,1,0:T(8,128)(2,1)S(1)}, u32[]{:S(2)}, u32[]{:S(2)}) collective-permute-start(bf16[2,4,16,1024]{3,2,1,0:T(8,128)(2,1)S(1)} %get-tuple-element.32), channel_id=1, source_target_pairs={{0,4},{4,0},{8,12},{12,8},{16,20},{20,16},{24,28},{28,24},{1,5},{5... | collective-permute-start | bytes 786440 | tf_op jit(solution)/shard_map/ppermute | solution.py:257
  37.8 5.2 %collective-permute-start.8 = (bf16[3,4,16,1024]{3,2,1,0:T(8,128)(2,1)S(1)}, bf16[3,4,16,1024]{3,2,1,0:T(8,128)(2,1)S(1)}, u32[]{:S(2)}, u32[]{:S(2)}) collective-permute-start(bf16[3,4,16,1024]{3,2,1,0:T(8,128)(2,1)S(1)} %get-tuple-element.34), channel_id=1, source_target_pairs={{0,4},{4,0},{8,12},{12,8},{16,20},{20,16},{24,28},{28,24},{1,5},{5... | collective-permute-start | bytes 1179656 | tf_op jit(solution)/shard_map/ppermute | solution.py:257
  38.0 5.0 %collective-permute-start.11 = (bf16[4,16,1024]{2,1,0:T(8,128)(2,1)S(1)}, bf16[4,16,1024]{2,1,0:T(8,128)(2,1)S(1)}, u32[]{:S(2)}, u32[]{:S(2)}) collective-permute-start(bf16[4,16,1024]{2,1,0:T(8,128)(2,1)S(1)} %get-tuple-element.36), channel_id=1, source_target_pairs={{0,16},{4,12},{8,24},{12,4},{16,0},{20,28},{24,8},{28,20},{1,17},{... | collective-permute-start | bytes 393224 | tf_op jit(solution)/shard_map/ppermute | solution.py:261
  38.7 5.1 %collective-permute-start.9 = (bf16[3,4,16,1024]{3,2,1,0:T(8,128)(2,1)S(1)}, bf16[3,4,16,1024]{3,2,1,0:T(8,128)(2,1)S(1)}, u32[]{:S(2)}, u32[]{:S(2)}) collective-permute-start(bf16[3,4,16,1024]{3,2,1,0:T(8,128)(2,1)S(1)} %get-tuple-element.35), channel_id=1, source_target_pairs={{0,4},{4,0},{8,12},{12,8},{16,20},{20,16},{24,28},{28,24},{1,5},{5... | collective-permute-start | bytes 1179656 | tf_op jit(solution)/shard_map/ppermute | solution.py:257
  38.7 5.7 %collective-permute-start.13 = (bf16[4,16,1024]{2,1,0:T(8,128)(2,1)S(1)}, bf16[4,16,1024]{2,1,0:T(8,128)(2,1)S(1)}, u32[]{:S(2)}, u32[]{:S(2)}) collective-permute-start(bf16[4,16,1024]{2,1,0:T(8,128)(2,1)S(1)} %get-tuple-element.37), channel_id=1, source_target_pairs={{0,16},{4,12},{8,24},{12,4},{16,0},{20,28},{24,8},{28,20},{1,17},{... | collective-permute-start | bytes 393224 | tf_op jit(solution)/shard_map/ppermute | solution.py:261
  43.0 6.4 %collective-permute-start.12 = (bf16[4,16,1024]{2,1,0:T(8,128)(2,1)S(1)}, bf16[4,16,1024]{2,1,0:T(8,128)(2,1)S(1)}, u32[]{:S(2)}, u32[]{:S(2)}) collective-permute-start(bf16[4,16,1024]{2,1,0:T(8,128)(2,1)S(1)} %fusion.2), channel_id=1, source_target_pairs={{0,8},{4,20},{8,0},{12,28},{16,24},{20,4},{24,16},{28,12},{1,9},{5... | collective-permute-start | bytes 393224 | tf_op jit(solution)/shard_map/ppermute | solution.py:261
  43.9 7.5 %collective-permute-start.10 = (bf16[4,16,2048]{2,1,0:T(8,128)(2,1)S(1)}, bf16[4,16,2048]{2,1,0:T(8,128)(2,1)S(1)}, u32[]{:S(2)}, u32[]{:S(2)}) collective-permute-start(bf16[4,16,2048]{2,1,0:T(8,128)(2,1)S(1)} %pad_maximum_fusion.1), channel_id=1, source_target_pairs={{0,16},{4,12},{8,24},{12,4},{16,0},{20,28},{24,8},{28,20},{1,17},{... | collective-permute-start | bytes 786440 | tf_op jit(solution)/shard_map/ppermute | solution.py:261
  44.5 6.9 %collective-permute-start.14 = (bf16[4,16,1024]{2,1,0:T(8,128)(2,1)S(1)}, bf16[4,16,1024]{2,1,0:T(8,128)(2,1)S(1)}, u32[]{:S(2)}, u32[]{:S(2)}) collective-permute-start(bf16[4,16,1024]{2,1,0:T(8,128)(2,1)S(1)} %fusion), channel_id=1, source_target_pairs={{0,8},{4,20},{8,0},{12,28},{16,24},{20,4},{24,16},{28,12},{1,9},{5... | collective-permute-start | bytes 393224 | tf_op jit(solution)/shard_map/ppermute | solution.py:261
  51.6 6.6 %collective-permute-start.15 = (bf16[16,2048]{1,0:T(8,128)(2,1)S(1)}, bf16[16,2048]{1,0:T(8,128)(2,1)S(1)}, u32[]{:S(2)}, u32[]{:S(2)}) collective-permute-start(bf16[16,2048]{1,0:T(8,128)(2,1)S(1)} %pad_maximum_fusion.2), channel_id=1, source_target_pairs={{0,3},{1,2},{2,1},{3,0},{4,7},{5,6},{6,5},{7,4},{8,11},{9,10},{10,... | collective-permute-start | bytes 196616 | tf_op jit(solution)/shard_map/ppermute | solution.py:264
  52.5 7.4 %collective-permute-start.16 = (bf16[16,2048]{1,0:T(8,128)(2,1)S(1)}, bf16[16,2048]{1,0:T(8,128)(2,1)S(1)}, u32[]{:S(2)}, u32[]{:S(2)}) collective-permute-start(bf16[16,2048]{1,0:T(8,128)(2,1)S(1)} %pad_maximum_fusion.3), channel_id=1, source_target_pairs={{0,2},{1,3},{2,0},{3,1},{4,6},{5,7},{6,4},{7,5},{8,10},{9,11},{10,... | collective-permute-start | bytes 196616 | tf_op jit(solution)/shard_map/ppermute | solution.py:264
  53.4 6.4 %collective-permute-start.17 = (bf16[16,2048]{1,0:T(8,128)(2,1)S(1)}, bf16[16,2048]{1,0:T(8,128)(2,1)S(1)}, u32[]{:S(2)}, u32[]{:S(2)}) collective-permute-start(bf16[16,2048]{1,0:T(8,128)(2,1)S(1)} %pad_maximum_fusion.4), channel_id=1, source_target_pairs={{0,1},{1,0},{2,3},{3,2},{4,5},{5,4},{6,7},{7,6},{8,9},{9,8},{10,11... | collective-permute-start | bytes 196616 | tf_op jit(solution)/shard_map/ppermute | solution.py:264

commit v9 on v8

--- a/solution.py
+++ b/solution.py
@@ -33,9 +33,10 @@
 
 
 def row_order(n_seq):
-    last = n_seq // 2 - 1
-    early = [(core, chip) for core in (0, 1) for chip in range(last)]
-    return early + [(0, last), (1, last)]
+    n_chip = n_seq // 2
+    cut = n_chip // 2
+    groups = [(core, range(low, low + cut)) for low in (0, cut) for core in (0, 1)]
+    return [(core, chip) for core, chips in groups for chip in chips]
 
 
 def owner_of(n_seq, core, chip):
@@ -195,9 +196,27 @@
     )(stats, picker)
 
 
-def gradient_kernel(n_seq, n_vocab, stats_ref, logits_ref, head_ref, *refs):
-    *out_refs, last_ref, columns, ordered = refs
-    near_refs, far_refs = out_refs[:PARTS], out_refs[PARTS:]
+def score_product(score_ref, picks, head_ref, out_refs):
+    rows = [score_ref[q * ACT_DEV : (q + 1) * ACT_DEV, :] for q in picks]
+    rows = jnp.concatenate(rows, axis=0)
+    _, n_vocab, _, size = out_refs[0].shape
+    for v in range(n_vocab):
+        for c in range(PARTS):
+            start = (v * PARTS + c) * size
+            part = lax.dot_general(
+                rows,
+                head_ref[start : start + size, :],
+                (((1,), (1,)), ((), ())),
+                preferred_element_type=F32,
+            ).astype(BF16)
+            blocks = part.reshape(len(picks), ACT_DEV, size)
+            half = len(picks) // 2
+            out_refs[c][:, v] = blocks[:half]
+            out_refs[PARTS + c][:, v] = blocks[half:]
+
+
+def first_kernel(n_seq, stats_ref, logits_ref, head_ref, *refs):
+    *out_refs, score, columns, ordered = refs
     top, total, centred = merged(stats_ref[...])
     row = iota((8, top.shape[1]), 0)
     lines = jnp.where(row == 0, top, jnp.where(row == 1, 1.0 / total, top + centred))
@@ -207,45 +226,48 @@
         ordered[q * ACT_DEV : (q + 1) * ACT_DEV] = columns[pl.ds(place, ACT_DEV), :]
     logits = logits_ref[...]
     prob = jnp.exp(logits - ordered[:, 0:1]) * ordered[:, 1:2]
-    score = (prob * (ordered[:, 2:3] - logits)).astype(BF16)
-    n_chip = n_seq // 2
-    last = n_chip - 1
-    size = near_refs[0].shape[3]
-    for v in range(n_vocab):
-        for c in range(PARTS):
-            start = (v * PARTS + c) * size
-            part = lax.dot_general(
-                score,
-                head_ref[start : start + size, :],
-                (((1,), (1,)), ((), ())),
-                preferred_element_type=F32,
-            ).astype(BF16)
-            blocks = part.reshape(n_seq, ACT_DEV, size)
-            near_refs[c][:last, v] = blocks[:last]
-            far_refs[c][:, v] = blocks[last : 2 * last]
-            near_refs[c][last, v] = blocks[2 * last]
-            last_ref[c, v] = blocks[2 * last + 1]
+    score[...] = (prob * (ordered[:, 2:3] - logits)).astype(BF16)
+    order = row_order(n_seq)
+    last = n_seq // 2 - 1
+    score_product(score, [order.index((core, last)) for core in (0, 1)], head_ref, out_refs)
+
+
+def rest_kernel(n_seq, score_ref, head_ref, *out_refs):
+    order = row_order(n_seq)
+    last = n_seq // 2 - 1
+    picks = [order.index((core, chip)) for core in (0, 1) for chip in range(last)]
+    score_product(score_ref, picks, head_ref, out_refs)
 
 
 def gradients(n_seq, n_vocab, stats, logits, head):
     rows = logits.shape[0]
-    n_chip = n_seq // 2
+    last = n_seq // 2 - 1
     block = (n_vocab, ACT_DEV, head.shape[0] // (n_vocab * PARTS))
-    outs = [jax.ShapeDtypeStruct((n_chip,) + block, BF16)] * PARTS
-    outs += [jax.ShapeDtypeStruct((n_chip - 1,) + block, BF16)] * PARTS
-    outs += [jax.ShapeDtypeStruct((PARTS,) + block, BF16)]
-    *outs, far_last = pl.pallas_call(
-        functools.partial(gradient_kernel, n_seq, n_vocab),
-        in_specs=[pl.BlockSpec(memory_space=pltpu.VMEM)] * 3,
-        out_shape=outs,
+    vmem = pl.BlockSpec(memory_space=pltpu.VMEM)
+    out = jax.ShapeDtypeStruct((1,) + block, BF16)
+    *first, score = pl.pallas_call(
+        functools.partial(first_kernel, n_seq),
+        in_specs=[vmem] * 3,
+        out_shape=[out] * 2 * PARTS + [jax.ShapeDtypeStruct(logits.shape, BF16)],
         scratch_shapes=[
             pltpu.VMEM((stats.shape[2], LANES), F32),
             pltpu.VMEM((rows, LANES), F32),
         ],
         compiler_params=params(),
-        name="gradients",
+        name="last_gradients",
     )(stats, logits, head)
-    return outs[:PARTS], outs[PARTS:], far_last
+    out = jax.ShapeDtypeStruct((last,) + block, BF16)
+    rest = pl.pallas_call(
+        functools.partial(rest_kernel, n_seq),
+        in_specs=[vmem] * 2,
+        out_shape=[out] * 2 * PARTS,
+        cost_estimate=pl.CostEstimate(
+            flops=2 * rows * head.size, bytes_accessed=2 * head.size, transcendentals=0
+        ),
+        compiler_params=params(),
+        name="other_gradients",
+    )(score, head)
+    return first[:PARTS], first[PARTS:], rest[:PARTS], rest[PARTS:]
 
 
 def body(n_seq, n_vocab, hidden, head, mask):
@@ -266,24 +288,29 @@
     own, picker = select(mask, hidden)
 
     near = [own]
+    cut = n_chip // 2
     for a in range(1, n_chip):
         step = a.bit_length() - 1
         source = near[a ^ (1 << step)]
         if a > 1 and a == 1 << step:
+            source, near[1][-1] = lax.optimization_barrier((source, near[1][-1]))
             moved = swap_chip(jnp.concatenate(source, axis=1), step)
             near.append(jnp.split(moved, PARTS, axis=1))
         else:
             near.append([swap_chip(part, step) for part in source])
-    early = jnp.concatenate([near[a][c] for c in range(PARTS) for a in range(last)], axis=0)
-    early, near[last][0] = lax.optimization_barrier((early, near[last][0]))
-    late = jnp.concatenate(near[last], axis=0)
+
+    def gather_rows(chips):
+        return jnp.concatenate([near[a][c] for c in range(PARTS) for a in chips], axis=0)
+
+    early, late = gather_rows(range(cut)), gather_rows(range(cut, n_chip))
     blocks = [early, swap_core(early), late, swap_core(late)]
 
     logits, stats = local_logits(n_seq, n_vocab, blocks, head, picker)
     stats = lax.all_to_all(stats, ("seq", "vocab"), 0, 0, tiled=True)
-    near, far, far_last = gradients(n_seq, n_vocab, stats, logits, head)
-    moved = swap_core(far_last)
-    first = [(near[c][last].astype(F32) + moved[c].astype(F32)).astype(BF16) for c in range(PARTS)]
+    near_last, far_last, near, far = gradients(n_seq, n_vocab, stats, logits, head)
+
+    moved = [swap_core(part) for part in far_last]
+    first = [(near_last[c][0].astype(F32) + moved[c][0].astype(F32)).astype(BF16) for c in range(PARTS)]
     far, first = lax.optimization_barrier((far, first))
     far = [swap_core(part) for part in far]
     sums = [[near[c][a].astype(F32) + far[c][a].astype(F32) for c in range(PARTS)] for a in range(last)]

time: 61.1 us -> 62.2 us (1.018)
  starting transfers between devices: 19.8 us -> 17.5 us
  waiting for transfers between devices: 18.8 us -> 21 us
  Pallas kernels: 6.13 us -> 7.35 us
    ppermute x10, waiting for transfers between devices: 12.8 us -> 16.1 us  [swap_chip(): lax.ppermute(value, 'seq', [(i, i ^ flips[i & 1]) for i in range(n_seq)])]
    ppermute x10, starting transfers between devices: 14.9 us -> 12.1 us  [swap_chip(): lax.ppermute(value, 'seq', [(i, i ^ flips[i & 1]) for i in range(n_seq)])]
    pallas_call x1 -> x2, Pallas kernels: 1.64 us -> 2.86 us  [the longest x1 1.47 us: gradients(): pl.pallas_call(functools.partial(first_kernel, n_seq), in_specs=[vmem] *...]
    ppermute x5 -> x6, waiting for transfers between devices: 3.05 us -> 1.9 us  [swap_core(): return lax.ppermute(value, 'seq', [(i, i ^ 1) for i in range(n_seq)])]
  transfers between devices with their start and end apart: 18 -> 19, of which waited for: 10 -> 10; matrix products, arithmetic and copies ran while one was open for 1% -> 1% of each run, Pallas kernels for 1% -> 3%
where the time goes in v9:
time: 62.2 us; the launch traced here: 62 us
  waiting for transfers between devices  21 us (34%)
  starting transfers between devices  17.5 us (28%)
  blocking collectives  13.7 us (22%)
  Pallas kernels  7.35 us (12%)
  matrix products  1.11 us (2%)
  between operations  0.83 us (1%)
    ppermute x10, waiting for transfers between devices, swap_chip(): lax.ppermute(value, 'seq', [(i, i ^ flips[i & 1]) for i in range(n_seq)])  16.1 us
    all_to_all x1, blocking collectives, body(): stats = lax.all_to_all(stats, ('seq', 'vocab'), 0, 0, tiled=True)  13.7 us
    ppermute x10, starting transfers between devices, swap_chip(): lax.ppermute(value, 'seq', [(i, i ^ flips[i & 1]) for i in range(n_seq)])  12.1 us
    ppermute x3, starting transfers between devices, send_vocab(): return lax.ppermute(value, 'vocab', [(i, i ^ k) for i in range(n_vocab)])  4.45 us
    ppermute x3, waiting for transfers between devices, send_vocab(): return lax.ppermute(value, 'vocab', [(i, i ^ k) for i in range(n_vocab)])  2.99 us
    pallas_call x1, Pallas kernels, select(): pl.pallas_call(select_kernel, in_specs=[pl.BlockSpec(memory_space=pltpu.H...  2.75 us
    ppermute x6, waiting for transfers between devices, swap_core(): return lax.ppermute(value, 'seq', [(i, i ^ 1) for i in range(n_seq)])  1.9 us
    pallas_call x1, Pallas kernels, gradients(): pl.pallas_call(functools.partial(first_kernel, n_seq), in_specs=[vmem] *...  1.47 us
  transfers between devices with their start and end apart: 19, of which 10 were waited for; matrix products, arithmetic and copies ran while one was open for 1% of the time, Pallas kernels for 3%

profile of v9, /device:TPU:0, one launch (start us, length us, event | category | flops | bytes accessed | tf_op | source)
XLA Modules:
  0.0 62.0 jit_solution(9394134144113889633)
XLA Ops:
  0.6 2.8 %select_rows.1 = (bf16[16,4096]{1,0:T(8,128)(2,1)S(1)}, bf16[16,4096]{1,0:T(8,128)(2,1)S(1)}, bf16[16,128]{1,0:T(8,128)(2,1)S(1)}) custom-call(s32[1,128]{1,0:T(1,128)} %bitcast.44, bf16[128,8192]{1,0:T(8,128)(2,1)} %hidden_ref.1), custom_call_target="tpu_custom_call" | custom-call | tf_op jit(solution)/shard_map/select_rows/pallas_call | solution.py:92
  3.4 3.0 %collective-permute-start.1 = (bf16[16,4096]{1,0:T(8,128)(2,1)S(1)}, bf16[16,4096]{1,0:T(8,128)(2,1)S(1)}, u32[]{:S(2)}, u32[]{:S(2)}) collective-permute-start(bf16[16,4096]{1,0:T(8,128)(2,1)S(1)} %get-tuple-element.31), channel_id=1, source_target_pairs={{0,8},{4,20},{8,0},{12,28},{16,24},{20,4},{24,16},{28,12},{1,9},{5... | collective-permute-start | bytes 393224 | tf_op jit(solution)/shard_map/ppermute | solution.py:283
  6.4 0.1 collective-permute-start
  6.5 2.9 %collective-permute-done.1 = bf16[16,4096]{1,0:T(8,128)(2,1)S(1)} collective-permute-done((bf16[16,4096]{1,0:T(8,128)(2,1)S(1)}, bf16[16,4096]{1,0:T(8,128)(2,1)S(1)}, u32[]{:S(2)}, u32[]{:S(2)}) %collective-permute-start.1) | collective-permute-done | bytes 131104 | tf_op jit(solution)/shard_map/ppermute | solution.py:283
  9.4 2.1 %collective-permute-start.3 = (bf16[16,8192]{1,0:T(8,128)(2,1)S(1)}, bf16[16,8192]{1,0:T(8,128)(2,1)S(1)}, u32[]{:S(2)}, u32[]{:S(2)}) collective-permute-start(bf16[16,8192]{1,0:T(8,128)(2,1)S(1)} %pad_maximum_fusion.1), channel_id=1, source_target_pairs={{0,16},{4,12},{8,24},{12,4},{16,0},{20,28},{24,8},{28,20},{1,17},{... | collective-permute-start | bytes 786440 | tf_op jit(solution)/shard_map/ppermute | solution.py:283
  11.5 0.1 collective-permute-start.5
  11.6 0.0 collective-permute-done
  11.6 0.1 collective-permute-start.2
  11.7 2.0 %collective-permute-start.4 = (bf16[16,4096]{1,0:T(8,128)(2,1)S(1)}, bf16[16,4096]{1,0:T(8,128)(2,1)S(1)}, u32[]{:S(2)}, u32[]{:S(2)}) collective-permute-start(bf16[16,4096]{1,0:T(8,128)(2,1)S(1)} %collective-permute-done), channel_id=1, source_target_pairs={{0,16},{4,12},{8,24},{12,4},{16,0},{20,28},{24,8},{28,20},{1,17},{... | collective-permute-start | bytes 393224 | tf_op jit(solution)/shard_map/ppermute | solution.py:283
  13.7 2.1 %collective-permute-done.3 = bf16[16,8192]{1,0:T(8,128)(2,1)S(1)} collective-permute-done((bf16[16,8192]{1,0:T(8,128)(2,1)S(1)}, bf16[16,8192]{1,0:T(8,128)(2,1)S(1)}, u32[]{:S(2)}, u32[]{:S(2)}) %collective-permute-start.3) | collective-permute-done | bytes 262176 | tf_op jit(solution)/shard_map/ppermute | solution.py:283
  15.9 1.4 %collective-permute-done.5 = bf16[16,4096]{1,0:T(8,128)(2,1)S(1)} collective-permute-done((bf16[16,4096]{1,0:T(8,128)(2,1)S(1)}, bf16[16,4096]{1,0:T(8,128)(2,1)S(1)}, u32[]{:S(2)}, u32[]{:S(2)}) %collective-permute-start.5) | collective-permute-done | bytes 131104 | tf_op jit(solution)/shard_map/ppermute | solution.py:283
  17.2 1.4 %collective-permute-done.4 = bf16[16,4096]{1,0:T(8,128)(2,1)S(1)} collective-permute-done((bf16[16,4096]{1,0:T(8,128)(2,1)S(1)}, bf16[16,4096]{1,0:T(8,128)(2,1)S(1)}, u32[]{:S(2)}, u32[]{:S(2)}) %collective-permute-start.4) | collective-permute-done | bytes 131104 | tf_op jit(solution)/shard_map/ppermute | solution.py:283
  18.7 0.1 collective-permute-start.6
  18.8 0.0 collective-permute-done.2.refs_1_
  18.8 1.9 %collective-permute-done.6.refs_3_ = bf16[64,4096]{1,0:T(8,128)(2,1)S(1)} collective-permute-done((bf16[64,4096]{1,0:T(8,128)(2,1)S(1)}, bf16[64,4096]{1,0:T(8,128)(2,1)S(1)}, u32[]{:S(2)}, u32[]{:S(2)}) %collective-permute-start.6) | collective-permute-done | bytes 524320 | tf_op jit(solution)/shard_map/ppermute | solution.py:279
  20.7 1.0 %local_logits.1 = (f32[128,256]{1,0:T(8,128)S(1)}, f32[32,4,128]{2,1,0:T(4,128)S(1)}) custom-call(bf16[64,4096]{1,0:T(8,128)(2,1)S(1)} %constant_dynamic-update-slice_fusion.refs_0_, bf16[64,4096]{1,0:T(8,128)(2,1)S(1)} %collective-permute-done.2.refs_1_, bf16[64,4096]{1,0:T(8,128)(2,1)S(1)} %pad_maximum_fusion.refs_2_, ...), custom_call_target="tpu_custom_call" | custom-call | tf_op jit(solution)/shard_map/local_logits/pallas_call | solution.py:147
  21.6 13.7 %all_to_all.5.stats_ref = f32[32,4,128]{2,1,0:T(4,128)S(1)} all-to-all(f32[32,4,128]{2,1,0:T(4,128)S(1)} %get-tuple-element.33), channel_id=1, replica_groups=mesh['seq'=8,'vocab'=4] {'seq','vocab'}, dimensions={0} | all-to-all | bytes 131072 | tf_op jit(solution)/shard_map/all_to_all | solution.py:309
  35.3 1.5 %last_gradients.1 = (bf16[1,4,16,1024]{3,2,1,0:T(8,128)(2,1)S(1)}, bf16[1,4,16,1024]{3,2,1,0:T(8,128)(2,1)S(1)}, bf16[1,4,16,1024]{3,2,1,0:T(8,128)(2,1)S(1)}, b...) custom-call(f32[32,4,128]{2,1,0:T(4,128)S(1)} %all_to_all.5.stats_ref, ...), custom_call_target="tpu_custom_call" | custom-call | tf_op jit(solution)/shard_map/last_gradients/pallas_call | solution.py:248
  36.8 0.1 collective-permute-start.8
  36.8 0.5 collective-permute-start.7
  37.3 1.4 %other_gradients.1 = (bf16[3,4,16,1024]{3,2,1,0:T(8,128)(2,1)S(1)}, bf16[3,4,16,1024]{3,2,1,0:T(8,128)(2,1)S(1)}, bf16[3,4,16,1024]{3,2,1,0:T(8,128)(2,1)S(1)}, bf16[3,4,16,1024]{3,2,1,0:T(8,128)(2,1)S(1)}) custom-call(bf16[128,256]{1,0:T(8,128)(2,1)S(1)} %get-tuple-element.35.score_ref, bf16[8192,256]{1,0:T(8,128)(2,1)S(1)} %copy-done), custom_call_target="tpu_custom_call" | custom-call | flops 536870912 | bytes 4194304 | tf_op jit(solution)/shard_map/other_gradients/pallas_call | solution.py:260
  38.7 0.0 collective-permute-done.8
  38.8 0.0 collective-permute-done.7
  38.8 0.1 collective-permute-start.9
  39.0 0.7 %collective-permute-start.12 = (bf16[4,16,1024]{2,1,0:T(8,128)(2,1)S(1)}, bf16[4,16,1024]{2,1,0:T(8,128)(2,1)S(1)}, u32[]{:S(2)}, u32[]{:S(2)}) collective-permute-start(bf16[4,16,1024]{2,1,0:T(8,128)(2,1)S(1)} %fusion.4), channel_id=1, source_target_pairs={{0,16},{4,12},{8,24},{12,4},{16,0},{20,28},{24,8},{28,20},{1,17},{... | collective-permute-start | bytes 393224 | tf_op jit(solution)/shard_map/ppermute | solution.py:283
  39.6 0.1 collective-permute-start.10
  39.8 1.2 %collective-permute-start.14 = (bf16[4,16,1024]{2,1,0:T(8,128)(2,1)S(1)}, bf16[4,16,1024]{2,1,0:T(8,128)(2,1)S(1)}, u32[]{:S(2)}, u32[]{:S(2)}) collective-permute-start(bf16[4,16,1024]{2,1,0:T(8,128)(2,1)S(1)} %fusion.5), channel_id=1, source_target_pairs={{0,16},{4,12},{8,24},{12,4},{16,0},{20,28},{24,8},{28,20},{1,17},{... | collective-permute-start | bytes 393224 | tf_op jit(solution)/shard_map/ppermute | solution.py:283
  41.0 2.9 %collective-permute-done.12 = bf16[4,16,1024]{2,1,0:T(8,128)(2,1)S(1)} collective-permute-done((bf16[4,16,1024]{2,1,0:T(8,128)(2,1)S(1)}, bf16[4,16,1024]{2,1,0:T(8,128)(2,1)S(1)}, u32[]{:S(2)}, u32[]{:S(2)}) %collective-permute-start.12) | collective-permute-done | bytes 131104 | tf_op jit(solution)/shard_map/ppermute | solution.py:283
  43.9 0.0 collective-permute-done.9
  43.9 0.1 fusion.2
  44.0 0.7 %collective-permute-start.13 = (bf16[4,16,1024]{2,1,0:T(8,128)(2,1)S(1)}, bf16[4,16,1024]{2,1,0:T(8,128)(2,1)S(1)}, u32[]{:S(2)}, u32[]{:S(2)}) collective-permute-start(bf16[4,16,1024]{2,1,0:T(8,128)(2,1)S(1)} %fusion.2), channel_id=1, source_target_pairs={{0,8},{4,20},{8,0},{12,28},{16,24},{20,4},{24,16},{28,12},{1,9},{5... | collective-permute-start | bytes 393224 | tf_op jit(solution)/shard_map/ppermute | solution.py:283
  44.8 0.0 collective-permute-done.10
  44.8 0.6 collective-permute-start.11
  45.4 0.0 collective-permute-done.14
  45.4 0.1 fusion
  45.5 1.6 %collective-permute-start.15 = (bf16[4,16,1024]{2,1,0:T(8,128)(2,1)S(1)}, bf16[4,16,1024]{2,1,0:T(8,128)(2,1)S(1)}, u32[]{:S(2)}, u32[]{:S(2)}) collective-permute-start(bf16[4,16,1024]{2,1,0:T(8,128)(2,1)S(1)} %fusion), channel_id=1, source_target_pairs={{0,8},{4,20},{8,0},{12,28},{16,24},{20,4},{24,16},{28,12},{1,9},{5... | collective-permute-start | bytes 393224 | tf_op jit(solution)/shard_map/ppermute | solution.py:283
  47.1 3.3 %collective-permute-done.13 = bf16[4,16,1024]{2,1,0:T(8,128)(2,1)S(1)} collective-permute-done((bf16[4,16,1024]{2,1,0:T(8,128)(2,1)S(1)}, bf16[4,16,1024]{2,1,0:T(8,128)(2,1)S(1)}, u32[]{:S(2)}, u32[]{:S(2)}) %collective-permute-start.13) | collective-permute-done | bytes 131104 | tf_op jit(solution)/shard_map/ppermute | solution.py:283
  50.4 2.0 %collective-permute-done.15 = bf16[4,16,1024]{2,1,0:T(8,128)(2,1)S(1)} collective-permute-done((bf16[4,16,1024]{2,1,0:T(8,128)(2,1)S(1)}, bf16[4,16,1024]{2,1,0:T(8,128)(2,1)S(1)}, u32[]{:S(2)}, u32[]{:S(2)}) %collective-permute-start.15) | collective-permute-done | bytes 131104 | tf_op jit(solution)/shard_map/ppermute | solution.py:283
  52.4 0.0 collective-permute-done.11
  52.4 0.2 fusion.1
  52.7 0.9 %collective-permute-start.16 = (bf16[16,2048]{1,0:T(8,128)(2,1)S(1)}, bf16[16,2048]{1,0:T(8,128)(2,1)S(1)}, u32[]{:S(2)}, u32[]{:S(2)}) collective-permute-start(bf16[16,2048]{1,0:T(8,128)(2,1)S(1)} %pad_maximum_fusion.3), channel_id=1, source_target_pairs={{0,3},{1,2},{2,1},{3,0},{4,7},{5,6},{6,5},{7,4},{8,11},{9,10},{10,... | collective-permute-start | bytes 196616 | tf_op jit(solution)/shard_map/ppermute | solution.py:286
  53.5 0.9 %collective-permute-start.17 = (bf16[16,2048]{1,0:T(8,128)(2,1)S(1)}, bf16[16,2048]{1,0:T(8,128)(2,1)S(1)}, u32[]{:S(2)}, u32[]{:S(2)}) collective-permute-start(bf16[16,2048]{1,0:T(8,128)(2,1)S(1)} %pad_maximum_fusion.4), channel_id=1, source_target_pairs={{0,2},{1,3},{2,0},{3,1},{4,6},{5,7},{6,4},{7,5},{8,10},{9,11},{10,... | collective-permute-start | bytes 196616 | tf_op jit(solution)/shard_map/ppermute | solution.py:286
  54.5 2.7 %collective-permute-start.18 = (bf16[16,2048]{1,0:T(8,128)(2,1)S(1)}, bf16[16,2048]{1,0:T(8,128)(2,1)S(1)}, u32[]{:S(2)}, u32[]{:S(2)}) collective-permute-start(bf16[16,2048]{1,0:T(8,128)(2,1)S(1)} %pad_maximum_fusion.5), channel_id=1, source_target_pairs={{0,1},{1,0},{2,3},{3,2},{4,5},{5,4},{6,7},{7,6},{8,9},{9,8},{10,11... | collective-permute-start | bytes 196616 | tf_op jit(solution)/shard_map/ppermute | solution.py:286
  57.1 0.8 %entropies.1 = (f32[1,128]{1,0:T(1,128)}, f32[1,1]{1,0:T(1,128)}) custom-call(f32[32,4,128]{2,1,0:T(4,128)S(1)} %all_to_all.5.stats_ref, bf16[16,128]{1,0:T(8,128)(2,1)S(1)} %get-tuple-element.32.refs_5_.picker_ref), custom_call_target="tpu_custom_call" | custom-call | tf_op jit(solution)/shard_map/entropies/pallas_call | solution.py:187
  57.9 1.4 %collective-permute-done.16 = bf16[16,2048]{1,0:T(8,128)(2,1)S(1)} collective-permute-done((bf16[16,2048]{1,0:T(8,128)(2,1)S(1)}, bf16[16,2048]{1,0:T(8,128)(2,1)S(1)}, u32[]{:S(2)}, u32[]{:S(2)}) %collective-permute-start.16) | collective-permute-done | bytes 65568 | tf_op jit(solution)/shard_map/ppermute | solution.py:286
  59.3 1.6 %collective-permute-done.17 = bf16[16,2048]{1,0:T(8,128)(2,1)S(1)} collective-permute-done((bf16[16,2048]{1,0:T(8,128)(2,1)S(1)}, bf16[16,2048]{1,0:T(8,128)(2,1)S(1)}, u32[]{:S(2)}, u32[]{:S(2)}) %collective-permute-start.17) | collective-permute-done | bytes 65568 | tf_op jit(solution)/shard_map/ppermute | solution.py:286
  60.9 0.0 collective-permute-done.18
  60.9 1.1 %convolution_convert_fusion = bf16[128,2048]{1,0:T(8,128)(2,1)} fusion(bf16[16,128]{1,0:T(8,128)(2,1)S(1)} %get-tuple-element.32.refs_5_.picker_ref, f32[16,1024]{1,0:T(8,128)S(1)} %get-tuple-element.61, f32[16,1024]{1,0:T(8,128)S(1)} %get-tuple-element.62, bf16[16,2048]{1,0:T(8,128)(2,1)S(1)} %collective-permute-done.18, ...), kind=kOutput, calls=%fused_computation | convolution fusion | flops 8912896 | bytes 856064 | tf_op jit(solution)/shard_map/dot_general | solution.py:340
  (19 shorter events, 0.3 us)
Async XLA Ops:
  0.6 20.0 %copy-start = (bf16[8192,256]{1,0:T(8,128)(2,1)S(1)}, bf16[8192,256]{1,0:T(8,128)(2,1)}, u32[]{:S(2)}) copy-start(bf16[8192,256]{1,0:T(8,128)(2,1)} %head_ref.3) | copy-start | bytes 12582916
  3.4 6.0 %collective-permute-start.1 = (bf16[16,4096]{1,0:T(8,128)(2,1)S(1)}, bf16[16,4096]{1,0:T(8,128)(2,1)S(1)}, u32[]{:S(2)}, u32[]{:S(2)}) collective-permute-start(bf16[16,4096]{1,0:T(8,128)(2,1)S(1)} %get-tuple-element.31), channel_id=1, source_target_pairs={{0,8},{4,20},{8,0},{12,28},{16,24},{20,4},{24,16},{28,12},{1,9},{5... | collective-permute-start | bytes 393224 | tf_op jit(solution)/shard_map/ppermute | solution.py:283
  6.4 5.2 %collective-permute-start = (bf16[16,4096]{1,0:T(8,128)(2,1)S(1)}, bf16[16,4096]{1,0:T(8,128)(2,1)S(1)}, u32[]{:S(2)}, u32[]{:S(2)}) collective-permute-start(bf16[16,4096]{1,0:T(8,128)(2,1)S(1)} %get-tuple-element.30), channel_id=1, source_target_pairs={{0,8},{4,20},{8,0},{12,28},{16,24},{20,4},{24,16},{28,12},{1,9},{5... | collective-permute-start | bytes 393224 | tf_op jit(solution)/shard_map/ppermute | solution.py:283
  9.4 6.5 %collective-permute-start.3 = (bf16[16,8192]{1,0:T(8,128)(2,1)S(1)}, bf16[16,8192]{1,0:T(8,128)(2,1)S(1)}, u32[]{:S(2)}, u32[]{:S(2)}) collective-permute-start(bf16[16,8192]{1,0:T(8,128)(2,1)S(1)} %pad_maximum_fusion.1), channel_id=1, source_target_pairs={{0,16},{4,12},{8,24},{12,4},{16,0},{20,28},{24,8},{28,20},{1,17},{... | collective-permute-start | bytes 786440 | tf_op jit(solution)/shard_map/ppermute | solution.py:283
  11.5 5.8 %collective-permute-start.5 = (bf16[16,4096]{1,0:T(8,128)(2,1)S(1)}, bf16[16,4096]{1,0:T(8,128)(2,1)S(1)}, u32[]{:S(2)}, u32[]{:S(2)}) collective-permute-start(bf16[16,4096]{1,0:T(8,128)(2,1)S(1)} %collective-permute-done.1), channel_id=1, source_target_pairs={{0,16},{4,12},{8,24},{12,4},{16,0},{20,28},{24,8},{28,20},{1,17},{... | collective-permute-start | bytes 393224 | tf_op jit(solution)/shard_map/ppermute | solution.py:283
  11.6 7.1 %collective-permute-start.2 = (bf16[64,4096]{1,0:T(8,128)(2,1)S(1)}, bf16[64,4096]{1,0:T(8,128)(2,1)S(1)}, u32[]{:S(2)}, u32[]{:S(2)}) collective-permute-start(bf16[64,4096]{1,0:T(8,128)(2,1)S(1)} %constant_dynamic-update-slice_fusion.refs_0_), channel_id=1, source_target_pairs={{0,4},{4,0},{8,12},{12,8},{16,20},{20,16},{24,28},{28,24},{1,5},{5... | collective-permute-start | bytes 1572872 | tf_op jit(solution)/shard_map/ppermute | solution.py:279
  11.7 6.9 %collective-permute-start.4 = (bf16[16,4096]{1,0:T(8,128)(2,1)S(1)}, bf16[16,4096]{1,0:T(8,128)(2,1)S(1)}, u32[]{:S(2)}, u32[]{:S(2)}) collective-permute-start(bf16[16,4096]{1,0:T(8,128)(2,1)S(1)} %collective-permute-done), channel_id=1, source_target_pairs={{0,16},{4,12},{8,24},{12,4},{16,0},{20,28},{24,8},{28,20},{1,17},{... | collective-permute-start | bytes 393224 | tf_op jit(solution)/shard_map/ppermute | solution.py:283
  18.7 2.0 %collective-permute-start.6 = (bf16[64,4096]{1,0:T(8,128)(2,1)S(1)}, bf16[64,4096]{1,0:T(8,128)(2,1)S(1)}, u32[]{:S(2)}, u32[]{:S(2)}) collective-permute-start(bf16[64,4096]{1,0:T(8,128)(2,1)S(1)} %pad_maximum_fusion.refs_2_), channel_id=1, source_target_pairs={{0,4},{4,0},{8,12},{12,8},{16,20},{20,16},{24,28},{28,24},{1,5},{5... | collective-permute-start | bytes 1572872 | tf_op jit(solution)/shard_map/ppermute | solution.py:279
  36.8 2.0 %collective-permute-start.8 = (bf16[1,4,16,1024]{3,2,1,0:T(8,128)(2,1)S(1)}, bf16[1,4,16,1024]{3,2,1,0:T(8,128)(2,1)S(1)}, u32[]{:S(2)}, u32[]{:S(2)}) collective-permute-start(bf16[1,4,16,1024]{3,2,1,0:T(8,128)(2,1)S(1)} %get-tuple-element.42), channel_id=1, source_target_pairs={{0,4},{4,0},{8,12},{12,8},{16,20},{20,16},{24,28},{28,24},{1,5},{5... | collective-permute-start | bytes 393224 | tf_op jit(solution)/shard_map/ppermute | solution.py:279
  36.8 2.0 %collective-permute-start.7 = (bf16[1,4,16,1024]{3,2,1,0:T(8,128)(2,1)S(1)}, bf16[1,4,16,1024]{3,2,1,0:T(8,128)(2,1)S(1)}, u32[]{:S(2)}, u32[]{:S(2)}) collective-permute-start(bf16[1,4,16,1024]{3,2,1,0:T(8,128)(2,1)S(1)} %get-tuple-element.40), channel_id=1, source_target_pairs={{0,4},{4,0},{8,12},{12,8},{16,20},{20,16},{24,28},{28,24},{1,5},{5... | collective-permute-start | bytes 393224 | tf_op jit(solution)/shard_map/ppermute | solution.py:279
  38.8 5.1 %collective-permute-start.9 = (bf16[3,4,16,1024]{3,2,1,0:T(8,128)(2,1)S(1)}, bf16[3,4,16,1024]{3,2,1,0:T(8,128)(2,1)S(1)}, u32[]{:S(2)}, u32[]{:S(2)}) collective-permute-start(bf16[3,4,16,1024]{3,2,1,0:T(8,128)(2,1)S(1)} %get-tuple-element.43), channel_id=1, source_target_pairs={{0,4},{4,0},{8,12},{12,8},{16,20},{20,16},{24,28},{28,24},{1,5},{5... | collective-permute-start | bytes 1179656 | tf_op jit(solution)/shard_map/ppermute | solution.py:279
  39.0 5.0 %collective-permute-start.12 = (bf16[4,16,1024]{2,1,0:T(8,128)(2,1)S(1)}, bf16[4,16,1024]{2,1,0:T(8,128)(2,1)S(1)}, u32[]{:S(2)}, u32[]{:S(2)}) collective-permute-start(bf16[4,16,1024]{2,1,0:T(8,128)(2,1)S(1)} %fusion.4), channel_id=1, source_target_pairs={{0,16},{4,12},{8,24},{12,4},{16,0},{20,28},{24,8},{28,20},{1,17},{... | collective-permute-start | bytes 393224 | tf_op jit(solution)/shard_map/ppermute | solution.py:283
  39.6 5.1 %collective-permute-start.10 = (bf16[3,4,16,1024]{3,2,1,0:T(8,128)(2,1)S(1)}, bf16[3,4,16,1024]{3,2,1,0:T(8,128)(2,1)S(1)}, u32[]{:S(2)}, u32[]{:S(2)}) collective-permute-start(bf16[3,4,16,1024]{3,2,1,0:T(8,128)(2,1)S(1)} %get-tuple-element.45), channel_id=1, source_target_pairs={{0,4},{4,0},{8,12},{12,8},{16,20},{20,16},{24,28},{28,24},{1,5},{5... | collective-permute-start | bytes 1179656 | tf_op jit(solution)/shard_map/ppermute | solution.py:279
  39.8 5.7 %collective-permute-start.14 = (bf16[4,16,1024]{2,1,0:T(8,128)(2,1)S(1)}, bf16[4,16,1024]{2,1,0:T(8,128)(2,1)S(1)}, u32[]{:S(2)}, u32[]{:S(2)}) collective-permute-start(bf16[4,16,1024]{2,1,0:T(8,128)(2,1)S(1)} %fusion.5), channel_id=1, source_target_pairs={{0,16},{4,12},{8,24},{12,4},{16,0},{20,28},{24,8},{28,20},{1,17},{... | collective-permute-start | bytes 393224 | tf_op jit(solution)/shard_map/ppermute | solution.py:283
  44.0 6.4 %collective-permute-start.13 = (bf16[4,16,1024]{2,1,0:T(8,128)(2,1)S(1)}, bf16[4,16,1024]{2,1,0:T(8,128)(2,1)S(1)}, u32[]{:S(2)}, u32[]{:S(2)}) collective-permute-start(bf16[4,16,1024]{2,1,0:T(8,128)(2,1)S(1)} %fusion.2), channel_id=1, source_target_pairs={{0,8},{4,20},{8,0},{12,28},{16,24},{20,4},{24,16},{28,12},{1,9},{5... | collective-permute-start | bytes 393224 | tf_op jit(solution)/shard_map/ppermute | solution.py:283
  44.8 7.6 %collective-permute-start.11 = (bf16[4,16,2048]{2,1,0:T(8,128)(2,1)S(1)}, bf16[4,16,2048]{2,1,0:T(8,128)(2,1)S(1)}, u32[]{:S(2)}, u32[]{:S(2)}) collective-permute-start(bf16[4,16,2048]{2,1,0:T(8,128)(2,1)S(1)} %pad_maximum_fusion.2), channel_id=1, source_target_pairs={{0,16},{4,12},{8,24},{12,4},{16,0},{20,28},{24,8},{28,20},{1,17},{... | collective-permute-start | bytes 786440 | tf_op jit(solution)/shard_map/ppermute | solution.py:283
  45.5 6.9 %collective-permute-start.15 = (bf16[4,16,1024]{2,1,0:T(8,128)(2,1)S(1)}, bf16[4,16,1024]{2,1,0:T(8,128)(2,1)S(1)}, u32[]{:S(2)}, u32[]{:S(2)}) collective-permute-start(bf16[4,16,1024]{2,1,0:T(8,128)(2,1)S(1)} %fusion), channel_id=1, source_target_pairs={{0,8},{4,20},{8,0},{12,28},{16,24},{20,4},{24,16},{28,12},{1,9},{5... | collective-permute-start | bytes 393224 | tf_op jit(solution)/shard_map/ppermute | solution.py:283
  52.7 6.7 %collective-permute-start.16 = (bf16[16,2048]{1,0:T(8,128)(2,1)S(1)}, bf16[16,2048]{1,0:T(8,128)(2,1)S(1)}, u32[]{:S(2)}, u32[]{:S(2)}) collective-permute-start(bf16[16,2048]{1,0:T(8,128)(2,1)S(1)} %pad_maximum_fusion.3), channel_id=1, source_target_pairs={{0,3},{1,2},{2,1},{3,0},{4,7},{5,6},{6,5},{7,4},{8,11},{9,10},{10,... | collective-permute-start | bytes 196616 | tf_op jit(solution)/shard_map/ppermute | solution.py:286
  53.5 7.4 %collective-permute-start.17 = (bf16[16,2048]{1,0:T(8,128)(2,1)S(1)}, bf16[16,2048]{1,0:T(8,128)(2,1)S(1)}, u32[]{:S(2)}, u32[]{:S(2)}) collective-permute-start(bf16[16,2048]{1,0:T(8,128)(2,1)S(1)} %pad_maximum_fusion.4), channel_id=1, source_target_pairs={{0,2},{1,3},{2,0},{3,1},{4,6},{5,7},{6,4},{7,5},{8,10},{9,11},{10,... | collective-permute-start | bytes 196616 | tf_op jit(solution)/shard_map/ppermute | solution.py:286
  54.5 6.4 %collective-permute-start.18 = (bf16[16,2048]{1,0:T(8,128)(2,1)S(1)}, bf16[16,2048]{1,0:T(8,128)(2,1)S(1)}, u32[]{:S(2)}, u32[]{:S(2)}) collective-permute-start(bf16[16,2048]{1,0:T(8,128)(2,1)S(1)} %pad_maximum_fusion.5), channel_id=1, source_target_pairs={{0,1},{1,0},{2,3},{3,2},{4,5},{5,4},{6,7},{7,6},{8,9},{9,8},{10,11... | collective-permute-start | bytes 196616 | tf_op jit(solution)/shard_map/ppermute | solution.py:286

commit v10 on v8

--- a/solution.py
+++ b/solution.py
@@ -11,7 +11,6 @@
 PARTS = 2
 LANES = 128
 CHUNKS = 8
-FLIGHT = 3
 VMEM_BYTES = 24 * 2**20
 F32, BF16 = jnp.float32, jnp.bfloat16
 
@@ -33,9 +32,10 @@
 
 
 def row_order(n_seq):
-    last = n_seq // 2 - 1
-    early = [(core, chip) for core in (0, 1) for chip in range(last)]
-    return early + [(0, last), (1, last)]
+    n_chip = n_seq // 2
+    cut = n_chip // 2
+    groups = [(core, range(low, low + cut)) for low in (0, cut) for core in (0, 1)]
+    return [(core, chip) for core, chips in groups for chip in chips]
 
 
 def owner_of(n_seq, core, chip):
@@ -47,12 +47,6 @@
 
 def lanes_of(n_seq):
     return -(-n_seq * ACT_DEV // LANES) * LANES
-
-
-def arrive(copies, i):
-    copies[i].wait()
-    if i + FLIGHT < len(copies):
-        copies[i + FLIGHT].start()
 
 
 def select_kernel(mask_ref, hidden_ref, *refs):
@@ -66,7 +60,7 @@
     ]
     mask_copy = pltpu.make_async_copy(mask_ref, mask_here, mask_sem)
     mask_copy.start()
-    for copy in copies[:FLIGHT]:
+    for copy in copies:
         copy.start()
     mask_copy.wait()
     mask = mask_here[...]
@@ -78,7 +72,7 @@
     picker_ref[...] = picker
     each = chunks // len(own_refs)
     for i in range(chunks):
-        arrive(copies, i)
+        copies[i].wait()
         own = jnp.dot(picker, hidden_here[i], preferred_element_type=F32)
         at = (i % each) * step
         own_refs[i // each][:, at : at + step] = own.astype(BF16)
@@ -86,7 +80,7 @@
 
 def select(mask, hidden):
     tokens, width = hidden.shape
-    chunks = 4
+    chunks = CHUNKS
     own = jax.ShapeDtypeStruct((ACT_DEV, width // PARTS), BF16)
     *own, picker = pl.pallas_call(
         select_kernel,
@@ -208,8 +202,7 @@
     logits = logits_ref[...]
     prob = jnp.exp(logits - ordered[:, 0:1]) * ordered[:, 1:2]
     score = (prob * (ordered[:, 2:3] - logits)).astype(BF16)
-    n_chip = n_seq // 2
-    last = n_chip - 1
+    cut = n_seq // 4
     size = near_refs[0].shape[3]
     for v in range(n_vocab):
         for c in range(PARTS):
@@ -221,10 +214,11 @@
                 preferred_element_type=F32,
             ).astype(BF16)
             blocks = part.reshape(n_seq, ACT_DEV, size)
-            near_refs[c][:last, v] = blocks[:last]
-            far_refs[c][:, v] = blocks[last : 2 * last]
-            near_refs[c][last, v] = blocks[2 * last]
-            last_ref[c, v] = blocks[2 * last + 1]
+            near_refs[c][:cut, v] = blocks[:cut]
+            far_refs[c][:cut, v] = blocks[cut : 2 * cut]
+            near_refs[c][cut:, v] = blocks[2 * cut : 3 * cut]
+            far_refs[c][cut:, v] = blocks[3 * cut : 4 * cut - 1]
+            last_ref[c, v] = blocks[4 * cut - 1]
 
 
 def gradients(n_seq, n_vocab, stats, logits, head):
@@ -266,17 +260,18 @@
     own, picker = select(mask, hidden)
 
     near = [own]
+    cut = n_chip // 2
     for a in range(1, n_chip):
         step = a.bit_length() - 1
         source = near[a ^ (1 << step)]
         if a > 1 and a == 1 << step:
-            moved = swap_chip(jnp.concatenate(source, axis=1), step)
-            near.append(jnp.split(moved, PARTS, axis=1))
-        else:
-            near.append([swap_chip(part, step) for part in source])
-    early = jnp.concatenate([near[a][c] for c in range(PARTS) for a in range(last)], axis=0)
-    early, near[last][0] = lax.optimization_barrier((early, near[last][0]))
-    late = jnp.concatenate(near[last], axis=0)
+            source, _ = lax.optimization_barrier((source, near[1]))
+        near.append([swap_chip(part, step) for part in source])
+
+    def gather_rows(chips):
+        return jnp.concatenate([near[a][c] for c in range(PARTS) for a in chips], axis=0)
+
+    early, late = gather_rows(range(cut)), gather_rows(range(cut, n_chip))
     blocks = [early, swap_core(early), late, swap_core(late)]
 
     logits, stats = local_logits(n_seq, n_vocab, blocks, head, picker)

time: 61.1 us -> 63.3 us (1.036)
  waiting for transfers between devices: 18.8 us -> 24.5 us
  starting transfers between devices: 19.8 us -> 17 us
  blocking collectives: 13.7 us -> 12.9 us
    ppermute x10 -> x11, waiting for transfers between devices: 12.8 us -> 18.1 us  [swap_chip(): lax.ppermute(value, 'seq', [(i, i ^ flips[i & 1]) for i in range(n_seq)])]
    ppermute x10 -> x11, starting transfers between devices: 14.9 us -> 12.1 us  [swap_chip(): lax.ppermute(value, 'seq', [(i, i ^ flips[i & 1]) for i in range(n_seq)])]
    all_to_all x1, blocking collectives: 13.7 us -> 12.9 us  [body(): stats = lax.all_to_all(stats, ('seq', 'vocab'), 0, 0, tiled=True)]
  transfers between devices with their start and end apart: 18 -> 19, of which waited for: 10 -> 12; matrix products, arithmetic and copies ran while one was open for 1% -> 0% of each run, Pallas kernels for 1% -> 1%
where the time goes in v10:
time: 63.3 us; the launch traced here: 63.1 us
  waiting for transfers between devices  24.5 us (39%)
  starting transfers between devices  17 us (27%)
  blocking collectives  12.9 us (20%)
  Pallas kernels  6.18 us (10%)
  matrix products  1.12 us (2%)
  between operations  0.82 us (1%)
    ppermute x11, waiting for transfers between devices, swap_chip(): lax.ppermute(value, 'seq', [(i, i ^ flips[i & 1]) for i in range(n_seq)])  18.1 us
    all_to_all x1, blocking collectives, body(): stats = lax.all_to_all(stats, ('seq', 'vocab'), 0, 0, tiled=True)  12.9 us
    ppermute x11, starting transfers between devices, swap_chip(): lax.ppermute(value, 'seq', [(i, i ^ flips[i & 1]) for i in range(n_seq)])  12.1 us
    ppermute x3, starting transfers between devices, send_vocab(): return lax.ppermute(value, 'vocab', [(i, i ^ k) for i in range(n_vocab)])  4.45 us
    ppermute x5, waiting for transfers between devices, swap_core(): return lax.ppermute(value, 'seq', [(i, i ^ 1) for i in range(n_seq)])  3.42 us
    ppermute x3, waiting for transfers between devices, send_vocab(): return lax.ppermute(value, 'vocab', [(i, i ^ k) for i in range(n_vocab)])  2.99 us
    pallas_call x1, Pallas kernels, select(): pl.pallas_call(select_kernel, in_specs=[pl.BlockSpec(memory_space=pltpu.H...  2.81 us
    pallas_call x1, Pallas kernels, gradients(): pl.pallas_call(functools.partial(gradient_kernel, n_seq, n_vocab), in_spe...  1.64 us
  transfers between devices with their start and end apart: 19, of which 12 were waited for; matrix products, arithmetic and copies ran while one was open for 0% of the time, Pallas kernels for 1%

profile of v10, /device:TPU:0, one launch (start us, length us, event | category | flops | bytes accessed | tf_op | source)
XLA Modules:
  0.0 63.1 jit_solution(7633192485618024139)
XLA Ops:
  0.6 2.8 %select_rows.1 = (bf16[16,4096]{1,0:T(8,128)(2,1)S(1)}, bf16[16,4096]{1,0:T(8,128)(2,1)S(1)}, bf16[16,128]{1,0:T(8,128)(2,1)S(1)}) custom-call(s32[1,128]{1,0:T(1,128)} %bitcast.44, bf16[128,8192]{1,0:T(8,128)(2,1)} %hidden_ref.1), custom_call_target="tpu_custom_call" | custom-call | tf_op jit(solution)/shard_map/select_rows/pallas_call | solution.py:85
  3.5 3.0 %collective-permute-start = (bf16[16,4096]{1,0:T(8,128)(2,1)S(1)}, bf16[16,4096]{1,0:T(8,128)(2,1)S(1)}, u32[]{:S(2)}, u32[]{:S(2)}) collective-permute-start(bf16[16,4096]{1,0:T(8,128)(2,1)S(1)} %get-tuple-element.24), channel_id=1, source_target_pairs={{0,8},{4,20},{8,0},{12,28},{16,24},{20,4},{24,16},{28,12},{1,9},{5... | collective-permute-start | bytes 393224 | tf_op jit(solution)/shard_map/ppermute | solution.py:255
  6.5 0.1 collective-permute-start.1
  6.6 2.9 %collective-permute-done = bf16[16,4096]{1,0:T(8,128)(2,1)S(1)} collective-permute-done((bf16[16,4096]{1,0:T(8,128)(2,1)S(1)}, bf16[16,4096]{1,0:T(8,128)(2,1)S(1)}, u32[]{:S(2)}, u32[]{:S(2)}) %collective-permute-start) | collective-permute-done | bytes 131104 | tf_op jit(solution)/shard_map/ppermute | solution.py:255
  9.4 2.0 %collective-permute-done.1 = bf16[16,4096]{1,0:T(8,128)(2,1)S(1)} collective-permute-done((bf16[16,4096]{1,0:T(8,128)(2,1)S(1)}, bf16[16,4096]{1,0:T(8,128)(2,1)S(1)}, u32[]{:S(2)}, u32[]{:S(2)}) %collective-permute-start.1) | collective-permute-done | bytes 131104 | tf_op jit(solution)/shard_map/ppermute | solution.py:255
  11.4 1.5 %collective-permute-start.3 = (bf16[16,4096]{1,0:T(8,128)(2,1)S(1)}, bf16[16,4096]{1,0:T(8,128)(2,1)S(1)}, u32[]{:S(2)}, u32[]{:S(2)}) collective-permute-start(bf16[16,4096]{1,0:T(8,128)(2,1)S(1)} %get-tuple-element.24), channel_id=1, source_target_pairs={{0,16},{4,12},{8,24},{12,4},{16,0},{20,28},{24,8},{28,20},{1,17},{... | collective-permute-start | bytes 393224 | tf_op jit(solution)/shard_map/ppermute | solution.py:255
  12.9 0.5 collective-permute-start.5
  13.5 0.1 collective-permute-start.2
  13.6 1.6 %collective-permute-start.4 = (bf16[16,4096]{1,0:T(8,128)(2,1)S(1)}, bf16[16,4096]{1,0:T(8,128)(2,1)S(1)}, u32[]{:S(2)}, u32[]{:S(2)}) collective-permute-start(bf16[16,4096]{1,0:T(8,128)(2,1)S(1)} %collective-permute-done), channel_id=1, source_target_pairs={{0,16},{4,12},{8,24},{12,4},{16,0},{20,28},{24,8},{28,20},{1,17},{... | collective-permute-start | bytes 393224 | tf_op jit(solution)/shard_map/ppermute | solution.py:255
  15.2 0.5 collective-permute-start.6
  15.7 0.7 %collective-permute-done.3 = bf16[16,4096]{1,0:T(8,128)(2,1)S(1)} collective-permute-done((bf16[16,4096]{1,0:T(8,128)(2,1)S(1)}, bf16[16,4096]{1,0:T(8,128)(2,1)S(1)}, u32[]{:S(2)}, u32[]{:S(2)}) %collective-permute-start.3) | collective-permute-done | bytes 131104 | tf_op jit(solution)/shard_map/ppermute | solution.py:255
  16.4 2.9 %collective-permute-done.4 = bf16[16,4096]{1,0:T(8,128)(2,1)S(1)} collective-permute-done((bf16[16,4096]{1,0:T(8,128)(2,1)S(1)}, bf16[16,4096]{1,0:T(8,128)(2,1)S(1)}, u32[]{:S(2)}, u32[]{:S(2)}) %collective-permute-start.4) | collective-permute-done | bytes 131104 | tf_op jit(solution)/shard_map/ppermute | solution.py:255
  19.3 0.0 collective-permute-done.5
  19.4 1.4 %collective-permute-done.6 = bf16[16,4096]{1,0:T(8,128)(2,1)S(1)} collective-permute-done((bf16[16,4096]{1,0:T(8,128)(2,1)S(1)}, bf16[16,4096]{1,0:T(8,128)(2,1)S(1)}, u32[]{:S(2)}, u32[]{:S(2)}) %collective-permute-start.6) | collective-permute-done | bytes 131104 | tf_op jit(solution)/shard_map/ppermute | solution.py:255
  20.7 0.1 collective-permute-start.7
  20.8 0.0 collective-permute-done.2.refs_1_
  20.8 1.9 %collective-permute-done.7.refs_3_ = bf16[64,4096]{1,0:T(8,128)(2,1)S(1)} collective-permute-done((bf16[64,4096]{1,0:T(8,128)(2,1)S(1)}, bf16[64,4096]{1,0:T(8,128)(2,1)S(1)}, u32[]{:S(2)}, u32[]{:S(2)}) %collective-permute-start.7) | collective-permute-done | bytes 524320 | tf_op jit(solution)/shard_map/ppermute | solution.py:251
  22.7 1.0 %local_logits.1 = (f32[128,256]{1,0:T(8,128)S(1)}, f32[32,4,128]{2,1,0:T(4,128)S(1)}) custom-call(bf16[64,4096]{1,0:T(8,128)(2,1)S(1)} %constant_dynamic-update-slice_fusion.refs_0_, bf16[64,4096]{1,0:T(8,128)(2,1)S(1)} %collective-permute-done.2.refs_1_, bf16[64,4096]{1,0:T(8,128)(2,1)S(1)} %constant_dynamic-update-slice_fusion.4.refs_2_, ...), custom_call_target="tpu_custom_call" | custom-call | tf_op jit(solution)/shard_map/local_logits/pallas_call | solution.py:140
  23.7 12.9 %all_to_all.5.stats_ref = f32[32,4,128]{2,1,0:T(4,128)S(1)} all-to-all(f32[32,4,128]{2,1,0:T(4,128)S(1)} %get-tuple-element.27), channel_id=1, replica_groups=mesh['seq'=8,'vocab'=4] {'seq','vocab'}, dimensions={0} | all-to-all | bytes 131072 | tf_op jit(solution)/shard_map/all_to_all | solution.py:278
  36.6 1.6 %gradients.1 = (bf16[4,4,16,1024]{3,2,1,0:T(8,128)(2,1)S(1)}, bf16[4,4,16,1024]{3,2,1,0:T(8,128)(2,1)S(1)}, bf16[3,4,16,1024]{3,2,1,0:T(8,128)(2,1)S(1)}, bf16[3...) custom-call(f32[32,4,128]{2,1,0:T(4,128)S(1)} %all_to_all.5.stats_ref, ...), custom_call_target="tpu_custom_call" | custom-call | tf_op jit(solution)/shard_map/gradients/pallas_call | solution.py:231
  38.3 0.1 collective-permute-start.8
  38.4 1.5 %collective-permute-done.8 = bf16[2,4,16,1024]{3,2,1,0:T(8,128)(2,1)S(1)} collective-permute-done((bf16[2,4,16,1024]{3,2,1,0:T(8,128)(2,1)S(1)}, bf16[2,4,16,1024]{3,2,1,0:T(8,128)(2,1)S(1)}, u32[]{:S(2)}, u32[]{:S(2)}) %collective-permute-start.8) | collective-permute-done | bytes 262176 | tf_op jit(solution)/shard_map/ppermute | solution.py:251
  39.9 0.1 fusion.5
  39.9 0.2 collective-permute-start.9
  40.1 0.7 %collective-permute-start.12 = (bf16[4,16,1024]{2,1,0:T(8,128)(2,1)S(1)}, bf16[4,16,1024]{2,1,0:T(8,128)(2,1)S(1)}, u32[]{:S(2)}, u32[]{:S(2)}) collective-permute-start(bf16[4,16,1024]{2,1,0:T(8,128)(2,1)S(1)} %get-tuple-element.36), channel_id=1, source_target_pairs={{0,16},{4,12},{8,24},{12,4},{16,0},{20,28},{24,8},{28,20},{1,17},{... | collective-permute-start | bytes 393224 | tf_op jit(solution)/shard_map/ppermute | solution.py:255
  40.8 0.1 collective-permute-start.10
  40.9 1.3 %collective-permute-start.14 = (bf16[4,16,1024]{2,1,0:T(8,128)(2,1)S(1)}, bf16[4,16,1024]{2,1,0:T(8,128)(2,1)S(1)}, u32[]{:S(2)}, u32[]{:S(2)}) collective-permute-start(bf16[4,16,1024]{2,1,0:T(8,128)(2,1)S(1)} %get-tuple-element.37), channel_id=1, source_target_pairs={{0,16},{4,12},{8,24},{12,4},{16,0},{20,28},{24,8},{28,20},{1,17},{... | collective-permute-start | bytes 393224 | tf_op jit(solution)/shard_map/ppermute | solution.py:255
  42.2 2.9 %collective-permute-done.12 = bf16[4,16,1024]{2,1,0:T(8,128)(2,1)S(1)} collective-permute-done((bf16[4,16,1024]{2,1,0:T(8,128)(2,1)S(1)}, bf16[4,16,1024]{2,1,0:T(8,128)(2,1)S(1)}, u32[]{:S(2)}, u32[]{:S(2)}) %collective-permute-start.12) | collective-permute-done | bytes 131104 | tf_op jit(solution)/shard_map/ppermute | solution.py:255
  45.1 0.0 collective-permute-done.9
  45.1 0.1 fusion.2
  45.2 0.7 %collective-permute-start.13 = (bf16[4,16,1024]{2,1,0:T(8,128)(2,1)S(1)}, bf16[4,16,1024]{2,1,0:T(8,128)(2,1)S(1)}, u32[]{:S(2)}, u32[]{:S(2)}) collective-permute-start(bf16[4,16,1024]{2,1,0:T(8,128)(2,1)S(1)} %fusion.2), channel_id=1, source_target_pairs={{0,8},{4,20},{8,0},{12,28},{16,24},{20,4},{24,16},{28,12},{1,9},{5... | collective-permute-start | bytes 393224 | tf_op jit(solution)/shard_map/ppermute | solution.py:255
  45.9 0.0 collective-permute-done.10
  46.0 0.6 collective-permute-start.11
  46.6 0.0 collective-permute-done.14
  46.6 0.1 fusion
  46.7 1.6 %collective-permute-start.15 = (bf16[4,16,1024]{2,1,0:T(8,128)(2,1)S(1)}, bf16[4,16,1024]{2,1,0:T(8,128)(2,1)S(1)}, u32[]{:S(2)}, u32[]{:S(2)}) collective-permute-start(bf16[4,16,1024]{2,1,0:T(8,128)(2,1)S(1)} %fusion), channel_id=1, source_target_pairs={{0,8},{4,20},{8,0},{12,28},{16,24},{20,4},{24,16},{28,12},{1,9},{5... | collective-permute-start | bytes 393224 | tf_op jit(solution)/shard_map/ppermute | solution.py:255
  48.3 3.3 %collective-permute-done.13 = bf16[4,16,1024]{2,1,0:T(8,128)(2,1)S(1)} collective-permute-done((bf16[4,16,1024]{2,1,0:T(8,128)(2,1)S(1)}, bf16[4,16,1024]{2,1,0:T(8,128)(2,1)S(1)}, u32[]{:S(2)}, u32[]{:S(2)}) %collective-permute-start.13) | collective-permute-done | bytes 131104 | tf_op jit(solution)/shard_map/ppermute | solution.py:255
  51.6 2.0 %collective-permute-done.15 = bf16[4,16,1024]{2,1,0:T(8,128)(2,1)S(1)} collective-permute-done((bf16[4,16,1024]{2,1,0:T(8,128)(2,1)S(1)}, bf16[4,16,1024]{2,1,0:T(8,128)(2,1)S(1)}, u32[]{:S(2)}, u32[]{:S(2)}) %collective-permute-start.15) | collective-permute-done | bytes 131104 | tf_op jit(solution)/shard_map/ppermute | solution.py:255
  53.6 0.0 collective-permute-done.11
  53.6 0.2 fusion.1
  53.8 0.9 %collective-permute-start.16 = (bf16[16,2048]{1,0:T(8,128)(2,1)S(1)}, bf16[16,2048]{1,0:T(8,128)(2,1)S(1)}, u32[]{:S(2)}, u32[]{:S(2)}) collective-permute-start(bf16[16,2048]{1,0:T(8,128)(2,1)S(1)} %pad_maximum_fusion.1), channel_id=1, source_target_pairs={{0,3},{1,2},{2,1},{3,0},{4,7},{5,6},{6,5},{7,4},{8,11},{9,10},{10,... | collective-permute-start | bytes 196616 | tf_op jit(solution)/shard_map/ppermute | solution.py:258
  54.7 0.9 %collective-permute-start.17 = (bf16[16,2048]{1,0:T(8,128)(2,1)S(1)}, bf16[16,2048]{1,0:T(8,128)(2,1)S(1)}, u32[]{:S(2)}, u32[]{:S(2)}) collective-permute-start(bf16[16,2048]{1,0:T(8,128)(2,1)S(1)} %pad_maximum_fusion.2), channel_id=1, source_target_pairs={{0,2},{1,3},{2,0},{3,1},{4,6},{5,7},{6,4},{7,5},{8,10},{9,11},{10,... | collective-permute-start | bytes 196616 | tf_op jit(solution)/shard_map/ppermute | solution.py:258
  55.6 2.7 %collective-permute-start.18 = (bf16[16,2048]{1,0:T(8,128)(2,1)S(1)}, bf16[16,2048]{1,0:T(8,128)(2,1)S(1)}, u32[]{:S(2)}, u32[]{:S(2)}) collective-permute-start(bf16[16,2048]{1,0:T(8,128)(2,1)S(1)} %pad_maximum_fusion.3), channel_id=1, source_target_pairs={{0,1},{1,0},{2,3},{3,2},{4,5},{5,4},{6,7},{7,6},{8,9},{9,8},{10,11... | collective-permute-start | bytes 196616 | tf_op jit(solution)/shard_map/ppermute | solution.py:258
  58.3 0.8 %entropies.1 = (f32[1,128]{1,0:T(1,128)}, f32[1,1]{1,0:T(1,128)}) custom-call(f32[32,4,128]{2,1,0:T(4,128)S(1)} %all_to_all.5.stats_ref, bf16[16,128]{1,0:T(8,128)(2,1)S(1)} %get-tuple-element.26.refs_5_.picker_ref), custom_call_target="tpu_custom_call" | custom-call | tf_op jit(solution)/shard_map/entropies/pallas_call | solution.py:180
  59.0 1.4 %collective-permute-done.16 = bf16[16,2048]{1,0:T(8,128)(2,1)S(1)} collective-permute-done((bf16[16,2048]{1,0:T(8,128)(2,1)S(1)}, bf16[16,2048]{1,0:T(8,128)(2,1)S(1)}, u32[]{:S(2)}, u32[]{:S(2)}) %collective-permute-start.16) | collective-permute-done | bytes 65568 | tf_op jit(solution)/shard_map/ppermute | solution.py:258
  60.4 1.6 %collective-permute-done.17 = bf16[16,2048]{1,0:T(8,128)(2,1)S(1)} collective-permute-done((bf16[16,2048]{1,0:T(8,128)(2,1)S(1)}, bf16[16,2048]{1,0:T(8,128)(2,1)S(1)}, u32[]{:S(2)}, u32[]{:S(2)}) %collective-permute-start.17) | collective-permute-done | bytes 65568 | tf_op jit(solution)/shard_map/ppermute | solution.py:258
  62.0 0.0 collective-permute-done.18
  62.0 1.1 %convolution_convert_fusion = bf16[128,2048]{1,0:T(8,128)(2,1)} fusion(bf16[16,128]{1,0:T(8,128)(2,1)S(1)} %get-tuple-element.26.refs_5_.picker_ref, f32[16,1024]{1,0:T(8,128)S(1)} %get-tuple-element.51, f32[16,1024]{1,0:T(8,128)S(1)} %get-tuple-element.52, bf16[16,2048]{1,0:T(8,128)(2,1)S(1)} %collective-permute-done.18, ...), kind=kOutput, calls=%fused_computation | convolution fusion | flops 8912896 | bytes 856064 | tf_op jit(solution)/shard_map/dot_general | solution.py:308
  (18 shorter events, 0.2 us)
Async XLA Ops:
  0.6 22.1 %copy-start = (bf16[8192,256]{1,0:T(8,128)(2,1)S(1)}, bf16[8192,256]{1,0:T(8,128)(2,1)}, u32[]{:S(2)}) copy-start(bf16[8192,256]{1,0:T(8,128)(2,1)} %head_ref.1) | copy-start | bytes 12582916
  3.5 6.0 %collective-permute-start = (bf16[16,4096]{1,0:T(8,128)(2,1)S(1)}, bf16[16,4096]{1,0:T(8,128)(2,1)S(1)}, u32[]{:S(2)}, u32[]{:S(2)}) collective-permute-start(bf16[16,4096]{1,0:T(8,128)(2,1)S(1)} %get-tuple-element.24), channel_id=1, source_target_pairs={{0,8},{4,20},{8,0},{12,28},{16,24},{20,4},{24,16},{28,12},{1,9},{5... | collective-permute-start | bytes 393224 | tf_op jit(solution)/shard_map/ppermute | solution.py:255
  6.5 5.0 %collective-permute-start.1 = (bf16[16,4096]{1,0:T(8,128)(2,1)S(1)}, bf16[16,4096]{1,0:T(8,128)(2,1)S(1)}, u32[]{:S(2)}, u32[]{:S(2)}) collective-permute-start(bf16[16,4096]{1,0:T(8,128)(2,1)S(1)} %get-tuple-element.25), channel_id=1, source_target_pairs={{0,8},{4,20},{8,0},{12,28},{16,24},{20,4},{24,16},{28,12},{1,9},{5... | collective-permute-start | bytes 393224 | tf_op jit(solution)/shard_map/ppermute | solution.py:255
  11.4 5.0 %collective-permute-start.3 = (bf16[16,4096]{1,0:T(8,128)(2,1)S(1)}, bf16[16,4096]{1,0:T(8,128)(2,1)S(1)}, u32[]{:S(2)}, u32[]{:S(2)}) collective-permute-start(bf16[16,4096]{1,0:T(8,128)(2,1)S(1)} %get-tuple-element.24), channel_id=1, source_target_pairs={{0,16},{4,12},{8,24},{12,4},{16,0},{20,28},{24,8},{28,20},{1,17},{... | collective-permute-start | bytes 393224 | tf_op jit(solution)/shard_map/ppermute | solution.py:255
  12.9 6.4 %collective-permute-start.5 = (bf16[16,4096]{1,0:T(8,128)(2,1)S(1)}, bf16[16,4096]{1,0:T(8,128)(2,1)S(1)}, u32[]{:S(2)}, u32[]{:S(2)}) collective-permute-start(bf16[16,4096]{1,0:T(8,128)(2,1)S(1)} %get-tuple-element.25), channel_id=1, source_target_pairs={{0,16},{4,12},{8,24},{12,4},{16,0},{20,28},{24,8},{28,20},{1,17},{... | collective-permute-start | bytes 393224 | tf_op jit(solution)/shard_map/ppermute | solution.py:255
  13.5 7.3 %collective-permute-start.2 = (bf16[64,4096]{1,0:T(8,128)(2,1)S(1)}, bf16[64,4096]{1,0:T(8,128)(2,1)S(1)}, u32[]{:S(2)}, u32[]{:S(2)}) collective-permute-start(bf16[64,4096]{1,0:T(8,128)(2,1)S(1)} %constant_dynamic-update-slice_fusion.refs_0_), channel_id=1, source_target_pairs={{0,4},{4,0},{8,12},{12,8},{16,20},{20,16},{24,28},{28,24},{1,5},{5... | collective-permute-start | bytes 1572872 | tf_op jit(solution)/shard_map/ppermute | solution.py:251
  13.6 5.7 %collective-permute-start.4 = (bf16[16,4096]{1,0:T(8,128)(2,1)S(1)}, bf16[16,4096]{1,0:T(8,128)(2,1)S(1)}, u32[]{:S(2)}, u32[]{:S(2)}) collective-permute-start(bf16[16,4096]{1,0:T(8,128)(2,1)S(1)} %collective-permute-done), channel_id=1, source_target_pairs={{0,16},{4,12},{8,24},{12,4},{16,0},{20,28},{24,8},{28,20},{1,17},{... | collective-permute-start | bytes 393224 | tf_op jit(solution)/shard_map/ppermute | solution.py:255
  15.2 5.6 %collective-permute-start.6 = (bf16[16,4096]{1,0:T(8,128)(2,1)S(1)}, bf16[16,4096]{1,0:T(8,128)(2,1)S(1)}, u32[]{:S(2)}, u32[]{:S(2)}) collective-permute-start(bf16[16,4096]{1,0:T(8,128)(2,1)S(1)} %collective-permute-done.1), channel_id=1, source_target_pairs={{0,16},{4,12},{8,24},{12,4},{16,0},{20,28},{24,8},{28,20},{1,17},{... | collective-permute-start | bytes 393224 | tf_op jit(solution)/shard_map/ppermute | solution.py:255
  20.7 2.0 %collective-permute-start.7 = (bf16[64,4096]{1,0:T(8,128)(2,1)S(1)}, bf16[64,4096]{1,0:T(8,128)(2,1)S(1)}, u32[]{:S(2)}, u32[]{:S(2)}) collective-permute-start(bf16[64,4096]{1,0:T(8,128)(2,1)S(1)} %constant_dynamic-update-slice_fusion.4.refs_2_), channel_id=1, source_target_pairs={{0,4},{4,0},{8,12},{12,8},{16,20},{20,16},{24,28},{28,24},{1,5},{5... | collective-permute-start | bytes 1572872 | tf_op jit(solution)/shard_map/ppermute | solution.py:251
  38.3 1.6 %collective-permute-start.8 = (bf16[2,4,16,1024]{3,2,1,0:T(8,128)(2,1)S(1)}, bf16[2,4,16,1024]{3,2,1,0:T(8,128)(2,1)S(1)}, u32[]{:S(2)}, u32[]{:S(2)}) collective-permute-start(bf16[2,4,16,1024]{3,2,1,0:T(8,128)(2,1)S(1)} %get-tuple-element.32), channel_id=1, source_target_pairs={{0,4},{4,0},{8,12},{12,8},{16,20},{20,16},{24,28},{28,24},{1,5},{5... | collective-permute-start | bytes 786440 | tf_op jit(solution)/shard_map/ppermute | solution.py:251
  39.9 5.2 %collective-permute-start.9 = (bf16[3,4,16,1024]{3,2,1,0:T(8,128)(2,1)S(1)}, bf16[3,4,16,1024]{3,2,1,0:T(8,128)(2,1)S(1)}, u32[]{:S(2)}, u32[]{:S(2)}) collective-permute-start(bf16[3,4,16,1024]{3,2,1,0:T(8,128)(2,1)S(1)} %get-tuple-element.34), channel_id=1, source_target_pairs={{0,4},{4,0},{8,12},{12,8},{16,20},{20,16},{24,28},{28,24},{1,5},{5... | collective-permute-start | bytes 1179656 | tf_op jit(solution)/shard_map/ppermute | solution.py:251
  40.1 5.0 %collective-permute-start.12 = (bf16[4,16,1024]{2,1,0:T(8,128)(2,1)S(1)}, bf16[4,16,1024]{2,1,0:T(8,128)(2,1)S(1)}, u32[]{:S(2)}, u32[]{:S(2)}) collective-permute-start(bf16[4,16,1024]{2,1,0:T(8,128)(2,1)S(1)} %get-tuple-element.36), channel_id=1, source_target_pairs={{0,16},{4,12},{8,24},{12,4},{16,0},{20,28},{24,8},{28,20},{1,17},{... | collective-permute-start | bytes 393224 | tf_op jit(solution)/shard_map/ppermute | solution.py:255
  40.8 5.1 %collective-permute-start.10 = (bf16[3,4,16,1024]{3,2,1,0:T(8,128)(2,1)S(1)}, bf16[3,4,16,1024]{3,2,1,0:T(8,128)(2,1)S(1)}, u32[]{:S(2)}, u32[]{:S(2)}) collective-permute-start(bf16[3,4,16,1024]{3,2,1,0:T(8,128)(2,1)S(1)} %get-tuple-element.35), channel_id=1, source_target_pairs={{0,4},{4,0},{8,12},{12,8},{16,20},{20,16},{24,28},{28,24},{1,5},{5... | collective-permute-start | bytes 1179656 | tf_op jit(solution)/shard_map/ppermute | solution.py:251
  40.9 5.7 %collective-permute-start.14 = (bf16[4,16,1024]{2,1,0:T(8,128)(2,1)S(1)}, bf16[4,16,1024]{2,1,0:T(8,128)(2,1)S(1)}, u32[]{:S(2)}, u32[]{:S(2)}) collective-permute-start(bf16[4,16,1024]{2,1,0:T(8,128)(2,1)S(1)} %get-tuple-element.37), channel_id=1, source_target_pairs={{0,16},{4,12},{8,24},{12,4},{16,0},{20,28},{24,8},{28,20},{1,17},{... | collective-permute-start | bytes 393224 | tf_op jit(solution)/shard_map/ppermute | solution.py:255
  45.2 6.4 %collective-permute-start.13 = (bf16[4,16,1024]{2,1,0:T(8,128)(2,1)S(1)}, bf16[4,16,1024]{2,1,0:T(8,128)(2,1)S(1)}, u32[]{:S(2)}, u32[]{:S(2)}) collective-permute-start(bf16[4,16,1024]{2,1,0:T(8,128)(2,1)S(1)} %fusion.2), channel_id=1, source_target_pairs={{0,8},{4,20},{8,0},{12,28},{16,24},{20,4},{24,16},{28,12},{1,9},{5... | collective-permute-start | bytes 393224 | tf_op jit(solution)/shard_map/ppermute | solution.py:255
  46.0 7.5 %collective-permute-start.11 = (bf16[4,16,2048]{2,1,0:T(8,128)(2,1)S(1)}, bf16[4,16,2048]{2,1,0:T(8,128)(2,1)S(1)}, u32[]{:S(2)}, u32[]{:S(2)}) collective-permute-start(bf16[4,16,2048]{2,1,0:T(8,128)(2,1)S(1)} %pad_maximum_fusion), channel_id=1, source_target_pairs={{0,16},{4,12},{8,24},{12,4},{16,0},{20,28},{24,8},{28,20},{1,17},{... | collective-permute-start | bytes 786440 | tf_op jit(solution)/shard_map/ppermute | solution.py:255
  46.7 6.9 %collective-permute-start.15 = (bf16[4,16,1024]{2,1,0:T(8,128)(2,1)S(1)}, bf16[4,16,1024]{2,1,0:T(8,128)(2,1)S(1)}, u32[]{:S(2)}, u32[]{:S(2)}) collective-permute-start(bf16[4,16,1024]{2,1,0:T(8,128)(2,1)S(1)} %fusion), channel_id=1, source_target_pairs={{0,8},{4,20},{8,0},{12,28},{16,24},{20,4},{24,16},{28,12},{1,9},{5... | collective-permute-start | bytes 393224 | tf_op jit(solution)/shard_map/ppermute | solution.py:255
  53.8 6.6 %collective-permute-start.16 = (bf16[16,2048]{1,0:T(8,128)(2,1)S(1)}, bf16[16,2048]{1,0:T(8,128)(2,1)S(1)}, u32[]{:S(2)}, u32[]{:S(2)}) collective-permute-start(bf16[16,2048]{1,0:T(8,128)(2,1)S(1)} %pad_maximum_fusion.1), channel_id=1, source_target_pairs={{0,3},{1,2},{2,1},{3,0},{4,7},{5,6},{6,5},{7,4},{8,11},{9,10},{10,... | collective-permute-start | bytes 196616 | tf_op jit(solution)/shard_map/ppermute | solution.py:258
  54.7 7.4 %collective-permute-start.17 = (bf16[16,2048]{1,0:T(8,128)(2,1)S(1)}, bf16[16,2048]{1,0:T(8,128)(2,1)S(1)}, u32[]{:S(2)}, u32[]{:S(2)}) collective-permute-start(bf16[16,2048]{1,0:T(8,128)(2,1)S(1)} %pad_maximum_fusion.2), channel_id=1, source_target_pairs={{0,2},{1,3},{2,0},{3,1},{4,6},{5,7},{6,4},{7,5},{8,10},{9,11},{10,... | collective-permute-start | bytes 196616 | tf_op jit(solution)/shard_map/ppermute | solution.py:258
  55.6 6.4 %collective-permute-start.18 = (bf16[16,2048]{1,0:T(8,128)(2,1)S(1)}, bf16[16,2048]{1,0:T(8,128)(2,1)S(1)}, u32[]{:S(2)}, u32[]{:S(2)}) collective-permute-start(bf16[16,2048]{1,0:T(8,128)(2,1)S(1)} %pad_maximum_fusion.3), channel_id=1, source_target_pairs={{0,1},{1,0},{2,3},{3,2},{4,5},{5,4},{6,7},{7,6},{8,9},{9,8},{10,11... | collective-permute-start | bytes 196616 | tf_op jit(solution)/shard_map/ppermute | solution.py:258

commit v11 on v8

--- a/solution.py
+++ b/solution.py
@@ -196,8 +196,8 @@
 
 
 def gradient_kernel(n_seq, n_vocab, stats_ref, logits_ref, head_ref, *refs):
-    *out_refs, last_ref, columns, ordered = refs
-    near_refs, far_refs = out_refs[:PARTS], out_refs[PARTS:]
+    *out_refs, columns, ordered = refs
+    near_refs, far_refs, last_refs = (out_refs[k * PARTS : (k + 1) * PARTS] for k in range(3))
     top, total, centred = merged(stats_ref[...])
     row = iota((8, top.shape[1]), 0)
     lines = jnp.where(row == 0, top, jnp.where(row == 1, 1.0 / total, top + centred))
@@ -224,7 +224,7 @@
             near_refs[c][:last, v] = blocks[:last]
             far_refs[c][:, v] = blocks[last : 2 * last]
             near_refs[c][last, v] = blocks[2 * last]
-            last_ref[c, v] = blocks[2 * last + 1]
+            last_refs[c][v] = blocks[2 * last + 1]
 
 
 def gradients(n_seq, n_vocab, stats, logits, head):
@@ -233,8 +233,8 @@
     block = (n_vocab, ACT_DEV, head.shape[0] // (n_vocab * PARTS))
     outs = [jax.ShapeDtypeStruct((n_chip,) + block, BF16)] * PARTS
     outs += [jax.ShapeDtypeStruct((n_chip - 1,) + block, BF16)] * PARTS
-    outs += [jax.ShapeDtypeStruct((PARTS,) + block, BF16)]
-    *outs, far_last = pl.pallas_call(
+    outs += [jax.ShapeDtypeStruct(block, BF16)] * PARTS
+    outs = pl.pallas_call(
         functools.partial(gradient_kernel, n_seq, n_vocab),
         in_specs=[pl.BlockSpec(memory_space=pltpu.VMEM)] * 3,
         out_shape=outs,
@@ -245,7 +245,7 @@
         compiler_params=params(),
         name="gradients",
     )(stats, logits, head)
-    return outs[:PARTS], outs[PARTS:], far_last
+    return [outs[k * PARTS : (k + 1) * PARTS] for k in range(3)]
 
 
 def body(n_seq, n_vocab, hidden, head, mask):
@@ -282,21 +282,26 @@
     logits, stats = local_logits(n_seq, n_vocab, blocks, head, picker)
     stats = lax.all_to_all(stats, ("seq", "vocab"), 0, 0, tiled=True)
     near, far, far_last = gradients(n_seq, n_vocab, stats, logits, head)
-    moved = swap_core(far_last)
-    first = [(near[c][last].astype(F32) + moved[c].astype(F32)).astype(BF16) for c in range(PARTS)]
-    far, first = lax.optimization_barrier((far, first))
+    moved = [swap_core(part) for part in far_last]
+    far, _ = lax.optimization_barrier((far, moved))
     far = [swap_core(part) for part in far]
     sums = [[near[c][a].astype(F32) + far[c][a].astype(F32) for c in range(PARTS)] for a in range(last)]
-    sums.append(first)
+    sums.append([near[c][last].astype(F32) + moved[c].astype(F32) for c in range(PARTS)])
+    direct = {
+        a: jnp.concatenate([part.astype(BF16) for part in sums[a]], axis=2)
+        for a in range(2, n_chip)
+        if a & (a - 1) == 0 and a > n_chip // 4
+    }
     for a in range(last, 0, -1):
         step = a.bit_length() - 1
-        parts = [part.astype(BF16) for part in sums[a]]
-        if a > 1 and a == 1 << step:
-            moved = jnp.split(swap_chip(jnp.concatenate(parts, axis=2), step), PARTS, axis=2)
+        target = sums[a ^ (1 << step)]
+        if a in direct:
+            moved = jnp.split(swap_chip(direct[a], step), PARTS, axis=2)
         else:
-            moved = [swap_chip(part, step) for part in parts]
-        target = sums[a ^ (1 << step)]
+            moved = [swap_chip(part.astype(BF16), step) for part in sums[a]]
         for c in range(PARTS):
+            if a == last:
+                moved[c], _ = lax.optimization_barrier((moved[c], direct))
             target[c] += moved[c].astype(F32)
 
     stats, _ = lax.optimization_barrier((stats, sums[0]))

time: 61.1 us -> 59.8 us (0.979)
  waiting for transfers between devices: 18.8 us -> 16.7 us
  starting transfers between devices: 19.8 us -> 20.7 us
    ppermute x10, waiting for transfers between devices: 12.8 us -> 10.5 us  [swap_chip(): lax.ppermute(value, 'seq', [(i, i ^ flips[i & 1]) for i in range(n_seq)])]
    ppermute x5 -> x6, waiting for transfers between devices: 3.05 us -> 2.76 us  [swap_core(): return lax.ppermute(value, 'seq', [(i, i ^ 1) for i in range(n_seq)])]
  transfers between devices with their start and end apart: 18 -> 19, of which waited for: 10 -> 13; matrix products, arithmetic and copies ran while one was open for 1% -> 1% of each run, Pallas kernels for 1% -> 1%
where the time goes in v11:
time: 59.8 us; the launch traced here: 59.6 us
  starting transfers between devices  20.7 us (35%)
  waiting for transfers between devices  16.7 us (28%)
  blocking collectives  13.7 us (23%)
  Pallas kernels  6.13 us (10%)
  matrix products  1.12 us (2%)
  between operations  0.81 us (1%)
    ppermute x10, starting transfers between devices, swap_chip(): lax.ppermute(value, 'seq', [(i, i ^ flips[i & 1]) for i in range(n_seq)])  15.2 us
    all_to_all x1, blocking collectives, body(): stats = lax.all_to_all(stats, ('seq', 'vocab'), 0, 0, tiled=True)  13.7 us
    ppermute x10, waiting for transfers between devices, swap_chip(): lax.ppermute(value, 'seq', [(i, i ^ flips[i & 1]) for i in range(n_seq)])  10.5 us
    ppermute x3, starting transfers between devices, send_vocab(): return lax.ppermute(value, 'vocab', [(i, i ^ k) for i in range(n_vocab)])  4.45 us
    ppermute x3, waiting for transfers between devices, send_vocab(): return lax.ppermute(value, 'vocab', [(i, i ^ k) for i in range(n_vocab)])  3.43 us
    ppermute x6, waiting for transfers between devices, swap_core(): return lax.ppermute(value, 'seq', [(i, i ^ 1) for i in range(n_seq)])  2.76 us
    pallas_call x1, Pallas kernels, select(): pl.pallas_call(select_kernel, in_specs=[pl.BlockSpec(memory_space=pltpu.H...  2.75 us
    pallas_call x1, Pallas kernels, gradients(): pl.pallas_call(functools.partial(gradient_kernel, n_seq, n_vocab), in_spe...  1.64 us
  transfers between devices with their start and end apart: 19, of which 13 were waited for; matrix products, arithmetic and copies ran while one was open for 1% of the time, Pallas kernels for 1%

profile of v11, /device:TPU:0, one launch (start us, length us, event | category | flops | bytes accessed | tf_op | source)
XLA Modules:
  0.0 59.6 jit_solution(4603099342705152988)
XLA Ops:
  0.6 0.0 copy-start
  0.6 2.8 %select_rows.1 = (bf16[16,4096]{1,0:T(8,128)(2,1)S(1)}, bf16[16,4096]{1,0:T(8,128)(2,1)S(1)}, bf16[16,128]{1,0:T(8,128)(2,1)S(1)}) custom-call(s32[1,128]{1,0:T(1,128)} %bitcast.46, bf16[128,8192]{1,0:T(8,128)(2,1)} %hidden_ref.1), custom_call_target="tpu_custom_call" | custom-call | tf_op jit(solution)/shard_map/select_rows/pallas_call | solution.py:91
  3.4 3.0 %collective-permute-start = (bf16[16,4096]{1,0:T(8,128)(2,1)S(1)}, bf16[16,4096]{1,0:T(8,128)(2,1)S(1)}, u32[]{:S(2)}, u32[]{:S(2)}) collective-permute-start(bf16[16,4096]{1,0:T(8,128)(2,1)S(1)} %get-tuple-element.23), channel_id=1, source_target_pairs={{0,8},{4,20},{8,0},{12,28},{16,24},{20,4},{24,16},{28,12},{1,9},{5... | collective-permute-start | bytes 393224 | tf_op jit(solution)/shard_map/ppermute | solution.py:261
  6.4 0.1 collective-permute-start.2
  6.5 2.0 %collective-permute-start.1 = (bf16[16,8192]{1,0:T(8,128)(2,1)S(1)}, bf16[16,8192]{1,0:T(8,128)(2,1)S(1)}, u32[]{:S(2)}, u32[]{:S(2)}) collective-permute-start(bf16[16,8192]{1,0:T(8,128)(2,1)S(1)} %pad_maximum_fusion), channel_id=1, source_target_pairs={{0,16},{4,12},{8,24},{12,4},{16,0},{20,28},{24,8},{28,20},{1,17},{... | collective-permute-start | bytes 786440 | tf_op jit(solution)/shard_map/ppermute | solution.py:261
  8.6 1.4 %collective-permute-done = bf16[16,4096]{1,0:T(8,128)(2,1)S(1)} collective-permute-done((bf16[16,4096]{1,0:T(8,128)(2,1)S(1)}, bf16[16,4096]{1,0:T(8,128)(2,1)S(1)}, u32[]{:S(2)}, u32[]{:S(2)}) %collective-permute-start) | collective-permute-done | bytes 131104 | tf_op jit(solution)/shard_map/ppermute | solution.py:261
  10.0 2.5 %collective-permute-start.3 = (bf16[16,4096]{1,0:T(8,128)(2,1)S(1)}, bf16[16,4096]{1,0:T(8,128)(2,1)S(1)}, u32[]{:S(2)}, u32[]{:S(2)}) collective-permute-start(bf16[16,4096]{1,0:T(8,128)(2,1)S(1)} %collective-permute-done), channel_id=1, source_target_pairs={{0,16},{4,12},{8,24},{12,4},{16,0},{20,28},{24,8},{28,20},{1,17},{... | collective-permute-start | bytes 393224 | tf_op jit(solution)/shard_map/ppermute | solution.py:261
  12.5 0.3 collective-permute-done.2
  12.8 2.5 %collective-permute-start.5 = (bf16[16,4096]{1,0:T(8,128)(2,1)S(1)}, bf16[16,4096]{1,0:T(8,128)(2,1)S(1)}, u32[]{:S(2)}, u32[]{:S(2)}) collective-permute-start(bf16[16,4096]{1,0:T(8,128)(2,1)S(1)} %collective-permute-done.2), channel_id=1, source_target_pairs={{0,16},{4,12},{8,24},{12,4},{16,0},{20,28},{24,8},{28,20},{1,17},{... | collective-permute-start | bytes 393224 | tf_op jit(solution)/shard_map/ppermute | solution.py:261
  15.3 0.0 collective-permute-done.1
  15.4 0.0 collective-permute-done.3
  15.4 0.0 collective-permute-start.4
  15.5 2.7 %collective-permute-done.5 = bf16[16,4096]{1,0:T(8,128)(2,1)S(1)} collective-permute-done((bf16[16,4096]{1,0:T(8,128)(2,1)S(1)}, bf16[16,4096]{1,0:T(8,128)(2,1)S(1)}, u32[]{:S(2)}, u32[]{:S(2)}) %collective-permute-start.5) | collective-permute-done | bytes 131104 | tf_op jit(solution)/shard_map/ppermute | solution.py:261
  18.2 0.1 collective-permute-start.6
  18.3 1.5 %collective-permute-done.6.refs_3_ = bf16[32,4096]{1,0:T(8,128)(2,1)S(1)} collective-permute-done((bf16[32,4096]{1,0:T(8,128)(2,1)S(1)}, bf16[32,4096]{1,0:T(8,128)(2,1)S(1)}, u32[]{:S(2)}, u32[]{:S(2)}) %collective-permute-start.6) | collective-permute-done | bytes 262176 | tf_op jit(solution)/shard_map/ppermute | solution.py:257
  19.8 0.0 collective-permute-done.4.refs_1_
  19.8 1.0 %local_logits.1 = (f32[128,256]{1,0:T(8,128)S(1)}, f32[32,4,128]{2,1,0:T(4,128)S(1)}) custom-call(bf16[96,4096]{1,0:T(8,128)(2,1)S(1)} %slice_dynamic-update-slice_fusion.refs_0_, bf16[96,4096]{1,0:T(8,128)(2,1)S(1)} %collective-permute-done.4.refs_1_, bf16[32,4096]{1,0:T(8,128)(2,1)S(1)} %constant_dynamic-update-slice_fusion.4.refs_2_, ...), custom_call_target="tpu_custom_call" | custom-call | tf_op jit(solution)/shard_map/local_logits/pallas_call | solution.py:146
  20.8 13.7 %all_to_all.5.stats_ref = f32[32,4,128]{2,1,0:T(4,128)S(1)} all-to-all(f32[32,4,128]{2,1,0:T(4,128)S(1)} %get-tuple-element.28), channel_id=1, replica_groups=mesh['seq'=8,'vocab'=4] {'seq','vocab'}, dimensions={0} | all-to-all | bytes 131072 | tf_op jit(solution)/shard_map/all_to_all | solution.py:283
  34.5 1.6 %gradients.1 = (bf16[4,4,16,1024]{3,2,1,0:T(8,128)(2,1)S(1)}, bf16[4,4,16,1024]{3,2,1,0:T(8,128)(2,1)S(1)}, bf16[3,4,16,1024]{3,2,1,0:T(8,128)(2,1)S(1)}, bf16[3...) custom-call(f32[32,4,128]{2,1,0:T(4,128)S(1)} %all_to_all.5.stats_ref, ...), custom_call_target="tpu_custom_call" | custom-call | tf_op jit(solution)/shard_map/gradients/pallas_call | solution.py:237
  36.1 0.1 collective-permute-start.7
  36.2 0.5 collective-permute-start.8
  36.7 0.8 %collective-permute-done.7 = bf16[4,16,1024]{2,1,0:T(8,128)(2,1)S(1)} collective-permute-done((bf16[4,16,1024]{2,1,0:T(8,128)(2,1)S(1)}, bf16[4,16,1024]{2,1,0:T(8,128)(2,1)S(1)}, u32[]{:S(2)}, u32[]{:S(2)}) %collective-permute-start.7) | collective-permute-done | bytes 131104 | tf_op jit(solution)/shard_map/ppermute | solution.py:257
  37.5 0.2 collective-permute-done.8
  37.7 0.3 collective-permute-start.9
  38.1 0.7 %collective-permute-start.12 = (bf16[4,16,1024]{2,1,0:T(8,128)(2,1)S(1)}, bf16[4,16,1024]{2,1,0:T(8,128)(2,1)S(1)}, u32[]{:S(2)}, u32[]{:S(2)}) collective-permute-start(bf16[4,16,1024]{2,1,0:T(8,128)(2,1)S(1)} %fusion.1), channel_id=1, source_target_pairs={{0,16},{4,12},{8,24},{12,4},{16,0},{20,28},{24,8},{28,20},{1,17},{... | collective-permute-start | bytes 393224 | tf_op jit(solution)/shard_map/ppermute | solution.py:261
  38.8 0.0 collective-permute-start.10
  38.8 1.4 %collective-permute-start.14 = (bf16[4,16,1024]{2,1,0:T(8,128)(2,1)S(1)}, bf16[4,16,1024]{2,1,0:T(8,128)(2,1)S(1)}, u32[]{:S(2)}, u32[]{:S(2)}) collective-permute-start(bf16[4,16,1024]{2,1,0:T(8,128)(2,1)S(1)} %fusion), channel_id=1, source_target_pairs={{0,16},{4,12},{8,24},{12,4},{16,0},{20,28},{24,8},{28,20},{1,17},{... | collective-permute-start | bytes 393224 | tf_op jit(solution)/shard_map/ppermute | solution.py:261
  40.3 0.0 collective-permute-done.9
  40.3 0.2 collective-permute-done.10
  40.6 1.4 %collective-permute-start.11 = (bf16[4,16,2048]{2,1,0:T(8,128)(2,1)S(1)}, bf16[4,16,2048]{2,1,0:T(8,128)(2,1)S(1)}, u32[]{:S(2)}, u32[]{:S(2)}) collective-permute-start(bf16[4,16,2048]{2,1,0:T(8,128)(2,1)S(1)} %pad_maximum_fusion.1), channel_id=1, source_target_pairs={{0,16},{4,12},{8,24},{12,4},{16,0},{20,28},{24,8},{28,20},{1,17},{... | collective-permute-start | bytes 786440 | tf_op jit(solution)/shard_map/ppermute | solution.py:261
  42.0 1.1 %collective-permute-done.12 = bf16[4,16,1024]{2,1,0:T(8,128)(2,1)S(1)} collective-permute-done((bf16[4,16,1024]{2,1,0:T(8,128)(2,1)S(1)}, bf16[4,16,1024]{2,1,0:T(8,128)(2,1)S(1)}, u32[]{:S(2)}, u32[]{:S(2)}) %collective-permute-start.12) | collective-permute-done | bytes 131104 | tf_op jit(solution)/shard_map/ppermute | solution.py:261
  43.1 0.1 fusion.4
  43.2 0.7 %collective-permute-start.13 = (bf16[4,16,1024]{2,1,0:T(8,128)(2,1)S(1)}, bf16[4,16,1024]{2,1,0:T(8,128)(2,1)S(1)}, u32[]{:S(2)}, u32[]{:S(2)}) collective-permute-start(bf16[4,16,1024]{2,1,0:T(8,128)(2,1)S(1)} %fusion.4), channel_id=1, source_target_pairs={{0,8},{4,20},{8,0},{12,28},{16,24},{20,4},{24,16},{28,12},{1,9},{5... | collective-permute-start | bytes 393224 | tf_op jit(solution)/shard_map/ppermute | solution.py:261
  43.9 0.6 %collective-permute-done.14 = bf16[4,16,1024]{2,1,0:T(8,128)(2,1)S(1)} collective-permute-done((bf16[4,16,1024]{2,1,0:T(8,128)(2,1)S(1)}, bf16[4,16,1024]{2,1,0:T(8,128)(2,1)S(1)}, u32[]{:S(2)}, u32[]{:S(2)}) %collective-permute-start.14) | collective-permute-done | bytes 131104 | tf_op jit(solution)/shard_map/ppermute | solution.py:261
  44.5 0.1 fusion.2
  44.6 0.8 %collective-permute-start.15 = (bf16[4,16,1024]{2,1,0:T(8,128)(2,1)S(1)}, bf16[4,16,1024]{2,1,0:T(8,128)(2,1)S(1)}, u32[]{:S(2)}, u32[]{:S(2)}) collective-permute-start(bf16[4,16,1024]{2,1,0:T(8,128)(2,1)S(1)} %fusion.2), channel_id=1, source_target_pairs={{0,8},{4,20},{8,0},{12,28},{16,24},{20,4},{24,16},{28,12},{1,9},{5... | collective-permute-start | bytes 393224 | tf_op jit(solution)/shard_map/ppermute | solution.py:261
  45.4 2.8 %collective-permute-done.13 = bf16[4,16,1024]{2,1,0:T(8,128)(2,1)S(1)} collective-permute-done((bf16[4,16,1024]{2,1,0:T(8,128)(2,1)S(1)}, bf16[4,16,1024]{2,1,0:T(8,128)(2,1)S(1)}, u32[]{:S(2)}, u32[]{:S(2)}) %collective-permute-start.13) | collective-permute-done | bytes 131104 | tf_op jit(solution)/shard_map/ppermute | solution.py:261
  48.2 1.4 %collective-permute-done.15 = bf16[4,16,1024]{2,1,0:T(8,128)(2,1)S(1)} collective-permute-done((bf16[4,16,1024]{2,1,0:T(8,128)(2,1)S(1)}, bf16[4,16,1024]{2,1,0:T(8,128)(2,1)S(1)}, u32[]{:S(2)}, u32[]{:S(2)}) %collective-permute-start.15) | collective-permute-done | bytes 131104 | tf_op jit(solution)/shard_map/ppermute | solution.py:261
  49.6 0.0 collective-permute-done.11
  49.6 0.2 fusion.3
  49.8 0.9 %collective-permute-start.16 = (bf16[16,2048]{1,0:T(8,128)(2,1)S(1)}, bf16[16,2048]{1,0:T(8,128)(2,1)S(1)}, u32[]{:S(2)}, u32[]{:S(2)}) collective-permute-start(bf16[16,2048]{1,0:T(8,128)(2,1)S(1)} %pad_maximum_fusion.2), channel_id=1, source_target_pairs={{0,3},{1,2},{2,1},{3,0},{4,7},{5,6},{6,5},{7,4},{8,11},{9,10},{10,... | collective-permute-start | bytes 196616 | tf_op jit(solution)/shard_map/ppermute | solution.py:264
  50.7 0.9 %collective-permute-start.17 = (bf16[16,2048]{1,0:T(8,128)(2,1)S(1)}, bf16[16,2048]{1,0:T(8,128)(2,1)S(1)}, u32[]{:S(2)}, u32[]{:S(2)}) collective-permute-start(bf16[16,2048]{1,0:T(8,128)(2,1)S(1)} %pad_maximum_fusion.3), channel_id=1, source_target_pairs={{0,2},{1,3},{2,0},{3,1},{4,6},{5,7},{6,4},{7,5},{8,10},{9,11},{10,... | collective-permute-start | bytes 196616 | tf_op jit(solution)/shard_map/ppermute | solution.py:264
  51.6 2.7 %collective-permute-start.18 = (bf16[16,2048]{1,0:T(8,128)(2,1)S(1)}, bf16[16,2048]{1,0:T(8,128)(2,1)S(1)}, u32[]{:S(2)}, u32[]{:S(2)}) collective-permute-start(bf16[16,2048]{1,0:T(8,128)(2,1)S(1)} %pad_maximum_fusion.4), channel_id=1, source_target_pairs={{0,1},{1,0},{2,3},{3,2},{4,5},{5,4},{6,7},{7,6},{8,9},{9,8},{10,11... | collective-permute-start | bytes 196616 | tf_op jit(solution)/shard_map/ppermute | solution.py:264
  54.3 0.8 %entropies.1 = (f32[1,128]{1,0:T(1,128)}, f32[1,1]{1,0:T(1,128)}) custom-call(f32[32,4,128]{2,1,0:T(4,128)S(1)} %all_to_all.5.stats_ref, bf16[16,128]{1,0:T(8,128)(2,1)S(1)} %get-tuple-element.27.refs_5_.picker_ref), custom_call_target="tpu_custom_call" | custom-call | tf_op jit(solution)/shard_map/entropies/pallas_call | solution.py:186
  55.1 1.6 %collective-permute-done.16 = bf16[16,2048]{1,0:T(8,128)(2,1)S(1)} collective-permute-done((bf16[16,2048]{1,0:T(8,128)(2,1)S(1)}, bf16[16,2048]{1,0:T(8,128)(2,1)S(1)}, u32[]{:S(2)}, u32[]{:S(2)}) %collective-permute-start.16) | collective-permute-done | bytes 65568 | tf_op jit(solution)/shard_map/ppermute | solution.py:264
  56.7 1.8 %collective-permute-done.17 = bf16[16,2048]{1,0:T(8,128)(2,1)S(1)} collective-permute-done((bf16[16,2048]{1,0:T(8,128)(2,1)S(1)}, bf16[16,2048]{1,0:T(8,128)(2,1)S(1)}, u32[]{:S(2)}, u32[]{:S(2)}) %collective-permute-start.17) | collective-permute-done | bytes 65568 | tf_op jit(solution)/shard_map/ppermute | solution.py:264
  58.5 0.0 collective-permute-done.18
  58.5 1.1 %convolution_convert_fusion = bf16[128,2048]{1,0:T(8,128)(2,1)} fusion(bf16[16,128]{1,0:T(8,128)(2,1)S(1)} %get-tuple-element.27.refs_5_.picker_ref, f32[16,1024]{1,0:T(8,128)S(1)} %get-tuple-element.51, f32[16,1024]{1,0:T(8,128)S(1)} %get-tuple-element.52, bf16[16,2048]{1,0:T(8,128)(2,1)S(1)} %collective-permute-done.18, ...), kind=kOutput, calls=%fused_computation | convolution fusion | flops 8912896 | bytes 856064 | tf_op jit(solution)/shard_map/dot_general | solution.py:318
  (20 shorter events, 0.3 us)
Async XLA Ops:
  0.6 19.2 %copy-start = (bf16[8192,256]{1,0:T(8,128)(2,1)S(1)}, bf16[8192,256]{1,0:T(8,128)(2,1)}, u32[]{:S(2)}) copy-start(bf16[8192,256]{1,0:T(8,128)(2,1)} %head_ref.1) | copy-start | bytes 12582916
  3.4 6.6 %collective-permute-start = (bf16[16,4096]{1,0:T(8,128)(2,1)S(1)}, bf16[16,4096]{1,0:T(8,128)(2,1)S(1)}, u32[]{:S(2)}, u32[]{:S(2)}) collective-permute-start(bf16[16,4096]{1,0:T(8,128)(2,1)S(1)} %get-tuple-element.23), channel_id=1, source_target_pairs={{0,8},{4,20},{8,0},{12,28},{16,24},{20,4},{24,16},{28,12},{1,9},{5... | collective-permute-start | bytes 393224 | tf_op jit(solution)/shard_map/ppermute | solution.py:261
  6.4 6.4 %collective-permute-start.2 = (bf16[16,4096]{1,0:T(8,128)(2,1)S(1)}, bf16[16,4096]{1,0:T(8,128)(2,1)S(1)}, u32[]{:S(2)}, u32[]{:S(2)}) collective-permute-start(bf16[16,4096]{1,0:T(8,128)(2,1)S(1)} %get-tuple-element.24), channel_id=1, source_target_pairs={{0,8},{4,20},{8,0},{12,28},{16,24},{20,4},{24,16},{28,12},{1,9},{5... | collective-permute-start | bytes 393224 | tf_op jit(solution)/shard_map/ppermute | solution.py:261
  6.5 8.8 %collective-permute-start.1 = (bf16[16,8192]{1,0:T(8,128)(2,1)S(1)}, bf16[16,8192]{1,0:T(8,128)(2,1)S(1)}, u32[]{:S(2)}, u32[]{:S(2)}) collective-permute-start(bf16[16,8192]{1,0:T(8,128)(2,1)S(1)} %pad_maximum_fusion), channel_id=1, source_target_pairs={{0,16},{4,12},{8,24},{12,4},{16,0},{20,28},{24,8},{28,20},{1,17},{... | collective-permute-start | bytes 786440 | tf_op jit(solution)/shard_map/ppermute | solution.py:261
  10.0 5.4 %collective-permute-start.3 = (bf16[16,4096]{1,0:T(8,128)(2,1)S(1)}, bf16[16,4096]{1,0:T(8,128)(2,1)S(1)}, u32[]{:S(2)}, u32[]{:S(2)}) collective-permute-start(bf16[16,4096]{1,0:T(8,128)(2,1)S(1)} %collective-permute-done), channel_id=1, source_target_pairs={{0,16},{4,12},{8,24},{12,4},{16,0},{20,28},{24,8},{28,20},{1,17},{... | collective-permute-start | bytes 393224 | tf_op jit(solution)/shard_map/ppermute | solution.py:261
  12.8 5.4 %collective-permute-start.5 = (bf16[16,4096]{1,0:T(8,128)(2,1)S(1)}, bf16[16,4096]{1,0:T(8,128)(2,1)S(1)}, u32[]{:S(2)}, u32[]{:S(2)}) collective-permute-start(bf16[16,4096]{1,0:T(8,128)(2,1)S(1)} %collective-permute-done.2), channel_id=1, source_target_pairs={{0,16},{4,12},{8,24},{12,4},{16,0},{20,28},{24,8},{28,20},{1,17},{... | collective-permute-start | bytes 393224 | tf_op jit(solution)/shard_map/ppermute | solution.py:261
  15.4 4.4 %collective-permute-start.4 = (bf16[96,4096]{1,0:T(8,128)(2,1)S(1)}, bf16[96,4096]{1,0:T(8,128)(2,1)S(1)}, u32[]{:S(2)}, u32[]{:S(2)}) collective-permute-start(bf16[96,4096]{1,0:T(8,128)(2,1)S(1)} %slice_dynamic-update-slice_fusion.refs_0_), channel_id=1, source_target_pairs={{0,4},{4,0},{8,12},{12,8},{16,20},{20,16},{24,28},{28,24},{1,5},{5... | collective-permute-start | bytes 2359304 | tf_op jit(solution)/shard_map/ppermute | solution.py:257
  18.2 1.6 %collective-permute-start.6 = (bf16[32,4096]{1,0:T(8,128)(2,1)S(1)}, bf16[32,4096]{1,0:T(8,128)(2,1)S(1)}, u32[]{:S(2)}, u32[]{:S(2)}) collective-permute-start(bf16[32,4096]{1,0:T(8,128)(2,1)S(1)} %constant_dynamic-update-slice_fusion.4.refs_2_), channel_id=1, source_target_pairs={{0,4},{4,0},{8,12},{12,8},{16,20},{20,16},{24,28},{28,24},{1,5},{5... | collective-permute-start | bytes 786440 | tf_op jit(solution)/shard_map/ppermute | solution.py:257
  36.1 1.4 %collective-permute-start.7 = (bf16[4,16,1024]{2,1,0:T(8,128)(2,1)S(1)}, bf16[4,16,1024]{2,1,0:T(8,128)(2,1)S(1)}, u32[]{:S(2)}, u32[]{:S(2)}) collective-permute-start(bf16[4,16,1024]{2,1,0:T(8,128)(2,1)S(1)} %get-tuple-element.33), channel_id=1, source_target_pairs={{0,4},{4,0},{8,12},{12,8},{16,20},{20,16},{24,28},{28,24},{1,5},{5... | collective-permute-start | bytes 393224 | tf_op jit(solution)/shard_map/ppermute | solution.py:257
  36.2 1.5 %collective-permute-start.8 = (bf16[4,16,1024]{2,1,0:T(8,128)(2,1)S(1)}, bf16[4,16,1024]{2,1,0:T(8,128)(2,1)S(1)}, u32[]{:S(2)}, u32[]{:S(2)}) collective-permute-start(bf16[4,16,1024]{2,1,0:T(8,128)(2,1)S(1)} %get-tuple-element.34), channel_id=1, source_target_pairs={{0,4},{4,0},{8,12},{12,8},{16,20},{20,16},{24,28},{28,24},{1,5},{5... | collective-permute-start | bytes 393224 | tf_op jit(solution)/shard_map/ppermute | solution.py:257
  37.7 2.6 %collective-permute-start.9 = (bf16[3,4,16,1024]{3,2,1,0:T(8,128)(2,1)S(1)}, bf16[3,4,16,1024]{3,2,1,0:T(8,128)(2,1)S(1)}, u32[]{:S(2)}, u32[]{:S(2)}) collective-permute-start(bf16[3,4,16,1024]{3,2,1,0:T(8,128)(2,1)S(1)} %get-tuple-element.35), channel_id=1, source_target_pairs={{0,4},{4,0},{8,12},{12,8},{16,20},{20,16},{24,28},{28,24},{1,5},{5... | collective-permute-start | bytes 1179656 | tf_op jit(solution)/shard_map/ppermute | solution.py:257
  38.1 5.0 %collective-permute-start.12 = (bf16[4,16,1024]{2,1,0:T(8,128)(2,1)S(1)}, bf16[4,16,1024]{2,1,0:T(8,128)(2,1)S(1)}, u32[]{:S(2)}, u32[]{:S(2)}) collective-permute-start(bf16[4,16,1024]{2,1,0:T(8,128)(2,1)S(1)} %fusion.1), channel_id=1, source_target_pairs={{0,16},{4,12},{8,24},{12,4},{16,0},{20,28},{24,8},{28,20},{1,17},{... | collective-permute-start | bytes 393224 | tf_op jit(solution)/shard_map/ppermute | solution.py:261
  38.8 1.7 %collective-permute-start.10 = (bf16[3,4,16,1024]{3,2,1,0:T(8,128)(2,1)S(1)}, bf16[3,4,16,1024]{3,2,1,0:T(8,128)(2,1)S(1)}, u32[]{:S(2)}, u32[]{:S(2)}) collective-permute-start(bf16[3,4,16,1024]{3,2,1,0:T(8,128)(2,1)S(1)} %get-tuple-element.37), channel_id=1, source_target_pairs={{0,4},{4,0},{8,12},{12,8},{16,20},{20,16},{24,28},{28,24},{1,5},{5... | collective-permute-start | bytes 1179656 | tf_op jit(solution)/shard_map/ppermute | solution.py:257
  38.8 5.7 %collective-permute-start.14 = (bf16[4,16,1024]{2,1,0:T(8,128)(2,1)S(1)}, bf16[4,16,1024]{2,1,0:T(8,128)(2,1)S(1)}, u32[]{:S(2)}, u32[]{:S(2)}) collective-permute-start(bf16[4,16,1024]{2,1,0:T(8,128)(2,1)S(1)} %fusion), channel_id=1, source_target_pairs={{0,16},{4,12},{8,24},{12,4},{16,0},{20,28},{24,8},{28,20},{1,17},{... | collective-permute-start | bytes 393224 | tf_op jit(solution)/shard_map/ppermute | solution.py:261
  40.6 9.0 %collective-permute-start.11 = (bf16[4,16,2048]{2,1,0:T(8,128)(2,1)S(1)}, bf16[4,16,2048]{2,1,0:T(8,128)(2,1)S(1)}, u32[]{:S(2)}, u32[]{:S(2)}) collective-permute-start(bf16[4,16,2048]{2,1,0:T(8,128)(2,1)S(1)} %pad_maximum_fusion.1), channel_id=1, source_target_pairs={{0,16},{4,12},{8,24},{12,4},{16,0},{20,28},{24,8},{28,20},{1,17},{... | collective-permute-start | bytes 786440 | tf_op jit(solution)/shard_map/ppermute | solution.py:261
  43.2 5.0 %collective-permute-start.13 = (bf16[4,16,1024]{2,1,0:T(8,128)(2,1)S(1)}, bf16[4,16,1024]{2,1,0:T(8,128)(2,1)S(1)}, u32[]{:S(2)}, u32[]{:S(2)}) collective-permute-start(bf16[4,16,1024]{2,1,0:T(8,128)(2,1)S(1)} %fusion.4), channel_id=1, source_target_pairs={{0,8},{4,20},{8,0},{12,28},{16,24},{20,4},{24,16},{28,12},{1,9},{5... | collective-permute-start | bytes 393224 | tf_op jit(solution)/shard_map/ppermute | solution.py:261
  44.6 5.0 %collective-permute-start.15 = (bf16[4,16,1024]{2,1,0:T(8,128)(2,1)S(1)}, bf16[4,16,1024]{2,1,0:T(8,128)(2,1)S(1)}, u32[]{:S(2)}, u32[]{:S(2)}) collective-permute-start(bf16[4,16,1024]{2,1,0:T(8,128)(2,1)S(1)} %fusion.2), channel_id=1, source_target_pairs={{0,8},{4,20},{8,0},{12,28},{16,24},{20,4},{24,16},{28,12},{1,9},{5... | collective-permute-start | bytes 393224 | tf_op jit(solution)/shard_map/ppermute | solution.py:261
  49.8 6.9 %collective-permute-start.16 = (bf16[16,2048]{1,0:T(8,128)(2,1)S(1)}, bf16[16,2048]{1,0:T(8,128)(2,1)S(1)}, u32[]{:S(2)}, u32[]{:S(2)}) collective-permute-start(bf16[16,2048]{1,0:T(8,128)(2,1)S(1)} %pad_maximum_fusion.2), channel_id=1, source_target_pairs={{0,3},{1,2},{2,1},{3,0},{4,7},{5,6},{6,5},{7,4},{8,11},{9,10},{10,... | collective-permute-start | bytes 196616 | tf_op jit(solution)/shard_map/ppermute | solution.py:264
  50.7 7.8 %collective-permute-start.17 = (bf16[16,2048]{1,0:T(8,128)(2,1)S(1)}, bf16[16,2048]{1,0:T(8,128)(2,1)S(1)}, u32[]{:S(2)}, u32[]{:S(2)}) collective-permute-start(bf16[16,2048]{1,0:T(8,128)(2,1)S(1)} %pad_maximum_fusion.3), channel_id=1, source_target_pairs={{0,2},{1,3},{2,0},{3,1},{4,6},{5,7},{6,4},{7,5},{8,10},{9,11},{10,... | collective-permute-start | bytes 196616 | tf_op jit(solution)/shard_map/ppermute | solution.py:264
  51.6 6.9 %collective-permute-start.18 = (bf16[16,2048]{1,0:T(8,128)(2,1)S(1)}, bf16[16,2048]{1,0:T(8,128)(2,1)S(1)}, u32[]{:S(2)}, u32[]{:S(2)}) collective-permute-start(bf16[16,2048]{1,0:T(8,128)(2,1)S(1)} %pad_maximum_fusion.4), channel_id=1, source_target_pairs={{0,1},{1,0},{2,3},{3,2},{4,5},{5,4},{6,7},{7,6},{8,9},{9,8},{10,11... | collective-permute-start | bytes 196616 | tf_op jit(solution)/shard_map/ppermute | solution.py:264

commit v12 on v11

--- a/solution.py
+++ b/solution.py
@@ -33,9 +33,10 @@
 
 
 def row_order(n_seq):
-    last = n_seq // 2 - 1
-    early = [(core, chip) for core in (0, 1) for chip in range(last)]
-    return early + [(0, last), (1, last)]
+    n_chip = n_seq // 2
+    cut = n_chip // 2
+    groups = [(core, range(low, low + cut)) for low in (0, cut) for core in (0, 1)]
+    return [(core, chip) for core, chips in groups for chip in chips]
 
 
 def owner_of(n_seq, core, chip):
@@ -208,8 +209,7 @@
     logits = logits_ref[...]
     prob = jnp.exp(logits - ordered[:, 0:1]) * ordered[:, 1:2]
     score = (prob * (ordered[:, 2:3] - logits)).astype(BF16)
-    n_chip = n_seq // 2
-    last = n_chip - 1
+    cut = n_seq // 4
     size = near_refs[0].shape[3]
     for v in range(n_vocab):
         for c in range(PARTS):
@@ -221,10 +221,11 @@
                 preferred_element_type=F32,
             ).astype(BF16)
             blocks = part.reshape(n_seq, ACT_DEV, size)
-            near_refs[c][:last, v] = blocks[:last]
-            far_refs[c][:, v] = blocks[last : 2 * last]
-            near_refs[c][last, v] = blocks[2 * last]
-            last_refs[c][v] = blocks[2 * last + 1]
+            near_refs[c][:cut, v] = blocks[:cut]
+            far_refs[c][:cut, v] = blocks[cut : 2 * cut]
+            near_refs[c][cut:, v] = blocks[2 * cut : 3 * cut]
+            far_refs[c][cut:, v] = blocks[3 * cut : 4 * cut - 1]
+            last_refs[c][v] = blocks[4 * cut - 1]
 
 
 def gradients(n_seq, n_vocab, stats, logits, head):
@@ -270,13 +271,15 @@
         step = a.bit_length() - 1
         source = near[a ^ (1 << step)]
         if a > 1 and a == 1 << step:
-            moved = swap_chip(jnp.concatenate(source, axis=1), step)
-            near.append(jnp.split(moved, PARTS, axis=1))
-        else:
-            near.append([swap_chip(part, step) for part in source])
-    early = jnp.concatenate([near[a][c] for c in range(PARTS) for a in range(last)], axis=0)
-    early, near[last][0] = lax.optimization_barrier((early, near[last][0]))
-    late = jnp.concatenate(near[last], axis=0)
+            whole = lax.optimization_barrier(jnp.concatenate(source, axis=1))
+            source = jnp.split(whole, PARTS, axis=1)
+        near.append([swap_chip(part, step) for part in source])
+
+    def gather_rows(chips):
+        return jnp.concatenate([near[a][c] for c in range(PARTS) for a in chips], axis=0)
+
+    cut = n_chip // 2
+    early, late = gather_rows(range(cut)), gather_rows(range(cut, n_chip))
     blocks = [early, swap_core(early), late, swap_core(late)]
 
     logits, stats = local_logits(n_seq, n_vocab, blocks, head, picker)

time: 59.8 us -> 61.7 us (1.032)
  waiting for transfers between devices: 16.7 us -> 21.4 us
  starting transfers between devices: 20.7 us -> 18.4 us
  blocking collectives: 13.7 us -> 13 us
    ppermute x10 -> x11, waiting for transfers between devices: 10.5 us -> 14.9 us  [swap_chip(): lax.ppermute(value, 'seq', [(i, i ^ flips[i & 1]) for i in range(n_seq)])]
    ppermute x10 -> x11, starting transfers between devices: 15.2 us -> 12.9 us  [swap_chip(): lax.ppermute(value, 'seq', [(i, i ^ flips[i & 1]) for i in range(n_seq)])]
  transfers between devices with their start and end apart: 19 -> 20, of which waited for: 13 -> 14; matrix products, arithmetic and copies ran while one was open for 1% -> 1% of each run, Pallas kernels for 1% -> 1%
where the time goes in v12:
time: 61.7 us; the launch traced here: 61.5 us
  waiting for transfers between devices  21.4 us (35%)
  starting transfers between devices  18.4 us (30%)
  blocking collectives  13 us (21%)
  Pallas kernels  6.12 us (10%)
  matrix products  1.11 us (2%)
  between operations  0.82 us (1%)
    ppermute x11, waiting for transfers between devices, swap_chip(): lax.ppermute(value, 'seq', [(i, i ^ flips[i & 1]) for i in range(n_seq)])  14.9 us
    all_to_all x1, blocking collectives, body(): stats = lax.all_to_all(stats, ('seq', 'vocab'), 0, 0, tiled=True)  13 us
    ppermute x11, starting transfers between devices, swap_chip(): lax.ppermute(value, 'seq', [(i, i ^ flips[i & 1]) for i in range(n_seq)])  12.9 us
    ppermute x3, starting transfers between devices, send_vocab(): return lax.ppermute(value, 'vocab', [(i, i ^ k) for i in range(n_vocab)])  4.45 us
    ppermute x3, waiting for transfers between devices, send_vocab(): return lax.ppermute(value, 'vocab', [(i, i ^ k) for i in range(n_vocab)])  3.43 us
    ppermute x6, waiting for transfers between devices, swap_core(): return lax.ppermute(value, 'seq', [(i, i ^ 1) for i in range(n_seq)])  3.14 us
    pallas_call x1, Pallas kernels, select(): pl.pallas_call(select_kernel, in_specs=[pl.BlockSpec(memory_space=pltpu.H...  2.75 us
    pallas_call x1, Pallas kernels, gradients(): pl.pallas_call(functools.partial(gradient_kernel, n_seq, n_vocab), in_spe...  1.64 us
  transfers between devices with their start and end apart: 20, of which 14 were waited for; matrix products, arithmetic and copies ran while one was open for 1% of the time, Pallas kernels for 1%

profile of v12, /device:TPU:0, one launch (start us, length us, event | category | flops | bytes accessed | tf_op | source)
XLA Modules:
  0.0 61.5 jit_solution(2805340486990046934)
XLA Ops:
  0.6 2.8 %select_rows.1 = (bf16[16,4096]{1,0:T(8,128)(2,1)S(1)}, bf16[16,4096]{1,0:T(8,128)(2,1)S(1)}, bf16[16,128]{1,0:T(8,128)(2,1)S(1)}) custom-call(s32[1,128]{1,0:T(1,128)} %bitcast.46, bf16[128,8192]{1,0:T(8,128)(2,1)} %hidden_ref.1), custom_call_target="tpu_custom_call" | custom-call | tf_op jit(solution)/shard_map/select_rows/pallas_call | solution.py:92
  3.4 3.0 %collective-permute-start = (bf16[16,4096]{1,0:T(8,128)(2,1)S(1)}, bf16[16,4096]{1,0:T(8,128)(2,1)S(1)}, u32[]{:S(2)}, u32[]{:S(2)}) collective-permute-start(bf16[16,4096]{1,0:T(8,128)(2,1)S(1)} %get-tuple-element.21), channel_id=1, source_target_pairs={{0,8},{4,20},{8,0},{12,28},{16,24},{20,4},{24,16},{28,12},{1,9},{5... | collective-permute-start | bytes 393224 | tf_op jit(solution)/shard_map/ppermute | solution.py:262
  6.4 0.1 collective-permute-start.1
  6.5 2.0 %collective-permute-start.3 = (bf16[16,4096]{1,0:T(8,128)(2,1)S(1)}, bf16[16,4096]{1,0:T(8,128)(2,1)S(1)}, u32[]{:S(2)}, u32[]{:S(2)}) collective-permute-start(bf16[16,4096]{1,0:T(8,128)(2,1)S(1)} %get-tuple-element.48), channel_id=1, source_target_pairs={{0,16},{4,12},{8,24},{12,4},{16,0},{20,28},{24,8},{28,20},{1,17},{... | collective-permute-start | bytes 393224 | tf_op jit(solution)/shard_map/ppermute | solution.py:262
  8.6 0.1 collective-permute-start.5
  8.7 1.3 %collective-permute-done = bf16[16,4096]{1,0:T(8,128)(2,1)S(1)} collective-permute-done((bf16[16,4096]{1,0:T(8,128)(2,1)S(1)}, bf16[16,4096]{1,0:T(8,128)(2,1)S(1)}, u32[]{:S(2)}, u32[]{:S(2)}) %collective-permute-start) | collective-permute-done | bytes 131104 | tf_op jit(solution)/shard_map/ppermute | solution.py:262
  10.0 2.8 %collective-permute-done.1 = bf16[16,4096]{1,0:T(8,128)(2,1)S(1)} collective-permute-done((bf16[16,4096]{1,0:T(8,128)(2,1)S(1)}, bf16[16,4096]{1,0:T(8,128)(2,1)S(1)}, u32[]{:S(2)}, u32[]{:S(2)}) %collective-permute-start.1) | collective-permute-done | bytes 131104 | tf_op jit(solution)/shard_map/ppermute | solution.py:262
  12.8 0.1 collective-permute-start.2
  12.9 2.5 %collective-permute-start.4 = (bf16[16,4096]{1,0:T(8,128)(2,1)S(1)}, bf16[16,4096]{1,0:T(8,128)(2,1)S(1)}, u32[]{:S(2)}, u32[]{:S(2)}) collective-permute-start(bf16[16,4096]{1,0:T(8,128)(2,1)S(1)} %collective-permute-done), channel_id=1, source_target_pairs={{0,16},{4,12},{8,24},{12,4},{16,0},{20,28},{24,8},{28,20},{1,17},{... | collective-permute-start | bytes 393224 | tf_op jit(solution)/shard_map/ppermute | solution.py:262
  15.4 0.1 collective-permute-start.6
  15.5 0.0 collective-permute-done.3
  15.5 2.9 %collective-permute-done.4 = bf16[16,4096]{1,0:T(8,128)(2,1)S(1)} collective-permute-done((bf16[16,4096]{1,0:T(8,128)(2,1)S(1)}, bf16[16,4096]{1,0:T(8,128)(2,1)S(1)}, u32[]{:S(2)}, u32[]{:S(2)}) %collective-permute-start.4) | collective-permute-done | bytes 131104 | tf_op jit(solution)/shard_map/ppermute | solution.py:262
  18.4 0.0 collective-permute-done.5
  18.4 2.0 %collective-permute-done.6 = bf16[16,4096]{1,0:T(8,128)(2,1)S(1)} collective-permute-done((bf16[16,4096]{1,0:T(8,128)(2,1)S(1)}, bf16[16,4096]{1,0:T(8,128)(2,1)S(1)}, u32[]{:S(2)}, u32[]{:S(2)}) %collective-permute-start.6) | collective-permute-done | bytes 131104 | tf_op jit(solution)/shard_map/ppermute | solution.py:262
  20.4 0.1 collective-permute-start.7
  20.5 0.0 collective-permute-done.2.refs_1_
  20.5 1.9 %collective-permute-done.7.refs_3_ = bf16[64,4096]{1,0:T(8,128)(2,1)S(1)} collective-permute-done((bf16[64,4096]{1,0:T(8,128)(2,1)S(1)}, bf16[64,4096]{1,0:T(8,128)(2,1)S(1)}, u32[]{:S(2)}, u32[]{:S(2)}) %collective-permute-start.7) | collective-permute-done | bytes 524320 | tf_op jit(solution)/shard_map/ppermute | solution.py:258
  22.4 1.0 %local_logits.1 = (f32[128,256]{1,0:T(8,128)S(1)}, f32[32,4,128]{2,1,0:T(4,128)S(1)}) custom-call(bf16[64,4096]{1,0:T(8,128)(2,1)S(1)} %constant_dynamic-update-slice_fusion.refs_0_, bf16[64,4096]{1,0:T(8,128)(2,1)S(1)} %collective-permute-done.2.refs_1_, bf16[64,4096]{1,0:T(8,128)(2,1)S(1)} %constant_dynamic-update-slice_fusion.4.refs_2_, ...), custom_call_target="tpu_custom_call" | custom-call | tf_op jit(solution)/shard_map/local_logits/pallas_call | solution.py:147
  23.3 13.0 %all_to_all.5.stats_ref = f32[32,4,128]{2,1,0:T(4,128)S(1)} all-to-all(f32[32,4,128]{2,1,0:T(4,128)S(1)} %get-tuple-element.24), channel_id=1, replica_groups=mesh['seq'=8,'vocab'=4] {'seq','vocab'}, dimensions={0} | all-to-all | bytes 131072 | tf_op jit(solution)/shard_map/all_to_all | solution.py:286
  36.4 1.6 %gradients.1 = (bf16[4,4,16,1024]{3,2,1,0:T(8,128)(2,1)S(1)}, bf16[4,4,16,1024]{3,2,1,0:T(8,128)(2,1)S(1)}, bf16[3,4,16,1024]{3,2,1,0:T(8,128)(2,1)S(1)}, bf16[3...) custom-call(f32[32,4,128]{2,1,0:T(4,128)S(1)} %all_to_all.5.stats_ref, ...), custom_call_target="tpu_custom_call" | custom-call | tf_op jit(solution)/shard_map/gradients/pallas_call | solution.py:238
  38.0 0.1 collective-permute-start.8
  38.1 0.5 collective-permute-start.9
  38.6 0.8 %collective-permute-done.8 = bf16[4,16,1024]{2,1,0:T(8,128)(2,1)S(1)} collective-permute-done((bf16[4,16,1024]{2,1,0:T(8,128)(2,1)S(1)}, bf16[4,16,1024]{2,1,0:T(8,128)(2,1)S(1)}, u32[]{:S(2)}, u32[]{:S(2)}) %collective-permute-start.8) | collective-permute-done | bytes 131104 | tf_op jit(solution)/shard_map/ppermute | solution.py:258
  39.4 0.2 collective-permute-done.9
  39.6 0.3 collective-permute-start.10
  40.0 0.7 %collective-permute-start.13 = (bf16[4,16,1024]{2,1,0:T(8,128)(2,1)S(1)}, bf16[4,16,1024]{2,1,0:T(8,128)(2,1)S(1)}, u32[]{:S(2)}, u32[]{:S(2)}) collective-permute-start(bf16[4,16,1024]{2,1,0:T(8,128)(2,1)S(1)} %fusion.1), channel_id=1, source_target_pairs={{0,16},{4,12},{8,24},{12,4},{16,0},{20,28},{24,8},{28,20},{1,17},{... | collective-permute-start | bytes 393224 | tf_op jit(solution)/shard_map/ppermute | solution.py:262
  40.7 0.0 collective-permute-start.11
  40.8 1.4 %collective-permute-start.15 = (bf16[4,16,1024]{2,1,0:T(8,128)(2,1)S(1)}, bf16[4,16,1024]{2,1,0:T(8,128)(2,1)S(1)}, u32[]{:S(2)}, u32[]{:S(2)}) collective-permute-start(bf16[4,16,1024]{2,1,0:T(8,128)(2,1)S(1)} %fusion), channel_id=1, source_target_pairs={{0,16},{4,12},{8,24},{12,4},{16,0},{20,28},{24,8},{28,20},{1,17},{... | collective-permute-start | bytes 393224 | tf_op jit(solution)/shard_map/ppermute | solution.py:262
  42.2 0.0 collective-permute-done.10
  42.2 0.2 collective-permute-done.11
  42.5 1.4 %collective-permute-start.12 = (bf16[4,16,2048]{2,1,0:T(8,128)(2,1)S(1)}, bf16[4,16,2048]{2,1,0:T(8,128)(2,1)S(1)}, u32[]{:S(2)}, u32[]{:S(2)}) collective-permute-start(bf16[4,16,2048]{2,1,0:T(8,128)(2,1)S(1)} %pad_maximum_fusion.1), channel_id=1, source_target_pairs={{0,16},{4,12},{8,24},{12,4},{16,0},{20,28},{24,8},{28,20},{1,17},{... | collective-permute-start | bytes 786440 | tf_op jit(solution)/shard_map/ppermute | solution.py:262
  43.9 1.1 %collective-permute-done.13 = bf16[4,16,1024]{2,1,0:T(8,128)(2,1)S(1)} collective-permute-done((bf16[4,16,1024]{2,1,0:T(8,128)(2,1)S(1)}, bf16[4,16,1024]{2,1,0:T(8,128)(2,1)S(1)}, u32[]{:S(2)}, u32[]{:S(2)}) %collective-permute-start.13) | collective-permute-done | bytes 131104 | tf_op jit(solution)/shard_map/ppermute | solution.py:262
  45.0 0.1 fusion.4
  45.1 0.7 %collective-permute-start.14 = (bf16[4,16,1024]{2,1,0:T(8,128)(2,1)S(1)}, bf16[4,16,1024]{2,1,0:T(8,128)(2,1)S(1)}, u32[]{:S(2)}, u32[]{:S(2)}) collective-permute-start(bf16[4,16,1024]{2,1,0:T(8,128)(2,1)S(1)} %fusion.4), channel_id=1, source_target_pairs={{0,8},{4,20},{8,0},{12,28},{16,24},{20,4},{24,16},{28,12},{1,9},{5... | collective-permute-start | bytes 393224 | tf_op jit(solution)/shard_map/ppermute | solution.py:262
  45.8 0.6 %collective-permute-done.15 = bf16[4,16,1024]{2,1,0:T(8,128)(2,1)S(1)} collective-permute-done((bf16[4,16,1024]{2,1,0:T(8,128)(2,1)S(1)}, bf16[4,16,1024]{2,1,0:T(8,128)(2,1)S(1)}, u32[]{:S(2)}, u32[]{:S(2)}) %collective-permute-start.15) | collective-permute-done | bytes 131104 | tf_op jit(solution)/shard_map/ppermute | solution.py:262
  46.4 0.1 fusion.2
  46.5 0.8 %collective-permute-start.16 = (bf16[4,16,1024]{2,1,0:T(8,128)(2,1)S(1)}, bf16[4,16,1024]{2,1,0:T(8,128)(2,1)S(1)}, u32[]{:S(2)}, u32[]{:S(2)}) collective-permute-start(bf16[4,16,1024]{2,1,0:T(8,128)(2,1)S(1)} %fusion.2), channel_id=1, source_target_pairs={{0,8},{4,20},{8,0},{12,28},{16,24},{20,4},{24,16},{28,12},{1,9},{5... | collective-permute-start | bytes 393224 | tf_op jit(solution)/shard_map/ppermute | solution.py:262
  47.3 2.8 %collective-permute-done.14 = bf16[4,16,1024]{2,1,0:T(8,128)(2,1)S(1)} collective-permute-done((bf16[4,16,1024]{2,1,0:T(8,128)(2,1)S(1)}, bf16[4,16,1024]{2,1,0:T(8,128)(2,1)S(1)}, u32[]{:S(2)}, u32[]{:S(2)}) %collective-permute-start.14) | collective-permute-done | bytes 131104 | tf_op jit(solution)/shard_map/ppermute | solution.py:262
  50.1 1.4 %collective-permute-done.16 = bf16[4,16,1024]{2,1,0:T(8,128)(2,1)S(1)} collective-permute-done((bf16[4,16,1024]{2,1,0:T(8,128)(2,1)S(1)}, bf16[4,16,1024]{2,1,0:T(8,128)(2,1)S(1)}, u32[]{:S(2)}, u32[]{:S(2)}) %collective-permute-start.16) | collective-permute-done | bytes 131104 | tf_op jit(solution)/shard_map/ppermute | solution.py:262
  51.5 0.2 fusion.3
  51.7 0.9 %collective-permute-start.17 = (bf16[16,2048]{1,0:T(8,128)(2,1)S(1)}, bf16[16,2048]{1,0:T(8,128)(2,1)S(1)}, u32[]{:S(2)}, u32[]{:S(2)}) collective-permute-start(bf16[16,2048]{1,0:T(8,128)(2,1)S(1)} %pad_maximum_fusion.2), channel_id=1, source_target_pairs={{0,3},{1,2},{2,1},{3,0},{4,7},{5,6},{6,5},{7,4},{8,11},{9,10},{10,... | collective-permute-start | bytes 196616 | tf_op jit(solution)/shard_map/ppermute | solution.py:265
  52.6 0.9 %collective-permute-start.18 = (bf16[16,2048]{1,0:T(8,128)(2,1)S(1)}, bf16[16,2048]{1,0:T(8,128)(2,1)S(1)}, u32[]{:S(2)}, u32[]{:S(2)}) collective-permute-start(bf16[16,2048]{1,0:T(8,128)(2,1)S(1)} %pad_maximum_fusion.3), channel_id=1, source_target_pairs={{0,2},{1,3},{2,0},{3,1},{4,6},{5,7},{6,4},{7,5},{8,10},{9,11},{10,... | collective-permute-start | bytes 196616 | tf_op jit(solution)/shard_map/ppermute | solution.py:265
  53.5 2.7 %collective-permute-start.19 = (bf16[16,2048]{1,0:T(8,128)(2,1)S(1)}, bf16[16,2048]{1,0:T(8,128)(2,1)S(1)}, u32[]{:S(2)}, u32[]{:S(2)}) collective-permute-start(bf16[16,2048]{1,0:T(8,128)(2,1)S(1)} %pad_maximum_fusion.4), channel_id=1, source_target_pairs={{0,1},{1,0},{2,3},{3,2},{4,5},{5,4},{6,7},{7,6},{8,9},{9,8},{10,11... | collective-permute-start | bytes 196616 | tf_op jit(solution)/shard_map/ppermute | solution.py:265
  56.2 0.8 %entropies.1 = (f32[1,128]{1,0:T(1,128)}, f32[1,1]{1,0:T(1,128)}) custom-call(f32[32,4,128]{2,1,0:T(4,128)S(1)} %all_to_all.5.stats_ref, bf16[16,128]{1,0:T(8,128)(2,1)S(1)} %get-tuple-element.23.refs_5_.picker_ref), custom_call_target="tpu_custom_call" | custom-call | tf_op jit(solution)/shard_map/entropies/pallas_call | solution.py:187
  57.0 1.6 %collective-permute-done.17 = bf16[16,2048]{1,0:T(8,128)(2,1)S(1)} collective-permute-done((bf16[16,2048]{1,0:T(8,128)(2,1)S(1)}, bf16[16,2048]{1,0:T(8,128)(2,1)S(1)}, u32[]{:S(2)}, u32[]{:S(2)}) %collective-permute-start.17) | collective-permute-done | bytes 65568 | tf_op jit(solution)/shard_map/ppermute | solution.py:265
  58.6 1.8 %collective-permute-done.18 = bf16[16,2048]{1,0:T(8,128)(2,1)S(1)} collective-permute-done((bf16[16,2048]{1,0:T(8,128)(2,1)S(1)}, bf16[16,2048]{1,0:T(8,128)(2,1)S(1)}, u32[]{:S(2)}, u32[]{:S(2)}) %collective-permute-start.18) | collective-permute-done | bytes 65568 | tf_op jit(solution)/shard_map/ppermute | solution.py:265
  60.4 0.0 collective-permute-done.19
  60.4 1.1 %convolution_convert_fusion = bf16[128,2048]{1,0:T(8,128)(2,1)} fusion(bf16[16,128]{1,0:T(8,128)(2,1)S(1)} %get-tuple-element.23.refs_5_.picker_ref, f32[16,1024]{1,0:T(8,128)S(1)} %get-tuple-element.49, f32[16,1024]{1,0:T(8,128)S(1)} %get-tuple-element.50, bf16[16,2048]{1,0:T(8,128)(2,1)S(1)} %collective-permute-done.19, ...), kind=kOutput, calls=%fused_computation | convolution fusion | flops 8912896 | bytes 856064 | tf_op jit(solution)/shard_map/dot_general | solution.py:321
  (23 shorter events, 0.3 us)
Async XLA Ops:
  0.6 21.7 %copy-start = (bf16[8192,256]{1,0:T(8,128)(2,1)S(1)}, bf16[8192,256]{1,0:T(8,128)(2,1)}, u32[]{:S(2)}) copy-start(bf16[8192,256]{1,0:T(8,128)(2,1)} %head_ref.1) | copy-start | bytes 12582916
  3.4 6.6 %collective-permute-start = (bf16[16,4096]{1,0:T(8,128)(2,1)S(1)}, bf16[16,4096]{1,0:T(8,128)(2,1)S(1)}, u32[]{:S(2)}, u32[]{:S(2)}) collective-permute-start(bf16[16,4096]{1,0:T(8,128)(2,1)S(1)} %get-tuple-element.21), channel_id=1, source_target_pairs={{0,8},{4,20},{8,0},{12,28},{16,24},{20,4},{24,16},{28,12},{1,9},{5... | collective-permute-start | bytes 393224 | tf_op jit(solution)/shard_map/ppermute | solution.py:262
  6.4 6.4 %collective-permute-start.1 = (bf16[16,4096]{1,0:T(8,128)(2,1)S(1)}, bf16[16,4096]{1,0:T(8,128)(2,1)S(1)}, u32[]{:S(2)}, u32[]{:S(2)}) collective-permute-start(bf16[16,4096]{1,0:T(8,128)(2,1)S(1)} %get-tuple-element.22), channel_id=1, source_target_pairs={{0,8},{4,20},{8,0},{12,28},{16,24},{20,4},{24,16},{28,12},{1,9},{5... | collective-permute-start | bytes 393224 | tf_op jit(solution)/shard_map/ppermute | solution.py:262
  6.5 9.0 %collective-permute-start.3 = (bf16[16,4096]{1,0:T(8,128)(2,1)S(1)}, bf16[16,4096]{1,0:T(8,128)(2,1)S(1)}, u32[]{:S(2)}, u32[]{:S(2)}) collective-permute-start(bf16[16,4096]{1,0:T(8,128)(2,1)S(1)} %get-tuple-element.48), channel_id=1, source_target_pairs={{0,16},{4,12},{8,24},{12,4},{16,0},{20,28},{24,8},{28,20},{1,17},{... | collective-permute-start | bytes 393224 | tf_op jit(solution)/shard_map/ppermute | solution.py:262
  8.6 9.8 %collective-permute-start.5 = (bf16[16,4096]{1,0:T(8,128)(2,1)S(1)}, bf16[16,4096]{1,0:T(8,128)(2,1)S(1)}, u32[]{:S(2)}, u32[]{:S(2)}) collective-permute-start(bf16[16,4096]{1,0:T(8,128)(2,1)S(1)} %get-tuple-element.47), channel_id=1, source_target_pairs={{0,16},{4,12},{8,24},{12,4},{16,0},{20,28},{24,8},{28,20},{1,17},{... | collective-permute-start | bytes 393224 | tf_op jit(solution)/shard_map/ppermute | solution.py:262
  12.8 7.7 %collective-permute-start.2 = (bf16[64,4096]{1,0:T(8,128)(2,1)S(1)}, bf16[64,4096]{1,0:T(8,128)(2,1)S(1)}, u32[]{:S(2)}, u32[]{:S(2)}) collective-permute-start(bf16[64,4096]{1,0:T(8,128)(2,1)S(1)} %constant_dynamic-update-slice_fusion.refs_0_), channel_id=1, source_target_pairs={{0,4},{4,0},{8,12},{12,8},{16,20},{20,16},{24,28},{28,24},{1,5},{5... | collective-permute-start | bytes 1572872 | tf_op jit(solution)/shard_map/ppermute | solution.py:258
  12.9 5.5 %collective-permute-start.4 = (bf16[16,4096]{1,0:T(8,128)(2,1)S(1)}, bf16[16,4096]{1,0:T(8,128)(2,1)S(1)}, u32[]{:S(2)}, u32[]{:S(2)}) collective-permute-start(bf16[16,4096]{1,0:T(8,128)(2,1)S(1)} %collective-permute-done), channel_id=1, source_target_pairs={{0,16},{4,12},{8,24},{12,4},{16,0},{20,28},{24,8},{28,20},{1,17},{... | collective-permute-start | bytes 393224 | tf_op jit(solution)/shard_map/ppermute | solution.py:262
  15.4 5.0 %collective-permute-start.6 = (bf16[16,4096]{1,0:T(8,128)(2,1)S(1)}, bf16[16,4096]{1,0:T(8,128)(2,1)S(1)}, u32[]{:S(2)}, u32[]{:S(2)}) collective-permute-start(bf16[16,4096]{1,0:T(8,128)(2,1)S(1)} %collective-permute-done.1), channel_id=1, source_target_pairs={{0,16},{4,12},{8,24},{12,4},{16,0},{20,28},{24,8},{28,20},{1,17},{... | collective-permute-start | bytes 393224 | tf_op jit(solution)/shard_map/ppermute | solution.py:262
  20.4 2.0 %collective-permute-start.7 = (bf16[64,4096]{1,0:T(8,128)(2,1)S(1)}, bf16[64,4096]{1,0:T(8,128)(2,1)S(1)}, u32[]{:S(2)}, u32[]{:S(2)}) collective-permute-start(bf16[64,4096]{1,0:T(8,128)(2,1)S(1)} %constant_dynamic-update-slice_fusion.4.refs_2_), channel_id=1, source_target_pairs={{0,4},{4,0},{8,12},{12,8},{16,20},{20,16},{24,28},{28,24},{1,5},{5... | collective-permute-start | bytes 1572872 | tf_op jit(solution)/shard_map/ppermute | solution.py:258
  38.0 1.4 %collective-permute-start.8 = (bf16[4,16,1024]{2,1,0:T(8,128)(2,1)S(1)}, bf16[4,16,1024]{2,1,0:T(8,128)(2,1)S(1)}, u32[]{:S(2)}, u32[]{:S(2)}) collective-permute-start(bf16[4,16,1024]{2,1,0:T(8,128)(2,1)S(1)} %get-tuple-element.29), channel_id=1, source_target_pairs={{0,4},{4,0},{8,12},{12,8},{16,20},{20,16},{24,28},{28,24},{1,5},{5... | collective-permute-start | bytes 393224 | tf_op jit(solution)/shard_map/ppermute | solution.py:258
  38.1 1.5 %collective-permute-start.9 = (bf16[4,16,1024]{2,1,0:T(8,128)(2,1)S(1)}, bf16[4,16,1024]{2,1,0:T(8,128)(2,1)S(1)}, u32[]{:S(2)}, u32[]{:S(2)}) collective-permute-start(bf16[4,16,1024]{2,1,0:T(8,128)(2,1)S(1)} %get-tuple-element.30), channel_id=1, source_target_pairs={{0,4},{4,0},{8,12},{12,8},{16,20},{20,16},{24,28},{28,24},{1,5},{5... | collective-permute-start | bytes 393224 | tf_op jit(solution)/shard_map/ppermute | solution.py:258
  39.6 2.6 %collective-permute-start.10 = (bf16[3,4,16,1024]{3,2,1,0:T(8,128)(2,1)S(1)}, bf16[3,4,16,1024]{3,2,1,0:T(8,128)(2,1)S(1)}, u32[]{:S(2)}, u32[]{:S(2)}) collective-permute-start(bf16[3,4,16,1024]{3,2,1,0:T(8,128)(2,1)S(1)} %get-tuple-element.31), channel_id=1, source_target_pairs={{0,4},{4,0},{8,12},{12,8},{16,20},{20,16},{24,28},{28,24},{1,5},{5... | collective-permute-start | bytes 1179656 | tf_op jit(solution)/shard_map/ppermute | solution.py:258
  40.0 5.0 %collective-permute-start.13 = (bf16[4,16,1024]{2,1,0:T(8,128)(2,1)S(1)}, bf16[4,16,1024]{2,1,0:T(8,128)(2,1)S(1)}, u32[]{:S(2)}, u32[]{:S(2)}) collective-permute-start(bf16[4,16,1024]{2,1,0:T(8,128)(2,1)S(1)} %fusion.1), channel_id=1, source_target_pairs={{0,16},{4,12},{8,24},{12,4},{16,0},{20,28},{24,8},{28,20},{1,17},{... | collective-permute-start | bytes 393224 | tf_op jit(solution)/shard_map/ppermute | solution.py:262
  40.7 1.7 %collective-permute-start.11 = (bf16[3,4,16,1024]{3,2,1,0:T(8,128)(2,1)S(1)}, bf16[3,4,16,1024]{3,2,1,0:T(8,128)(2,1)S(1)}, u32[]{:S(2)}, u32[]{:S(2)}) collective-permute-start(bf16[3,4,16,1024]{3,2,1,0:T(8,128)(2,1)S(1)} %get-tuple-element.33), channel_id=1, source_target_pairs={{0,4},{4,0},{8,12},{12,8},{16,20},{20,16},{24,28},{28,24},{1,5},{5... | collective-permute-start | bytes 1179656 | tf_op jit(solution)/shard_map/ppermute | solution.py:258
  40.8 5.7 %collective-permute-start.15 = (bf16[4,16,1024]{2,1,0:T(8,128)(2,1)S(1)}, bf16[4,16,1024]{2,1,0:T(8,128)(2,1)S(1)}, u32[]{:S(2)}, u32[]{:S(2)}) collective-permute-start(bf16[4,16,1024]{2,1,0:T(8,128)(2,1)S(1)} %fusion), channel_id=1, source_target_pairs={{0,16},{4,12},{8,24},{12,4},{16,0},{20,28},{24,8},{28,20},{1,17},{... | collective-permute-start | bytes 393224 | tf_op jit(solution)/shard_map/ppermute | solution.py:262
  42.5 9.0 %collective-permute-start.12 = (bf16[4,16,2048]{2,1,0:T(8,128)(2,1)S(1)}, bf16[4,16,2048]{2,1,0:T(8,128)(2,1)S(1)}, u32[]{:S(2)}, u32[]{:S(2)}) collective-permute-start(bf16[4,16,2048]{2,1,0:T(8,128)(2,1)S(1)} %pad_maximum_fusion.1), channel_id=1, source_target_pairs={{0,16},{4,12},{8,24},{12,4},{16,0},{20,28},{24,8},{28,20},{1,17},{... | collective-permute-start | bytes 786440 | tf_op jit(solution)/shard_map/ppermute | solution.py:262
  45.1 5.0 %collective-permute-start.14 = (bf16[4,16,1024]{2,1,0:T(8,128)(2,1)S(1)}, bf16[4,16,1024]{2,1,0:T(8,128)(2,1)S(1)}, u32[]{:S(2)}, u32[]{:S(2)}) collective-permute-start(bf16[4,16,1024]{2,1,0:T(8,128)(2,1)S(1)} %fusion.4), channel_id=1, source_target_pairs={{0,8},{4,20},{8,0},{12,28},{16,24},{20,4},{24,16},{28,12},{1,9},{5... | collective-permute-start | bytes 393224 | tf_op jit(solution)/shard_map/ppermute | solution.py:262
  46.5 5.0 %collective-permute-start.16 = (bf16[4,16,1024]{2,1,0:T(8,128)(2,1)S(1)}, bf16[4,16,1024]{2,1,0:T(8,128)(2,1)S(1)}, u32[]{:S(2)}, u32[]{:S(2)}) collective-permute-start(bf16[4,16,1024]{2,1,0:T(8,128)(2,1)S(1)} %fusion.2), channel_id=1, source_target_pairs={{0,8},{4,20},{8,0},{12,28},{16,24},{20,4},{24,16},{28,12},{1,9},{5... | collective-permute-start | bytes 393224 | tf_op jit(solution)/shard_map/ppermute | solution.py:262
  51.7 6.9 %collective-permute-start.17 = (bf16[16,2048]{1,0:T(8,128)(2,1)S(1)}, bf16[16,2048]{1,0:T(8,128)(2,1)S(1)}, u32[]{:S(2)}, u32[]{:S(2)}) collective-permute-start(bf16[16,2048]{1,0:T(8,128)(2,1)S(1)} %pad_maximum_fusion.2), channel_id=1, source_target_pairs={{0,3},{1,2},{2,1},{3,0},{4,7},{5,6},{6,5},{7,4},{8,11},{9,10},{10,... | collective-permute-start | bytes 196616 | tf_op jit(solution)/shard_map/ppermute | solution.py:265
  52.6 7.8 %collective-permute-start.18 = (bf16[16,2048]{1,0:T(8,128)(2,1)S(1)}, bf16[16,2048]{1,0:T(8,128)(2,1)S(1)}, u32[]{:S(2)}, u32[]{:S(2)}) collective-permute-start(bf16[16,2048]{1,0:T(8,128)(2,1)S(1)} %pad_maximum_fusion.3), channel_id=1, source_target_pairs={{0,2},{1,3},{2,0},{3,1},{4,6},{5,7},{6,4},{7,5},{8,10},{9,11},{10,... | collective-permute-start | bytes 196616 | tf_op jit(solution)/shard_map/ppermute | solution.py:265
  53.5 6.9 %collective-permute-start.19 = (bf16[16,2048]{1,0:T(8,128)(2,1)S(1)}, bf16[16,2048]{1,0:T(8,128)(2,1)S(1)}, u32[]{:S(2)}, u32[]{:S(2)}) collective-permute-start(bf16[16,2048]{1,0:T(8,128)(2,1)S(1)} %pad_maximum_fusion.4), channel_id=1, source_target_pairs={{0,1},{1,0},{2,3},{3,2},{4,5},{5,4},{6,7},{7,6},{8,9},{9,8},{10,11... | collective-permute-start | bytes 196616 | tf_op jit(solution)/shard_map/ppermute | solution.py:265

commit v13 on v11

--- a/solution.py
+++ b/solution.py
@@ -248,6 +248,42 @@
     return [outs[k * PARTS : (k + 1) * PARTS] for k in range(3)]
 
 
+def place_kernel(picker_ref, *refs):
+    *part_refs, out_ref, rows, sems = refs
+    picker = picker_ref[...]
+    chunks, _, step = rows.shape
+    copies = []
+    for i in range(chunks):
+        cut = slice(i * step, (i + 1) * step)
+        total = part_refs[0][:, cut]
+        for ref in part_refs[1:]:
+            total = total + ref[:, cut].astype(F32)
+        rows[i] = lax.dot_general(
+            picker, total.astype(BF16), (((0,), (0,)), ((), ())), preferred_element_type=F32
+        ).astype(BF16)
+        copy = pltpu.make_async_copy(rows.at[i], out_ref.at[:, pl.ds(i * step, step)], sems.at[i])
+        copy.start()
+        copies.append(copy)
+    for copy in copies:
+        copy.wait()
+
+
+def place(picker, parts):
+    tokens, wide = picker.shape[1], parts[0].shape[1]
+    chunks = 4
+    return pl.pallas_call(
+        place_kernel,
+        out_specs=pl.BlockSpec(memory_space=pltpu.HBM),
+        out_shape=jax.ShapeDtypeStruct((tokens, wide), BF16),
+        scratch_shapes=[
+            pltpu.VMEM((chunks, tokens, wide // chunks), BF16),
+            pltpu.SemaphoreType.DMA((chunks,)),
+        ],
+        compiler_params=params(),
+        name="place_rows",
+    )(picker, *parts)
+
+
 def body(n_seq, n_vocab, hidden, head, mask):
     n_chip = n_seq // 2
     last = n_chip - 1
@@ -312,12 +348,10 @@
         parts = [lax.dynamic_index_in_dim(part, column ^ k, 0, keepdims=False) for part in sums[0]]
         return jnp.concatenate(parts, axis=1)
 
-    result = piece(0)
+    parts = [piece(0)]
     for k in range(n_vocab - 1, 0, -1):
-        result = result + send_vocab(piece(k).astype(BF16), k).astype(F32)
-    derivative = lax.dot_general(
-        picker, result.astype(BF16), (((0,), (0,)), ((), ())), preferred_element_type=F32
-    ).astype(BF16)
+        parts.append(send_vocab(piece(k).astype(BF16), k))
+    derivative = place(picker, parts)
     return each.reshape(-1), average.reshape(()), derivative
 
 

time: 59.8 us -> 60 us (level)
  matrix products: 1.12 us -> 0 us
  Pallas kernels: 6.13 us -> 7.16 us
    dot_general x1 -> x0, matrix products: 1.12 us -> none  [body(): lax.dot_general(picker, result.astype(BF16), (((0,), (0,)), ((), ())), pr...]
    pallas_call x0 -> x1, Pallas kernels: none -> 1.03 us  [place(): pl.pallas_call(place_kernel, out_specs=pl.BlockSpec(memory_space=pltpu.HB...]
where the time goes in v13:
time: 60 us; the launch traced here: 59.8 us
  starting transfers between devices  20.7 us (34%)
  waiting for transfers between devices  16.9 us (28%)
  blocking collectives  13.7 us (23%)
  Pallas kernels  7.16 us (12%)
  between operations  0.82 us (1%)
    ppermute x10, starting transfers between devices, swap_chip(): lax.ppermute(value, 'seq', [(i, i ^ flips[i & 1]) for i in range(n_seq)])  15.2 us
    all_to_all x1, blocking collectives, body(): stats = lax.all_to_all(stats, ('seq', 'vocab'), 0, 0, tiled=True)  13.7 us
    ppermute x10, waiting for transfers between devices, swap_chip(): lax.ppermute(value, 'seq', [(i, i ^ flips[i & 1]) for i in range(n_seq)])  10.5 us
    ppermute x3, starting transfers between devices, send_vocab(): return lax.ppermute(value, 'vocab', [(i, i ^ k) for i in range(n_vocab)])  4.45 us
    ppermute x3, waiting for transfers between devices, send_vocab(): return lax.ppermute(value, 'vocab', [(i, i ^ k) for i in range(n_vocab)])  3.65 us
    ppermute x6, waiting for transfers between devices, swap_core(): return lax.ppermute(value, 'seq', [(i, i ^ 1) for i in range(n_seq)])  2.76 us
    pallas_call x1, Pallas kernels, select(): pl.pallas_call(select_kernel, in_specs=[pl.BlockSpec(memory_space=pltpu.H...  2.75 us
    pallas_call x1, Pallas kernels, gradients(): pl.pallas_call(functools.partial(gradient_kernel, n_seq, n_vocab), in_spe...  1.64 us
  transfers between devices with their start and end apart: 19, of which 13 were waited for; matrix products, arithmetic and copies ran while one was open for 1% of the time, Pallas kernels for 1%

profile of v13, /device:TPU:0, one launch (start us, length us, event | category | flops | bytes accessed | tf_op | source)
XLA Modules:
  0.0 59.8 jit_solution(840594760690587155)
XLA Ops:
  0.6 0.0 copy-start
  0.6 2.8 %select_rows.1 = (bf16[16,4096]{1,0:T(8,128)(2,1)S(1)}, bf16[16,4096]{1,0:T(8,128)(2,1)S(1)}, bf16[16,128]{1,0:T(8,128)(2,1)S(1)}) custom-call(s32[1,128]{1,0:T(1,128)} %bitcast.45, bf16[128,8192]{1,0:T(8,128)(2,1)} %hidden_ref.1), custom_call_target="tpu_custom_call" | custom-call | tf_op jit(solution)/shard_map/select_rows/pallas_call | solution.py:91
  3.4 3.0 %collective-permute-start = (bf16[16,4096]{1,0:T(8,128)(2,1)S(1)}, bf16[16,4096]{1,0:T(8,128)(2,1)S(1)}, u32[]{:S(2)}, u32[]{:S(2)}) collective-permute-start(bf16[16,4096]{1,0:T(8,128)(2,1)S(1)} %get-tuple-element.23), channel_id=1, source_target_pairs={{0,8},{4,20},{8,0},{12,28},{16,24},{20,4},{24,16},{28,12},{1,9},{5... | collective-permute-start | bytes 393224 | tf_op jit(solution)/shard_map/ppermute | solution.py:297
  6.4 0.1 collective-permute-start.2
  6.5 2.0 %collective-permute-start.1 = (bf16[16,8192]{1,0:T(8,128)(2,1)S(1)}, bf16[16,8192]{1,0:T(8,128)(2,1)S(1)}, u32[]{:S(2)}, u32[]{:S(2)}) collective-permute-start(bf16[16,8192]{1,0:T(8,128)(2,1)S(1)} %pad_maximum_fusion), channel_id=1, source_target_pairs={{0,16},{4,12},{8,24},{12,4},{16,0},{20,28},{24,8},{28,20},{1,17},{... | collective-permute-start | bytes 786440 | tf_op jit(solution)/shard_map/ppermute | solution.py:297
  8.6 1.4 %collective-permute-done = bf16[16,4096]{1,0:T(8,128)(2,1)S(1)} collective-permute-done((bf16[16,4096]{1,0:T(8,128)(2,1)S(1)}, bf16[16,4096]{1,0:T(8,128)(2,1)S(1)}, u32[]{:S(2)}, u32[]{:S(2)}) %collective-permute-start) | collective-permute-done | bytes 131104 | tf_op jit(solution)/shard_map/ppermute | solution.py:297
  10.0 2.5 %collective-permute-start.3 = (bf16[16,4096]{1,0:T(8,128)(2,1)S(1)}, bf16[16,4096]{1,0:T(8,128)(2,1)S(1)}, u32[]{:S(2)}, u32[]{:S(2)}) collective-permute-start(bf16[16,4096]{1,0:T(8,128)(2,1)S(1)} %collective-permute-done), channel_id=1, source_target_pairs={{0,16},{4,12},{8,24},{12,4},{16,0},{20,28},{24,8},{28,20},{1,17},{... | collective-permute-start | bytes 393224 | tf_op jit(solution)/shard_map/ppermute | solution.py:297
  12.5 0.3 collective-permute-done.2
  12.8 2.5 %collective-permute-start.5 = (bf16[16,4096]{1,0:T(8,128)(2,1)S(1)}, bf16[16,4096]{1,0:T(8,128)(2,1)S(1)}, u32[]{:S(2)}, u32[]{:S(2)}) collective-permute-start(bf16[16,4096]{1,0:T(8,128)(2,1)S(1)} %collective-permute-done.2), channel_id=1, source_target_pairs={{0,16},{4,12},{8,24},{12,4},{16,0},{20,28},{24,8},{28,20},{1,17},{... | collective-permute-start | bytes 393224 | tf_op jit(solution)/shard_map/ppermute | solution.py:297
  15.3 0.0 collective-permute-done.1
  15.4 0.0 collective-permute-done.3
  15.4 0.0 collective-permute-start.4
  15.5 2.7 %collective-permute-done.5 = bf16[16,4096]{1,0:T(8,128)(2,1)S(1)} collective-permute-done((bf16[16,4096]{1,0:T(8,128)(2,1)S(1)}, bf16[16,4096]{1,0:T(8,128)(2,1)S(1)}, u32[]{:S(2)}, u32[]{:S(2)}) %collective-permute-start.5) | collective-permute-done | bytes 131104 | tf_op jit(solution)/shard_map/ppermute | solution.py:297
  18.2 0.1 collective-permute-start.6
  18.3 1.5 %collective-permute-done.6.refs_3_ = bf16[32,4096]{1,0:T(8,128)(2,1)S(1)} collective-permute-done((bf16[32,4096]{1,0:T(8,128)(2,1)S(1)}, bf16[32,4096]{1,0:T(8,128)(2,1)S(1)}, u32[]{:S(2)}, u32[]{:S(2)}) %collective-permute-start.6) | collective-permute-done | bytes 262176 | tf_op jit(solution)/shard_map/ppermute | solution.py:293
  19.8 0.0 collective-permute-done.4.refs_1_
  19.8 1.0 %local_logits.1 = (f32[128,256]{1,0:T(8,128)S(1)}, f32[32,4,128]{2,1,0:T(4,128)S(1)}) custom-call(bf16[96,4096]{1,0:T(8,128)(2,1)S(1)} %slice_dynamic-update-slice_fusion.refs_0_, bf16[96,4096]{1,0:T(8,128)(2,1)S(1)} %collective-permute-done.4.refs_1_, bf16[32,4096]{1,0:T(8,128)(2,1)S(1)} %constant_dynamic-update-slice_fusion.4.refs_2_, ...), custom_call_target="tpu_custom_call" | custom-call | tf_op jit(solution)/shard_map/local_logits/pallas_call | solution.py:146
  20.8 13.7 %all_to_all.5.stats_ref = f32[32,4,128]{2,1,0:T(4,128)S(1)} all-to-all(f32[32,4,128]{2,1,0:T(4,128)S(1)} %get-tuple-element.28), channel_id=1, replica_groups=mesh['seq'=8,'vocab'=4] {'seq','vocab'}, dimensions={0} | all-to-all | bytes 131072 | tf_op jit(solution)/shard_map/all_to_all | solution.py:319
  34.5 1.6 %gradients.1 = (bf16[4,4,16,1024]{3,2,1,0:T(8,128)(2,1)S(1)}, bf16[4,4,16,1024]{3,2,1,0:T(8,128)(2,1)S(1)}, bf16[3,4,16,1024]{3,2,1,0:T(8,128)(2,1)S(1)}, bf16[3...) custom-call(f32[32,4,128]{2,1,0:T(4,128)S(1)} %all_to_all.5.stats_ref, ...), custom_call_target="tpu_custom_call" | custom-call | tf_op jit(solution)/shard_map/gradients/pallas_call | solution.py:237
  36.1 0.1 collective-permute-start.7
  36.2 0.5 collective-permute-start.8
  36.7 0.8 %collective-permute-done.7 = bf16[4,16,1024]{2,1,0:T(8,128)(2,1)S(1)} collective-permute-done((bf16[4,16,1024]{2,1,0:T(8,128)(2,1)S(1)}, bf16[4,16,1024]{2,1,0:T(8,128)(2,1)S(1)}, u32[]{:S(2)}, u32[]{:S(2)}) %collective-permute-start.7) | collective-permute-done | bytes 131104 | tf_op jit(solution)/shard_map/ppermute | solution.py:293
  37.5 0.2 collective-permute-done.8
  37.7 0.3 collective-permute-start.9
  38.1 0.7 %collective-permute-start.12 = (bf16[4,16,1024]{2,1,0:T(8,128)(2,1)S(1)}, bf16[4,16,1024]{2,1,0:T(8,128)(2,1)S(1)}, u32[]{:S(2)}, u32[]{:S(2)}) collective-permute-start(bf16[4,16,1024]{2,1,0:T(8,128)(2,1)S(1)} %fusion.1), channel_id=1, source_target_pairs={{0,16},{4,12},{8,24},{12,4},{16,0},{20,28},{24,8},{28,20},{1,17},{... | collective-permute-start | bytes 393224 | tf_op jit(solution)/shard_map/ppermute | solution.py:297
  38.8 0.0 collective-permute-start.10
  38.8 1.4 %collective-permute-start.14 = (bf16[4,16,1024]{2,1,0:T(8,128)(2,1)S(1)}, bf16[4,16,1024]{2,1,0:T(8,128)(2,1)S(1)}, u32[]{:S(2)}, u32[]{:S(2)}) collective-permute-start(bf16[4,16,1024]{2,1,0:T(8,128)(2,1)S(1)} %fusion), channel_id=1, source_target_pairs={{0,16},{4,12},{8,24},{12,4},{16,0},{20,28},{24,8},{28,20},{1,17},{... | collective-permute-start | bytes 393224 | tf_op jit(solution)/shard_map/ppermute | solution.py:297
  40.3 0.0 collective-permute-done.9
  40.3 0.2 collective-permute-done.10
  40.6 1.4 %collective-permute-start.11 = (bf16[4,16,2048]{2,1,0:T(8,128)(2,1)S(1)}, bf16[4,16,2048]{2,1,0:T(8,128)(2,1)S(1)}, u32[]{:S(2)}, u32[]{:S(2)}) collective-permute-start(bf16[4,16,2048]{2,1,0:T(8,128)(2,1)S(1)} %pad_maximum_fusion.1), channel_id=1, source_target_pairs={{0,16},{4,12},{8,24},{12,4},{16,0},{20,28},{24,8},{28,20},{1,17},{... | collective-permute-start | bytes 786440 | tf_op jit(solution)/shard_map/ppermute | solution.py:297
  42.0 1.1 %collective-permute-done.12 = bf16[4,16,1024]{2,1,0:T(8,128)(2,1)S(1)} collective-permute-done((bf16[4,16,1024]{2,1,0:T(8,128)(2,1)S(1)}, bf16[4,16,1024]{2,1,0:T(8,128)(2,1)S(1)}, u32[]{:S(2)}, u32[]{:S(2)}) %collective-permute-start.12) | collective-permute-done | bytes 131104 | tf_op jit(solution)/shard_map/ppermute | solution.py:297
  43.1 0.1 fusion.4
  43.2 0.7 %collective-permute-start.13 = (bf16[4,16,1024]{2,1,0:T(8,128)(2,1)S(1)}, bf16[4,16,1024]{2,1,0:T(8,128)(2,1)S(1)}, u32[]{:S(2)}, u32[]{:S(2)}) collective-permute-start(bf16[4,16,1024]{2,1,0:T(8,128)(2,1)S(1)} %fusion.4), channel_id=1, source_target_pairs={{0,8},{4,20},{8,0},{12,28},{16,24},{20,4},{24,16},{28,12},{1,9},{5... | collective-permute-start | bytes 393224 | tf_op jit(solution)/shard_map/ppermute | solution.py:297
  43.9 0.6 %collective-permute-done.14 = bf16[4,16,1024]{2,1,0:T(8,128)(2,1)S(1)} collective-permute-done((bf16[4,16,1024]{2,1,0:T(8,128)(2,1)S(1)}, bf16[4,16,1024]{2,1,0:T(8,128)(2,1)S(1)}, u32[]{:S(2)}, u32[]{:S(2)}) %collective-permute-start.14) | collective-permute-done | bytes 131104 | tf_op jit(solution)/shard_map/ppermute | solution.py:297
  44.5 0.1 fusion.2
  44.6 0.8 %collective-permute-start.15 = (bf16[4,16,1024]{2,1,0:T(8,128)(2,1)S(1)}, bf16[4,16,1024]{2,1,0:T(8,128)(2,1)S(1)}, u32[]{:S(2)}, u32[]{:S(2)}) collective-permute-start(bf16[4,16,1024]{2,1,0:T(8,128)(2,1)S(1)} %fusion.2), channel_id=1, source_target_pairs={{0,8},{4,20},{8,0},{12,28},{16,24},{20,4},{24,16},{28,12},{1,9},{5... | collective-permute-start | bytes 393224 | tf_op jit(solution)/shard_map/ppermute | solution.py:297
  45.4 2.8 %collective-permute-done.13 = bf16[4,16,1024]{2,1,0:T(8,128)(2,1)S(1)} collective-permute-done((bf16[4,16,1024]{2,1,0:T(8,128)(2,1)S(1)}, bf16[4,16,1024]{2,1,0:T(8,128)(2,1)S(1)}, u32[]{:S(2)}, u32[]{:S(2)}) %collective-permute-start.13) | collective-permute-done | bytes 131104 | tf_op jit(solution)/shard_map/ppermute | solution.py:297
  48.2 1.4 %collective-permute-done.15 = bf16[4,16,1024]{2,1,0:T(8,128)(2,1)S(1)} collective-permute-done((bf16[4,16,1024]{2,1,0:T(8,128)(2,1)S(1)}, bf16[4,16,1024]{2,1,0:T(8,128)(2,1)S(1)}, u32[]{:S(2)}, u32[]{:S(2)}) %collective-permute-start.15) | collective-permute-done | bytes 131104 | tf_op jit(solution)/shard_map/ppermute | solution.py:297
  49.6 0.0 collective-permute-done.11
  49.6 0.2 fusion.3
  49.8 0.3 collective-permute-start.18
  50.1 1.2 %collective-permute-start.17 = (bf16[16,2048]{1,0:T(8,128)(2,1)S(1)}, bf16[16,2048]{1,0:T(8,128)(2,1)S(1)}, u32[]{:S(2)}, u32[]{:S(2)}) collective-permute-start(bf16[16,2048]{1,0:T(8,128)(2,1)S(1)} %pad_maximum_fusion.4), channel_id=1, source_target_pairs={{0,2},{1,3},{2,0},{3,1},{4,6},{5,7},{6,4},{7,5},{8,10},{9,11},{10,... | collective-permute-start | bytes 196616 | tf_op jit(solution)/shard_map/ppermute | solution.py:300
  51.3 3.0 %collective-permute-start.16 = (bf16[16,2048]{1,0:T(8,128)(2,1)S(1)}, bf16[16,2048]{1,0:T(8,128)(2,1)S(1)}, u32[]{:S(2)}, u32[]{:S(2)}) collective-permute-start(bf16[16,2048]{1,0:T(8,128)(2,1)S(1)} %pad_maximum_fusion.3), channel_id=1, source_target_pairs={{0,3},{1,2},{2,1},{3,0},{4,7},{5,6},{6,5},{7,4},{8,11},{9,10},{10,... | collective-permute-start | bytes 196616 | tf_op jit(solution)/shard_map/ppermute | solution.py:300
  54.3 0.8 %entropies.1 = (f32[1,128]{1,0:T(1,128)}, f32[1,1]{1,0:T(1,128)}) custom-call(f32[32,4,128]{2,1,0:T(4,128)S(1)} %all_to_all.5.stats_ref, bf16[16,128]{1,0:T(8,128)(2,1)S(1)} %get-tuple-element.27.refs_5_.picker_ref), custom_call_target="tpu_custom_call" | custom-call | tf_op jit(solution)/shard_map/entropies/pallas_call | solution.py:186
  55.1 0.1 collective-permute-done.18.refs_3_
  55.2 3.6 %collective-permute-done.17.refs_2_ = bf16[16,2048]{1,0:T(8,128)(2,1)S(1)} collective-permute-done((bf16[16,2048]{1,0:T(8,128)(2,1)S(1)}, bf16[16,2048]{1,0:T(8,128)(2,1)S(1)}, u32[]{:S(2)}, u32[]{:S(2)}) %collective-permute-start.17) | collective-permute-done | bytes 65568 | tf_op jit(solution)/shard_map/ppermute | solution.py:300
  58.7 0.0 collective-permute-done.16.refs_1_
  58.8 1.0 %place_rows.1 = bf16[128,2048]{1,0:T(8,128)(2,1)} custom-call(bf16[16,128]{1,0:T(8,128)(2,1)S(1)} %get-tuple-element.27.refs_5_.picker_ref, f32[16,2048]{1,0:T(8,128)S(1)} %pad_maximum_fusion.2.refs_0_, bf16[16,2048]{1,0:T(8,128)(2,1)S(1)} %collective-permute-done.16.refs_1_, bf16[16,2048]{1,0:T(8,128)(2,1)S(1)} %collective-permute-done.17.refs_2_, ...), custom_call_target="tpu_custom_call" | custom-call | tf_op jit(solution)/shard_map/place_rows/pallas_call | solution.py:274
  (21 shorter events, 0.3 us)
Async XLA Ops:
  0.6 19.2 %copy-start = (bf16[8192,256]{1,0:T(8,128)(2,1)S(1)}, bf16[8192,256]{1,0:T(8,128)(2,1)}, u32[]{:S(2)}) copy-start(bf16[8192,256]{1,0:T(8,128)(2,1)} %head_ref.1) | copy-start | bytes 12582916
  3.4 6.6 %collective-permute-start = (bf16[16,4096]{1,0:T(8,128)(2,1)S(1)}, bf16[16,4096]{1,0:T(8,128)(2,1)S(1)}, u32[]{:S(2)}, u32[]{:S(2)}) collective-permute-start(bf16[16,4096]{1,0:T(8,128)(2,1)S(1)} %get-tuple-element.23), channel_id=1, source_target_pairs={{0,8},{4,20},{8,0},{12,28},{16,24},{20,4},{24,16},{28,12},{1,9},{5... | collective-permute-start | bytes 393224 | tf_op jit(solution)/shard_map/ppermute | solution.py:297
  6.4 6.4 %collective-permute-start.2 = (bf16[16,4096]{1,0:T(8,128)(2,1)S(1)}, bf16[16,4096]{1,0:T(8,128)(2,1)S(1)}, u32[]{:S(2)}, u32[]{:S(2)}) collective-permute-start(bf16[16,4096]{1,0:T(8,128)(2,1)S(1)} %get-tuple-element.24), channel_id=1, source_target_pairs={{0,8},{4,20},{8,0},{12,28},{16,24},{20,4},{24,16},{28,12},{1,9},{5... | collective-permute-start | bytes 393224 | tf_op jit(solution)/shard_map/ppermute | solution.py:297
  6.5 8.8 %collective-permute-start.1 = (bf16[16,8192]{1,0:T(8,128)(2,1)S(1)}, bf16[16,8192]{1,0:T(8,128)(2,1)S(1)}, u32[]{:S(2)}, u32[]{:S(2)}) collective-permute-start(bf16[16,8192]{1,0:T(8,128)(2,1)S(1)} %pad_maximum_fusion), channel_id=1, source_target_pairs={{0,16},{4,12},{8,24},{12,4},{16,0},{20,28},{24,8},{28,20},{1,17},{... | collective-permute-start | bytes 786440 | tf_op jit(solution)/shard_map/ppermute | solution.py:297
  10.0 5.4 %collective-permute-start.3 = (bf16[16,4096]{1,0:T(8,128)(2,1)S(1)}, bf16[16,4096]{1,0:T(8,128)(2,1)S(1)}, u32[]{:S(2)}, u32[]{:S(2)}) collective-permute-start(bf16[16,4096]{1,0:T(8,128)(2,1)S(1)} %collective-permute-done), channel_id=1, source_target_pairs={{0,16},{4,12},{8,24},{12,4},{16,0},{20,28},{24,8},{28,20},{1,17},{... | collective-permute-start | bytes 393224 | tf_op jit(solution)/shard_map/ppermute | solution.py:297
  12.8 5.4 %collective-permute-start.5 = (bf16[16,4096]{1,0:T(8,128)(2,1)S(1)}, bf16[16,4096]{1,0:T(8,128)(2,1)S(1)}, u32[]{:S(2)}, u32[]{:S(2)}) collective-permute-start(bf16[16,4096]{1,0:T(8,128)(2,1)S(1)} %collective-permute-done.2), channel_id=1, source_target_pairs={{0,16},{4,12},{8,24},{12,4},{16,0},{20,28},{24,8},{28,20},{1,17},{... | collective-permute-start | bytes 393224 | tf_op jit(solution)/shard_map/ppermute | solution.py:297
  15.4 4.4 %collective-permute-start.4 = (bf16[96,4096]{1,0:T(8,128)(2,1)S(1)}, bf16[96,4096]{1,0:T(8,128)(2,1)S(1)}, u32[]{:S(2)}, u32[]{:S(2)}) collective-permute-start(bf16[96,4096]{1,0:T(8,128)(2,1)S(1)} %slice_dynamic-update-slice_fusion.refs_0_), channel_id=1, source_target_pairs={{0,4},{4,0},{8,12},{12,8},{16,20},{20,16},{24,28},{28,24},{1,5},{5... | collective-permute-start | bytes 2359304 | tf_op jit(solution)/shard_map/ppermute | solution.py:293
  18.2 1.6 %collective-permute-start.6 = (bf16[32,4096]{1,0:T(8,128)(2,1)S(1)}, bf16[32,4096]{1,0:T(8,128)(2,1)S(1)}, u32[]{:S(2)}, u32[]{:S(2)}) collective-permute-start(bf16[32,4096]{1,0:T(8,128)(2,1)S(1)} %constant_dynamic-update-slice_fusion.4.refs_2_), channel_id=1, source_target_pairs={{0,4},{4,0},{8,12},{12,8},{16,20},{20,16},{24,28},{28,24},{1,5},{5... | collective-permute-start | bytes 786440 | tf_op jit(solution)/shard_map/ppermute | solution.py:293
  36.1 1.4 %collective-permute-start.7 = (bf16[4,16,1024]{2,1,0:T(8,128)(2,1)S(1)}, bf16[4,16,1024]{2,1,0:T(8,128)(2,1)S(1)}, u32[]{:S(2)}, u32[]{:S(2)}) collective-permute-start(bf16[4,16,1024]{2,1,0:T(8,128)(2,1)S(1)} %get-tuple-element.33), channel_id=1, source_target_pairs={{0,4},{4,0},{8,12},{12,8},{16,20},{20,16},{24,28},{28,24},{1,5},{5... | collective-permute-start | bytes 393224 | tf_op jit(solution)/shard_map/ppermute | solution.py:293
  36.2 1.5 %collective-permute-start.8 = (bf16[4,16,1024]{2,1,0:T(8,128)(2,1)S(1)}, bf16[4,16,1024]{2,1,0:T(8,128)(2,1)S(1)}, u32[]{:S(2)}, u32[]{:S(2)}) collective-permute-start(bf16[4,16,1024]{2,1,0:T(8,128)(2,1)S(1)} %get-tuple-element.34), channel_id=1, source_target_pairs={{0,4},{4,0},{8,12},{12,8},{16,20},{20,16},{24,28},{28,24},{1,5},{5... | collective-permute-start | bytes 393224 | tf_op jit(solution)/shard_map/ppermute | solution.py:293
  37.7 2.6 %collective-permute-start.9 = (bf16[3,4,16,1024]{3,2,1,0:T(8,128)(2,1)S(1)}, bf16[3,4,16,1024]{3,2,1,0:T(8,128)(2,1)S(1)}, u32[]{:S(2)}, u32[]{:S(2)}) collective-permute-start(bf16[3,4,16,1024]{3,2,1,0:T(8,128)(2,1)S(1)} %get-tuple-element.35), channel_id=1, source_target_pairs={{0,4},{4,0},{8,12},{12,8},{16,20},{20,16},{24,28},{28,24},{1,5},{5... | collective-permute-start | bytes 1179656 | tf_op jit(solution)/shard_map/ppermute | solution.py:293
  38.1 5.0 %collective-permute-start.12 = (bf16[4,16,1024]{2,1,0:T(8,128)(2,1)S(1)}, bf16[4,16,1024]{2,1,0:T(8,128)(2,1)S(1)}, u32[]{:S(2)}, u32[]{:S(2)}) collective-permute-start(bf16[4,16,1024]{2,1,0:T(8,128)(2,1)S(1)} %fusion.1), channel_id=1, source_target_pairs={{0,16},{4,12},{8,24},{12,4},{16,0},{20,28},{24,8},{28,20},{1,17},{... | collective-permute-start | bytes 393224 | tf_op jit(solution)/shard_map/ppermute | solution.py:297
  38.8 1.7 %collective-permute-start.10 = (bf16[3,4,16,1024]{3,2,1,0:T(8,128)(2,1)S(1)}, bf16[3,4,16,1024]{3,2,1,0:T(8,128)(2,1)S(1)}, u32[]{:S(2)}, u32[]{:S(2)}) collective-permute-start(bf16[3,4,16,1024]{3,2,1,0:T(8,128)(2,1)S(1)} %get-tuple-element.37), channel_id=1, source_target_pairs={{0,4},{4,0},{8,12},{12,8},{16,20},{20,16},{24,28},{28,24},{1,5},{5... | collective-permute-start | bytes 1179656 | tf_op jit(solution)/shard_map/ppermute | solution.py:293
  38.8 5.7 %collective-permute-start.14 = (bf16[4,16,1024]{2,1,0:T(8,128)(2,1)S(1)}, bf16[4,16,1024]{2,1,0:T(8,128)(2,1)S(1)}, u32[]{:S(2)}, u32[]{:S(2)}) collective-permute-start(bf16[4,16,1024]{2,1,0:T(8,128)(2,1)S(1)} %fusion), channel_id=1, source_target_pairs={{0,16},{4,12},{8,24},{12,4},{16,0},{20,28},{24,8},{28,20},{1,17},{... | collective-permute-start | bytes 393224 | tf_op jit(solution)/shard_map/ppermute | solution.py:297
  40.6 9.0 %collective-permute-start.11 = (bf16[4,16,2048]{2,1,0:T(8,128)(2,1)S(1)}, bf16[4,16,2048]{2,1,0:T(8,128)(2,1)S(1)}, u32[]{:S(2)}, u32[]{:S(2)}) collective-permute-start(bf16[4,16,2048]{2,1,0:T(8,128)(2,1)S(1)} %pad_maximum_fusion.1), channel_id=1, source_target_pairs={{0,16},{4,12},{8,24},{12,4},{16,0},{20,28},{24,8},{28,20},{1,17},{... | collective-permute-start | bytes 786440 | tf_op jit(solution)/shard_map/ppermute | solution.py:297
  43.2 5.0 %collective-permute-start.13 = (bf16[4,16,1024]{2,1,0:T(8,128)(2,1)S(1)}, bf16[4,16,1024]{2,1,0:T(8,128)(2,1)S(1)}, u32[]{:S(2)}, u32[]{:S(2)}) collective-permute-start(bf16[4,16,1024]{2,1,0:T(8,128)(2,1)S(1)} %fusion.4), channel_id=1, source_target_pairs={{0,8},{4,20},{8,0},{12,28},{16,24},{20,4},{24,16},{28,12},{1,9},{5... | collective-permute-start | bytes 393224 | tf_op jit(solution)/shard_map/ppermute | solution.py:297
  44.6 5.0 %collective-permute-start.15 = (bf16[4,16,1024]{2,1,0:T(8,128)(2,1)S(1)}, bf16[4,16,1024]{2,1,0:T(8,128)(2,1)S(1)}, u32[]{:S(2)}, u32[]{:S(2)}) collective-permute-start(bf16[4,16,1024]{2,1,0:T(8,128)(2,1)S(1)} %fusion.2), channel_id=1, source_target_pairs={{0,8},{4,20},{8,0},{12,28},{16,24},{20,4},{24,16},{28,12},{1,9},{5... | collective-permute-start | bytes 393224 | tf_op jit(solution)/shard_map/ppermute | solution.py:297
  49.8 5.3 %collective-permute-start.18 = (bf16[16,2048]{1,0:T(8,128)(2,1)S(1)}, bf16[16,2048]{1,0:T(8,128)(2,1)S(1)}, u32[]{:S(2)}, u32[]{:S(2)}) collective-permute-start(bf16[16,2048]{1,0:T(8,128)(2,1)S(1)} %pad_maximum_fusion.5), channel_id=1, source_target_pairs={{0,1},{1,0},{2,3},{3,2},{4,5},{5,4},{6,7},{7,6},{8,9},{9,8},{10,11... | collective-permute-start | bytes 196616 | tf_op jit(solution)/shard_map/ppermute | solution.py:300
  50.1 8.6 %collective-permute-start.17 = (bf16[16,2048]{1,0:T(8,128)(2,1)S(1)}, bf16[16,2048]{1,0:T(8,128)(2,1)S(1)}, u32[]{:S(2)}, u32[]{:S(2)}) collective-permute-start(bf16[16,2048]{1,0:T(8,128)(2,1)S(1)} %pad_maximum_fusion.4), channel_id=1, source_target_pairs={{0,2},{1,3},{2,0},{3,1},{4,6},{5,7},{6,4},{7,5},{8,10},{9,11},{10,... | collective-permute-start | bytes 196616 | tf_op jit(solution)/shard_map/ppermute | solution.py:300
  51.3 7.5 %collective-permute-start.16 = (bf16[16,2048]{1,0:T(8,128)(2,1)S(1)}, bf16[16,2048]{1,0:T(8,128)(2,1)S(1)}, u32[]{:S(2)}, u32[]{:S(2)}) collective-permute-start(bf16[16,2048]{1,0:T(8,128)(2,1)S(1)} %pad_maximum_fusion.3), channel_id=1, source_target_pairs={{0,3},{1,2},{2,1},{3,0},{4,7},{5,6},{6,5},{7,4},{8,11},{9,10},{10,... | collective-permute-start | bytes 196616 | tf_op jit(solution)/shard_map/ppermute | solution.py:300

commit v14 on v11

--- a/solution.py
+++ b/solution.py
@@ -102,6 +102,33 @@
         name="select_rows",
     )(in_hbm(mask.reshape(1, tokens)), in_hbm(hidden))
     return own, picker
+
+
+def join_kernel(*refs):
+    *part_refs, out_ref, sems = refs
+    size = part_refs[0].shape[1]
+    copies = [
+        pltpu.make_async_copy(ref, out_ref.at[:, pl.ds(c * size, size)], sems.at[c])
+        for c, ref in enumerate(part_refs)
+    ]
+    for copy in copies:
+        copy.start()
+    for copy in copies:
+        copy.wait()
+
+
+def join(parts):
+    rows, size = parts[0].shape
+    vmem = pl.BlockSpec(memory_space=pltpu.VMEM)
+    return pl.pallas_call(
+        join_kernel,
+        in_specs=[vmem] * len(parts),
+        out_specs=vmem,
+        out_shape=jax.ShapeDtypeStruct((rows, size * len(parts)), parts[0].dtype),
+        scratch_shapes=[pltpu.SemaphoreType.DMA((len(parts),))],
+        compiler_params=params(),
+        name="join_parts",
+    )(*parts)
 
 
 def logits_kernel(n_seq, *refs):
@@ -270,7 +297,7 @@
         step = a.bit_length() - 1
         source = near[a ^ (1 << step)]
         if a > 1 and a == 1 << step:
-            moved = swap_chip(jnp.concatenate(source, axis=1), step)
+            moved = swap_chip(join(source), step)
             near.append(jnp.split(moved, PARTS, axis=1))
         else:
             near.append([swap_chip(part, step) for part in source])

time: 59.8 us -> 59.6 us (level)
  transfers between devices with their start and end apart: 19 -> 19, of which waited for: 13 -> 13; matrix products, arithmetic and copies ran while one was open for 1% -> 1% of each run, Pallas kernels for 1% -> 2%
where the time goes in v14:
time: 59.6 us; the launch traced here: 59.4 us
  starting transfers between devices  20.5 us (34%)
  waiting for transfers between devices  16.5 us (28%)
  blocking collectives  13.7 us (23%)
  Pallas kernels  6.29 us (11%)
  matrix products  1.11 us (2%)
  between operations  0.82 us (1%)
    ppermute x10, starting transfers between devices, swap_chip(): lax.ppermute(value, 'seq', [(i, i ^ flips[i & 1]) for i in range(n_seq)])  15 us
    all_to_all x1, blocking collectives, body(): stats = lax.all_to_all(stats, ('seq', 'vocab'), 0, 0, tiled=True)  13.7 us
    ppermute x10, waiting for transfers between devices, swap_chip(): lax.ppermute(value, 'seq', [(i, i ^ flips[i & 1]) for i in range(n_seq)])  10.3 us
    ppermute x3, starting transfers between devices, send_vocab(): return lax.ppermute(value, 'vocab', [(i, i ^ k) for i in range(n_vocab)])  4.45 us
    ppermute x3, waiting for transfers between devices, send_vocab(): return lax.ppermute(value, 'vocab', [(i, i ^ k) for i in range(n_vocab)])  3.43 us
    ppermute x6, waiting for transfers between devices, swap_core(): return lax.ppermute(value, 'seq', [(i, i ^ 1) for i in range(n_seq)])  2.77 us
    pallas_call x1, Pallas kernels, select(): pl.pallas_call(select_kernel, in_specs=[pl.BlockSpec(memory_space=pltpu.H...  2.75 us
    pallas_call x1, Pallas kernels, gradients(): pl.pallas_call(functools.partial(gradient_kernel, n_seq, n_vocab), in_spe...  1.64 us
  transfers between devices with their start and end apart: 19, of which 13 were waited for; matrix products, arithmetic and copies ran while one was open for 1% of the time, Pallas kernels for 2%

profile of v14, /device:TPU:0, one launch (start us, length us, event | category | flops | bytes accessed | tf_op | source)
XLA Modules:
  0.0 59.4 jit_solution(7072336630330694774)
XLA Ops:
  0.6 2.8 %select_rows.1 = (bf16[16,4096]{1,0:T(8,128)(2,1)S(1)}, bf16[16,4096]{1,0:T(8,128)(2,1)S(1)}, bf16[16,128]{1,0:T(8,128)(2,1)S(1)}) custom-call(s32[1,128]{1,0:T(1,128)} %bitcast.46, bf16[128,8192]{1,0:T(8,128)(2,1)} %hidden_ref.1), custom_call_target="tpu_custom_call" | custom-call | tf_op jit(solution)/shard_map/select_rows/pallas_call | solution.py:91
  3.4 3.0 %collective-permute-start = (bf16[16,4096]{1,0:T(8,128)(2,1)S(1)}, bf16[16,4096]{1,0:T(8,128)(2,1)S(1)}, u32[]{:S(2)}, u32[]{:S(2)}) collective-permute-start(bf16[16,4096]{1,0:T(8,128)(2,1)S(1)} %get-tuple-element.23.refs_0_), channel_id=1, source_target_pairs={{0,8},{4,20},{8,0},{12,28},{16,24},{20,4},{24,16},{28,12},{1,9},{5... | collective-permute-start | bytes 393224 | tf_op jit(solution)/shard_map/ppermute | solution.py:288
  6.4 0.1 collective-permute-start.2
  6.5 0.2 join_parts.1
  6.7 2.0 %collective-permute-start.1 = (bf16[16,8192]{1,0:T(8,128)(2,1)S(1)}, bf16[16,8192]{1,0:T(8,128)(2,1)S(1)}, u32[]{:S(2)}, u32[]{:S(2)}) collective-permute-start(bf16[16,8192]{1,0:T(8,128)(2,1)S(1)} %join_parts.1), channel_id=1, source_target_pairs={{0,16},{4,12},{8,24},{12,4},{16,0},{20,28},{24,8},{28,20},{1,17},{... | collective-permute-start | bytes 786440 | tf_op jit(solution)/shard_map/ppermute | solution.py:288
  8.7 1.1 %collective-permute-done = bf16[16,4096]{1,0:T(8,128)(2,1)S(1)} collective-permute-done((bf16[16,4096]{1,0:T(8,128)(2,1)S(1)}, bf16[16,4096]{1,0:T(8,128)(2,1)S(1)}, u32[]{:S(2)}, u32[]{:S(2)}) %collective-permute-start) | collective-permute-done | bytes 131104 | tf_op jit(solution)/shard_map/ppermute | solution.py:288
  9.8 2.5 %collective-permute-start.3 = (bf16[16,4096]{1,0:T(8,128)(2,1)S(1)}, bf16[16,4096]{1,0:T(8,128)(2,1)S(1)}, u32[]{:S(2)}, u32[]{:S(2)}) collective-permute-start(bf16[16,4096]{1,0:T(8,128)(2,1)S(1)} %collective-permute-done), channel_id=1, source_target_pairs={{0,16},{4,12},{8,24},{12,4},{16,0},{20,28},{24,8},{28,20},{1,17},{... | collective-permute-start | bytes 393224 | tf_op jit(solution)/shard_map/ppermute | solution.py:288
  12.3 0.5 collective-permute-done.2
  12.8 2.3 %collective-permute-start.5 = (bf16[16,4096]{1,0:T(8,128)(2,1)S(1)}, bf16[16,4096]{1,0:T(8,128)(2,1)S(1)}, u32[]{:S(2)}, u32[]{:S(2)}) collective-permute-start(bf16[16,4096]{1,0:T(8,128)(2,1)S(1)} %collective-permute-done.2), channel_id=1, source_target_pairs={{0,16},{4,12},{8,24},{12,4},{16,0},{20,28},{24,8},{28,20},{1,17},{... | collective-permute-start | bytes 393224 | tf_op jit(solution)/shard_map/ppermute | solution.py:288
  15.1 0.0 collective-permute-done.1
  15.2 0.0 collective-permute-done.3
  15.2 0.0 collective-permute-start.4
  15.3 2.7 %collective-permute-done.5 = bf16[16,4096]{1,0:T(8,128)(2,1)S(1)} collective-permute-done((bf16[16,4096]{1,0:T(8,128)(2,1)S(1)}, bf16[16,4096]{1,0:T(8,128)(2,1)S(1)}, u32[]{:S(2)}, u32[]{:S(2)}) %collective-permute-start.5) | collective-permute-done | bytes 131104 | tf_op jit(solution)/shard_map/ppermute | solution.py:288
  18.1 0.1 collective-permute-start.6
  18.1 1.5 %collective-permute-done.6.refs_3_ = bf16[32,4096]{1,0:T(8,128)(2,1)S(1)} collective-permute-done((bf16[32,4096]{1,0:T(8,128)(2,1)S(1)}, bf16[32,4096]{1,0:T(8,128)(2,1)S(1)}, u32[]{:S(2)}, u32[]{:S(2)}) %collective-permute-start.6) | collective-permute-done | bytes 262176 | tf_op jit(solution)/shard_map/ppermute | solution.py:284
  19.7 0.0 collective-permute-done.4.refs_1_
  19.7 1.0 %local_logits.1 = (f32[128,256]{1,0:T(8,128)S(1)}, f32[32,4,128]{2,1,0:T(4,128)S(1)}) custom-call(bf16[96,4096]{1,0:T(8,128)(2,1)S(1)} %slice_dynamic-update-slice_fusion.refs_0_, bf16[96,4096]{1,0:T(8,128)(2,1)S(1)} %collective-permute-done.4.refs_1_, bf16[32,4096]{1,0:T(8,128)(2,1)S(1)} %constant_dynamic-update-slice_fusion.4.refs_2_, ...), custom_call_target="tpu_custom_call" | custom-call | tf_op jit(solution)/shard_map/local_logits/pallas_call | solution.py:173
  20.6 13.7 %all_to_all.5.stats_ref = f32[32,4,128]{2,1,0:T(4,128)S(1)} all-to-all(f32[32,4,128]{2,1,0:T(4,128)S(1)} %get-tuple-element.28), channel_id=1, replica_groups=mesh['seq'=8,'vocab'=4] {'seq','vocab'}, dimensions={0} | all-to-all | bytes 131072 | tf_op jit(solution)/shard_map/all_to_all | solution.py:310
  34.3 1.6 %gradients.1 = (bf16[4,4,16,1024]{3,2,1,0:T(8,128)(2,1)S(1)}, bf16[4,4,16,1024]{3,2,1,0:T(8,128)(2,1)S(1)}, bf16[3,4,16,1024]{3,2,1,0:T(8,128)(2,1)S(1)}, bf16[3...) custom-call(f32[32,4,128]{2,1,0:T(4,128)S(1)} %all_to_all.5.stats_ref, ...), custom_call_target="tpu_custom_call" | custom-call | tf_op jit(solution)/shard_map/gradients/pallas_call | solution.py:264
  35.9 0.1 collective-permute-start.7
  36.0 0.5 collective-permute-start.8
  36.5 0.8 %collective-permute-done.7 = bf16[4,16,1024]{2,1,0:T(8,128)(2,1)S(1)} collective-permute-done((bf16[4,16,1024]{2,1,0:T(8,128)(2,1)S(1)}, bf16[4,16,1024]{2,1,0:T(8,128)(2,1)S(1)}, u32[]{:S(2)}, u32[]{:S(2)}) %collective-permute-start.7) | collective-permute-done | bytes 131104 | tf_op jit(solution)/shard_map/ppermute | solution.py:284
  37.3 0.2 collective-permute-done.8
  37.5 0.3 collective-permute-start.9
  37.9 0.7 %collective-permute-start.12 = (bf16[4,16,1024]{2,1,0:T(8,128)(2,1)S(1)}, bf16[4,16,1024]{2,1,0:T(8,128)(2,1)S(1)}, u32[]{:S(2)}, u32[]{:S(2)}) collective-permute-start(bf16[4,16,1024]{2,1,0:T(8,128)(2,1)S(1)} %fusion.1), channel_id=1, source_target_pairs={{0,16},{4,12},{8,24},{12,4},{16,0},{20,28},{24,8},{28,20},{1,17},{... | collective-permute-start | bytes 393224 | tf_op jit(solution)/shard_map/ppermute | solution.py:288
  38.6 0.0 collective-permute-start.10
  38.7 1.4 %collective-permute-start.14 = (bf16[4,16,1024]{2,1,0:T(8,128)(2,1)S(1)}, bf16[4,16,1024]{2,1,0:T(8,128)(2,1)S(1)}, u32[]{:S(2)}, u32[]{:S(2)}) collective-permute-start(bf16[4,16,1024]{2,1,0:T(8,128)(2,1)S(1)} %fusion), channel_id=1, source_target_pairs={{0,16},{4,12},{8,24},{12,4},{16,0},{20,28},{24,8},{28,20},{1,17},{... | collective-permute-start | bytes 393224 | tf_op jit(solution)/shard_map/ppermute | solution.py:288
  40.1 0.0 collective-permute-done.9
  40.1 0.2 collective-permute-done.10
  40.4 1.4 %collective-permute-start.11 = (bf16[4,16,2048]{2,1,0:T(8,128)(2,1)S(1)}, bf16[4,16,2048]{2,1,0:T(8,128)(2,1)S(1)}, u32[]{:S(2)}, u32[]{:S(2)}) collective-permute-start(bf16[4,16,2048]{2,1,0:T(8,128)(2,1)S(1)} %pad_maximum_fusion), channel_id=1, source_target_pairs={{0,16},{4,12},{8,24},{12,4},{16,0},{20,28},{24,8},{28,20},{1,17},{... | collective-permute-start | bytes 786440 | tf_op jit(solution)/shard_map/ppermute | solution.py:288
  41.8 1.1 %collective-permute-done.12 = bf16[4,16,1024]{2,1,0:T(8,128)(2,1)S(1)} collective-permute-done((bf16[4,16,1024]{2,1,0:T(8,128)(2,1)S(1)}, bf16[4,16,1024]{2,1,0:T(8,128)(2,1)S(1)}, u32[]{:S(2)}, u32[]{:S(2)}) %collective-permute-start.12) | collective-permute-done | bytes 131104 | tf_op jit(solution)/shard_map/ppermute | solution.py:288
  42.9 0.1 fusion.4
  43.0 0.7 %collective-permute-start.13 = (bf16[4,16,1024]{2,1,0:T(8,128)(2,1)S(1)}, bf16[4,16,1024]{2,1,0:T(8,128)(2,1)S(1)}, u32[]{:S(2)}, u32[]{:S(2)}) collective-permute-start(bf16[4,16,1024]{2,1,0:T(8,128)(2,1)S(1)} %fusion.4), channel_id=1, source_target_pairs={{0,8},{4,20},{8,0},{12,28},{16,24},{20,4},{24,16},{28,12},{1,9},{5... | collective-permute-start | bytes 393224 | tf_op jit(solution)/shard_map/ppermute | solution.py:288
  43.7 0.6 %collective-permute-done.14 = bf16[4,16,1024]{2,1,0:T(8,128)(2,1)S(1)} collective-permute-done((bf16[4,16,1024]{2,1,0:T(8,128)(2,1)S(1)}, bf16[4,16,1024]{2,1,0:T(8,128)(2,1)S(1)}, u32[]{:S(2)}, u32[]{:S(2)}) %collective-permute-start.14) | collective-permute-done | bytes 131104 | tf_op jit(solution)/shard_map/ppermute | solution.py:288
  44.3 0.1 fusion.2
  44.4 0.8 %collective-permute-start.15 = (bf16[4,16,1024]{2,1,0:T(8,128)(2,1)S(1)}, bf16[4,16,1024]{2,1,0:T(8,128)(2,1)S(1)}, u32[]{:S(2)}, u32[]{:S(2)}) collective-permute-start(bf16[4,16,1024]{2,1,0:T(8,128)(2,1)S(1)} %fusion.2), channel_id=1, source_target_pairs={{0,8},{4,20},{8,0},{12,28},{16,24},{20,4},{24,16},{28,12},{1,9},{5... | collective-permute-start | bytes 393224 | tf_op jit(solution)/shard_map/ppermute | solution.py:288
  45.2 2.8 %collective-permute-done.13 = bf16[4,16,1024]{2,1,0:T(8,128)(2,1)S(1)} collective-permute-done((bf16[4,16,1024]{2,1,0:T(8,128)(2,1)S(1)}, bf16[4,16,1024]{2,1,0:T(8,128)(2,1)S(1)}, u32[]{:S(2)}, u32[]{:S(2)}) %collective-permute-start.13) | collective-permute-done | bytes 131104 | tf_op jit(solution)/shard_map/ppermute | solution.py:288
  48.0 1.4 %collective-permute-done.15 = bf16[4,16,1024]{2,1,0:T(8,128)(2,1)S(1)} collective-permute-done((bf16[4,16,1024]{2,1,0:T(8,128)(2,1)S(1)}, bf16[4,16,1024]{2,1,0:T(8,128)(2,1)S(1)}, u32[]{:S(2)}, u32[]{:S(2)}) %collective-permute-start.15) | collective-permute-done | bytes 131104 | tf_op jit(solution)/shard_map/ppermute | solution.py:288
  49.4 0.0 collective-permute-done.11
  49.4 0.2 fusion.3
  49.7 0.9 %collective-permute-start.16 = (bf16[16,2048]{1,0:T(8,128)(2,1)S(1)}, bf16[16,2048]{1,0:T(8,128)(2,1)S(1)}, u32[]{:S(2)}, u32[]{:S(2)}) collective-permute-start(bf16[16,2048]{1,0:T(8,128)(2,1)S(1)} %pad_maximum_fusion.1), channel_id=1, source_target_pairs={{0,3},{1,2},{2,1},{3,0},{4,7},{5,6},{6,5},{7,4},{8,11},{9,10},{10,... | collective-permute-start | bytes 196616 | tf_op jit(solution)/shard_map/ppermute | solution.py:291
  50.6 0.9 %collective-permute-start.17 = (bf16[16,2048]{1,0:T(8,128)(2,1)S(1)}, bf16[16,2048]{1,0:T(8,128)(2,1)S(1)}, u32[]{:S(2)}, u32[]{:S(2)}) collective-permute-start(bf16[16,2048]{1,0:T(8,128)(2,1)S(1)} %pad_maximum_fusion.2), channel_id=1, source_target_pairs={{0,2},{1,3},{2,0},{3,1},{4,6},{5,7},{6,4},{7,5},{8,10},{9,11},{10,... | collective-permute-start | bytes 196616 | tf_op jit(solution)/shard_map/ppermute | solution.py:291
  51.4 2.7 %collective-permute-start.18 = (bf16[16,2048]{1,0:T(8,128)(2,1)S(1)}, bf16[16,2048]{1,0:T(8,128)(2,1)S(1)}, u32[]{:S(2)}, u32[]{:S(2)}) collective-permute-start(bf16[16,2048]{1,0:T(8,128)(2,1)S(1)} %pad_maximum_fusion.3), channel_id=1, source_target_pairs={{0,1},{1,0},{2,3},{3,2},{4,5},{5,4},{6,7},{7,6},{8,9},{9,8},{10,11... | collective-permute-start | bytes 196616 | tf_op jit(solution)/shard_map/ppermute | solution.py:291
  54.1 0.8 %entropies.1 = (f32[1,128]{1,0:T(1,128)}, f32[1,1]{1,0:T(1,128)}) custom-call(f32[32,4,128]{2,1,0:T(4,128)S(1)} %all_to_all.5.stats_ref, bf16[16,128]{1,0:T(8,128)(2,1)S(1)} %get-tuple-element.27.refs_5_.picker_ref), custom_call_target="tpu_custom_call" | custom-call | tf_op jit(solution)/shard_map/entropies/pallas_call | solution.py:213
  54.9 1.6 %collective-permute-done.16 = bf16[16,2048]{1,0:T(8,128)(2,1)S(1)} collective-permute-done((bf16[16,2048]{1,0:T(8,128)(2,1)S(1)}, bf16[16,2048]{1,0:T(8,128)(2,1)S(1)}, u32[]{:S(2)}, u32[]{:S(2)}) %collective-permute-start.16) | collective-permute-done | bytes 65568 | tf_op jit(solution)/shard_map/ppermute | solution.py:291
  56.5 1.8 %collective-permute-done.17 = bf16[16,2048]{1,0:T(8,128)(2,1)S(1)} collective-permute-done((bf16[16,2048]{1,0:T(8,128)(2,1)S(1)}, bf16[16,2048]{1,0:T(8,128)(2,1)S(1)}, u32[]{:S(2)}, u32[]{:S(2)}) %collective-permute-start.17) | collective-permute-done | bytes 65568 | tf_op jit(solution)/shard_map/ppermute | solution.py:291
  58.3 0.0 collective-permute-done.18
  58.3 1.1 %convolution_convert_fusion = bf16[128,2048]{1,0:T(8,128)(2,1)} fusion(bf16[16,128]{1,0:T(8,128)(2,1)S(1)} %get-tuple-element.27.refs_5_.picker_ref, f32[16,1024]{1,0:T(8,128)S(1)} %get-tuple-element.51, f32[16,1024]{1,0:T(8,128)S(1)} %get-tuple-element.52, bf16[16,2048]{1,0:T(8,128)(2,1)S(1)} %collective-permute-done.18, ...), kind=kOutput, calls=%fused_computation | convolution fusion | flops 8912896 | bytes 856064 | tf_op jit(solution)/shard_map/dot_general | solution.py:345
  (20 shorter events, 0.3 us)
Async XLA Ops:
  0.6 19.0 %copy-start = (bf16[8192,256]{1,0:T(8,128)(2,1)S(1)}, bf16[8192,256]{1,0:T(8,128)(2,1)}, u32[]{:S(2)}) copy-start(bf16[8192,256]{1,0:T(8,128)(2,1)} %head_ref.1) | copy-start | bytes 12582916
  3.4 6.4 %collective-permute-start = (bf16[16,4096]{1,0:T(8,128)(2,1)S(1)}, bf16[16,4096]{1,0:T(8,128)(2,1)S(1)}, u32[]{:S(2)}, u32[]{:S(2)}) collective-permute-start(bf16[16,4096]{1,0:T(8,128)(2,1)S(1)} %get-tuple-element.23.refs_0_), channel_id=1, source_target_pairs={{0,8},{4,20},{8,0},{12,28},{16,24},{20,4},{24,16},{28,12},{1,9},{5... | collective-permute-start | bytes 393224 | tf_op jit(solution)/shard_map/ppermute | solution.py:288
  6.4 6.4 %collective-permute-start.2 = (bf16[16,4096]{1,0:T(8,128)(2,1)S(1)}, bf16[16,4096]{1,0:T(8,128)(2,1)S(1)}, u32[]{:S(2)}, u32[]{:S(2)}) collective-permute-start(bf16[16,4096]{1,0:T(8,128)(2,1)S(1)} %get-tuple-element.24.refs_1_), channel_id=1, source_target_pairs={{0,8},{4,20},{8,0},{12,28},{16,24},{20,4},{24,16},{28,12},{1,9},{5... | collective-permute-start | bytes 393224 | tf_op jit(solution)/shard_map/ppermute | solution.py:288
  6.7 8.5 %collective-permute-start.1 = (bf16[16,8192]{1,0:T(8,128)(2,1)S(1)}, bf16[16,8192]{1,0:T(8,128)(2,1)S(1)}, u32[]{:S(2)}, u32[]{:S(2)}) collective-permute-start(bf16[16,8192]{1,0:T(8,128)(2,1)S(1)} %join_parts.1), channel_id=1, source_target_pairs={{0,16},{4,12},{8,24},{12,4},{16,0},{20,28},{24,8},{28,20},{1,17},{... | collective-permute-start | bytes 786440 | tf_op jit(solution)/shard_map/ppermute | solution.py:288
  9.8 5.4 %collective-permute-start.3 = (bf16[16,4096]{1,0:T(8,128)(2,1)S(1)}, bf16[16,4096]{1,0:T(8,128)(2,1)S(1)}, u32[]{:S(2)}, u32[]{:S(2)}) collective-permute-start(bf16[16,4096]{1,0:T(8,128)(2,1)S(1)} %collective-permute-done), channel_id=1, source_target_pairs={{0,16},{4,12},{8,24},{12,4},{16,0},{20,28},{24,8},{28,20},{1,17},{... | collective-permute-start | bytes 393224 | tf_op jit(solution)/shard_map/ppermute | solution.py:288
  12.8 5.3 %collective-permute-start.5 = (bf16[16,4096]{1,0:T(8,128)(2,1)S(1)}, bf16[16,4096]{1,0:T(8,128)(2,1)S(1)}, u32[]{:S(2)}, u32[]{:S(2)}) collective-permute-start(bf16[16,4096]{1,0:T(8,128)(2,1)S(1)} %collective-permute-done.2), channel_id=1, source_target_pairs={{0,16},{4,12},{8,24},{12,4},{16,0},{20,28},{24,8},{28,20},{1,17},{... | collective-permute-start | bytes 393224 | tf_op jit(solution)/shard_map/ppermute | solution.py:288
  15.2 4.4 %collective-permute-start.4 = (bf16[96,4096]{1,0:T(8,128)(2,1)S(1)}, bf16[96,4096]{1,0:T(8,128)(2,1)S(1)}, u32[]{:S(2)}, u32[]{:S(2)}) collective-permute-start(bf16[96,4096]{1,0:T(8,128)(2,1)S(1)} %slice_dynamic-update-slice_fusion.refs_0_), channel_id=1, source_target_pairs={{0,4},{4,0},{8,12},{12,8},{16,20},{20,16},{24,28},{28,24},{1,5},{5... | collective-permute-start | bytes 2359304 | tf_op jit(solution)/shard_map/ppermute | solution.py:284
  18.1 1.6 %collective-permute-start.6 = (bf16[32,4096]{1,0:T(8,128)(2,1)S(1)}, bf16[32,4096]{1,0:T(8,128)(2,1)S(1)}, u32[]{:S(2)}, u32[]{:S(2)}) collective-permute-start(bf16[32,4096]{1,0:T(8,128)(2,1)S(1)} %constant_dynamic-update-slice_fusion.4.refs_2_), channel_id=1, source_target_pairs={{0,4},{4,0},{8,12},{12,8},{16,20},{20,16},{24,28},{28,24},{1,5},{5... | collective-permute-start | bytes 786440 | tf_op jit(solution)/shard_map/ppermute | solution.py:284
  35.9 1.4 %collective-permute-start.7 = (bf16[4,16,1024]{2,1,0:T(8,128)(2,1)S(1)}, bf16[4,16,1024]{2,1,0:T(8,128)(2,1)S(1)}, u32[]{:S(2)}, u32[]{:S(2)}) collective-permute-start(bf16[4,16,1024]{2,1,0:T(8,128)(2,1)S(1)} %get-tuple-element.33), channel_id=1, source_target_pairs={{0,4},{4,0},{8,12},{12,8},{16,20},{20,16},{24,28},{28,24},{1,5},{5... | collective-permute-start | bytes 393224 | tf_op jit(solution)/shard_map/ppermute | solution.py:284
  36.0 1.5 %collective-permute-start.8 = (bf16[4,16,1024]{2,1,0:T(8,128)(2,1)S(1)}, bf16[4,16,1024]{2,1,0:T(8,128)(2,1)S(1)}, u32[]{:S(2)}, u32[]{:S(2)}) collective-permute-start(bf16[4,16,1024]{2,1,0:T(8,128)(2,1)S(1)} %get-tuple-element.34), channel_id=1, source_target_pairs={{0,4},{4,0},{8,12},{12,8},{16,20},{20,16},{24,28},{28,24},{1,5},{5... | collective-permute-start | bytes 393224 | tf_op jit(solution)/shard_map/ppermute | solution.py:284
  37.5 2.6 %collective-permute-start.9 = (bf16[3,4,16,1024]{3,2,1,0:T(8,128)(2,1)S(1)}, bf16[3,4,16,1024]{3,2,1,0:T(8,128)(2,1)S(1)}, u32[]{:S(2)}, u32[]{:S(2)}) collective-permute-start(bf16[3,4,16,1024]{3,2,1,0:T(8,128)(2,1)S(1)} %get-tuple-element.35), channel_id=1, source_target_pairs={{0,4},{4,0},{8,12},{12,8},{16,20},{20,16},{24,28},{28,24},{1,5},{5... | collective-permute-start | bytes 1179656 | tf_op jit(solution)/shard_map/ppermute | solution.py:284
  37.9 5.0 %collective-permute-start.12 = (bf16[4,16,1024]{2,1,0:T(8,128)(2,1)S(1)}, bf16[4,16,1024]{2,1,0:T(8,128)(2,1)S(1)}, u32[]{:S(2)}, u32[]{:S(2)}) collective-permute-start(bf16[4,16,1024]{2,1,0:T(8,128)(2,1)S(1)} %fusion.1), channel_id=1, source_target_pairs={{0,16},{4,12},{8,24},{12,4},{16,0},{20,28},{24,8},{28,20},{1,17},{... | collective-permute-start | bytes 393224 | tf_op jit(solution)/shard_map/ppermute | solution.py:288
  38.6 1.7 %collective-permute-start.10 = (bf16[3,4,16,1024]{3,2,1,0:T(8,128)(2,1)S(1)}, bf16[3,4,16,1024]{3,2,1,0:T(8,128)(2,1)S(1)}, u32[]{:S(2)}, u32[]{:S(2)}) collective-permute-start(bf16[3,4,16,1024]{3,2,1,0:T(8,128)(2,1)S(1)} %get-tuple-element.37), channel_id=1, source_target_pairs={{0,4},{4,0},{8,12},{12,8},{16,20},{20,16},{24,28},{28,24},{1,5},{5... | collective-permute-start | bytes 1179656 | tf_op jit(solution)/shard_map/ppermute | solution.py:284
  38.7 5.7 %collective-permute-start.14 = (bf16[4,16,1024]{2,1,0:T(8,128)(2,1)S(1)}, bf16[4,16,1024]{2,1,0:T(8,128)(2,1)S(1)}, u32[]{:S(2)}, u32[]{:S(2)}) collective-permute-start(bf16[4,16,1024]{2,1,0:T(8,128)(2,1)S(1)} %fusion), channel_id=1, source_target_pairs={{0,16},{4,12},{8,24},{12,4},{16,0},{20,28},{24,8},{28,20},{1,17},{... | collective-permute-start | bytes 393224 | tf_op jit(solution)/shard_map/ppermute | solution.py:288
  40.4 9.0 %collective-permute-start.11 = (bf16[4,16,2048]{2,1,0:T(8,128)(2,1)S(1)}, bf16[4,16,2048]{2,1,0:T(8,128)(2,1)S(1)}, u32[]{:S(2)}, u32[]{:S(2)}) collective-permute-start(bf16[4,16,2048]{2,1,0:T(8,128)(2,1)S(1)} %pad_maximum_fusion), channel_id=1, source_target_pairs={{0,16},{4,12},{8,24},{12,4},{16,0},{20,28},{24,8},{28,20},{1,17},{... | collective-permute-start | bytes 786440 | tf_op jit(solution)/shard_map/ppermute | solution.py:288
  43.0 5.0 %collective-permute-start.13 = (bf16[4,16,1024]{2,1,0:T(8,128)(2,1)S(1)}, bf16[4,16,1024]{2,1,0:T(8,128)(2,1)S(1)}, u32[]{:S(2)}, u32[]{:S(2)}) collective-permute-start(bf16[4,16,1024]{2,1,0:T(8,128)(2,1)S(1)} %fusion.4), channel_id=1, source_target_pairs={{0,8},{4,20},{8,0},{12,28},{16,24},{20,4},{24,16},{28,12},{1,9},{5... | collective-permute-start | bytes 393224 | tf_op jit(solution)/shard_map/ppermute | solution.py:288
  44.4 5.0 %collective-permute-start.15 = (bf16[4,16,1024]{2,1,0:T(8,128)(2,1)S(1)}, bf16[4,16,1024]{2,1,0:T(8,128)(2,1)S(1)}, u32[]{:S(2)}, u32[]{:S(2)}) collective-permute-start(bf16[4,16,1024]{2,1,0:T(8,128)(2,1)S(1)} %fusion.2), channel_id=1, source_target_pairs={{0,8},{4,20},{8,0},{12,28},{16,24},{20,4},{24,16},{28,12},{1,9},{5... | collective-permute-start | bytes 393224 | tf_op jit(solution)/shard_map/ppermute | solution.py:288
  49.7 6.9 %collective-permute-start.16 = (bf16[16,2048]{1,0:T(8,128)(2,1)S(1)}, bf16[16,2048]{1,0:T(8,128)(2,1)S(1)}, u32[]{:S(2)}, u32[]{:S(2)}) collective-permute-start(bf16[16,2048]{1,0:T(8,128)(2,1)S(1)} %pad_maximum_fusion.1), channel_id=1, source_target_pairs={{0,3},{1,2},{2,1},{3,0},{4,7},{5,6},{6,5},{7,4},{8,11},{9,10},{10,... | collective-permute-start | bytes 196616 | tf_op jit(solution)/shard_map/ppermute | solution.py:291
  50.6 7.8 %collective-permute-start.17 = (bf16[16,2048]{1,0:T(8,128)(2,1)S(1)}, bf16[16,2048]{1,0:T(8,128)(2,1)S(1)}, u32[]{:S(2)}, u32[]{:S(2)}) collective-permute-start(bf16[16,2048]{1,0:T(8,128)(2,1)S(1)} %pad_maximum_fusion.2), channel_id=1, source_target_pairs={{0,2},{1,3},{2,0},{3,1},{4,6},{5,7},{6,4},{7,5},{8,10},{9,11},{10,... | collective-permute-start | bytes 196616 | tf_op jit(solution)/shard_map/ppermute | solution.py:291
  51.4 6.9 %collective-permute-start.18 = (bf16[16,2048]{1,0:T(8,128)(2,1)S(1)}, bf16[16,2048]{1,0:T(8,128)(2,1)S(1)}, u32[]{:S(2)}, u32[]{:S(2)}) collective-permute-start(bf16[16,2048]{1,0:T(8,128)(2,1)S(1)} %pad_maximum_fusion.3), channel_id=1, source_target_pairs={{0,1},{1,0},{2,3},{3,2},{4,5},{5,4},{6,7},{7,6},{8,9},{9,8},{10,11... | collective-permute-start | bytes 196616 | tf_op jit(solution)/shard_map/ppermute | solution.py:291

commit v15 on v11

--- a/solution.py
+++ b/solution.py
@@ -104,22 +104,45 @@
     return own, picker
 
 
+def own_kernel(*refs):
+    *part_refs, head_ref, out_ref = refs
+    total = None
+    size = part_refs[0].shape[1]
+    for c, ref in enumerate(part_refs):
+        head = head_ref[c * size : (c + 1) * size, :]
+        part = jnp.dot(ref[...], head, preferred_element_type=F32)
+        total = part if total is None else total + part
+    out_ref[...] = total
+
+
+def own_logits(own, head):
+    return pl.pallas_call(
+        own_kernel,
+        in_specs=[pl.BlockSpec(memory_space=pltpu.VMEM)] * (len(own) + 1),
+        out_shape=jax.ShapeDtypeStruct((ACT_DEV, head.shape[1]), F32),
+        compiler_params=params(),
+        name="own_logits",
+    )(*own, head)
+
+
 def logits_kernel(n_seq, *refs):
-    *block_refs, head_ref, picker_ref, logits_ref, stats_ref, packed = refs
+    own_ref, *block_refs, head_ref, picker_ref, logits_ref, stats_ref, packed = refs
     step = head_ref.shape[0] // CHUNKS
     each = CHUNKS // PARTS
     logits = None
     for i in range(CHUNKS):
         at = (i % each) * step
         rows = []
-        for ref in block_refs:
+        for k, ref in enumerate(block_refs):
             size = ref.shape[0] // PARTS
             start = (i // each) * size
-            rows.append(ref[start : start + size, at : at + step])
+            first = start + ACT_DEV if k == 0 else start
+            rows.append(ref[first : start + size, at : at + step])
         rows = jnp.concatenate(rows, axis=0)
         head = head_ref[i * step : (i + 1) * step, :]
         part = jnp.dot(rows, head, preferred_element_type=F32)
         logits = part if logits is None else logits + part
+    logits = jnp.concatenate([own_ref[...], logits], axis=0)
     logits_ref[...] = logits
     top = jnp.max(logits, axis=1, keepdims=True)
     away = logits - top
@@ -140,12 +163,12 @@
     stats_ref[...] = jnp.broadcast_to(lines[None], stats_ref.shape)
 
 
-def local_logits(n_seq, n_vocab, blocks, head, picker):
+def local_logits(n_seq, n_vocab, mine, blocks, head, picker):
     shard = head.shape[1]
     rows, lanes = n_seq * ACT_DEV, lanes_of(n_seq)
     return pl.pallas_call(
         functools.partial(logits_kernel, n_seq),
-        in_specs=[pl.BlockSpec(memory_space=pltpu.VMEM)] * 6,
+        in_specs=[pl.BlockSpec(memory_space=pltpu.VMEM)] * 7,
         out_shape=[
             jax.ShapeDtypeStruct((rows, shard), F32),
             jax.ShapeDtypeStruct((n_seq * n_vocab, 4, lanes), F32),
@@ -153,7 +176,7 @@
         scratch_shapes=[pltpu.VMEM((lanes, LANES), F32)],
         compiler_params=params(),
         name="local_logits",
-    )(*blocks, head, picker)
+    )(mine, *blocks, head, picker)
 
 
 def merged(stats):
@@ -266,11 +289,13 @@
     own, picker = select(mask, hidden)
 
     near = [own]
+    mine = own_logits(own, head)
     for a in range(1, n_chip):
         step = a.bit_length() - 1
         source = near[a ^ (1 << step)]
         if a > 1 and a == 1 << step:
-            moved = swap_chip(jnp.concatenate(source, axis=1), step)
+            source, mine = lax.optimization_barrier((jnp.concatenate(source, axis=1), mine))
+            moved = swap_chip(source, step)
             near.append(jnp.split(moved, PARTS, axis=1))
         else:
             near.append([swap_chip(part, step) for part in source])
@@ -279,7 +304,7 @@
     late = jnp.concatenate(near[last], axis=0)
     blocks = [early, swap_core(early), late, swap_core(late)]
 
-    logits, stats = local_logits(n_seq, n_vocab, blocks, head, picker)
+    logits, stats = local_logits(n_seq, n_vocab, mine, blocks, head, picker)
     stats = lax.all_to_all(stats, ("seq", "vocab"), 0, 0, tiled=True)
     near, far, far_last = gradients(n_seq, n_vocab, stats, logits, head)
     moved = [swap_core(part) for part in far_last]

time: 59.8 us -> 59.9 us (level)
  starting transfers between devices: 20.7 us -> 17.7 us
  local copies, waits for them, and re-layouts: 0.13 us -> 2.31 us
    ppermute x10, starting transfers between devices: 15.2 us -> 12.3 us  [swap_chip(): lax.ppermute(value, 'seq', [(i, i ^ flips[i & 1]) for i in range(n_seq)])]
    unnamed x8 -> x10, local copies, waits for them, and re-layouts: 0.07 us -> 2.25 us
    pallas_call x0 -> x1, Pallas kernels: none -> 0.65 us  [own_logits(): pl.pallas_call(own_kernel, in_specs=[pl.BlockSpec(memory_space=pltpu.VMEM...]
  transfers between devices with their start and end apart: 19 -> 19, of which waited for: 13 -> 13; matrix products, arithmetic and copies ran while one was open for 1% -> 1% of each run, Pallas kernels for 1% -> 2%
where the time goes in v15:
time: 59.9 us; the launch traced here: 59.7 us
  starting transfers between devices  17.7 us (30%)
  waiting for transfers between devices  17.1 us (29%)
  blocking collectives  13.6 us (23%)
  Pallas kernels  6.59 us (11%)
  local copies, waits for them, and re-layouts  2.31 us (4%)
  matrix products  1.11 us (2%)
  between operations  0.8 us (1%)
    all_to_all x1, blocking collectives, body(): stats = lax.all_to_all(stats, ('seq', 'vocab'), 0, 0, tiled=True)  13.6 us
    ppermute x10, starting transfers between devices, swap_chip(): lax.ppermute(value, 'seq', [(i, i ^ flips[i & 1]) for i in range(n_seq)])  12.3 us
    ppermute x10, waiting for transfers between devices, swap_chip(): lax.ppermute(value, 'seq', [(i, i ^ flips[i & 1]) for i in range(n_seq)])  10.9 us
    ppermute x3, starting transfers between devices, send_vocab(): return lax.ppermute(value, 'vocab', [(i, i ^ k) for i in range(n_vocab)])  4.45 us
    ppermute x3, waiting for transfers between devices, send_vocab(): return lax.ppermute(value, 'vocab', [(i, i ^ k) for i in range(n_vocab)])  3.42 us
    ppermute x6, waiting for transfers between devices, swap_core(): return lax.ppermute(value, 'seq', [(i, i ^ 1) for i in range(n_seq)])  2.76 us
    pallas_call x1, Pallas kernels, select(): pl.pallas_call(select_kernel, in_specs=[pl.BlockSpec(memory_space=pltpu.H...  2.47 us
    unnamed x10, local copies, waits for them, and re-layouts  2.25 us
  transfers between devices with their start and end apart: 19, of which 13 were waited for; matrix products, arithmetic and copies ran while one was open for 1% of the time, Pallas kernels for 2%

profile of v15, /device:TPU:0, one launch (start us, length us, event | category | flops | bytes accessed | tf_op | source)
XLA Modules:
  0.0 59.7 jit_solution(13226521547228984260)
XLA Ops:
  0.6 2.5 %select_rows.1 = (bf16[16,4096]{1,0:T(8,128)(2,1)S(1)}, bf16[16,4096]{1,0:T(8,128)(2,1)S(1)}, bf16[16,128]{1,0:T(8,128)(2,1)S(1)}) custom-call(s32[1,128]{1,0:T(1,128)} %bitcast.46, bf16[128,8192]{1,0:T(8,128)(2,1)} %hidden_ref.1), custom_call_target="tpu_custom_call" | custom-call | tf_op jit(solution)/shard_map/select_rows/pallas_call | solution.py:91
  3.1 3.0 %collective-permute-start = (bf16[16,4096]{1,0:T(8,128)(2,1)S(1)}, bf16[16,4096]{1,0:T(8,128)(2,1)S(1)}, u32[]{:S(2)}, u32[]{:S(2)}) collective-permute-start(bf16[16,4096]{1,0:T(8,128)(2,1)S(1)} %get-tuple-element.25.refs_0_), channel_id=1, source_target_pairs={{0,8},{4,20},{8,0},{12,28},{16,24},{20,4},{24,16},{28,12},{1,9},{5... | collective-permute-start | bytes 393224 | tf_op jit(solution)/shard_map/ppermute | solution.py:284
  6.1 0.1 collective-permute-start.2
  6.2 0.0 copy-start
  6.2 2.2 %copy-done = bf16[8192,256]{1,0:T(8,128)(2,1)S(1)} copy-done((bf16[8192,256]{1,0:T(8,128)(2,1)S(1)}, bf16[8192,256]{1,0:T(8,128)(2,1)}, u32[]{:S(2)}) %copy-start) | copy-done | bytes 4194328
  8.4 0.6 %own_logits.1.refs_0_ = f32[16,256]{1,0:T(8,128)S(1)} custom-call(bf16[16,4096]{1,0:T(8,128)(2,1)S(1)} %get-tuple-element.25.refs_0_, bf16[16,4096]{1,0:T(8,128)(2,1)S(1)} %get-tuple-element.26.refs_1_, bf16[8192,256]{1,0:T(8,128)(2,1)S(1)} %copy-done), custom_call_target="tpu_custom_call" | custom-call | tf_op jit(solution)/shard_map/own_logits/pallas_call | solution.py:119
  9.1 2.0 %collective-permute-start.1 = (bf16[16,8192]{1,0:T(8,128)(2,1)S(1)}, bf16[16,8192]{1,0:T(8,128)(2,1)S(1)}, u32[]{:S(2)}, u32[]{:S(2)}) collective-permute-start(bf16[16,8192]{1,0:T(8,128)(2,1)S(1)} %pad_maximum_fusion), channel_id=1, source_target_pairs={{0,16},{4,12},{8,24},{12,4},{16,0},{20,28},{24,8},{28,20},{1,17},{... | collective-permute-start | bytes 786440 | tf_op jit(solution)/shard_map/ppermute | solution.py:284
  11.0 0.0 collective-permute-done
  11.1 0.1 collective-permute-start.3
  11.2 0.0 collective-permute-done.2
  11.2 2.0 %collective-permute-start.5 = (bf16[16,4096]{1,0:T(8,128)(2,1)S(1)}, bf16[16,4096]{1,0:T(8,128)(2,1)S(1)}, u32[]{:S(2)}, u32[]{:S(2)}) collective-permute-start(bf16[16,4096]{1,0:T(8,128)(2,1)S(1)} %collective-permute-done.2), channel_id=1, source_target_pairs={{0,16},{4,12},{8,24},{12,4},{16,0},{20,28},{24,8},{28,20},{1,17},{... | collective-permute-start | bytes 393224 | tf_op jit(solution)/shard_map/ppermute | solution.py:284
  13.2 2.3 %collective-permute-done.1 = bf16[16,8192]{1,0:T(8,128)(2,1)S(1)} collective-permute-done((bf16[16,8192]{1,0:T(8,128)(2,1)S(1)}, bf16[16,8192]{1,0:T(8,128)(2,1)S(1)}, u32[]{:S(2)}, u32[]{:S(2)}) %collective-permute-start.1) | collective-permute-done | bytes 262176 | tf_op jit(solution)/shard_map/ppermute | solution.py:284
  15.5 1.3 %collective-permute-done.3 = bf16[16,4096]{1,0:T(8,128)(2,1)S(1)} collective-permute-done((bf16[16,4096]{1,0:T(8,128)(2,1)S(1)}, bf16[16,4096]{1,0:T(8,128)(2,1)S(1)}, u32[]{:S(2)}, u32[]{:S(2)}) %collective-permute-start.3) | collective-permute-done | bytes 131104 | tf_op jit(solution)/shard_map/ppermute | solution.py:284
  16.8 0.0 collective-permute-start.4
  16.9 1.4 %collective-permute-done.5 = bf16[16,4096]{1,0:T(8,128)(2,1)S(1)} collective-permute-done((bf16[16,4096]{1,0:T(8,128)(2,1)S(1)}, bf16[16,4096]{1,0:T(8,128)(2,1)S(1)}, u32[]{:S(2)}, u32[]{:S(2)}) %collective-permute-start.5) | collective-permute-done | bytes 131104 | tf_op jit(solution)/shard_map/ppermute | solution.py:284
  18.3 0.1 collective-permute-start.6
  18.3 1.5 %collective-permute-done.6.refs_4_ = bf16[32,4096]{1,0:T(8,128)(2,1)S(1)} collective-permute-done((bf16[32,4096]{1,0:T(8,128)(2,1)S(1)}, bf16[32,4096]{1,0:T(8,128)(2,1)S(1)}, u32[]{:S(2)}, u32[]{:S(2)}) %collective-permute-start.6) | collective-permute-done | bytes 262176 | tf_op jit(solution)/shard_map/ppermute | solution.py:280
  19.9 0.0 collective-permute-done.4.refs_2_
  19.9 1.1 %local_logits.1 = (f32[128,256]{1,0:T(8,128)S(1)}, f32[32,4,128]{2,1,0:T(4,128)S(1)}) custom-call(f32[16,256]{1,0:T(8,128)S(1)} %own_logits.1.refs_0_, bf16[96,4096]{1,0:T(8,128)(2,1)S(1)} %slice_dynamic-update-slice_fusion.refs_1_, bf16[96,4096]{1,0:T(8,128)(2,1)S(1)} %collective-permute-done.4.refs_2_, ...), custom_call_target="tpu_custom_call" | custom-call | tf_op jit(solution)/shard_map/local_logits/pallas_call | solution.py:169
  20.9 13.6 %all_to_all.5.stats_ref = f32[32,4,128]{2,1,0:T(4,128)S(1)} all-to-all(f32[32,4,128]{2,1,0:T(4,128)S(1)} %get-tuple-element.32), channel_id=1, replica_groups=mesh['seq'=8,'vocab'=4] {'seq','vocab'}, dimensions={0} | all-to-all | bytes 131072 | tf_op jit(solution)/shard_map/all_to_all | solution.py:308
  34.5 1.6 %gradients.1 = (bf16[4,4,16,1024]{3,2,1,0:T(8,128)(2,1)S(1)}, bf16[4,4,16,1024]{3,2,1,0:T(8,128)(2,1)S(1)}, bf16[3,4,16,1024]{3,2,1,0:T(8,128)(2,1)S(1)}, bf16[3...) custom-call(f32[32,4,128]{2,1,0:T(4,128)S(1)} %all_to_all.5.stats_ref, ...), custom_call_target="tpu_custom_call" | custom-call | tf_op jit(solution)/shard_map/gradients/pallas_call | solution.py:260
  36.2 0.1 collective-permute-start.7
  36.3 0.5 collective-permute-start.8
  36.8 0.8 %collective-permute-done.7 = bf16[4,16,1024]{2,1,0:T(8,128)(2,1)S(1)} collective-permute-done((bf16[4,16,1024]{2,1,0:T(8,128)(2,1)S(1)}, bf16[4,16,1024]{2,1,0:T(8,128)(2,1)S(1)}, u32[]{:S(2)}, u32[]{:S(2)}) %collective-permute-start.7) | collective-permute-done | bytes 131104 | tf_op jit(solution)/shard_map/ppermute | solution.py:280
  37.6 0.2 collective-permute-done.8
  37.8 0.3 collective-permute-start.9
  38.2 0.7 %collective-permute-start.12 = (bf16[4,16,1024]{2,1,0:T(8,128)(2,1)S(1)}, bf16[4,16,1024]{2,1,0:T(8,128)(2,1)S(1)}, u32[]{:S(2)}, u32[]{:S(2)}) collective-permute-start(bf16[4,16,1024]{2,1,0:T(8,128)(2,1)S(1)} %fusion.1), channel_id=1, source_target_pairs={{0,16},{4,12},{8,24},{12,4},{16,0},{20,28},{24,8},{28,20},{1,17},{... | collective-permute-start | bytes 393224 | tf_op jit(solution)/shard_map/ppermute | solution.py:284
  38.9 0.0 collective-permute-start.10
  38.9 1.4 %collective-permute-start.14 = (bf16[4,16,1024]{2,1,0:T(8,128)(2,1)S(1)}, bf16[4,16,1024]{2,1,0:T(8,128)(2,1)S(1)}, u32[]{:S(2)}, u32[]{:S(2)}) collective-permute-start(bf16[4,16,1024]{2,1,0:T(8,128)(2,1)S(1)} %fusion), channel_id=1, source_target_pairs={{0,16},{4,12},{8,24},{12,4},{16,0},{20,28},{24,8},{28,20},{1,17},{... | collective-permute-start | bytes 393224 | tf_op jit(solution)/shard_map/ppermute | solution.py:284
  40.4 0.2 collective-permute-done.10
  40.7 1.4 %collective-permute-start.11 = (bf16[4,16,2048]{2,1,0:T(8,128)(2,1)S(1)}, bf16[4,16,2048]{2,1,0:T(8,128)(2,1)S(1)}, u32[]{:S(2)}, u32[]{:S(2)}) collective-permute-start(bf16[4,16,2048]{2,1,0:T(8,128)(2,1)S(1)} %pad_maximum_fusion.1), channel_id=1, source_target_pairs={{0,16},{4,12},{8,24},{12,4},{16,0},{20,28},{24,8},{28,20},{1,17},{... | collective-permute-start | bytes 786440 | tf_op jit(solution)/shard_map/ppermute | solution.py:284
  42.1 1.1 %collective-permute-done.12 = bf16[4,16,1024]{2,1,0:T(8,128)(2,1)S(1)} collective-permute-done((bf16[4,16,1024]{2,1,0:T(8,128)(2,1)S(1)}, bf16[4,16,1024]{2,1,0:T(8,128)(2,1)S(1)}, u32[]{:S(2)}, u32[]{:S(2)}) %collective-permute-start.12) | collective-permute-done | bytes 131104 | tf_op jit(solution)/shard_map/ppermute | solution.py:284
  43.2 0.1 fusion.4
  43.2 0.7 %collective-permute-start.13 = (bf16[4,16,1024]{2,1,0:T(8,128)(2,1)S(1)}, bf16[4,16,1024]{2,1,0:T(8,128)(2,1)S(1)}, u32[]{:S(2)}, u32[]{:S(2)}) collective-permute-start(bf16[4,16,1024]{2,1,0:T(8,128)(2,1)S(1)} %fusion.4), channel_id=1, source_target_pairs={{0,8},{4,20},{8,0},{12,28},{16,24},{20,4},{24,16},{28,12},{1,9},{5... | collective-permute-start | bytes 393224 | tf_op jit(solution)/shard_map/ppermute | solution.py:284
  44.0 0.6 %collective-permute-done.14 = bf16[4,16,1024]{2,1,0:T(8,128)(2,1)S(1)} collective-permute-done((bf16[4,16,1024]{2,1,0:T(8,128)(2,1)S(1)}, bf16[4,16,1024]{2,1,0:T(8,128)(2,1)S(1)}, u32[]{:S(2)}, u32[]{:S(2)}) %collective-permute-start.14) | collective-permute-done | bytes 131104 | tf_op jit(solution)/shard_map/ppermute | solution.py:284
  44.6 0.1 fusion.2
  44.6 0.8 %collective-permute-start.15 = (bf16[4,16,1024]{2,1,0:T(8,128)(2,1)S(1)}, bf16[4,16,1024]{2,1,0:T(8,128)(2,1)S(1)}, u32[]{:S(2)}, u32[]{:S(2)}) collective-permute-start(bf16[4,16,1024]{2,1,0:T(8,128)(2,1)S(1)} %fusion.2), channel_id=1, source_target_pairs={{0,8},{4,20},{8,0},{12,28},{16,24},{20,4},{24,16},{28,12},{1,9},{5... | collective-permute-start | bytes 393224 | tf_op jit(solution)/shard_map/ppermute | solution.py:284
  45.5 2.8 %collective-permute-done.13 = bf16[4,16,1024]{2,1,0:T(8,128)(2,1)S(1)} collective-permute-done((bf16[4,16,1024]{2,1,0:T(8,128)(2,1)S(1)}, bf16[4,16,1024]{2,1,0:T(8,128)(2,1)S(1)}, u32[]{:S(2)}, u32[]{:S(2)}) %collective-permute-start.13) | collective-permute-done | bytes 131104 | tf_op jit(solution)/shard_map/ppermute | solution.py:284
  48.3 1.4 %collective-permute-done.15 = bf16[4,16,1024]{2,1,0:T(8,128)(2,1)S(1)} collective-permute-done((bf16[4,16,1024]{2,1,0:T(8,128)(2,1)S(1)}, bf16[4,16,1024]{2,1,0:T(8,128)(2,1)S(1)}, u32[]{:S(2)}, u32[]{:S(2)}) %collective-permute-start.15) | collective-permute-done | bytes 131104 | tf_op jit(solution)/shard_map/ppermute | solution.py:284
  49.7 0.2 fusion.3
  49.9 0.9 %collective-permute-start.16 = (bf16[16,2048]{1,0:T(8,128)(2,1)S(1)}, bf16[16,2048]{1,0:T(8,128)(2,1)S(1)}, u32[]{:S(2)}, u32[]{:S(2)}) collective-permute-start(bf16[16,2048]{1,0:T(8,128)(2,1)S(1)} %pad_maximum_fusion.2), channel_id=1, source_target_pairs={{0,3},{1,2},{2,1},{3,0},{4,7},{5,6},{6,5},{7,4},{8,11},{9,10},{10,... | collective-permute-start | bytes 196616 | tf_op jit(solution)/shard_map/ppermute | solution.py:287
  50.8 0.9 %collective-permute-start.17 = (bf16[16,2048]{1,0:T(8,128)(2,1)S(1)}, bf16[16,2048]{1,0:T(8,128)(2,1)S(1)}, u32[]{:S(2)}, u32[]{:S(2)}) collective-permute-start(bf16[16,2048]{1,0:T(8,128)(2,1)S(1)} %pad_maximum_fusion.3), channel_id=1, source_target_pairs={{0,2},{1,3},{2,0},{3,1},{4,6},{5,7},{6,4},{7,5},{8,10},{9,11},{10,... | collective-permute-start | bytes 196616 | tf_op jit(solution)/shard_map/ppermute | solution.py:287
  51.7 2.7 %collective-permute-start.18 = (bf16[16,2048]{1,0:T(8,128)(2,1)S(1)}, bf16[16,2048]{1,0:T(8,128)(2,1)S(1)}, u32[]{:S(2)}, u32[]{:S(2)}) collective-permute-start(bf16[16,2048]{1,0:T(8,128)(2,1)S(1)} %pad_maximum_fusion.4), channel_id=1, source_target_pairs={{0,1},{1,0},{2,3},{3,2},{4,5},{5,4},{6,7},{7,6},{8,9},{9,8},{10,11... | collective-permute-start | bytes 196616 | tf_op jit(solution)/shard_map/ppermute | solution.py:287
  54.4 0.8 %entropies.1 = (f32[1,128]{1,0:T(1,128)}, f32[1,1]{1,0:T(1,128)}) custom-call(f32[32,4,128]{2,1,0:T(4,128)S(1)} %all_to_all.5.stats_ref, bf16[16,128]{1,0:T(8,128)(2,1)S(1)} %get-tuple-element.31.refs_6_.picker_ref), custom_call_target="tpu_custom_call" | custom-call | tf_op jit(solution)/shard_map/entropies/pallas_call | solution.py:209
  55.2 1.6 %collective-permute-done.16 = bf16[16,2048]{1,0:T(8,128)(2,1)S(1)} collective-permute-done((bf16[16,2048]{1,0:T(8,128)(2,1)S(1)}, bf16[16,2048]{1,0:T(8,128)(2,1)S(1)}, u32[]{:S(2)}, u32[]{:S(2)}) %collective-permute-start.16) | collective-permute-done | bytes 65568 | tf_op jit(solution)/shard_map/ppermute | solution.py:287
  56.8 1.8 %collective-permute-done.17 = bf16[16,2048]{1,0:T(8,128)(2,1)S(1)} collective-permute-done((bf16[16,2048]{1,0:T(8,128)(2,1)S(1)}, bf16[16,2048]{1,0:T(8,128)(2,1)S(1)}, u32[]{:S(2)}, u32[]{:S(2)}) %collective-permute-start.17) | collective-permute-done | bytes 65568 | tf_op jit(solution)/shard_map/ppermute | solution.py:287
  58.6 0.0 collective-permute-done.18
  58.6 1.1 %convolution_convert_fusion = bf16[128,2048]{1,0:T(8,128)(2,1)} fusion(bf16[16,128]{1,0:T(8,128)(2,1)S(1)} %get-tuple-element.31.refs_6_.picker_ref, f32[16,1024]{1,0:T(8,128)S(1)} %get-tuple-element.55, f32[16,1024]{1,0:T(8,128)S(1)} %get-tuple-element.56, bf16[16,2048]{1,0:T(8,128)(2,1)S(1)} %collective-permute-done.18, ...), kind=kOutput, calls=%fused_computation | convolution fusion | flops 8912896 | bytes 856064 | tf_op jit(solution)/shard_map/dot_general | solution.py:343
  (23 shorter events, 0.3 us)
Async XLA Ops:
  3.1 7.9 %collective-permute-start = (bf16[16,4096]{1,0:T(8,128)(2,1)S(1)}, bf16[16,4096]{1,0:T(8,128)(2,1)S(1)}, u32[]{:S(2)}, u32[]{:S(2)}) collective-permute-start(bf16[16,4096]{1,0:T(8,128)(2,1)S(1)} %get-tuple-element.25.refs_0_), channel_id=1, source_target_pairs={{0,8},{4,20},{8,0},{12,28},{16,24},{20,4},{24,16},{28,12},{1,9},{5... | collective-permute-start | bytes 393224 | tf_op jit(solution)/shard_map/ppermute | solution.py:284
  6.1 5.1 %collective-permute-start.2 = (bf16[16,4096]{1,0:T(8,128)(2,1)S(1)}, bf16[16,4096]{1,0:T(8,128)(2,1)S(1)}, u32[]{:S(2)}, u32[]{:S(2)}) collective-permute-start(bf16[16,4096]{1,0:T(8,128)(2,1)S(1)} %get-tuple-element.26.refs_1_), channel_id=1, source_target_pairs={{0,8},{4,20},{8,0},{12,28},{16,24},{20,4},{24,16},{28,12},{1,9},{5... | collective-permute-start | bytes 393224 | tf_op jit(solution)/shard_map/ppermute | solution.py:284
  6.2 2.2 %copy-start = (bf16[8192,256]{1,0:T(8,128)(2,1)S(1)}, bf16[8192,256]{1,0:T(8,128)(2,1)}, u32[]{:S(2)}) copy-start(bf16[8192,256]{1,0:T(8,128)(2,1)} %head_ref.1) | copy-start | bytes 12582916
  8.4 11.5 %copy-start.1 = (bf16[8192,256]{1,0:T(8,128)(2,1)S(1)}, bf16[8192,256]{1,0:T(8,128)(2,1)}, u32[]{:S(2)}) copy-start(bf16[8192,256]{1,0:T(8,128)(2,1)} %head_ref.1) | copy-start | bytes 12582916
  9.1 6.4 %collective-permute-start.1 = (bf16[16,8192]{1,0:T(8,128)(2,1)S(1)}, bf16[16,8192]{1,0:T(8,128)(2,1)S(1)}, u32[]{:S(2)}, u32[]{:S(2)}) collective-permute-start(bf16[16,8192]{1,0:T(8,128)(2,1)S(1)} %pad_maximum_fusion), channel_id=1, source_target_pairs={{0,16},{4,12},{8,24},{12,4},{16,0},{20,28},{24,8},{28,20},{1,17},{... | collective-permute-start | bytes 786440 | tf_op jit(solution)/shard_map/ppermute | solution.py:284
  11.1 5.8 %collective-permute-start.3 = (bf16[16,4096]{1,0:T(8,128)(2,1)S(1)}, bf16[16,4096]{1,0:T(8,128)(2,1)S(1)}, u32[]{:S(2)}, u32[]{:S(2)}) collective-permute-start(bf16[16,4096]{1,0:T(8,128)(2,1)S(1)} %collective-permute-done), channel_id=1, source_target_pairs={{0,16},{4,12},{8,24},{12,4},{16,0},{20,28},{24,8},{28,20},{1,17},{... | collective-permute-start | bytes 393224 | tf_op jit(solution)/shard_map/ppermute | solution.py:284
  11.2 7.1 %collective-permute-start.5 = (bf16[16,4096]{1,0:T(8,128)(2,1)S(1)}, bf16[16,4096]{1,0:T(8,128)(2,1)S(1)}, u32[]{:S(2)}, u32[]{:S(2)}) collective-permute-start(bf16[16,4096]{1,0:T(8,128)(2,1)S(1)} %collective-permute-done.2), channel_id=1, source_target_pairs={{0,16},{4,12},{8,24},{12,4},{16,0},{20,28},{24,8},{28,20},{1,17},{... | collective-permute-start | bytes 393224 | tf_op jit(solution)/shard_map/ppermute | solution.py:284
  16.8 3.0 %collective-permute-start.4 = (bf16[96,4096]{1,0:T(8,128)(2,1)S(1)}, bf16[96,4096]{1,0:T(8,128)(2,1)S(1)}, u32[]{:S(2)}, u32[]{:S(2)}) collective-permute-start(bf16[96,4096]{1,0:T(8,128)(2,1)S(1)} %slice_dynamic-update-slice_fusion.refs_1_), channel_id=1, source_target_pairs={{0,4},{4,0},{8,12},{12,8},{16,20},{20,16},{24,28},{28,24},{1,5},{5... | collective-permute-start | bytes 2359304 | tf_op jit(solution)/shard_map/ppermute | solution.py:280
  18.3 1.6 %collective-permute-start.6 = (bf16[32,4096]{1,0:T(8,128)(2,1)S(1)}, bf16[32,4096]{1,0:T(8,128)(2,1)S(1)}, u32[]{:S(2)}, u32[]{:S(2)}) collective-permute-start(bf16[32,4096]{1,0:T(8,128)(2,1)S(1)} %constant_dynamic-update-slice_fusion.4.refs_3_), channel_id=1, source_target_pairs={{0,4},{4,0},{8,12},{12,8},{16,20},{20,16},{24,28},{28,24},{1,5},{5... | collective-permute-start | bytes 786440 | tf_op jit(solution)/shard_map/ppermute | solution.py:280
  36.2 1.4 %collective-permute-start.7 = (bf16[4,16,1024]{2,1,0:T(8,128)(2,1)S(1)}, bf16[4,16,1024]{2,1,0:T(8,128)(2,1)S(1)}, u32[]{:S(2)}, u32[]{:S(2)}) collective-permute-start(bf16[4,16,1024]{2,1,0:T(8,128)(2,1)S(1)} %get-tuple-element.37), channel_id=1, source_target_pairs={{0,4},{4,0},{8,12},{12,8},{16,20},{20,16},{24,28},{28,24},{1,5},{5... | collective-permute-start | bytes 393224 | tf_op jit(solution)/shard_map/ppermute | solution.py:280
  36.3 1.5 %collective-permute-start.8 = (bf16[4,16,1024]{2,1,0:T(8,128)(2,1)S(1)}, bf16[4,16,1024]{2,1,0:T(8,128)(2,1)S(1)}, u32[]{:S(2)}, u32[]{:S(2)}) collective-permute-start(bf16[4,16,1024]{2,1,0:T(8,128)(2,1)S(1)} %get-tuple-element.38), channel_id=1, source_target_pairs={{0,4},{4,0},{8,12},{12,8},{16,20},{20,16},{24,28},{28,24},{1,5},{5... | collective-permute-start | bytes 393224 | tf_op jit(solution)/shard_map/ppermute | solution.py:280
  37.8 2.6 %collective-permute-start.9 = (bf16[3,4,16,1024]{3,2,1,0:T(8,128)(2,1)S(1)}, bf16[3,4,16,1024]{3,2,1,0:T(8,128)(2,1)S(1)}, u32[]{:S(2)}, u32[]{:S(2)}) collective-permute-start(bf16[3,4,16,1024]{3,2,1,0:T(8,128)(2,1)S(1)} %get-tuple-element.39), channel_id=1, source_target_pairs={{0,4},{4,0},{8,12},{12,8},{16,20},{20,16},{24,28},{28,24},{1,5},{5... | collective-permute-start | bytes 1179656 | tf_op jit(solution)/shard_map/ppermute | solution.py:280
  38.2 5.0 %collective-permute-start.12 = (bf16[4,16,1024]{2,1,0:T(8,128)(2,1)S(1)}, bf16[4,16,1024]{2,1,0:T(8,128)(2,1)S(1)}, u32[]{:S(2)}, u32[]{:S(2)}) collective-permute-start(bf16[4,16,1024]{2,1,0:T(8,128)(2,1)S(1)} %fusion.1), channel_id=1, source_target_pairs={{0,16},{4,12},{8,24},{12,4},{16,0},{20,28},{24,8},{28,20},{1,17},{... | collective-permute-start | bytes 393224 | tf_op jit(solution)/shard_map/ppermute | solution.py:284
  38.9 1.7 %collective-permute-start.10 = (bf16[3,4,16,1024]{3,2,1,0:T(8,128)(2,1)S(1)}, bf16[3,4,16,1024]{3,2,1,0:T(8,128)(2,1)S(1)}, u32[]{:S(2)}, u32[]{:S(2)}) collective-permute-start(bf16[3,4,16,1024]{3,2,1,0:T(8,128)(2,1)S(1)} %get-tuple-element.41), channel_id=1, source_target_pairs={{0,4},{4,0},{8,12},{12,8},{16,20},{20,16},{24,28},{28,24},{1,5},{5... | collective-permute-start | bytes 1179656 | tf_op jit(solution)/shard_map/ppermute | solution.py:280
  38.9 5.7 %collective-permute-start.14 = (bf16[4,16,1024]{2,1,0:T(8,128)(2,1)S(1)}, bf16[4,16,1024]{2,1,0:T(8,128)(2,1)S(1)}, u32[]{:S(2)}, u32[]{:S(2)}) collective-permute-start(bf16[4,16,1024]{2,1,0:T(8,128)(2,1)S(1)} %fusion), channel_id=1, source_target_pairs={{0,16},{4,12},{8,24},{12,4},{16,0},{20,28},{24,8},{28,20},{1,17},{... | collective-permute-start | bytes 393224 | tf_op jit(solution)/shard_map/ppermute | solution.py:284
  40.7 9.0 %collective-permute-start.11 = (bf16[4,16,2048]{2,1,0:T(8,128)(2,1)S(1)}, bf16[4,16,2048]{2,1,0:T(8,128)(2,1)S(1)}, u32[]{:S(2)}, u32[]{:S(2)}) collective-permute-start(bf16[4,16,2048]{2,1,0:T(8,128)(2,1)S(1)} %pad_maximum_fusion.1), channel_id=1, source_target_pairs={{0,16},{4,12},{8,24},{12,4},{16,0},{20,28},{24,8},{28,20},{1,17},{... | collective-permute-start | bytes 786440 | tf_op jit(solution)/shard_map/ppermute | solution.py:284
  43.2 5.0 %collective-permute-start.13 = (bf16[4,16,1024]{2,1,0:T(8,128)(2,1)S(1)}, bf16[4,16,1024]{2,1,0:T(8,128)(2,1)S(1)}, u32[]{:S(2)}, u32[]{:S(2)}) collective-permute-start(bf16[4,16,1024]{2,1,0:T(8,128)(2,1)S(1)} %fusion.4), channel_id=1, source_target_pairs={{0,8},{4,20},{8,0},{12,28},{16,24},{20,4},{24,16},{28,12},{1,9},{5... | collective-permute-start | bytes 393224 | tf_op jit(solution)/shard_map/ppermute | solution.py:284
  44.6 5.0 %collective-permute-start.15 = (bf16[4,16,1024]{2,1,0:T(8,128)(2,1)S(1)}, bf16[4,16,1024]{2,1,0:T(8,128)(2,1)S(1)}, u32[]{:S(2)}, u32[]{:S(2)}) collective-permute-start(bf16[4,16,1024]{2,1,0:T(8,128)(2,1)S(1)} %fusion.2), channel_id=1, source_target_pairs={{0,8},{4,20},{8,0},{12,28},{16,24},{20,4},{24,16},{28,12},{1,9},{5... | collective-permute-start | bytes 393224 | tf_op jit(solution)/shard_map/ppermute | solution.py:284
  49.9 6.9 %collective-permute-start.16 = (bf16[16,2048]{1,0:T(8,128)(2,1)S(1)}, bf16[16,2048]{1,0:T(8,128)(2,1)S(1)}, u32[]{:S(2)}, u32[]{:S(2)}) collective-permute-start(bf16[16,2048]{1,0:T(8,128)(2,1)S(1)} %pad_maximum_fusion.2), channel_id=1, source_target_pairs={{0,3},{1,2},{2,1},{3,0},{4,7},{5,6},{6,5},{7,4},{8,11},{9,10},{10,... | collective-permute-start | bytes 196616 | tf_op jit(solution)/shard_map/ppermute | solution.py:287
  50.8 7.8 %collective-permute-start.17 = (bf16[16,2048]{1,0:T(8,128)(2,1)S(1)}, bf16[16,2048]{1,0:T(8,128)(2,1)S(1)}, u32[]{:S(2)}, u32[]{:S(2)}) collective-permute-start(bf16[16,2048]{1,0:T(8,128)(2,1)S(1)} %pad_maximum_fusion.3), channel_id=1, source_target_pairs={{0,2},{1,3},{2,0},{3,1},{4,6},{5,7},{6,4},{7,5},{8,10},{9,11},{10,... | collective-permute-start | bytes 196616 | tf_op jit(solution)/shard_map/ppermute | solution.py:287
  51.7 6.9 %collective-permute-start.18 = (bf16[16,2048]{1,0:T(8,128)(2,1)S(1)}, bf16[16,2048]{1,0:T(8,128)(2,1)S(1)}, u32[]{:S(2)}, u32[]{:S(2)}) collective-permute-start(bf16[16,2048]{1,0:T(8,128)(2,1)S(1)} %pad_maximum_fusion.4), channel_id=1, source_target_pairs={{0,1},{1,0},{2,3},{3,2},{4,5},{5,4},{6,7},{7,6},{8,9},{9,8},{10,11... | collective-permute-start | bytes 196616 | tf_op jit(solution)/shard_map/ppermute | solution.py:287

commit v16 on v15

--- a/solution.py
+++ b/solution.py
@@ -11,6 +11,7 @@
 PARTS = 2
 LANES = 128
 CHUNKS = 8
+OWN_CHUNKS = 2
 FLIGHT = 3
 VMEM_BYTES = 24 * 2**20
 F32, BF16 = jnp.float32, jnp.bfloat16
@@ -104,25 +105,36 @@
     return own, picker
 
 
-def own_kernel(*refs):
-    *part_refs, head_ref, out_ref = refs
+def own_kernel(own_ref, head_ref, out_ref, head_here, sems):
+    chunks, step, _ = head_here.shape
+    copies = [
+        pltpu.make_async_copy(head_ref.at[pl.ds(i * step, step), :], head_here.at[i], sems.at[i])
+        for i in range(chunks)
+    ]
+    for copy in copies:
+        copy.start()
     total = None
-    size = part_refs[0].shape[1]
-    for c, ref in enumerate(part_refs):
-        head = head_ref[c * size : (c + 1) * size, :]
-        part = jnp.dot(ref[...], head, preferred_element_type=F32)
+    for i in range(chunks):
+        copies[i].wait()
+        rows = own_ref[:, i * step : (i + 1) * step]
+        part = jnp.dot(rows, head_here[i], preferred_element_type=F32)
         total = part if total is None else total + part
     out_ref[...] = total
 
 
 def own_logits(own, head):
+    width, shard = head.shape
     return pl.pallas_call(
         own_kernel,
-        in_specs=[pl.BlockSpec(memory_space=pltpu.VMEM)] * (len(own) + 1),
-        out_shape=jax.ShapeDtypeStruct((ACT_DEV, head.shape[1]), F32),
+        in_specs=[pl.BlockSpec(memory_space=pltpu.VMEM), pl.BlockSpec(memory_space=pltpu.HBM)],
+        out_shape=jax.ShapeDtypeStruct((ACT_DEV, shard), F32),
+        scratch_shapes=[
+            pltpu.VMEM((OWN_CHUNKS, width // CHUNKS, shard), BF16),
+            pltpu.SemaphoreType.DMA((OWN_CHUNKS,)),
+        ],
         compiler_params=params(),
         name="own_logits",
-    )(*own, head)
+    )(own[0], in_hbm(head))
 
 
 def logits_kernel(n_seq, *refs):
@@ -136,13 +148,15 @@
         for k, ref in enumerate(block_refs):
             size = ref.shape[0] // PARTS
             start = (i // each) * size
-            first = start + ACT_DEV if k == 0 else start
+            first = start + ACT_DEV if k == 0 and i < OWN_CHUNKS else start
             rows.append(ref[first : start + size, at : at + step])
         rows = jnp.concatenate(rows, axis=0)
         head = head_ref[i * step : (i + 1) * step, :]
         part = jnp.dot(rows, head, preferred_element_type=F32)
+        if i < OWN_CHUNKS:
+            mine = own_ref[...] if i == 0 else jnp.zeros(own_ref.shape, F32)
+            part = jnp.concatenate([mine, part], axis=0)
         logits = part if logits is None else logits + part
-    logits = jnp.concatenate([own_ref[...], logits], axis=0)
     logits_ref[...] = logits
     top = jnp.max(logits, axis=1, keepdims=True)
     away = logits - top

time: 59.9 us -> 58.7 us (0.980)
  local copies, waits for them, and re-layouts: 2.31 us -> 0.13 us
  Pallas kernels: 6.59 us -> 7.6 us
  starting transfers between devices: 17.7 us -> 18.5 us
    unnamed x10 -> x8, local copies, waits for them, and re-layouts: 2.25 us -> 0.07 us
    pallas_call x1, Pallas kernels: 0.65 us -> 1.47 us  [own_logits(): pl.pallas_call(own_kernel, in_specs=[pl.BlockSpec(memory_space=pltpu.VMEM...]
    ppermute x10, starting transfers between devices: 12.3 us -> 13 us  [swap_chip(): lax.ppermute(value, 'seq', [(i, i ^ flips[i & 1]) for i in range(n_seq)])]
  transfers between devices with their start and end apart: 19 -> 19, of which waited for: 13 -> 14; matrix products, arithmetic and copies ran while one was open for 1% -> 1% of each run, Pallas kernels for 2% -> 4%
where the time goes in v16:
time: 58.7 us; the launch traced here: 58.6 us
  starting transfers between devices  18.5 us (32%)
  waiting for transfers between devices  16.6 us (28%)
  blocking collectives  13.4 us (23%)
  Pallas kernels  7.6 us (13%)
  matrix products  1.11 us (2%)
  between operations  0.81 us (1%)
    all_to_all x1, blocking collectives, body(): stats = lax.all_to_all(stats, ('seq', 'vocab'), 0, 0, tiled=True)  13.4 us
    ppermute x10, starting transfers between devices, swap_chip(): lax.ppermute(value, 'seq', [(i, i ^ flips[i & 1]) for i in range(n_seq)])  13 us
    ppermute x10, waiting for transfers between devices, swap_chip(): lax.ppermute(value, 'seq', [(i, i ^ flips[i & 1]) for i in range(n_seq)])  10.5 us
    ppermute x3, starting transfers between devices, send_vocab(): return lax.ppermute(value, 'vocab', [(i, i ^ k) for i in range(n_vocab)])  4.45 us
    ppermute x3, waiting for transfers between devices, send_vocab(): return lax.ppermute(value, 'vocab', [(i, i ^ k) for i in range(n_vocab)])  3.42 us
    ppermute x6, waiting for transfers between devices, swap_core(): return lax.ppermute(value, 'seq', [(i, i ^ 1) for i in range(n_seq)])  2.76 us
    pallas_call x1, Pallas kernels, select(): pl.pallas_call(select_kernel, in_specs=[pl.BlockSpec(memory_space=pltpu.H...  2.75 us
    pallas_call x1, Pallas kernels, gradients(): pl.pallas_call(functools.partial(gradient_kernel, n_seq, n_vocab), in_spe...  1.64 us
  transfers between devices with their start and end apart: 19, of which 14 were waited for; matrix products, arithmetic and copies ran while one was open for 1% of the time, Pallas kernels for 4%

profile of v16, /device:TPU:0, one launch (start us, length us, event | category | flops | bytes accessed | tf_op | source)
XLA Modules:
  0.0 58.6 jit_solution(1972644425219562250)
XLA Ops:
  0.6 0.0 copy-start
  0.6 2.8 %select_rows.1 = (bf16[16,4096]{1,0:T(8,128)(2,1)S(1)}, bf16[16,4096]{1,0:T(8,128)(2,1)S(1)}, bf16[16,128]{1,0:T(8,128)(2,1)S(1)}) custom-call(s32[1,128]{1,0:T(1,128)} %bitcast.46, bf16[128,8192]{1,0:T(8,128)(2,1)} %hidden_ref.1), custom_call_target="tpu_custom_call" | custom-call | tf_op jit(solution)/shard_map/select_rows/pallas_call | solution.py:92
  3.4 3.0 %collective-permute-start = (bf16[16,4096]{1,0:T(8,128)(2,1)S(1)}, bf16[16,4096]{1,0:T(8,128)(2,1)S(1)}, u32[]{:S(2)}, u32[]{:S(2)}) collective-permute-start(bf16[16,4096]{1,0:T(8,128)(2,1)S(1)} %get-tuple-element.25.own_ref), channel_id=1, source_target_pairs={{0,8},{4,20},{8,0},{12,28},{16,24},{20,4},{24,16},{28,12},{1,9},{5... | collective-permute-start | bytes 393224 | tf_op jit(solution)/shard_map/ppermute | solution.py:298
  6.4 0.1 collective-permute-start.2
  6.5 1.5 %own_logits.1.refs_0_ = f32[16,256]{1,0:T(8,128)S(1)} custom-call(bf16[16,4096]{1,0:T(8,128)(2,1)S(1)} %get-tuple-element.25.own_ref, bf16[8192,256]{1,0:T(8,128)(2,1)} %head_ref.3), custom_call_target="tpu_custom_call" | custom-call | tf_op jit(solution)/shard_map/own_logits/pallas_call | solution.py:127
  8.0 2.0 %collective-permute-start.1 = (bf16[16,8192]{1,0:T(8,128)(2,1)S(1)}, bf16[16,8192]{1,0:T(8,128)(2,1)S(1)}, u32[]{:S(2)}, u32[]{:S(2)}) collective-permute-start(bf16[16,8192]{1,0:T(8,128)(2,1)S(1)} %pad_maximum_fusion), channel_id=1, source_target_pairs={{0,16},{4,12},{8,24},{12,4},{16,0},{20,28},{24,8},{28,20},{1,17},{... | collective-permute-start | bytes 786440 | tf_op jit(solution)/shard_map/ppermute | solution.py:298
  10.0 0.0 collective-permute-done
  10.1 1.4 %collective-permute-start.3 = (bf16[16,4096]{1,0:T(8,128)(2,1)S(1)}, bf16[16,4096]{1,0:T(8,128)(2,1)S(1)}, u32[]{:S(2)}, u32[]{:S(2)}) collective-permute-start(bf16[16,4096]{1,0:T(8,128)(2,1)S(1)} %collective-permute-done), channel_id=1, source_target_pairs={{0,16},{4,12},{8,24},{12,4},{16,0},{20,28},{24,8},{28,20},{1,17},{... | collective-permute-start | bytes 393224 | tf_op jit(solution)/shard_map/ppermute | solution.py:298
  11.4 1.1 %collective-permute-done.2 = bf16[16,4096]{1,0:T(8,128)(2,1)S(1)} collective-permute-done((bf16[16,4096]{1,0:T(8,128)(2,1)S(1)}, bf16[16,4096]{1,0:T(8,128)(2,1)S(1)}, u32[]{:S(2)}, u32[]{:S(2)}) %collective-permute-start.2) | collective-permute-done | bytes 131104 | tf_op jit(solution)/shard_map/ppermute | solution.py:298
  12.5 1.5 %collective-permute-start.5 = (bf16[16,4096]{1,0:T(8,128)(2,1)S(1)}, bf16[16,4096]{1,0:T(8,128)(2,1)S(1)}, u32[]{:S(2)}, u32[]{:S(2)}) collective-permute-start(bf16[16,4096]{1,0:T(8,128)(2,1)S(1)} %collective-permute-done.2), channel_id=1, source_target_pairs={{0,16},{4,12},{8,24},{12,4},{16,0},{20,28},{24,8},{28,20},{1,17},{... | collective-permute-start | bytes 393224 | tf_op jit(solution)/shard_map/ppermute | solution.py:298
  14.0 0.4 collective-permute-done.1
  14.5 1.3 %collective-permute-done.3 = bf16[16,4096]{1,0:T(8,128)(2,1)S(1)} collective-permute-done((bf16[16,4096]{1,0:T(8,128)(2,1)S(1)}, bf16[16,4096]{1,0:T(8,128)(2,1)S(1)}, u32[]{:S(2)}, u32[]{:S(2)}) %collective-permute-start.3) | collective-permute-done | bytes 131104 | tf_op jit(solution)/shard_map/ppermute | solution.py:298
  15.8 0.0 collective-permute-start.4
  15.8 1.6 %collective-permute-done.5 = bf16[16,4096]{1,0:T(8,128)(2,1)S(1)} collective-permute-done((bf16[16,4096]{1,0:T(8,128)(2,1)S(1)}, bf16[16,4096]{1,0:T(8,128)(2,1)S(1)}, u32[]{:S(2)}, u32[]{:S(2)}) %collective-permute-start.5) | collective-permute-done | bytes 131104 | tf_op jit(solution)/shard_map/ppermute | solution.py:298
  17.5 0.1 collective-permute-start.6
  17.6 1.5 %collective-permute-done.6.refs_4_ = bf16[32,4096]{1,0:T(8,128)(2,1)S(1)} collective-permute-done((bf16[32,4096]{1,0:T(8,128)(2,1)S(1)}, bf16[32,4096]{1,0:T(8,128)(2,1)S(1)}, u32[]{:S(2)}, u32[]{:S(2)}) %collective-permute-start.6) | collective-permute-done | bytes 262176 | tf_op jit(solution)/shard_map/ppermute | solution.py:294
  19.1 0.0 collective-permute-done.4.refs_2_
  19.1 1.0 %local_logits.1 = (f32[128,256]{1,0:T(8,128)S(1)}, f32[32,4,128]{2,1,0:T(4,128)S(1)}) custom-call(f32[16,256]{1,0:T(8,128)S(1)} %own_logits.1.refs_0_, bf16[96,4096]{1,0:T(8,128)(2,1)S(1)} %slice_dynamic-update-slice_fusion.refs_1_, bf16[96,4096]{1,0:T(8,128)(2,1)S(1)} %collective-permute-done.4.refs_2_, ...), custom_call_target="tpu_custom_call" | custom-call | tf_op jit(solution)/shard_map/local_logits/pallas_call | solution.py:183
  20.1 13.4 %all_to_all.5.stats_ref = f32[32,4,128]{2,1,0:T(4,128)S(1)} all-to-all(f32[32,4,128]{2,1,0:T(4,128)S(1)} %get-tuple-element.32), channel_id=1, replica_groups=mesh['seq'=8,'vocab'=4] {'seq','vocab'}, dimensions={0} | all-to-all | bytes 131072 | tf_op jit(solution)/shard_map/all_to_all | solution.py:322
  33.4 1.6 %gradients.1 = (bf16[4,4,16,1024]{3,2,1,0:T(8,128)(2,1)S(1)}, bf16[4,4,16,1024]{3,2,1,0:T(8,128)(2,1)S(1)}, bf16[3,4,16,1024]{3,2,1,0:T(8,128)(2,1)S(1)}, bf16[3...) custom-call(f32[32,4,128]{2,1,0:T(4,128)S(1)} %all_to_all.5.stats_ref, ...), custom_call_target="tpu_custom_call" | custom-call | tf_op jit(solution)/shard_map/gradients/pallas_call | solution.py:274
  35.1 0.1 collective-permute-start.7
  35.2 0.5 collective-permute-start.8
  35.7 0.8 %collective-permute-done.7 = bf16[4,16,1024]{2,1,0:T(8,128)(2,1)S(1)} collective-permute-done((bf16[4,16,1024]{2,1,0:T(8,128)(2,1)S(1)}, bf16[4,16,1024]{2,1,0:T(8,128)(2,1)S(1)}, u32[]{:S(2)}, u32[]{:S(2)}) %collective-permute-start.7) | collective-permute-done | bytes 131104 | tf_op jit(solution)/shard_map/ppermute | solution.py:294
  36.5 0.2 collective-permute-done.8
  36.7 0.3 collective-permute-start.9
  37.0 0.7 %collective-permute-start.12 = (bf16[4,16,1024]{2,1,0:T(8,128)(2,1)S(1)}, bf16[4,16,1024]{2,1,0:T(8,128)(2,1)S(1)}, u32[]{:S(2)}, u32[]{:S(2)}) collective-permute-start(bf16[4,16,1024]{2,1,0:T(8,128)(2,1)S(1)} %fusion.1), channel_id=1, source_target_pairs={{0,16},{4,12},{8,24},{12,4},{16,0},{20,28},{24,8},{28,20},{1,17},{... | collective-permute-start | bytes 393224 | tf_op jit(solution)/shard_map/ppermute | solution.py:298
  37.8 0.0 collective-permute-start.10
  37.8 1.4 %collective-permute-start.14 = (bf16[4,16,1024]{2,1,0:T(8,128)(2,1)S(1)}, bf16[4,16,1024]{2,1,0:T(8,128)(2,1)S(1)}, u32[]{:S(2)}, u32[]{:S(2)}) collective-permute-start(bf16[4,16,1024]{2,1,0:T(8,128)(2,1)S(1)} %fusion), channel_id=1, source_target_pairs={{0,16},{4,12},{8,24},{12,4},{16,0},{20,28},{24,8},{28,20},{1,17},{... | collective-permute-start | bytes 393224 | tf_op jit(solution)/shard_map/ppermute | solution.py:298
  39.2 0.0 collective-permute-done.9
  39.3 0.2 collective-permute-done.10
  39.6 1.4 %collective-permute-start.11 = (bf16[4,16,2048]{2,1,0:T(8,128)(2,1)S(1)}, bf16[4,16,2048]{2,1,0:T(8,128)(2,1)S(1)}, u32[]{:S(2)}, u32[]{:S(2)}) collective-permute-start(bf16[4,16,2048]{2,1,0:T(8,128)(2,1)S(1)} %pad_maximum_fusion.1), channel_id=1, source_target_pairs={{0,16},{4,12},{8,24},{12,4},{16,0},{20,28},{24,8},{28,20},{1,17},{... | collective-permute-start | bytes 786440 | tf_op jit(solution)/shard_map/ppermute | solution.py:298
  41.0 1.1 %collective-permute-done.12 = bf16[4,16,1024]{2,1,0:T(8,128)(2,1)S(1)} collective-permute-done((bf16[4,16,1024]{2,1,0:T(8,128)(2,1)S(1)}, bf16[4,16,1024]{2,1,0:T(8,128)(2,1)S(1)}, u32[]{:S(2)}, u32[]{:S(2)}) %collective-permute-start.12) | collective-permute-done | bytes 131104 | tf_op jit(solution)/shard_map/ppermute | solution.py:298
  42.1 0.1 fusion.4
  42.1 0.7 %collective-permute-start.13 = (bf16[4,16,1024]{2,1,0:T(8,128)(2,1)S(1)}, bf16[4,16,1024]{2,1,0:T(8,128)(2,1)S(1)}, u32[]{:S(2)}, u32[]{:S(2)}) collective-permute-start(bf16[4,16,1024]{2,1,0:T(8,128)(2,1)S(1)} %fusion.4), channel_id=1, source_target_pairs={{0,8},{4,20},{8,0},{12,28},{16,24},{20,4},{24,16},{28,12},{1,9},{5... | collective-permute-start | bytes 393224 | tf_op jit(solution)/shard_map/ppermute | solution.py:298
  42.9 0.6 %collective-permute-done.14 = bf16[4,16,1024]{2,1,0:T(8,128)(2,1)S(1)} collective-permute-done((bf16[4,16,1024]{2,1,0:T(8,128)(2,1)S(1)}, bf16[4,16,1024]{2,1,0:T(8,128)(2,1)S(1)}, u32[]{:S(2)}, u32[]{:S(2)}) %collective-permute-start.14) | collective-permute-done | bytes 131104 | tf_op jit(solution)/shard_map/ppermute | solution.py:298
  43.5 0.1 fusion.2
  43.5 0.8 %collective-permute-start.15 = (bf16[4,16,1024]{2,1,0:T(8,128)(2,1)S(1)}, bf16[4,16,1024]{2,1,0:T(8,128)(2,1)S(1)}, u32[]{:S(2)}, u32[]{:S(2)}) collective-permute-start(bf16[4,16,1024]{2,1,0:T(8,128)(2,1)S(1)} %fusion.2), channel_id=1, source_target_pairs={{0,8},{4,20},{8,0},{12,28},{16,24},{20,4},{24,16},{28,12},{1,9},{5... | collective-permute-start | bytes 393224 | tf_op jit(solution)/shard_map/ppermute | solution.py:298
  44.4 2.8 %collective-permute-done.13 = bf16[4,16,1024]{2,1,0:T(8,128)(2,1)S(1)} collective-permute-done((bf16[4,16,1024]{2,1,0:T(8,128)(2,1)S(1)}, bf16[4,16,1024]{2,1,0:T(8,128)(2,1)S(1)}, u32[]{:S(2)}, u32[]{:S(2)}) %collective-permute-start.13) | collective-permute-done | bytes 131104 | tf_op jit(solution)/shard_map/ppermute | solution.py:298
  47.2 1.4 %collective-permute-done.15 = bf16[4,16,1024]{2,1,0:T(8,128)(2,1)S(1)} collective-permute-done((bf16[4,16,1024]{2,1,0:T(8,128)(2,1)S(1)}, bf16[4,16,1024]{2,1,0:T(8,128)(2,1)S(1)}, u32[]{:S(2)}, u32[]{:S(2)}) %collective-permute-start.15) | collective-permute-done | bytes 131104 | tf_op jit(solution)/shard_map/ppermute | solution.py:298
  48.6 0.2 fusion.3
  48.8 0.9 %collective-permute-start.16 = (bf16[16,2048]{1,0:T(8,128)(2,1)S(1)}, bf16[16,2048]{1,0:T(8,128)(2,1)S(1)}, u32[]{:S(2)}, u32[]{:S(2)}) collective-permute-start(bf16[16,2048]{1,0:T(8,128)(2,1)S(1)} %pad_maximum_fusion.2), channel_id=1, source_target_pairs={{0,3},{1,2},{2,1},{3,0},{4,7},{5,6},{6,5},{7,4},{8,11},{9,10},{10,... | collective-permute-start | bytes 196616 | tf_op jit(solution)/shard_map/ppermute | solution.py:301
  49.7 0.9 %collective-permute-start.17 = (bf16[16,2048]{1,0:T(8,128)(2,1)S(1)}, bf16[16,2048]{1,0:T(8,128)(2,1)S(1)}, u32[]{:S(2)}, u32[]{:S(2)}) collective-permute-start(bf16[16,2048]{1,0:T(8,128)(2,1)S(1)} %pad_maximum_fusion.3), channel_id=1, source_target_pairs={{0,2},{1,3},{2,0},{3,1},{4,6},{5,7},{6,4},{7,5},{8,10},{9,11},{10,... | collective-permute-start | bytes 196616 | tf_op jit(solution)/shard_map/ppermute | solution.py:301
  50.6 2.7 %collective-permute-start.18 = (bf16[16,2048]{1,0:T(8,128)(2,1)S(1)}, bf16[16,2048]{1,0:T(8,128)(2,1)S(1)}, u32[]{:S(2)}, u32[]{:S(2)}) collective-permute-start(bf16[16,2048]{1,0:T(8,128)(2,1)S(1)} %pad_maximum_fusion.4), channel_id=1, source_target_pairs={{0,1},{1,0},{2,3},{3,2},{4,5},{5,4},{6,7},{7,6},{8,9},{9,8},{10,11... | collective-permute-start | bytes 196616 | tf_op jit(solution)/shard_map/ppermute | solution.py:301
  53.3 0.8 %entropies.1 = (f32[1,128]{1,0:T(1,128)}, f32[1,1]{1,0:T(1,128)}) custom-call(f32[32,4,128]{2,1,0:T(4,128)S(1)} %all_to_all.5.stats_ref, bf16[16,128]{1,0:T(8,128)(2,1)S(1)} %get-tuple-element.31.refs_6_.picker_ref), custom_call_target="tpu_custom_call" | custom-call | tf_op jit(solution)/shard_map/entropies/pallas_call | solution.py:223
  54.0 1.6 %collective-permute-done.16 = bf16[16,2048]{1,0:T(8,128)(2,1)S(1)} collective-permute-done((bf16[16,2048]{1,0:T(8,128)(2,1)S(1)}, bf16[16,2048]{1,0:T(8,128)(2,1)S(1)}, u32[]{:S(2)}, u32[]{:S(2)}) %collective-permute-start.16) | collective-permute-done | bytes 65568 | tf_op jit(solution)/shard_map/ppermute | solution.py:301
  55.7 1.8 %collective-permute-done.17 = bf16[16,2048]{1,0:T(8,128)(2,1)S(1)} collective-permute-done((bf16[16,2048]{1,0:T(8,128)(2,1)S(1)}, bf16[16,2048]{1,0:T(8,128)(2,1)S(1)}, u32[]{:S(2)}, u32[]{:S(2)}) %collective-permute-start.17) | collective-permute-done | bytes 65568 | tf_op jit(solution)/shard_map/ppermute | solution.py:301
  57.5 0.0 collective-permute-done.18
  57.5 1.1 %convolution_convert_fusion = bf16[128,2048]{1,0:T(8,128)(2,1)} fusion(bf16[16,128]{1,0:T(8,128)(2,1)S(1)} %get-tuple-element.31.refs_6_.picker_ref, f32[16,1024]{1,0:T(8,128)S(1)} %get-tuple-element.55, f32[16,1024]{1,0:T(8,128)S(1)} %get-tuple-element.56, bf16[16,2048]{1,0:T(8,128)(2,1)S(1)} %collective-permute-done.18, ...), kind=kOutput, calls=%fused_computation | convolution fusion | flops 8912896 | bytes 856064 | tf_op jit(solution)/shard_map/dot_general | solution.py:357
  (21 shorter events, 0.3 us)
Async XLA Ops:
  0.6 18.5 %copy-start = (bf16[8192,256]{1,0:T(8,128)(2,1)S(1)}, bf16[8192,256]{1,0:T(8,128)(2,1)}, u32[]{:S(2)}) copy-start(bf16[8192,256]{1,0:T(8,128)(2,1)} %head_ref.3) | copy-start | bytes 12582916
  3.4 6.6 %collective-permute-start = (bf16[16,4096]{1,0:T(8,128)(2,1)S(1)}, bf16[16,4096]{1,0:T(8,128)(2,1)S(1)}, u32[]{:S(2)}, u32[]{:S(2)}) collective-permute-start(bf16[16,4096]{1,0:T(8,128)(2,1)S(1)} %get-tuple-element.25.own_ref), channel_id=1, source_target_pairs={{0,8},{4,20},{8,0},{12,28},{16,24},{20,4},{24,16},{28,12},{1,9},{5... | collective-permute-start | bytes 393224 | tf_op jit(solution)/shard_map/ppermute | solution.py:298
  6.4 6.1 %collective-permute-start.2 = (bf16[16,4096]{1,0:T(8,128)(2,1)S(1)}, bf16[16,4096]{1,0:T(8,128)(2,1)S(1)}, u32[]{:S(2)}, u32[]{:S(2)}) collective-permute-start(bf16[16,4096]{1,0:T(8,128)(2,1)S(1)} %get-tuple-element.26), channel_id=1, source_target_pairs={{0,8},{4,20},{8,0},{12,28},{16,24},{20,4},{24,16},{28,12},{1,9},{5... | collective-permute-start | bytes 393224 | tf_op jit(solution)/shard_map/ppermute | solution.py:298
  8.0 6.4 %collective-permute-start.1 = (bf16[16,8192]{1,0:T(8,128)(2,1)S(1)}, bf16[16,8192]{1,0:T(8,128)(2,1)S(1)}, u32[]{:S(2)}, u32[]{:S(2)}) collective-permute-start(bf16[16,8192]{1,0:T(8,128)(2,1)S(1)} %pad_maximum_fusion), channel_id=1, source_target_pairs={{0,16},{4,12},{8,24},{12,4},{16,0},{20,28},{24,8},{28,20},{1,17},{... | collective-permute-start | bytes 786440 | tf_op jit(solution)/shard_map/ppermute | solution.py:298
  10.1 5.8 %collective-permute-start.3 = (bf16[16,4096]{1,0:T(8,128)(2,1)S(1)}, bf16[16,4096]{1,0:T(8,128)(2,1)S(1)}, u32[]{:S(2)}, u32[]{:S(2)}) collective-permute-start(bf16[16,4096]{1,0:T(8,128)(2,1)S(1)} %collective-permute-done), channel_id=1, source_target_pairs={{0,16},{4,12},{8,24},{12,4},{16,0},{20,28},{24,8},{28,20},{1,17},{... | collective-permute-start | bytes 393224 | tf_op jit(solution)/shard_map/ppermute | solution.py:298
  12.5 5.0 %collective-permute-start.5 = (bf16[16,4096]{1,0:T(8,128)(2,1)S(1)}, bf16[16,4096]{1,0:T(8,128)(2,1)S(1)}, u32[]{:S(2)}, u32[]{:S(2)}) collective-permute-start(bf16[16,4096]{1,0:T(8,128)(2,1)S(1)} %collective-permute-done.2), channel_id=1, source_target_pairs={{0,16},{4,12},{8,24},{12,4},{16,0},{20,28},{24,8},{28,20},{1,17},{... | collective-permute-start | bytes 393224 | tf_op jit(solution)/shard_map/ppermute | solution.py:298
  15.8 3.3 %collective-permute-start.4 = (bf16[96,4096]{1,0:T(8,128)(2,1)S(1)}, bf16[96,4096]{1,0:T(8,128)(2,1)S(1)}, u32[]{:S(2)}, u32[]{:S(2)}) collective-permute-start(bf16[96,4096]{1,0:T(8,128)(2,1)S(1)} %slice_dynamic-update-slice_fusion.refs_1_), channel_id=1, source_target_pairs={{0,4},{4,0},{8,12},{12,8},{16,20},{20,16},{24,28},{28,24},{1,5},{5... | collective-permute-start | bytes 2359304 | tf_op jit(solution)/shard_map/ppermute | solution.py:294
  17.5 1.6 %collective-permute-start.6 = (bf16[32,4096]{1,0:T(8,128)(2,1)S(1)}, bf16[32,4096]{1,0:T(8,128)(2,1)S(1)}, u32[]{:S(2)}, u32[]{:S(2)}) collective-permute-start(bf16[32,4096]{1,0:T(8,128)(2,1)S(1)} %constant_dynamic-update-slice_fusion.4.refs_3_), channel_id=1, source_target_pairs={{0,4},{4,0},{8,12},{12,8},{16,20},{20,16},{24,28},{28,24},{1,5},{5... | collective-permute-start | bytes 786440 | tf_op jit(solution)/shard_map/ppermute | solution.py:294
  35.1 1.4 %collective-permute-start.7 = (bf16[4,16,1024]{2,1,0:T(8,128)(2,1)S(1)}, bf16[4,16,1024]{2,1,0:T(8,128)(2,1)S(1)}, u32[]{:S(2)}, u32[]{:S(2)}) collective-permute-start(bf16[4,16,1024]{2,1,0:T(8,128)(2,1)S(1)} %get-tuple-element.37), channel_id=1, source_target_pairs={{0,4},{4,0},{8,12},{12,8},{16,20},{20,16},{24,28},{28,24},{1,5},{5... | collective-permute-start | bytes 393224 | tf_op jit(solution)/shard_map/ppermute | solution.py:294
  35.2 1.5 %collective-permute-start.8 = (bf16[4,16,1024]{2,1,0:T(8,128)(2,1)S(1)}, bf16[4,16,1024]{2,1,0:T(8,128)(2,1)S(1)}, u32[]{:S(2)}, u32[]{:S(2)}) collective-permute-start(bf16[4,16,1024]{2,1,0:T(8,128)(2,1)S(1)} %get-tuple-element.38), channel_id=1, source_target_pairs={{0,4},{4,0},{8,12},{12,8},{16,20},{20,16},{24,28},{28,24},{1,5},{5... | collective-permute-start | bytes 393224 | tf_op jit(solution)/shard_map/ppermute | solution.py:294
  36.7 2.6 %collective-permute-start.9 = (bf16[3,4,16,1024]{3,2,1,0:T(8,128)(2,1)S(1)}, bf16[3,4,16,1024]{3,2,1,0:T(8,128)(2,1)S(1)}, u32[]{:S(2)}, u32[]{:S(2)}) collective-permute-start(bf16[3,4,16,1024]{3,2,1,0:T(8,128)(2,1)S(1)} %get-tuple-element.39), channel_id=1, source_target_pairs={{0,4},{4,0},{8,12},{12,8},{16,20},{20,16},{24,28},{28,24},{1,5},{5... | collective-permute-start | bytes 1179656 | tf_op jit(solution)/shard_map/ppermute | solution.py:294
  37.0 5.0 %collective-permute-start.12 = (bf16[4,16,1024]{2,1,0:T(8,128)(2,1)S(1)}, bf16[4,16,1024]{2,1,0:T(8,128)(2,1)S(1)}, u32[]{:S(2)}, u32[]{:S(2)}) collective-permute-start(bf16[4,16,1024]{2,1,0:T(8,128)(2,1)S(1)} %fusion.1), channel_id=1, source_target_pairs={{0,16},{4,12},{8,24},{12,4},{16,0},{20,28},{24,8},{28,20},{1,17},{... | collective-permute-start | bytes 393224 | tf_op jit(solution)/shard_map/ppermute | solution.py:298
  37.8 1.7 %collective-permute-start.10 = (bf16[3,4,16,1024]{3,2,1,0:T(8,128)(2,1)S(1)}, bf16[3,4,16,1024]{3,2,1,0:T(8,128)(2,1)S(1)}, u32[]{:S(2)}, u32[]{:S(2)}) collective-permute-start(bf16[3,4,16,1024]{3,2,1,0:T(8,128)(2,1)S(1)} %get-tuple-element.41), channel_id=1, source_target_pairs={{0,4},{4,0},{8,12},{12,8},{16,20},{20,16},{24,28},{28,24},{1,5},{5... | collective-permute-start | bytes 1179656 | tf_op jit(solution)/shard_map/ppermute | solution.py:294
  37.8 5.7 %collective-permute-start.14 = (bf16[4,16,1024]{2,1,0:T(8,128)(2,1)S(1)}, bf16[4,16,1024]{2,1,0:T(8,128)(2,1)S(1)}, u32[]{:S(2)}, u32[]{:S(2)}) collective-permute-start(bf16[4,16,1024]{2,1,0:T(8,128)(2,1)S(1)} %fusion), channel_id=1, source_target_pairs={{0,16},{4,12},{8,24},{12,4},{16,0},{20,28},{24,8},{28,20},{1,17},{... | collective-permute-start | bytes 393224 | tf_op jit(solution)/shard_map/ppermute | solution.py:298
  39.6 9.0 %collective-permute-start.11 = (bf16[4,16,2048]{2,1,0:T(8,128)(2,1)S(1)}, bf16[4,16,2048]{2,1,0:T(8,128)(2,1)S(1)}, u32[]{:S(2)}, u32[]{:S(2)}) collective-permute-start(bf16[4,16,2048]{2,1,0:T(8,128)(2,1)S(1)} %pad_maximum_fusion.1), channel_id=1, source_target_pairs={{0,16},{4,12},{8,24},{12,4},{16,0},{20,28},{24,8},{28,20},{1,17},{... | collective-permute-start | bytes 786440 | tf_op jit(solution)/shard_map/ppermute | solution.py:298
  42.1 5.0 %collective-permute-start.13 = (bf16[4,16,1024]{2,1,0:T(8,128)(2,1)S(1)}, bf16[4,16,1024]{2,1,0:T(8,128)(2,1)S(1)}, u32[]{:S(2)}, u32[]{:S(2)}) collective-permute-start(bf16[4,16,1024]{2,1,0:T(8,128)(2,1)S(1)} %fusion.4), channel_id=1, source_target_pairs={{0,8},{4,20},{8,0},{12,28},{16,24},{20,4},{24,16},{28,12},{1,9},{5... | collective-permute-start | bytes 393224 | tf_op jit(solution)/shard_map/ppermute | solution.py:298
  43.5 5.0 %collective-permute-start.15 = (bf16[4,16,1024]{2,1,0:T(8,128)(2,1)S(1)}, bf16[4,16,1024]{2,1,0:T(8,128)(2,1)S(1)}, u32[]{:S(2)}, u32[]{:S(2)}) collective-permute-start(bf16[4,16,1024]{2,1,0:T(8,128)(2,1)S(1)} %fusion.2), channel_id=1, source_target_pairs={{0,8},{4,20},{8,0},{12,28},{16,24},{20,4},{24,16},{28,12},{1,9},{5... | collective-permute-start | bytes 393224 | tf_op jit(solution)/shard_map/ppermute | solution.py:298
  48.8 6.9 %collective-permute-start.16 = (bf16[16,2048]{1,0:T(8,128)(2,1)S(1)}, bf16[16,2048]{1,0:T(8,128)(2,1)S(1)}, u32[]{:S(2)}, u32[]{:S(2)}) collective-permute-start(bf16[16,2048]{1,0:T(8,128)(2,1)S(1)} %pad_maximum_fusion.2), channel_id=1, source_target_pairs={{0,3},{1,2},{2,1},{3,0},{4,7},{5,6},{6,5},{7,4},{8,11},{9,10},{10,... | collective-permute-start | bytes 196616 | tf_op jit(solution)/shard_map/ppermute | solution.py:301
  49.7 7.8 %collective-permute-start.17 = (bf16[16,2048]{1,0:T(8,128)(2,1)S(1)}, bf16[16,2048]{1,0:T(8,128)(2,1)S(1)}, u32[]{:S(2)}, u32[]{:S(2)}) collective-permute-start(bf16[16,2048]{1,0:T(8,128)(2,1)S(1)} %pad_maximum_fusion.3), channel_id=1, source_target_pairs={{0,2},{1,3},{2,0},{3,1},{4,6},{5,7},{6,4},{7,5},{8,10},{9,11},{10,... | collective-permute-start | bytes 196616 | tf_op jit(solution)/shard_map/ppermute | solution.py:301
  50.6 6.9 %collective-permute-start.18 = (bf16[16,2048]{1,0:T(8,128)(2,1)S(1)}, bf16[16,2048]{1,0:T(8,128)(2,1)S(1)}, u32[]{:S(2)}, u32[]{:S(2)}) collective-permute-start(bf16[16,2048]{1,0:T(8,128)(2,1)S(1)} %pad_maximum_fusion.4), channel_id=1, source_target_pairs={{0,1},{1,0},{2,3},{3,2},{4,5},{5,4},{6,7},{7,6},{8,9},{9,8},{10,11... | collective-permute-start | bytes 196616 | tf_op jit(solution)/shard_map/ppermute | solution.py:301

commit v17 on v16

--- a/solution.py
+++ b/solution.py
@@ -11,7 +11,7 @@
 PARTS = 2
 LANES = 128
 CHUNKS = 8
-OWN_CHUNKS = 2
+OWN_CHUNKS = 1
 FLIGHT = 3
 VMEM_BYTES = 24 * 2**20
 F32, BF16 = jnp.float32, jnp.bfloat16

time: 58.7 us -> 58.5 us (level)
  transfers between devices with their start and end apart: 19 -> 19, of which waited for: 14 -> 14; matrix products, arithmetic and copies ran while one was open for 1% -> 1% of each run, Pallas kernels for 4% -> 3%
where the time goes in v17:
time: 58.5 us; the launch traced here: 58.3 us
  starting transfers between devices  18.7 us (32%)
  waiting for transfers between devices  16.9 us (29%)
  blocking collectives  12.9 us (22%)
  Pallas kernels  7.36 us (13%)
  matrix products  1.11 us (2%)
  between operations  0.8 us (1%)
    ppermute x10, starting transfers between devices, swap_chip(): lax.ppermute(value, 'seq', [(i, i ^ flips[i & 1]) for i in range(n_seq)])  13.2 us
    all_to_all x1, blocking collectives, body(): stats = lax.all_to_all(stats, ('seq', 'vocab'), 0, 0, tiled=True)  12.9 us
    ppermute x10, waiting for transfers between devices, swap_chip(): lax.ppermute(value, 'seq', [(i, i ^ flips[i & 1]) for i in range(n_seq)])  10.7 us
    ppermute x3, starting transfers between devices, send_vocab(): return lax.ppermute(value, 'vocab', [(i, i ^ k) for i in range(n_vocab)])  4.45 us
    ppermute x3, waiting for transfers between devices, send_vocab(): return lax.ppermute(value, 'vocab', [(i, i ^ k) for i in range(n_vocab)])  3.43 us
    ppermute x6, waiting for transfers between devices, swap_core(): return lax.ppermute(value, 'seq', [(i, i ^ 1) for i in range(n_seq)])  2.76 us
    pallas_call x1, Pallas kernels, select(): pl.pallas_call(select_kernel, in_specs=[pl.BlockSpec(memory_space=pltpu.H...  2.75 us
    pallas_call x1, Pallas kernels, gradients(): pl.pallas_call(functools.partial(gradient_kernel, n_seq, n_vocab), in_spe...  1.64 us
  transfers between devices with their start and end apart: 19, of which 14 were waited for; matrix products, arithmetic and copies ran while one was open for 1% of the time, Pallas kernels for 3%

profile of v17, /device:TPU:0, one launch (start us, length us, event | category | flops | bytes accessed | tf_op | source)
XLA Modules:
  0.0 58.3 jit_solution(14685027676074229056)
XLA Ops:
  0.6 0.0 copy-start
  0.6 2.8 %select_rows.1 = (bf16[16,4096]{1,0:T(8,128)(2,1)S(1)}, bf16[16,4096]{1,0:T(8,128)(2,1)S(1)}, bf16[16,128]{1,0:T(8,128)(2,1)S(1)}) custom-call(s32[1,128]{1,0:T(1,128)} %bitcast.46, bf16[128,8192]{1,0:T(8,128)(2,1)} %hidden_ref.1), custom_call_target="tpu_custom_call" | custom-call | tf_op jit(solution)/shard_map/select_rows/pallas_call | solution.py:92
  3.4 3.0 %collective-permute-start = (bf16[16,4096]{1,0:T(8,128)(2,1)S(1)}, bf16[16,4096]{1,0:T(8,128)(2,1)S(1)}, u32[]{:S(2)}, u32[]{:S(2)}) collective-permute-start(bf16[16,4096]{1,0:T(8,128)(2,1)S(1)} %get-tuple-element.25.own_ref), channel_id=1, source_target_pairs={{0,8},{4,20},{8,0},{12,28},{16,24},{20,4},{24,16},{28,12},{1,9},{5... | collective-permute-start | bytes 393224 | tf_op jit(solution)/shard_map/ppermute | solution.py:298
  6.4 0.1 collective-permute-start.2
  6.5 1.2 %own_logits.1.refs_0_ = f32[16,256]{1,0:T(8,128)S(1)} custom-call(bf16[16,4096]{1,0:T(8,128)(2,1)S(1)} %get-tuple-element.25.own_ref, bf16[8192,256]{1,0:T(8,128)(2,1)} %head_ref.3), custom_call_target="tpu_custom_call" | custom-call | tf_op jit(solution)/shard_map/own_logits/pallas_call | solution.py:127
  7.8 2.0 %collective-permute-start.1 = (bf16[16,8192]{1,0:T(8,128)(2,1)S(1)}, bf16[16,8192]{1,0:T(8,128)(2,1)S(1)}, u32[]{:S(2)}, u32[]{:S(2)}) collective-permute-start(bf16[16,8192]{1,0:T(8,128)(2,1)S(1)} %pad_maximum_fusion), channel_id=1, source_target_pairs={{0,16},{4,12},{8,24},{12,4},{16,0},{20,28},{24,8},{28,20},{1,17},{... | collective-permute-start | bytes 786440 | tf_op jit(solution)/shard_map/ppermute | solution.py:298
  9.8 0.0 collective-permute-done
  9.8 1.6 %collective-permute-start.3 = (bf16[16,4096]{1,0:T(8,128)(2,1)S(1)}, bf16[16,4096]{1,0:T(8,128)(2,1)S(1)}, u32[]{:S(2)}, u32[]{:S(2)}) collective-permute-start(bf16[16,4096]{1,0:T(8,128)(2,1)S(1)} %collective-permute-done), channel_id=1, source_target_pairs={{0,16},{4,12},{8,24},{12,4},{16,0},{20,28},{24,8},{28,20},{1,17},{... | collective-permute-start | bytes 393224 | tf_op jit(solution)/shard_map/ppermute | solution.py:298
  11.4 1.3 %collective-permute-done.2 = bf16[16,4096]{1,0:T(8,128)(2,1)S(1)} collective-permute-done((bf16[16,4096]{1,0:T(8,128)(2,1)S(1)}, bf16[16,4096]{1,0:T(8,128)(2,1)S(1)}, u32[]{:S(2)}, u32[]{:S(2)}) %collective-permute-start.2) | collective-permute-done | bytes 131104 | tf_op jit(solution)/shard_map/ppermute | solution.py:298
  12.8 1.4 %collective-permute-start.5 = (bf16[16,4096]{1,0:T(8,128)(2,1)S(1)}, bf16[16,4096]{1,0:T(8,128)(2,1)S(1)}, u32[]{:S(2)}, u32[]{:S(2)}) collective-permute-start(bf16[16,4096]{1,0:T(8,128)(2,1)S(1)} %collective-permute-done.2), channel_id=1, source_target_pairs={{0,16},{4,12},{8,24},{12,4},{16,0},{20,28},{24,8},{28,20},{1,17},{... | collective-permute-start | bytes 393224 | tf_op jit(solution)/shard_map/ppermute | solution.py:298
  14.1 0.1 collective-permute-done.1
  14.3 1.3 %collective-permute-done.3 = bf16[16,4096]{1,0:T(8,128)(2,1)S(1)} collective-permute-done((bf16[16,4096]{1,0:T(8,128)(2,1)S(1)}, bf16[16,4096]{1,0:T(8,128)(2,1)S(1)}, u32[]{:S(2)}, u32[]{:S(2)}) %collective-permute-start.3) | collective-permute-done | bytes 131104 | tf_op jit(solution)/shard_map/ppermute | solution.py:298
  15.6 0.1 collective-permute-start.4
  15.7 2.0 %collective-permute-done.5 = bf16[16,4096]{1,0:T(8,128)(2,1)S(1)} collective-permute-done((bf16[16,4096]{1,0:T(8,128)(2,1)S(1)}, bf16[16,4096]{1,0:T(8,128)(2,1)S(1)}, u32[]{:S(2)}, u32[]{:S(2)}) %collective-permute-start.5) | collective-permute-done | bytes 131104 | tf_op jit(solution)/shard_map/ppermute | solution.py:298
  17.7 0.1 collective-permute-start.6
  17.8 1.5 %collective-permute-done.6.refs_4_ = bf16[32,4096]{1,0:T(8,128)(2,1)S(1)} collective-permute-done((bf16[32,4096]{1,0:T(8,128)(2,1)S(1)}, bf16[32,4096]{1,0:T(8,128)(2,1)S(1)}, u32[]{:S(2)}, u32[]{:S(2)}) %collective-permute-start.6) | collective-permute-done | bytes 262176 | tf_op jit(solution)/shard_map/ppermute | solution.py:294
  19.3 0.0 collective-permute-done.4.refs_2_
  19.3 1.0 %local_logits.1 = (f32[128,256]{1,0:T(8,128)S(1)}, f32[32,4,128]{2,1,0:T(4,128)S(1)}) custom-call(f32[16,256]{1,0:T(8,128)S(1)} %own_logits.1.refs_0_, bf16[96,4096]{1,0:T(8,128)(2,1)S(1)} %slice_dynamic-update-slice_fusion.refs_1_, bf16[96,4096]{1,0:T(8,128)(2,1)S(1)} %collective-permute-done.4.refs_2_, ...), custom_call_target="tpu_custom_call" | custom-call | tf_op jit(solution)/shard_map/local_logits/pallas_call | solution.py:183
  20.3 12.9 %all_to_all.5.stats_ref = f32[32,4,128]{2,1,0:T(4,128)S(1)} all-to-all(f32[32,4,128]{2,1,0:T(4,128)S(1)} %get-tuple-element.32), channel_id=1, replica_groups=mesh['seq'=8,'vocab'=4] {'seq','vocab'}, dimensions={0} | all-to-all | bytes 131072 | tf_op jit(solution)/shard_map/all_to_all | solution.py:322
  33.2 1.6 %gradients.1 = (bf16[4,4,16,1024]{3,2,1,0:T(8,128)(2,1)S(1)}, bf16[4,4,16,1024]{3,2,1,0:T(8,128)(2,1)S(1)}, bf16[3,4,16,1024]{3,2,1,0:T(8,128)(2,1)S(1)}, bf16[3...) custom-call(f32[32,4,128]{2,1,0:T(4,128)S(1)} %all_to_all.5.stats_ref, ...), custom_call_target="tpu_custom_call" | custom-call | tf_op jit(solution)/shard_map/gradients/pallas_call | solution.py:274
  34.8 0.1 collective-permute-start.7
  34.9 0.5 collective-permute-start.8
  35.4 0.8 %collective-permute-done.7 = bf16[4,16,1024]{2,1,0:T(8,128)(2,1)S(1)} collective-permute-done((bf16[4,16,1024]{2,1,0:T(8,128)(2,1)S(1)}, bf16[4,16,1024]{2,1,0:T(8,128)(2,1)S(1)}, u32[]{:S(2)}, u32[]{:S(2)}) %collective-permute-start.7) | collective-permute-done | bytes 131104 | tf_op jit(solution)/shard_map/ppermute | solution.py:294
  36.3 0.2 collective-permute-done.8
  36.4 0.3 collective-permute-start.9
  36.8 0.7 %collective-permute-start.12 = (bf16[4,16,1024]{2,1,0:T(8,128)(2,1)S(1)}, bf16[4,16,1024]{2,1,0:T(8,128)(2,1)S(1)}, u32[]{:S(2)}, u32[]{:S(2)}) collective-permute-start(bf16[4,16,1024]{2,1,0:T(8,128)(2,1)S(1)} %fusion.1), channel_id=1, source_target_pairs={{0,16},{4,12},{8,24},{12,4},{16,0},{20,28},{24,8},{28,20},{1,17},{... | collective-permute-start | bytes 393224 | tf_op jit(solution)/shard_map/ppermute | solution.py:298
  37.5 0.0 collective-permute-start.10
  37.6 1.4 %collective-permute-start.14 = (bf16[4,16,1024]{2,1,0:T(8,128)(2,1)S(1)}, bf16[4,16,1024]{2,1,0:T(8,128)(2,1)S(1)}, u32[]{:S(2)}, u32[]{:S(2)}) collective-permute-start(bf16[4,16,1024]{2,1,0:T(8,128)(2,1)S(1)} %fusion), channel_id=1, source_target_pairs={{0,16},{4,12},{8,24},{12,4},{16,0},{20,28},{24,8},{28,20},{1,17},{... | collective-permute-start | bytes 393224 | tf_op jit(solution)/shard_map/ppermute | solution.py:298
  39.0 0.0 collective-permute-done.9
  39.1 0.2 collective-permute-done.10
  39.3 1.4 %collective-permute-start.11 = (bf16[4,16,2048]{2,1,0:T(8,128)(2,1)S(1)}, bf16[4,16,2048]{2,1,0:T(8,128)(2,1)S(1)}, u32[]{:S(2)}, u32[]{:S(2)}) collective-permute-start(bf16[4,16,2048]{2,1,0:T(8,128)(2,1)S(1)} %pad_maximum_fusion.1), channel_id=1, source_target_pairs={{0,16},{4,12},{8,24},{12,4},{16,0},{20,28},{24,8},{28,20},{1,17},{... | collective-permute-start | bytes 786440 | tf_op jit(solution)/shard_map/ppermute | solution.py:298
  40.8 1.1 %collective-permute-done.12 = bf16[4,16,1024]{2,1,0:T(8,128)(2,1)S(1)} collective-permute-done((bf16[4,16,1024]{2,1,0:T(8,128)(2,1)S(1)}, bf16[4,16,1024]{2,1,0:T(8,128)(2,1)S(1)}, u32[]{:S(2)}, u32[]{:S(2)}) %collective-permute-start.12) | collective-permute-done | bytes 131104 | tf_op jit(solution)/shard_map/ppermute | solution.py:298
  41.8 0.1 fusion.4
  41.9 0.7 %collective-permute-start.13 = (bf16[4,16,1024]{2,1,0:T(8,128)(2,1)S(1)}, bf16[4,16,1024]{2,1,0:T(8,128)(2,1)S(1)}, u32[]{:S(2)}, u32[]{:S(2)}) collective-permute-start(bf16[4,16,1024]{2,1,0:T(8,128)(2,1)S(1)} %fusion.4), channel_id=1, source_target_pairs={{0,8},{4,20},{8,0},{12,28},{16,24},{20,4},{24,16},{28,12},{1,9},{5... | collective-permute-start | bytes 393224 | tf_op jit(solution)/shard_map/ppermute | solution.py:298
  42.6 0.6 %collective-permute-done.14 = bf16[4,16,1024]{2,1,0:T(8,128)(2,1)S(1)} collective-permute-done((bf16[4,16,1024]{2,1,0:T(8,128)(2,1)S(1)}, bf16[4,16,1024]{2,1,0:T(8,128)(2,1)S(1)}, u32[]{:S(2)}, u32[]{:S(2)}) %collective-permute-start.14) | collective-permute-done | bytes 131104 | tf_op jit(solution)/shard_map/ppermute | solution.py:298
  43.2 0.1 fusion.2
  43.3 0.8 %collective-permute-start.15 = (bf16[4,16,1024]{2,1,0:T(8,128)(2,1)S(1)}, bf16[4,16,1024]{2,1,0:T(8,128)(2,1)S(1)}, u32[]{:S(2)}, u32[]{:S(2)}) collective-permute-start(bf16[4,16,1024]{2,1,0:T(8,128)(2,1)S(1)} %fusion.2), channel_id=1, source_target_pairs={{0,8},{4,20},{8,0},{12,28},{16,24},{20,4},{24,16},{28,12},{1,9},{5... | collective-permute-start | bytes 393224 | tf_op jit(solution)/shard_map/ppermute | solution.py:298
  44.1 2.8 %collective-permute-done.13 = bf16[4,16,1024]{2,1,0:T(8,128)(2,1)S(1)} collective-permute-done((bf16[4,16,1024]{2,1,0:T(8,128)(2,1)S(1)}, bf16[4,16,1024]{2,1,0:T(8,128)(2,1)S(1)}, u32[]{:S(2)}, u32[]{:S(2)}) %collective-permute-start.13) | collective-permute-done | bytes 131104 | tf_op jit(solution)/shard_map/ppermute | solution.py:298
  46.9 1.4 %collective-permute-done.15 = bf16[4,16,1024]{2,1,0:T(8,128)(2,1)S(1)} collective-permute-done((bf16[4,16,1024]{2,1,0:T(8,128)(2,1)S(1)}, bf16[4,16,1024]{2,1,0:T(8,128)(2,1)S(1)}, u32[]{:S(2)}, u32[]{:S(2)}) %collective-permute-start.15) | collective-permute-done | bytes 131104 | tf_op jit(solution)/shard_map/ppermute | solution.py:298
  48.3 0.2 fusion.3
  48.6 0.9 %collective-permute-start.16 = (bf16[16,2048]{1,0:T(8,128)(2,1)S(1)}, bf16[16,2048]{1,0:T(8,128)(2,1)S(1)}, u32[]{:S(2)}, u32[]{:S(2)}) collective-permute-start(bf16[16,2048]{1,0:T(8,128)(2,1)S(1)} %pad_maximum_fusion.2), channel_id=1, source_target_pairs={{0,3},{1,2},{2,1},{3,0},{4,7},{5,6},{6,5},{7,4},{8,11},{9,10},{10,... | collective-permute-start | bytes 196616 | tf_op jit(solution)/shard_map/ppermute | solution.py:301
  49.5 0.9 %collective-permute-start.17 = (bf16[16,2048]{1,0:T(8,128)(2,1)S(1)}, bf16[16,2048]{1,0:T(8,128)(2,1)S(1)}, u32[]{:S(2)}, u32[]{:S(2)}) collective-permute-start(bf16[16,2048]{1,0:T(8,128)(2,1)S(1)} %pad_maximum_fusion.3), channel_id=1, source_target_pairs={{0,2},{1,3},{2,0},{3,1},{4,6},{5,7},{6,4},{7,5},{8,10},{9,11},{10,... | collective-permute-start | bytes 196616 | tf_op jit(solution)/shard_map/ppermute | solution.py:301
  50.3 2.7 %collective-permute-start.18 = (bf16[16,2048]{1,0:T(8,128)(2,1)S(1)}, bf16[16,2048]{1,0:T(8,128)(2,1)S(1)}, u32[]{:S(2)}, u32[]{:S(2)}) collective-permute-start(bf16[16,2048]{1,0:T(8,128)(2,1)S(1)} %pad_maximum_fusion.4), channel_id=1, source_target_pairs={{0,1},{1,0},{2,3},{3,2},{4,5},{5,4},{6,7},{7,6},{8,9},{9,8},{10,11... | collective-permute-start | bytes 196616 | tf_op jit(solution)/shard_map/ppermute | solution.py:301
  53.0 0.8 %entropies.1 = (f32[1,128]{1,0:T(1,128)}, f32[1,1]{1,0:T(1,128)}) custom-call(f32[32,4,128]{2,1,0:T(4,128)S(1)} %all_to_all.5.stats_ref, bf16[16,128]{1,0:T(8,128)(2,1)S(1)} %get-tuple-element.31.refs_6_.picker_ref), custom_call_target="tpu_custom_call" | custom-call | tf_op jit(solution)/shard_map/entropies/pallas_call | solution.py:223
  53.8 1.6 %collective-permute-done.16 = bf16[16,2048]{1,0:T(8,128)(2,1)S(1)} collective-permute-done((bf16[16,2048]{1,0:T(8,128)(2,1)S(1)}, bf16[16,2048]{1,0:T(8,128)(2,1)S(1)}, u32[]{:S(2)}, u32[]{:S(2)}) %collective-permute-start.16) | collective-permute-done | bytes 65568 | tf_op jit(solution)/shard_map/ppermute | solution.py:301
  55.4 1.8 %collective-permute-done.17 = bf16[16,2048]{1,0:T(8,128)(2,1)S(1)} collective-permute-done((bf16[16,2048]{1,0:T(8,128)(2,1)S(1)}, bf16[16,2048]{1,0:T(8,128)(2,1)S(1)}, u32[]{:S(2)}, u32[]{:S(2)}) %collective-permute-start.17) | collective-permute-done | bytes 65568 | tf_op jit(solution)/shard_map/ppermute | solution.py:301
  57.2 0.0 collective-permute-done.18
  57.2 1.1 %convolution_convert_fusion = bf16[128,2048]{1,0:T(8,128)(2,1)} fusion(bf16[16,128]{1,0:T(8,128)(2,1)S(1)} %get-tuple-element.31.refs_6_.picker_ref, f32[16,1024]{1,0:T(8,128)S(1)} %get-tuple-element.55, f32[16,1024]{1,0:T(8,128)S(1)} %get-tuple-element.56, bf16[16,2048]{1,0:T(8,128)(2,1)S(1)} %collective-permute-done.18, ...), kind=kOutput, calls=%fused_computation | convolution fusion | flops 8912896 | bytes 856064 | tf_op jit(solution)/shard_map/dot_general | solution.py:357
  (21 shorter events, 0.3 us)
Async XLA Ops:
  0.6 18.7 %copy-start = (bf16[8192,256]{1,0:T(8,128)(2,1)S(1)}, bf16[8192,256]{1,0:T(8,128)(2,1)}, u32[]{:S(2)}) copy-start(bf16[8192,256]{1,0:T(8,128)(2,1)} %head_ref.3) | copy-start | bytes 12582916
  3.4 6.4 %collective-permute-start = (bf16[16,4096]{1,0:T(8,128)(2,1)S(1)}, bf16[16,4096]{1,0:T(8,128)(2,1)S(1)}, u32[]{:S(2)}, u32[]{:S(2)}) collective-permute-start(bf16[16,4096]{1,0:T(8,128)(2,1)S(1)} %get-tuple-element.25.own_ref), channel_id=1, source_target_pairs={{0,8},{4,20},{8,0},{12,28},{16,24},{20,4},{24,16},{28,12},{1,9},{5... | collective-permute-start | bytes 393224 | tf_op jit(solution)/shard_map/ppermute | solution.py:298
  6.4 6.3 %collective-permute-start.2 = (bf16[16,4096]{1,0:T(8,128)(2,1)S(1)}, bf16[16,4096]{1,0:T(8,128)(2,1)S(1)}, u32[]{:S(2)}, u32[]{:S(2)}) collective-permute-start(bf16[16,4096]{1,0:T(8,128)(2,1)S(1)} %get-tuple-element.26), channel_id=1, source_target_pairs={{0,8},{4,20},{8,0},{12,28},{16,24},{20,4},{24,16},{28,12},{1,9},{5... | collective-permute-start | bytes 393224 | tf_op jit(solution)/shard_map/ppermute | solution.py:298
  7.8 6.4 %collective-permute-start.1 = (bf16[16,8192]{1,0:T(8,128)(2,1)S(1)}, bf16[16,8192]{1,0:T(8,128)(2,1)S(1)}, u32[]{:S(2)}, u32[]{:S(2)}) collective-permute-start(bf16[16,8192]{1,0:T(8,128)(2,1)S(1)} %pad_maximum_fusion), channel_id=1, source_target_pairs={{0,16},{4,12},{8,24},{12,4},{16,0},{20,28},{24,8},{28,20},{1,17},{... | collective-permute-start | bytes 786440 | tf_op jit(solution)/shard_map/ppermute | solution.py:298
  9.8 5.8 %collective-permute-start.3 = (bf16[16,4096]{1,0:T(8,128)(2,1)S(1)}, bf16[16,4096]{1,0:T(8,128)(2,1)S(1)}, u32[]{:S(2)}, u32[]{:S(2)}) collective-permute-start(bf16[16,4096]{1,0:T(8,128)(2,1)S(1)} %collective-permute-done), channel_id=1, source_target_pairs={{0,16},{4,12},{8,24},{12,4},{16,0},{20,28},{24,8},{28,20},{1,17},{... | collective-permute-start | bytes 393224 | tf_op jit(solution)/shard_map/ppermute | solution.py:298
  12.8 5.0 %collective-permute-start.5 = (bf16[16,4096]{1,0:T(8,128)(2,1)S(1)}, bf16[16,4096]{1,0:T(8,128)(2,1)S(1)}, u32[]{:S(2)}, u32[]{:S(2)}) collective-permute-start(bf16[16,4096]{1,0:T(8,128)(2,1)S(1)} %collective-permute-done.2), channel_id=1, source_target_pairs={{0,16},{4,12},{8,24},{12,4},{16,0},{20,28},{24,8},{28,20},{1,17},{... | collective-permute-start | bytes 393224 | tf_op jit(solution)/shard_map/ppermute | solution.py:298
  15.6 3.7 %collective-permute-start.4 = (bf16[96,4096]{1,0:T(8,128)(2,1)S(1)}, bf16[96,4096]{1,0:T(8,128)(2,1)S(1)}, u32[]{:S(2)}, u32[]{:S(2)}) collective-permute-start(bf16[96,4096]{1,0:T(8,128)(2,1)S(1)} %slice_dynamic-update-slice_fusion.refs_1_), channel_id=1, source_target_pairs={{0,4},{4,0},{8,12},{12,8},{16,20},{20,16},{24,28},{28,24},{1,5},{5... | collective-permute-start | bytes 2359304 | tf_op jit(solution)/shard_map/ppermute | solution.py:294
  17.7 1.6 %collective-permute-start.6 = (bf16[32,4096]{1,0:T(8,128)(2,1)S(1)}, bf16[32,4096]{1,0:T(8,128)(2,1)S(1)}, u32[]{:S(2)}, u32[]{:S(2)}) collective-permute-start(bf16[32,4096]{1,0:T(8,128)(2,1)S(1)} %constant_dynamic-update-slice_fusion.4.refs_3_), channel_id=1, source_target_pairs={{0,4},{4,0},{8,12},{12,8},{16,20},{20,16},{24,28},{28,24},{1,5},{5... | collective-permute-start | bytes 786440 | tf_op jit(solution)/shard_map/ppermute | solution.py:294
  34.8 1.4 %collective-permute-start.7 = (bf16[4,16,1024]{2,1,0:T(8,128)(2,1)S(1)}, bf16[4,16,1024]{2,1,0:T(8,128)(2,1)S(1)}, u32[]{:S(2)}, u32[]{:S(2)}) collective-permute-start(bf16[4,16,1024]{2,1,0:T(8,128)(2,1)S(1)} %get-tuple-element.37), channel_id=1, source_target_pairs={{0,4},{4,0},{8,12},{12,8},{16,20},{20,16},{24,28},{28,24},{1,5},{5... | collective-permute-start | bytes 393224 | tf_op jit(solution)/shard_map/ppermute | solution.py:294
  34.9 1.5 %collective-permute-start.8 = (bf16[4,16,1024]{2,1,0:T(8,128)(2,1)S(1)}, bf16[4,16,1024]{2,1,0:T(8,128)(2,1)S(1)}, u32[]{:S(2)}, u32[]{:S(2)}) collective-permute-start(bf16[4,16,1024]{2,1,0:T(8,128)(2,1)S(1)} %get-tuple-element.38), channel_id=1, source_target_pairs={{0,4},{4,0},{8,12},{12,8},{16,20},{20,16},{24,28},{28,24},{1,5},{5... | collective-permute-start | bytes 393224 | tf_op jit(solution)/shard_map/ppermute | solution.py:294
  36.4 2.6 %collective-permute-start.9 = (bf16[3,4,16,1024]{3,2,1,0:T(8,128)(2,1)S(1)}, bf16[3,4,16,1024]{3,2,1,0:T(8,128)(2,1)S(1)}, u32[]{:S(2)}, u32[]{:S(2)}) collective-permute-start(bf16[3,4,16,1024]{3,2,1,0:T(8,128)(2,1)S(1)} %get-tuple-element.39), channel_id=1, source_target_pairs={{0,4},{4,0},{8,12},{12,8},{16,20},{20,16},{24,28},{28,24},{1,5},{5... | collective-permute-start | bytes 1179656 | tf_op jit(solution)/shard_map/ppermute | solution.py:294
  36.8 5.0 %collective-permute-start.12 = (bf16[4,16,1024]{2,1,0:T(8,128)(2,1)S(1)}, bf16[4,16,1024]{2,1,0:T(8,128)(2,1)S(1)}, u32[]{:S(2)}, u32[]{:S(2)}) collective-permute-start(bf16[4,16,1024]{2,1,0:T(8,128)(2,1)S(1)} %fusion.1), channel_id=1, source_target_pairs={{0,16},{4,12},{8,24},{12,4},{16,0},{20,28},{24,8},{28,20},{1,17},{... | collective-permute-start | bytes 393224 | tf_op jit(solution)/shard_map/ppermute | solution.py:298
  37.5 1.7 %collective-permute-start.10 = (bf16[3,4,16,1024]{3,2,1,0:T(8,128)(2,1)S(1)}, bf16[3,4,16,1024]{3,2,1,0:T(8,128)(2,1)S(1)}, u32[]{:S(2)}, u32[]{:S(2)}) collective-permute-start(bf16[3,4,16,1024]{3,2,1,0:T(8,128)(2,1)S(1)} %get-tuple-element.41), channel_id=1, source_target_pairs={{0,4},{4,0},{8,12},{12,8},{16,20},{20,16},{24,28},{28,24},{1,5},{5... | collective-permute-start | bytes 1179656 | tf_op jit(solution)/shard_map/ppermute | solution.py:294
  37.6 5.7 %collective-permute-start.14 = (bf16[4,16,1024]{2,1,0:T(8,128)(2,1)S(1)}, bf16[4,16,1024]{2,1,0:T(8,128)(2,1)S(1)}, u32[]{:S(2)}, u32[]{:S(2)}) collective-permute-start(bf16[4,16,1024]{2,1,0:T(8,128)(2,1)S(1)} %fusion), channel_id=1, source_target_pairs={{0,16},{4,12},{8,24},{12,4},{16,0},{20,28},{24,8},{28,20},{1,17},{... | collective-permute-start | bytes 393224 | tf_op jit(solution)/shard_map/ppermute | solution.py:298
  39.3 9.0 %collective-permute-start.11 = (bf16[4,16,2048]{2,1,0:T(8,128)(2,1)S(1)}, bf16[4,16,2048]{2,1,0:T(8,128)(2,1)S(1)}, u32[]{:S(2)}, u32[]{:S(2)}) collective-permute-start(bf16[4,16,2048]{2,1,0:T(8,128)(2,1)S(1)} %pad_maximum_fusion.1), channel_id=1, source_target_pairs={{0,16},{4,12},{8,24},{12,4},{16,0},{20,28},{24,8},{28,20},{1,17},{... | collective-permute-start | bytes 786440 | tf_op jit(solution)/shard_map/ppermute | solution.py:298
  41.9 5.0 %collective-permute-start.13 = (bf16[4,16,1024]{2,1,0:T(8,128)(2,1)S(1)}, bf16[4,16,1024]{2,1,0:T(8,128)(2,1)S(1)}, u32[]{:S(2)}, u32[]{:S(2)}) collective-permute-start(bf16[4,16,1024]{2,1,0:T(8,128)(2,1)S(1)} %fusion.4), channel_id=1, source_target_pairs={{0,8},{4,20},{8,0},{12,28},{16,24},{20,4},{24,16},{28,12},{1,9},{5... | collective-permute-start | bytes 393224 | tf_op jit(solution)/shard_map/ppermute | solution.py:298
  43.3 5.0 %collective-permute-start.15 = (bf16[4,16,1024]{2,1,0:T(8,128)(2,1)S(1)}, bf16[4,16,1024]{2,1,0:T(8,128)(2,1)S(1)}, u32[]{:S(2)}, u32[]{:S(2)}) collective-permute-start(bf16[4,16,1024]{2,1,0:T(8,128)(2,1)S(1)} %fusion.2), channel_id=1, source_target_pairs={{0,8},{4,20},{8,0},{12,28},{16,24},{20,4},{24,16},{28,12},{1,9},{5... | collective-permute-start | bytes 393224 | tf_op jit(solution)/shard_map/ppermute | solution.py:298
  48.6 6.9 %collective-permute-start.16 = (bf16[16,2048]{1,0:T(8,128)(2,1)S(1)}, bf16[16,2048]{1,0:T(8,128)(2,1)S(1)}, u32[]{:S(2)}, u32[]{:S(2)}) collective-permute-start(bf16[16,2048]{1,0:T(8,128)(2,1)S(1)} %pad_maximum_fusion.2), channel_id=1, source_target_pairs={{0,3},{1,2},{2,1},{3,0},{4,7},{5,6},{6,5},{7,4},{8,11},{9,10},{10,... | collective-permute-start | bytes 196616 | tf_op jit(solution)/shard_map/ppermute | solution.py:301
  49.5 7.8 %collective-permute-start.17 = (bf16[16,2048]{1,0:T(8,128)(2,1)S(1)}, bf16[16,2048]{1,0:T(8,128)(2,1)S(1)}, u32[]{:S(2)}, u32[]{:S(2)}) collective-permute-start(bf16[16,2048]{1,0:T(8,128)(2,1)S(1)} %pad_maximum_fusion.3), channel_id=1, source_target_pairs={{0,2},{1,3},{2,0},{3,1},{4,6},{5,7},{6,4},{7,5},{8,10},{9,11},{10,... | collective-permute-start | bytes 196616 | tf_op jit(solution)/shard_map/ppermute | solution.py:301
  50.3 6.9 %collective-permute-start.18 = (bf16[16,2048]{1,0:T(8,128)(2,1)S(1)}, bf16[16,2048]{1,0:T(8,128)(2,1)S(1)}, u32[]{:S(2)}, u32[]{:S(2)}) collective-permute-start(bf16[16,2048]{1,0:T(8,128)(2,1)S(1)} %pad_maximum_fusion.4), channel_id=1, source_target_pairs={{0,1},{1,0},{2,3},{3,2},{4,5},{5,4},{6,7},{7,6},{8,9},{9,8},{10,11... | collective-permute-start | bytes 196616 | tf_op jit(solution)/shard_map/ppermute | solution.py:301

commit v18 on v17

--- a/solution.py
+++ b/solution.py
@@ -17,8 +17,8 @@
 F32, BF16 = jnp.float32, jnp.bfloat16
 
 
-def params():
-    return pltpu.CompilerParams(vmem_limit_bytes=VMEM_BYTES)
+def params(size=VMEM_BYTES):
+    return pltpu.CompilerParams(vmem_limit_bytes=size)
 
 
 def in_hbm(value):
@@ -99,7 +99,7 @@
             pltpu.SemaphoreType.DMA,
             pltpu.SemaphoreType.DMA((chunks,)),
         ],
-        compiler_params=params(),
+        compiler_params=params(60 * 2**20),
         name="select_rows",
     )(in_hbm(mask.reshape(1, tokens)), in_hbm(hidden))
     return own, picker

time: 58.5 us -> 60.9 us (1.041)
  starting transfers between devices: 18.7 us -> 17.7 us
  other arithmetic: 0.47 us -> 1.43 us
  local copies, waits for them, and re-layouts: 0.13 us -> 1.04 us
  blocking collectives: 12.9 us -> 13.6 us
    concatenate x1, other arithmetic: 0.02 us -> 0.99 us  [body(): jnp.concatenate(source, axis=1)]
    unnamed x8 -> x14, local copies, waits for them, and re-layouts: 0.07 us -> 0.97 us
    ppermute x10, starting transfers between devices: 13.2 us -> 12.3 us  [swap_chip(): lax.ppermute(value, 'seq', [(i, i ^ flips[i & 1]) for i in range(n_seq)])]
    all_to_all x1, blocking collectives: 12.9 us -> 13.6 us  [body(): stats = lax.all_to_all(stats, ('seq', 'vocab'), 0, 0, tiled=True)]
  transfers between devices with their start and end apart: 19 -> 19, of which waited for: 14 -> 13; matrix products, arithmetic and copies ran while one was open for 1% -> 2% of each run, Pallas kernels for 3% -> 3%
where the time goes in v18:
time: 60.9 us; the launch traced here: 60.7 us
  starting transfers between devices  17.7 us (29%)
  waiting for transfers between devices  17.1 us (28%)
  blocking collectives  13.6 us (22%)
  Pallas kernels  7.78 us (13%)
  other arithmetic  1.43 us (2%)
  matrix products  1.11 us (2%)
  local copies, waits for them, and re-layouts  1.04 us (2%)
  between operations  0.83 us (1%)
    all_to_all x1, blocking collectives, body(): stats = lax.all_to_all(stats, ('seq', 'vocab'), 0, 0, tiled=True)  13.6 us
    ppermute x10, starting transfers between devices, swap_chip(): lax.ppermute(value, 'seq', [(i, i ^ flips[i & 1]) for i in range(n_seq)])  12.3 us
    ppermute x10, waiting for transfers between devices, swap_chip(): lax.ppermute(value, 'seq', [(i, i ^ flips[i & 1]) for i in range(n_seq)])  10.9 us
    ppermute x3, starting transfers between devices, send_vocab(): return lax.ppermute(value, 'vocab', [(i, i ^ k) for i in range(n_vocab)])  4.45 us
    ppermute x3, waiting for transfers between devices, send_vocab(): return lax.ppermute(value, 'vocab', [(i, i ^ k) for i in range(n_vocab)])  3.43 us
    pallas_call x1, Pallas kernels, select(): pl.pallas_call(select_kernel, in_specs=[pl.BlockSpec(memory_space=pltpu.H...  3.12 us
    ppermute x6, waiting for transfers between devices, swap_core(): return lax.ppermute(value, 'seq', [(i, i ^ 1) for i in range(n_seq)])  2.77 us
    pallas_call x1, Pallas kernels, gradients(): pl.pallas_call(functools.partial(gradient_kernel, n_seq, n_vocab), in_spe...  1.63 us
  transfers between devices with their start and end apart: 19, of which 13 were waited for; matrix products, arithmetic and copies ran while one was open for 2% of the time, Pallas kernels for 3%

profile of v18, /device:TPU:0, one launch (start us, length us, event | category | flops | bytes accessed | tf_op | source)
XLA Modules:
  0.0 60.7 jit_solution(7059275421620508902)
XLA Ops:
  0.6 3.1 %select_rows.1 = (bf16[16,4096]{1,0:T(8,128)(2,1)}, bf16[16,4096]{1,0:T(8,128)(2,1)}, bf16[16,128]{1,0:T(8,128)(2,1)}) custom-call(s32[1,128]{1,0:T(1,128)} %bitcast.46, bf16[128,8192]{1,0:T(8,128)(2,1)} %hidden_ref.1), custom_call_target="tpu_custom_call" | custom-call | tf_op jit(solution)/shard_map/select_rows/pallas_call | solution.py:92
  3.8 0.0 copy-start
  3.8 3.0 %collective-permute-start = (bf16[16,4096]{1,0:T(8,128)(2,1)}, bf16[16,4096]{1,0:T(8,128)(2,1)S(1)}, u32[]{:S(2)}, u32[]{:S(2)}) collective-permute-start(bf16[16,4096]{1,0:T(8,128)(2,1)} %get-tuple-element.25.own_ref), channel_id=1, source_target_pairs={{0,8},{4,20},{8,0},{12,28},{16,24},{20,4},{24,16},{28,12},{1,9},{5... | collective-permute-start | bytes 393224 | tf_op jit(solution)/shard_map/ppermute | solution.py:298
  6.8 0.1 collective-permute-start.2
  6.8 1.0 %pad_maximum_fusion = bf16[16,8192]{1,0:T(8,128)(2,1)S(1)} fusion(bf16[16,4096]{1,0:T(8,128)(2,1)} %get-tuple-element.26, bf16[16,4096]{1,0:T(8,128)(2,1)} %get-tuple-element.25.own_ref), kind=kLoop, calls=%fused_computation.1 | loop fusion | flops 524288 | bytes 524288 | tf_op jit(solution)/shard_map/concatenate | solution.py:311
  7.8 0.0 copy-start.1
  7.8 0.9 %copy-done.1 = bf16[16,4096]{1,0:T(8,128)(2,1)S(1)} copy-done((bf16[16,4096]{1,0:T(8,128)(2,1)S(1)}, bf16[16,4096]{1,0:T(8,128)(2,1)}, u32[]{:S(2)}) %copy-start.1) | copy-done | bytes 131096
  8.7 1.3 %own_logits.1.refs_0_ = f32[16,256]{1,0:T(8,128)S(1)} custom-call(bf16[16,4096]{1,0:T(8,128)(2,1)S(1)} %copy-done.1, bf16[8192,256]{1,0:T(8,128)(2,1)} %head_ref.3), custom_call_target="tpu_custom_call" | custom-call | tf_op jit(solution)/shard_map/own_logits/pallas_call | solution.py:127
  10.0 2.0 %collective-permute-start.1 = (bf16[16,8192]{1,0:T(8,128)(2,1)S(1)}, bf16[16,8192]{1,0:T(8,128)(2,1)S(1)}, u32[]{:S(2)}, u32[]{:S(2)}) collective-permute-start(bf16[16,8192]{1,0:T(8,128)(2,1)S(1)} %pad_maximum_fusion), channel_id=1, source_target_pairs={{0,16},{4,12},{8,24},{12,4},{16,0},{20,28},{24,8},{28,20},{1,17},{... | collective-permute-start | bytes 786440 | tf_op jit(solution)/shard_map/ppermute | solution.py:298
  12.1 0.1 collective-permute-start.3
  12.2 0.0 collective-permute-done.2
  12.2 2.0 %collective-permute-start.5 = (bf16[16,4096]{1,0:T(8,128)(2,1)S(1)}, bf16[16,4096]{1,0:T(8,128)(2,1)S(1)}, u32[]{:S(2)}, u32[]{:S(2)}) collective-permute-start(bf16[16,4096]{1,0:T(8,128)(2,1)S(1)} %collective-permute-done.2), channel_id=1, source_target_pairs={{0,16},{4,12},{8,24},{12,4},{16,0},{20,28},{24,8},{28,20},{1,17},{... | collective-permute-start | bytes 393224 | tf_op jit(solution)/shard_map/ppermute | solution.py:298
  14.2 2.3 %collective-permute-done.1 = bf16[16,8192]{1,0:T(8,128)(2,1)S(1)} collective-permute-done((bf16[16,8192]{1,0:T(8,128)(2,1)S(1)}, bf16[16,8192]{1,0:T(8,128)(2,1)S(1)}, u32[]{:S(2)}, u32[]{:S(2)}) %collective-permute-start.1) | collective-permute-done | bytes 262176 | tf_op jit(solution)/shard_map/ppermute | solution.py:298
  16.5 1.3 %collective-permute-done.3 = bf16[16,4096]{1,0:T(8,128)(2,1)S(1)} collective-permute-done((bf16[16,4096]{1,0:T(8,128)(2,1)S(1)}, bf16[16,4096]{1,0:T(8,128)(2,1)S(1)}, u32[]{:S(2)}, u32[]{:S(2)}) %collective-permute-start.3) | collective-permute-done | bytes 131104 | tf_op jit(solution)/shard_map/ppermute | solution.py:298
  17.9 0.0 collective-permute-start.4
  17.9 1.4 %collective-permute-done.5 = bf16[16,4096]{1,0:T(8,128)(2,1)S(1)} collective-permute-done((bf16[16,4096]{1,0:T(8,128)(2,1)S(1)}, bf16[16,4096]{1,0:T(8,128)(2,1)S(1)}, u32[]{:S(2)}, u32[]{:S(2)}) %collective-permute-start.5) | collective-permute-done | bytes 131104 | tf_op jit(solution)/shard_map/ppermute | solution.py:298
  19.3 0.1 collective-permute-start.6
  19.4 1.5 %collective-permute-done.6.refs_4_ = bf16[32,4096]{1,0:T(8,128)(2,1)S(1)} collective-permute-done((bf16[32,4096]{1,0:T(8,128)(2,1)S(1)}, bf16[32,4096]{1,0:T(8,128)(2,1)S(1)}, u32[]{:S(2)}, u32[]{:S(2)}) %collective-permute-start.6) | collective-permute-done | bytes 262176 | tf_op jit(solution)/shard_map/ppermute | solution.py:294
  20.9 1.0 %local_logits.1 = (f32[128,256]{1,0:T(8,128)S(1)}, f32[32,4,128]{2,1,0:T(4,128)S(1)}) custom-call(f32[16,256]{1,0:T(8,128)S(1)} %own_logits.1.refs_0_, bf16[96,4096]{1,0:T(8,128)(2,1)S(1)} %slice_dynamic-update-slice_fusion.refs_1_, bf16[96,4096]{1,0:T(8,128)(2,1)S(1)} %collective-permute-done.4.refs_2_, ...), custom_call_target="tpu_custom_call" | custom-call | tf_op jit(solution)/shard_map/local_logits/pallas_call | solution.py:183
  21.9 13.6 %all_to_all.5.stats_ref = f32[32,4,128]{2,1,0:T(4,128)S(1)} all-to-all(f32[32,4,128]{2,1,0:T(4,128)S(1)} %get-tuple-element.32), channel_id=1, replica_groups=mesh['seq'=8,'vocab'=4] {'seq','vocab'}, dimensions={0} | all-to-all | bytes 131072 | tf_op jit(solution)/shard_map/all_to_all | solution.py:322
  35.5 1.6 %gradients.1 = (bf16[4,4,16,1024]{3,2,1,0:T(8,128)(2,1)S(1)}, bf16[4,4,16,1024]{3,2,1,0:T(8,128)(2,1)S(1)}, bf16[3,4,16,1024]{3,2,1,0:T(8,128)(2,1)S(1)}, bf16[3...) custom-call(f32[32,4,128]{2,1,0:T(4,128)S(1)} %all_to_all.5.stats_ref, ...), custom_call_target="tpu_custom_call" | custom-call | tf_op jit(solution)/shard_map/gradients/pallas_call | solution.py:274
  37.1 0.1 collective-permute-start.7
  37.2 0.5 collective-permute-start.8
  37.7 0.8 %collective-permute-done.7 = bf16[4,16,1024]{2,1,0:T(8,128)(2,1)S(1)} collective-permute-done((bf16[4,16,1024]{2,1,0:T(8,128)(2,1)S(1)}, bf16[4,16,1024]{2,1,0:T(8,128)(2,1)S(1)}, u32[]{:S(2)}, u32[]{:S(2)}) %collective-permute-start.7) | collective-permute-done | bytes 131104 | tf_op jit(solution)/shard_map/ppermute | solution.py:294
  38.6 0.2 collective-permute-done.8
  38.7 0.3 collective-permute-start.9
  39.1 0.7 %collective-permute-start.12 = (bf16[4,16,1024]{2,1,0:T(8,128)(2,1)S(1)}, bf16[4,16,1024]{2,1,0:T(8,128)(2,1)S(1)}, u32[]{:S(2)}, u32[]{:S(2)}) collective-permute-start(bf16[4,16,1024]{2,1,0:T(8,128)(2,1)S(1)} %fusion.1), channel_id=1, source_target_pairs={{0,16},{4,12},{8,24},{12,4},{16,0},{20,28},{24,8},{28,20},{1,17},{... | collective-permute-start | bytes 393224 | tf_op jit(solution)/shard_map/ppermute | solution.py:298
  39.9 1.4 %collective-permute-start.14 = (bf16[4,16,1024]{2,1,0:T(8,128)(2,1)S(1)}, bf16[4,16,1024]{2,1,0:T(8,128)(2,1)S(1)}, u32[]{:S(2)}, u32[]{:S(2)}) collective-permute-start(bf16[4,16,1024]{2,1,0:T(8,128)(2,1)S(1)} %fusion), channel_id=1, source_target_pairs={{0,16},{4,12},{8,24},{12,4},{16,0},{20,28},{24,8},{28,20},{1,17},{... | collective-permute-start | bytes 393224 | tf_op jit(solution)/shard_map/ppermute | solution.py:298
  41.3 0.0 collective-permute-done.9
  41.4 0.2 collective-permute-done.10
  41.6 1.4 %collective-permute-start.11 = (bf16[4,16,2048]{2,1,0:T(8,128)(2,1)S(1)}, bf16[4,16,2048]{2,1,0:T(8,128)(2,1)S(1)}, u32[]{:S(2)}, u32[]{:S(2)}) collective-permute-start(bf16[4,16,2048]{2,1,0:T(8,128)(2,1)S(1)} %pad_maximum_fusion.1), channel_id=1, source_target_pairs={{0,16},{4,12},{8,24},{12,4},{16,0},{20,28},{24,8},{28,20},{1,17},{... | collective-permute-start | bytes 786440 | tf_op jit(solution)/shard_map/ppermute | solution.py:298
  43.1 1.1 %collective-permute-done.12 = bf16[4,16,1024]{2,1,0:T(8,128)(2,1)S(1)} collective-permute-done((bf16[4,16,1024]{2,1,0:T(8,128)(2,1)S(1)}, bf16[4,16,1024]{2,1,0:T(8,128)(2,1)S(1)}, u32[]{:S(2)}, u32[]{:S(2)}) %collective-permute-start.12) | collective-permute-done | bytes 131104 | tf_op jit(solution)/shard_map/ppermute | solution.py:298
  44.1 0.1 fusion.4
  44.2 0.7 %collective-permute-start.13 = (bf16[4,16,1024]{2,1,0:T(8,128)(2,1)S(1)}, bf16[4,16,1024]{2,1,0:T(8,128)(2,1)S(1)}, u32[]{:S(2)}, u32[]{:S(2)}) collective-permute-start(bf16[4,16,1024]{2,1,0:T(8,128)(2,1)S(1)} %fusion.4), channel_id=1, source_target_pairs={{0,8},{4,20},{8,0},{12,28},{16,24},{20,4},{24,16},{28,12},{1,9},{5... | collective-permute-start | bytes 393224 | tf_op jit(solution)/shard_map/ppermute | solution.py:298
  44.9 0.6 %collective-permute-done.14 = bf16[4,16,1024]{2,1,0:T(8,128)(2,1)S(1)} collective-permute-done((bf16[4,16,1024]{2,1,0:T(8,128)(2,1)S(1)}, bf16[4,16,1024]{2,1,0:T(8,128)(2,1)S(1)}, u32[]{:S(2)}, u32[]{:S(2)}) %collective-permute-start.14) | collective-permute-done | bytes 131104 | tf_op jit(solution)/shard_map/ppermute | solution.py:298
  45.5 0.1 fusion.2
  45.6 0.8 %collective-permute-start.15 = (bf16[4,16,1024]{2,1,0:T(8,128)(2,1)S(1)}, bf16[4,16,1024]{2,1,0:T(8,128)(2,1)S(1)}, u32[]{:S(2)}, u32[]{:S(2)}) collective-permute-start(bf16[4,16,1024]{2,1,0:T(8,128)(2,1)S(1)} %fusion.2), channel_id=1, source_target_pairs={{0,8},{4,20},{8,0},{12,28},{16,24},{20,4},{24,16},{28,12},{1,9},{5... | collective-permute-start | bytes 393224 | tf_op jit(solution)/shard_map/ppermute | solution.py:298
  46.4 2.8 %collective-permute-done.13 = bf16[4,16,1024]{2,1,0:T(8,128)(2,1)S(1)} collective-permute-done((bf16[4,16,1024]{2,1,0:T(8,128)(2,1)S(1)}, bf16[4,16,1024]{2,1,0:T(8,128)(2,1)S(1)}, u32[]{:S(2)}, u32[]{:S(2)}) %collective-permute-start.13) | collective-permute-done | bytes 131104 | tf_op jit(solution)/shard_map/ppermute | solution.py:298
  49.2 1.4 %collective-permute-done.15 = bf16[4,16,1024]{2,1,0:T(8,128)(2,1)S(1)} collective-permute-done((bf16[4,16,1024]{2,1,0:T(8,128)(2,1)S(1)}, bf16[4,16,1024]{2,1,0:T(8,128)(2,1)S(1)}, u32[]{:S(2)}, u32[]{:S(2)}) %collective-permute-start.15) | collective-permute-done | bytes 131104 | tf_op jit(solution)/shard_map/ppermute | solution.py:298
  50.6 0.0 collective-permute-done.11
  50.6 0.2 fusion.3
  50.9 0.9 %collective-permute-start.16 = (bf16[16,2048]{1,0:T(8,128)(2,1)S(1)}, bf16[16,2048]{1,0:T(8,128)(2,1)S(1)}, u32[]{:S(2)}, u32[]{:S(2)}) collective-permute-start(bf16[16,2048]{1,0:T(8,128)(2,1)S(1)} %pad_maximum_fusion.2), channel_id=1, source_target_pairs={{0,3},{1,2},{2,1},{3,0},{4,7},{5,6},{6,5},{7,4},{8,11},{9,10},{10,... | collective-permute-start | bytes 196616 | tf_op jit(solution)/shard_map/ppermute | solution.py:301
  51.8 0.9 %collective-permute-start.17 = (bf16[16,2048]{1,0:T(8,128)(2,1)S(1)}, bf16[16,2048]{1,0:T(8,128)(2,1)S(1)}, u32[]{:S(2)}, u32[]{:S(2)}) collective-permute-start(bf16[16,2048]{1,0:T(8,128)(2,1)S(1)} %pad_maximum_fusion.3), channel_id=1, source_target_pairs={{0,2},{1,3},{2,0},{3,1},{4,6},{5,7},{6,4},{7,5},{8,10},{9,11},{10,... | collective-permute-start | bytes 196616 | tf_op jit(solution)/shard_map/ppermute | solution.py:301
  52.6 2.7 %collective-permute-start.18 = (bf16[16,2048]{1,0:T(8,128)(2,1)S(1)}, bf16[16,2048]{1,0:T(8,128)(2,1)S(1)}, u32[]{:S(2)}, u32[]{:S(2)}) collective-permute-start(bf16[16,2048]{1,0:T(8,128)(2,1)S(1)} %pad_maximum_fusion.4), channel_id=1, source_target_pairs={{0,1},{1,0},{2,3},{3,2},{4,5},{5,4},{6,7},{7,6},{8,9},{9,8},{10,11... | collective-permute-start | bytes 196616 | tf_op jit(solution)/shard_map/ppermute | solution.py:301
  55.3 0.8 %entropies.1 = (f32[1,128]{1,0:T(1,128)}, f32[1,1]{1,0:T(1,128)}) custom-call(f32[32,4,128]{2,1,0:T(4,128)S(1)} %all_to_all.5.stats_ref, bf16[16,128]{1,0:T(8,128)(2,1)S(1)} %copy-done.2), custom_call_target="tpu_custom_call" | custom-call | tf_op jit(solution)/shard_map/entropies/pallas_call | solution.py:223
  56.1 1.6 %collective-permute-done.16 = bf16[16,2048]{1,0:T(8,128)(2,1)S(1)} collective-permute-done((bf16[16,2048]{1,0:T(8,128)(2,1)S(1)}, bf16[16,2048]{1,0:T(8,128)(2,1)S(1)}, u32[]{:S(2)}, u32[]{:S(2)}) %collective-permute-start.16) | collective-permute-done | bytes 65568 | tf_op jit(solution)/shard_map/ppermute | solution.py:301
  57.7 1.8 %collective-permute-done.17 = bf16[16,2048]{1,0:T(8,128)(2,1)S(1)} collective-permute-done((bf16[16,2048]{1,0:T(8,128)(2,1)S(1)}, bf16[16,2048]{1,0:T(8,128)(2,1)S(1)}, u32[]{:S(2)}, u32[]{:S(2)}) %collective-permute-start.17) | collective-permute-done | bytes 65568 | tf_op jit(solution)/shard_map/ppermute | solution.py:301
  59.5 1.1 %convolution_convert_fusion = bf16[128,2048]{1,0:T(8,128)(2,1)} fusion(bf16[16,128]{1,0:T(8,128)(2,1)S(1)} %copy-done.2, f32[16,1024]{1,0:T(8,128)S(1)} %get-tuple-element.55, f32[16,1024]{1,0:T(8,128)S(1)} %get-tuple-element.56, bf16[16,2048]{1,0:T(8,128)(2,1)S(1)} %collective-permute-done.18, bf16[16,2048]{1,0:T(8,128)(2,1)S(1)} %collective-permute-done.17, ...), kind=kOutput, calls=%fused_computation | convolution fusion | flops 8912896 | bytes 856064 | tf_op jit(solution)/shard_map/dot_general | solution.py:357
  (27 shorter events, 0.3 us)
Async XLA Ops:
  3.8 17.1 %copy-start = (bf16[8192,256]{1,0:T(8,128)(2,1)S(1)}, bf16[8192,256]{1,0:T(8,128)(2,1)}, u32[]{:S(2)}) copy-start(bf16[8192,256]{1,0:T(8,128)(2,1)} %head_ref.3) | copy-start | bytes 12582916
  3.8 8.3 %collective-permute-start = (bf16[16,4096]{1,0:T(8,128)(2,1)}, bf16[16,4096]{1,0:T(8,128)(2,1)S(1)}, u32[]{:S(2)}, u32[]{:S(2)}) collective-permute-start(bf16[16,4096]{1,0:T(8,128)(2,1)} %get-tuple-element.25.own_ref), channel_id=1, source_target_pairs={{0,8},{4,20},{8,0},{12,28},{16,24},{20,4},{24,16},{28,12},{1,9},{5... | collective-permute-start | bytes 393224 | tf_op jit(solution)/shard_map/ppermute | solution.py:298
  6.8 5.4 %collective-permute-start.2 = (bf16[16,4096]{1,0:T(8,128)(2,1)}, bf16[16,4096]{1,0:T(8,128)(2,1)S(1)}, u32[]{:S(2)}, u32[]{:S(2)}) collective-permute-start(bf16[16,4096]{1,0:T(8,128)(2,1)} %get-tuple-element.26), channel_id=1, source_target_pairs={{0,8},{4,20},{8,0},{12,28},{16,24},{20,4},{24,16},{28,12},{1,9},{5... | collective-permute-start | bytes 393224 | tf_op jit(solution)/shard_map/ppermute | solution.py:298
  7.8 0.9 %copy-start.1 = (bf16[16,4096]{1,0:T(8,128)(2,1)S(1)}, bf16[16,4096]{1,0:T(8,128)(2,1)}, u32[]{:S(2)}) copy-start(bf16[16,4096]{1,0:T(8,128)(2,1)} %get-tuple-element.25.own_ref) | copy-start | bytes 393220
  8.7 7.7 %copy-start.3 = (bf16[16,4096]{1,0:T(8,128)(2,1)S(1)}, bf16[16,4096]{1,0:T(8,128)(2,1)}, u32[]{:S(2)}) copy-start(bf16[16,4096]{1,0:T(8,128)(2,1)} %get-tuple-element.26) | copy-start | bytes 393220
  8.7 12.1 %copy-start.2 = (bf16[16,128]{1,0:T(8,128)(2,1)S(1)}, bf16[16,128]{1,0:T(8,128)(2,1)}, u32[]{:S(2)}) copy-start(bf16[16,128]{1,0:T(8,128)(2,1)} %get-tuple-element.31.refs_6_.picker_ref) | copy-start | bytes 12292
  10.0 6.4 %collective-permute-start.1 = (bf16[16,8192]{1,0:T(8,128)(2,1)S(1)}, bf16[16,8192]{1,0:T(8,128)(2,1)S(1)}, u32[]{:S(2)}, u32[]{:S(2)}) collective-permute-start(bf16[16,8192]{1,0:T(8,128)(2,1)S(1)} %pad_maximum_fusion), channel_id=1, source_target_pairs={{0,16},{4,12},{8,24},{12,4},{16,0},{20,28},{24,8},{28,20},{1,17},{... | collective-permute-start | bytes 786440 | tf_op jit(solution)/shard_map/ppermute | solution.py:298
  12.1 5.8 %collective-permute-start.3 = (bf16[16,4096]{1,0:T(8,128)(2,1)S(1)}, bf16[16,4096]{1,0:T(8,128)(2,1)S(1)}, u32[]{:S(2)}, u32[]{:S(2)}) collective-permute-start(bf16[16,4096]{1,0:T(8,128)(2,1)S(1)} %collective-permute-done), channel_id=1, source_target_pairs={{0,16},{4,12},{8,24},{12,4},{16,0},{20,28},{24,8},{28,20},{1,17},{... | collective-permute-start | bytes 393224 | tf_op jit(solution)/shard_map/ppermute | solution.py:298
  12.2 7.1 %collective-permute-start.5 = (bf16[16,4096]{1,0:T(8,128)(2,1)S(1)}, bf16[16,4096]{1,0:T(8,128)(2,1)S(1)}, u32[]{:S(2)}, u32[]{:S(2)}) collective-permute-start(bf16[16,4096]{1,0:T(8,128)(2,1)S(1)} %collective-permute-done.2), channel_id=1, source_target_pairs={{0,16},{4,12},{8,24},{12,4},{16,0},{20,28},{24,8},{28,20},{1,17},{... | collective-permute-start | bytes 393224 | tf_op jit(solution)/shard_map/ppermute | solution.py:298
  17.9 3.0 %collective-permute-start.4 = (bf16[96,4096]{1,0:T(8,128)(2,1)S(1)}, bf16[96,4096]{1,0:T(8,128)(2,1)S(1)}, u32[]{:S(2)}, u32[]{:S(2)}) collective-permute-start(bf16[96,4096]{1,0:T(8,128)(2,1)S(1)} %slice_dynamic-update-slice_fusion.refs_1_), channel_id=1, source_target_pairs={{0,4},{4,0},{8,12},{12,8},{16,20},{20,16},{24,28},{28,24},{1,5},{5... | collective-permute-start | bytes 2359304 | tf_op jit(solution)/shard_map/ppermute | solution.py:294
  19.3 1.6 %collective-permute-start.6 = (bf16[32,4096]{1,0:T(8,128)(2,1)S(1)}, bf16[32,4096]{1,0:T(8,128)(2,1)S(1)}, u32[]{:S(2)}, u32[]{:S(2)}) collective-permute-start(bf16[32,4096]{1,0:T(8,128)(2,1)S(1)} %constant_dynamic-update-slice_fusion.4.refs_3_), channel_id=1, source_target_pairs={{0,4},{4,0},{8,12},{12,8},{16,20},{20,16},{24,28},{28,24},{1,5},{5... | collective-permute-start | bytes 786440 | tf_op jit(solution)/shard_map/ppermute | solution.py:294
  37.1 1.4 %collective-permute-start.7 = (bf16[4,16,1024]{2,1,0:T(8,128)(2,1)S(1)}, bf16[4,16,1024]{2,1,0:T(8,128)(2,1)S(1)}, u32[]{:S(2)}, u32[]{:S(2)}) collective-permute-start(bf16[4,16,1024]{2,1,0:T(8,128)(2,1)S(1)} %get-tuple-element.37), channel_id=1, source_target_pairs={{0,4},{4,0},{8,12},{12,8},{16,20},{20,16},{24,28},{28,24},{1,5},{5... | collective-permute-start | bytes 393224 | tf_op jit(solution)/shard_map/ppermute | solution.py:294
  37.2 1.5 %collective-permute-start.8 = (bf16[4,16,1024]{2,1,0:T(8,128)(2,1)S(1)}, bf16[4,16,1024]{2,1,0:T(8,128)(2,1)S(1)}, u32[]{:S(2)}, u32[]{:S(2)}) collective-permute-start(bf16[4,16,1024]{2,1,0:T(8,128)(2,1)S(1)} %get-tuple-element.38), channel_id=1, source_target_pairs={{0,4},{4,0},{8,12},{12,8},{16,20},{20,16},{24,28},{28,24},{1,5},{5... | collective-permute-start | bytes 393224 | tf_op jit(solution)/shard_map/ppermute | solution.py:294
  38.7 2.6 %collective-permute-start.9 = (bf16[3,4,16,1024]{3,2,1,0:T(8,128)(2,1)S(1)}, bf16[3,4,16,1024]{3,2,1,0:T(8,128)(2,1)S(1)}, u32[]{:S(2)}, u32[]{:S(2)}) collective-permute-start(bf16[3,4,16,1024]{3,2,1,0:T(8,128)(2,1)S(1)} %get-tuple-element.39), channel_id=1, source_target_pairs={{0,4},{4,0},{8,12},{12,8},{16,20},{20,16},{24,28},{28,24},{1,5},{5... | collective-permute-start | bytes 1179656 | tf_op jit(solution)/shard_map/ppermute | solution.py:294
  39.1 5.0 %collective-permute-start.12 = (bf16[4,16,1024]{2,1,0:T(8,128)(2,1)S(1)}, bf16[4,16,1024]{2,1,0:T(8,128)(2,1)S(1)}, u32[]{:S(2)}, u32[]{:S(2)}) collective-permute-start(bf16[4,16,1024]{2,1,0:T(8,128)(2,1)S(1)} %fusion.1), channel_id=1, source_target_pairs={{0,16},{4,12},{8,24},{12,4},{16,0},{20,28},{24,8},{28,20},{1,17},{... | collective-permute-start | bytes 393224 | tf_op jit(solution)/shard_map/ppermute | solution.py:298
  39.9 1.7 %collective-permute-start.10 = (bf16[3,4,16,1024]{3,2,1,0:T(8,128)(2,1)S(1)}, bf16[3,4,16,1024]{3,2,1,0:T(8,128)(2,1)S(1)}, u32[]{:S(2)}, u32[]{:S(2)}) collective-permute-start(bf16[3,4,16,1024]{3,2,1,0:T(8,128)(2,1)S(1)} %get-tuple-element.41), channel_id=1, source_target_pairs={{0,4},{4,0},{8,12},{12,8},{16,20},{20,16},{24,28},{28,24},{1,5},{5... | collective-permute-start | bytes 1179656 | tf_op jit(solution)/shard_map/ppermute | solution.py:294
  39.9 5.7 %collective-permute-start.14 = (bf16[4,16,1024]{2,1,0:T(8,128)(2,1)S(1)}, bf16[4,16,1024]{2,1,0:T(8,128)(2,1)S(1)}, u32[]{:S(2)}, u32[]{:S(2)}) collective-permute-start(bf16[4,16,1024]{2,1,0:T(8,128)(2,1)S(1)} %fusion), channel_id=1, source_target_pairs={{0,16},{4,12},{8,24},{12,4},{16,0},{20,28},{24,8},{28,20},{1,17},{... | collective-permute-start | bytes 393224 | tf_op jit(solution)/shard_map/ppermute | solution.py:298
  41.6 9.0 %collective-permute-start.11 = (bf16[4,16,2048]{2,1,0:T(8,128)(2,1)S(1)}, bf16[4,16,2048]{2,1,0:T(8,128)(2,1)S(1)}, u32[]{:S(2)}, u32[]{:S(2)}) collective-permute-start(bf16[4,16,2048]{2,1,0:T(8,128)(2,1)S(1)} %pad_maximum_fusion.1), channel_id=1, source_target_pairs={{0,16},{4,12},{8,24},{12,4},{16,0},{20,28},{24,8},{28,20},{1,17},{... | collective-permute-start | bytes 786440 | tf_op jit(solution)/shard_map/ppermute | solution.py:298
  44.2 5.0 %collective-permute-start.13 = (bf16[4,16,1024]{2,1,0:T(8,128)(2,1)S(1)}, bf16[4,16,1024]{2,1,0:T(8,128)(2,1)S(1)}, u32[]{:S(2)}, u32[]{:S(2)}) collective-permute-start(bf16[4,16,1024]{2,1,0:T(8,128)(2,1)S(1)} %fusion.4), channel_id=1, source_target_pairs={{0,8},{4,20},{8,0},{12,28},{16,24},{20,4},{24,16},{28,12},{1,9},{5... | collective-permute-start | bytes 393224 | tf_op jit(solution)/shard_map/ppermute | solution.py:298
  45.6 5.0 %collective-permute-start.15 = (bf16[4,16,1024]{2,1,0:T(8,128)(2,1)S(1)}, bf16[4,16,1024]{2,1,0:T(8,128)(2,1)S(1)}, u32[]{:S(2)}, u32[]{:S(2)}) collective-permute-start(bf16[4,16,1024]{2,1,0:T(8,128)(2,1)S(1)} %fusion.2), channel_id=1, source_target_pairs={{0,8},{4,20},{8,0},{12,28},{16,24},{20,4},{24,16},{28,12},{1,9},{5... | collective-permute-start | bytes 393224 | tf_op jit(solution)/shard_map/ppermute | solution.py:298
  50.9 6.9 %collective-permute-start.16 = (bf16[16,2048]{1,0:T(8,128)(2,1)S(1)}, bf16[16,2048]{1,0:T(8,128)(2,1)S(1)}, u32[]{:S(2)}, u32[]{:S(2)}) collective-permute-start(bf16[16,2048]{1,0:T(8,128)(2,1)S(1)} %pad_maximum_fusion.2), channel_id=1, source_target_pairs={{0,3},{1,2},{2,1},{3,0},{4,7},{5,6},{6,5},{7,4},{8,11},{9,10},{10,... | collective-permute-start | bytes 196616 | tf_op jit(solution)/shard_map/ppermute | solution.py:301
  51.8 7.8 %collective-permute-start.17 = (bf16[16,2048]{1,0:T(8,128)(2,1)S(1)}, bf16[16,2048]{1,0:T(8,128)(2,1)S(1)}, u32[]{:S(2)}, u32[]{:S(2)}) collective-permute-start(bf16[16,2048]{1,0:T(8,128)(2,1)S(1)} %pad_maximum_fusion.3), channel_id=1, source_target_pairs={{0,2},{1,3},{2,0},{3,1},{4,6},{5,7},{6,4},{7,5},{8,10},{9,11},{10,... | collective-permute-start | bytes 196616 | tf_op jit(solution)/shard_map/ppermute | solution.py:301
  52.6 6.9 %collective-permute-start.18 = (bf16[16,2048]{1,0:T(8,128)(2,1)S(1)}, bf16[16,2048]{1,0:T(8,128)(2,1)S(1)}, u32[]{:S(2)}, u32[]{:S(2)}) collective-permute-start(bf16[16,2048]{1,0:T(8,128)(2,1)S(1)} %pad_maximum_fusion.4), channel_id=1, source_target_pairs={{0,1},{1,0},{2,3},{3,2},{4,5},{5,4},{6,7},{7,6},{8,9},{9,8},{10,11... | collective-permute-start | bytes 196616 | tf_op jit(solution)/shard_map/ppermute | solution.py:301

commit v19 on v17

--- a/solution.py
+++ b/solution.py
@@ -319,7 +319,7 @@
     blocks = [early, swap_core(early), late, swap_core(late)]
 
     logits, stats = local_logits(n_seq, n_vocab, mine, blocks, head, picker)
-    stats = lax.all_to_all(stats, ("seq", "vocab"), 0, 0, tiled=True)
+    stats = lax.all_to_all(stats, ("vocab", "seq"), 0, 0, tiled=True)
     near, far, far_last = gradients(n_seq, n_vocab, stats, logits, head)
     moved = [swap_core(part) for part in far_last]
     far, _ = lax.optimization_barrier((far, moved))

time: 58.5 us -> 58.5 us (level)
  no operation moved by 1% of the time
where the time goes in v19:
time: 58.5 us; the launch traced here: 58.3 us
  starting transfers between devices  18.6 us (32%)
  waiting for transfers between devices  17.1 us (29%)
  blocking collectives  12.8 us (22%)
  Pallas kernels  7.36 us (13%)
  matrix products  1.11 us (2%)
  between operations  0.8 us (1%)
    ppermute x10, starting transfers between devices, swap_chip(): lax.ppermute(value, 'seq', [(i, i ^ flips[i & 1]) for i in range(n_seq)])  13 us
    all_to_all x1, blocking collectives, body(): stats = lax.all_to_all(stats, ('vocab', 'seq'), 0, 0, tiled=True)  12.8 us
    ppermute x10, waiting for transfers between devices, swap_chip(): lax.ppermute(value, 'seq', [(i, i ^ flips[i & 1]) for i in range(n_seq)])  10.9 us
    ppermute x3, starting transfers between devices, send_vocab(): return lax.ppermute(value, 'vocab', [(i, i ^ k) for i in range(n_vocab)])  4.45 us
    ppermute x3, waiting for transfers between devices, send_vocab(): return lax.ppermute(value, 'vocab', [(i, i ^ k) for i in range(n_vocab)])  3.51 us
    pallas_call x1, Pallas kernels, select(): pl.pallas_call(select_kernel, in_specs=[pl.BlockSpec(memory_space=pltpu.H...  2.75 us
    ppermute x6, waiting for transfers between devices, swap_core(): return lax.ppermute(value, 'seq', [(i, i ^ 1) for i in range(n_seq)])  2.69 us
    pallas_call x1, Pallas kernels, gradients(): pl.pallas_call(functools.partial(gradient_kernel, n_seq, n_vocab), in_spe...  1.63 us
  transfers between devices with their start and end apart: 19, of which 14 were waited for; matrix products, arithmetic and copies ran while one was open for 1% of the time, Pallas kernels for 3%

profile of v19, /device:TPU:0, one launch (start us, length us, event | category | flops | bytes accessed | tf_op | source)
XLA Modules:
  0.0 58.3 jit_solution(9822445735388091100)
XLA Ops:
  0.6 0.0 copy-start
  0.6 2.8 %select_rows.1 = (bf16[16,4096]{1,0:T(8,128)(2,1)S(1)}, bf16[16,4096]{1,0:T(8,128)(2,1)S(1)}, bf16[16,128]{1,0:T(8,128)(2,1)S(1)}) custom-call(s32[1,128]{1,0:T(1,128)} %bitcast.46, bf16[128,8192]{1,0:T(8,128)(2,1)} %hidden_ref.1), custom_call_target="tpu_custom_call" | custom-call | tf_op jit(solution)/shard_map/select_rows/pallas_call | solution.py:92
  3.4 3.0 %collective-permute-start = (bf16[16,4096]{1,0:T(8,128)(2,1)S(1)}, bf16[16,4096]{1,0:T(8,128)(2,1)S(1)}, u32[]{:S(2)}, u32[]{:S(2)}) collective-permute-start(bf16[16,4096]{1,0:T(8,128)(2,1)S(1)} %get-tuple-element.25.own_ref), channel_id=1, source_target_pairs={{0,8},{4,20},{8,0},{12,28},{16,24},{20,4},{24,16},{28,12},{1,9},{5... | collective-permute-start | bytes 393224 | tf_op jit(solution)/shard_map/ppermute | solution.py:298
  6.4 0.1 collective-permute-start.2
  6.5 1.2 %own_logits.1.refs_0_ = f32[16,256]{1,0:T(8,128)S(1)} custom-call(bf16[16,4096]{1,0:T(8,128)(2,1)S(1)} %get-tuple-element.25.own_ref, bf16[8192,256]{1,0:T(8,128)(2,1)} %head_ref.3), custom_call_target="tpu_custom_call" | custom-call | tf_op jit(solution)/shard_map/own_logits/pallas_call | solution.py:127
  7.8 2.0 %collective-permute-start.1 = (bf16[16,8192]{1,0:T(8,128)(2,1)S(1)}, bf16[16,8192]{1,0:T(8,128)(2,1)S(1)}, u32[]{:S(2)}, u32[]{:S(2)}) collective-permute-start(bf16[16,8192]{1,0:T(8,128)(2,1)S(1)} %pad_maximum_fusion), channel_id=1, source_target_pairs={{0,16},{4,12},{8,24},{12,4},{16,0},{20,28},{24,8},{28,20},{1,17},{... | collective-permute-start | bytes 786440 | tf_op jit(solution)/shard_map/ppermute | solution.py:298
  9.8 0.0 collective-permute-done
  9.8 1.6 %collective-permute-start.3 = (bf16[16,4096]{1,0:T(8,128)(2,1)S(1)}, bf16[16,4096]{1,0:T(8,128)(2,1)S(1)}, u32[]{:S(2)}, u32[]{:S(2)}) collective-permute-start(bf16[16,4096]{1,0:T(8,128)(2,1)S(1)} %collective-permute-done), channel_id=1, source_target_pairs={{0,16},{4,12},{8,24},{12,4},{16,0},{20,28},{24,8},{28,20},{1,17},{... | collective-permute-start | bytes 393224 | tf_op jit(solution)/shard_map/ppermute | solution.py:298
  11.4 1.3 %collective-permute-done.2 = bf16[16,4096]{1,0:T(8,128)(2,1)S(1)} collective-permute-done((bf16[16,4096]{1,0:T(8,128)(2,1)S(1)}, bf16[16,4096]{1,0:T(8,128)(2,1)S(1)}, u32[]{:S(2)}, u32[]{:S(2)}) %collective-permute-start.2) | collective-permute-done | bytes 131104 | tf_op jit(solution)/shard_map/ppermute | solution.py:298
  12.8 1.4 %collective-permute-start.5 = (bf16[16,4096]{1,0:T(8,128)(2,1)S(1)}, bf16[16,4096]{1,0:T(8,128)(2,1)S(1)}, u32[]{:S(2)}, u32[]{:S(2)}) collective-permute-start(bf16[16,4096]{1,0:T(8,128)(2,1)S(1)} %collective-permute-done.2), channel_id=1, source_target_pairs={{0,16},{4,12},{8,24},{12,4},{16,0},{20,28},{24,8},{28,20},{1,17},{... | collective-permute-start | bytes 393224 | tf_op jit(solution)/shard_map/ppermute | solution.py:298
  14.1 0.1 collective-permute-done.1
  14.3 1.3 %collective-permute-done.3 = bf16[16,4096]{1,0:T(8,128)(2,1)S(1)} collective-permute-done((bf16[16,4096]{1,0:T(8,128)(2,1)S(1)}, bf16[16,4096]{1,0:T(8,128)(2,1)S(1)}, u32[]{:S(2)}, u32[]{:S(2)}) %collective-permute-start.3) | collective-permute-done | bytes 131104 | tf_op jit(solution)/shard_map/ppermute | solution.py:298
  15.6 0.1 collective-permute-start.4
  15.7 2.0 %collective-permute-done.5 = bf16[16,4096]{1,0:T(8,128)(2,1)S(1)} collective-permute-done((bf16[16,4096]{1,0:T(8,128)(2,1)S(1)}, bf16[16,4096]{1,0:T(8,128)(2,1)S(1)}, u32[]{:S(2)}, u32[]{:S(2)}) %collective-permute-start.5) | collective-permute-done | bytes 131104 | tf_op jit(solution)/shard_map/ppermute | solution.py:298
  17.7 0.1 collective-permute-start.6
  17.8 1.5 %collective-permute-done.6.refs_4_ = bf16[32,4096]{1,0:T(8,128)(2,1)S(1)} collective-permute-done((bf16[32,4096]{1,0:T(8,128)(2,1)S(1)}, bf16[32,4096]{1,0:T(8,128)(2,1)S(1)}, u32[]{:S(2)}, u32[]{:S(2)}) %collective-permute-start.6) | collective-permute-done | bytes 262176 | tf_op jit(solution)/shard_map/ppermute | solution.py:294
  19.3 0.0 collective-permute-done.4.refs_2_
  19.3 1.0 %local_logits.1 = (f32[128,256]{1,0:T(8,128)S(1)}, f32[32,4,128]{2,1,0:T(4,128)S(1)}) custom-call(f32[16,256]{1,0:T(8,128)S(1)} %own_logits.1.refs_0_, bf16[96,4096]{1,0:T(8,128)(2,1)S(1)} %slice_dynamic-update-slice_fusion.refs_1_, bf16[96,4096]{1,0:T(8,128)(2,1)S(1)} %collective-permute-done.4.refs_2_, ...), custom_call_target="tpu_custom_call" | custom-call | tf_op jit(solution)/shard_map/local_logits/pallas_call | solution.py:183
  20.3 12.8 %all_to_all.5.stats_ref = f32[32,4,128]{2,1,0:T(4,128)S(1)} all-to-all(f32[32,4,128]{2,1,0:T(4,128)S(1)} %get-tuple-element.32), channel_id=1, replica_groups=mesh['seq'=8,'vocab'=4] {'vocab','seq'}, dimensions={0} | all-to-all | bytes 131072 | tf_op jit(solution)/shard_map/all_to_all | solution.py:322
  33.1 1.6 %gradients.1 = (bf16[4,4,16,1024]{3,2,1,0:T(8,128)(2,1)S(1)}, bf16[4,4,16,1024]{3,2,1,0:T(8,128)(2,1)S(1)}, bf16[3,4,16,1024]{3,2,1,0:T(8,128)(2,1)S(1)}, bf16[3...) custom-call(f32[32,4,128]{2,1,0:T(4,128)S(1)} %all_to_all.5.stats_ref, ...), custom_call_target="tpu_custom_call" | custom-call | tf_op jit(solution)/shard_map/gradients/pallas_call | solution.py:274
  34.7 0.2 collective-permute-start.7
  34.9 0.4 collective-permute-start.8
  35.3 0.8 %collective-permute-done.7 = bf16[4,16,1024]{2,1,0:T(8,128)(2,1)S(1)} collective-permute-done((bf16[4,16,1024]{2,1,0:T(8,128)(2,1)S(1)}, bf16[4,16,1024]{2,1,0:T(8,128)(2,1)S(1)}, u32[]{:S(2)}, u32[]{:S(2)}) %collective-permute-start.7) | collective-permute-done | bytes 131104 | tf_op jit(solution)/shard_map/ppermute | solution.py:294
  36.2 0.2 collective-permute-done.8
  36.3 0.3 collective-permute-start.9
  36.7 0.7 %collective-permute-start.12 = (bf16[4,16,1024]{2,1,0:T(8,128)(2,1)S(1)}, bf16[4,16,1024]{2,1,0:T(8,128)(2,1)S(1)}, u32[]{:S(2)}, u32[]{:S(2)}) collective-permute-start(bf16[4,16,1024]{2,1,0:T(8,128)(2,1)S(1)} %fusion.1), channel_id=1, source_target_pairs={{0,16},{4,12},{8,24},{12,4},{16,0},{20,28},{24,8},{28,20},{1,17},{... | collective-permute-start | bytes 393224 | tf_op jit(solution)/shard_map/ppermute | solution.py:298
  37.4 0.0 collective-permute-start.10
  37.4 1.5 %collective-permute-start.14 = (bf16[4,16,1024]{2,1,0:T(8,128)(2,1)S(1)}, bf16[4,16,1024]{2,1,0:T(8,128)(2,1)S(1)}, u32[]{:S(2)}, u32[]{:S(2)}) collective-permute-start(bf16[4,16,1024]{2,1,0:T(8,128)(2,1)S(1)} %fusion), channel_id=1, source_target_pairs={{0,16},{4,12},{8,24},{12,4},{16,0},{20,28},{24,8},{28,20},{1,17},{... | collective-permute-start | bytes 393224 | tf_op jit(solution)/shard_map/ppermute | solution.py:298
  39.0 0.1 collective-permute-done.10
  39.2 1.5 %collective-permute-start.11 = (bf16[4,16,2048]{2,1,0:T(8,128)(2,1)S(1)}, bf16[4,16,2048]{2,1,0:T(8,128)(2,1)S(1)}, u32[]{:S(2)}, u32[]{:S(2)}) collective-permute-start(bf16[4,16,2048]{2,1,0:T(8,128)(2,1)S(1)} %pad_maximum_fusion.1), channel_id=1, source_target_pairs={{0,16},{4,12},{8,24},{12,4},{16,0},{20,28},{24,8},{28,20},{1,17},{... | collective-permute-start | bytes 786440 | tf_op jit(solution)/shard_map/ppermute | solution.py:298
  40.7 1.1 %collective-permute-done.12 = bf16[4,16,1024]{2,1,0:T(8,128)(2,1)S(1)} collective-permute-done((bf16[4,16,1024]{2,1,0:T(8,128)(2,1)S(1)}, bf16[4,16,1024]{2,1,0:T(8,128)(2,1)S(1)}, u32[]{:S(2)}, u32[]{:S(2)}) %collective-permute-start.12) | collective-permute-done | bytes 131104 | tf_op jit(solution)/shard_map/ppermute | solution.py:298
  41.7 0.1 fusion.4
  41.8 0.5 collective-permute-start.13
  42.3 0.8 %collective-permute-done.14 = bf16[4,16,1024]{2,1,0:T(8,128)(2,1)S(1)} collective-permute-done((bf16[4,16,1024]{2,1,0:T(8,128)(2,1)S(1)}, bf16[4,16,1024]{2,1,0:T(8,128)(2,1)S(1)}, u32[]{:S(2)}, u32[]{:S(2)}) %collective-permute-start.14) | collective-permute-done | bytes 131104 | tf_op jit(solution)/shard_map/ppermute | solution.py:298
  43.2 0.1 fusion.2
  43.2 0.8 %collective-permute-start.15 = (bf16[4,16,1024]{2,1,0:T(8,128)(2,1)S(1)}, bf16[4,16,1024]{2,1,0:T(8,128)(2,1)S(1)}, u32[]{:S(2)}, u32[]{:S(2)}) collective-permute-start(bf16[4,16,1024]{2,1,0:T(8,128)(2,1)S(1)} %fusion.2), channel_id=1, source_target_pairs={{0,8},{4,20},{8,0},{12,28},{16,24},{20,4},{24,16},{28,12},{1,9},{5... | collective-permute-start | bytes 393224 | tf_op jit(solution)/shard_map/ppermute | solution.py:298
  44.0 2.8 %collective-permute-done.13 = bf16[4,16,1024]{2,1,0:T(8,128)(2,1)S(1)} collective-permute-done((bf16[4,16,1024]{2,1,0:T(8,128)(2,1)S(1)}, bf16[4,16,1024]{2,1,0:T(8,128)(2,1)S(1)}, u32[]{:S(2)}, u32[]{:S(2)}) %collective-permute-start.13) | collective-permute-done | bytes 131104 | tf_op jit(solution)/shard_map/ppermute | solution.py:298
  46.8 1.4 %collective-permute-done.15 = bf16[4,16,1024]{2,1,0:T(8,128)(2,1)S(1)} collective-permute-done((bf16[4,16,1024]{2,1,0:T(8,128)(2,1)S(1)}, bf16[4,16,1024]{2,1,0:T(8,128)(2,1)S(1)}, u32[]{:S(2)}, u32[]{:S(2)}) %collective-permute-start.15) | collective-permute-done | bytes 131104 | tf_op jit(solution)/shard_map/ppermute | solution.py:298
  48.2 0.0 collective-permute-done.11
  48.2 0.2 fusion.3
  48.5 1.0 %collective-permute-start.16 = (bf16[16,2048]{1,0:T(8,128)(2,1)S(1)}, bf16[16,2048]{1,0:T(8,128)(2,1)S(1)}, u32[]{:S(2)}, u32[]{:S(2)}) collective-permute-start(bf16[16,2048]{1,0:T(8,128)(2,1)S(1)} %pad_maximum_fusion.2), channel_id=1, source_target_pairs={{0,3},{1,2},{2,1},{3,0},{4,7},{5,6},{6,5},{7,4},{8,11},{9,10},{10,... | collective-permute-start | bytes 196616 | tf_op jit(solution)/shard_map/ppermute | solution.py:301
  49.5 1.2 %collective-permute-start.17 = (bf16[16,2048]{1,0:T(8,128)(2,1)S(1)}, bf16[16,2048]{1,0:T(8,128)(2,1)S(1)}, u32[]{:S(2)}, u32[]{:S(2)}) collective-permute-start(bf16[16,2048]{1,0:T(8,128)(2,1)S(1)} %pad_maximum_fusion.3), channel_id=1, source_target_pairs={{0,2},{1,3},{2,0},{3,1},{4,6},{5,7},{6,4},{7,5},{8,10},{9,11},{10,... | collective-permute-start | bytes 196616 | tf_op jit(solution)/shard_map/ppermute | solution.py:301
  50.6 2.3 %collective-permute-start.18 = (bf16[16,2048]{1,0:T(8,128)(2,1)S(1)}, bf16[16,2048]{1,0:T(8,128)(2,1)S(1)}, u32[]{:S(2)}, u32[]{:S(2)}) collective-permute-start(bf16[16,2048]{1,0:T(8,128)(2,1)S(1)} %pad_maximum_fusion.4), channel_id=1, source_target_pairs={{0,1},{1,0},{2,3},{3,2},{4,5},{5,4},{6,7},{7,6},{8,9},{9,8},{10,11... | collective-permute-start | bytes 196616 | tf_op jit(solution)/shard_map/ppermute | solution.py:301
  52.9 0.8 %entropies.1 = (f32[1,128]{1,0:T(1,128)}, f32[1,1]{1,0:T(1,128)}) custom-call(f32[32,4,128]{2,1,0:T(4,128)S(1)} %all_to_all.5.stats_ref, bf16[16,128]{1,0:T(8,128)(2,1)S(1)} %get-tuple-element.31.refs_6_.picker_ref), custom_call_target="tpu_custom_call" | custom-call | tf_op jit(solution)/shard_map/entropies/pallas_call | solution.py:223
  53.7 1.6 %collective-permute-done.16 = bf16[16,2048]{1,0:T(8,128)(2,1)S(1)} collective-permute-done((bf16[16,2048]{1,0:T(8,128)(2,1)S(1)}, bf16[16,2048]{1,0:T(8,128)(2,1)S(1)}, u32[]{:S(2)}, u32[]{:S(2)}) %collective-permute-start.16) | collective-permute-done | bytes 65568 | tf_op jit(solution)/shard_map/ppermute | solution.py:301
  55.3 1.9 %collective-permute-done.17 = bf16[16,2048]{1,0:T(8,128)(2,1)S(1)} collective-permute-done((bf16[16,2048]{1,0:T(8,128)(2,1)S(1)}, bf16[16,2048]{1,0:T(8,128)(2,1)S(1)}, u32[]{:S(2)}, u32[]{:S(2)}) %collective-permute-start.17) | collective-permute-done | bytes 65568 | tf_op jit(solution)/shard_map/ppermute | solution.py:301
  57.2 0.0 collective-permute-done.18
  57.2 1.1 %convolution_convert_fusion = bf16[128,2048]{1,0:T(8,128)(2,1)} fusion(bf16[16,128]{1,0:T(8,128)(2,1)S(1)} %get-tuple-element.31.refs_6_.picker_ref, f32[16,1024]{1,0:T(8,128)S(1)} %get-tuple-element.55, f32[16,1024]{1,0:T(8,128)S(1)} %get-tuple-element.56, bf16[16,2048]{1,0:T(8,128)(2,1)S(1)} %collective-permute-done.18, ...), kind=kOutput, calls=%fused_computation | convolution fusion | flops 8912896 | bytes 856064 | tf_op jit(solution)/shard_map/dot_general | solution.py:357
  (21 shorter events, 0.3 us)
Async XLA Ops:
  0.6 18.7 %copy-start = (bf16[8192,256]{1,0:T(8,128)(2,1)S(1)}, bf16[8192,256]{1,0:T(8,128)(2,1)}, u32[]{:S(2)}) copy-start(bf16[8192,256]{1,0:T(8,128)(2,1)} %head_ref.3) | copy-start | bytes 12582916
  3.4 6.4 %collective-permute-start = (bf16[16,4096]{1,0:T(8,128)(2,1)S(1)}, bf16[16,4096]{1,0:T(8,128)(2,1)S(1)}, u32[]{:S(2)}, u32[]{:S(2)}) collective-permute-start(bf16[16,4096]{1,0:T(8,128)(2,1)S(1)} %get-tuple-element.25.own_ref), channel_id=1, source_target_pairs={{0,8},{4,20},{8,0},{12,28},{16,24},{20,4},{24,16},{28,12},{1,9},{5... | collective-permute-start | bytes 393224 | tf_op jit(solution)/shard_map/ppermute | solution.py:298
  6.4 6.3 %collective-permute-start.2 = (bf16[16,4096]{1,0:T(8,128)(2,1)S(1)}, bf16[16,4096]{1,0:T(8,128)(2,1)S(1)}, u32[]{:S(2)}, u32[]{:S(2)}) collective-permute-start(bf16[16,4096]{1,0:T(8,128)(2,1)S(1)} %get-tuple-element.26), channel_id=1, source_target_pairs={{0,8},{4,20},{8,0},{12,28},{16,24},{20,4},{24,16},{28,12},{1,9},{5... | collective-permute-start | bytes 393224 | tf_op jit(solution)/shard_map/ppermute | solution.py:298
  7.8 6.4 %collective-permute-start.1 = (bf16[16,8192]{1,0:T(8,128)(2,1)S(1)}, bf16[16,8192]{1,0:T(8,128)(2,1)S(1)}, u32[]{:S(2)}, u32[]{:S(2)}) collective-permute-start(bf16[16,8192]{1,0:T(8,128)(2,1)S(1)} %pad_maximum_fusion), channel_id=1, source_target_pairs={{0,16},{4,12},{8,24},{12,4},{16,0},{20,28},{24,8},{28,20},{1,17},{... | collective-permute-start | bytes 786440 | tf_op jit(solution)/shard_map/ppermute | solution.py:298
  9.8 5.8 %collective-permute-start.3 = (bf16[16,4096]{1,0:T(8,128)(2,1)S(1)}, bf16[16,4096]{1,0:T(8,128)(2,1)S(1)}, u32[]{:S(2)}, u32[]{:S(2)}) collective-permute-start(bf16[16,4096]{1,0:T(8,128)(2,1)S(1)} %collective-permute-done), channel_id=1, source_target_pairs={{0,16},{4,12},{8,24},{12,4},{16,0},{20,28},{24,8},{28,20},{1,17},{... | collective-permute-start | bytes 393224 | tf_op jit(solution)/shard_map/ppermute | solution.py:298
  12.8 5.0 %collective-permute-start.5 = (bf16[16,4096]{1,0:T(8,128)(2,1)S(1)}, bf16[16,4096]{1,0:T(8,128)(2,1)S(1)}, u32[]{:S(2)}, u32[]{:S(2)}) collective-permute-start(bf16[16,4096]{1,0:T(8,128)(2,1)S(1)} %collective-permute-done.2), channel_id=1, source_target_pairs={{0,16},{4,12},{8,24},{12,4},{16,0},{20,28},{24,8},{28,20},{1,17},{... | collective-permute-start | bytes 393224 | tf_op jit(solution)/shard_map/ppermute | solution.py:298
  15.6 3.7 %collective-permute-start.4 = (bf16[96,4096]{1,0:T(8,128)(2,1)S(1)}, bf16[96,4096]{1,0:T(8,128)(2,1)S(1)}, u32[]{:S(2)}, u32[]{:S(2)}) collective-permute-start(bf16[96,4096]{1,0:T(8,128)(2,1)S(1)} %slice_dynamic-update-slice_fusion.refs_1_), channel_id=1, source_target_pairs={{0,4},{4,0},{8,12},{12,8},{16,20},{20,16},{24,28},{28,24},{1,5},{5... | collective-permute-start | bytes 2359304 | tf_op jit(solution)/shard_map/ppermute | solution.py:294
  17.7 1.6 %collective-permute-start.6 = (bf16[32,4096]{1,0:T(8,128)(2,1)S(1)}, bf16[32,4096]{1,0:T(8,128)(2,1)S(1)}, u32[]{:S(2)}, u32[]{:S(2)}) collective-permute-start(bf16[32,4096]{1,0:T(8,128)(2,1)S(1)} %constant_dynamic-update-slice_fusion.4.refs_3_), channel_id=1, source_target_pairs={{0,4},{4,0},{8,12},{12,8},{16,20},{20,16},{24,28},{28,24},{1,5},{5... | collective-permute-start | bytes 786440 | tf_op jit(solution)/shard_map/ppermute | solution.py:294
  34.7 1.4 %collective-permute-start.7 = (bf16[4,16,1024]{2,1,0:T(8,128)(2,1)S(1)}, bf16[4,16,1024]{2,1,0:T(8,128)(2,1)S(1)}, u32[]{:S(2)}, u32[]{:S(2)}) collective-permute-start(bf16[4,16,1024]{2,1,0:T(8,128)(2,1)S(1)} %get-tuple-element.37), channel_id=1, source_target_pairs={{0,4},{4,0},{8,12},{12,8},{16,20},{20,16},{24,28},{28,24},{1,5},{5... | collective-permute-start | bytes 393224 | tf_op jit(solution)/shard_map/ppermute | solution.py:294
  34.9 1.4 %collective-permute-start.8 = (bf16[4,16,1024]{2,1,0:T(8,128)(2,1)S(1)}, bf16[4,16,1024]{2,1,0:T(8,128)(2,1)S(1)}, u32[]{:S(2)}, u32[]{:S(2)}) collective-permute-start(bf16[4,16,1024]{2,1,0:T(8,128)(2,1)S(1)} %get-tuple-element.38), channel_id=1, source_target_pairs={{0,4},{4,0},{8,12},{12,8},{16,20},{20,16},{24,28},{28,24},{1,5},{5... | collective-permute-start | bytes 393224 | tf_op jit(solution)/shard_map/ppermute | solution.py:294
  36.3 2.6 %collective-permute-start.9 = (bf16[3,4,16,1024]{3,2,1,0:T(8,128)(2,1)S(1)}, bf16[3,4,16,1024]{3,2,1,0:T(8,128)(2,1)S(1)}, u32[]{:S(2)}, u32[]{:S(2)}) collective-permute-start(bf16[3,4,16,1024]{3,2,1,0:T(8,128)(2,1)S(1)} %get-tuple-element.39), channel_id=1, source_target_pairs={{0,4},{4,0},{8,12},{12,8},{16,20},{20,16},{24,28},{28,24},{1,5},{5... | collective-permute-start | bytes 1179656 | tf_op jit(solution)/shard_map/ppermute | solution.py:294
  36.7 5.0 %collective-permute-start.12 = (bf16[4,16,1024]{2,1,0:T(8,128)(2,1)S(1)}, bf16[4,16,1024]{2,1,0:T(8,128)(2,1)S(1)}, u32[]{:S(2)}, u32[]{:S(2)}) collective-permute-start(bf16[4,16,1024]{2,1,0:T(8,128)(2,1)S(1)} %fusion.1), channel_id=1, source_target_pairs={{0,16},{4,12},{8,24},{12,4},{16,0},{20,28},{24,8},{28,20},{1,17},{... | collective-permute-start | bytes 393224 | tf_op jit(solution)/shard_map/ppermute | solution.py:298
  37.4 1.7 %collective-permute-start.10 = (bf16[3,4,16,1024]{3,2,1,0:T(8,128)(2,1)S(1)}, bf16[3,4,16,1024]{3,2,1,0:T(8,128)(2,1)S(1)}, u32[]{:S(2)}, u32[]{:S(2)}) collective-permute-start(bf16[3,4,16,1024]{3,2,1,0:T(8,128)(2,1)S(1)} %get-tuple-element.41), channel_id=1, source_target_pairs={{0,4},{4,0},{8,12},{12,8},{16,20},{20,16},{24,28},{28,24},{1,5},{5... | collective-permute-start | bytes 1179656 | tf_op jit(solution)/shard_map/ppermute | solution.py:294
  37.4 5.7 %collective-permute-start.14 = (bf16[4,16,1024]{2,1,0:T(8,128)(2,1)S(1)}, bf16[4,16,1024]{2,1,0:T(8,128)(2,1)S(1)}, u32[]{:S(2)}, u32[]{:S(2)}) collective-permute-start(bf16[4,16,1024]{2,1,0:T(8,128)(2,1)S(1)} %fusion), channel_id=1, source_target_pairs={{0,16},{4,12},{8,24},{12,4},{16,0},{20,28},{24,8},{28,20},{1,17},{... | collective-permute-start | bytes 393224 | tf_op jit(solution)/shard_map/ppermute | solution.py:298
  39.2 9.1 %collective-permute-start.11 = (bf16[4,16,2048]{2,1,0:T(8,128)(2,1)S(1)}, bf16[4,16,2048]{2,1,0:T(8,128)(2,1)S(1)}, u32[]{:S(2)}, u32[]{:S(2)}) collective-permute-start(bf16[4,16,2048]{2,1,0:T(8,128)(2,1)S(1)} %pad_maximum_fusion.1), channel_id=1, source_target_pairs={{0,16},{4,12},{8,24},{12,4},{16,0},{20,28},{24,8},{28,20},{1,17},{... | collective-permute-start | bytes 786440 | tf_op jit(solution)/shard_map/ppermute | solution.py:298
  41.8 5.0 %collective-permute-start.13 = (bf16[4,16,1024]{2,1,0:T(8,128)(2,1)S(1)}, bf16[4,16,1024]{2,1,0:T(8,128)(2,1)S(1)}, u32[]{:S(2)}, u32[]{:S(2)}) collective-permute-start(bf16[4,16,1024]{2,1,0:T(8,128)(2,1)S(1)} %fusion.4), channel_id=1, source_target_pairs={{0,8},{4,20},{8,0},{12,28},{16,24},{20,4},{24,16},{28,12},{1,9},{5... | collective-permute-start | bytes 393224 | tf_op jit(solution)/shard_map/ppermute | solution.py:298
  43.2 5.0 %collective-permute-start.15 = (bf16[4,16,1024]{2,1,0:T(8,128)(2,1)S(1)}, bf16[4,16,1024]{2,1,0:T(8,128)(2,1)S(1)}, u32[]{:S(2)}, u32[]{:S(2)}) collective-permute-start(bf16[4,16,1024]{2,1,0:T(8,128)(2,1)S(1)} %fusion.2), channel_id=1, source_target_pairs={{0,8},{4,20},{8,0},{12,28},{16,24},{20,4},{24,16},{28,12},{1,9},{5... | collective-permute-start | bytes 393224 | tf_op jit(solution)/shard_map/ppermute | solution.py:298
  48.5 6.9 %collective-permute-start.16 = (bf16[16,2048]{1,0:T(8,128)(2,1)S(1)}, bf16[16,2048]{1,0:T(8,128)(2,1)S(1)}, u32[]{:S(2)}, u32[]{:S(2)}) collective-permute-start(bf16[16,2048]{1,0:T(8,128)(2,1)S(1)} %pad_maximum_fusion.2), channel_id=1, source_target_pairs={{0,3},{1,2},{2,1},{3,0},{4,7},{5,6},{6,5},{7,4},{8,11},{9,10},{10,... | collective-permute-start | bytes 196616 | tf_op jit(solution)/shard_map/ppermute | solution.py:301
  49.5 7.8 %collective-permute-start.17 = (bf16[16,2048]{1,0:T(8,128)(2,1)S(1)}, bf16[16,2048]{1,0:T(8,128)(2,1)S(1)}, u32[]{:S(2)}, u32[]{:S(2)}) collective-permute-start(bf16[16,2048]{1,0:T(8,128)(2,1)S(1)} %pad_maximum_fusion.3), channel_id=1, source_target_pairs={{0,2},{1,3},{2,0},{3,1},{4,6},{5,7},{6,4},{7,5},{8,10},{9,11},{10,... | collective-permute-start | bytes 196616 | tf_op jit(solution)/shard_map/ppermute | solution.py:301
  50.6 6.6 %collective-permute-start.18 = (bf16[16,2048]{1,0:T(8,128)(2,1)S(1)}, bf16[16,2048]{1,0:T(8,128)(2,1)S(1)}, u32[]{:S(2)}, u32[]{:S(2)}) collective-permute-start(bf16[16,2048]{1,0:T(8,128)(2,1)S(1)} %pad_maximum_fusion.4), channel_id=1, source_target_pairs={{0,1},{1,0},{2,3},{3,2},{4,5},{5,4},{6,7},{7,6},{8,9},{9,8},{10,11... | collective-permute-start | bytes 196616 | tf_op jit(solution)/shard_map/ppermute | solution.py:301

commit v20 on v17

--- a/solution.py
+++ b/solution.py
@@ -307,8 +307,10 @@
     for a in range(1, n_chip):
         step = a.bit_length() - 1
         source = near[a ^ (1 << step)]
-        if a > 1 and a == 1 << step:
-            source, mine = lax.optimization_barrier((jnp.concatenate(source, axis=1), mine))
+        if a == 1 << step:
+            source = jnp.concatenate(source, axis=1)
+            if a > 1:
+                source, mine = lax.optimization_barrier((source, mine))
             moved = swap_chip(source, step)
             near.append(jnp.split(moved, PARTS, axis=1))
         else:

time: 58.5 us -> 61.4 us (1.050)
  waiting for transfers between devices: 16.9 us -> 21.3 us
  starting transfers between devices: 18.7 us -> 17.2 us
    ppermute x10 -> x9, waiting for transfers between devices: 10.7 us -> 15.2 us  [swap_chip(): lax.ppermute(value, 'seq', [(i, i ^ flips[i & 1]) for i in range(n_seq)])]
    ppermute x10 -> x9, starting transfers between devices: 13.2 us -> 11.8 us  [swap_chip(): lax.ppermute(value, 'seq', [(i, i ^ flips[i & 1]) for i in range(n_seq)])]
  transfers between devices with their start and end apart: 19 -> 18, of which waited for: 14 -> 14; matrix products, arithmetic and copies ran while one was open for 1% -> 1% of each run, Pallas kernels for 3% -> 3%
where the time goes in v20:
time: 61.4 us; the launch traced here: 61.3 us
  waiting for transfers between devices  21.3 us (35%)
  starting transfers between devices  17.2 us (28%)
  blocking collectives  12.8 us (21%)
  Pallas kernels  7.39 us (12%)
  matrix products  1.11 us (2%)
  between operations  0.8 us (1%)
    ppermute x9, waiting for transfers between devices, swap_chip(): lax.ppermute(value, 'seq', [(i, i ^ flips[i & 1]) for i in range(n_seq)])  15.2 us
    all_to_all x1, blocking collectives, body(): stats = lax.all_to_all(stats, ('seq', 'vocab'), 0, 0, tiled=True)  12.8 us
    ppermute x9, starting transfers between devices, swap_chip(): lax.ppermute(value, 'seq', [(i, i ^ flips[i & 1]) for i in range(n_seq)])  11.8 us
    ppermute x3, starting transfers between devices, send_vocab(): return lax.ppermute(value, 'vocab', [(i, i ^ k) for i in range(n_vocab)])  4.45 us
    ppermute x3, waiting for transfers between devices, send_vocab(): return lax.ppermute(value, 'vocab', [(i, i ^ k) for i in range(n_vocab)])  3.42 us
    ppermute x6, waiting for transfers between devices, swap_core(): return lax.ppermute(value, 'seq', [(i, i ^ 1) for i in range(n_seq)])  2.76 us
    pallas_call x1, Pallas kernels, select(): pl.pallas_call(select_kernel, in_specs=[pl.BlockSpec(memory_space=pltpu.H...  2.75 us
    pallas_call x1, Pallas kernels, gradients(): pl.pallas_call(functools.partial(gradient_kernel, n_seq, n_vocab), in_spe...  1.64 us
  transfers between devices with their start and end apart: 18, of which 14 were waited for; matrix products, arithmetic and copies ran while one was open for 1% of the time, Pallas kernels for 3%

profile of v20, /device:TPU:0, one launch (start us, length us, event | category | flops | bytes accessed | tf_op | source)
XLA Modules:
  0.0 61.3 jit_solution(8198546221300738700)
XLA Ops:
  0.6 0.0 copy-start
  0.6 2.8 %select_rows.1 = (bf16[16,4096]{1,0:T(8,128)(2,1)S(1)}, bf16[16,4096]{1,0:T(8,128)(2,1)S(1)}, bf16[16,128]{1,0:T(8,128)(2,1)S(1)}) custom-call(s32[1,128]{1,0:T(1,128)} %bitcast.46, bf16[128,8192]{1,0:T(8,128)(2,1)} %hidden_ref.1), custom_call_target="tpu_custom_call" | custom-call | tf_op jit(solution)/shard_map/select_rows/pallas_call | solution.py:92
  3.4 3.0 %collective-permute-start = (bf16[16,8192]{1,0:T(8,128)(2,1)S(1)}, bf16[16,8192]{1,0:T(8,128)(2,1)S(1)}, u32[]{:S(2)}, u32[]{:S(2)}) collective-permute-start(bf16[16,8192]{1,0:T(8,128)(2,1)S(1)} %constant_dynamic-update-slice_fusion), channel_id=1, source_target_pairs={{0,8},{4,20},{8,0},{12,28},{16,24},{20,4},{24,16},{28,12},{1,9},{5... | collective-permute-start | bytes 786440 | tf_op jit(solution)/shard_map/ppermute | solution.py:298
  6.5 1.2 %own_logits.1.refs_0_ = f32[16,256]{1,0:T(8,128)S(1)} custom-call(bf16[16,4096]{1,0:T(8,128)(2,1)S(1)} %get-tuple-element.25.own_ref, bf16[8192,256]{1,0:T(8,128)(2,1)} %head_ref.3), custom_call_target="tpu_custom_call" | custom-call | tf_op jit(solution)/shard_map/own_logits/pallas_call | solution.py:127
  7.7 1.6 %collective-permute-start.1 = (bf16[16,8192]{1,0:T(8,128)(2,1)S(1)}, bf16[16,8192]{1,0:T(8,128)(2,1)S(1)}, u32[]{:S(2)}, u32[]{:S(2)}) collective-permute-start(bf16[16,8192]{1,0:T(8,128)(2,1)S(1)} %constant_dynamic-update-slice_fusion), channel_id=1, source_target_pairs={{0,16},{4,12},{8,24},{12,4},{16,0},{20,28},{24,8},{28,20},{1,17},{... | collective-permute-start | bytes 786440 | tf_op jit(solution)/shard_map/ppermute | solution.py:298
  9.3 2.4 %collective-permute-done = bf16[16,8192]{1,0:T(8,128)(2,1)S(1)} collective-permute-done((bf16[16,8192]{1,0:T(8,128)(2,1)S(1)}, bf16[16,8192]{1,0:T(8,128)(2,1)S(1)}, u32[]{:S(2)}, u32[]{:S(2)}) %collective-permute-start) | collective-permute-done | bytes 262176 | tf_op jit(solution)/shard_map/ppermute | solution.py:298
  11.7 2.4 %collective-permute-done.1 = bf16[16,8192]{1,0:T(8,128)(2,1)S(1)} collective-permute-done((bf16[16,8192]{1,0:T(8,128)(2,1)S(1)}, bf16[16,8192]{1,0:T(8,128)(2,1)S(1)}, u32[]{:S(2)}, u32[]{:S(2)}) %collective-permute-start.1) | collective-permute-done | bytes 262176 | tf_op jit(solution)/shard_map/ppermute | solution.py:298
  14.2 1.6 %collective-permute-start.2 = (bf16[16,4096]{1,0:T(8,128)(2,1)S(1)}, bf16[16,4096]{1,0:T(8,128)(2,1)S(1)}, u32[]{:S(2)}, u32[]{:S(2)}) collective-permute-start(bf16[16,4096]{1,0:T(8,128)(2,1)S(1)} %get-tuple-element.57), channel_id=1, source_target_pairs={{0,16},{4,12},{8,24},{12,4},{16,0},{20,28},{24,8},{28,20},{1,17},{... | collective-permute-start | bytes 393224 | tf_op jit(solution)/shard_map/ppermute | solution.py:298
  15.7 0.5 collective-permute-start.4
  16.3 2.9 %collective-permute-done.2 = bf16[16,4096]{1,0:T(8,128)(2,1)S(1)} collective-permute-done((bf16[16,4096]{1,0:T(8,128)(2,1)S(1)}, bf16[16,4096]{1,0:T(8,128)(2,1)S(1)}, u32[]{:S(2)}, u32[]{:S(2)}) %collective-permute-start.2) | collective-permute-done | bytes 131104 | tf_op jit(solution)/shard_map/ppermute | solution.py:298
  19.2 0.0 collective-permute-start.3
  19.2 1.5 %collective-permute-done.4 = bf16[16,4096]{1,0:T(8,128)(2,1)S(1)} collective-permute-done((bf16[16,4096]{1,0:T(8,128)(2,1)S(1)}, bf16[16,4096]{1,0:T(8,128)(2,1)S(1)}, u32[]{:S(2)}, u32[]{:S(2)}) %collective-permute-start.4) | collective-permute-done | bytes 131104 | tf_op jit(solution)/shard_map/ppermute | solution.py:298
  20.7 0.1 collective-permute-start.5
  20.8 1.5 %collective-permute-done.5.refs_4_ = bf16[32,4096]{1,0:T(8,128)(2,1)S(1)} collective-permute-done((bf16[32,4096]{1,0:T(8,128)(2,1)S(1)}, bf16[32,4096]{1,0:T(8,128)(2,1)S(1)}, u32[]{:S(2)}, u32[]{:S(2)}) %collective-permute-start.5) | collective-permute-done | bytes 262176 | tf_op jit(solution)/shard_map/ppermute | solution.py:294
  22.3 0.0 collective-permute-done.3.refs_2_
  22.3 0.0 copy-done
  22.3 1.0 %local_logits.1 = (f32[128,256]{1,0:T(8,128)S(1)}, f32[32,4,128]{2,1,0:T(4,128)S(1)}) custom-call(f32[16,256]{1,0:T(8,128)S(1)} %own_logits.1.refs_0_, bf16[96,4096]{1,0:T(8,128)(2,1)S(1)} %slice_dynamic-update-slice_fusion.refs_1_, bf16[96,4096]{1,0:T(8,128)(2,1)S(1)} %collective-permute-done.3.refs_2_, ...), custom_call_target="tpu_custom_call" | custom-call | tf_op jit(solution)/shard_map/local_logits/pallas_call | solution.py:183
  23.3 12.8 %all_to_all.5.stats_ref = f32[32,4,128]{2,1,0:T(4,128)S(1)} all-to-all(f32[32,4,128]{2,1,0:T(4,128)S(1)} %get-tuple-element.32), channel_id=1, replica_groups=mesh['seq'=8,'vocab'=4] {'seq','vocab'}, dimensions={0} | all-to-all | bytes 131072 | tf_op jit(solution)/shard_map/all_to_all | solution.py:324
  36.1 1.6 %gradients.1 = (bf16[4,4,16,1024]{3,2,1,0:T(8,128)(2,1)S(1)}, bf16[4,4,16,1024]{3,2,1,0:T(8,128)(2,1)S(1)}, bf16[3,4,16,1024]{3,2,1,0:T(8,128)(2,1)S(1)}, bf16[3...) custom-call(f32[32,4,128]{2,1,0:T(4,128)S(1)} %all_to_all.5.stats_ref, ...), custom_call_target="tpu_custom_call" | custom-call | tf_op jit(solution)/shard_map/gradients/pallas_call | solution.py:274
  37.8 0.1 collective-permute-start.6
  37.8 0.5 collective-permute-start.7
  38.3 0.8 %collective-permute-done.6 = bf16[4,16,1024]{2,1,0:T(8,128)(2,1)S(1)} collective-permute-done((bf16[4,16,1024]{2,1,0:T(8,128)(2,1)S(1)}, bf16[4,16,1024]{2,1,0:T(8,128)(2,1)S(1)}, u32[]{:S(2)}, u32[]{:S(2)}) %collective-permute-start.6) | collective-permute-done | bytes 131104 | tf_op jit(solution)/shard_map/ppermute | solution.py:294
  39.2 0.2 collective-permute-done.7
  39.4 0.3 collective-permute-start.8
  39.7 0.7 %collective-permute-start.11 = (bf16[4,16,1024]{2,1,0:T(8,128)(2,1)S(1)}, bf16[4,16,1024]{2,1,0:T(8,128)(2,1)S(1)}, u32[]{:S(2)}, u32[]{:S(2)}) collective-permute-start(bf16[4,16,1024]{2,1,0:T(8,128)(2,1)S(1)} %fusion.1), channel_id=1, source_target_pairs={{0,16},{4,12},{8,24},{12,4},{16,0},{20,28},{24,8},{28,20},{1,17},{... | collective-permute-start | bytes 393224 | tf_op jit(solution)/shard_map/ppermute | solution.py:298
  40.5 0.0 collective-permute-start.9
  40.5 1.4 %collective-permute-start.13 = (bf16[4,16,1024]{2,1,0:T(8,128)(2,1)S(1)}, bf16[4,16,1024]{2,1,0:T(8,128)(2,1)S(1)}, u32[]{:S(2)}, u32[]{:S(2)}) collective-permute-start(bf16[4,16,1024]{2,1,0:T(8,128)(2,1)S(1)} %fusion), channel_id=1, source_target_pairs={{0,16},{4,12},{8,24},{12,4},{16,0},{20,28},{24,8},{28,20},{1,17},{... | collective-permute-start | bytes 393224 | tf_op jit(solution)/shard_map/ppermute | solution.py:298
  41.9 0.0 collective-permute-done.8
  42.0 0.2 collective-permute-done.9
  42.3 1.4 %collective-permute-start.10 = (bf16[4,16,2048]{2,1,0:T(8,128)(2,1)S(1)}, bf16[4,16,2048]{2,1,0:T(8,128)(2,1)S(1)}, u32[]{:S(2)}, u32[]{:S(2)}) collective-permute-start(bf16[4,16,2048]{2,1,0:T(8,128)(2,1)S(1)} %pad_maximum_fusion), channel_id=1, source_target_pairs={{0,16},{4,12},{8,24},{12,4},{16,0},{20,28},{24,8},{28,20},{1,17},{... | collective-permute-start | bytes 786440 | tf_op jit(solution)/shard_map/ppermute | solution.py:298
  43.7 1.1 %collective-permute-done.11 = bf16[4,16,1024]{2,1,0:T(8,128)(2,1)S(1)} collective-permute-done((bf16[4,16,1024]{2,1,0:T(8,128)(2,1)S(1)}, bf16[4,16,1024]{2,1,0:T(8,128)(2,1)S(1)}, u32[]{:S(2)}, u32[]{:S(2)}) %collective-permute-start.11) | collective-permute-done | bytes 131104 | tf_op jit(solution)/shard_map/ppermute | solution.py:298
  44.8 0.1 fusion.4
  44.8 0.7 %collective-permute-start.12 = (bf16[4,16,1024]{2,1,0:T(8,128)(2,1)S(1)}, bf16[4,16,1024]{2,1,0:T(8,128)(2,1)S(1)}, u32[]{:S(2)}, u32[]{:S(2)}) collective-permute-start(bf16[4,16,1024]{2,1,0:T(8,128)(2,1)S(1)} %fusion.4), channel_id=1, source_target_pairs={{0,8},{4,20},{8,0},{12,28},{16,24},{20,4},{24,16},{28,12},{1,9},{5... | collective-permute-start | bytes 393224 | tf_op jit(solution)/shard_map/ppermute | solution.py:298
  45.5 0.6 %collective-permute-done.13 = bf16[4,16,1024]{2,1,0:T(8,128)(2,1)S(1)} collective-permute-done((bf16[4,16,1024]{2,1,0:T(8,128)(2,1)S(1)}, bf16[4,16,1024]{2,1,0:T(8,128)(2,1)S(1)}, u32[]{:S(2)}, u32[]{:S(2)}) %collective-permute-start.13) | collective-permute-done | bytes 131104 | tf_op jit(solution)/shard_map/ppermute | solution.py:298
  46.2 0.1 fusion.2
  46.2 0.8 %collective-permute-start.14 = (bf16[4,16,1024]{2,1,0:T(8,128)(2,1)S(1)}, bf16[4,16,1024]{2,1,0:T(8,128)(2,1)S(1)}, u32[]{:S(2)}, u32[]{:S(2)}) collective-permute-start(bf16[4,16,1024]{2,1,0:T(8,128)(2,1)S(1)} %fusion.2), channel_id=1, source_target_pairs={{0,8},{4,20},{8,0},{12,28},{16,24},{20,4},{24,16},{28,12},{1,9},{5... | collective-permute-start | bytes 393224 | tf_op jit(solution)/shard_map/ppermute | solution.py:298
  47.0 2.8 %collective-permute-done.12 = bf16[4,16,1024]{2,1,0:T(8,128)(2,1)S(1)} collective-permute-done((bf16[4,16,1024]{2,1,0:T(8,128)(2,1)S(1)}, bf16[4,16,1024]{2,1,0:T(8,128)(2,1)S(1)}, u32[]{:S(2)}, u32[]{:S(2)}) %collective-permute-start.12) | collective-permute-done | bytes 131104 | tf_op jit(solution)/shard_map/ppermute | solution.py:298
  49.9 1.4 %collective-permute-done.14 = bf16[4,16,1024]{2,1,0:T(8,128)(2,1)S(1)} collective-permute-done((bf16[4,16,1024]{2,1,0:T(8,128)(2,1)S(1)}, bf16[4,16,1024]{2,1,0:T(8,128)(2,1)S(1)}, u32[]{:S(2)}, u32[]{:S(2)}) %collective-permute-start.14) | collective-permute-done | bytes 131104 | tf_op jit(solution)/shard_map/ppermute | solution.py:298
  51.3 0.0 collective-permute-done.10
  51.3 0.2 fusion.3
  51.5 0.9 %collective-permute-start.15 = (bf16[16,2048]{1,0:T(8,128)(2,1)S(1)}, bf16[16,2048]{1,0:T(8,128)(2,1)S(1)}, u32[]{:S(2)}, u32[]{:S(2)}) collective-permute-start(bf16[16,2048]{1,0:T(8,128)(2,1)S(1)} %pad_maximum_fusion.1), channel_id=1, source_target_pairs={{0,3},{1,2},{2,1},{3,0},{4,7},{5,6},{6,5},{7,4},{8,11},{9,10},{10,... | collective-permute-start | bytes 196616 | tf_op jit(solution)/shard_map/ppermute | solution.py:301
  52.4 0.9 %collective-permute-start.16 = (bf16[16,2048]{1,0:T(8,128)(2,1)S(1)}, bf16[16,2048]{1,0:T(8,128)(2,1)S(1)}, u32[]{:S(2)}, u32[]{:S(2)}) collective-permute-start(bf16[16,2048]{1,0:T(8,128)(2,1)S(1)} %pad_maximum_fusion.2), channel_id=1, source_target_pairs={{0,2},{1,3},{2,0},{3,1},{4,6},{5,7},{6,4},{7,5},{8,10},{9,11},{10,... | collective-permute-start | bytes 196616 | tf_op jit(solution)/shard_map/ppermute | solution.py:301
  53.3 2.7 %collective-permute-start.17 = (bf16[16,2048]{1,0:T(8,128)(2,1)S(1)}, bf16[16,2048]{1,0:T(8,128)(2,1)S(1)}, u32[]{:S(2)}, u32[]{:S(2)}) collective-permute-start(bf16[16,2048]{1,0:T(8,128)(2,1)S(1)} %pad_maximum_fusion.3), channel_id=1, source_target_pairs={{0,1},{1,0},{2,3},{3,2},{4,5},{5,4},{6,7},{7,6},{8,9},{9,8},{10,11... | collective-permute-start | bytes 196616 | tf_op jit(solution)/shard_map/ppermute | solution.py:301
  55.9 0.8 %entropies.1 = (f32[1,128]{1,0:T(1,128)}, f32[1,1]{1,0:T(1,128)}) custom-call(f32[32,4,128]{2,1,0:T(4,128)S(1)} %all_to_all.5.stats_ref, bf16[16,128]{1,0:T(8,128)(2,1)S(1)} %get-tuple-element.31.refs_6_.picker_ref), custom_call_target="tpu_custom_call" | custom-call | tf_op jit(solution)/shard_map/entropies/pallas_call | solution.py:223
  56.7 1.6 %collective-permute-done.15 = bf16[16,2048]{1,0:T(8,128)(2,1)S(1)} collective-permute-done((bf16[16,2048]{1,0:T(8,128)(2,1)S(1)}, bf16[16,2048]{1,0:T(8,128)(2,1)S(1)}, u32[]{:S(2)}, u32[]{:S(2)}) %collective-permute-start.15) | collective-permute-done | bytes 65568 | tf_op jit(solution)/shard_map/ppermute | solution.py:301
  58.4 1.8 %collective-permute-done.16 = bf16[16,2048]{1,0:T(8,128)(2,1)S(1)} collective-permute-done((bf16[16,2048]{1,0:T(8,128)(2,1)S(1)}, bf16[16,2048]{1,0:T(8,128)(2,1)S(1)}, u32[]{:S(2)}, u32[]{:S(2)}) %collective-permute-start.16) | collective-permute-done | bytes 65568 | tf_op jit(solution)/shard_map/ppermute | solution.py:301
  60.1 0.0 collective-permute-done.17
  60.1 1.1 %convolution_convert_fusion = bf16[128,2048]{1,0:T(8,128)(2,1)} fusion(bf16[16,128]{1,0:T(8,128)(2,1)S(1)} %get-tuple-element.31.refs_6_.picker_ref, f32[16,1024]{1,0:T(8,128)S(1)} %get-tuple-element.60, f32[16,1024]{1,0:T(8,128)S(1)} %get-tuple-element.61, bf16[16,2048]{1,0:T(8,128)(2,1)S(1)} %collective-permute-done.17, ...), kind=kOutput, calls=%fused_computation | convolution fusion | flops 8912896 | bytes 856064 | tf_op jit(solution)/shard_map/dot_general | solution.py:359
  (19 shorter events, 0.3 us)
Async XLA Ops:
  0.6 21.7 %copy-start = (bf16[8192,256]{1,0:T(8,128)(2,1)S(1)}, bf16[8192,256]{1,0:T(8,128)(2,1)}, u32[]{:S(2)}) copy-start(bf16[8192,256]{1,0:T(8,128)(2,1)} %head_ref.3) | copy-start | bytes 12582916
  3.4 8.2 %collective-permute-start = (bf16[16,8192]{1,0:T(8,128)(2,1)S(1)}, bf16[16,8192]{1,0:T(8,128)(2,1)S(1)}, u32[]{:S(2)}, u32[]{:S(2)}) collective-permute-start(bf16[16,8192]{1,0:T(8,128)(2,1)S(1)} %constant_dynamic-update-slice_fusion), channel_id=1, source_target_pairs={{0,8},{4,20},{8,0},{12,28},{16,24},{20,4},{24,16},{28,12},{1,9},{5... | collective-permute-start | bytes 786440 | tf_op jit(solution)/shard_map/ppermute | solution.py:298
  7.7 6.4 %collective-permute-start.1 = (bf16[16,8192]{1,0:T(8,128)(2,1)S(1)}, bf16[16,8192]{1,0:T(8,128)(2,1)S(1)}, u32[]{:S(2)}, u32[]{:S(2)}) collective-permute-start(bf16[16,8192]{1,0:T(8,128)(2,1)S(1)} %constant_dynamic-update-slice_fusion), channel_id=1, source_target_pairs={{0,16},{4,12},{8,24},{12,4},{16,0},{20,28},{24,8},{28,20},{1,17},{... | collective-permute-start | bytes 786440 | tf_op jit(solution)/shard_map/ppermute | solution.py:298
  14.2 5.0 %collective-permute-start.2 = (bf16[16,4096]{1,0:T(8,128)(2,1)S(1)}, bf16[16,4096]{1,0:T(8,128)(2,1)S(1)}, u32[]{:S(2)}, u32[]{:S(2)}) collective-permute-start(bf16[16,4096]{1,0:T(8,128)(2,1)S(1)} %get-tuple-element.57), channel_id=1, source_target_pairs={{0,16},{4,12},{8,24},{12,4},{16,0},{20,28},{24,8},{28,20},{1,17},{... | collective-permute-start | bytes 393224 | tf_op jit(solution)/shard_map/ppermute | solution.py:298
  15.7 5.0 %collective-permute-start.4 = (bf16[16,4096]{1,0:T(8,128)(2,1)S(1)}, bf16[16,4096]{1,0:T(8,128)(2,1)S(1)}, u32[]{:S(2)}, u32[]{:S(2)}) collective-permute-start(bf16[16,4096]{1,0:T(8,128)(2,1)S(1)} %get-tuple-element.55), channel_id=1, source_target_pairs={{0,16},{4,12},{8,24},{12,4},{16,0},{20,28},{24,8},{28,20},{1,17},{... | collective-permute-start | bytes 393224 | tf_op jit(solution)/shard_map/ppermute | solution.py:298
  19.2 3.1 %collective-permute-start.3 = (bf16[96,4096]{1,0:T(8,128)(2,1)S(1)}, bf16[96,4096]{1,0:T(8,128)(2,1)S(1)}, u32[]{:S(2)}, u32[]{:S(2)}) collective-permute-start(bf16[96,4096]{1,0:T(8,128)(2,1)S(1)} %slice_dynamic-update-slice_fusion.refs_1_), channel_id=1, source_target_pairs={{0,4},{4,0},{8,12},{12,8},{16,20},{20,16},{24,28},{28,24},{1,5},{5... | collective-permute-start | bytes 2359304 | tf_op jit(solution)/shard_map/ppermute | solution.py:294
  20.7 1.6 %collective-permute-start.5 = (bf16[32,4096]{1,0:T(8,128)(2,1)S(1)}, bf16[32,4096]{1,0:T(8,128)(2,1)S(1)}, u32[]{:S(2)}, u32[]{:S(2)}) collective-permute-start(bf16[32,4096]{1,0:T(8,128)(2,1)S(1)} %constant_dynamic-update-slice_fusion.6.refs_3_), channel_id=1, source_target_pairs={{0,4},{4,0},{8,12},{12,8},{16,20},{20,16},{24,28},{28,24},{1,5},{5... | collective-permute-start | bytes 786440 | tf_op jit(solution)/shard_map/ppermute | solution.py:294
  37.8 1.4 %collective-permute-start.6 = (bf16[4,16,1024]{2,1,0:T(8,128)(2,1)S(1)}, bf16[4,16,1024]{2,1,0:T(8,128)(2,1)S(1)}, u32[]{:S(2)}, u32[]{:S(2)}) collective-permute-start(bf16[4,16,1024]{2,1,0:T(8,128)(2,1)S(1)} %get-tuple-element.37), channel_id=1, source_target_pairs={{0,4},{4,0},{8,12},{12,8},{16,20},{20,16},{24,28},{28,24},{1,5},{5... | collective-permute-start | bytes 393224 | tf_op jit(solution)/shard_map/ppermute | solution.py:294
  37.8 1.5 %collective-permute-start.7 = (bf16[4,16,1024]{2,1,0:T(8,128)(2,1)S(1)}, bf16[4,16,1024]{2,1,0:T(8,128)(2,1)S(1)}, u32[]{:S(2)}, u32[]{:S(2)}) collective-permute-start(bf16[4,16,1024]{2,1,0:T(8,128)(2,1)S(1)} %get-tuple-element.38), channel_id=1, source_target_pairs={{0,4},{4,0},{8,12},{12,8},{16,20},{20,16},{24,28},{28,24},{1,5},{5... | collective-permute-start | bytes 393224 | tf_op jit(solution)/shard_map/ppermute | solution.py:294
  39.4 2.6 %collective-permute-start.8 = (bf16[3,4,16,1024]{3,2,1,0:T(8,128)(2,1)S(1)}, bf16[3,4,16,1024]{3,2,1,0:T(8,128)(2,1)S(1)}, u32[]{:S(2)}, u32[]{:S(2)}) collective-permute-start(bf16[3,4,16,1024]{3,2,1,0:T(8,128)(2,1)S(1)} %get-tuple-element.39), channel_id=1, source_target_pairs={{0,4},{4,0},{8,12},{12,8},{16,20},{20,16},{24,28},{28,24},{1,5},{5... | collective-permute-start | bytes 1179656 | tf_op jit(solution)/shard_map/ppermute | solution.py:294
  39.7 5.0 %collective-permute-start.11 = (bf16[4,16,1024]{2,1,0:T(8,128)(2,1)S(1)}, bf16[4,16,1024]{2,1,0:T(8,128)(2,1)S(1)}, u32[]{:S(2)}, u32[]{:S(2)}) collective-permute-start(bf16[4,16,1024]{2,1,0:T(8,128)(2,1)S(1)} %fusion.1), channel_id=1, source_target_pairs={{0,16},{4,12},{8,24},{12,4},{16,0},{20,28},{24,8},{28,20},{1,17},{... | collective-permute-start | bytes 393224 | tf_op jit(solution)/shard_map/ppermute | solution.py:298
  40.5 1.7 %collective-permute-start.9 = (bf16[3,4,16,1024]{3,2,1,0:T(8,128)(2,1)S(1)}, bf16[3,4,16,1024]{3,2,1,0:T(8,128)(2,1)S(1)}, u32[]{:S(2)}, u32[]{:S(2)}) collective-permute-start(bf16[3,4,16,1024]{3,2,1,0:T(8,128)(2,1)S(1)} %get-tuple-element.41), channel_id=1, source_target_pairs={{0,4},{4,0},{8,12},{12,8},{16,20},{20,16},{24,28},{28,24},{1,5},{5... | collective-permute-start | bytes 1179656 | tf_op jit(solution)/shard_map/ppermute | solution.py:294
  40.5 5.7 %collective-permute-start.13 = (bf16[4,16,1024]{2,1,0:T(8,128)(2,1)S(1)}, bf16[4,16,1024]{2,1,0:T(8,128)(2,1)S(1)}, u32[]{:S(2)}, u32[]{:S(2)}) collective-permute-start(bf16[4,16,1024]{2,1,0:T(8,128)(2,1)S(1)} %fusion), channel_id=1, source_target_pairs={{0,16},{4,12},{8,24},{12,4},{16,0},{20,28},{24,8},{28,20},{1,17},{... | collective-permute-start | bytes 393224 | tf_op jit(solution)/shard_map/ppermute | solution.py:298
  42.3 9.0 %collective-permute-start.10 = (bf16[4,16,2048]{2,1,0:T(8,128)(2,1)S(1)}, bf16[4,16,2048]{2,1,0:T(8,128)(2,1)S(1)}, u32[]{:S(2)}, u32[]{:S(2)}) collective-permute-start(bf16[4,16,2048]{2,1,0:T(8,128)(2,1)S(1)} %pad_maximum_fusion), channel_id=1, source_target_pairs={{0,16},{4,12},{8,24},{12,4},{16,0},{20,28},{24,8},{28,20},{1,17},{... | collective-permute-start | bytes 786440 | tf_op jit(solution)/shard_map/ppermute | solution.py:298
  44.8 5.0 %collective-permute-start.12 = (bf16[4,16,1024]{2,1,0:T(8,128)(2,1)S(1)}, bf16[4,16,1024]{2,1,0:T(8,128)(2,1)S(1)}, u32[]{:S(2)}, u32[]{:S(2)}) collective-permute-start(bf16[4,16,1024]{2,1,0:T(8,128)(2,1)S(1)} %fusion.4), channel_id=1, source_target_pairs={{0,8},{4,20},{8,0},{12,28},{16,24},{20,4},{24,16},{28,12},{1,9},{5... | collective-permute-start | bytes 393224 | tf_op jit(solution)/shard_map/ppermute | solution.py:298
  46.2 5.0 %collective-permute-start.14 = (bf16[4,16,1024]{2,1,0:T(8,128)(2,1)S(1)}, bf16[4,16,1024]{2,1,0:T(8,128)(2,1)S(1)}, u32[]{:S(2)}, u32[]{:S(2)}) collective-permute-start(bf16[4,16,1024]{2,1,0:T(8,128)(2,1)S(1)} %fusion.2), channel_id=1, source_target_pairs={{0,8},{4,20},{8,0},{12,28},{16,24},{20,4},{24,16},{28,12},{1,9},{5... | collective-permute-start | bytes 393224 | tf_op jit(solution)/shard_map/ppermute | solution.py:298
  51.5 6.9 %collective-permute-start.15 = (bf16[16,2048]{1,0:T(8,128)(2,1)S(1)}, bf16[16,2048]{1,0:T(8,128)(2,1)S(1)}, u32[]{:S(2)}, u32[]{:S(2)}) collective-permute-start(bf16[16,2048]{1,0:T(8,128)(2,1)S(1)} %pad_maximum_fusion.1), channel_id=1, source_target_pairs={{0,3},{1,2},{2,1},{3,0},{4,7},{5,6},{6,5},{7,4},{8,11},{9,10},{10,... | collective-permute-start | bytes 196616 | tf_op jit(solution)/shard_map/ppermute | solution.py:301
  52.4 7.8 %collective-permute-start.16 = (bf16[16,2048]{1,0:T(8,128)(2,1)S(1)}, bf16[16,2048]{1,0:T(8,128)(2,1)S(1)}, u32[]{:S(2)}, u32[]{:S(2)}) collective-permute-start(bf16[16,2048]{1,0:T(8,128)(2,1)S(1)} %pad_maximum_fusion.2), channel_id=1, source_target_pairs={{0,2},{1,3},{2,0},{3,1},{4,6},{5,7},{6,4},{7,5},{8,10},{9,11},{10,... | collective-permute-start | bytes 196616 | tf_op jit(solution)/shard_map/ppermute | solution.py:301
  53.3 6.9 %collective-permute-start.17 = (bf16[16,2048]{1,0:T(8,128)(2,1)S(1)}, bf16[16,2048]{1,0:T(8,128)(2,1)S(1)}, u32[]{:S(2)}, u32[]{:S(2)}) collective-permute-start(bf16[16,2048]{1,0:T(8,128)(2,1)S(1)} %pad_maximum_fusion.3), channel_id=1, source_target_pairs={{0,1},{1,0},{2,3},{3,2},{4,5},{5,4},{6,7},{7,6},{8,9},{9,8},{10,11... | collective-permute-start | bytes 196616 | tf_op jit(solution)/shard_map/ppermute | solution.py:301

commit v21 on v17

--- a/solution.py
+++ b/solution.py
@@ -12,7 +12,7 @@
 LANES = 128
 CHUNKS = 8
 OWN_CHUNKS = 1
-FLIGHT = 3
+FLIGHT = 4
 VMEM_BYTES = 24 * 2**20
 F32, BF16 = jnp.float32, jnp.bfloat16
 

time: 58.5 us -> 58 us (level)
  no operation moved by 1% of the time
where the time goes in v21:
time: 58 us; the launch traced here: 57.8 us
  starting transfers between devices  18.7 us (32%)
  waiting for transfers between devices  16.9 us (29%)
  blocking collectives  12.9 us (22%)
  Pallas kernels  6.82 us (12%)
  matrix products  1.11 us (2%)
  between operations  0.8 us (1%)
    ppermute x10, starting transfers between devices, swap_chip(): lax.ppermute(value, 'seq', [(i, i ^ flips[i & 1]) for i in range(n_seq)])  13.2 us
    all_to_all x1, blocking collectives, body(): stats = lax.all_to_all(stats, ('seq', 'vocab'), 0, 0, tiled=True)  12.9 us
    ppermute x10, waiting for transfers between devices, swap_chip(): lax.ppermute(value, 'seq', [(i, i ^ flips[i & 1]) for i in range(n_seq)])  10.7 us
    ppermute x3, starting transfers between devices, send_vocab(): return lax.ppermute(value, 'vocab', [(i, i ^ k) for i in range(n_vocab)])  4.45 us
    ppermute x3, waiting for transfers between devices, send_vocab(): return lax.ppermute(value, 'vocab', [(i, i ^ k) for i in range(n_vocab)])  3.43 us
    ppermute x6, waiting for transfers between devices, swap_core(): return lax.ppermute(value, 'seq', [(i, i ^ 1) for i in range(n_seq)])  2.76 us
    pallas_call x1, Pallas kernels, select(): pl.pallas_call(select_kernel, in_specs=[pl.BlockSpec(memory_space=pltpu.H...  2.21 us
    pallas_call x1, Pallas kernels, gradients(): pl.pallas_call(functools.partial(gradient_kernel, n_seq, n_vocab), in_spe...  1.64 us
  transfers between devices with their start and end apart: 19, of which 14 were waited for; matrix products, arithmetic and copies ran while one was open for 1% of the time, Pallas kernels for 3%

profile of v21, /device:TPU:0, one launch (start us, length us, event | category | flops | bytes accessed | tf_op | source)
XLA Modules:
  0.0 57.8 jit_solution(1544019258090447628)
XLA Ops:
  0.6 0.0 copy-start
  0.6 2.2 %select_rows.1 = (bf16[16,4096]{1,0:T(8,128)(2,1)S(1)}, bf16[16,4096]{1,0:T(8,128)(2,1)S(1)}, bf16[16,128]{1,0:T(8,128)(2,1)S(1)}) custom-call(s32[1,128]{1,0:T(1,128)} %bitcast.46, bf16[128,8192]{1,0:T(8,128)(2,1)} %hidden_ref.1), custom_call_target="tpu_custom_call" | custom-call | tf_op jit(solution)/shard_map/select_rows/pallas_call | solution.py:92
  2.9 3.0 %collective-permute-start = (bf16[16,4096]{1,0:T(8,128)(2,1)S(1)}, bf16[16,4096]{1,0:T(8,128)(2,1)S(1)}, u32[]{:S(2)}, u32[]{:S(2)}) collective-permute-start(bf16[16,4096]{1,0:T(8,128)(2,1)S(1)} %get-tuple-element.25.own_ref), channel_id=1, source_target_pairs={{0,8},{4,20},{8,0},{12,28},{16,24},{20,4},{24,16},{28,12},{1,9},{5... | collective-permute-start | bytes 393224 | tf_op jit(solution)/shard_map/ppermute | solution.py:298
  5.9 0.1 collective-permute-start.2
  6.0 1.2 %own_logits.1.refs_0_ = f32[16,256]{1,0:T(8,128)S(1)} custom-call(bf16[16,4096]{1,0:T(8,128)(2,1)S(1)} %get-tuple-element.25.own_ref, bf16[8192,256]{1,0:T(8,128)(2,1)} %head_ref.3), custom_call_target="tpu_custom_call" | custom-call | tf_op jit(solution)/shard_map/own_logits/pallas_call | solution.py:127
  7.2 2.0 %collective-permute-start.1 = (bf16[16,8192]{1,0:T(8,128)(2,1)S(1)}, bf16[16,8192]{1,0:T(8,128)(2,1)S(1)}, u32[]{:S(2)}, u32[]{:S(2)}) collective-permute-start(bf16[16,8192]{1,0:T(8,128)(2,1)S(1)} %pad_maximum_fusion), channel_id=1, source_target_pairs={{0,16},{4,12},{8,24},{12,4},{16,0},{20,28},{24,8},{28,20},{1,17},{... | collective-permute-start | bytes 786440 | tf_op jit(solution)/shard_map/ppermute | solution.py:298
  9.3 0.0 collective-permute-done
  9.3 1.6 %collective-permute-start.3 = (bf16[16,4096]{1,0:T(8,128)(2,1)S(1)}, bf16[16,4096]{1,0:T(8,128)(2,1)S(1)}, u32[]{:S(2)}, u32[]{:S(2)}) collective-permute-start(bf16[16,4096]{1,0:T(8,128)(2,1)S(1)} %collective-permute-done), channel_id=1, source_target_pairs={{0,16},{4,12},{8,24},{12,4},{16,0},{20,28},{24,8},{28,20},{1,17},{... | collective-permute-start | bytes 393224 | tf_op jit(solution)/shard_map/ppermute | solution.py:298
  10.9 1.3 %collective-permute-done.2 = bf16[16,4096]{1,0:T(8,128)(2,1)S(1)} collective-permute-done((bf16[16,4096]{1,0:T(8,128)(2,1)S(1)}, bf16[16,4096]{1,0:T(8,128)(2,1)S(1)}, u32[]{:S(2)}, u32[]{:S(2)}) %collective-permute-start.2) | collective-permute-done | bytes 131104 | tf_op jit(solution)/shard_map/ppermute | solution.py:298
  12.2 1.4 %collective-permute-start.5 = (bf16[16,4096]{1,0:T(8,128)(2,1)S(1)}, bf16[16,4096]{1,0:T(8,128)(2,1)S(1)}, u32[]{:S(2)}, u32[]{:S(2)}) collective-permute-start(bf16[16,4096]{1,0:T(8,128)(2,1)S(1)} %collective-permute-done.2), channel_id=1, source_target_pairs={{0,16},{4,12},{8,24},{12,4},{16,0},{20,28},{24,8},{28,20},{1,17},{... | collective-permute-start | bytes 393224 | tf_op jit(solution)/shard_map/ppermute | solution.py:298
  13.6 0.1 collective-permute-done.1
  13.7 1.3 %collective-permute-done.3 = bf16[16,4096]{1,0:T(8,128)(2,1)S(1)} collective-permute-done((bf16[16,4096]{1,0:T(8,128)(2,1)S(1)}, bf16[16,4096]{1,0:T(8,128)(2,1)S(1)}, u32[]{:S(2)}, u32[]{:S(2)}) %collective-permute-start.3) | collective-permute-done | bytes 131104 | tf_op jit(solution)/shard_map/ppermute | solution.py:298
  15.1 0.1 collective-permute-start.4
  15.2 2.0 %collective-permute-done.5 = bf16[16,4096]{1,0:T(8,128)(2,1)S(1)} collective-permute-done((bf16[16,4096]{1,0:T(8,128)(2,1)S(1)}, bf16[16,4096]{1,0:T(8,128)(2,1)S(1)}, u32[]{:S(2)}, u32[]{:S(2)}) %collective-permute-start.5) | collective-permute-done | bytes 131104 | tf_op jit(solution)/shard_map/ppermute | solution.py:298
  17.2 0.1 collective-permute-start.6
  17.3 1.5 %collective-permute-done.6.refs_4_ = bf16[32,4096]{1,0:T(8,128)(2,1)S(1)} collective-permute-done((bf16[32,4096]{1,0:T(8,128)(2,1)S(1)}, bf16[32,4096]{1,0:T(8,128)(2,1)S(1)}, u32[]{:S(2)}, u32[]{:S(2)}) %collective-permute-start.6) | collective-permute-done | bytes 262176 | tf_op jit(solution)/shard_map/ppermute | solution.py:294
  18.8 0.0 collective-permute-done.4.refs_2_
  18.8 1.0 %local_logits.1 = (f32[128,256]{1,0:T(8,128)S(1)}, f32[32,4,128]{2,1,0:T(4,128)S(1)}) custom-call(f32[16,256]{1,0:T(8,128)S(1)} %own_logits.1.refs_0_, bf16[96,4096]{1,0:T(8,128)(2,1)S(1)} %slice_dynamic-update-slice_fusion.refs_1_, bf16[96,4096]{1,0:T(8,128)(2,1)S(1)} %collective-permute-done.4.refs_2_, ...), custom_call_target="tpu_custom_call" | custom-call | tf_op jit(solution)/shard_map/local_logits/pallas_call | solution.py:183
  19.8 12.9 %all_to_all.5.stats_ref = f32[32,4,128]{2,1,0:T(4,128)S(1)} all-to-all(f32[32,4,128]{2,1,0:T(4,128)S(1)} %get-tuple-element.32), channel_id=1, replica_groups=mesh['seq'=8,'vocab'=4] {'seq','vocab'}, dimensions={0} | all-to-all | bytes 131072 | tf_op jit(solution)/shard_map/all_to_all | solution.py:322
  32.7 1.6 %gradients.1 = (bf16[4,4,16,1024]{3,2,1,0:T(8,128)(2,1)S(1)}, bf16[4,4,16,1024]{3,2,1,0:T(8,128)(2,1)S(1)}, bf16[3,4,16,1024]{3,2,1,0:T(8,128)(2,1)S(1)}, bf16[3...) custom-call(f32[32,4,128]{2,1,0:T(4,128)S(1)} %all_to_all.5.stats_ref, ...), custom_call_target="tpu_custom_call" | custom-call | tf_op jit(solution)/shard_map/gradients/pallas_call | solution.py:274
  34.3 0.1 collective-permute-start.7
  34.4 0.5 collective-permute-start.8
  34.9 0.8 %collective-permute-done.7 = bf16[4,16,1024]{2,1,0:T(8,128)(2,1)S(1)} collective-permute-done((bf16[4,16,1024]{2,1,0:T(8,128)(2,1)S(1)}, bf16[4,16,1024]{2,1,0:T(8,128)(2,1)S(1)}, u32[]{:S(2)}, u32[]{:S(2)}) %collective-permute-start.7) | collective-permute-done | bytes 131104 | tf_op jit(solution)/shard_map/ppermute | solution.py:294
  35.7 0.2 collective-permute-done.8
  35.9 0.3 collective-permute-start.9
  36.3 0.7 %collective-permute-start.12 = (bf16[4,16,1024]{2,1,0:T(8,128)(2,1)S(1)}, bf16[4,16,1024]{2,1,0:T(8,128)(2,1)S(1)}, u32[]{:S(2)}, u32[]{:S(2)}) collective-permute-start(bf16[4,16,1024]{2,1,0:T(8,128)(2,1)S(1)} %fusion.1), channel_id=1, source_target_pairs={{0,16},{4,12},{8,24},{12,4},{16,0},{20,28},{24,8},{28,20},{1,17},{... | collective-permute-start | bytes 393224 | tf_op jit(solution)/shard_map/ppermute | solution.py:298
  37.0 0.0 collective-permute-start.10
  37.0 1.4 %collective-permute-start.14 = (bf16[4,16,1024]{2,1,0:T(8,128)(2,1)S(1)}, bf16[4,16,1024]{2,1,0:T(8,128)(2,1)S(1)}, u32[]{:S(2)}, u32[]{:S(2)}) collective-permute-start(bf16[4,16,1024]{2,1,0:T(8,128)(2,1)S(1)} %fusion), channel_id=1, source_target_pairs={{0,16},{4,12},{8,24},{12,4},{16,0},{20,28},{24,8},{28,20},{1,17},{... | collective-permute-start | bytes 393224 | tf_op jit(solution)/shard_map/ppermute | solution.py:298
  38.5 0.0 collective-permute-done.9
  38.5 0.2 collective-permute-done.10
  38.8 1.4 %collective-permute-start.11 = (bf16[4,16,2048]{2,1,0:T(8,128)(2,1)S(1)}, bf16[4,16,2048]{2,1,0:T(8,128)(2,1)S(1)}, u32[]{:S(2)}, u32[]{:S(2)}) collective-permute-start(bf16[4,16,2048]{2,1,0:T(8,128)(2,1)S(1)} %pad_maximum_fusion.1), channel_id=1, source_target_pairs={{0,16},{4,12},{8,24},{12,4},{16,0},{20,28},{24,8},{28,20},{1,17},{... | collective-permute-start | bytes 786440 | tf_op jit(solution)/shard_map/ppermute | solution.py:298
  40.2 1.1 %collective-permute-done.12 = bf16[4,16,1024]{2,1,0:T(8,128)(2,1)S(1)} collective-permute-done((bf16[4,16,1024]{2,1,0:T(8,128)(2,1)S(1)}, bf16[4,16,1024]{2,1,0:T(8,128)(2,1)S(1)}, u32[]{:S(2)}, u32[]{:S(2)}) %collective-permute-start.12) | collective-permute-done | bytes 131104 | tf_op jit(solution)/shard_map/ppermute | solution.py:298
  41.3 0.1 fusion.4
  41.4 0.7 %collective-permute-start.13 = (bf16[4,16,1024]{2,1,0:T(8,128)(2,1)S(1)}, bf16[4,16,1024]{2,1,0:T(8,128)(2,1)S(1)}, u32[]{:S(2)}, u32[]{:S(2)}) collective-permute-start(bf16[4,16,1024]{2,1,0:T(8,128)(2,1)S(1)} %fusion.4), channel_id=1, source_target_pairs={{0,8},{4,20},{8,0},{12,28},{16,24},{20,4},{24,16},{28,12},{1,9},{5... | collective-permute-start | bytes 393224 | tf_op jit(solution)/shard_map/ppermute | solution.py:298
  42.1 0.6 %collective-permute-done.14 = bf16[4,16,1024]{2,1,0:T(8,128)(2,1)S(1)} collective-permute-done((bf16[4,16,1024]{2,1,0:T(8,128)(2,1)S(1)}, bf16[4,16,1024]{2,1,0:T(8,128)(2,1)S(1)}, u32[]{:S(2)}, u32[]{:S(2)}) %collective-permute-start.14) | collective-permute-done | bytes 131104 | tf_op jit(solution)/shard_map/ppermute | solution.py:298
  42.7 0.1 fusion.2
  42.8 0.8 %collective-permute-start.15 = (bf16[4,16,1024]{2,1,0:T(8,128)(2,1)S(1)}, bf16[4,16,1024]{2,1,0:T(8,128)(2,1)S(1)}, u32[]{:S(2)}, u32[]{:S(2)}) collective-permute-start(bf16[4,16,1024]{2,1,0:T(8,128)(2,1)S(1)} %fusion.2), channel_id=1, source_target_pairs={{0,8},{4,20},{8,0},{12,28},{16,24},{20,4},{24,16},{28,12},{1,9},{5... | collective-permute-start | bytes 393224 | tf_op jit(solution)/shard_map/ppermute | solution.py:298
  43.6 2.8 %collective-permute-done.13 = bf16[4,16,1024]{2,1,0:T(8,128)(2,1)S(1)} collective-permute-done((bf16[4,16,1024]{2,1,0:T(8,128)(2,1)S(1)}, bf16[4,16,1024]{2,1,0:T(8,128)(2,1)S(1)}, u32[]{:S(2)}, u32[]{:S(2)}) %collective-permute-start.13) | collective-permute-done | bytes 131104 | tf_op jit(solution)/shard_map/ppermute | solution.py:298
  46.4 1.4 %collective-permute-done.15 = bf16[4,16,1024]{2,1,0:T(8,128)(2,1)S(1)} collective-permute-done((bf16[4,16,1024]{2,1,0:T(8,128)(2,1)S(1)}, bf16[4,16,1024]{2,1,0:T(8,128)(2,1)S(1)}, u32[]{:S(2)}, u32[]{:S(2)}) %collective-permute-start.15) | collective-permute-done | bytes 131104 | tf_op jit(solution)/shard_map/ppermute | solution.py:298
  47.8 0.0 collective-permute-done.11
  47.8 0.2 fusion.3
  48.0 0.9 %collective-permute-start.16 = (bf16[16,2048]{1,0:T(8,128)(2,1)S(1)}, bf16[16,2048]{1,0:T(8,128)(2,1)S(1)}, u32[]{:S(2)}, u32[]{:S(2)}) collective-permute-start(bf16[16,2048]{1,0:T(8,128)(2,1)S(1)} %pad_maximum_fusion.2), channel_id=1, source_target_pairs={{0,3},{1,2},{2,1},{3,0},{4,7},{5,6},{6,5},{7,4},{8,11},{9,10},{10,... | collective-permute-start | bytes 196616 | tf_op jit(solution)/shard_map/ppermute | solution.py:301
  48.9 0.9 %collective-permute-start.17 = (bf16[16,2048]{1,0:T(8,128)(2,1)S(1)}, bf16[16,2048]{1,0:T(8,128)(2,1)S(1)}, u32[]{:S(2)}, u32[]{:S(2)}) collective-permute-start(bf16[16,2048]{1,0:T(8,128)(2,1)S(1)} %pad_maximum_fusion.3), channel_id=1, source_target_pairs={{0,2},{1,3},{2,0},{3,1},{4,6},{5,7},{6,4},{7,5},{8,10},{9,11},{10,... | collective-permute-start | bytes 196616 | tf_op jit(solution)/shard_map/ppermute | solution.py:301
  49.8 2.7 %collective-permute-start.18 = (bf16[16,2048]{1,0:T(8,128)(2,1)S(1)}, bf16[16,2048]{1,0:T(8,128)(2,1)S(1)}, u32[]{:S(2)}, u32[]{:S(2)}) collective-permute-start(bf16[16,2048]{1,0:T(8,128)(2,1)S(1)} %pad_maximum_fusion.4), channel_id=1, source_target_pairs={{0,1},{1,0},{2,3},{3,2},{4,5},{5,4},{6,7},{7,6},{8,9},{9,8},{10,11... | collective-permute-start | bytes 196616 | tf_op jit(solution)/shard_map/ppermute | solution.py:301
  52.5 0.8 %entropies.1 = (f32[1,128]{1,0:T(1,128)}, f32[1,1]{1,0:T(1,128)}) custom-call(f32[32,4,128]{2,1,0:T(4,128)S(1)} %all_to_all.5.stats_ref, bf16[16,128]{1,0:T(8,128)(2,1)S(1)} %get-tuple-element.31.refs_6_.picker_ref), custom_call_target="tpu_custom_call" | custom-call | tf_op jit(solution)/shard_map/entropies/pallas_call | solution.py:223
  53.3 1.6 %collective-permute-done.16 = bf16[16,2048]{1,0:T(8,128)(2,1)S(1)} collective-permute-done((bf16[16,2048]{1,0:T(8,128)(2,1)S(1)}, bf16[16,2048]{1,0:T(8,128)(2,1)S(1)}, u32[]{:S(2)}, u32[]{:S(2)}) %collective-permute-start.16) | collective-permute-done | bytes 65568 | tf_op jit(solution)/shard_map/ppermute | solution.py:301
  54.9 1.8 %collective-permute-done.17 = bf16[16,2048]{1,0:T(8,128)(2,1)S(1)} collective-permute-done((bf16[16,2048]{1,0:T(8,128)(2,1)S(1)}, bf16[16,2048]{1,0:T(8,128)(2,1)S(1)}, u32[]{:S(2)}, u32[]{:S(2)}) %collective-permute-start.17) | collective-permute-done | bytes 65568 | tf_op jit(solution)/shard_map/ppermute | solution.py:301
  56.7 1.1 %convolution_convert_fusion = bf16[128,2048]{1,0:T(8,128)(2,1)} fusion(bf16[16,128]{1,0:T(8,128)(2,1)S(1)} %get-tuple-element.31.refs_6_.picker_ref, f32[16,1024]{1,0:T(8,128)S(1)} %get-tuple-element.55, f32[16,1024]{1,0:T(8,128)S(1)} %get-tuple-element.56, bf16[16,2048]{1,0:T(8,128)(2,1)S(1)} %collective-permute-done.18, ...), kind=kOutput, calls=%fused_computation | convolution fusion | flops 8912896 | bytes 856064 | tf_op jit(solution)/shard_map/dot_general | solution.py:357
  (21 shorter events, 0.3 us)
Async XLA Ops:
  0.6 18.2 %copy-start = (bf16[8192,256]{1,0:T(8,128)(2,1)S(1)}, bf16[8192,256]{1,0:T(8,128)(2,1)}, u32[]{:S(2)}) copy-start(bf16[8192,256]{1,0:T(8,128)(2,1)} %head_ref.3) | copy-start | bytes 12582916
  2.9 6.4 %collective-permute-start = (bf16[16,4096]{1,0:T(8,128)(2,1)S(1)}, bf16[16,4096]{1,0:T(8,128)(2,1)S(1)}, u32[]{:S(2)}, u32[]{:S(2)}) collective-permute-start(bf16[16,4096]{1,0:T(8,128)(2,1)S(1)} %get-tuple-element.25.own_ref), channel_id=1, source_target_pairs={{0,8},{4,20},{8,0},{12,28},{16,24},{20,4},{24,16},{28,12},{1,9},{5... | collective-permute-start | bytes 393224 | tf_op jit(solution)/shard_map/ppermute | solution.py:298
  5.9 6.3 %collective-permute-start.2 = (bf16[16,4096]{1,0:T(8,128)(2,1)S(1)}, bf16[16,4096]{1,0:T(8,128)(2,1)S(1)}, u32[]{:S(2)}, u32[]{:S(2)}) collective-permute-start(bf16[16,4096]{1,0:T(8,128)(2,1)S(1)} %get-tuple-element.26), channel_id=1, source_target_pairs={{0,8},{4,20},{8,0},{12,28},{16,24},{20,4},{24,16},{28,12},{1,9},{5... | collective-permute-start | bytes 393224 | tf_op jit(solution)/shard_map/ppermute | solution.py:298
  7.2 6.4 %collective-permute-start.1 = (bf16[16,8192]{1,0:T(8,128)(2,1)S(1)}, bf16[16,8192]{1,0:T(8,128)(2,1)S(1)}, u32[]{:S(2)}, u32[]{:S(2)}) collective-permute-start(bf16[16,8192]{1,0:T(8,128)(2,1)S(1)} %pad_maximum_fusion), channel_id=1, source_target_pairs={{0,16},{4,12},{8,24},{12,4},{16,0},{20,28},{24,8},{28,20},{1,17},{... | collective-permute-start | bytes 786440 | tf_op jit(solution)/shard_map/ppermute | solution.py:298
  9.3 5.8 %collective-permute-start.3 = (bf16[16,4096]{1,0:T(8,128)(2,1)S(1)}, bf16[16,4096]{1,0:T(8,128)(2,1)S(1)}, u32[]{:S(2)}, u32[]{:S(2)}) collective-permute-start(bf16[16,4096]{1,0:T(8,128)(2,1)S(1)} %collective-permute-done), channel_id=1, source_target_pairs={{0,16},{4,12},{8,24},{12,4},{16,0},{20,28},{24,8},{28,20},{1,17},{... | collective-permute-start | bytes 393224 | tf_op jit(solution)/shard_map/ppermute | solution.py:298
  12.2 5.0 %collective-permute-start.5 = (bf16[16,4096]{1,0:T(8,128)(2,1)S(1)}, bf16[16,4096]{1,0:T(8,128)(2,1)S(1)}, u32[]{:S(2)}, u32[]{:S(2)}) collective-permute-start(bf16[16,4096]{1,0:T(8,128)(2,1)S(1)} %collective-permute-done.2), channel_id=1, source_target_pairs={{0,16},{4,12},{8,24},{12,4},{16,0},{20,28},{24,8},{28,20},{1,17},{... | collective-permute-start | bytes 393224 | tf_op jit(solution)/shard_map/ppermute | solution.py:298
  15.1 3.7 %collective-permute-start.4 = (bf16[96,4096]{1,0:T(8,128)(2,1)S(1)}, bf16[96,4096]{1,0:T(8,128)(2,1)S(1)}, u32[]{:S(2)}, u32[]{:S(2)}) collective-permute-start(bf16[96,4096]{1,0:T(8,128)(2,1)S(1)} %slice_dynamic-update-slice_fusion.refs_1_), channel_id=1, source_target_pairs={{0,4},{4,0},{8,12},{12,8},{16,20},{20,16},{24,28},{28,24},{1,5},{5... | collective-permute-start | bytes 2359304 | tf_op jit(solution)/shard_map/ppermute | solution.py:294
  17.2 1.6 %collective-permute-start.6 = (bf16[32,4096]{1,0:T(8,128)(2,1)S(1)}, bf16[32,4096]{1,0:T(8,128)(2,1)S(1)}, u32[]{:S(2)}, u32[]{:S(2)}) collective-permute-start(bf16[32,4096]{1,0:T(8,128)(2,1)S(1)} %constant_dynamic-update-slice_fusion.4.refs_3_), channel_id=1, source_target_pairs={{0,4},{4,0},{8,12},{12,8},{16,20},{20,16},{24,28},{28,24},{1,5},{5... | collective-permute-start | bytes 786440 | tf_op jit(solution)/shard_map/ppermute | solution.py:294
  34.3 1.4 %collective-permute-start.7 = (bf16[4,16,1024]{2,1,0:T(8,128)(2,1)S(1)}, bf16[4,16,1024]{2,1,0:T(8,128)(2,1)S(1)}, u32[]{:S(2)}, u32[]{:S(2)}) collective-permute-start(bf16[4,16,1024]{2,1,0:T(8,128)(2,1)S(1)} %get-tuple-element.37), channel_id=1, source_target_pairs={{0,4},{4,0},{8,12},{12,8},{16,20},{20,16},{24,28},{28,24},{1,5},{5... | collective-permute-start | bytes 393224 | tf_op jit(solution)/shard_map/ppermute | solution.py:294
  34.4 1.5 %collective-permute-start.8 = (bf16[4,16,1024]{2,1,0:T(8,128)(2,1)S(1)}, bf16[4,16,1024]{2,1,0:T(8,128)(2,1)S(1)}, u32[]{:S(2)}, u32[]{:S(2)}) collective-permute-start(bf16[4,16,1024]{2,1,0:T(8,128)(2,1)S(1)} %get-tuple-element.38), channel_id=1, source_target_pairs={{0,4},{4,0},{8,12},{12,8},{16,20},{20,16},{24,28},{28,24},{1,5},{5... | collective-permute-start | bytes 393224 | tf_op jit(solution)/shard_map/ppermute | solution.py:294
  35.9 2.6 %collective-permute-start.9 = (bf16[3,4,16,1024]{3,2,1,0:T(8,128)(2,1)S(1)}, bf16[3,4,16,1024]{3,2,1,0:T(8,128)(2,1)S(1)}, u32[]{:S(2)}, u32[]{:S(2)}) collective-permute-start(bf16[3,4,16,1024]{3,2,1,0:T(8,128)(2,1)S(1)} %get-tuple-element.39), channel_id=1, source_target_pairs={{0,4},{4,0},{8,12},{12,8},{16,20},{20,16},{24,28},{28,24},{1,5},{5... | collective-permute-start | bytes 1179656 | tf_op jit(solution)/shard_map/ppermute | solution.py:294
  36.3 5.0 %collective-permute-start.12 = (bf16[4,16,1024]{2,1,0:T(8,128)(2,1)S(1)}, bf16[4,16,1024]{2,1,0:T(8,128)(2,1)S(1)}, u32[]{:S(2)}, u32[]{:S(2)}) collective-permute-start(bf16[4,16,1024]{2,1,0:T(8,128)(2,1)S(1)} %fusion.1), channel_id=1, source_target_pairs={{0,16},{4,12},{8,24},{12,4},{16,0},{20,28},{24,8},{28,20},{1,17},{... | collective-permute-start | bytes 393224 | tf_op jit(solution)/shard_map/ppermute | solution.py:298
  37.0 1.7 %collective-permute-start.10 = (bf16[3,4,16,1024]{3,2,1,0:T(8,128)(2,1)S(1)}, bf16[3,4,16,1024]{3,2,1,0:T(8,128)(2,1)S(1)}, u32[]{:S(2)}, u32[]{:S(2)}) collective-permute-start(bf16[3,4,16,1024]{3,2,1,0:T(8,128)(2,1)S(1)} %get-tuple-element.41), channel_id=1, source_target_pairs={{0,4},{4,0},{8,12},{12,8},{16,20},{20,16},{24,28},{28,24},{1,5},{5... | collective-permute-start | bytes 1179656 | tf_op jit(solution)/shard_map/ppermute | solution.py:294
  37.0 5.7 %collective-permute-start.14 = (bf16[4,16,1024]{2,1,0:T(8,128)(2,1)S(1)}, bf16[4,16,1024]{2,1,0:T(8,128)(2,1)S(1)}, u32[]{:S(2)}, u32[]{:S(2)}) collective-permute-start(bf16[4,16,1024]{2,1,0:T(8,128)(2,1)S(1)} %fusion), channel_id=1, source_target_pairs={{0,16},{4,12},{8,24},{12,4},{16,0},{20,28},{24,8},{28,20},{1,17},{... | collective-permute-start | bytes 393224 | tf_op jit(solution)/shard_map/ppermute | solution.py:298
  38.8 9.0 %collective-permute-start.11 = (bf16[4,16,2048]{2,1,0:T(8,128)(2,1)S(1)}, bf16[4,16,2048]{2,1,0:T(8,128)(2,1)S(1)}, u32[]{:S(2)}, u32[]{:S(2)}) collective-permute-start(bf16[4,16,2048]{2,1,0:T(8,128)(2,1)S(1)} %pad_maximum_fusion.1), channel_id=1, source_target_pairs={{0,16},{4,12},{8,24},{12,4},{16,0},{20,28},{24,8},{28,20},{1,17},{... | collective-permute-start | bytes 786440 | tf_op jit(solution)/shard_map/ppermute | solution.py:298
  41.4 5.0 %collective-permute-start.13 = (bf16[4,16,1024]{2,1,0:T(8,128)(2,1)S(1)}, bf16[4,16,1024]{2,1,0:T(8,128)(2,1)S(1)}, u32[]{:S(2)}, u32[]{:S(2)}) collective-permute-start(bf16[4,16,1024]{2,1,0:T(8,128)(2,1)S(1)} %fusion.4), channel_id=1, source_target_pairs={{0,8},{4,20},{8,0},{12,28},{16,24},{20,4},{24,16},{28,12},{1,9},{5... | collective-permute-start | bytes 393224 | tf_op jit(solution)/shard_map/ppermute | solution.py:298
  42.8 5.0 %collective-permute-start.15 = (bf16[4,16,1024]{2,1,0:T(8,128)(2,1)S(1)}, bf16[4,16,1024]{2,1,0:T(8,128)(2,1)S(1)}, u32[]{:S(2)}, u32[]{:S(2)}) collective-permute-start(bf16[4,16,1024]{2,1,0:T(8,128)(2,1)S(1)} %fusion.2), channel_id=1, source_target_pairs={{0,8},{4,20},{8,0},{12,28},{16,24},{20,4},{24,16},{28,12},{1,9},{5... | collective-permute-start | bytes 393224 | tf_op jit(solution)/shard_map/ppermute | solution.py:298
  48.0 6.9 %collective-permute-start.16 = (bf16[16,2048]{1,0:T(8,128)(2,1)S(1)}, bf16[16,2048]{1,0:T(8,128)(2,1)S(1)}, u32[]{:S(2)}, u32[]{:S(2)}) collective-permute-start(bf16[16,2048]{1,0:T(8,128)(2,1)S(1)} %pad_maximum_fusion.2), channel_id=1, source_target_pairs={{0,3},{1,2},{2,1},{3,0},{4,7},{5,6},{6,5},{7,4},{8,11},{9,10},{10,... | collective-permute-start | bytes 196616 | tf_op jit(solution)/shard_map/ppermute | solution.py:301
  48.9 7.8 %collective-permute-start.17 = (bf16[16,2048]{1,0:T(8,128)(2,1)S(1)}, bf16[16,2048]{1,0:T(8,128)(2,1)S(1)}, u32[]{:S(2)}, u32[]{:S(2)}) collective-permute-start(bf16[16,2048]{1,0:T(8,128)(2,1)S(1)} %pad_maximum_fusion.3), channel_id=1, source_target_pairs={{0,2},{1,3},{2,0},{3,1},{4,6},{5,7},{6,4},{7,5},{8,10},{9,11},{10,... | collective-permute-start | bytes 196616 | tf_op jit(solution)/shard_map/ppermute | solution.py:301
  49.8 6.9 %collective-permute-start.18 = (bf16[16,2048]{1,0:T(8,128)(2,1)S(1)}, bf16[16,2048]{1,0:T(8,128)(2,1)S(1)}, u32[]{:S(2)}, u32[]{:S(2)}) collective-permute-start(bf16[16,2048]{1,0:T(8,128)(2,1)S(1)} %pad_maximum_fusion.4), channel_id=1, source_target_pairs={{0,1},{1,0},{2,3},{3,2},{4,5},{5,4},{6,7},{7,6},{8,9},{9,8},{10,11... | collective-permute-start | bytes 196616 | tf_op jit(solution)/shard_map/ppermute | solution.py:301
